TPU v7x, 32 devices: a whole 2x2x4 slice. The times are simulated.
32 devices in a mesh: gz: 8 (over z, y), gy: 4 (over x, core).
Axes of the slice: x: 2, y: 2, z: 4, core: 2. Of those that a mesh axis runs over, the one named last changes fastest.
Arguments:
- features: bfloat16 [64, 16, 32, 128], P(None, 'gz', 'gy'), may hold values from -6 to 6
- conv_weight: bfloat16 [3, 3, 64, 192], replicated, may hold values from -0.15625 to 0.15625
- down_weight: bfloat16 [2, 2, 128, 128], replicated, may hold values from -0.25 to 0.25
- cotangent: bfloat16 [128, 8, 1024], P(None, 'gz', 'gy'), may hold values from -6 to 6
Outputs:
- section_out: bfloat16 [128, 8, 1024], P(None, 'gz', 'gy')
- grad_field: float32 [64, 16, 32, 128], P(None, 'gz', 'gy')
- grad_conv: float32 [3, 3, 64, 192], replicated
- grad_down: float32 [2, 2, 128, 128], replicated
All inputs are finite; a program needn't handle non-finite values.
Results may differ from a plain program's by a relative error of at most 0.005.
Values may be sent and summed in bfloat16 or wider, within the bound.
No kernel may reach another device: no remote copies, remote signals or barrier semaphores. Data moves between devices by JAX's collectives and lax.ppermute only.
A program may use at most 64 MiB of HBM per device.

v0:
```python
import math

import jax
import jax.numpy as jnp
from jax import lax
from jax.sharding import PartitionSpec as P


def extended(cells, sides, width):
    for axis, dim in sides:
        count = lax.axis_size(axis)
        head = lax.slice_in_dim(cells, 0, width, axis=dim)
        tail = lax.slice_in_dim(cells, cells.shape[dim] - width, cells.shape[dim], axis=dim)
        cells = jnp.concatenate(
            [
                lax.ppermute(tail, axis, [(i, (i + 1) % count) for i in range(count)]),
                cells,
                lax.ppermute(head, axis, [((i + 1) % count, i) for i in range(count)]),
            ],
            axis=dim,
        )
    return cells


def widen(framed):
    return jnp.concatenate([jnp.roll(framed, 1 - tap_x, axis=3) for tap_x in range(3)], axis=0)


def fold_along(spread, channels):
    result = jnp.roll(spread[0:channels], -1, axis=3)
    result = result + spread[channels : 2 * channels]
    result = result + jnp.roll(spread[2 * channels : 3 * channels], 1, axis=3)
    return result


def body(features, conv_weight, down_weight, cotangent):
    channels, plane_count, row_count, breadth = features.shape
    out_channels = down_weight.shape[2]
    cell_count = plane_count * row_count * breadth * lax.axis_size("gz") * lax.axis_size("gy")
    grad_scale = 1.0 / math.sqrt(cell_count)
    framed = extended(features, (("gz", 1), ("gy", 2)), 1)
    columns = widen(framed)
    preact = jnp.zeros((channels, plane_count, row_count, breadth), jnp.float32)
    for tap_z in range(3):
        for tap_y in range(3):
            window = columns[:, tap_z : tap_z + plane_count, tap_y : tap_y + row_count]
            preact = preact + jnp.einsum(
                "oj,jzyx->ozyx",
                conv_weight[tap_z, tap_y],
                window,
                preferred_element_type=jnp.float32,
            )
    hidden = jax.nn.silu(preact).astype(jnp.bfloat16)
    blocks = hidden.reshape(channels, plane_count // 2, 2, row_count // 2, 2, breadth // 2, 2)
    down_split = down_weight.reshape(2, 2, out_channels, 2, channels)
    coarse = jnp.einsum(
        "aboei,iZaYbXe->oZYX", down_split, blocks, preferred_element_type=jnp.float32
    )
    section_out = coarse.reshape(out_channels, plane_count // 2, -1).astype(jnp.bfloat16)
    coarse_cot = cotangent.reshape(out_channels, plane_count // 2, row_count // 2, breadth // 2)
    hidden_grad = jnp.einsum(
        "aboei,oZYX->iZaYbXe", down_split, coarse_cot, preferred_element_type=jnp.float32
    )
    hidden_grad = hidden_grad.reshape(channels, plane_count, row_count, breadth)
    local_down = jnp.einsum(
        "oZYX,iZaYbXe->aboei", coarse_cot, blocks, preferred_element_type=jnp.float32
    )
    local_down = local_down.reshape(2, 2, out_channels, 2 * channels)
    gate_sig = jax.nn.sigmoid(preact)
    gate_grad = (hidden_grad * gate_sig * (1.0 + preact * (1.0 - gate_sig))).astype(jnp.bfloat16)
    kernel_rows = []
    for tap_z in range(3):
        row_list = []
        for tap_y in range(3):
            window = columns[:, tap_z : tap_z + plane_count, tap_y : tap_y + row_count]
            row_list.append(
                jnp.einsum("ozyx,jzyx->oj", gate_grad, window, preferred_element_type=jnp.float32)
            )
        kernel_rows.append(jnp.stack(row_list, axis=0))
    local_conv = jnp.stack(kernel_rows, axis=0)
    spread = jnp.zeros((3 * channels, plane_count + 2, row_count + 2, breadth), jnp.float32)
    for tap_z in range(3):
        for tap_y in range(3):
            term = jnp.einsum(
                "oj,ozyx->jzyx",
                conv_weight[tap_z, tap_y],
                gate_grad,
                preferred_element_type=jnp.float32,
            )
            spread = spread.at[:, tap_z : tap_z + plane_count, tap_y : tap_y + row_count].add(term)
    folded = fold_along(spread, channels)
    bordered = extended(folded.astype(jnp.bfloat16), (("gz", 1), ("gy", 2)), 1).astype(folded.dtype)
    plane_fold = bordered[:, 2 : plane_count + 2]
    plane_fold = plane_fold.at[:, 0].add(bordered[:, 0])
    plane_fold = plane_fold.at[:, plane_count - 1].add(bordered[:, plane_count + 3])
    row_fold = plane_fold[:, :, 2 : row_count + 2]
    row_fold = row_fold.at[:, :, 0].add(plane_fold[:, :, 0])
    row_fold = row_fold.at[:, :, row_count - 1].add(plane_fold[:, :, row_count + 3])
    summed_conv, summed_down = lax.psum((local_conv, local_down), ("gz", "gy"))
    grad_conv = summed_conv * grad_scale
    grad_down = summed_down * grad_scale
    return (section_out, row_fold, grad_conv, grad_down)


def solution(mesh):
    return jax.shard_map(
        body,
        mesh=mesh,
        in_specs=(P(None, "gz", "gy", None), P(), P(), P(None, "gz", "gy")),
        out_specs=(P(None, "gz", "gy"), P(None, "gz", "gy", None), P(), P()),
        check_vma=False,
    )
```

profile of v0, /device:TPU:0, one launch (start us, length us, event | category | flops | bytes accessed | tf_op | source)
XLA Modules:
  0.0 207.0 jit_solution(7143356639437755437)
XLA Ops:
  7.2 1.0 fusion.104
  8.2 3.0 %collective-permute-start = (bf16[64,1,8,128]{3,0,2,1:T(8,128)(2,1)S(1)}, bf16[64,1,8,128]{3,0,2,1:T(8,128)(2,1)S(1)}, u32[]{:S(2)}, u32[]{:S(2)}) collective-permute-start(bf16[64,1,8,128]{3,0,2,1:T(8,128)(2,1)S(1)} %copy.161), channel_id=1, source_target_pairs={{0,4},{4,8},{8,12},{12,16},{16,20},{20,24},{24,28},{28,0},{1,5},{5... | collective-permute-start | bytes 393224 | tf_op jit(solution)/shard_map/ppermute | solution.py:16
  11.3 3.1 %collective-permute-start.1 = (bf16[64,1,8,128]{3,0,2,1:T(8,128)(2,1)S(1)}, bf16[64,1,8,128]{3,0,2,1:T(8,128)(2,1)S(1)}, u32[]{:S(2)}, u32[]{:S(2)}) collective-permute-start(bf16[64,1,8,128]{3,0,2,1:T(8,128)(2,1)S(1)} %copy.162), channel_id=1, source_target_pairs={{4,0},{8,4},{12,8},{16,12},{20,16},{24,20},{28,24},{0,28},{5,1},{9... | collective-permute-start | bytes 393224 | tf_op jit(solution)/shard_map/ppermute | solution.py:18
  14.4 1.0 copy.74
  15.4 1.0 copy.75
  16.7 0.6 fusion.105
  17.3 0.8 copy.76
  18.4 0.8 and_reduce_fusion
  19.5 1.7 collective-permute-start.3
  21.2 0.6 fusion.106
  21.8 1.4 collective-permute-done.2
  23.9 1.2 maximum_maximum_fusion
  27.2 1.8 fusion.99
  28.9 0.5 multiply_convert_fusion
  30.3 1.8 fusion.7
  32.1 2.4 %fusion = f32[192,4,10,128]{3,0,2,1:T(8,128)S(1)} fusion(f32[192,4,10,128]{3,0,2,1:T(8,128)S(1)} %fusion.7, s32[]{:T(128)} %bitcast.50, s32[]{:T(128)} %bitcast.51, bf16[64,2,8,128]{3,0,2,1:T(8,128)(2,1)S(1)} %get-tuple-element.195, pred[]{:T(512)} %and_reduce_fusion, bf16[3,3,64,192]{3,2,1,0:T(8,128)(2,1)S(1)} %copy-done.2), kind=kOutput, calls=%fused_computation.2 | convolution fusion | flops 51118080 | bytes 3440649 | tf_op jit(solution)/shard_map/oj,ozyx->jzyx/dot_general | solution.py:84
  34.5 0.6 fusion.6
  35.1 0.6 fusion.5
  35.7 0.6 fusion.4
  36.3 0.6 fusion.3
  36.9 0.6 fusion.2
  37.6 0.6 fusion.1
  38.2 0.5 fusion.97
  38.6 1.4 copy-done
  40.1 2.0 fusion.98
  42.4 1.0 convolution_bitcast_fusion.11
  43.4 1.0 convolution_bitcast_fusion.6
  44.4 1.0 convolution_bitcast_fusion.7
  45.4 1.0 convolution_bitcast_fusion.8
  46.4 1.0 convolution_bitcast_fusion.9
  47.4 1.0 convolution_bitcast_fusion.3
  48.4 1.0 convolution_bitcast_fusion.4
  49.4 1.0 convolution_bitcast_fusion.5
  50.4 1.0 copy.72
  51.4 2.8 %fusion.9 = bf16[64,4,10,128]{3,0,2,1:T(8,128)(2,1)S(1)} fusion(f32[192,4,10,128]{3,0,2,1:T(8,128)} %copy-done, f32[64,4,10,1]{3,0,2,1:T(8,128)S(1)} %get-tuple-element.175, f32[64,4,10,127]{3,0,2,1:T(8,128)} %get-tuple-element.177, f32[64,4,10,127]{3,0,2,1:T(8,128)} %get-tuple-element.176, f32[64,4,10,1]{3,0,2,1:T(8,128)S(1)} %get-tuple-element.174), kind=kLoop, calls=%fused_computation.21 | loop fusion | flops 1638400 | bytes 4587520 | tf_op jit(solution)/shard_map/convert_element_type | solution.py:92
  54.5 4.7 %collective-permute-start.5 = (bf16[64,1,10,128]{3,0,2,1:T(8,128)(2,1)S(1)}, bf16[64,1,10,128]{3,0,2,1:T(8,128)(2,1)S(1)}, u32[]{:S(2)}, u32[]{:S(2)}) collective-permute-start(bf16[64,1,10,128]{3,0,2,1:T(8,128)(2,1)S(1)} %get-tuple-element.190), channel_id=1, source_target_pairs={{4,0},{8,4},{12,8},{16,12},{20,16},{24,20},{28,24},{0,28},{5,1},{9... | collective-permute-start | bytes 491528 | tf_op jit(solution)/shard_map/ppermute | solution.py:18
  59.2 1.6 copy.73
  61.7 0.8 copy.97
  62.6 0.7 copy.98
  63.5 1.1 collective-permute-done.5
  64.7 0.6 collective-permute-start.6
  65.3 1.2 collective-permute-start.7
  66.5 0.9 pad_maximum_fusion.1
  67.4 1.4 collective-permute-done.6
  69.8 1.1 copy.99
  70.9 125.7 %all-reduce.4.cloned.1.call-done = (f32[3,3,64,192]{3,2,1,0:T(8,128)}, f32[2,2,128,128]{3,2,1,0:T(8,128)}) async-done(((f32[3,3,64,192]{3,2,1,0:T(8,128)}, f32[2,2,128,128]{3,2,1,0:T(8,128)}), (f32[3,3,64,192]{3,2,1,0:T(8,128)}, f32[2,2,128,128]{3,2,1,0:T(8,128)})) %all-reduce.4.cloned.1.call-update) | async-done | bytes 704528 | tf_op jit(solution)/shard_map/psum | solution.py:99
  196.5 1.9 broadcast_multiply_fusion
  198.5 1.7 broadcast_multiply_fusion.1
  (72 shorter events, 7.2 us)
Async XLA Ops:
  7.2 189.4 %all-reduce.4.cloned.1.call-start = ((), (), s32[]{:S(2)}) async-start(), calls=%async_computation | async-start | bytes 1703936 | tf_op jit(solution)/shard_map/psum | solution.py:99
  8.2 11.0 %collective-permute-start = (bf16[64,1,8,128]{3,0,2,1:T(8,128)(2,1)S(1)}, bf16[64,1,8,128]{3,0,2,1:T(8,128)(2,1)S(1)}, u32[]{:S(2)}, u32[]{:S(2)}) collective-permute-start(bf16[64,1,8,128]{3,0,2,1:T(8,128)(2,1)S(1)} %copy.161), channel_id=1, source_target_pairs={{0,4},{4,8},{8,12},{12,16},{16,20},{20,24},{24,28},{28,0},{1,5},{5... | collective-permute-start | bytes 393224 | tf_op jit(solution)/shard_map/ppermute | solution.py:16
  11.3 8.1 %collective-permute-start.1 = (bf16[64,1,8,128]{3,0,2,1:T(8,128)(2,1)S(1)}, bf16[64,1,8,128]{3,0,2,1:T(8,128)(2,1)S(1)}, u32[]{:S(2)}, u32[]{:S(2)}) collective-permute-start(bf16[64,1,8,128]{3,0,2,1:T(8,128)(2,1)S(1)} %copy.162), channel_id=1, source_target_pairs={{4,0},{8,4},{12,8},{16,12},{20,16},{24,20},{28,24},{0,28},{5,1},{9... | collective-permute-start | bytes 393224 | tf_op jit(solution)/shard_map/ppermute | solution.py:18
  16.7 1.7 copy-start.12
  17.3 2.0 copy-start.3
  19.4 3.7 %collective-permute-start.2 = (bf16[64,4,1,128]{3,0,2,1:T(8,128)(2,1)S(1)}, bf16[64,4,1,128]{3,0,2,1:T(8,128)(2,1)S(1)}, u32[]{:S(2)}, u32[]{:S(2)}) collective-permute-start(bf16[64,4,1,128]{3,0,2,1:T(8,128)(2,1)S(1)} %get-tuple-element.197), channel_id=1, source_target_pairs={{0,1},{1,2},{2,3},{3,0},{4,5},{5,6},{6,7},{7,4},{8,9},{9,10},{10,1... | collective-permute-start | bytes 196616 | tf_op jit(solution)/shard_map/ppermute | solution.py:16
  19.5 3.7 %collective-permute-start.3 = (bf16[64,4,1,128]{3,0,2,1:T(8,128)(2,1)S(1)}, bf16[64,4,1,128]{3,0,2,1:T(8,128)(2,1)S(1)}, u32[]{:S(2)}, u32[]{:S(2)}) collective-permute-start(bf16[64,4,1,128]{3,0,2,1:T(8,128)(2,1)S(1)} %get-tuple-element.198), channel_id=1, source_target_pairs={{1,0},{2,1},{3,2},{0,3},{5,4},{6,5},{7,6},{4,7},{9,8},{10,9},{11,1... | collective-permute-start | bytes 196616 | tf_op jit(solution)/shard_map/ppermute | solution.py:18
  23.9 1.2 copy-start.2
  38.2 1.9 copy-start
  54.3 6.8 %copy-start.1 = (bf16[64,2,8,128]{0,3,2,1:T(8,128)(2,1)S(1)}, bf16[64,2,8,128]{0,3,2,1:T(8,128)(2,1)}, u32[]{:S(2)}) copy-start(bf16[64,2,8,128]{0,3,2,1:T(8,128)(2,1)} %copy.72) | copy-start | bytes 786436
  54.3 7.4 %copy-start.9 = (f32[1,64,192]{2,1,0:T(8,128)S(1)}, f32[1,64,192]{2,1,0:T(8,128)}, u32[]{:S(2)}) copy-start(f32[1,64,192]{2,1,0:T(8,128)} %convolution_bitcast_fusion.3) | copy-start | bytes 147460
  54.3 7.4 %copy-start.10 = (f32[1,64,192]{2,1,0:T(8,128)S(1)}, f32[1,64,192]{2,1,0:T(8,128)}, u32[]{:S(2)}) copy-start(f32[1,64,192]{2,1,0:T(8,128)} %convolution_bitcast_fusion.4) | copy-start | bytes 147460
  54.3 7.4 %copy-start.11 = (f32[1,64,192]{2,1,0:T(8,128)S(1)}, f32[1,64,192]{2,1,0:T(8,128)}, u32[]{:S(2)}) copy-start(f32[1,64,192]{2,1,0:T(8,128)} %convolution_bitcast_fusion.5) | copy-start | bytes 147460
  54.4 9.2 %collective-permute-start.4 = (bf16[64,1,10,128]{3,0,2,1:T(8,128)(2,1)S(1)}, bf16[64,1,10,128]{3,0,2,1:T(8,128)(2,1)S(1)}, u32[]{:S(2)}, u32[]{:S(2)}) collective-permute-start(bf16[64,1,10,128]{3,0,2,1:T(8,128)(2,1)S(1)} %get-tuple-element.189), channel_id=1, source_target_pairs={{0,4},{4,8},{8,12},{12,16},{16,20},{20,24},{24,28},{28,0},{1,5},{5... | collective-permute-start | bytes 491528 | tf_op jit(solution)/shard_map/ppermute | solution.py:16
  54.5 10.1 %collective-permute-start.5 = (bf16[64,1,10,128]{3,0,2,1:T(8,128)(2,1)S(1)}, bf16[64,1,10,128]{3,0,2,1:T(8,128)(2,1)S(1)}, u32[]{:S(2)}, u32[]{:S(2)}) collective-permute-start(bf16[64,1,10,128]{3,0,2,1:T(8,128)(2,1)S(1)} %get-tuple-element.190), channel_id=1, source_target_pairs={{4,0},{8,4},{12,8},{16,12},{20,16},{24,20},{28,24},{0,28},{5,1},{9... | collective-permute-start | bytes 491528 | tf_op jit(solution)/shard_map/ppermute | solution.py:18
  59.2 4.2 %copy-start.4 = (f32[1,64,192]{2,1,0:T(8,128)S(1)}, f32[1,64,192]{2,1,0:T(8,128)}, u32[]{:S(2)}) copy-start(f32[1,64,192]{2,1,0:T(8,128)} %convolution_bitcast_fusion.11) | copy-start | bytes 147460
  59.2 4.2 %copy-start.5 = (f32[1,64,192]{2,1,0:T(8,128)S(1)}, f32[1,64,192]{2,1,0:T(8,128)}, u32[]{:S(2)}) copy-start(f32[1,64,192]{2,1,0:T(8,128)} %convolution_bitcast_fusion.6) | copy-start | bytes 147460
  59.2 4.2 %copy-start.6 = (f32[1,64,192]{2,1,0:T(8,128)S(1)}, f32[1,64,192]{2,1,0:T(8,128)}, u32[]{:S(2)}) copy-start(f32[1,64,192]{2,1,0:T(8,128)} %convolution_bitcast_fusion.7) | copy-start | bytes 147460
  59.2 4.2 %copy-start.7 = (f32[1,64,192]{2,1,0:T(8,128)S(1)}, f32[1,64,192]{2,1,0:T(8,128)}, u32[]{:S(2)}) copy-start(f32[1,64,192]{2,1,0:T(8,128)} %convolution_bitcast_fusion.8) | copy-start | bytes 147460
  59.2 4.2 %copy-start.8 = (f32[1,64,192]{2,1,0:T(8,128)S(1)}, f32[1,64,192]{2,1,0:T(8,128)}, u32[]{:S(2)}) copy-start(f32[1,64,192]{2,1,0:T(8,128)} %convolution_bitcast_fusion.9) | copy-start | bytes 147460
  64.7 4.1 %collective-permute-start.6 = (bf16[64,6,1,128]{3,0,2,1:T(8,128)(2,1)S(1)}, bf16[64,6,1,128]{3,0,2,1:T(8,128)(2,1)S(1)}, u32[]{:S(2)}, u32[]{:S(2)}) collective-permute-start(bf16[64,6,1,128]{3,0,2,1:T(8,128)(2,1)S(1)} %get-tuple-element.187), channel_id=1, source_target_pairs={{0,1},{1,2},{2,3},{3,0},{4,5},{5,6},{6,7},{7,4},{8,9},{9,10},{10,1... | collective-permute-start | bytes 294920 | tf_op jit(solution)/shard_map/ppermute | solution.py:16
  65.3 4.0 %collective-permute-start.7 = (bf16[64,6,1,128]{3,0,2,1:T(8,128)(2,1)S(1)}, bf16[64,6,1,128]{3,0,2,1:T(8,128)(2,1)S(1)}, u32[]{:S(2)}, u32[]{:S(2)}) collective-permute-start(bf16[64,6,1,128]{3,0,2,1:T(8,128)(2,1)S(1)} %get-tuple-element.188), channel_id=1, source_target_pairs={{1,0},{2,1},{3,2},{0,3},{5,4},{6,5},{7,6},{4,7},{9,8},{10,9},{11,1... | collective-permute-start | bytes 294920 | tf_op jit(solution)/shard_map/ppermute | solution.py:18
Sparse Core Ops, SparseCore 0:
  67.5 129.0 all-reduce.3
where the time goes:
time: 207 us
  waiting for transfers between devices  130 us (63%)
  matrix products  20.1 us (10%)
  local copies, waits for them, and re-layouts  17.8 us (9%)
  between operations  14.6 us (7%)
  starting transfers between devices  14.5 us (7%)
  other arithmetic  9.84 us (5%)
    psum x1, waiting for transfers between devices, body(): summed_conv, summed_down = lax.psum((local_conv, local_down), ('gz', 'gy'))  126 us
    ppermute x4, starting transfers between devices, extended(): lax.ppermute(head, axis, [((i + 1) % count, i) for i in range(count)])  10.7 us
    dot_general x9, matrix products, body(): jnp.einsum('ozyx,jzyx->oj', gate_grad, window, preferred_element_type=jnp...  8.38 us
    dot_general x9, matrix products, body(): jnp.einsum('oj,ozyx->jzyx', conv_weight[tap_z, tap_y], gate_grad, preferr...  8.23 us
    unnamed x34, local copies, waits for them, and re-layouts  5.43 us
  transfers between devices with their start and end apart: 9, of which 6 were waited for; matrix products, arithmetic and copies ran while one was open for 6% of the time, Pallas kernels for 0%

commit v1 on v0

--- a/solution.py
+++ b/solution.py
@@ -31,6 +31,21 @@
     result = result + spread[channels : 2 * channels]
     result = result + jnp.roll(spread[2 * channels : 3 * channels], 1, axis=3)
     return result
+
+
+def summed_over_devices(local_conv, local_down):
+    axes = ("gz", "gy")
+    count = lax.axis_size("gz") * lax.axis_size("gy")
+    flat = jnp.concatenate([local_conv.reshape(-1, 128), local_down.reshape(-1, 128)], axis=0)
+    rows = flat.shape[0]
+    share = -(-rows // (16 * count)) * 16
+    flat = jnp.pad(flat, ((0, share * count - rows), (0, 0))).astype(jnp.bfloat16)
+    terms = lax.all_to_all(flat.reshape(count, share, 128), axes, 0, 0, tiled=True)
+    mine = jnp.sum(terms.astype(jnp.float32), axis=0).astype(jnp.bfloat16)
+    copies = jnp.broadcast_to(mine[None], (count, share, 128))
+    sums = lax.all_to_all(copies, axes, 0, 0, tiled=True).reshape(count * share, 128).astype(jnp.float32)
+    split = local_conv.size // 128
+    return sums[:split].reshape(local_conv.shape), sums[split:rows].reshape(local_down.shape)
 
 
 def body(features, conv_weight, down_weight, cotangent):
@@ -96,7 +111,7 @@
     row_fold = plane_fold[:, :, 2 : row_count + 2]
     row_fold = row_fold.at[:, :, 0].add(plane_fold[:, :, 0])
     row_fold = row_fold.at[:, :, row_count - 1].add(plane_fold[:, :, row_count + 3])
-    summed_conv, summed_down = lax.psum((local_conv, local_down), ("gz", "gy"))
+    summed_conv, summed_down = summed_over_devices(local_conv, local_down)
     grad_conv = summed_conv * grad_scale
     grad_down = summed_down * grad_scale
     return (section_out, row_fold, grad_conv, grad_down)

time: 207 us -> 92.6 us (0.45)
  waiting for transfers between devices: 130 us -> 20.3 us
  between operations: 14.6 us -> 1.16 us
  starting transfers between devices: 14.5 us -> 24 us
  matrix products: 20.1 us -> 16.7 us
  local copies, waits for them, and re-layouts: 17.8 us -> 20.9 us
    psum x1 -> x0, waiting for transfers between devices: 126 us -> none  [body(): summed_conv, summed_down = lax.psum((local_conv, local_down), ('gz', 'gy'))]
    all_to_all x0 -> x2, waiting for transfers between devices: none -> 11.8 us  [the longest x1 11.8 us: summed_over_devices(): lax.all_to_all(copies, axes, 0, 0, tiled=True).reshape(count * share, 128)]
    all_to_all x0 -> x2, starting transfers between devices: none -> 9.5 us  [the longest x1 4.87 us: summed_over_devices(): lax.all_to_all(flat.reshape(count, share, 128), axes, 0, 0, tiled=True)]
    ppermute x4, waiting for transfers between devices: 2.93 us -> 8.47 us  [extended(): lax.ppermute(tail, axis, [(i, (i + 1) % count) for i in range(count)])]
    dot_general x9, matrix products: 8.38 us -> 3.4 us  [body(): jnp.einsum('ozyx,jzyx->oj', gate_grad, window, preferred_element_type=jnp...]
    unnamed x34 -> x20, local copies, waits for them, and re-layouts: 5.43 us -> 5.39 us
  transfers between devices with their start and end apart: 9 -> 10, of which waited for: 6 -> 4; matrix products, arithmetic and copies ran while one was open for 6% -> 14% of each run, Pallas kernels for 0% -> 0%
where the time goes in v1:
time: 92.6 us; the launch traced here: 92 us
  starting transfers between devices  24 us (26%)
  local copies, waits for them, and re-layouts  20.9 us (23%)
  waiting for transfers between devices  20.3 us (22%)
  matrix products  16.7 us (18%)
  other arithmetic  9.06 us (10%)
  between operations  1.16 us (1%)
    all_to_all x1, waiting for transfers between devices, summed_over_devices(): lax.all_to_all(copies, axes, 0, 0, tiled=True).reshape(count * share, 128)  11.8 us
    ppermute x4, starting transfers between devices, extended(): lax.ppermute(head, axis, [((i + 1) % count, i) for i in range(count)])  9.76 us
    ppermute x4, waiting for transfers between devices, extended(): lax.ppermute(tail, axis, [(i, (i + 1) % count) for i in range(count)])  8.47 us
    dot_general x9, matrix products, body(): jnp.einsum('oj,ozyx->jzyx', conv_weight[tap_z, tap_y], gate_grad, preferr...  8.21 us
    unnamed x20, local copies, waits for them, and re-layouts  5.39 us
    all_to_all x1, starting transfers between devices, summed_over_devices(): lax.all_to_all(flat.reshape(count, share, 128), axes, 0, 0, tiled=True)  4.87 us
    ppermute x4, starting transfers between devices, extended(): lax.ppermute(tail, axis, [(i, (i + 1) % count) for i in range(count)])  4.72 us
    all_to_all x1, starting transfers between devices, summed_over_devices(): lax.all_to_all(copies, axes, 0, 0, tiled=True).reshape(count * share, 128)  4.63 us
  transfers between devices with their start and end apart: 10, of which 4 were waited for; matrix products, arithmetic and copies ran while one was open for 14% of the time, Pallas kernels for 0%

profile of v1, /device:TPU:0, one launch (start us, length us, event | category | flops | bytes accessed | tf_op | source)
XLA Modules:
  0.0 92.0 jit_solution(10474009573412515948)
XLA Ops:
  0.6 1.0 %fusion.126 = (bf16[64,1,8,128]{3,2,1,0:T(8,128)(2,1)S(1)}, bf16[64,1,8,128]{3,2,1,0:T(8,128)(2,1)S(1)}) fusion(bf16[64,2,8,128]{3,2,1,0:T(8,128)(2,1)} %param.30), kind=kLoop, calls=%fused_computation.174 | loop fusion | bytes 524288 | tf_op jit(solution)/shard_map/slice | solution.py:12
  1.6 3.0 %collective-permute-start = (bf16[64,1,8,128]{3,0,2,1:T(8,128)(2,1)S(1)}, bf16[64,1,8,128]{3,0,2,1:T(8,128)(2,1)S(1)}, u32[]{:S(2)}, u32[]{:S(2)}) collective-permute-start(bf16[64,1,8,128]{3,0,2,1:T(8,128)(2,1)S(1)} %copy.164), channel_id=1, source_target_pairs={{0,4},{4,8},{8,12},{12,16},{16,20},{20,24},{24,28},{28,0},{1,5},{5... | collective-permute-start | bytes 393224 | tf_op jit(solution)/shard_map/ppermute | solution.py:16
  4.7 3.1 %collective-permute-start.1 = (bf16[64,1,8,128]{3,0,2,1:T(8,128)(2,1)S(1)}, bf16[64,1,8,128]{3,0,2,1:T(8,128)(2,1)S(1)}, u32[]{:S(2)}, u32[]{:S(2)}) collective-permute-start(bf16[64,1,8,128]{3,0,2,1:T(8,128)(2,1)S(1)} %copy.165), channel_id=1, source_target_pairs={{4,0},{8,4},{12,8},{16,12},{20,16},{24,20},{28,24},{0,28},{5,1},{9... | collective-permute-start | bytes 393224 | tf_op jit(solution)/shard_map/ppermute | solution.py:18
  7.8 1.0 %copy.74 = bf16[2,2,128,128]{2,3,1,0:T(8,128)(2,1)S(1)} copy(bf16[2,2,128,128]{3,2,1,0:T(8,128)(2,1)} %param.32) | data formatting | bytes 262144 | tf_op args[2]
  8.8 1.0 %copy.75 = bf16[128,1,256]{0,2,1:T(8,128)(2,1)S(1)} copy(bf16[128,1,256]{2,0,1:T(8,128)(2,1)} %param.33) | data formatting | bytes 131072 | tf_op args[3]
  10.1 0.6 fusion.127
  10.7 0.8 copy.76
  11.9 0.7 and_reduce_fusion
  12.9 1.7 %collective-permute-start.3 = (bf16[64,4,1,128]{3,0,2,1:T(8,128)(2,1)S(1)}, bf16[64,4,1,128]{3,0,2,1:T(8,128)(2,1)S(1)}, u32[]{:S(2)}, u32[]{:S(2)}) collective-permute-start(bf16[64,4,1,128]{3,0,2,1:T(8,128)(2,1)S(1)} %get-tuple-element.196), channel_id=1, source_target_pairs={{1,0},{2,1},{3,2},{0,3},{5,4},{6,5},{7,6},{4,7},{9,8},{10,9},{11,1... | collective-permute-start | bytes 196616 | tf_op jit(solution)/shard_map/ppermute | solution.py:18
  14.6 0.6 fusion.128
  15.2 1.4 %collective-permute-done.2 = bf16[64,4,1,128]{3,0,2,1:T(8,128)(2,1)S(1)} collective-permute-done((bf16[64,4,1,128]{3,0,2,1:T(8,128)(2,1)S(1)}, bf16[64,4,1,128]{3,0,2,1:T(8,128)(2,1)S(1)}, u32[]{:S(2)}, u32[]{:S(2)}) %collective-permute-start.2) | collective-permute-done | bytes 65568 | tf_op jit(solution)/shard_map/ppermute | solution.py:16
  17.3 1.2 %maximum_maximum_fusion = bf16[192,4,10,128]{3,0,2,1:T(8,128)(2,1)S(1)} fusion(bf16[64,4,10,1]{3,0,2,1:T(8,128)(2,1)S(1)} %get-tuple-element.190, bf16[64,4,10,127]{3,0,2,1:T(8,128)(2,1)S(1)} %get-tuple-element.192, bf16[64,4,1,128]{3,0,2,1:T(8,128)(2,1)S(1)} %collective-permute-done.3, bf16[64,4,8,128]{3,0,2,1:T(8,128)(2,1)S(1)} %constant_dynamic-update-slice_fusion, ...), kind=kLoop, calls=%fused_computation.1 | loop fusion | flops 13762560 | bytes 3932160 | tf_op jit(solution)/shard_map/concatenate | solution.py:26
  20.5 1.8 %fusion.121 = (bf16[192,2,8,128]{3,0,2,1:T(8,128)(2,1)S(1)}, bf16[192,2,8,128]{3,0,2,1:T(8,128)(2,1)S(1)}, bf16[192,2,8,128]{3,0,2,1:T(8,128)(2,1)S(1)}, bf16[19...) fusion(bf16[192,4,10,128]{3,0,2,1:T(8,128)(2,1)S(1)} %maximum_m, ...), kind=kLoop, calls=%fused_computation.169 | loop fusion | bytes 14155776 | tf_op jit(solution)/shard_map/slice | solution.py:61
  22.3 0.5 multiply_convert_fusion
  22.8 0.4 convolution_bitcast_fusion
  23.2 0.4 scatter-add.44
  23.7 1.8 %fusion.7 = f32[192,4,10,128]{3,0,2,1:T(8,128)S(1)} fusion(f32[192,4,10,128]{3,0,2,1:T(8,128)S(1)} %scatter-add.44, s32[]{:T(128)} %bitcast.45, s32[]{:T(128)} %bitcast.46, bf16[64,2,8,128]{3,0,2,1:T(8,128)(2,1)S(1)} %get-tuple-element.193, bf16[3,3,64,192]{3,2,1,0:T(8,128)(2,1)S(1)} %copy-done.2), kind=kOutput, calls=%fused_computation.16 | convolution fusion | flops 50724864 | bytes 3440648 | tf_op jit(solution)/shard_map/oj,ozyx->jzyx/dot_general | solution.py:99
  25.5 2.4 %fusion = f32[192,4,10,128]{3,0,2,1:T(8,128)S(1)} fusion(f32[192,4,10,128]{3,0,2,1:T(8,128)S(1)} %fusion.7, s32[]{:T(128)} %bitcast.50, s32[]{:T(128)} %bitcast.51, bf16[64,2,8,128]{3,0,2,1:T(8,128)(2,1)S(1)} %get-tuple-element.193, pred[]{:T(512)} %and_reduce_fusion, bf16[3,3,64,192]{3,2,1,0:T(8,128)(2,1)S(1)} %copy-done.2), kind=kOutput, calls=%fused_computation.2 | convolution fusion | flops 51118080 | bytes 3440649 | tf_op jit(solution)/shard_map/oj,ozyx->jzyx/dot_general | solution.py:99
  27.9 0.6 fusion.6
  28.5 0.6 fusion.5
  29.1 0.6 fusion.4
  29.7 0.6 fusion.3
  30.3 0.6 fusion.2
  30.9 0.6 fusion.1
  31.5 0.5 fusion.119
  32.0 1.4 %copy-done = f32[192,4,10,128]{3,0,2,1:T(8,128)} copy-done((f32[192,4,10,128]{3,0,2,1:T(8,128)}, f32[192,4,10,128]{3,0,2,1:T(8,128)S(1)}, u32[]{:S(2)}) %copy-start) | copy-done | bytes 3932184
  33.4 2.0 %fusion.120 = (f32[64,4,10,127]{3,0,2,1:T(8,128)}, f32[64,4,10,127]{3,0,2,1:T(8,128)}) fusion(f32[192,4,10,128]{3,0,2,1:T(8,128)S(1)} %fusion.1), kind=kLoop, calls=%fused_computation.168 | loop fusion | bytes 5201920 | tf_op jit(solution)/shard_map/jit(_roll_static)/slice | solution.py:32
  39.0 1.1 %reshape.556 = bf16[864,128]{1,0:T(8,128)(2,1)} reshape(bf16[3,3,64,192]{3,2,1,0:T(8,128)(2,1)S(1)} %pad_maximum_fusion.1) | data formatting | bytes 442368 | tf_op jit(solution)/shard_map/reshape | solution.py:39
  40.3 1.9 %fusion.19 = bf16[2,2,128,2,64]{2,4,3,1,0:T(8,128)(2,1)} fusion(bf16[128,4,64,1,1,1]{0,2,1,5,4,3:T(8,128)(2,1)} %bitcast.272, bf16[64,2,4,2,64,2]{0,5,4,3,2,1:T(2,128)(2,1)S(1)} %bitcast.267), kind=kOutput, calls=%fused_computation.34 | convolution fusion | flops 33619968 | bytes 458752 | tf_op jit(solution)/shard_map/oZYX,iZaYbXe->aboei/dot_general | solution.py:80
  42.2 1.1 %copy.123 = bf16[2,2,128,2,64]{4,3,2,1,0:T(2,128)(2,1)S(1)} copy(bf16[2,2,128,2,64]{2,4,3,1,0:T(8,128)(2,1)} %fusion.19) | data formatting | bytes 262144 | tf_op jit(solution)/shard_map/reshape;reshape | solution.py:39
  43.3 0.8 reshape.580
  44.1 1.8 %fusion.52 = bf16[1536,128]{1,0:T(8,128)(2,1)} fusion(bf16[512,128]{1,0:T(8,128)(2,1)} %reshape.580, bf16[864,128]{1,0:T(8,128)(2,1)} %reshape.556), kind=kLoop, calls=%fused_computation.83 | loop fusion | flops 1376256 | bytes 745472 | tf_op jit(solution)/shard_map/concatenate | solution.py:39
  45.9 4.9 %all-to-all-start = ((bf16[32,48,128]{2,1,0:T(8,128)(2,1)}), bf16[32,48,128]{2,1,0:T(8,128)(2,1)}, u32[]{:S(2)}, u32[]{:S(2)}) async-start(bf16[32,48,128]{2,1,0:T(8,128)(2,1)} %bitcast.108), calls=%async_computation | async-start | bytes 786432 | tf_op jit(solution)/shard_map/all_to_all | solution.py:43
  50.8 2.9 %fusion.9 = bf16[64,4,10,128]{3,0,2,1:T(8,128)(2,1)S(1)} fusion(f32[192,4,10,128]{3,0,2,1:T(8,128)} %copy-done, f32[64,4,10,1]{3,0,2,1:T(8,128)S(1)} %get-tuple-element.173, f32[64,4,10,127]{3,0,2,1:T(8,128)} %get-tuple-element.175, f32[64,4,10,127]{3,0,2,1:T(8,128)} %get-tuple-element.174, f32[64,4,10,1]{3,0,2,1:T(8,128)S(1)} %get-tuple-element.172), kind=kLoop, calls=%fused_computation.21 | loop fusion | flops 1638400 | bytes 4587520 | tf_op jit(solution)/shard_map/convert_element_type | solution.py:107
  53.6 1.6 %collective-permute-start.4 = (bf16[64,1,10,128]{3,0,2,1:T(8,128)(2,1)S(1)}, bf16[64,1,10,128]{3,0,2,1:T(8,128)(2,1)S(1)}, u32[]{:S(2)}, u32[]{:S(2)}) collective-permute-start(bf16[64,1,10,128]{3,0,2,1:T(8,128)(2,1)S(1)} %get-tuple-element.187), channel_id=1, source_target_pairs={{0,4},{4,8},{8,12},{12,16},{16,20},{20,24},{24,28},{28,0},{1,5},{5... | collective-permute-start | bytes 491528 | tf_op jit(solution)/shard_map/ppermute | solution.py:16
  55.2 3.2 %collective-permute-start.5 = (bf16[64,1,10,128]{3,0,2,1:T(8,128)(2,1)S(1)}, bf16[64,1,10,128]{3,0,2,1:T(8,128)(2,1)S(1)}, u32[]{:S(2)}, u32[]{:S(2)}) collective-permute-start(bf16[64,1,10,128]{3,0,2,1:T(8,128)(2,1)S(1)} %get-tuple-element.188), channel_id=1, source_target_pairs={{4,0},{8,4},{12,8},{16,12},{20,16},{24,20},{28,24},{0,28},{5,1},{9... | collective-permute-start | bytes 491528 | tf_op jit(solution)/shard_map/ppermute | solution.py:18
  58.4 1.5 %copy.73 = bf16[4,64,2,2,2,64]{1,0,5,4,3,2:T(4,128)(2,1)S(1)} copy(bf16[4,64,2,2,2,64]{5,4,1,3,0,2:T(2,128)(2,1)} %bitcast.268) | data formatting | bytes 524288 | tf_op jit(solution)/shard_map/aboei,iZaYbXe->oZYX/dot_general | solution.py:71
  60.3 5.8 %collective-permute-done.4 = bf16[64,1,10,128]{3,0,2,1:T(8,128)(2,1)S(1)} collective-permute-done((bf16[64,1,10,128]{3,0,2,1:T(8,128)(2,1)S(1)}, bf16[64,1,10,128]{3,0,2,1:T(8,128)(2,1)S(1)}, u32[]{:S(2)}, u32[]{:S(2)}) %collective-permute-start.4) | collective-permute-done | bytes 163872 | tf_op jit(solution)/shard_map/ppermute | solution.py:16
  66.2 1.7 %collective-permute-start.7 = (bf16[64,6,1,128]{3,0,2,1:T(8,128)(2,1)S(1)}, bf16[64,6,1,128]{3,0,2,1:T(8,128)(2,1)S(1)}, u32[]{:S(2)}, u32[]{:S(2)}) collective-permute-start(bf16[64,6,1,128]{3,0,2,1:T(8,128)(2,1)S(1)} %get-tuple-element.186), channel_id=1, source_target_pairs={{1,0},{2,1},{3,2},{0,3},{5,4},{6,5},{7,6},{4,7},{9,8},{10,9},{11,1... | collective-permute-start | bytes 294920 | tf_op jit(solution)/shard_map/ppermute | solution.py:18
  68.2 0.7 copy.99
  69.0 1.3 %collective-permute-done.6 = bf16[64,6,1,128]{3,0,2,1:T(8,128)(2,1)S(1)} collective-permute-done((bf16[64,6,1,128]{3,0,2,1:T(8,128)(2,1)S(1)}, bf16[64,6,1,128]{3,0,2,1:T(8,128)(2,1)S(1)}, u32[]{:S(2)}, u32[]{:S(2)}) %collective-permute-start.6) | collective-permute-done | bytes 98336 | tf_op jit(solution)/shard_map/ppermute | solution.py:16
  70.6 1.1 %reduce_sum.12 = bf16[48,128]{1,0:T(8,128)(2,1)S(1)} reduce(bf16[32,48,128]{2,1,0:T(8,128)(2,1)} %all-to-all-done, bf16[]{:T(256)} %constant.385.clone.1), dimensions={0}, to_apply=%region_1.2 | reduce | flops 190464 | bytes 405506 | tf_op jit(solution)/shard_map/reduce_sum | solution.py:44
  71.6 0.8 broadcast_in_dim.2
  72.4 4.6 %all-to-all-start.1 = ((bf16[32,48,128]{2,1,0:T(8,128)(2,1)}), bf16[32,48,128]{2,1,0:T(8,128)(2,1)S(1)}, u32[]{:S(2)}, u32[]{:S(2)}) async-start(bf16[32,48,128]{2,1,0:T(8,128)(2,1)} %broadcast_in_dim.2), calls=%async_computation.1 | async-start | bytes 786432 | tf_op jit(solution)/shard_map/all_to_all | solution.py:46
  77.3 1.1 %copy.100 = f32[64,2,8,128]{3,2,1,0:T(8,128)} copy(f32[64,2,8,128]{3,0,2,1:T(8,128)S(1)} %fusion.55) | data formatting | bytes 1048576
  78.4 11.8 %all-to-all-done.1 = bf16[32,48,128]{2,1,0:T(8,128)(2,1)S(1)} async-done(((bf16[32,48,128]{2,1,0:T(8,128)(2,1)}), bf16[32,48,128]{2,1,0:T(8,128)(2,1)S(1)}, u32[]{:S(2)}, u32[]{:S(2)}) %all-to-all-start.1) | async-done | bytes 393248 | tf_op jit(solution)/shard_map/all_to_all | solution.py:46
  90.4 1.0 %mul.38 = f32[3,3,64,192]{3,2,1,0:T(8,128)} reshape(f32[18,48,128]{2,1,0:T(8,128)S(1)} %slice_multiply_fusion) | data formatting | bytes 884736 | tf_op jit(solution)/shard_map/mul | solution.py:115
  91.3 0.7 slice_multiply_fusion.1
  (66 shorter events, 8.8 us)
Async XLA Ops:
  1.6 11.0 %collective-permute-start = (bf16[64,1,8,128]{3,0,2,1:T(8,128)(2,1)S(1)}, bf16[64,1,8,128]{3,0,2,1:T(8,128)(2,1)S(1)}, u32[]{:S(2)}, u32[]{:S(2)}) collective-permute-start(bf16[64,1,8,128]{3,0,2,1:T(8,128)(2,1)S(1)} %copy.164), channel_id=1, source_target_pairs={{0,4},{4,8},{8,12},{12,16},{16,20},{20,24},{24,28},{28,0},{1,5},{5... | collective-permute-start | bytes 393224 | tf_op jit(solution)/shard_map/ppermute | solution.py:16
  4.7 8.0 %collective-permute-start.1 = (bf16[64,1,8,128]{3,0,2,1:T(8,128)(2,1)S(1)}, bf16[64,1,8,128]{3,0,2,1:T(8,128)(2,1)S(1)}, u32[]{:S(2)}, u32[]{:S(2)}) collective-permute-start(bf16[64,1,8,128]{3,0,2,1:T(8,128)(2,1)S(1)} %copy.165), channel_id=1, source_target_pairs={{4,0},{8,4},{12,8},{16,12},{20,16},{24,20},{28,24},{0,28},{5,1},{9... | collective-permute-start | bytes 393224 | tf_op jit(solution)/shard_map/ppermute | solution.py:18
  9.8 1.8 %copy-start.4 = (bf16[128,1,256]{0,2,1:T(8,128)(2,1)}, bf16[128,1,256]{0,2,1:T(8,128)(2,1)S(1)}, u32[]{:S(2)}) copy-start(bf16[128,1,256]{0,2,1:T(8,128)(2,1)S(1)} %copy.75) | copy-start | bytes 196612
  10.1 1.8 %copy-start.5 = (s32[4]{0:T(128)S(1)}, s32[4]{0:T(128)}, u32[]{:S(2)}) copy-start(s32[4]{0:T(128)} %constant.381.clone.1) | copy-start | bytes 52
  10.7 1.9 %copy-start.3 = (bf16[64,2,8,128]{3,2,1,0:T(8,128)(2,1)S(1)}, bf16[64,2,8,128]{3,2,1,0:T(8,128)(2,1)}, u32[]{:S(2)}) copy-start(bf16[64,2,8,128]{3,2,1,0:T(8,128)(2,1)} %param.30) | copy-start | bytes 786436
  12.8 3.7 %collective-permute-start.2 = (bf16[64,4,1,128]{3,0,2,1:T(8,128)(2,1)S(1)}, bf16[64,4,1,128]{3,0,2,1:T(8,128)(2,1)S(1)}, u32[]{:S(2)}, u32[]{:S(2)}) collective-permute-start(bf16[64,4,1,128]{3,0,2,1:T(8,128)(2,1)S(1)} %get-tuple-element.195), channel_id=1, source_target_pairs={{0,1},{1,2},{2,3},{3,0},{4,5},{5,6},{6,7},{7,4},{8,9},{9,10},{10,1... | collective-permute-start | bytes 196616 | tf_op jit(solution)/shard_map/ppermute | solution.py:16
  12.9 3.7 %collective-permute-start.3 = (bf16[64,4,1,128]{3,0,2,1:T(8,128)(2,1)S(1)}, bf16[64,4,1,128]{3,0,2,1:T(8,128)(2,1)S(1)}, u32[]{:S(2)}, u32[]{:S(2)}) collective-permute-start(bf16[64,4,1,128]{3,0,2,1:T(8,128)(2,1)S(1)} %get-tuple-element.196), channel_id=1, source_target_pairs={{1,0},{2,1},{3,2},{0,3},{5,4},{6,5},{7,6},{4,7},{9,8},{10,9},{11,1... | collective-permute-start | bytes 196616 | tf_op jit(solution)/shard_map/ppermute | solution.py:18
  17.2 1.2 %copy-start.2 = (bf16[3,3,64,192]{3,2,1,0:T(8,128)(2,1)S(1)}, bf16[3,3,64,192]{3,2,1,0:T(8,128)(2,1)}, u32[]{:S(2)}) copy-start(bf16[3,3,64,192]{3,2,1,0:T(8,128)(2,1)} %param.31) | copy-start | bytes 663556
  31.5 1.9 %copy-start = (f32[192,4,10,128]{3,0,2,1:T(8,128)}, f32[192,4,10,128]{3,0,2,1:T(8,128)S(1)}, u32[]{:S(2)}) copy-start(f32[192,4,10,128]{3,0,2,1:T(8,128)S(1)} %fusion.1) | copy-start | bytes 11796484
  40.3 10.4 %copy-start.1 = (bf16[64,2,8,128]{0,3,2,1:T(8,128)(2,1)}, bf16[64,2,8,128]{0,3,2,1:T(8,128)(2,1)S(1)}, u32[]{:S(2)}) copy-start(bf16[64,2,8,128]{0,3,2,1:T(8,128)(2,1)S(1)} %copy.72) | copy-start | bytes 786436
  45.9 24.7 %all-to-all-start = ((bf16[32,48,128]{2,1,0:T(8,128)(2,1)}), bf16[32,48,128]{2,1,0:T(8,128)(2,1)}, u32[]{:S(2)}, u32[]{:S(2)}) async-start(bf16[32,48,128]{2,1,0:T(8,128)(2,1)} %bitcast.108), calls=%async_computation | async-start | bytes 786432 | tf_op jit(solution)/shard_map/all_to_all | solution.py:43
  53.6 12.5 %collective-permute-start.4 = (bf16[64,1,10,128]{3,0,2,1:T(8,128)(2,1)S(1)}, bf16[64,1,10,128]{3,0,2,1:T(8,128)(2,1)S(1)}, u32[]{:S(2)}, u32[]{:S(2)}) collective-permute-start(bf16[64,1,10,128]{3,0,2,1:T(8,128)(2,1)S(1)} %get-tuple-element.187), channel_id=1, source_target_pairs={{0,4},{4,8},{8,12},{12,16},{16,20},{20,24},{24,28},{28,0},{1,5},{5... | collective-permute-start | bytes 491528 | tf_op jit(solution)/shard_map/ppermute | solution.py:16
  55.2 10.9 %collective-permute-start.5 = (bf16[64,1,10,128]{3,0,2,1:T(8,128)(2,1)S(1)}, bf16[64,1,10,128]{3,0,2,1:T(8,128)(2,1)S(1)}, u32[]{:S(2)}, u32[]{:S(2)}) collective-permute-start(bf16[64,1,10,128]{3,0,2,1:T(8,128)(2,1)S(1)} %get-tuple-element.188), channel_id=1, source_target_pairs={{4,0},{8,4},{12,8},{16,12},{20,16},{24,20},{28,24},{0,28},{5,1},{9... | collective-permute-start | bytes 491528 | tf_op jit(solution)/shard_map/ppermute | solution.py:18
  66.1 4.1 %collective-permute-start.6 = (bf16[64,6,1,128]{3,0,2,1:T(8,128)(2,1)S(1)}, bf16[64,6,1,128]{3,0,2,1:T(8,128)(2,1)S(1)}, u32[]{:S(2)}, u32[]{:S(2)}) collective-permute-start(bf16[64,6,1,128]{3,0,2,1:T(8,128)(2,1)S(1)} %get-tuple-element.185), channel_id=1, source_target_pairs={{0,1},{1,2},{2,3},{3,0},{4,5},{5,6},{6,7},{7,4},{8,9},{9,10},{10,1... | collective-permute-start | bytes 294920 | tf_op jit(solution)/shard_map/ppermute | solution.py:16
  66.2 4.0 %collective-permute-start.7 = (bf16[64,6,1,128]{3,0,2,1:T(8,128)(2,1)S(1)}, bf16[64,6,1,128]{3,0,2,1:T(8,128)(2,1)S(1)}, u32[]{:S(2)}, u32[]{:S(2)}) collective-permute-start(bf16[64,6,1,128]{3,0,2,1:T(8,128)(2,1)S(1)} %get-tuple-element.186), channel_id=1, source_target_pairs={{1,0},{2,1},{3,2},{0,3},{5,4},{6,5},{7,6},{4,7},{9,8},{10,9},{11,1... | collective-permute-start | bytes 294920 | tf_op jit(solution)/shard_map/ppermute | solution.py:18
  72.4 17.8 %all-to-all-start.1 = ((bf16[32,48,128]{2,1,0:T(8,128)(2,1)}), bf16[32,48,128]{2,1,0:T(8,128)(2,1)S(1)}, u32[]{:S(2)}, u32[]{:S(2)}) async-start(bf16[32,48,128]{2,1,0:T(8,128)(2,1)} %broadcast_in_dim.2), calls=%async_computation.1 | async-start | bytes 786432 | tf_op jit(solution)/shard_map/all_to_all | solution.py:46

commit v2 on v0

v2 whole, which is shorter than its diff:
```python
import functools
import math

import jax
import jax.numpy as jnp
from jax import lax
from jax.experimental import pallas as pl
from jax.experimental.pallas import tpu as pltpu
from jax.sharding import PartitionSpec as P

F32 = jnp.float32
BF16 = jnp.bfloat16
PARAMS = pltpu.CompilerParams(vmem_limit_bytes=24 * 1024 * 1024)


def call(kernel, outs, scratch, flops, operands):
    moved = sum(x.size * x.dtype.itemsize for x in operands)
    moved += sum(math.prod(s) * jnp.dtype(d).itemsize for s, d in outs)
    return pl.pallas_call(
        kernel,
        out_shape=[jax.ShapeDtypeStruct(s, d) for s, d in outs],
        in_specs=[pl.BlockSpec(memory_space=pltpu.VMEM)] * len(operands),
        out_specs=[pl.BlockSpec(memory_space=pltpu.VMEM)] * len(outs),
        scratch_shapes=[pltpu.VMEM(s, d) for s, d in scratch],
        compiler_params=PARAMS,
        cost_estimate=pl.CostEstimate(flops=flops, bytes_accessed=moved, transcendentals=0),
    )(*operands)


def lines_kernel(f_ref, f0_ref, f1_ref, first_ref, last_ref, wide):
    channels, planes, rows, breadth = f_ref.shape
    wide[...] = f_ref[...].astype(F32).reshape(channels * planes * rows, breadth)
    for z, plane_ref in enumerate((f0_ref, f1_ref)):
        for y in range(rows):
            line = wide[pl.ds(z * rows + y, channels, stride=planes * rows), :].astype(BF16)
            plane_ref[y] = line
            if y == 0:
                first_ref[z] = line
            if y == rows - 1:
                last_ref[z] = line


def fill_columns(cols, planes, sides, corners, turn):
    rows, channels, _ = planes[0].shape

    def put(p, q, line):
        wide = line.astype(F32)
        cols[p, q, 0:channels] = pltpu.roll(wide, turn % 128, 1).astype(BF16)
        cols[p, q, channels : 2 * channels] = line
        cols[p, q, 2 * channels : 3 * channels] = pltpu.roll(wide, -turn % 128, 1).astype(BF16)

    for p in range(4):
        def step(y, carry, p=p):
            put(p, y + 1, planes[p][y])
            return carry

        lax.fori_loop(0, rows, step, 0, unroll=2)
    low, high = sides
    for z in range(2):
        put(z + 1, 0, low[z])
        put(z + 1, rows + 1, high[z])
    for p, corner in zip((0, 3), corners):
        put(p, 0, corner[0])
        put(p, rows + 1, corner[1])


def convolve(cols, w_ref, y):
    channels = w_ref.shape[0] // 3
    depth = w_ref.shape[1]
    breadth = cols.shape[3]

    def window(p):
        pair = [cols[p, pl.ds(y + s, 3)].reshape(depth, breadth) for s in range(2)]
        return jnp.concatenate(pair, axis=1)

    dot = functools.partial(jnp.dot, preferred_element_type=F32)
    acc = dot(w_ref[0 : 2 * channels], window(1)) + dot(w_ref[channels : 3 * channels], window(2))
    upper = acc[0:channels] + dot(w_ref[2 * channels : 3 * channels], window(3))
    lower = acc[channels : 2 * channels] + dot(w_ref[0:channels], window(0))
    return lower, upper


def forward_kernel(
    zlo, f0, f1, zhi, ylo, yhi, clo, chi, w_ref, dt_ref, cot_ref,
    cols, g0_ref, g1_ref, first_ref, last_ref, h_ref, up,
):
    rows, channels, breadth = f0.shape
    half = breadth // 2
    fill_columns(cols, (zlo, f0, f1, zhi), (ylo, yhi), (clo, chi), 1)
    source = lax.broadcasted_iota(jnp.int32, (breadth, 2 * breadth), 0)
    target = lax.broadcasted_iota(jnp.int32, (breadth, 2 * breadth), 1)
    spread = jnp.where(source == target // 2, 1.0, 0.0).astype(BF16)
    for pair in range(rows // 4):
        both = jnp.dot(cot_ref[:, pair * breadth : (pair + 1) * breadth], spread, preferred_element_type=F32)
        up[2 * pair] = both[:, 0:breadth].astype(BF16)
        up[2 * pair + 1] = both[:, breadth : 2 * breadth].astype(BF16)
    lane = lax.broadcasted_iota(jnp.int32, (channels, breadth), 1)
    even = lane % 2 == 0

    def step(t, carry):
        y = 2 * t
        preacts = convolve(cols, w_ref, y)
        for z, plane_ref in enumerate((g0_ref, g1_ref)):
            for b in range(2):
                preact = preacts[z][:, b * breadth : (b + 1) * breadth]
                sig = 1.0 / (1.0 + jnp.exp(-preact))
                h_ref[z, y + b] = (preact * sig).astype(BF16)
                terms = jnp.dot(dt_ref[z, b], up[t], preferred_element_type=F32)
                grad = jnp.where(even, terms[0:channels], terms[channels : 2 * channels])
                plane_ref[y + b] = (grad * sig * (1.0 + preact * (1.0 - sig))).astype(BF16)
        return carry

    lax.fori_loop(0, rows // 2, step, 0)
    for z, plane_ref in enumerate((g0_ref, g1_ref)):
        first_ref[z] = plane_ref[0]
        last_ref[z] = plane_ref[rows - 1]


def weight_grad_kernel(cols, g0_ref, g1_ref, h_ref, d_ref, cot_ref, out_ref, packed):
    rows, channels, breadth = g0_ref.shape
    across = (((1,), (1,)), ((), ()))
    flat = lambda ref, rows_of: jnp.concatenate([ref[r] for r in rows_of], axis=1)
    gates = jnp.concatenate([flat(g0_ref, range(rows)), flat(g1_ref, range(rows))], axis=0)
    lane = lax.broadcasted_iota(jnp.int32, (channels // 2, breadth), 1)
    for b in range(3):
        parts = []
        for p in range(4):
            window = jnp.concatenate([cols[p, y + b] for y in range(rows)], axis=1)
            lhs = gates[0:channels] if p == 0 else gates[channels:] if p == 3 else gates
            parts.append(lax.dot_general(lhs, window, across, preferred_element_type=F32))
        for a in range(3):
            low = parts[a][0:channels]
            high = parts[a + 1] if a == 2 else parts[a + 1][channels:]
            total = low + high
            base = (a * 3 + b) * 3 * channels // 2
            packed[base : base + channels] = total[:, 0:breadth].astype(BF16)
            rest = jnp.concatenate([total[:, breadth:], total[:, breadth:]], axis=1)
            mix = jnp.where(lane < channels, rest[0 : channels // 2], rest[channels // 2 :])
            packed[base + channels : base + 3 * channels // 2] = mix.astype(BF16)
    base = 9 * 3 * channels // 2
    source = lax.broadcasted_iota(jnp.int32, (2 * breadth, 2 * breadth), 0)
    target = lax.broadcasted_iota(jnp.int32, (2 * breadth, 2 * breadth), 1)
    wanted = 2 * (target % breadth) + target // breadth
    pick = jnp.where(source == wanted, 1.0, 0.0).astype(BF16)
    coarse = None
    for a in range(2):
        for b in range(2):
            pairs = []
            for pair in range(rows // 4):
                both = jnp.concatenate([h_ref[a, 4 * pair + b], h_ref[a, 4 * pair + 2 + b]], axis=1)
                pairs.append(jnp.dot(both, pick, preferred_element_type=F32).astype(BF16))
            hidden = jnp.concatenate(
                [jnp.concatenate([x[:, e * breadth : (e + 1) * breadth] for x in pairs], axis=1) for e in range(2)],
                axis=0,
            )
            term = jnp.dot(d_ref[a, b], hidden, preferred_element_type=F32)
            coarse = term if coarse is None else coarse + term
            down = lax.dot_general(cot_ref[...], hidden, across, preferred_element_type=F32)
            at = base + (2 * a + b) * d_ref.shape[2]
            packed[at : at + d_ref.shape[2]] = down.astype(BF16)
    out_ref[...] = coarse.astype(BF16)
    end = base + 4 * d_ref.shape[2]
    if end < packed.shape[0]:
        packed[end:] = jnp.zeros((packed.shape[0] - end, packed.shape[1]), BF16)


def field_kernel(zlo, g0, g1, zhi, ylo, yhi, clo, chi, w_ref, out_ref, cols):
    rows, channels, breadth = g0.shape
    fill_columns(cols, (zlo, g0, g1, zhi), (ylo, yhi), (clo, chi), 1)

    def step(t, carry):
        y = 2 * t
        lines = convolve(cols, w_ref, y)
        for z in range(2):
            for b in range(2):
                part = lines[z][:, b * breadth : (b + 1) * breadth]
                out_ref[pl.ds(z * rows + y + b, channels, stride=2 * rows), :] = part
        return carry

    lax.fori_loop(0, rows // 2, step, 0)


def unpack_kernel(sums_ref, conv_ref, down_ref, *, scale):
    channels = conv_ref.shape[2]
    for a in range(3):
        for b in range(3):
            base = (a * 3 + b) * 3 * channels // 2
            conv_ref[a, b, :, 0 : 2 * channels] = sums_ref[base : base + channels].astype(F32) * scale
            rest = sums_ref[base + channels : base + 3 * channels // 2].astype(F32) * scale
            conv_ref[a, b, 0 : channels // 2, 2 * channels :] = rest[:, 0:channels]
            conv_ref[a, b, channels // 2 :, 2 * channels :] = rest[:, channels:]
    base = 9 * 3 * channels // 2
    height = down_ref.shape[2]
    for a in range(2):
        for b in range(2):
            at = base + (2 * a + b) * height
            down_ref[a, b] = sums_ref[at : at + height].astype(F32) * scale


def shifted(cells, axis, step):
    count = lax.axis_size(axis)
    return lax.ppermute(cells, axis, [(i, (i + step) % count) for i in range(count)])


def halos(plane0, plane1, first, last):
    zlo, zhi = shifted(plane1, "gz", 1), shifted(plane0, "gz", -1)
    ylo, yhi = shifted(last, "gy", 1), shifted(first, "gy", -1)
    clo = shifted(jnp.stack([ylo[1], yhi[1]]), "gz", 1)
    chi = shifted(jnp.stack([ylo[0], yhi[0]]), "gz", -1)
    return zlo, zhi, ylo, yhi, clo, chi


def summed_over_devices(packed, count):
    axes = ("gz", "gy")
    share = packed.shape[0] // count
    terms = lax.all_to_all(packed.reshape(count, share, 128), axes, 0, 0, tiled=True)
    mine = jnp.sum(terms.astype(F32), axis=0).astype(BF16)
    copies = jnp.broadcast_to(mine[None], (count, share, 128))
    return lax.all_to_all(copies, axes, 0, 0, tiled=True).reshape(count * share, 128)


def body(features, conv_weight, down_weight, cotangent):
    channels, plane_count, row_count, breadth = features.shape
    out_channels = down_weight.shape[2]
    count = lax.axis_size("gz") * lax.axis_size("gy")
    grad_scale = 1.0 / math.sqrt(plane_count * row_count * breadth * count)
    depth = 9 * channels
    weight_fwd = conv_weight.transpose(0, 2, 1, 3).reshape(3 * channels, depth)
    taps = conv_weight.reshape(3, 3, channels, 3, channels)[::-1, ::-1, :, ::-1]
    weight_bwd = taps.transpose(0, 4, 1, 3, 2).reshape(3 * channels, depth)
    down_turned = down_weight.transpose(0, 1, 3, 2)
    cot = cotangent.reshape(out_channels, -1)
    plane = ((row_count, channels, breadth), BF16)
    edge = ((plane_count, channels, breadth), BF16)
    cols = ((4, row_count + 2, 3 * channels, breadth), BF16)
    conv_flops = 2 * 27 * channels * channels * plane_count * row_count * breadth

    f0, f1, first, last = call(
        lines_kernel, [plane, plane, edge, edge],
        [((channels * plane_count * row_count, breadth), F32)], 0, (features,),
    )
    zlo, zhi, ylo, yhi, clo, chi = halos(f0, f1, first, last)
    columns, g0, g1, gate_first, gate_last, hidden = call(
        forward_kernel,
        [cols, plane, plane, edge, edge, ((plane_count, row_count, channels, breadth), BF16)],
        [((row_count // 2, out_channels, breadth), BF16)],
        conv_flops,
        (zlo, f0, f1, zhi, ylo, yhi, clo, chi, weight_fwd, down_turned, cot),
    )
    gate_halos = halos(g0, g1, gate_first, gate_last)
    used = 27 * channels // 2 * channels // 64 + 4 * out_channels
    share = -(-used // (16 * count)) * 16
    section_out, packed = call(
        weight_grad_kernel,
        [((out_channels, cot.shape[1]), BF16), ((share * count, 128), BF16)],
        [], conv_flops, (columns, g0, g1, hidden, down_weight, cot),
    )
    sums = summed_over_devices(packed, count)
    zlo, zhi, ylo, yhi, clo, chi = gate_halos
    (field,) = call(
        field_kernel, [((channels * plane_count * row_count, breadth), F32)], [cols], conv_flops,
        (zlo, g0, g1, zhi, ylo, yhi, clo, chi, weight_bwd),
    )
    grad_conv, grad_down = call(
        functools.partial(unpack_kernel, scale=grad_scale),
        [(conv_weight.shape, F32), (down_weight.shape, F32)], [], 0, (sums,),
    )
    section_out = section_out.reshape(out_channels, plane_count // 2, -1)
    return (section_out, field.reshape(features.shape), grad_conv, grad_down)


def solution(mesh):
    return jax.shard_map(
        body,
        mesh=mesh,
        in_specs=(P(None, "gz", "gy", None), P(), P(), P(None, "gz", "gy")),
        out_specs=(P(None, "gz", "gy"), P(None, "gz", "gy", None), P(), P()),
        check_vma=False,
    )
```

time: 207 us -> 67.7 us (0.33)
  waiting for transfers between devices: 130 us -> 19.7 us
  matrix products: 20.1 us -> 0 us
  starting transfers between devices: 14.5 us -> 30.1 us
  between operations: 14.6 us -> 0.83 us
  local copies, waits for them, and re-layouts: 17.8 us -> 5.41 us
  Pallas kernels: 0 us -> 11.2 us
  other arithmetic: 9.84 us -> 0.1 us
    psum x1 -> x0, waiting for transfers between devices: 126 us -> none  [body(): summed_conv, summed_down = lax.psum((local_conv, local_down), ('gz', 'gy'))]
    dot_general x30 -> x0, matrix products: 20.1 us -> none  [the longest x9 8.38 us: body(): jnp.einsum('ozyx,jzyx->oj', gate_grad, window, preferred_element_type=jnp...]
    pallas_call x0 -> x5, Pallas kernels: none -> 11.2 us  [call(): pl.pallas_call(kernel, out_shape=[jax.ShapeDtypeStruct(s, d) for s, d in...]
    all_to_all x0 -> x2, waiting for transfers between devices: none -> 9.37 us  [the longest x1 9.37 us: summed_over_devices(): lax.all_to_all(packed.reshape(count, share, 128), axes, 0, 0, tiled=True)]
    ppermute x8 -> x12, starting transfers between devices: 14.5 us -> 23 us  [shifted(): lax.ppermute(cells, axis, [(i, (i + step) % count) for i in range(count)])]
    all_to_all x0 -> x2, starting transfers between devices: none -> 7.05 us  [the longest x1 4.45 us: summed_over_devices(): lax.all_to_all(packed.reshape(count, share, 128), axes, 0, 0, tiled=True)]
    slice x10 -> x4, local copies, waits for them, and re-layouts: 5.92 us -> 0.02 us  [halos(): chi = shifted(jnp.stack([ylo[0], yhi[0]]), 'gz', -1)]
    ppermute x8 -> x12, waiting for transfers between devices: 4.48 us -> 10.4 us  [shifted(): lax.ppermute(cells, axis, [(i, (i + step) % count) for i in range(count)])]
  transfers between devices with their start and end apart: 9 -> 14, of which waited for: 6 -> 3; matrix products, arithmetic and copies ran while one was open for 6% -> 7% of each run, Pallas kernels for 0% -> 6%
where the time goes in v2:
time: 67.7 us; the launch traced here: 67.3 us
  starting transfers between devices  30.1 us (44%)
  waiting for transfers between devices  19.7 us (29%)
  Pallas kernels  11.2 us (17%)
  local copies, waits for them, and re-layouts  5.41 us (8%)
  between operations  0.83 us (1%)
    ppermute x12, starting transfers between devices, shifted(): lax.ppermute(cells, axis, [(i, (i + step) % count) for i in range(count)])  23 us
    pallas_call x5, Pallas kernels, call(): pl.pallas_call(kernel, out_shape=[jax.ShapeDtypeStruct(s, d) for s, d in...  11.2 us
    ppermute x12, waiting for transfers between devices, shifted(): lax.ppermute(cells, axis, [(i, (i + step) % count) for i in range(count)])  10.4 us
    all_to_all x1, waiting for transfers between devices, summed_over_devices(): lax.all_to_all(packed.reshape(count, share, 128), axes, 0, 0, tiled=True)  9.37 us
    all_to_all x1, starting transfers between devices, summed_over_devices(): lax.all_to_all(packed.reshape(count, share, 128), axes, 0, 0, tiled=True)  4.45 us
    all_to_all x1, starting transfers between devices, summed_over_devices(): lax.all_to_all(copies, axes, 0, 0, tiled=True).reshape(count * share, 128)  2.6 us
    unnamed x10, local copies, waits for them, and re-layouts  2.28 us
  transfers between devices with their start and end apart: 14, of which 3 were waited for; matrix products, arithmetic and copies ran while one was open for 7% of the time, Pallas kernels for 6%

profile of v2, /device:TPU:0, one launch (start us, length us, event | category | flops | bytes accessed | tf_op | source)
XLA Modules:
  0.0 67.3 jit_solution(16527764892672451409)
XLA Ops:
  0.6 0.0 copy-start
  0.6 0.0 copy-start.1
  0.7 1.0 %copy-done.1 = bf16[64,2,8,128]{3,2,1,0:T(8,128)(2,1)S(1)} copy-done((bf16[64,2,8,128]{3,2,1,0:T(8,128)(2,1)S(1)}, bf16[64,2,8,128]{3,2,1,0:T(8,128)(2,1)}, u32[]{:S(2)}) %copy-start.1) | copy-done | bytes 262168
  1.6 0.2 shard_map.75
  1.8 2.4 %collective-permute-start.3 = (bf16[2,64,128]{2,1,0:T(8,128)(2,1)S(1)}, bf16[2,64,128]{2,1,0:T(8,128)(2,1)S(1)}, u32[]{:S(2)}, u32[]{:S(2)}) collective-permute-start(bf16[2,64,128]{2,1,0:T(8,128)(2,1)S(1)} %get-tuple-element.21), channel_id=1, source_target_pairs={{0,3},{1,0},{2,1},{3,2},{4,7},{5,4},{6,5},{7,6},{8,11},{9,8},{10,9... | collective-permute-start | bytes 98312 | tf_op jit(solution)/shard_map/ppermute | solution.py:202
  4.3 1.5 %collective-permute-start = (bf16[8,64,128]{2,1,0:T(8,128)(2,1)S(1)}, bf16[8,64,128]{2,1,0:T(8,128)(2,1)S(1)}, u32[]{:S(2)}, u32[]{:S(2)}) collective-permute-start(bf16[8,64,128]{2,1,0:T(8,128)(2,1)S(1)} %get-tuple-element.18.f1), channel_id=1, source_target_pairs={{0,4},{4,8},{8,12},{12,16},{16,20},{20,24},{24,28},{28,0},{1,5},{5... | collective-permute-start | bytes 393224 | tf_op jit(solution)/shard_map/ppermute | solution.py:202
  5.8 3.2 %collective-permute-start.1 = (bf16[8,64,128]{2,1,0:T(8,128)(2,1)S(1)}, bf16[8,64,128]{2,1,0:T(8,128)(2,1)S(1)}, u32[]{:S(2)}, u32[]{:S(2)}) collective-permute-start(bf16[8,64,128]{2,1,0:T(8,128)(2,1)S(1)} %get-tuple-element.19.f0), channel_id=1, source_target_pairs={{0,28},{4,0},{8,4},{12,8},{16,12},{20,16},{24,20},{28,24},{1,29},{... | collective-permute-start | bytes 393224 | tf_op jit(solution)/shard_map/ppermute | solution.py:202
  9.0 0.0 collective-permute-start.2
  9.0 0.0 collective-permute-done.3.yhi
  9.0 3.3 %collective-permute-done.2.ylo = bf16[2,64,128]{2,1,0:T(8,128)(2,1)S(1)} collective-permute-done((bf16[2,64,128]{2,1,0:T(8,128)(2,1)S(1)}, bf16[2,64,128]{2,1,0:T(8,128)(2,1)S(1)}, u32[]{:S(2)}, u32[]{:S(2)}) %collective-permute-start.2) | collective-permute-done | bytes 32800 | tf_op jit(solution)/shard_map/ppermute | solution.py:202
  12.3 0.1 collective-permute-start.4
  12.4 4.7 %collective-permute-start.5 = (bf16[2,64,128]{2,1,0:T(8,128)(2,1)S(1)}, bf16[2,64,128]{2,1,0:T(8,128)(2,1)S(1)}, u32[]{:S(2)}, u32[]{:S(2)}) collective-permute-start(bf16[2,64,128]{2,1,0:T(8,128)(2,1)S(1)} %pad_maximum_fusion.1), channel_id=1, source_target_pairs={{0,28},{4,0},{8,4},{12,8},{16,12},{20,16},{24,20},{28,24},{1,29},{... | collective-permute-start | bytes 98312 | tf_op jit(solution)/shard_map/ppermute | solution.py:202
  17.1 1.2 %copy.11 = bf16[3,64,3,192]{3,2,1,0:T(4,128)(2,1)S(1)} copy(bf16[3,64,3,192]{3,1,2,0:T(8,128)(2,1)} %bitcast.15) | data formatting | bytes 442368 | tf_op jit(solution)/shard_map/transpose | solution.py:228
  18.3 0.3 reshape.33.w_ref
  18.6 1.0 %copy.12 = bf16[2,2,128,128]{2,3,1,0:T(8,128)(2,1)S(1)} copy(bf16[2,2,128,128]{3,2,1,0:T(8,128)(2,1)} %d_ref.1) | data formatting | bytes 262144 | tf_op args[2]
  19.7 0.0 collective-permute-done.4.clo
  19.7 0.0 collective-permute-done.5.chi
  19.7 0.0 collective-permute-done.zlo
  19.7 0.0 collective-permute-done.1.zhi
  19.7 0.0 copy-done.2
  19.7 3.2 %shard_map.76 = (bf16[4,10,192,128]{3,2,1,0:T(8,128)(2,1)S(1)}, bf16[8,64,128]{2,1,0:T(8,128)(2,1)S(1)}, bf16[8,64,128]{2,1,0:T(8,128)(2,1)S(1)}, bf16[2,64,128]...) custom-call(bf16[8,64,128]{2,1,0:T(8,128)(2,1)S(1)} %collective-permute-done.zlo, ...), custom_call_target="tpu_custom_call" | custom-call | flops 452984832 | bytes 3629056 | tf_op jit(solution)/shard_map/pallas_call | solution.py:19
  22.9 0.0 copy-start.3
  22.9 0.0 copy-done
  22.9 3.1 %shard_map.77 = (bf16[128,256]{1,0:T(8,128)(2,1)}, bf16[1536,128]{1,0:T(8,128)(2,1)}) custom-call(bf16[4,10,192,128]{3,2,1,0:T(8,128)(2,1)S(1)} %get-tuple-element.22.cols, bf16[8,64,128]{2,1,0:T(8,128)(2,1)S(1)} %get-tuple-element.23.g0_ref.g0, bf16[8,64,128]{2,1,0:T(8,128)(2,1)S(1)} %get-tuple-element.24.g1_ref.g1, ...), custom_call_target="tpu_custom_call" | custom-call | flops 452984832 | bytes 3145728 | tf_op jit(solution)/shard_map/pallas_call | solution.py:19
  26.0 4.5 %all-to-all-start = ((bf16[32,48,128]{2,1,0:T(8,128)(2,1)}), bf16[32,48,128]{2,1,0:T(8,128)(2,1)S(1)}, u32[]{:S(2)}, u32[]{:S(2)}) async-start(bf16[32,48,128]{2,1,0:T(8,128)(2,1)} %bitcast.7), calls=%async_computation | async-start | bytes 786432 | tf_op jit(solution)/shard_map/all_to_all | solution.py:216
  30.4 1.6 %collective-permute-start.9 = (bf16[2,64,128]{2,1,0:T(8,128)(2,1)S(1)}, bf16[2,64,128]{2,1,0:T(8,128)(2,1)S(1)}, u32[]{:S(2)}, u32[]{:S(2)}) collective-permute-start(bf16[2,64,128]{2,1,0:T(8,128)(2,1)S(1)} %get-tuple-element.28), channel_id=1, source_target_pairs={{0,3},{1,0},{2,1},{3,2},{4,7},{5,4},{6,5},{7,6},{8,11},{9,8},{10,9... | collective-permute-start | bytes 98312 | tf_op jit(solution)/shard_map/ppermute | solution.py:202
  32.0 0.0 copy-done.3
  32.0 0.3 copy.13
  32.3 1.5 %collective-permute-start.6 = (bf16[8,64,128]{2,1,0:T(8,128)(2,1)S(1)}, bf16[8,64,128]{2,1,0:T(8,128)(2,1)S(1)}, u32[]{:S(2)}, u32[]{:S(2)}) collective-permute-start(bf16[8,64,128]{2,1,0:T(8,128)(2,1)S(1)} %get-tuple-element.24.g1_ref.g1), channel_id=1, source_target_pairs={{0,4},{4,8},{8,12},{12,16},{16,20},{20,24},{24,28},{28,0},{1,5},{5... | collective-permute-start | bytes 393224 | tf_op jit(solution)/shard_map/ppermute | solution.py:202
  33.8 3.3 %collective-permute-start.7 = (bf16[8,64,128]{2,1,0:T(8,128)(2,1)S(1)}, bf16[8,64,128]{2,1,0:T(8,128)(2,1)S(1)}, u32[]{:S(2)}, u32[]{:S(2)}) collective-permute-start(bf16[8,64,128]{2,1,0:T(8,128)(2,1)S(1)} %get-tuple-element.23.g0_ref.g0), channel_id=1, source_target_pairs={{0,28},{4,0},{8,4},{12,8},{16,12},{20,16},{24,20},{28,24},{1,29},{... | collective-permute-start | bytes 393224 | tf_op jit(solution)/shard_map/ppermute | solution.py:202
  37.1 0.0 collective-permute-start.8
  37.1 9.4 %all-to-all-done = bf16[32,48,128]{2,1,0:T(8,128)(2,1)S(1)} async-done(((bf16[32,48,128]{2,1,0:T(8,128)(2,1)}), bf16[32,48,128]{2,1,0:T(8,128)(2,1)S(1)}, u32[]{:S(2)}, u32[]{:S(2)}) %all-to-all-start) | async-done | bytes 393248 | tf_op jit(solution)/shard_map/all_to_all | solution.py:216
  46.4 0.1 reduce_sum.12
  46.5 0.8 %broadcast_in_dim.2 = bf16[32,48,128]{2,1,0:T(8,128)(2,1)} broadcast(bf16[48,128]{1,0:T(8,128)(2,1)S(1)} %reduce_sum.12), dimensions={1,2} | broadcast | bytes 405504 | tf_op jit(solution)/shard_map/broadcast_in_dim | solution.py:218
  47.3 2.6 %all-to-all-start.1 = ((bf16[32,48,128]{2,1,0:T(8,128)(2,1)}), bf16[32,48,128]{2,1,0:T(8,128)(2,1)S(1)}, u32[]{:S(2)}, u32[]{:S(2)}) async-start(bf16[32,48,128]{2,1,0:T(8,128)(2,1)} %broadcast_in_dim.2), calls=%async_computation.1 | async-start | bytes 786432 | tf_op jit(solution)/shard_map/all_to_all | solution.py:219
  49.9 0.0 collective-permute-done.9.yhi
  49.9 0.0 collective-permute-done.8.ylo
  50.0 1.7 %collective-permute-start.10 = (bf16[2,64,128]{2,1,0:T(8,128)(2,1)S(1)}, bf16[2,64,128]{2,1,0:T(8,128)(2,1)S(1)}, u32[]{:S(2)}, u32[]{:S(2)}) collective-permute-start(bf16[2,64,128]{2,1,0:T(8,128)(2,1)S(1)} %pad_maximum_fusion.2), channel_id=1, source_target_pairs={{0,4},{4,8},{8,12},{12,16},{16,20},{20,24},{24,28},{28,0},{1,5},{5... | collective-permute-start | bytes 98312 | tf_op jit(solution)/shard_map/ppermute | solution.py:202
  51.7 3.1 %collective-permute-start.11 = (bf16[2,64,128]{2,1,0:T(8,128)(2,1)S(1)}, bf16[2,64,128]{2,1,0:T(8,128)(2,1)S(1)}, u32[]{:S(2)}, u32[]{:S(2)}) collective-permute-start(bf16[2,64,128]{2,1,0:T(8,128)(2,1)S(1)} %pad_maximum_fusion.3), channel_id=1, source_target_pairs={{0,28},{4,0},{8,4},{12,8},{16,12},{20,16},{24,20},{28,24},{1,29},{... | collective-permute-start | bytes 98312 | tf_op jit(solution)/shard_map/ppermute | solution.py:202
  54.8 0.4 copy.14
  55.2 0.4 reshape.37.w_ref
  55.6 7.0 %collective-permute-done.10.clo = bf16[2,64,128]{2,1,0:T(8,128)(2,1)S(1)} collective-permute-done((bf16[2,64,128]{2,1,0:T(8,128)(2,1)S(1)}, bf16[2,64,128]{2,1,0:T(8,128)(2,1)S(1)}, u32[]{:S(2)}, u32[]{:S(2)}) %collective-permute-start.10) | collective-permute-done | bytes 32800 | tf_op jit(solution)/shard_map/ppermute | solution.py:202
  62.6 0.0 collective-permute-done.11.chi
  62.6 0.0 collective-permute-done.6.zlo
  62.6 0.0 collective-permute-done.7.zhi
  62.6 3.8 %shard_map.78 = f32[1024,128]{1,0:T(8,128)} custom-call(bf16[8,64,128]{2,1,0:T(8,128)(2,1)S(1)} %collective-permute-done.6.zlo, bf16[8,64,128]{2,1,0:T(8,128)(2,1)S(1)} %get-tuple-element.23.g0_ref.g0, bf16[8,64,128]{2,1,0:T(8,128)(2,1)S(1)} %get-tuple-element.24.g1_ref.g1, bf16[8,64,128]{2,1,0:T(8,128)(2,1)S(1)} %collective-permute-done.7.zhi, ...), custom_call_target="tpu_custom_call" | custom-call | flops 452984832 | bytes 1400832 | tf_op jit(solution)/shard_map/pallas_call | solution.py:19
  66.4 0.0 all-to-all-done.1
  66.4 1.0 %shard_map.79 = (f32[3,3,64,192]{3,2,1,0:T(8,128)}, f32[2,2,128,128]{3,2,1,0:T(8,128)}) custom-call(bf16[1536,128]{1,0:T(8,128)(2,1)S(1)} %bitcast.10), custom_call_target="tpu_custom_call" | custom-call | bytes 1097728 | tf_op jit(solution)/shard_map/pallas_call | solution.py:19
  (10 shorter events, 0.1 us)
Async XLA Ops:
  0.6 22.3 %copy-start = (bf16[2,2,128,128]{3,2,1,0:T(8,128)(2,1)S(1)}, bf16[2,2,128,128]{3,2,1,0:T(8,128)(2,1)}, u32[]{:S(2)}) copy-start(bf16[2,2,128,128]{3,2,1,0:T(8,128)(2,1)} %d_ref.1) | copy-start | bytes 393220
  0.6 1.0 %copy-start.1 = (bf16[64,2,8,128]{3,2,1,0:T(8,128)(2,1)S(1)}, bf16[64,2,8,128]{3,2,1,0:T(8,128)(2,1)}, u32[]{:S(2)}) copy-start(bf16[64,2,8,128]{3,2,1,0:T(8,128)(2,1)} %f_ref.1) | copy-start | bytes 786436
  1.6 18.1 %copy-start.2 = (bf16[128,1,256]{2,0,1:T(8,128)(2,1)S(1)}, bf16[128,1,256]{2,0,1:T(8,128)(2,1)}, u32[]{:S(2)}) copy-start(bf16[128,1,256]{2,0,1:T(8,128)(2,1)} %param.7) | copy-start | bytes 196612
  1.8 7.2 %collective-permute-start.3 = (bf16[2,64,128]{2,1,0:T(8,128)(2,1)S(1)}, bf16[2,64,128]{2,1,0:T(8,128)(2,1)S(1)}, u32[]{:S(2)}, u32[]{:S(2)}) collective-permute-start(bf16[2,64,128]{2,1,0:T(8,128)(2,1)S(1)} %get-tuple-element.21), channel_id=1, source_target_pairs={{0,3},{1,0},{2,1},{3,2},{4,7},{5,4},{6,5},{7,6},{8,11},{9,8},{10,9... | collective-permute-start | bytes 98312 | tf_op jit(solution)/shard_map/ppermute | solution.py:202
  4.3 15.4 %collective-permute-start = (bf16[8,64,128]{2,1,0:T(8,128)(2,1)S(1)}, bf16[8,64,128]{2,1,0:T(8,128)(2,1)S(1)}, u32[]{:S(2)}, u32[]{:S(2)}) collective-permute-start(bf16[8,64,128]{2,1,0:T(8,128)(2,1)S(1)} %get-tuple-element.18.f1), channel_id=1, source_target_pairs={{0,4},{4,8},{8,12},{12,16},{16,20},{20,24},{24,28},{28,0},{1,5},{5... | collective-permute-start | bytes 393224 | tf_op jit(solution)/shard_map/ppermute | solution.py:202
  5.8 13.9 %collective-permute-start.1 = (bf16[8,64,128]{2,1,0:T(8,128)(2,1)S(1)}, bf16[8,64,128]{2,1,0:T(8,128)(2,1)S(1)}, u32[]{:S(2)}, u32[]{:S(2)}) collective-permute-start(bf16[8,64,128]{2,1,0:T(8,128)(2,1)S(1)} %get-tuple-element.19.f0), channel_id=1, source_target_pairs={{0,28},{4,0},{8,4},{12,8},{16,12},{20,16},{24,20},{28,24},{1,29},{... | collective-permute-start | bytes 393224 | tf_op jit(solution)/shard_map/ppermute | solution.py:202
  9.0 3.3 %collective-permute-start.2 = (bf16[2,64,128]{2,1,0:T(8,128)(2,1)S(1)}, bf16[2,64,128]{2,1,0:T(8,128)(2,1)S(1)}, u32[]{:S(2)}, u32[]{:S(2)}) collective-permute-start(bf16[2,64,128]{2,1,0:T(8,128)(2,1)S(1)} %get-tuple-element.20), channel_id=1, source_target_pairs={{0,1},{1,2},{2,3},{3,0},{4,5},{5,6},{6,7},{7,4},{8,9},{9,10},{10,1... | collective-permute-start | bytes 98312 | tf_op jit(solution)/shard_map/ppermute | solution.py:202
  12.3 7.3 %collective-permute-start.4 = (bf16[2,64,128]{2,1,0:T(8,128)(2,1)S(1)}, bf16[2,64,128]{2,1,0:T(8,128)(2,1)S(1)}, u32[]{:S(2)}, u32[]{:S(2)}) collective-permute-start(bf16[2,64,128]{2,1,0:T(8,128)(2,1)S(1)} %pad_maximum_fusion), channel_id=1, source_target_pairs={{0,4},{4,8},{8,12},{12,16},{16,20},{20,24},{24,28},{28,0},{1,5},{5... | collective-permute-start | bytes 98312 | tf_op jit(solution)/shard_map/ppermute | solution.py:202
  12.4 7.3 %collective-permute-start.5 = (bf16[2,64,128]{2,1,0:T(8,128)(2,1)S(1)}, bf16[2,64,128]{2,1,0:T(8,128)(2,1)S(1)}, u32[]{:S(2)}, u32[]{:S(2)}) collective-permute-start(bf16[2,64,128]{2,1,0:T(8,128)(2,1)S(1)} %pad_maximum_fusion.1), channel_id=1, source_target_pairs={{0,28},{4,0},{8,4},{12,8},{16,12},{20,16},{24,20},{28,24},{1,29},{... | collective-permute-start | bytes 98312 | tf_op jit(solution)/shard_map/ppermute | solution.py:202
  22.9 9.1 %copy-start.3 = (bf16[3,3,64,192]{3,2,1,0:T(8,128)(2,1)S(1)}, bf16[3,3,64,192]{3,2,1,0:T(8,128)(2,1)}, u32[]{:S(2)}) copy-start(bf16[3,3,64,192]{3,2,1,0:T(8,128)(2,1)} %param.5) | copy-start | bytes 663556
  26.0 20.4 %all-to-all-start = ((bf16[32,48,128]{2,1,0:T(8,128)(2,1)}), bf16[32,48,128]{2,1,0:T(8,128)(2,1)S(1)}, u32[]{:S(2)}, u32[]{:S(2)}) async-start(bf16[32,48,128]{2,1,0:T(8,128)(2,1)} %bitcast.7), calls=%async_computation | async-start | bytes 786432 | tf_op jit(solution)/shard_map/all_to_all | solution.py:216
  30.4 19.5 %collective-permute-start.9 = (bf16[2,64,128]{2,1,0:T(8,128)(2,1)S(1)}, bf16[2,64,128]{2,1,0:T(8,128)(2,1)S(1)}, u32[]{:S(2)}, u32[]{:S(2)}) collective-permute-start(bf16[2,64,128]{2,1,0:T(8,128)(2,1)S(1)} %get-tuple-element.28), channel_id=1, source_target_pairs={{0,3},{1,0},{2,1},{3,2},{4,7},{5,4},{6,5},{7,6},{8,11},{9,8},{10,9... | collective-permute-start | bytes 98312 | tf_op jit(solution)/shard_map/ppermute | solution.py:202
  32.3 30.3 %collective-permute-start.6 = (bf16[8,64,128]{2,1,0:T(8,128)(2,1)S(1)}, bf16[8,64,128]{2,1,0:T(8,128)(2,1)S(1)}, u32[]{:S(2)}, u32[]{:S(2)}) collective-permute-start(bf16[8,64,128]{2,1,0:T(8,128)(2,1)S(1)} %get-tuple-element.24.g1_ref.g1), channel_id=1, source_target_pairs={{0,4},{4,8},{8,12},{12,16},{16,20},{20,24},{24,28},{28,0},{1,5},{5... | collective-permute-start | bytes 393224 | tf_op jit(solution)/shard_map/ppermute | solution.py:202
  33.8 28.8 %collective-permute-start.7 = (bf16[8,64,128]{2,1,0:T(8,128)(2,1)S(1)}, bf16[8,64,128]{2,1,0:T(8,128)(2,1)S(1)}, u32[]{:S(2)}, u32[]{:S(2)}) collective-permute-start(bf16[8,64,128]{2,1,0:T(8,128)(2,1)S(1)} %get-tuple-element.23.g0_ref.g0), channel_id=1, source_target_pairs={{0,28},{4,0},{8,4},{12,8},{16,12},{20,16},{24,20},{28,24},{1,29},{... | collective-permute-start | bytes 393224 | tf_op jit(solution)/shard_map/ppermute | solution.py:202
  37.1 12.9 %collective-permute-start.8 = (bf16[2,64,128]{2,1,0:T(8,128)(2,1)S(1)}, bf16[2,64,128]{2,1,0:T(8,128)(2,1)S(1)}, u32[]{:S(2)}, u32[]{:S(2)}) collective-permute-start(bf16[2,64,128]{2,1,0:T(8,128)(2,1)S(1)} %get-tuple-element.27), channel_id=1, source_target_pairs={{0,1},{1,2},{2,3},{3,0},{4,5},{5,6},{6,7},{7,4},{8,9},{9,10},{10,1... | collective-permute-start | bytes 98312 | tf_op jit(solution)/shard_map/ppermute | solution.py:202
  47.3 19.1 %all-to-all-start.1 = ((bf16[32,48,128]{2,1,0:T(8,128)(2,1)}), bf16[32,48,128]{2,1,0:T(8,128)(2,1)S(1)}, u32[]{:S(2)}, u32[]{:S(2)}) async-start(bf16[32,48,128]{2,1,0:T(8,128)(2,1)} %broadcast_in_dim.2), calls=%async_computation.1 | async-start | bytes 786432 | tf_op jit(solution)/shard_map/all_to_all | solution.py:219
  50.0 12.6 %collective-permute-start.10 = (bf16[2,64,128]{2,1,0:T(8,128)(2,1)S(1)}, bf16[2,64,128]{2,1,0:T(8,128)(2,1)S(1)}, u32[]{:S(2)}, u32[]{:S(2)}) collective-permute-start(bf16[2,64,128]{2,1,0:T(8,128)(2,1)S(1)} %pad_maximum_fusion.2), channel_id=1, source_target_pairs={{0,4},{4,8},{8,12},{12,16},{16,20},{20,24},{24,28},{28,0},{1,5},{5... | collective-permute-start | bytes 98312 | tf_op jit(solution)/shard_map/ppermute | solution.py:202
  51.7 10.9 %collective-permute-start.11 = (bf16[2,64,128]{2,1,0:T(8,128)(2,1)S(1)}, bf16[2,64,128]{2,1,0:T(8,128)(2,1)S(1)}, u32[]{:S(2)}, u32[]{:S(2)}) collective-permute-start(bf16[2,64,128]{2,1,0:T(8,128)(2,1)S(1)} %pad_maximum_fusion.3), channel_id=1, source_target_pairs={{0,28},{4,0},{8,4},{12,8},{16,12},{20,16},{24,20},{28,24},{1,29},{... | collective-permute-start | bytes 98312 | tf_op jit(solution)/shard_map/ppermute | solution.py:202

commit v3 on v2

v3 whole, which is shorter than its diff:
```python
import functools
import math

import jax
import jax.numpy as jnp
from jax import lax
from jax.experimental import pallas as pl
from jax.experimental.pallas import tpu as pltpu
from jax.sharding import PartitionSpec as P

F32 = jnp.float32
BF16 = jnp.bfloat16
PARAMS = pltpu.CompilerParams(vmem_limit_bytes=24 * 1024 * 1024)


def call(kernel, outs, scratch, flops, scalars, operands):
    moved = sum(x.size * x.dtype.itemsize for x in operands)
    moved += sum(math.prod(s) * jnp.dtype(d).itemsize for s, d in outs)
    vmem = pl.BlockSpec(memory_space=pltpu.VMEM)
    return pl.pallas_call(
        kernel,
        out_shape=[jax.ShapeDtypeStruct(s, d) for s, d in outs],
        in_specs=[pl.BlockSpec(memory_space=pltpu.SMEM)] * len(scalars) + [vmem] * len(operands),
        out_specs=[vmem] * len(outs),
        scratch_shapes=[pltpu.VMEM(s, d) for s, d in scratch],
        compiler_params=PARAMS,
        cost_estimate=pl.CostEstimate(flops=flops, bytes_accessed=moved, transcendentals=0),
    )(*scalars, *operands)


def choose(cond, yes, no):
    return jnp.where(jnp.broadcast_to(cond, yes.shape), yes, no)


def lines_kernel(place, f_ref, f0_ref, f1_ref, near_ref, far_ref, wide):
    channels, planes, rows, breadth = f_ref.shape
    wide[...] = f_ref[...].astype(F32).reshape(channels * planes * rows, breadth)

    def line(z, y):
        return wide[pl.ds(z * rows + y, channels, stride=planes * rows), :].astype(BF16)

    even = place[1] == 0
    for z, plane_ref in enumerate((f0_ref, f1_ref)):
        first, last = line(z, 0), line(z, rows - 1)
        near_ref[z] = choose(even, last, first)
        far_ref[z] = choose(even, first, last)
        plane_ref[0] = first
        plane_ref[rows - 1] = last
        for y in range(1, rows - 1):
            plane_ref[y] = line(z, y)


def faces_kernel(place, p0, p1, near, far, near_ref, far_ref):
    rows = p0.shape[0]
    even_z, even_y = place[0] == 0, place[1] == 0

    def put(q, low, high):
        near_ref[q] = choose(even_z, high, low)
        far_ref[q] = choose(even_z, low, high)

    put(0, choose(even_y, far[0], near[0]), choose(even_y, far[1], near[1]))
    for y in range(rows):
        put(y + 1, p0[y], p1[y])
    put(rows + 1, choose(even_y, near[0], far[0]), choose(even_y, near[1], far[1]))


def put_columns(cols, p, q, line):
    channels = line.shape[0]
    wide = line.astype(F32)
    cols[p, q, 0:channels] = pltpu.roll(wide, 1, 1).astype(BF16)
    cols[p, q, channels : 2 * channels] = line
    cols[p, q, 2 * channels : 3 * channels] = pltpu.roll(wide, line.shape[1] - 1, 1).astype(BF16)


def fill_columns(cols, near, far, near_first):
    def step(q, carry):
        put_columns(cols, 0, q, choose(near_first, near[q], far[q]))
        put_columns(cols, 1, q, choose(near_first, far[q], near[q]))
        return carry

    lax.fori_loop(0, near.shape[0], step, 0, unroll=2)


def window(cols, p, q):
    return jnp.concatenate([cols[p, q], cols[p, q + 1]], axis=1)


def inner_terms(cols, taps, y):
    acc = None
    for b in range(3):
        w = taps(b)
        count = w.shape[0] // 3
        for p in range(2):
            term = jnp.dot(w[p * count : (p + 2) * count], window(cols, p, y + b), preferred_element_type=F32)
            acc = term if acc is None else acc + term
    half = acc.shape[0] // 2
    return acc[half:], acc[:half]


def outer_terms(cols, taps, y):
    lower = upper = None
    for b in range(3):
        w = taps(b)
        count = w.shape[0] // 3
        low = jnp.dot(w[0:count], window(cols, 0, y + b), preferred_element_type=F32)
        high = jnp.dot(w[2 * count :], window(cols, 1, y + b), preferred_element_type=F32)
        lower = low if lower is None else lower + low
        upper = high if upper is None else upper + high
    return lower, upper


def stacked(w_ref):
    return lambda b: jnp.concatenate([w_ref[a, b] for a in range(3)], axis=0)


def inner_kernel(place, near, far, w_ref, d_ref, cot_ref, cols, acc_ref, grad_ref, up):
    channels, breadth = near.shape[1:]
    rows = near.shape[0] - 2
    fill_columns(cols, near, far, place[0] == 1)
    source = lax.broadcasted_iota(jnp.int32, (breadth, 2 * breadth), 0)
    target = lax.broadcasted_iota(jnp.int32, (breadth, 2 * breadth), 1)
    spread = jnp.where(source == target // 2, 1.0, 0.0).astype(BF16)
    for pair in range(rows // 4):
        both = jnp.dot(cot_ref[:, pair * breadth : (pair + 1) * breadth], spread, preferred_element_type=F32)
        up[:, 2 * pair * breadth : 2 * (pair + 1) * breadth] = both.astype(BF16)
    even = lax.broadcasted_iota(jnp.int32, (channels, breadth), 1) % 2 == 0
    for a in range(2):
        for b in range(2):
            terms = lax.dot_general(d_ref[a, b], up[...], (((0,), (0,)), ((), ())), preferred_element_type=F32)
            for t in range(rows // 2):
                part = terms[:, t * breadth : (t + 1) * breadth]
                grad_ref[a, 2 * t + b] = jnp.where(even, part[0:channels], part[channels:])

    def step(t, carry):
        y = 2 * t
        for z, lines in enumerate(inner_terms(cols, stacked(w_ref), y)):
            for b in range(2):
                acc_ref[z, y + b] = lines[:, b * breadth : (b + 1) * breadth]
        return carry

    lax.fori_loop(0, rows // 2, step, 0)


def gate_kernel(place, near, far, acc_ref, grad_ref, w_ref, cols, g0_ref, g1_ref, near_ref, far_ref, h_ref):
    channels, breadth = near.shape[1:]
    rows = near.shape[0] - 2
    fill_columns(cols, near, far, place[0] == 1)

    def step(t, carry):
        y = 2 * t
        outer = outer_terms(cols, stacked(w_ref), y)
        for z, plane_ref in enumerate((g0_ref, g1_ref)):
            for b in range(2):
                preact = acc_ref[z, y + b] + outer[z][:, b * breadth : (b + 1) * breadth]
                sig = 1.0 / (1.0 + jnp.exp(-preact))
                h_ref[z, y + b] = (preact * sig).astype(BF16)
                plane_ref[y + b] = (grad_ref[z, y + b] * sig * (1.0 + preact * (1.0 - sig))).astype(BF16)
        return carry

    lax.fori_loop(0, rows // 2, step, 0)
    even = place[1] == 0
    for z, plane_ref in enumerate((g0_ref, g1_ref)):
        near_ref[z] = choose(even, plane_ref[rows - 1], plane_ref[0])
        far_ref[z] = choose(even, plane_ref[0], plane_ref[rows - 1])


def weight_grad_kernel(place, inner, outer, g0_ref, g1_ref, h_ref, d_ref, cot_ref, out_ref, keep, send, packed):
    rows, channels, breadth = g0_ref.shape
    across = (((1,), (1,)), ((), ()))
    flat = lambda ref, rows_of: jnp.concatenate([ref[r] for r in rows_of], axis=1)
    gates = jnp.concatenate([flat(g0_ref, range(rows)), flat(g1_ref, range(rows))], axis=0)
    lane = lax.broadcasted_iota(jnp.int32, (channels // 2, breadth), 1)
    for b in range(3):
        parts = []
        for p in range(4):
            cols, at = (inner, p - 1) if p in (1, 2) else (outer, p // 3)
            window = jnp.concatenate([cols[at, y + b] for y in range(rows)], axis=1)
            lhs = gates[0:channels] if p == 0 else gates[channels:] if p == 3 else gates
            parts.append(lax.dot_general(lhs, window, across, preferred_element_type=F32))
        for a in range(3):
            low = parts[a][0:channels]
            high = parts[a + 1] if a == 2 else parts[a + 1][channels:]
            total = low + high
            base = (a * 3 + b) * 3 * channels // 2
            packed[base : base + channels] = total[:, 0:breadth].astype(BF16)
            rest = jnp.concatenate([total[:, breadth:], total[:, breadth:]], axis=1)
            mix = jnp.where(lane < channels, rest[0 : channels // 2], rest[channels // 2 :])
            packed[base + channels : base + 3 * channels // 2] = mix.astype(BF16)
    base = 9 * 3 * channels // 2
    source = lax.broadcasted_iota(jnp.int32, (2 * breadth, 2 * breadth), 0)
    target = lax.broadcasted_iota(jnp.int32, (2 * breadth, 2 * breadth), 1)
    wanted = 2 * (target % breadth) + target // breadth
    pick = jnp.where(source == wanted, 1.0, 0.0).astype(BF16)
    coarse = None
    for a in range(2):
        for b in range(2):
            pairs = []
            for pair in range(rows // 4):
                both = jnp.concatenate([h_ref[a, 4 * pair + b], h_ref[a, 4 * pair + 2 + b]], axis=1)
                pairs.append(jnp.dot(both, pick, preferred_element_type=F32).astype(BF16))
            hidden = jnp.concatenate(
                [jnp.concatenate([x[:, e * breadth : (e + 1) * breadth] for x in pairs], axis=1) for e in range(2)],
                axis=0,
            )
            term = jnp.dot(d_ref[a, b], hidden, preferred_element_type=F32)
            coarse = term if coarse is None else coarse + term
            down = lax.dot_general(cot_ref[...], hidden, across, preferred_element_type=F32)
            at = base + (2 * a + b) * d_ref.shape[2]
            packed[at : at + d_ref.shape[2]] = down.astype(BF16)
    out_ref[...] = coarse.astype(BF16)
    end = base + 4 * d_ref.shape[2]
    if end < packed.shape[0]:
        packed[end:] = jnp.zeros((packed.shape[0] - end, packed.shape[1]), BF16)
    half = packed.shape[0] // 2
    keep[...] = packed[pl.ds(pl.multiple_of(place[2] * half, 16), half)]
    send[...] = packed[pl.ds(pl.multiple_of((1 - place[2]) * half, 16), half)]


def add_kernel(x, y, out):
    out[...] = (x[...].astype(F32) + y[...].astype(F32)).astype(BF16)


def total_kernel(terms, out):
    total = jnp.sum(terms[...].astype(F32), axis=0).astype(BF16)
    for member in range(out.shape[0]):
        out[member] = total


def field_kernel(place, near, far, near_in, far_in, w_ref, out_ref, inner, outer):
    channels, breadth = near.shape[1:]
    rows = near.shape[0] - 2
    fill_columns(inner, near, far, place[0] == 1)
    fill_columns(outer, near_in, far_in, place[0] == 1)

    def step(t, carry):
        y = 2 * t
        own = inner_terms(inner, stacked(w_ref), y)
        rest = outer_terms(outer, stacked(w_ref), y)
        for z in range(2):
            total = own[z] + rest[z]
            for b in range(2):
                part = total[:, b * breadth : (b + 1) * breadth]
                out_ref[pl.ds(z * rows + y + b, channels, stride=2 * rows), :] = part
        return carry

    lax.fori_loop(0, rows // 2, step, 0)


def unpack_kernel(place, mine, other, conv_ref, down_ref, sums_ref, *, scale):
    half = mine.shape[0]
    sums_ref[pl.ds(pl.multiple_of(place[2] * half, 16), half)] = mine[...]
    sums_ref[pl.ds(pl.multiple_of((1 - place[2]) * half, 16), half)] = other[...]
    channels = conv_ref.shape[2]
    for a in range(3):
        for b in range(3):
            base = (a * 3 + b) * 3 * channels // 2
            conv_ref[a, b, :, 0 : 2 * channels] = sums_ref[base : base + channels].astype(F32) * scale
            rest = sums_ref[base + channels : base + 3 * channels // 2].astype(F32) * scale
            conv_ref[a, b, 0 : channels // 2, 2 * channels :] = rest[:, 0:channels]
            conv_ref[a, b, channels // 2 :, 2 * channels :] = rest[:, channels:]
    base = 9 * 3 * channels // 2
    height = down_ref.shape[2]
    for a in range(2):
        for b in range(2):
            at = base + (2 * a + b) * height
            down_ref[a, b] = sums_ref[at : at + height].astype(F32) * scale


def swap(cells, axis, low):
    count = lax.axis_size(axis)
    pairs = [(i % count, (i + 1) % count) for i in range(low, low + count, 2)]
    return lax.ppermute(cells, axis, pairs + [(b, a) for a, b in pairs])


def swapped(near, far, axis):
    return swap(near, axis, 0), swap(far, axis, 1)


def body(features, conv_weight, down_weight, cotangent):
    channels, plane_count, row_count, breadth = features.shape
    out_channels = down_weight.shape[2]
    count = lax.axis_size("gz") * lax.axis_size("gy")
    grad_scale = 1.0 / math.sqrt(plane_count * row_count * breadth * count)
    taps = conv_weight.reshape(3, 3, channels, 3, channels)[::-1, ::-1, :, ::-1]
    weight_bwd = taps.transpose(0, 1, 4, 3, 2).reshape(3, 3, channels, 3 * channels)
    cot = cotangent.reshape(out_channels, -1)
    along_z, along_y = lax.axis_index("gz"), lax.axis_index("gy")
    place = jnp.stack([along_z % 2, along_y % 2, along_y % 2]).astype(jnp.int32)
    plane = ((row_count, channels, breadth), BF16)
    edge = ((plane_count, channels, breadth), BF16)
    face = ((row_count + 2, channels, breadth), BF16)
    cols = ((2, row_count + 2, 3 * channels, breadth), BF16)
    lines = (plane_count, row_count, channels, breadth)
    conv_flops = 2 * 27 * channels * channels * plane_count * row_count * breadth

    f0, f1, near, far = call(
        lines_kernel, [plane, plane, edge, edge],
        [((channels * plane_count * row_count, breadth), F32)], 0, (place,), (features,),
    )
    near, far = swapped(near, far, "gy")
    near_own, far_own = call(faces_kernel, [face, face], [], 0, (place,), (f0, f1, near, far))
    near_face, far_face = swapped(near_own, far_own, "gz")
    inner, partial, hidden_grad = call(
        inner_kernel, [cols, (lines, F32), (lines, F32)],
        [((out_channels, row_count // 2 * breadth), BF16)],
        2 * conv_flops // 3, (place,), (near_own, far_own, conv_weight, down_weight, cot),
    )
    outer, g0, g1, near, far, hidden = call(
        gate_kernel, [cols, plane, plane, edge, edge, (lines, BF16)], [],
        conv_flops // 3, (place,), (near_face, far_face, partial, hidden_grad, conv_weight),
    )
    near, far = swapped(near, far, "gy")
    near_own, far_own = call(faces_kernel, [face, face], [], 0, (place,), (g0, g1, near, far))
    near_face, far_face = swapped(near_own, far_own, "gz")

    chips = count // 2
    used = 27 * channels * channels // 128 + 4 * out_channels
    share = -(-used // (16 * count)) * 16
    half = ((chips * share, 128), BF16)
    section_out, keep, send = call(
        weight_grad_kernel, [((out_channels, cot.shape[1]), BF16), half, half],
        [((share * count, 128), BF16)], conv_flops, (place,),
        (inner, outer, g0, g1, hidden, down_weight, cot),
    )
    (terms,) = call(add_kernel, [half], [], 0, (), (keep, swap(send, "gy", 0)))
    groups = [list(range(core, count, 2)) for core in range(2)]
    exchange = functools.partial(
        lax.all_to_all, axis_name=("gz", "gy"), split_axis=0, concat_axis=0, axis_index_groups=groups, tiled=True
    )
    parts = ((chips, share, 128), BF16)
    (mine,) = call(total_kernel, [parts], [], 0, (), (exchange(terms.reshape(parts[0])),))
    sums = exchange(mine).reshape(half[0])
    other = swap(sums, "gy", 0)

    (field,) = call(
        field_kernel, [((channels * plane_count * row_count, breadth), F32)], [cols, cols], conv_flops,
        (place,), (near_own, far_own, near_face, far_face, weight_bwd),
    )
    grad_conv, grad_down = call(
        functools.partial(unpack_kernel, scale=grad_scale),
        [(conv_weight.shape, F32), (down_weight.shape, F32)], [((share * count, 128), BF16)], 0,
        (place,), (sums, other),
    )
    section_out = section_out.reshape(out_channels, plane_count // 2, -1)
    return (section_out, field.reshape(features.shape), grad_conv, grad_down)


def solution(mesh):
    return jax.shard_map(
        body,
        mesh=mesh,
        in_specs=(P(None, "gz", "gy", None), P(), P(), P(None, "gz", "gy")),
        out_specs=(P(None, "gz", "gy"), P(None, "gz", "gy", None), P(), P()),
        check_vma=False,
    )
```

time: 67.7 us -> 66.2 us (0.978)
  blocking collectives: 0 us -> 15.2 us
  starting transfers between devices: 30.1 us -> 19.5 us
  waiting for transfers between devices: 19.7 us -> 12.3 us
  Pallas kernels: 11.2 us -> 16.4 us
  local copies, waits for them, and re-layouts: 5.41 us -> 1.8 us
    all_to_all x0 -> x1, blocking collectives: none -> 15.2 us  [body(): exchange(terms.reshape(parts[0]))]
    all_to_all x2 -> x1, waiting for transfers between devices: 9.37 us -> 0.01 us  [body(): sums = exchange(mine).reshape(half[0])]
    ppermute x12 -> x10, starting transfers between devices: 23 us -> 16 us  [swap(): return lax.ppermute(cells, axis, pairs + [(b, a) for a, b in pairs])]
    pallas_call x5 -> x10, Pallas kernels: 11.2 us -> 16.4 us  [call(): pl.pallas_call(kernel, out_shape=[jax.ShapeDtypeStruct(s, d) for s, d in...]
    all_to_all x2 -> x1, starting transfers between devices: 7.05 us -> 3.52 us  [body(): sums = exchange(mine).reshape(half[0])]
    ppermute x12 -> x10, waiting for transfers between devices: 10.4 us -> 12.3 us  [swap(): return lax.ppermute(cells, axis, pairs + [(b, a) for a, b in pairs])]
    transpose x3 -> x2, local copies, waits for them, and re-layouts: 1.63 us -> 0.32 us  [body(): taps.transpose(0, 1, 4, 3, 2).reshape(3, 3, channels, 3 * channels)]
    unnamed x10 -> x9, local copies, waits for them, and re-layouts: 2.28 us -> 1.24 us
  transfers between devices with their start and end apart: 14 -> 11, of which waited for: 3 -> 7; matrix products, arithmetic and copies ran while one was open for 7% -> 1% of each run, Pallas kernels for 6% -> 11%
where the time goes in v3:
time: 66.2 us; the launch traced here: 66 us
  starting transfers between devices  19.5 us (29%)
  Pallas kernels  16.4 us (25%)
  blocking collectives  15.2 us (23%)
  waiting for transfers between devices  12.3 us (19%)
  local copies, waits for them, and re-layouts  1.8 us (3%)
  between operations  0.74 us (1%)
    pallas_call x10, Pallas kernels, call(): pl.pallas_call(kernel, out_shape=[jax.ShapeDtypeStruct(s, d) for s, d in...  16.4 us
    ppermute x10, starting transfers between devices, swap(): return lax.ppermute(cells, axis, pairs + [(b, a) for a, b in pairs])  16 us
    all_to_all x1, blocking collectives, body(): exchange(terms.reshape(parts[0]))  15.2 us
    ppermute x10, waiting for transfers between devices, swap(): return lax.ppermute(cells, axis, pairs + [(b, a) for a, b in pairs])  12.3 us
    all_to_all x1, starting transfers between devices, body(): sums = exchange(mine).reshape(half[0])  3.52 us
  transfers between devices with their start and end apart: 11, of which 7 were waited for; matrix products, arithmetic and copies ran while one was open for 1% of the time, Pallas kernels for 11%

profile of v3, /device:TPU:0, one launch (start us, length us, event | category | flops | bytes accessed | tf_op | source)
XLA Modules:
  0.0 66.0 jit_solution(2555030655234992015)
XLA Ops:
  0.6 0.1 pad_add_fusion.place
  0.7 0.0 copy-start.1
  0.7 0.9 %copy-done.1 = bf16[64,2,8,128]{3,2,1,0:T(8,128)(2,1)S(1)} copy-done((bf16[64,2,8,128]{3,2,1,0:T(8,128)(2,1)S(1)}, bf16[64,2,8,128]{3,2,1,0:T(8,128)(2,1)}, u32[]{:S(2)}) %copy-start.1) | copy-done | bytes 262168
  1.7 0.0 copy-start
  1.7 0.7 %shard_map.75 = (bf16[8,64,128]{2,1,0:T(8,128)(2,1)S(1)}, bf16[8,64,128]{2,1,0:T(8,128)(2,1)S(1)}, bf16[2,64,128]{2,1,0:T(8,128)(2,1)S(1)}, bf16[2,64,128]{2,1,0:T(8,128)(2,1)S(1)}) custom-call(s32[3]{0:T(128)S(1)} %pad_add_fusion.place, bf16[64,2,8,128]{3,2,1,0:T(8,128)(2,1)S(1)} %copy-done.1), custom_call_target="tpu_custom_call" | custom-call | bytes 589824 | tf_op jit(solution)/shard_map/pallas_call | solution.py:20
  2.4 0.5 collective-permute-start
  2.9 2.6 %collective-permute-start.1 = (bf16[2,64,128]{2,1,0:T(8,128)(2,1)S(1)}, bf16[2,64,128]{2,1,0:T(8,128)(2,1)S(1)}, u32[]{:S(2)}, u32[]{:S(2)}) collective-permute-start(bf16[2,64,128]{2,1,0:T(8,128)(2,1)S(1)} %get-tuple-element.29), channel_id=1, source_target_pairs={{1,2},{3,0},{2,1},{0,3},{5,6},{7,4},{6,5},{4,7},{9,10},{11,8},{10,... | collective-permute-start | bytes 98312 | tf_op jit(solution)/shard_map/ppermute | solution.py:272
  5.6 0.0 collective-permute-done.near
  5.6 1.7 %collective-permute-done.1.far = bf16[2,64,128]{2,1,0:T(8,128)(2,1)S(1)} collective-permute-done((bf16[2,64,128]{2,1,0:T(8,128)(2,1)S(1)}, bf16[2,64,128]{2,1,0:T(8,128)(2,1)S(1)}, u32[]{:S(2)}, u32[]{:S(2)}) %collective-permute-start.1) | collective-permute-done | bytes 32800 | tf_op jit(solution)/shard_map/ppermute | solution.py:272
  7.2 0.0 copy-start.2
  7.2 0.0 copy-start.3
  7.2 0.6 shard_map.76
  7.8 1.7 %collective-permute-start.2 = (bf16[10,64,128]{2,1,0:T(8,128)(2,1)S(1)}, bf16[10,64,128]{2,1,0:T(8,128)(2,1)S(1)}, u32[]{:S(2)}, u32[]{:S(2)}) collective-permute-start(bf16[10,64,128]{2,1,0:T(8,128)(2,1)S(1)} %get-tuple-element.30.near), channel_id=1, source_target_pairs={{0,4},{8,12},{16,20},{24,28},{4,0},{12,8},{20,16},{28,24},{1,5},{9... | collective-permute-start | bytes 491528 | tf_op jit(solution)/shard_map/ppermute | solution.py:272
  9.5 3.5 %collective-permute-start.3 = (bf16[10,64,128]{2,1,0:T(8,128)(2,1)S(1)}, bf16[10,64,128]{2,1,0:T(8,128)(2,1)S(1)}, u32[]{:S(2)}, u32[]{:S(2)}) collective-permute-start(bf16[10,64,128]{2,1,0:T(8,128)(2,1)S(1)} %get-tuple-element.31.far), channel_id=1, source_target_pairs={{4,8},{12,16},{20,24},{28,0},{8,4},{16,12},{24,20},{0,28},{5,9},{1... | collective-permute-start | bytes 491528 | tf_op jit(solution)/shard_map/ppermute | solution.py:272
  13.1 0.0 copy-done
  13.1 0.0 copy-done.2
  13.1 0.0 copy-done.3
  13.1 2.6 %shard_map.77 = (bf16[2,10,192,128]{3,2,1,0:T(8,128)(2,1)S(1)}, f32[2,8,64,128]{3,2,1,0:T(8,128)S(1)}, f32[2,8,64,128]{3,2,1,0:T(8,128)S(1)}) custom-call(s32[3]{0:T(128)S(1)} %pad_add_fusion.place, bf16[10,64,128]{2,1,0:T(8,128)(2,1)S(1)} %get-tuple-element.30.near, bf16[10,64,128]{2,1,0:T(8,128)(2,1)S(1)} %get-tuple-element.31.far, ...), custom_call_target="tpu_custom_call" | custom-call | flops 301989888 | bytes 2777088 | tf_op jit(solution)/shard_map/pallas_call | solution.py:20
  15.7 1.5 %collective-permute-done.2.near = bf16[10,64,128]{2,1,0:T(8,128)(2,1)S(1)} collective-permute-done((bf16[10,64,128]{2,1,0:T(8,128)(2,1)S(1)}, bf16[10,64,128]{2,1,0:T(8,128)(2,1)S(1)}, u32[]{:S(2)}, u32[]{:S(2)}) %collective-permute-start.2) | collective-permute-done | bytes 163872 | tf_op jit(solution)/shard_map/ppermute | solution.py:272
  17.1 1.4 %collective-permute-done.3.far = bf16[10,64,128]{2,1,0:T(8,128)(2,1)S(1)} collective-permute-done((bf16[10,64,128]{2,1,0:T(8,128)(2,1)S(1)}, bf16[10,64,128]{2,1,0:T(8,128)(2,1)S(1)}, u32[]{:S(2)}, u32[]{:S(2)}) %collective-permute-start.3) | collective-permute-done | bytes 163872 | tf_op jit(solution)/shard_map/ppermute | solution.py:272
  18.5 2.2 %shard_map.78 = (bf16[2,10,192,128]{3,2,1,0:T(8,128)(2,1)S(1)}, bf16[8,64,128]{2,1,0:T(8,128)(2,1)S(1)}, bf16[8,64,128]{2,1,0:T(8,128)(2,1)S(1)}, bf16[2,64,128]...) custom-call(s32[3]{0:T(128)S(1)} %pad_add_fusion.place, ...), custom_call_target="tpu_custom_call" | custom-call | flops 150994944 | bytes 3170304 | tf_op jit(solution)/shard_map/pallas_call | solution.py:20
  20.8 3.5 %shard_map.79 = (bf16[128,256]{1,0:T(8,128)(2,1)}, bf16[768,128]{1,0:T(8,128)(2,1)S(1)}, bf16[768,128]{1,0:T(8,128)(2,1)S(1)}) custom-call(s32[3]{0:T(128)S(1)} %pad_add_fusion.place, bf16[2,10,192,128]{3,2,1,0:T(8,128)(2,1)S(1)} %get-tuple-element.32.inner, bf16[2,10,192,128]{3,2,1,0:T(8,128)(2,1)S(1)} %get-tuple-element.35.outer, ...), custom_call_target="tpu_custom_call" | custom-call | flops 452984832 | bytes 3145728 | tf_op jit(solution)/shard_map/pallas_call | solution.py:20
  24.2 0.0 collective-permute-start.8
  24.2 1.4 %collective-permute-done.8.y = bf16[768,128]{1,0:T(8,128)(2,1)S(1)} collective-permute-done((bf16[768,128]{1,0:T(8,128)(2,1)S(1)}, bf16[768,128]{1,0:T(8,128)(2,1)S(1)}, u32[]{:S(2)}, u32[]{:S(2)}) %collective-permute-start.8) | collective-permute-done | bytes 196640 | tf_op jit(solution)/shard_map/ppermute | solution.py:272
  25.7 15.2 %all_to_all.10.terms = bf16[16,48,128]{2,1,0:T(8,128)(2,1)S(1)} all-to-all(bf16[16,48,128]{2,1,0:T(8,128)(2,1)S(1)} %bitcast.13), channel_id=1, replica_groups={{0,2,4,6,8,10,12,14,16,18,20,22,24,26,28,30},{1,3,5,7,9,11,13,15,17,19,..., dimensions={0} | all-to-all | bytes 393216 | tf_op jit(solution)/shard_map/all_to_all | solution.py:331
  40.9 0.7 %shard_map.83 = bf16[16,48,128]{2,1,0:T(8,128)(2,1)} custom-call(bf16[16,48,128]{2,1,0:T(8,128)(2,1)S(1)} %all_to_all.10.terms), custom_call_target="tpu_custom_call" | custom-call | bytes 393216 | tf_op jit(solution)/shard_map/pallas_call | solution.py:20
  41.6 3.5 %all-to-all-start.1 = ((bf16[16,48,128]{2,1,0:T(8,128)(2,1)}), bf16[16,48,128]{2,1,0:T(8,128)(2,1)S(1)}, u32[]{:S(2)}, u32[]{:S(2)}) async-start(bf16[16,48,128]{2,1,0:T(8,128)(2,1)} %shard_map.83), calls=%async_computation.1 | async-start | bytes 393216 | tf_op jit(solution)/shard_map/all_to_all | solution.py:332
  45.2 0.1 collective-permute-start.4
  45.2 1.8 %collective-permute-start.5 = (bf16[2,64,128]{2,1,0:T(8,128)(2,1)S(1)}, bf16[2,64,128]{2,1,0:T(8,128)(2,1)S(1)}, u32[]{:S(2)}, u32[]{:S(2)}) collective-permute-start(bf16[2,64,128]{2,1,0:T(8,128)(2,1)S(1)} %get-tuple-element.41), channel_id=1, source_target_pairs={{1,2},{3,0},{2,1},{0,3},{5,6},{7,4},{6,5},{4,7},{9,10},{11,8},{10,... | collective-permute-start | bytes 98312 | tf_op jit(solution)/shard_map/ppermute | solution.py:272
  47.1 0.0 collective-permute-done.4.near
  47.1 2.0 %collective-permute-done.5.far = bf16[2,64,128]{2,1,0:T(8,128)(2,1)S(1)} collective-permute-done((bf16[2,64,128]{2,1,0:T(8,128)(2,1)S(1)}, bf16[2,64,128]{2,1,0:T(8,128)(2,1)S(1)}, u32[]{:S(2)}, u32[]{:S(2)}) %collective-permute-start.5) | collective-permute-done | bytes 32800 | tf_op jit(solution)/shard_map/ppermute | solution.py:272
  49.1 0.6 shard_map.80
  49.7 1.6 %collective-permute-start.6 = (bf16[10,64,128]{2,1,0:T(8,128)(2,1)S(1)}, bf16[10,64,128]{2,1,0:T(8,128)(2,1)S(1)}, u32[]{:S(2)}, u32[]{:S(2)}) collective-permute-start(bf16[10,64,128]{2,1,0:T(8,128)(2,1)S(1)} %get-tuple-element.42.near), channel_id=1, source_target_pairs={{0,4},{8,12},{16,20},{24,28},{4,0},{12,8},{20,16},{28,24},{1,5},{9... | collective-permute-start | bytes 491528 | tf_op jit(solution)/shard_map/ppermute | solution.py:272
  51.3 3.7 %collective-permute-start.7 = (bf16[10,64,128]{2,1,0:T(8,128)(2,1)S(1)}, bf16[10,64,128]{2,1,0:T(8,128)(2,1)S(1)}, u32[]{:S(2)}, u32[]{:S(2)}) collective-permute-start(bf16[10,64,128]{2,1,0:T(8,128)(2,1)S(1)} %get-tuple-element.43.far), channel_id=1, source_target_pairs={{4,8},{12,16},{20,24},{28,0},{8,4},{16,12},{24,20},{0,28},{5,9},{1... | collective-permute-start | bytes 491528 | tf_op jit(solution)/shard_map/ppermute | solution.py:272
  55.0 0.0 all-to-all-done.1
  55.0 0.4 collective-permute-start.9
  55.3 0.3 copy.9
  55.7 0.3 copy.10
  56.0 0.2 copy.11.w_ref
  56.2 3.0 %collective-permute-done.6.near_in = bf16[10,64,128]{2,1,0:T(8,128)(2,1)S(1)} collective-permute-done((bf16[10,64,128]{2,1,0:T(8,128)(2,1)S(1)}, bf16[10,64,128]{2,1,0:T(8,128)(2,1)S(1)}, u32[]{:S(2)}, u32[]{:S(2)}) %collective-permute-start.6) | collective-permute-done | bytes 163872 | tf_op jit(solution)/shard_map/ppermute | solution.py:272
  59.2 1.4 %collective-permute-done.7.far_in = bf16[10,64,128]{2,1,0:T(8,128)(2,1)S(1)} collective-permute-done((bf16[10,64,128]{2,1,0:T(8,128)(2,1)S(1)}, bf16[10,64,128]{2,1,0:T(8,128)(2,1)S(1)}, u32[]{:S(2)}, u32[]{:S(2)}) %collective-permute-start.7) | collective-permute-done | bytes 163872 | tf_op jit(solution)/shard_map/ppermute | solution.py:272
  60.6 3.9 %shard_map.81 = f32[1024,128]{1,0:T(8,128)} custom-call(s32[3]{0:T(128)S(1)} %pad_add_fusion.place, bf16[10,64,128]{2,1,0:T(8,128)(2,1)S(1)} %get-tuple-element.42.near, bf16[10,64,128]{2,1,0:T(8,128)(2,1)S(1)} %get-tuple-element.43.far, bf16[10,64,128]{2,1,0:T(8,128)(2,1)S(1)} %collective-permute-done.6.near_in, ...), custom_call_target="tpu_custom_call" | custom-call | flops 452984832 | bytes 1400832 | tf_op jit(solution)/shard_map/pallas_call | solution.py:20
  64.4 0.0 collective-permute-done.9.other
  64.4 1.5 %shard_map.84 = (f32[3,3,64,192]{3,2,1,0:T(8,128)}, f32[2,2,128,128]{3,2,1,0:T(8,128)}) custom-call(s32[3]{0:T(128)S(1)} %pad_add_fusion.place, bf16[768,128]{1,0:T(8,128)(2,1)S(1)} %bitcast.12, bf16[768,128]{1,0:T(8,128)(2,1)S(1)} %collective-permute-done.9.other), custom_call_target="tpu_custom_call" | custom-call | bytes 1097728 | tf_op jit(solution)/shard_map/pallas_call | solution.py:20
  (2 shorter events, 0.1 us)
Async XLA Ops:
  0.7 1.0 %copy-start.1 = (bf16[64,2,8,128]{3,2,1,0:T(8,128)(2,1)S(1)}, bf16[64,2,8,128]{3,2,1,0:T(8,128)(2,1)}, u32[]{:S(2)}) copy-start(bf16[64,2,8,128]{3,2,1,0:T(8,128)(2,1)} %f_ref.1) | copy-start | bytes 786436
  1.7 11.4 %copy-start = (bf16[3,3,64,192]{3,2,1,0:T(8,128)(2,1)S(1)}, bf16[3,3,64,192]{3,2,1,0:T(8,128)(2,1)}, u32[]{:S(2)}) copy-start(bf16[3,3,64,192]{3,2,1,0:T(8,128)(2,1)} %w_ref.3) | copy-start | bytes 663556
  2.4 3.1 %collective-permute-start = (bf16[2,64,128]{2,1,0:T(8,128)(2,1)S(1)}, bf16[2,64,128]{2,1,0:T(8,128)(2,1)S(1)}, u32[]{:S(2)}, u32[]{:S(2)}) collective-permute-start(bf16[2,64,128]{2,1,0:T(8,128)(2,1)S(1)} %get-tuple-element.28), channel_id=1, source_target_pairs={{0,1},{2,3},{1,0},{3,2},{4,5},{6,7},{5,4},{7,6},{8,9},{10,11},{9,8... | collective-permute-start | bytes 98312 | tf_op jit(solution)/shard_map/ppermute | solution.py:272
  2.9 4.3 %collective-permute-start.1 = (bf16[2,64,128]{2,1,0:T(8,128)(2,1)S(1)}, bf16[2,64,128]{2,1,0:T(8,128)(2,1)S(1)}, u32[]{:S(2)}, u32[]{:S(2)}) collective-permute-start(bf16[2,64,128]{2,1,0:T(8,128)(2,1)S(1)} %get-tuple-element.29), channel_id=1, source_target_pairs={{1,2},{3,0},{2,1},{0,3},{5,6},{7,4},{6,5},{4,7},{9,10},{11,8},{10,... | collective-permute-start | bytes 98312 | tf_op jit(solution)/shard_map/ppermute | solution.py:272
  7.2 5.9 %copy-start.2 = (bf16[2,2,128,128]{3,2,1,0:T(8,128)(2,1)S(1)}, bf16[2,2,128,128]{3,2,1,0:T(8,128)(2,1)}, u32[]{:S(2)}) copy-start(bf16[2,2,128,128]{3,2,1,0:T(8,128)(2,1)} %d_ref.3) | copy-start | bytes 393220
  7.2 5.9 %copy-start.3 = (bf16[128,1,256]{2,0,1:T(8,128)(2,1)S(1)}, bf16[128,1,256]{2,0,1:T(8,128)(2,1)}, u32[]{:S(2)}) copy-start(bf16[128,1,256]{2,0,1:T(8,128)(2,1)} %param.7) | copy-start | bytes 196612
  7.8 9.3 %collective-permute-start.2 = (bf16[10,64,128]{2,1,0:T(8,128)(2,1)S(1)}, bf16[10,64,128]{2,1,0:T(8,128)(2,1)S(1)}, u32[]{:S(2)}, u32[]{:S(2)}) collective-permute-start(bf16[10,64,128]{2,1,0:T(8,128)(2,1)S(1)} %get-tuple-element.30.near), channel_id=1, source_target_pairs={{0,4},{8,12},{16,20},{24,28},{4,0},{12,8},{20,16},{28,24},{1,5},{9... | collective-permute-start | bytes 491528 | tf_op jit(solution)/shard_map/ppermute | solution.py:272
  9.5 9.0 %collective-permute-start.3 = (bf16[10,64,128]{2,1,0:T(8,128)(2,1)S(1)}, bf16[10,64,128]{2,1,0:T(8,128)(2,1)S(1)}, u32[]{:S(2)}, u32[]{:S(2)}) collective-permute-start(bf16[10,64,128]{2,1,0:T(8,128)(2,1)S(1)} %get-tuple-element.31.far), channel_id=1, source_target_pairs={{4,8},{12,16},{20,24},{28,0},{8,4},{16,12},{24,20},{0,28},{5,9},{1... | collective-permute-start | bytes 491528 | tf_op jit(solution)/shard_map/ppermute | solution.py:272
  24.2 1.4 %collective-permute-start.8 = (bf16[768,128]{1,0:T(8,128)(2,1)S(1)}, bf16[768,128]{1,0:T(8,128)(2,1)S(1)}, u32[]{:S(2)}, u32[]{:S(2)}) collective-permute-start(bf16[768,128]{1,0:T(8,128)(2,1)S(1)} %get-tuple-element.45), channel_id=1, source_target_pairs={{0,1},{2,3},{1,0},{3,2},{4,5},{6,7},{5,4},{7,6},{8,9},{10,11},{9,8... | collective-permute-start | bytes 589832 | tf_op jit(solution)/shard_map/ppermute | solution.py:272
  41.6 13.3 %all-to-all-start.1 = ((bf16[16,48,128]{2,1,0:T(8,128)(2,1)}), bf16[16,48,128]{2,1,0:T(8,128)(2,1)S(1)}, u32[]{:S(2)}, u32[]{:S(2)}) async-start(bf16[16,48,128]{2,1,0:T(8,128)(2,1)} %shard_map.83), calls=%async_computation.1 | async-start | bytes 393216 | tf_op jit(solution)/shard_map/all_to_all | solution.py:332
  45.2 1.9 %collective-permute-start.4 = (bf16[2,64,128]{2,1,0:T(8,128)(2,1)S(1)}, bf16[2,64,128]{2,1,0:T(8,128)(2,1)S(1)}, u32[]{:S(2)}, u32[]{:S(2)}) collective-permute-start(bf16[2,64,128]{2,1,0:T(8,128)(2,1)S(1)} %get-tuple-element.40), channel_id=1, source_target_pairs={{0,1},{2,3},{1,0},{3,2},{4,5},{6,7},{5,4},{7,6},{8,9},{10,11},{9,8... | collective-permute-start | bytes 98312 | tf_op jit(solution)/shard_map/ppermute | solution.py:272
  45.2 3.8 %collective-permute-start.5 = (bf16[2,64,128]{2,1,0:T(8,128)(2,1)S(1)}, bf16[2,64,128]{2,1,0:T(8,128)(2,1)S(1)}, u32[]{:S(2)}, u32[]{:S(2)}) collective-permute-start(bf16[2,64,128]{2,1,0:T(8,128)(2,1)S(1)} %get-tuple-element.41), channel_id=1, source_target_pairs={{1,2},{3,0},{2,1},{0,3},{5,6},{7,4},{6,5},{4,7},{9,10},{11,8},{10,... | collective-permute-start | bytes 98312 | tf_op jit(solution)/shard_map/ppermute | solution.py:272
  49.7 9.5 %collective-permute-start.6 = (bf16[10,64,128]{2,1,0:T(8,128)(2,1)S(1)}, bf16[10,64,128]{2,1,0:T(8,128)(2,1)S(1)}, u32[]{:S(2)}, u32[]{:S(2)}) collective-permute-start(bf16[10,64,128]{2,1,0:T(8,128)(2,1)S(1)} %get-tuple-element.42.near), channel_id=1, source_target_pairs={{0,4},{8,12},{16,20},{24,28},{4,0},{12,8},{20,16},{28,24},{1,5},{9... | collective-permute-start | bytes 491528 | tf_op jit(solution)/shard_map/ppermute | solution.py:272
  51.3 9.3 %collective-permute-start.7 = (bf16[10,64,128]{2,1,0:T(8,128)(2,1)S(1)}, bf16[10,64,128]{2,1,0:T(8,128)(2,1)S(1)}, u32[]{:S(2)}, u32[]{:S(2)}) collective-permute-start(bf16[10,64,128]{2,1,0:T(8,128)(2,1)S(1)} %get-tuple-element.43.far), channel_id=1, source_target_pairs={{4,8},{12,16},{20,24},{28,0},{8,4},{16,12},{24,20},{0,28},{5,9},{1... | collective-permute-start | bytes 491528 | tf_op jit(solution)/shard_map/ppermute | solution.py:272
  55.0 9.5 %collective-permute-start.9 = (bf16[768,128]{1,0:T(8,128)(2,1)S(1)}, bf16[768,128]{1,0:T(8,128)(2,1)S(1)}, u32[]{:S(2)}, u32[]{:S(2)}) collective-permute-start(bf16[768,128]{1,0:T(8,128)(2,1)S(1)} %bitcast.11), channel_id=1, source_target_pairs={{0,1},{2,3},{1,0},{3,2},{4,5},{6,7},{5,4},{7,6},{8,9},{10,11},{9,8... | collective-permute-start | bytes 589832 | tf_op jit(solution)/shard_map/ppermute | solution.py:272

commit v4 on v3

v4 whole, which is shorter than its diff:
```python
import functools
import math

import jax
import jax.numpy as jnp
from jax import lax
from jax.experimental import pallas as pl
from jax.experimental.pallas import tpu as pltpu
from jax.sharding import PartitionSpec as P

F32 = jnp.float32
BF16 = jnp.bfloat16
PARAMS = pltpu.CompilerParams(vmem_limit_bytes=24 * 1024 * 1024)


def call(kernel, outs, scratch, flops, operands):
    moved = sum(x.size * x.dtype.itemsize for x in operands)
    moved += sum(math.prod(s) * jnp.dtype(d).itemsize for s, d in outs)
    vmem = pl.BlockSpec(memory_space=pltpu.VMEM)
    return pl.pallas_call(
        kernel,
        out_shape=[jax.ShapeDtypeStruct(s, d) for s, d in outs],
        in_specs=[vmem] * len(operands),
        out_specs=[vmem] * len(outs),
        scratch_shapes=[pltpu.VMEM(s, d) for s, d in scratch],
        compiler_params=PARAMS,
        cost_estimate=pl.CostEstimate(flops=flops, bytes_accessed=moved, transcendentals=0),
    )(*operands)


def is_even(axis):
    return lax.rem(lax.axis_index(axis), 2) == 0


def choose(cond, yes, no):
    return jnp.where(jnp.broadcast_to(cond, yes.shape), yes, no)


def lines_kernel(f_ref, near_ref, far_ref, wide):
    channels, planes, rows, breadth = f_ref.shape
    wide[...] = f_ref[...].astype(F32).reshape(channels * planes * rows, breadth)
    even = is_even("gz")
    for y in range(rows):
        low, high = (
            wide[pl.ds(z * rows + y, channels, stride=planes * rows), :].astype(BF16) for z in range(2)
        )
        near_ref[y] = choose(even, high, low)
        far_ref[y] = choose(even, low, high)


def edges_kernel(near, far, near_in, far_in, near_ref, far_ref):
    rows = near.shape[0]
    even_z, even_y = is_even("gz"), is_even("gy")

    def put(p, one, other):
        first = choose(even_z, one[0], other[0])
        last = choose(even_z, one[rows - 1], other[rows - 1])
        near_ref[p] = choose(even_y, last, first)
        far_ref[p] = choose(even_y, first, last)

    put(0, far_in, near_in)
    put(1, far, near)
    put(2, near, far)
    put(3, near_in, far_in)


def put_columns(cols, p, q, line):
    channels = line.shape[0]
    wide = line.astype(F32)
    cols[p, q, 0:channels] = pltpu.roll(wide, 1, 1).astype(BF16)
    cols[p, q, channels : 2 * channels] = line
    cols[p, q, 2 * channels : 3 * channels] = pltpu.roll(wide, line.shape[1] - 1, 1).astype(BF16)


def fill_columns(cols, near, far):
    rows = near.shape[0]
    even = is_even("gz")

    def step(y, carry):
        put_columns(cols, 0, y + 1, choose(even, far[y], near[y]))
        put_columns(cols, 1, y + 1, choose(even, near[y], far[y]))
        return carry

    lax.fori_loop(0, rows, step, 0, unroll=2)
    for p in range(2):
        for q in (0, rows + 1):
            cols[p, q] = jnp.zeros(cols.shape[2:], BF16)


def fill_edges(cols, near, far):
    even = is_even("gy")
    for p in range(4):
        put_columns(cols, p, 0, choose(even, far[p], near[p]))
        put_columns(cols, p, 1, choose(even, near[p], far[p]))


def dot(lhs, rhs):
    return jnp.dot(lhs, rhs, preferred_element_type=F32)


def taps(w_ref, b, first, last):
    return jnp.concatenate([w_ref[a, b] for a in range(first, last)], axis=0)


def window(cols, p, q):
    return jnp.concatenate([cols[p, q], cols[p, q + 1]], axis=1)


def inner_terms(cols, w_ref, y):
    acc = None
    for b in range(3):
        for p in range(2):
            term = dot(taps(w_ref, b, p, p + 2), window(cols, p, y + b))
            acc = term if acc is None else acc + term
    half = acc.shape[0] // 2
    return acc[half:], acc[:half]


def outer_terms(cols, w_ref, y):
    lower = upper = None
    for b in range(3):
        low, high = dot(w_ref[0, b], window(cols, 0, y + b)), dot(w_ref[2, b], window(cols, 1, y + b))
        lower = low if lower is None else lower + low
        upper = high if upper is None else upper + high
    return lower, upper


def edge_terms(edges, w_ref, side):
    b = 2 * side
    half = w_ref.shape[2]
    acc = dot(taps(w_ref, b, 0, 2), edges[1, side]) + dot(taps(w_ref, b, 1, 3), edges[2, side])
    return acc[half:] + dot(w_ref[0, b], edges[0, side]), acc[:half] + dot(w_ref[2, b], edges[3, side])


def inner_kernel(near, far, w_ref, d_ref, cot_ref, cols, acc_ref, grad_ref, up):
    rows, channels, breadth = near.shape
    fill_columns(cols, near, far)
    source = lax.broadcasted_iota(jnp.int32, (breadth, 2 * breadth), 0)
    target = lax.broadcasted_iota(jnp.int32, (breadth, 2 * breadth), 1)
    spread = jnp.where(source == target // 2, 1.0, 0.0).astype(BF16)
    for pair in range(rows // 4):
        both = dot(cot_ref[:, pair * breadth : (pair + 1) * breadth], spread)
        up[:, 2 * pair * breadth : 2 * (pair + 1) * breadth] = both.astype(BF16)
    even = lax.broadcasted_iota(jnp.int32, (channels, breadth), 1) % 2 == 0
    for a in range(2):
        for b in range(2):
            terms = lax.dot_general(d_ref[a, b], up[...], (((0,), (0,)), ((), ())), preferred_element_type=F32)
            for t in range(rows // 2):
                part = terms[:, t * breadth : (t + 1) * breadth]
                grad_ref[a, 2 * t + b] = jnp.where(even, part[0:channels], part[channels:])

    def step(t, carry):
        y = 2 * t
        for z, lines in enumerate(inner_terms(cols, w_ref, y)):
            for b in range(2):
                acc_ref[z, y + b] = lines[:, b * breadth : (b + 1) * breadth]
        return carry

    lax.fori_loop(0, rows // 2, step, 0)


def outer_kernel(near, far, w_ref, acc_ref, cols, out_ref):
    rows, channels, breadth = near.shape
    fill_columns(cols, near, far)

    def step(t, carry):
        y = 2 * t
        for z, lines in enumerate(outer_terms(cols, w_ref, y)):
            for b in range(2):
                out_ref[z, y + b] = acc_ref[z, y + b] + lines[:, b * breadth : (b + 1) * breadth]
        return carry

    lax.fori_loop(0, rows // 2, step, 0)


def gate_kernel(near, far, acc_ref, grad_ref, w_ref, edges, near_ref, far_ref, h_ref):
    rows, channels, breadth = acc_ref.shape[1:]
    fill_edges(edges, near, far)
    sides = [edge_terms(edges, w_ref, side) for side in range(2)]
    even = is_even("gz")

    def gate(y, extra):
        found = []
        for z in range(2):
            preact = acc_ref[z, y] if extra is None else acc_ref[z, y] + extra[z]
            sig = 1.0 / (1.0 + jnp.exp(-preact))
            h_ref[z, y] = (preact * sig).astype(BF16)
            found.append((grad_ref[z, y] * sig * (1.0 + preact * (1.0 - sig))).astype(BF16))
        near_ref[y] = choose(even, found[1], found[0])
        far_ref[y] = choose(even, found[0], found[1])

    gate(0, sides[0])
    for y in range(1, rows - 1):
        gate(y, None)
    gate(rows - 1, sides[1])


def weight_grad_kernel(inner, outer, edges, near, far, h_ref, d_ref, cot_ref, out_ref, keep, send, packed):
    rows, channels, breadth = near.shape
    across = (((1,), (1,)), ((), ()))
    even = is_even("gz")
    low = [choose(even, far[y], near[y]) for y in range(rows)]
    high = [choose(even, near[y], far[y]) for y in range(rows)]
    gates = jnp.concatenate([jnp.concatenate(low, axis=1), jnp.concatenate(high, axis=1)], axis=0)

    def columns(p, q):
        if q in (0, rows + 1):
            return edges[p, 0 if q == 0 else 1]
        return inner[p - 1, q] if p in (1, 2) else outer[p // 3, q]

    lane = lax.broadcasted_iota(jnp.int32, (channels // 2, breadth), 1)
    for b in range(3):
        parts = []
        for p in range(4):
            across_rows = jnp.concatenate([columns(p, y + b) for y in range(rows)], axis=1)
            lhs = gates[0:channels] if p == 0 else gates[channels:] if p == 3 else gates
            parts.append(lax.dot_general(lhs, across_rows, across, preferred_element_type=F32))
        for a in range(3):
            low = parts[a][0:channels]
            high = parts[a + 1] if a == 2 else parts[a + 1][channels:]
            total = low + high
            base = (a * 3 + b) * 3 * channels // 2
            packed[base : base + channels] = total[:, 0:breadth].astype(BF16)
            rest = jnp.concatenate([total[:, breadth:], total[:, breadth:]], axis=1)
            mix = jnp.where(lane < channels, rest[0 : channels // 2], rest[channels // 2 :])
            packed[base + channels : base + 3 * channels // 2] = mix.astype(BF16)
    base = 9 * 3 * channels // 2
    source = lax.broadcasted_iota(jnp.int32, (2 * breadth, 2 * breadth), 0)
    target = lax.broadcasted_iota(jnp.int32, (2 * breadth, 2 * breadth), 1)
    wanted = 2 * (target % breadth) + target // breadth
    pick = jnp.where(source == wanted, 1.0, 0.0).astype(BF16)
    coarse = None
    for a in range(2):
        for b in range(2):
            pairs = []
            for pair in range(rows // 4):
                both = jnp.concatenate([h_ref[a, 4 * pair + b], h_ref[a, 4 * pair + 2 + b]], axis=1)
                pairs.append(jnp.dot(both, pick, preferred_element_type=F32).astype(BF16))
            hidden = jnp.concatenate(
                [jnp.concatenate([x[:, e * breadth : (e + 1) * breadth] for x in pairs], axis=1) for e in range(2)],
                axis=0,
            )
            term = jnp.dot(d_ref[a, b], hidden, preferred_element_type=F32)
            coarse = term if coarse is None else coarse + term
            down = lax.dot_general(cot_ref[...], hidden, across, preferred_element_type=F32)
            at = base + (2 * a + b) * d_ref.shape[2]
            packed[at : at + d_ref.shape[2]] = down.astype(BF16)
    out_ref[...] = coarse.astype(BF16)
    end = base + 4 * d_ref.shape[2]
    if end < packed.shape[0]:
        packed[end:] = jnp.zeros((packed.shape[0] - end, packed.shape[1]), BF16)
    half = packed.shape[0] // 2
    core = lax.rem(lax.axis_index("gy"), 2)
    keep[...] = packed[pl.ds(pl.multiple_of(core * half, 16), half)]
    send[...] = packed[pl.ds(pl.multiple_of((1 - core) * half, 16), half)]


def add_kernel(x, y, out):
    out[...] = (x[...].astype(F32) + y[...].astype(F32)).astype(BF16)


def total_kernel(terms, out):
    total = jnp.sum(terms[...].astype(F32), axis=0).astype(BF16)
    for member in range(out.shape[0]):
        out[member] = total


def field_kernel(near, far, near_in, far_in, w_ref, acc_ref, inner, outer):
    rows, channels, breadth = near.shape
    fill_columns(inner, near, far)
    fill_columns(outer, near_in, far_in)

    def step(t, carry):
        y = 2 * t
        own = inner_terms(inner, w_ref, y)
        rest = outer_terms(outer, w_ref, y)
        for z in range(2):
            total = own[z] + rest[z]
            for b in range(2):
                acc_ref[z, y + b] = total[:, b * breadth : (b + 1) * breadth]
        return carry

    lax.fori_loop(0, rows // 2, step, 0)


def field_edges_kernel(near, far, acc_ref, w_ref, out_ref, edges):
    rows, channels, breadth = acc_ref.shape[1:]
    fill_edges(edges, near, far)
    sides = [edge_terms(edges, w_ref, side) for side in range(2)]
    for z in range(2):
        for y in range(rows):
            line = acc_ref[z, y]
            if y in (0, rows - 1):
                line = line + sides[0 if y == 0 else 1][z]
            out_ref[pl.ds(z * rows + y, channels, stride=2 * rows), :] = line


def unpack_kernel(mine, other, conv_ref, down_ref, sums_ref, *, scale):
    half = mine.shape[0]
    core = lax.rem(lax.axis_index("gy"), 2)
    sums_ref[pl.ds(pl.multiple_of(core * half, 16), half)] = mine[...]
    sums_ref[pl.ds(pl.multiple_of((1 - core) * half, 16), half)] = other[...]
    channels = conv_ref.shape[2]
    for a in range(3):
        for b in range(3):
            base = (a * 3 + b) * 3 * channels // 2
            conv_ref[a, b, :, 0 : 2 * channels] = sums_ref[base : base + channels].astype(F32) * scale
            rest = sums_ref[base + channels : base + 3 * channels // 2].astype(F32) * scale
            conv_ref[a, b, 0 : channels // 2, 2 * channels :] = rest[:, 0:channels]
            conv_ref[a, b, channels // 2 :, 2 * channels :] = rest[:, channels:]
    base = 9 * 3 * channels // 2
    height = down_ref.shape[2]
    for a in range(2):
        for b in range(2):
            at = base + (2 * a + b) * height
            down_ref[a, b] = sums_ref[at : at + height].astype(F32) * scale


def swap(cells, axis, low):
    count = lax.axis_size(axis)
    pairs = [(i % count, (i + 1) % count) for i in range(low, low + count, 2)]
    return lax.ppermute(cells, axis, pairs + [(b, a) for a, b in pairs])


def swapped(near, far, axis):
    return swap(near, axis, 0), swap(far, axis, 1)


def body(features, conv_weight, down_weight, cotangent):
    channels, plane_count, row_count, breadth = features.shape
    out_channels = down_weight.shape[2]
    count = lax.axis_size("gz") * lax.axis_size("gy")
    grad_scale = 1.0 / math.sqrt(plane_count * row_count * breadth * count)
    turned = conv_weight.reshape(3, 3, channels, 3, channels)[::-1, ::-1, :, ::-1]
    weight_bwd = turned.transpose(0, 1, 4, 3, 2).reshape(3, 3, channels, 3 * channels)
    cot = cotangent.reshape(out_channels, -1)
    plane = ((row_count, channels, breadth), BF16)
    edge = ((plane_count + 2, channels, breadth), BF16)
    cols = ((plane_count, row_count + 2, 3 * channels, breadth), BF16)
    edge_cols = ((plane_count + 2, 2, 3 * channels, breadth), BF16)
    lines = (plane_count, row_count, channels, breadth)
    conv_flops = 2 * 27 * channels * channels * plane_count * row_count * breadth

    own = call(
        lines_kernel, [plane, plane], [((channels * plane_count * row_count, breadth), F32)], 0, (features,)
    )
    outside = swapped(*own, "gz")
    inner, acc, hidden_grad = call(
        inner_kernel, [cols, (lines, F32), (lines, F32)],
        [((out_channels, row_count // 2 * breadth), BF16)],
        2 * conv_flops // 3, (*own, conv_weight, down_weight, cot),
    )
    near, far, acc = lax.optimization_barrier((*outside, acc))
    outside = (near, far)
    beside = swapped(*call(edges_kernel, [edge, edge], [], 0, (*own, *outside)), "gy")
    outer, acc = call(
        outer_kernel, [cols, (lines, F32)], [], conv_flops // 3, (*outside, conv_weight, acc)
    )
    edges, near, far, hidden = call(
        gate_kernel, [edge_cols, plane, plane, (lines, BF16)], [], conv_flops // 10,
        (*beside, acc, hidden_grad, conv_weight),
    )
    gates = (near, far)

    chips = count // 2
    used = 27 * channels * channels // 128 + 4 * out_channels
    share = -(-used // (16 * count)) * 16
    half = ((chips * share, 128), BF16)
    section_out, keep, send = call(
        weight_grad_kernel, [((out_channels, cot.shape[1]), BF16), half, half],
        [((share * count, 128), BF16)], conv_flops,
        (inner, outer, edges, *gates, hidden, down_weight, cot),
    )
    (terms,) = call(add_kernel, [half], [], 0, (keep, swap(send, "gy", 0)))
    groups = [list(range(core, count, 2)) for core in range(2)]
    exchange = functools.partial(
        lax.all_to_all, axis_name=("gz", "gy"), split_axis=0, concat_axis=0, axis_index_groups=groups, tiled=True
    )
    parts = ((chips, share, 128), BF16)
    terms, near, far = lax.optimization_barrier((terms, *gates))
    gates = (near, far)
    terms = exchange(terms.reshape(parts[0]))
    outside = swapped(*gates, "gz")
    terms, near, far = lax.optimization_barrier((terms, *outside))
    outside = (near, far)
    (mine,) = call(total_kernel, [parts], [], 0, (terms,))
    sends = call(edges_kernel, [edge, edge], [], 0, (*gates, *outside))
    mine, near, far = lax.optimization_barrier((mine, *sends))
    sums = exchange(mine).reshape(half[0])
    beside = swapped(near, far, "gy")
    (acc,) = call(
        field_kernel, [(lines, F32)], [cols, cols], conv_flops, (*gates, *outside, weight_bwd)
    )
    (field,) = call(
        field_edges_kernel, [((channels * plane_count * row_count, breadth), F32)], [edge_cols],
        conv_flops // 10, (*beside, acc, weight_bwd),
    )
    sums, field = lax.optimization_barrier((sums, field))
    grad_conv, grad_down = call(
        functools.partial(unpack_kernel, scale=grad_scale),
        [(conv_weight.shape, F32), (down_weight.shape, F32)], [((share * count, 128), BF16)], 0,
        (sums, swap(sums, "gy", 0)),
    )
    section_out = section_out.reshape(out_channels, plane_count // 2, -1)
    return (section_out, field.reshape(features.shape), grad_conv, grad_down)


def solution(mesh):
    return jax.shard_map(
        body,
        mesh=mesh,
        in_specs=(P(None, "gz", "gy", None), P(), P(), P(None, "gz", "gy")),
        out_specs=(P(None, "gz", "gy"), P(None, "gz", "gy", None), P(), P()),
        check_vma=False,
    )
```

time: 66.2 us -> 56.4 us (0.85)
  blocking collectives: 15.2 us -> 0 us
  starting transfers between devices: 19.5 us -> 26.7 us
  Pallas kernels: 16.4 us -> 13.1 us
  local copies, waits for them, and re-layouts: 1.8 us -> 2.68 us
    all_to_all x1 -> x0, blocking collectives: 15.2 us -> none  [body(): exchange(terms.reshape(parts[0]))]
    all_to_all x0 -> x1, starting transfers between devices: none -> 5.87 us  [body(): terms = exchange(terms.reshape(parts[0]))]
    pallas_call x10 -> x12, Pallas kernels: 16.4 us -> 13.1 us  [call(): pl.pallas_call(kernel, out_shape=[jax.ShapeDtypeStruct(s, d) for s, d in...]
    all_to_all x1, waiting for transfers between devices: 0.01 us -> 1.61 us  [body(): sums = exchange(mine).reshape(half[0])]
    all_to_all x1, starting transfers between devices: 3.52 us -> 4.85 us  [body(): sums = exchange(mine).reshape(half[0])]
    ppermute x10, waiting for transfers between devices: 12.3 us -> 11.2 us  [swap(): return lax.ppermute(cells, axis, pairs + [(b, a) for a, b in pairs])]
    unnamed x9 -> x11, local copies, waits for them, and re-layouts: 1.24 us -> 2.18 us
  transfers between devices with their start and end apart: 11 -> 12, of which waited for: 7 -> 8; matrix products, arithmetic and copies ran while one was open for 1% -> 1% of each run, Pallas kernels for 11% -> 12%
where the time goes in v4:
time: 56.4 us; the launch traced here: 56.1 us
  starting transfers between devices  26.7 us (47%)
  Pallas kernels  13.1 us (23%)
  waiting for transfers between devices  12.9 us (23%)
  local copies, waits for them, and re-layouts  2.68 us (5%)
  between operations  0.77 us (1%)
    ppermute x10, starting transfers between devices, swap(): return lax.ppermute(cells, axis, pairs + [(b, a) for a, b in pairs])  15.9 us
    pallas_call x12, Pallas kernels, call(): pl.pallas_call(kernel, out_shape=[jax.ShapeDtypeStruct(s, d) for s, d in...  13.1 us
    ppermute x10, waiting for transfers between devices, swap(): return lax.ppermute(cells, axis, pairs + [(b, a) for a, b in pairs])  11.2 us
    all_to_all x1, starting transfers between devices, body(): terms = exchange(terms.reshape(parts[0]))  5.87 us
    all_to_all x1, starting transfers between devices, body(): sums = exchange(mine).reshape(half[0])  4.85 us
    unnamed x11, local copies, waits for them, and re-layouts  2.18 us
    all_to_all x1, waiting for transfers between devices, body(): sums = exchange(mine).reshape(half[0])  1.61 us
  transfers between devices with their start and end apart: 12, of which 8 were waited for; matrix products, arithmetic and copies ran while one was open for 1% of the time, Pallas kernels for 12%

profile of v4, /device:TPU:0, one launch (start us, length us, event | category | flops | bytes accessed | tf_op | source)
XLA Modules:
  0.0 56.1 jit_solution(71302709070672140)
XLA Ops:
  0.6 0.0 copy-start.2
  0.6 0.9 %copy-done.2 = bf16[64,2,8,128]{3,2,1,0:T(8,128)(2,1)S(1)} copy-done((bf16[64,2,8,128]{3,2,1,0:T(8,128)(2,1)S(1)}, bf16[64,2,8,128]{3,2,1,0:T(8,128)(2,1)}, u32[]{:S(2)}) %copy-start.2) | copy-done | bytes 262168
  1.6 0.0 copy-start.3
  1.6 0.0 copy-start.4
  1.6 0.2 shard_map.75
  1.8 3.0 %collective-permute-start = (bf16[8,64,128]{2,1,0:T(8,128)(2,1)S(1)}, bf16[8,64,128]{2,1,0:T(8,128)(2,1)S(1)}, u32[]{:S(2)}, u32[]{:S(2)}) collective-permute-start(bf16[8,64,128]{2,1,0:T(8,128)(2,1)S(1)} %get-tuple-element.38.near), channel_id=1, source_target_pairs={{0,4},{8,12},{16,20},{24,28},{4,0},{12,8},{20,16},{28,24},{1,5},{9... | collective-permute-start | bytes 393224 | tf_op jit(solution)/shard_map/ppermute | solution.py:322
  4.8 3.5 %collective-permute-start.1 = (bf16[8,64,128]{2,1,0:T(8,128)(2,1)S(1)}, bf16[8,64,128]{2,1,0:T(8,128)(2,1)S(1)}, u32[]{:S(2)}, u32[]{:S(2)}) collective-permute-start(bf16[8,64,128]{2,1,0:T(8,128)(2,1)S(1)} %get-tuple-element.39.far), channel_id=1, source_target_pairs={{4,8},{12,16},{20,24},{28,0},{8,4},{16,12},{24,20},{0,28},{5,9},{1... | collective-permute-start | bytes 393224 | tf_op jit(solution)/shard_map/ppermute | solution.py:322
  8.4 0.0 copy-done.3
  8.4 0.0 copy-done.4
  8.4 0.0 copy-start
  8.4 1.0 %copy-done = bf16[3,3,64,192]{3,2,1,0:T(8,128)(2,1)S(1)} copy-done((bf16[3,3,64,192]{3,2,1,0:T(8,128)(2,1)S(1)}, bf16[3,3,64,192]{3,2,1,0:T(8,128)(2,1)}, u32[]{:S(2)}) %copy-start) | copy-done | bytes 221208
  9.3 1.9 %shard_map.76 = (bf16[2,10,192,128]{3,2,1,0:T(8,128)(2,1)S(1)}, f32[2,8,64,128]{3,2,1,0:T(8,128)S(1)}, f32[2,8,64,128]{3,2,1,0:T(8,128)S(1)}) custom-call(bf16[8,64,128]{2,1,0:T(8,128)(2,1)S(1)} %get-tuple-element.38.near, bf16[8,64,128]{2,1,0:T(8,128)(2,1)S(1)} %get-tuple-element.39.far, bf16[3,3,64,192]{3,2,1,0:T(8,128)(2,1)S(1)} %copy-done, ...), custom_call_target="tpu_custom_call" | custom-call | flops 301989888 | bytes 2711552 | tf_op jit(solution)/shard_map/pallas_call | solution.py:20
  11.3 0.0 copy-start.1
  11.3 0.0 collective-permute-done.near.near_in
  11.3 1.2 %collective-permute-done.1.far.far_in = bf16[8,64,128]{2,1,0:T(8,128)(2,1)S(1)} collective-permute-done((bf16[8,64,128]{2,1,0:T(8,128)(2,1)S(1)}, bf16[8,64,128]{2,1,0:T(8,128)(2,1)S(1)}, u32[]{:S(2)}, u32[]{:S(2)}) %collective-permute-start.1) | collective-permute-done | bytes 131104 | tf_op jit(solution)/shard_map/ppermute | solution.py:322
  12.5 0.1 collective-permute-start.2
  12.6 1.6 %collective-permute-start.3 = (bf16[4,64,128]{2,1,0:T(8,128)(2,1)S(1)}, bf16[4,64,128]{2,1,0:T(8,128)(2,1)S(1)}, u32[]{:S(2)}, u32[]{:S(2)}) collective-permute-start(bf16[4,64,128]{2,1,0:T(8,128)(2,1)S(1)} %get-tuple-element.47), channel_id=1, source_target_pairs={{1,2},{3,0},{2,1},{0,3},{5,6},{7,4},{6,5},{4,7},{9,10},{11,8},{10,... | collective-permute-start | bytes 196616 | tf_op jit(solution)/shard_map/ppermute | solution.py:322
  14.2 0.0 copy-done.1
  14.2 1.4 %shard_map.77 = (bf16[2,10,192,128]{3,2,1,0:T(8,128)(2,1)S(1)}, f32[2,8,64,128]{3,2,1,0:T(8,128)S(1)}) custom-call(bf16[8,64,128]{2,1,0:T(8,128)(2,1)S(1)} %collective-permute-done.near.near_in, bf16[8,64,128]{2,1,0:T(8,128)(2,1)S(1)} %collective-permute-done.1.far.far_in, bf16[3,3,64,192]{3,2,1,0:T(8,128)(2,1)S(1)} %copy-done.1, ...), custom_call_target="tpu_custom_call" | custom-call | flops 150994944 | bytes 2514944 | tf_op jit(solution)/shard_map/pallas_call | solution.py:20
  15.6 0.0 collective-permute-done.2.near
  15.6 0.9 %collective-permute-done.3.far = bf16[4,64,128]{2,1,0:T(8,128)(2,1)S(1)} collective-permute-done((bf16[4,64,128]{2,1,0:T(8,128)(2,1)S(1)}, bf16[4,64,128]{2,1,0:T(8,128)(2,1)S(1)}, u32[]{:S(2)}, u32[]{:S(2)}) %collective-permute-start.3) | collective-permute-done | bytes 65568 | tf_op jit(solution)/shard_map/ppermute | solution.py:322
  16.5 0.5 shard_map.79
  17.0 3.0 %shard_map.80 = (bf16[128,256]{1,0:T(8,128)(2,1)}, bf16[768,128]{1,0:T(8,128)(2,1)S(1)}, bf16[768,128]{1,0:T(8,128)(2,1)S(1)}) custom-call(bf16[2,10,192,128]{3,2,1,0:T(8,128)(2,1)S(1)} %get-tuple-element.40.inner, bf16[2,10,192,128]{3,2,1,0:T(8,128)(2,1)S(1)} %get-tuple-element.45.outer, bf16[4,2,192,128]{3,2,1,0:T(8,128)(2,1)S(1)} %get-tuple-element.50.edges, ...), custom_call_target="tpu_custom_call" | custom-call | flops 452984832 | bytes 3538944 | tf_op jit(solution)/shard_map/pallas_call | solution.py:20
  20.0 0.4 collective-permute-start.4
  20.4 1.1 %collective-permute-done.4.y = bf16[768,128]{1,0:T(8,128)(2,1)S(1)} collective-permute-done((bf16[768,128]{1,0:T(8,128)(2,1)S(1)}, bf16[768,128]{1,0:T(8,128)(2,1)S(1)}, u32[]{:S(2)}, u32[]{:S(2)}) %collective-permute-start.4) | collective-permute-done | bytes 196640 | tf_op jit(solution)/shard_map/ppermute | solution.py:322
  21.5 0.7 %shard_map.81 = bf16[768,128]{1,0:T(8,128)(2,1)} custom-call(bf16[768,128]{1,0:T(8,128)(2,1)S(1)} %get-tuple-element.55.x, bf16[768,128]{1,0:T(8,128)(2,1)S(1)} %collective-permute-done.4.y), custom_call_target="tpu_custom_call" | custom-call | bytes 589824 | tf_op jit(solution)/shard_map/pallas_call | solution.py:20
  22.2 5.9 %all-to-all-start = ((bf16[16,48,128]{2,1,0:T(8,128)(2,1)}), bf16[16,48,128]{2,1,0:T(8,128)(2,1)S(1)}, u32[]{:S(2)}, u32[]{:S(2)}) async-start(bf16[16,48,128]{2,1,0:T(8,128)(2,1)} %bitcast.2), calls=%async_computation | async-start | bytes 393216 | tf_op jit(solution)/shard_map/all_to_all | solution.py:382
  28.1 1.9 %collective-permute-start.5 = (bf16[8,64,128]{2,1,0:T(8,128)(2,1)S(1)}, bf16[8,64,128]{2,1,0:T(8,128)(2,1)S(1)}, u32[]{:S(2)}, u32[]{:S(2)}) collective-permute-start(bf16[8,64,128]{2,1,0:T(8,128)(2,1)S(1)} %get-tuple-element.58.near), channel_id=1, source_target_pairs={{0,4},{8,12},{16,20},{24,28},{4,0},{12,8},{20,16},{28,24},{1,5},{9... | collective-permute-start | bytes 393224 | tf_op jit(solution)/shard_map/ppermute | solution.py:322
  30.0 3.3 %collective-permute-start.6 = (bf16[8,64,128]{2,1,0:T(8,128)(2,1)S(1)}, bf16[8,64,128]{2,1,0:T(8,128)(2,1)S(1)}, u32[]{:S(2)}, u32[]{:S(2)}) collective-permute-start(bf16[8,64,128]{2,1,0:T(8,128)(2,1)S(1)} %get-tuple-element.59.far), channel_id=1, source_target_pairs={{4,8},{12,16},{20,24},{28,0},{8,4},{16,12},{24,20},{0,28},{5,9},{1... | collective-permute-start | bytes 393224 | tf_op jit(solution)/shard_map/ppermute | solution.py:322
  33.2 4.0 %collective-permute-done.5.near_in = bf16[8,64,128]{2,1,0:T(8,128)(2,1)S(1)} collective-permute-done((bf16[8,64,128]{2,1,0:T(8,128)(2,1)S(1)}, bf16[8,64,128]{2,1,0:T(8,128)(2,1)S(1)}, u32[]{:S(2)}, u32[]{:S(2)}) %collective-permute-start.5) | collective-permute-done | bytes 131104 | tf_op jit(solution)/shard_map/ppermute | solution.py:322
  37.3 2.2 %collective-permute-done.6.far_in = bf16[8,64,128]{2,1,0:T(8,128)(2,1)S(1)} collective-permute-done((bf16[8,64,128]{2,1,0:T(8,128)(2,1)S(1)}, bf16[8,64,128]{2,1,0:T(8,128)(2,1)S(1)}, u32[]{:S(2)}, u32[]{:S(2)}) %collective-permute-start.6) | collective-permute-done | bytes 131104 | tf_op jit(solution)/shard_map/ppermute | solution.py:322
  39.5 0.0 all-to-all-done.terms
  39.5 0.7 %shard_map.82 = bf16[16,48,128]{2,1,0:T(8,128)(2,1)} custom-call(bf16[16,48,128]{2,1,0:T(8,128)(2,1)S(1)} %all-to-all-done.terms), custom_call_target="tpu_custom_call" | custom-call | bytes 393216 | tf_op jit(solution)/shard_map/pallas_call | solution.py:20
  40.3 4.9 %all-to-all-start.1 = ((bf16[16,48,128]{2,1,0:T(8,128)(2,1)}), bf16[16,48,128]{2,1,0:T(8,128)(2,1)S(1)}, u32[]{:S(2)}, u32[]{:S(2)}) async-start(bf16[16,48,128]{2,1,0:T(8,128)(2,1)} %shard_map.82), calls=%async_computation.1 | async-start | bytes 393216 | tf_op jit(solution)/shard_map/all_to_all | solution.py:389
  45.1 0.3 copy.9
  45.4 0.1 collective-permute-start.7
  45.5 2.0 %collective-permute-start.8 = (bf16[4,64,128]{2,1,0:T(8,128)(2,1)S(1)}, bf16[4,64,128]{2,1,0:T(8,128)(2,1)S(1)}, u32[]{:S(2)}, u32[]{:S(2)}) collective-permute-start(bf16[4,64,128]{2,1,0:T(8,128)(2,1)S(1)} %get-tuple-element.67), channel_id=1, source_target_pairs={{1,2},{3,0},{2,1},{0,3},{5,6},{7,4},{6,5},{4,7},{9,10},{11,8},{10,... | collective-permute-start | bytes 196616 | tf_op jit(solution)/shard_map/ppermute | solution.py:322
  47.6 0.2 copy.10
  47.8 0.2 copy.11.w_ref
  48.0 2.3 %shard_map.84.acc_ref = f32[2,8,64,128]{3,2,1,0:T(8,128)S(1)} custom-call(bf16[8,64,128]{2,1,0:T(8,128)(2,1)S(1)} %get-tuple-element.58.near, bf16[8,64,128]{2,1,0:T(8,128)(2,1)S(1)} %get-tuple-element.59.far, bf16[8,64,128]{2,1,0:T(8,128)(2,1)S(1)} %collective-permute-done.5.near_in, bf16[8,64,128]{2,1,0:T(8,128)(2,1)S(1)} %collective-permute-done.6.far_in, ...), custom_call_target="tpu_custom_call" | custom-call | flops 452984832 | bytes 1269760 | tf_op jit(solution)/shard_map/pallas_call | solution.py:20
  50.3 0.0 collective-permute-done.7.near
  50.3 0.3 collective-permute-done.8.far
  50.7 1.3 %shard_map.85 = f32[1024,128]{1,0:T(8,128)} custom-call(bf16[4,64,128]{2,1,0:T(8,128)(2,1)S(1)} %collective-permute-done.7.near, bf16[4,64,128]{2,1,0:T(8,128)(2,1)S(1)} %collective-permute-done.8.far, f32[2,8,64,128]{3,2,1,0:T(8,128)S(1)} %shard_map.84.acc_ref, bf16[3,3,64,192]{3,2,1,0:T(8,128)(2,1)S(1)} %copy.11.w_ref), custom_call_target="tpu_custom_call" | custom-call | flops 45298484 | bytes 1400832 | tf_op jit(solution)/shard_map/pallas_call | solution.py:20
  52.0 1.6 %all-to-all-done.1 = bf16[16,48,128]{2,1,0:T(8,128)(2,1)S(1)} async-done(((bf16[16,48,128]{2,1,0:T(8,128)(2,1)}), bf16[16,48,128]{2,1,0:T(8,128)(2,1)S(1)}, u32[]{:S(2)}, u32[]{:S(2)}) %all-to-all-start.1) | async-done | bytes 196640 | tf_op jit(solution)/shard_map/all_to_all | solution.py:389
  53.6 0.0 collective-permute-start.9
  53.6 1.4 %collective-permute-done.9.other = bf16[768,128]{1,0:T(8,128)(2,1)S(1)} collective-permute-done((bf16[768,128]{1,0:T(8,128)(2,1)S(1)}, bf16[768,128]{1,0:T(8,128)(2,1)S(1)}, u32[]{:S(2)}, u32[]{:S(2)}) %collective-permute-start.9) | collective-permute-done | bytes 196640 | tf_op jit(solution)/shard_map/ppermute | solution.py:322
  55.1 1.0 %shard_map.86 = (f32[3,3,64,192]{3,2,1,0:T(8,128)}, f32[2,2,128,128]{3,2,1,0:T(8,128)}) custom-call(bf16[768,128]{1,0:T(8,128)(2,1)S(1)} %bitcast.10, bf16[768,128]{1,0:T(8,128)(2,1)S(1)} %collective-permute-done.9.other), custom_call_target="tpu_custom_call" | custom-call | bytes 1097728 | tf_op jit(solution)/shard_map/pallas_call | solution.py:20
  (3 shorter events, 0.1 us)
Async XLA Ops:
  0.6 1.0 %copy-start.2 = (bf16[64,2,8,128]{3,2,1,0:T(8,128)(2,1)S(1)}, bf16[64,2,8,128]{3,2,1,0:T(8,128)(2,1)}, u32[]{:S(2)}) copy-start(bf16[64,2,8,128]{3,2,1,0:T(8,128)(2,1)} %f_ref.1) | copy-start | bytes 786436
  1.6 6.8 %copy-start.3 = (bf16[2,2,128,128]{3,2,1,0:T(8,128)(2,1)S(1)}, bf16[2,2,128,128]{3,2,1,0:T(8,128)(2,1)}, u32[]{:S(2)}) copy-start(bf16[2,2,128,128]{3,2,1,0:T(8,128)(2,1)} %d_ref.3) | copy-start | bytes 393220
  1.6 6.8 %copy-start.4 = (bf16[128,1,256]{2,0,1:T(8,128)(2,1)S(1)}, bf16[128,1,256]{2,0,1:T(8,128)(2,1)}, u32[]{:S(2)}) copy-start(bf16[128,1,256]{2,0,1:T(8,128)(2,1)} %param.7) | copy-start | bytes 196612
  1.8 9.5 %collective-permute-start = (bf16[8,64,128]{2,1,0:T(8,128)(2,1)S(1)}, bf16[8,64,128]{2,1,0:T(8,128)(2,1)S(1)}, u32[]{:S(2)}, u32[]{:S(2)}) collective-permute-start(bf16[8,64,128]{2,1,0:T(8,128)(2,1)S(1)} %get-tuple-element.38.near), channel_id=1, source_target_pairs={{0,4},{8,12},{16,20},{24,28},{4,0},{12,8},{20,16},{28,24},{1,5},{9... | collective-permute-start | bytes 393224 | tf_op jit(solution)/shard_map/ppermute | solution.py:322
  4.8 7.7 %collective-permute-start.1 = (bf16[8,64,128]{2,1,0:T(8,128)(2,1)S(1)}, bf16[8,64,128]{2,1,0:T(8,128)(2,1)S(1)}, u32[]{:S(2)}, u32[]{:S(2)}) collective-permute-start(bf16[8,64,128]{2,1,0:T(8,128)(2,1)S(1)} %get-tuple-element.39.far), channel_id=1, source_target_pairs={{4,8},{12,16},{20,24},{28,0},{8,4},{16,12},{24,20},{0,28},{5,9},{1... | collective-permute-start | bytes 393224 | tf_op jit(solution)/shard_map/ppermute | solution.py:322
  8.4 1.0 %copy-start = (bf16[3,3,64,192]{3,2,1,0:T(8,128)(2,1)S(1)}, bf16[3,3,64,192]{3,2,1,0:T(8,128)(2,1)}, u32[]{:S(2)}) copy-start(bf16[3,3,64,192]{3,2,1,0:T(8,128)(2,1)} %w_ref.5) | copy-start | bytes 663556
  11.3 3.0 %copy-start.1 = (bf16[3,3,64,192]{3,2,1,0:T(8,128)(2,1)S(1)}, bf16[3,3,64,192]{3,2,1,0:T(8,128)(2,1)}, u32[]{:S(2)}) copy-start(bf16[3,3,64,192]{3,2,1,0:T(8,128)(2,1)} %w_ref.5) | copy-start | bytes 663556
  12.5 3.1 %collective-permute-start.2 = (bf16[4,64,128]{2,1,0:T(8,128)(2,1)S(1)}, bf16[4,64,128]{2,1,0:T(8,128)(2,1)S(1)}, u32[]{:S(2)}, u32[]{:S(2)}) collective-permute-start(bf16[4,64,128]{2,1,0:T(8,128)(2,1)S(1)} %get-tuple-element.46), channel_id=1, source_target_pairs={{0,1},{2,3},{1,0},{3,2},{4,5},{6,7},{5,4},{7,6},{8,9},{10,11},{9,8... | collective-permute-start | bytes 196616 | tf_op jit(solution)/shard_map/ppermute | solution.py:322
  12.6 3.9 %collective-permute-start.3 = (bf16[4,64,128]{2,1,0:T(8,128)(2,1)S(1)}, bf16[4,64,128]{2,1,0:T(8,128)(2,1)S(1)}, u32[]{:S(2)}, u32[]{:S(2)}) collective-permute-start(bf16[4,64,128]{2,1,0:T(8,128)(2,1)S(1)} %get-tuple-element.47), channel_id=1, source_target_pairs={{1,2},{3,0},{2,1},{0,3},{5,6},{7,4},{6,5},{4,7},{9,10},{11,8},{10,... | collective-permute-start | bytes 196616 | tf_op jit(solution)/shard_map/ppermute | solution.py:322
  20.0 1.5 %collective-permute-start.4 = (bf16[768,128]{1,0:T(8,128)(2,1)S(1)}, bf16[768,128]{1,0:T(8,128)(2,1)S(1)}, u32[]{:S(2)}, u32[]{:S(2)}) collective-permute-start(bf16[768,128]{1,0:T(8,128)(2,1)S(1)} %get-tuple-element.56), channel_id=1, source_target_pairs={{0,1},{2,3},{1,0},{3,2},{4,5},{6,7},{5,4},{7,6},{8,9},{10,11},{9,8... | collective-permute-start | bytes 589832 | tf_op jit(solution)/shard_map/ppermute | solution.py:322
  22.2 17.3 %all-to-all-start = ((bf16[16,48,128]{2,1,0:T(8,128)(2,1)}), bf16[16,48,128]{2,1,0:T(8,128)(2,1)S(1)}, u32[]{:S(2)}, u32[]{:S(2)}) async-start(bf16[16,48,128]{2,1,0:T(8,128)(2,1)} %bitcast.2), calls=%async_computation | async-start | bytes 393216 | tf_op jit(solution)/shard_map/all_to_all | solution.py:382
  28.1 9.2 %collective-permute-start.5 = (bf16[8,64,128]{2,1,0:T(8,128)(2,1)S(1)}, bf16[8,64,128]{2,1,0:T(8,128)(2,1)S(1)}, u32[]{:S(2)}, u32[]{:S(2)}) collective-permute-start(bf16[8,64,128]{2,1,0:T(8,128)(2,1)S(1)} %get-tuple-element.58.near), channel_id=1, source_target_pairs={{0,4},{8,12},{16,20},{24,28},{4,0},{12,8},{20,16},{28,24},{1,5},{9... | collective-permute-start | bytes 393224 | tf_op jit(solution)/shard_map/ppermute | solution.py:322
  30.0 9.5 %collective-permute-start.6 = (bf16[8,64,128]{2,1,0:T(8,128)(2,1)S(1)}, bf16[8,64,128]{2,1,0:T(8,128)(2,1)S(1)}, u32[]{:S(2)}, u32[]{:S(2)}) collective-permute-start(bf16[8,64,128]{2,1,0:T(8,128)(2,1)S(1)} %get-tuple-element.59.far), channel_id=1, source_target_pairs={{4,8},{12,16},{20,24},{28,0},{8,4},{16,12},{24,20},{0,28},{5,9},{1... | collective-permute-start | bytes 393224 | tf_op jit(solution)/shard_map/ppermute | solution.py:322
  40.3 13.3 %all-to-all-start.1 = ((bf16[16,48,128]{2,1,0:T(8,128)(2,1)}), bf16[16,48,128]{2,1,0:T(8,128)(2,1)S(1)}, u32[]{:S(2)}, u32[]{:S(2)}) async-start(bf16[16,48,128]{2,1,0:T(8,128)(2,1)} %shard_map.82), calls=%async_computation.1 | async-start | bytes 393216 | tf_op jit(solution)/shard_map/all_to_all | solution.py:389
  45.4 4.9 %collective-permute-start.7 = (bf16[4,64,128]{2,1,0:T(8,128)(2,1)S(1)}, bf16[4,64,128]{2,1,0:T(8,128)(2,1)S(1)}, u32[]{:S(2)}, u32[]{:S(2)}) collective-permute-start(bf16[4,64,128]{2,1,0:T(8,128)(2,1)S(1)} %get-tuple-element.66), channel_id=1, source_target_pairs={{0,1},{2,3},{1,0},{3,2},{4,5},{6,7},{5,4},{7,6},{8,9},{10,11},{9,8... | collective-permute-start | bytes 196616 | tf_op jit(solution)/shard_map/ppermute | solution.py:322
  45.5 5.2 %collective-permute-start.8 = (bf16[4,64,128]{2,1,0:T(8,128)(2,1)S(1)}, bf16[4,64,128]{2,1,0:T(8,128)(2,1)S(1)}, u32[]{:S(2)}, u32[]{:S(2)}) collective-permute-start(bf16[4,64,128]{2,1,0:T(8,128)(2,1)S(1)} %get-tuple-element.67), channel_id=1, source_target_pairs={{1,2},{3,0},{2,1},{0,3},{5,6},{7,4},{6,5},{4,7},{9,10},{11,8},{10,... | collective-permute-start | bytes 196616 | tf_op jit(solution)/shard_map/ppermute | solution.py:322
  53.6 1.4 %collective-permute-start.9 = (bf16[768,128]{1,0:T(8,128)(2,1)S(1)}, bf16[768,128]{1,0:T(8,128)(2,1)S(1)}, u32[]{:S(2)}, u32[]{:S(2)}) collective-permute-start(bf16[768,128]{1,0:T(8,128)(2,1)S(1)} %bitcast.9), channel_id=1, source_target_pairs={{0,1},{2,3},{1,0},{3,2},{4,5},{6,7},{5,4},{7,6},{8,9},{10,11},{9,8... | collective-permute-start | bytes 589832 | tf_op jit(solution)/shard_map/ppermute | solution.py:322

commit v5 on v4

--- a/solution.py
+++ b/solution.py
@@ -220,10 +220,10 @@
             high = parts[a + 1] if a == 2 else parts[a + 1][channels:]
             total = low + high
             base = (a * 3 + b) * 3 * channels // 2
-            packed[base : base + channels] = total[:, 0:breadth].astype(BF16)
+            packed[base : base + channels] = total[:, 0:breadth]
             rest = jnp.concatenate([total[:, breadth:], total[:, breadth:]], axis=1)
             mix = jnp.where(lane < channels, rest[0 : channels // 2], rest[channels // 2 :])
-            packed[base + channels : base + 3 * channels // 2] = mix.astype(BF16)
+            packed[base + channels : base + 3 * channels // 2] = mix
     base = 9 * 3 * channels // 2
     source = lax.broadcasted_iota(jnp.int32, (2 * breadth, 2 * breadth), 0)
     target = lax.broadcasted_iota(jnp.int32, (2 * breadth, 2 * breadth), 1)
@@ -244,25 +244,43 @@
             coarse = term if coarse is None else coarse + term
             down = lax.dot_general(cot_ref[...], hidden, across, preferred_element_type=F32)
             at = base + (2 * a + b) * d_ref.shape[2]
-            packed[at : at + d_ref.shape[2]] = down.astype(BF16)
+            packed[at : at + d_ref.shape[2]] = down
     out_ref[...] = coarse.astype(BF16)
     end = base + 4 * d_ref.shape[2]
     if end < packed.shape[0]:
-        packed[end:] = jnp.zeros((packed.shape[0] - end, packed.shape[1]), BF16)
+        packed[end:] = jnp.zeros((packed.shape[0] - end, packed.shape[1]), F32)
     half = packed.shape[0] // 2
-    core = lax.rem(lax.axis_index("gy"), 2)
-    keep[...] = packed[pl.ds(pl.multiple_of(core * half, 16), half)]
-    send[...] = packed[pl.ds(pl.multiple_of((1 - core) * half, 16), half)]
+    split(packed, keep, send, half, "gy", 1)
+
+
+def side_of(axis, bit):
+    return lax.rem(lax.axis_index(axis) // bit, 2)
+
+
+def part(side, rows):
+    return pl.ds(pl.multiple_of(side * rows, 16), rows)
+
+
+def split(packed, keep, send, half, axis, bit):
+    side = side_of(axis, bit)
+    keep[...] = packed[part(side, half)]
+    send[...] = packed[part(1 - side, half)].astype(BF16)
+
+
+def halve_kernel(mine, other, keep, send, total, *, axis, bit):
+    total[...] = mine[...] + other[...].astype(F32)
+    split(total, keep, send, total.shape[0] // 2, axis, bit)
 
 
 def add_kernel(x, y, out):
     out[...] = (x[...].astype(F32) + y[...].astype(F32)).astype(BF16)
 
 
-def total_kernel(terms, out):
-    total = jnp.sum(terms[...].astype(F32), axis=0).astype(BF16)
-    for member in range(out.shape[0]):
-        out[member] = total
+def join_kernel(mine, other, out, *, axis, bit):
+    rows = mine.shape[0]
+    side = side_of(axis, bit)
+    out[part(side, rows)] = mine[...]
+    out[part(1 - side, rows)] = other[...]
 
 
 def field_kernel(near, far, near_in, far_in, w_ref, acc_ref, inner, outer):
@@ -296,10 +314,7 @@
 
 
 def unpack_kernel(mine, other, conv_ref, down_ref, sums_ref, *, scale):
-    half = mine.shape[0]
-    core = lax.rem(lax.axis_index("gy"), 2)
-    sums_ref[pl.ds(pl.multiple_of(core * half, 16), half)] = mine[...]
-    sums_ref[pl.ds(pl.multiple_of((1 - core) * half, 16), half)] = other[...]
+    join_kernel(mine, other, sums_ref, axis="gy", bit=1)
     channels = conv_ref.shape[2]
     for a in range(3):
         for b in range(3):
@@ -322,6 +337,15 @@
     return lax.ppermute(cells, axis, pairs + [(b, a) for a, b in pairs])
 
 
+def flip(cells, axis, bit):
+    return lax.ppermute(cells, axis, [(i, i ^ bit) for i in range(lax.axis_size(axis))])
+
+
+def tied(first, *others):
+    found = lax.optimization_barrier((first, *others))
+    return found[0], tuple(found[1:])
+
+
 def swapped(near, far, axis):
     return swap(near, axis, 0), swap(far, axis, 1)
 
@@ -362,44 +386,58 @@
     )
     gates = (near, far)
 
-    chips = count // 2
     used = 27 * channels * channels // 128 + 4 * out_channels
-    share = -(-used // (16 * count)) * 16
-    half = ((chips * share, 128), BF16)
+    rows = -(-used // 128) * 128
     section_out, keep, send = call(
-        weight_grad_kernel, [((out_channels, cot.shape[1]), BF16), half, half],
-        [((share * count, 128), BF16)], conv_flops,
+        weight_grad_kernel,
+        [((out_channels, cot.shape[1]), BF16), ((rows // 2, 128), F32), ((rows // 2, 128), BF16)],
+        [((rows, 128), F32)], conv_flops,
         (inner, outer, edges, *gates, hidden, down_weight, cot),
     )
-    (terms,) = call(add_kernel, [half], [], 0, (keep, swap(send, "gy", 0)))
-    groups = [list(range(core, count, 2)) for core in range(2)]
-    exchange = functools.partial(
-        lax.all_to_all, axis_name=("gz", "gy"), split_axis=0, concat_axis=0, axis_index_groups=groups, tiled=True
-    )
-    parts = ((chips, share, 128), BF16)
-    terms, near, far = lax.optimization_barrier((terms, *gates))
-    gates = (near, far)
-    terms = exchange(terms.reshape(parts[0]))
-    outside = swapped(*gates, "gz")
-    terms, near, far = lax.optimization_barrier((terms, *outside))
-    outside = (near, far)
-    (mine,) = call(total_kernel, [parts], [], 0, (terms,))
+    keep, gates = tied(keep, *gates)
+    near, far = gates
+    near_in = swap(near, "gz", 0)
+    for level, (axis, bit) in enumerate((("gy", 2), ("gz", 1))):
+        size = rows >> (level + 2)
+        mine, got = keep, flip(send, *(("gy", 1), ("gy", 2))[level])
+        keep, send = call(
+            functools.partial(halve_kernel, axis=axis, bit=bit),
+            [((size, 128), F32), ((size, 128), BF16)], [((2 * size, 128), F32)], 0, (mine, got),
+        )
+        if level == 0:
+            keep, (far,) = tied(keep, far)
+            far_in = swap(far, "gz", 1)
+    shard = ((rows // 8, 128), BF16)
+    (sums,) = call(add_kernel, [shard], [], 0, (keep, flip(send, "gz", 1)))
+    sums, outside = tied(sums, near_in, far_in)
     sends = call(edges_kernel, [edge, edge], [], 0, (*gates, *outside))
-    mine, near, far = lax.optimization_barrier((mine, *sends))
-    sums = exchange(mine).reshape(half[0])
-    beside = swapped(near, far, "gy")
+    beside = swapped(*sends, "gy")
     (acc,) = call(
         field_kernel, [(lines, F32)], [cols, cols], conv_flops, (*gates, *outside, weight_bwd)
     )
+    wide = [("gy", 1 << k) for k in range(2, lax.axis_size("gy").bit_length() - 1)]
+    wide += [("gz", 1 << k) for k in range(1, lax.axis_size("gz").bit_length() - 1)]
+    for axis, bit in wide:
+        (sums,) = call(add_kernel, [shard], [], 0, (sums, flip(sums, axis, bit)))
+    sums, beside = tied(sums, *beside)
+    (sums,) = call(
+        functools.partial(join_kernel, axis="gz", bit=1), [((rows // 4, 128), BF16)], [], 0,
+        (sums, flip(sums, "gz", 1)),
+    )
+    sums, (acc,) = tied(sums, acc)
     (field,) = call(
         field_edges_kernel, [((channels * plane_count * row_count, breadth), F32)], [edge_cols],
         conv_flops // 10, (*beside, acc, weight_bwd),
     )
-    sums, field = lax.optimization_barrier((sums, field))
+    (sums,) = call(
+        functools.partial(join_kernel, axis="gy", bit=2), [((rows // 2, 128), BF16)], [], 0,
+        (sums, flip(sums, "gy", 2)),
+    )
+    sums, (field,) = tied(sums, field)
     grad_conv, grad_down = call(
         functools.partial(unpack_kernel, scale=grad_scale),
-        [(conv_weight.shape, F32), (down_weight.shape, F32)], [((share * count, 128), BF16)], 0,
-        (sums, swap(sums, "gy", 0)),
+        [(conv_weight.shape, F32), (down_weight.shape, F32)], [((rows, 128), BF16)], 0,
+        (sums, flip(sums, "gy", 1)),
     )
     section_out = section_out.reshape(out_channels, plane_count // 2, -1)
     return (section_out, field.reshape(features.shape), grad_conv, grad_down)

time: 56.4 us -> 53.3 us (0.945)
  starting transfers between devices: 26.7 us -> 17.7 us
  waiting for transfers between devices: 12.9 us -> 20.1 us
  Pallas kernels: 13.1 us -> 11.8 us
    ppermute x0 -> x8, waiting for transfers between devices: none -> 18 us  [flip(): lax.ppermute(cells, axis, [(i, i ^ bit) for i in range(lax.axis_size(axis...]
    all_to_all x2 -> x0, starting transfers between devices: 10.7 us -> none  [the longest x1 5.87 us: body(): terms = exchange(terms.reshape(parts[0]))]
    ppermute x10 -> x8, waiting for transfers between devices: 11.2 us -> 2.13 us  [swap(): return lax.ppermute(cells, axis, pairs + [(b, a) for a, b in pairs])]
    ppermute x0 -> x8, starting transfers between devices: none -> 4.81 us  [flip(): lax.ppermute(cells, axis, [(i, i ^ bit) for i in range(lax.axis_size(axis...]
    ppermute x10 -> x8, starting transfers between devices: 15.9 us -> 12.9 us  [swap(): return lax.ppermute(cells, axis, pairs + [(b, a) for a, b in pairs])]
    all_to_all x2 -> x0, waiting for transfers between devices: 1.61 us -> none  [the longest x1 1.61 us: body(): sums = exchange(mine).reshape(half[0])]
    pallas_call x12 -> x17, Pallas kernels: 13.1 us -> 11.8 us  [call(): pl.pallas_call(kernel, out_shape=[jax.ShapeDtypeStruct(s, d) for s, d in...]
  transfers between devices with their start and end apart: 12 -> 16, of which waited for: 8 -> 9; matrix products, arithmetic and copies ran while one was open for 1% -> 1% of each run, Pallas kernels for 12% -> 13%
where the time goes in v5:
time: 53.3 us; the launch traced here: 53.1 us
  waiting for transfers between devices  20.1 us (38%)
  starting transfers between devices  17.7 us (33%)
  Pallas kernels  11.8 us (22%)
  local copies, waits for them, and re-layouts  2.7 us (5%)
  between operations  0.83 us (2%)
    ppermute x8, waiting for transfers between devices, flip(): lax.ppermute(cells, axis, [(i, i ^ bit) for i in range(lax.axis_size(axis...  18 us
    ppermute x8, starting transfers between devices, swap(): return lax.ppermute(cells, axis, pairs + [(b, a) for a, b in pairs])  12.9 us
    pallas_call x17, Pallas kernels, call(): pl.pallas_call(kernel, out_shape=[jax.ShapeDtypeStruct(s, d) for s, d in...  11.8 us
    ppermute x8, starting transfers between devices, flip(): lax.ppermute(cells, axis, [(i, i ^ bit) for i in range(lax.axis_size(axis...  4.81 us
    unnamed x11, local copies, waits for them, and re-layouts  2.18 us
    ppermute x8, waiting for transfers between devices, swap(): return lax.ppermute(cells, axis, pairs + [(b, a) for a, b in pairs])  2.13 us
  transfers between devices with their start and end apart: 16, of which 9 were waited for; matrix products, arithmetic and copies ran while one was open for 1% of the time, Pallas kernels for 13%

profile of v5, /device:TPU:0, one launch (start us, length us, event | category | flops | bytes accessed | tf_op | source)
XLA Modules:
  0.0 53.1 jit_solution(16685548595581362279)
XLA Ops:
  0.6 0.9 %copy-done.2 = bf16[64,2,8,128]{3,2,1,0:T(8,128)(2,1)S(1)} copy-done((bf16[64,2,8,128]{3,2,1,0:T(8,128)(2,1)S(1)}, bf16[64,2,8,128]{3,2,1,0:T(8,128)(2,1)}, u32[]{:S(2)}) %copy-start.2) | copy-done | bytes 262168
  1.6 0.2 shard_map.75
  1.8 3.0 %collective-permute-start = (bf16[8,64,128]{2,1,0:T(8,128)(2,1)S(1)}, bf16[8,64,128]{2,1,0:T(8,128)(2,1)S(1)}, u32[]{:S(2)}, u32[]{:S(2)}) collective-permute-start(bf16[8,64,128]{2,1,0:T(8,128)(2,1)S(1)} %get-tuple-element.46.near), channel_id=1, source_target_pairs={{0,4},{8,12},{16,20},{24,28},{4,0},{12,8},{20,16},{28,24},{1,5},{9... | collective-permute-start | bytes 393224 | tf_op jit(solution)/shard_map/ppermute | solution.py:337
  4.8 3.5 %collective-permute-start.1 = (bf16[8,64,128]{2,1,0:T(8,128)(2,1)S(1)}, bf16[8,64,128]{2,1,0:T(8,128)(2,1)S(1)}, u32[]{:S(2)}, u32[]{:S(2)}) collective-permute-start(bf16[8,64,128]{2,1,0:T(8,128)(2,1)S(1)} %get-tuple-element.47.far), channel_id=1, source_target_pairs={{4,8},{12,16},{20,24},{28,0},{8,4},{16,12},{24,20},{0,28},{5,9},{1... | collective-permute-start | bytes 393224 | tf_op jit(solution)/shard_map/ppermute | solution.py:337
  8.4 0.0 copy-done.4
  8.4 1.0 %copy-done = bf16[3,3,64,192]{3,2,1,0:T(8,128)(2,1)S(1)} copy-done((bf16[3,3,64,192]{3,2,1,0:T(8,128)(2,1)S(1)}, bf16[3,3,64,192]{3,2,1,0:T(8,128)(2,1)}, u32[]{:S(2)}) %copy-start) | copy-done | bytes 221208
  9.3 1.9 %shard_map.76 = (bf16[2,10,192,128]{3,2,1,0:T(8,128)(2,1)S(1)}, f32[2,8,64,128]{3,2,1,0:T(8,128)S(1)}, f32[2,8,64,128]{3,2,1,0:T(8,128)S(1)}) custom-call(bf16[8,64,128]{2,1,0:T(8,128)(2,1)S(1)} %get-tuple-element.46.near, bf16[8,64,128]{2,1,0:T(8,128)(2,1)S(1)} %get-tuple-element.47.far, bf16[3,3,64,192]{3,2,1,0:T(8,128)(2,1)S(1)} %copy-done, ...), custom_call_target="tpu_custom_call" | custom-call | flops 301989888 | bytes 2711552 | tf_op jit(solution)/shard_map/pallas_call | solution.py:20
  11.3 0.0 copy-start.1
  11.3 0.0 collective-permute-done.near.near_in
  11.3 1.2 %collective-permute-done.1.far.far_in = bf16[8,64,128]{2,1,0:T(8,128)(2,1)S(1)} collective-permute-done((bf16[8,64,128]{2,1,0:T(8,128)(2,1)S(1)}, bf16[8,64,128]{2,1,0:T(8,128)(2,1)S(1)}, u32[]{:S(2)}, u32[]{:S(2)}) %collective-permute-start.1) | collective-permute-done | bytes 131104 | tf_op jit(solution)/shard_map/ppermute | solution.py:337
  12.5 0.1 collective-permute-start.2
  12.6 1.6 %collective-permute-start.3 = (bf16[4,64,128]{2,1,0:T(8,128)(2,1)S(1)}, bf16[4,64,128]{2,1,0:T(8,128)(2,1)S(1)}, u32[]{:S(2)}, u32[]{:S(2)}) collective-permute-start(bf16[4,64,128]{2,1,0:T(8,128)(2,1)S(1)} %get-tuple-element.55), channel_id=1, source_target_pairs={{1,2},{3,0},{2,1},{0,3},{5,6},{7,4},{6,5},{4,7},{9,10},{11,8},{10,... | collective-permute-start | bytes 196616 | tf_op jit(solution)/shard_map/ppermute | solution.py:337
  14.2 1.4 %shard_map.77 = (bf16[2,10,192,128]{3,2,1,0:T(8,128)(2,1)S(1)}, f32[2,8,64,128]{3,2,1,0:T(8,128)S(1)}) custom-call(bf16[8,64,128]{2,1,0:T(8,128)(2,1)S(1)} %collective-permute-done.near.near_in, bf16[8,64,128]{2,1,0:T(8,128)(2,1)S(1)} %collective-permute-done.1.far.far_in, bf16[3,3,64,192]{3,2,1,0:T(8,128)(2,1)S(1)} %copy-done.1, ...), custom_call_target="tpu_custom_call" | custom-call | flops 150994944 | bytes 2514944 | tf_op jit(solution)/shard_map/pallas_call | solution.py:20
  15.6 0.0 collective-permute-done.2.near
  15.6 0.9 %collective-permute-done.3.far = bf16[4,64,128]{2,1,0:T(8,128)(2,1)S(1)} collective-permute-done((bf16[4,64,128]{2,1,0:T(8,128)(2,1)S(1)}, bf16[4,64,128]{2,1,0:T(8,128)(2,1)S(1)}, u32[]{:S(2)}, u32[]{:S(2)}) %collective-permute-start.3) | collective-permute-done | bytes 65568 | tf_op jit(solution)/shard_map/ppermute | solution.py:337
  16.5 0.5 shard_map.79
  17.0 3.0 %shard_map.80 = (bf16[128,256]{1,0:T(8,128)(2,1)}, f32[704,128]{1,0:T(8,128)S(1)}, bf16[704,128]{1,0:T(8,128)(2,1)S(1)}) custom-call(bf16[2,10,192,128]{3,2,1,0:T(8,128)(2,1)S(1)} %get-tuple-element.48.inner, bf16[2,10,192,128]{3,2,1,0:T(8,128)(2,1)S(1)} %get-tuple-element.53.outer, bf16[4,2,192,128]{3,2,1,0:T(8,128)(2,1)S(1)} %get-tuple-element.58.edges, ...), custom_call_target="tpu_custom_call" | custom-call | flops 452984832 | bytes 3686400 | tf_op jit(solution)/shard_map/pallas_call | solution.py:20
  20.0 0.4 collective-permute-start.4
  20.4 1.0 %collective-permute-done.4.other = bf16[704,128]{1,0:T(8,128)(2,1)S(1)} collective-permute-done((bf16[704,128]{1,0:T(8,128)(2,1)S(1)}, bf16[704,128]{1,0:T(8,128)(2,1)S(1)}, u32[]{:S(2)}, u32[]{:S(2)}) %collective-permute-start.4) | collective-permute-done | bytes 180256 | tf_op jit(solution)/shard_map/ppermute | solution.py:341
  21.4 0.1 shard_map.81
  21.5 1.6 %collective-permute-start.5 = (bf16[352,128]{1,0:T(8,128)(2,1)S(1)}, bf16[352,128]{1,0:T(8,128)(2,1)S(1)}, u32[]{:S(2)}, u32[]{:S(2)}) collective-permute-start(bf16[352,128]{1,0:T(8,128)(2,1)S(1)} %get-tuple-element.69), channel_id=1, source_target_pairs={{0,2},{1,3},{2,0},{3,1},{4,6},{5,7},{6,4},{7,5},{8,10},{9,11},{10,... | collective-permute-start | bytes 270344 | tf_op jit(solution)/shard_map/ppermute | solution.py:341
  23.1 0.4 collective-permute-start.7
  23.5 3.6 %collective-permute-start.8 = (bf16[8,64,128]{2,1,0:T(8,128)(2,1)S(1)}, bf16[8,64,128]{2,1,0:T(8,128)(2,1)S(1)}, u32[]{:S(2)}, u32[]{:S(2)}) collective-permute-start(bf16[8,64,128]{2,1,0:T(8,128)(2,1)S(1)} %get-tuple-element.73.far), channel_id=1, source_target_pairs={{4,8},{12,16},{20,24},{28,0},{8,4},{16,12},{24,20},{0,28},{5,9},{1... | collective-permute-start | bytes 393224 | tf_op jit(solution)/shard_map/ppermute | solution.py:337
  27.0 0.0 collective-permute-done.5.other
  27.1 0.1 collective-permute-start.6
  27.1 5.2 %collective-permute-done.6.y = bf16[176,128]{1,0:T(8,128)(2,1)S(1)} collective-permute-done((bf16[176,128]{1,0:T(8,128)(2,1)S(1)}, bf16[176,128]{1,0:T(8,128)(2,1)S(1)}, u32[]{:S(2)}, u32[]{:S(2)}) %collective-permute-start.6) | collective-permute-done | bytes 45088 | tf_op jit(solution)/shard_map/ppermute | solution.py:341
  32.4 0.0 collective-permute-done.7.near_in
  32.4 0.0 collective-permute-done.8.far_in
  32.4 0.5 collective-permute-start.9
  32.9 0.1 collective-permute-start.11
  33.0 0.7 %collective-permute-start.12 = (bf16[4,64,128]{2,1,0:T(8,128)(2,1)S(1)}, bf16[4,64,128]{2,1,0:T(8,128)(2,1)S(1)}, u32[]{:S(2)}, u32[]{:S(2)}) collective-permute-start(bf16[4,64,128]{2,1,0:T(8,128)(2,1)S(1)} %get-tuple-element.78), channel_id=1, source_target_pairs={{1,2},{3,0},{2,1},{0,3},{5,6},{7,4},{6,5},{4,7},{9,10},{11,8},{10,... | collective-permute-start | bytes 196616 | tf_op jit(solution)/shard_map/ppermute | solution.py:337
  33.7 2.8 %collective-permute-done.9.y = bf16[176,128]{1,0:T(8,128)(2,1)S(1)} collective-permute-done((bf16[176,128]{1,0:T(8,128)(2,1)S(1)}, bf16[176,128]{1,0:T(8,128)(2,1)S(1)}, u32[]{:S(2)}, u32[]{:S(2)}) %collective-permute-start.9) | collective-permute-done | bytes 45088 | tf_op jit(solution)/shard_map/ppermute | solution.py:341
  36.5 1.5 %collective-permute-start.10 = (bf16[176,128]{1,0:T(8,128)(2,1)S(1)}, bf16[176,128]{1,0:T(8,128)(2,1)S(1)}, u32[]{:S(2)}, u32[]{:S(2)}) collective-permute-start(bf16[176,128]{1,0:T(8,128)(2,1)S(1)} %shard_map.84.x), channel_id=1, source_target_pairs={{0,16},{4,20},{8,24},{12,28},{16,0},{20,4},{24,8},{28,12},{1,17},{... | collective-permute-start | bytes 135176 | tf_op jit(solution)/shard_map/ppermute | solution.py:341
  38.0 0.3 copy.9
  38.3 3.6 %collective-permute-done.10.y = bf16[176,128]{1,0:T(8,128)(2,1)S(1)} collective-permute-done((bf16[176,128]{1,0:T(8,128)(2,1)S(1)}, bf16[176,128]{1,0:T(8,128)(2,1)S(1)}, u32[]{:S(2)}, u32[]{:S(2)}) %collective-permute-start.10) | collective-permute-done | bytes 45088 | tf_op jit(solution)/shard_map/ppermute | solution.py:341
  41.9 0.0 collective-permute-done.11.near
  41.9 0.0 collective-permute-done.12.far
  41.9 0.1 collective-permute-start.13
  42.0 0.3 copy.10
  42.3 0.2 copy.11.w_ref
  42.5 2.3 %shard_map.88.acc_ref = f32[2,8,64,128]{3,2,1,0:T(8,128)S(1)} custom-call(bf16[8,64,128]{2,1,0:T(8,128)(2,1)S(1)} %get-tuple-element.72.near, bf16[8,64,128]{2,1,0:T(8,128)(2,1)S(1)} %get-tuple-element.73.far, bf16[8,64,128]{2,1,0:T(8,128)(2,1)S(1)} %collective-permute-done.7.near_in, bf16[8,64,128]{2,1,0:T(8,128)(2,1)S(1)} %collective-permute-done.8.far_in, ...), custom_call_target="tpu_custom_call" | custom-call | flops 452984832 | bytes 1269760 | tf_op jit(solution)/shard_map/pallas_call | solution.py:20
  44.8 1.2 %collective-permute-done.13.other = bf16[176,128]{1,0:T(8,128)(2,1)S(1)} collective-permute-done((bf16[176,128]{1,0:T(8,128)(2,1)S(1)}, bf16[176,128]{1,0:T(8,128)(2,1)S(1)}, u32[]{:S(2)}, u32[]{:S(2)}) %collective-permute-start.13) | collective-permute-done | bytes 45088 | tf_op jit(solution)/shard_map/ppermute | solution.py:341
  46.0 0.6 %collective-permute-start.14 = (bf16[352,128]{1,0:T(8,128)(2,1)S(1)}, bf16[352,128]{1,0:T(8,128)(2,1)S(1)}, u32[]{:S(2)}, u32[]{:S(2)}) collective-permute-start(bf16[352,128]{1,0:T(8,128)(2,1)S(1)} %shard_map.87.mine), channel_id=1, source_target_pairs={{0,2},{1,3},{2,0},{3,1},{4,6},{5,7},{6,4},{7,5},{8,10},{9,11},{10,... | collective-permute-start | bytes 270344 | tf_op jit(solution)/shard_map/ppermute | solution.py:341
  46.6 1.3 %shard_map.90 = f32[1024,128]{1,0:T(8,128)} custom-call(bf16[4,64,128]{2,1,0:T(8,128)(2,1)S(1)} %collective-permute-done.11.near, bf16[4,64,128]{2,1,0:T(8,128)(2,1)S(1)} %collective-permute-done.12.far, f32[2,8,64,128]{3,2,1,0:T(8,128)S(1)} %shard_map.88.acc_ref, bf16[3,3,64,192]{3,2,1,0:T(8,128)(2,1)S(1)} %copy.11.w_ref), custom_call_target="tpu_custom_call" | custom-call | flops 45298484 | bytes 1400832 | tf_op jit(solution)/shard_map/pallas_call | solution.py:20
  48.0 2.7 %collective-permute-done.14.other = bf16[352,128]{1,0:T(8,128)(2,1)S(1)} collective-permute-done((bf16[352,128]{1,0:T(8,128)(2,1)S(1)}, bf16[352,128]{1,0:T(8,128)(2,1)S(1)}, u32[]{:S(2)}, u32[]{:S(2)}) %collective-permute-start.14) | collective-permute-done | bytes 90144 | tf_op jit(solution)/shard_map/ppermute | solution.py:341
  50.7 0.1 collective-permute-start.15
  50.8 1.4 %collective-permute-done.15.other = bf16[704,128]{1,0:T(8,128)(2,1)S(1)} collective-permute-done((bf16[704,128]{1,0:T(8,128)(2,1)S(1)}, bf16[704,128]{1,0:T(8,128)(2,1)S(1)}, u32[]{:S(2)}, u32[]{:S(2)}) %collective-permute-start.15) | collective-permute-done | bytes 180256 | tf_op jit(solution)/shard_map/ppermute | solution.py:341
  52.2 1.0 %shard_map.91 = (f32[3,3,64,192]{3,2,1,0:T(8,128)}, f32[2,2,128,128]{3,2,1,0:T(8,128)}) custom-call(bf16[704,128]{1,0:T(8,128)(2,1)S(1)} %shard_map.89.mine, bf16[704,128]{1,0:T(8,128)(2,1)S(1)} %collective-permute-done.15.other), custom_call_target="tpu_custom_call" | custom-call | bytes 1064960 | tf_op jit(solution)/shard_map/pallas_call | solution.py:20
  (15 shorter events, 0.2 us)
Async XLA Ops:
  0.6 1.0 %copy-start.2 = (bf16[64,2,8,128]{3,2,1,0:T(8,128)(2,1)S(1)}, bf16[64,2,8,128]{3,2,1,0:T(8,128)(2,1)}, u32[]{:S(2)}) copy-start(bf16[64,2,8,128]{3,2,1,0:T(8,128)(2,1)} %f_ref.1) | copy-start | bytes 786436
  1.6 6.8 %copy-start.3 = (bf16[2,2,128,128]{3,2,1,0:T(8,128)(2,1)S(1)}, bf16[2,2,128,128]{3,2,1,0:T(8,128)(2,1)}, u32[]{:S(2)}) copy-start(bf16[2,2,128,128]{3,2,1,0:T(8,128)(2,1)} %d_ref.3) | copy-start | bytes 393220
  1.6 6.8 %copy-start.4 = (bf16[128,1,256]{2,0,1:T(8,128)(2,1)S(1)}, bf16[128,1,256]{2,0,1:T(8,128)(2,1)}, u32[]{:S(2)}) copy-start(bf16[128,1,256]{2,0,1:T(8,128)(2,1)} %param.7) | copy-start | bytes 196612
  1.8 9.5 %collective-permute-start = (bf16[8,64,128]{2,1,0:T(8,128)(2,1)S(1)}, bf16[8,64,128]{2,1,0:T(8,128)(2,1)S(1)}, u32[]{:S(2)}, u32[]{:S(2)}) collective-permute-start(bf16[8,64,128]{2,1,0:T(8,128)(2,1)S(1)} %get-tuple-element.46.near), channel_id=1, source_target_pairs={{0,4},{8,12},{16,20},{24,28},{4,0},{12,8},{20,16},{28,24},{1,5},{9... | collective-permute-start | bytes 393224 | tf_op jit(solution)/shard_map/ppermute | solution.py:337
  4.8 7.7 %collective-permute-start.1 = (bf16[8,64,128]{2,1,0:T(8,128)(2,1)S(1)}, bf16[8,64,128]{2,1,0:T(8,128)(2,1)S(1)}, u32[]{:S(2)}, u32[]{:S(2)}) collective-permute-start(bf16[8,64,128]{2,1,0:T(8,128)(2,1)S(1)} %get-tuple-element.47.far), channel_id=1, source_target_pairs={{4,8},{12,16},{20,24},{28,0},{8,4},{16,12},{24,20},{0,28},{5,9},{1... | collective-permute-start | bytes 393224 | tf_op jit(solution)/shard_map/ppermute | solution.py:337
  8.4 1.0 %copy-start = (bf16[3,3,64,192]{3,2,1,0:T(8,128)(2,1)S(1)}, bf16[3,3,64,192]{3,2,1,0:T(8,128)(2,1)}, u32[]{:S(2)}) copy-start(bf16[3,3,64,192]{3,2,1,0:T(8,128)(2,1)} %w_ref.5) | copy-start | bytes 663556
  11.3 3.0 %copy-start.1 = (bf16[3,3,64,192]{3,2,1,0:T(8,128)(2,1)S(1)}, bf16[3,3,64,192]{3,2,1,0:T(8,128)(2,1)}, u32[]{:S(2)}) copy-start(bf16[3,3,64,192]{3,2,1,0:T(8,128)(2,1)} %w_ref.5) | copy-start | bytes 663556
  12.5 3.1 %collective-permute-start.2 = (bf16[4,64,128]{2,1,0:T(8,128)(2,1)S(1)}, bf16[4,64,128]{2,1,0:T(8,128)(2,1)S(1)}, u32[]{:S(2)}, u32[]{:S(2)}) collective-permute-start(bf16[4,64,128]{2,1,0:T(8,128)(2,1)S(1)} %get-tuple-element.54), channel_id=1, source_target_pairs={{0,1},{2,3},{1,0},{3,2},{4,5},{6,7},{5,4},{7,6},{8,9},{10,11},{9,8... | collective-permute-start | bytes 196616 | tf_op jit(solution)/shard_map/ppermute | solution.py:337
  12.6 3.9 %collective-permute-start.3 = (bf16[4,64,128]{2,1,0:T(8,128)(2,1)S(1)}, bf16[4,64,128]{2,1,0:T(8,128)(2,1)S(1)}, u32[]{:S(2)}, u32[]{:S(2)}) collective-permute-start(bf16[4,64,128]{2,1,0:T(8,128)(2,1)S(1)} %get-tuple-element.55), channel_id=1, source_target_pairs={{1,2},{3,0},{2,1},{0,3},{5,6},{7,4},{6,5},{4,7},{9,10},{11,8},{10,... | collective-permute-start | bytes 196616 | tf_op jit(solution)/shard_map/ppermute | solution.py:337
  20.0 1.4 %collective-permute-start.4 = (bf16[704,128]{1,0:T(8,128)(2,1)S(1)}, bf16[704,128]{1,0:T(8,128)(2,1)S(1)}, u32[]{:S(2)}, u32[]{:S(2)}) collective-permute-start(bf16[704,128]{1,0:T(8,128)(2,1)S(1)} %get-tuple-element.65), channel_id=1, source_target_pairs={{0,1},{1,0},{2,3},{3,2},{4,5},{5,4},{6,7},{7,6},{8,9},{9,8},{10,11... | collective-permute-start | bytes 540680 | tf_op jit(solution)/shard_map/ppermute | solution.py:341
  21.5 5.5 %collective-permute-start.5 = (bf16[352,128]{1,0:T(8,128)(2,1)S(1)}, bf16[352,128]{1,0:T(8,128)(2,1)S(1)}, u32[]{:S(2)}, u32[]{:S(2)}) collective-permute-start(bf16[352,128]{1,0:T(8,128)(2,1)S(1)} %get-tuple-element.69), channel_id=1, source_target_pairs={{0,2},{1,3},{2,0},{3,1},{4,6},{5,7},{6,4},{7,5},{8,10},{9,11},{10,... | collective-permute-start | bytes 270344 | tf_op jit(solution)/shard_map/ppermute | solution.py:341
  23.1 9.3 %collective-permute-start.7 = (bf16[8,64,128]{2,1,0:T(8,128)(2,1)S(1)}, bf16[8,64,128]{2,1,0:T(8,128)(2,1)S(1)}, u32[]{:S(2)}, u32[]{:S(2)}) collective-permute-start(bf16[8,64,128]{2,1,0:T(8,128)(2,1)S(1)} %get-tuple-element.72.near), channel_id=1, source_target_pairs={{0,4},{8,12},{16,20},{24,28},{4,0},{12,8},{20,16},{28,24},{1,5},{9... | collective-permute-start | bytes 393224 | tf_op jit(solution)/shard_map/ppermute | solution.py:337
  23.5 8.9 %collective-permute-start.8 = (bf16[8,64,128]{2,1,0:T(8,128)(2,1)S(1)}, bf16[8,64,128]{2,1,0:T(8,128)(2,1)S(1)}, u32[]{:S(2)}, u32[]{:S(2)}) collective-permute-start(bf16[8,64,128]{2,1,0:T(8,128)(2,1)S(1)} %get-tuple-element.73.far), channel_id=1, source_target_pairs={{4,8},{12,16},{20,24},{28,0},{8,4},{16,12},{24,20},{0,28},{5,9},{1... | collective-permute-start | bytes 393224 | tf_op jit(solution)/shard_map/ppermute | solution.py:337
  27.1 5.3 %collective-permute-start.6 = (bf16[176,128]{1,0:T(8,128)(2,1)S(1)}, bf16[176,128]{1,0:T(8,128)(2,1)S(1)}, u32[]{:S(2)}, u32[]{:S(2)}) collective-permute-start(bf16[176,128]{1,0:T(8,128)(2,1)S(1)} %get-tuple-element.71), channel_id=1, source_target_pairs={{0,4},{4,0},{8,12},{12,8},{16,20},{20,16},{24,28},{28,24},{1,5},{5... | collective-permute-start | bytes 135176 | tf_op jit(solution)/shard_map/ppermute | solution.py:341
  32.4 4.1 %collective-permute-start.9 = (bf16[176,128]{1,0:T(8,128)(2,1)S(1)}, bf16[176,128]{1,0:T(8,128)(2,1)S(1)}, u32[]{:S(2)}, u32[]{:S(2)}) collective-permute-start(bf16[176,128]{1,0:T(8,128)(2,1)S(1)} %shard_map.83.x), channel_id=1, source_target_pairs={{0,8},{4,12},{8,0},{12,4},{16,24},{20,28},{24,16},{28,20},{1,9},{5... | collective-permute-start | bytes 135176 | tf_op jit(solution)/shard_map/ppermute | solution.py:341
  32.9 9.0 %collective-permute-start.11 = (bf16[4,64,128]{2,1,0:T(8,128)(2,1)S(1)}, bf16[4,64,128]{2,1,0:T(8,128)(2,1)S(1)}, u32[]{:S(2)}, u32[]{:S(2)}) collective-permute-start(bf16[4,64,128]{2,1,0:T(8,128)(2,1)S(1)} %get-tuple-element.77), channel_id=1, source_target_pairs={{0,1},{2,3},{1,0},{3,2},{4,5},{6,7},{5,4},{7,6},{8,9},{10,11},{9,8... | collective-permute-start | bytes 196616 | tf_op jit(solution)/shard_map/ppermute | solution.py:337
  33.0 8.9 %collective-permute-start.12 = (bf16[4,64,128]{2,1,0:T(8,128)(2,1)S(1)}, bf16[4,64,128]{2,1,0:T(8,128)(2,1)S(1)}, u32[]{:S(2)}, u32[]{:S(2)}) collective-permute-start(bf16[4,64,128]{2,1,0:T(8,128)(2,1)S(1)} %get-tuple-element.78), channel_id=1, source_target_pairs={{1,2},{3,0},{2,1},{0,3},{5,6},{7,4},{6,5},{4,7},{9,10},{11,8},{10,... | collective-permute-start | bytes 196616 | tf_op jit(solution)/shard_map/ppermute | solution.py:337
  36.5 5.4 %collective-permute-start.10 = (bf16[176,128]{1,0:T(8,128)(2,1)S(1)}, bf16[176,128]{1,0:T(8,128)(2,1)S(1)}, u32[]{:S(2)}, u32[]{:S(2)}) collective-permute-start(bf16[176,128]{1,0:T(8,128)(2,1)S(1)} %shard_map.84.x), channel_id=1, source_target_pairs={{0,16},{4,20},{8,24},{12,28},{16,0},{20,4},{24,8},{28,12},{1,17},{... | collective-permute-start | bytes 135176 | tf_op jit(solution)/shard_map/ppermute | solution.py:341
  41.9 4.1 %collective-permute-start.13 = (bf16[176,128]{1,0:T(8,128)(2,1)S(1)}, bf16[176,128]{1,0:T(8,128)(2,1)S(1)}, u32[]{:S(2)}, u32[]{:S(2)}) collective-permute-start(bf16[176,128]{1,0:T(8,128)(2,1)S(1)} %shard_map.85.mine), channel_id=1, source_target_pairs={{0,4},{4,0},{8,12},{12,8},{16,20},{20,16},{24,28},{28,24},{1,5},{5... | collective-permute-start | bytes 135176 | tf_op jit(solution)/shard_map/ppermute | solution.py:341
  46.0 4.6 %collective-permute-start.14 = (bf16[352,128]{1,0:T(8,128)(2,1)S(1)}, bf16[352,128]{1,0:T(8,128)(2,1)S(1)}, u32[]{:S(2)}, u32[]{:S(2)}) collective-permute-start(bf16[352,128]{1,0:T(8,128)(2,1)S(1)} %shard_map.87.mine), channel_id=1, source_target_pairs={{0,2},{1,3},{2,0},{3,1},{4,6},{5,7},{6,4},{7,5},{8,10},{9,11},{10,... | collective-permute-start | bytes 270344 | tf_op jit(solution)/shard_map/ppermute | solution.py:341
  50.7 1.5 %collective-permute-start.15 = (bf16[704,128]{1,0:T(8,128)(2,1)S(1)}, bf16[704,128]{1,0:T(8,128)(2,1)S(1)}, u32[]{:S(2)}, u32[]{:S(2)}) collective-permute-start(bf16[704,128]{1,0:T(8,128)(2,1)S(1)} %shard_map.89.mine), channel_id=1, source_target_pairs={{0,1},{1,0},{2,3},{3,2},{4,5},{5,4},{6,7},{7,6},{8,9},{9,8},{10,11... | collective-permute-start | bytes 540680 | tf_op jit(solution)/shard_map/ppermute | solution.py:341

commit v6 on v5

--- a/solution.py
+++ b/solution.py
@@ -36,16 +36,28 @@
     return jnp.where(jnp.broadcast_to(cond, yes.shape), yes, no)
 
 
-def lines_kernel(f_ref, near_ref, far_ref, wide):
+def lines_kernel(f_ref, near_ref, far_ref, near_row, far_row, wide):
     channels, planes, rows, breadth = f_ref.shape
     wide[...] = f_ref[...].astype(F32).reshape(channels * planes * rows, breadth)
-    even = is_even("gz")
-    for y in range(rows):
-        low, high = (
+    even, even_y = is_even("gz"), is_even("gy")
+    ends = {}
+    for y in (0, rows - 1, *range(1, rows - 1)):
+        low, high = ends[y] = [
             wide[pl.ds(z * rows + y, channels, stride=planes * rows), :].astype(BF16) for z in range(2)
-        )
+        ]
         near_ref[y] = choose(even, high, low)
         far_ref[y] = choose(even, low, high)
+    for z in range(2):
+        near_row[z] = choose(even_y, ends[rows - 1][z], ends[0][z])
+        far_row[z] = choose(even_y, ends[0][z], ends[rows - 1][z])
+
+
+def corners_kernel(near, far, near_ref, far_ref):
+    even_z, even_y = is_even("gz"), is_even("gy")
+    for side in range(2):
+        below, above = (choose(even_y, *((far[z], near[z]) if side == 0 else (near[z], far[z]))) for z in range(2))
+        near_ref[side] = choose(even_z, above, below)
+        far_ref[side] = choose(even_z, below, above)
 
 
 def edges_kernel(near, far, near_in, far_in, near_ref, far_ref):
@@ -92,6 +104,16 @@
     for p in range(4):
         put_columns(cols, p, 0, choose(even, far[p], near[p]))
         put_columns(cols, p, 1, choose(even, near[p], far[p]))
+
+
+def fill_edges_and_corners(cols, near, far, near_corner, far_corner):
+    even_z, even_y = is_even("gz"), is_even("gy")
+    for side in range(2):
+        put_columns(cols, 0, side, choose(even_z, far_corner[side], near_corner[side]))
+        put_columns(cols, 3, side, choose(even_z, near_corner[side], far_corner[side]))
+        for z in range(2):
+            pair = (far[z], near[z]) if side == 0 else (near[z], far[z])
+            put_columns(cols, z + 1, side, choose(even_y, *pair))
 
 
 def dot(lhs, rhs):
@@ -173,9 +195,9 @@
     lax.fori_loop(0, rows // 2, step, 0)
 
 
-def gate_kernel(near, far, acc_ref, grad_ref, w_ref, edges, near_ref, far_ref, h_ref):
+def gate_kernel(near, far, near_corner, far_corner, acc_ref, grad_ref, w_ref, edges, near_ref, far_ref, h_ref):
     rows, channels, breadth = acc_ref.shape[1:]
-    fill_edges(edges, near, far)
+    fill_edges_and_corners(edges, near, far, near_corner, far_corner)
     sides = [edge_terms(edges, w_ref, side) for side in range(2)]
     even = is_even("gz")
 
@@ -267,13 +289,32 @@
     send[...] = packed[part(1 - side, half)].astype(BF16)
 
 
-def halve_kernel(mine, other, keep, send, total, *, axis, bit):
+def quarter(flips=0):
+    x, y = side_of("gy", 2), side_of("gz", 1)
+    return 2 * (1 - x if flips & 2 else x) + (1 - y if flips & 1 else y)
+
+
+def quarter_kernel(mine, other, keep, to_x, to_y, to_both, total):
     total[...] = mine[...] + other[...].astype(F32)
-    split(total, keep, send, total.shape[0] // 2, axis, bit)
-
-
-def add_kernel(x, y, out):
-    out[...] = (x[...].astype(F32) + y[...].astype(F32)).astype(BF16)
+    rows = keep.shape[0]
+    keep[...] = total[part(quarter(), rows)]
+    for flips, send in ((2, to_x), (1, to_y), (3, to_both)):
+        send[...] = total[part(quarter(flips), rows)].astype(BF16)
+
+
+def add_kernel(own, x, y, both, out):
+    found = [ref[...].astype(F32) for ref in (own, x, y, both)]
+    out[...] = ((found[0] + found[1]) + (found[2] + found[3])).astype(BF16)
+
+
+def add_two_kernel(own, other, out):
+    out[...] = (own[...].astype(F32) + other[...].astype(F32)).astype(BF16)
+
+
+def gather_kernel(own, x, y, both, out):
+    rows = own.shape[0]
+    for flips, ref in ((0, own), (2, x), (1, y), (3, both)):
+        out[part(quarter(flips), rows)] = ref[...]
 
 
 def join_kernel(mine, other, out, *, axis, bit):
@@ -337,8 +378,11 @@
     return lax.ppermute(cells, axis, pairs + [(b, a) for a, b in pairs])
 
 
-def flip(cells, axis, bit):
-    return lax.ppermute(cells, axis, [(i, i ^ bit) for i in range(lax.axis_size(axis))])
+def flip(cells, z_bits, y_bits):
+    row = lax.axis_size("gy")
+    count = lax.axis_size("gz") * row
+    mask = z_bits * row + y_bits
+    return lax.ppermute(cells, ("gz", "gy"), [(i, i ^ mask) for i in range(count)])
 
 
 def tied(first, *others):
@@ -365,10 +409,17 @@
     lines = (plane_count, row_count, channels, breadth)
     conv_flops = 2 * 27 * channels * channels * plane_count * row_count * breadth
 
-    own = call(
-        lines_kernel, [plane, plane], [((channels * plane_count * row_count, breadth), F32)], 0, (features,)
-    )
+    pair = ((2, channels, breadth), BF16)
+    *own, near_row, far_row = call(
+        lines_kernel, [plane, plane, pair, pair],
+        [((channels * plane_count * row_count, breadth), F32)], 0, (features,),
+    )
+    beside = swapped(near_row, far_row, "gy")
     outside = swapped(*own, "gz")
+    corners = call(corners_kernel, [pair, pair], [], 0, beside)
+    near, far, *corners = lax.optimization_barrier((*own, *corners))
+    own = (near, far)
+    corners = swapped(*corners, "gz")
     inner, acc, hidden_grad = call(
         inner_kernel, [cols, (lines, F32), (lines, F32)],
         [((out_channels, row_count // 2 * breadth), BF16)],
@@ -376,13 +427,12 @@
     )
     near, far, acc = lax.optimization_barrier((*outside, acc))
     outside = (near, far)
-    beside = swapped(*call(edges_kernel, [edge, edge], [], 0, (*own, *outside)), "gy")
     outer, acc = call(
         outer_kernel, [cols, (lines, F32)], [], conv_flops // 3, (*outside, conv_weight, acc)
     )
     edges, near, far, hidden = call(
         gate_kernel, [edge_cols, plane, plane, (lines, BF16)], [], conv_flops // 10,
-        (*beside, acc, hidden_grad, conv_weight),
+        (*beside, *corners, acc, hidden_grad, conv_weight),
     )
     gates = (near, far)
 
@@ -394,50 +444,49 @@
         [((rows, 128), F32)], conv_flops,
         (inner, outer, edges, *gates, hidden, down_weight, cot),
     )
-    keep, gates = tied(keep, *gates)
     near, far = gates
     near_in = swap(near, "gz", 0)
-    for level, (axis, bit) in enumerate((("gy", 2), ("gz", 1))):
-        size = rows >> (level + 2)
-        mine, got = keep, flip(send, *(("gy", 1), ("gy", 2))[level])
-        keep, send = call(
-            functools.partial(halve_kernel, axis=axis, bit=bit),
-            [((size, 128), F32), ((size, 128), BF16)], [((2 * size, 128), F32)], 0, (mine, got),
-        )
-        if level == 0:
-            keep, (far,) = tied(keep, far)
-            far_in = swap(far, "gz", 1)
+    other, (near_in,) = tied(flip(send, 0, 1), near_in)
     shard = ((rows // 8, 128), BF16)
-    (sums,) = call(add_kernel, [shard], [], 0, (keep, flip(send, "gz", 1)))
+    keep, to_x, to_y, to_both = call(
+        quarter_kernel, [((rows // 8, 128), F32), shard, shard, shard], [((rows // 2, 128), F32)], 0,
+        (keep, other),
+    )
+    keep, (far,) = tied(keep, far)
+    found = flip(to_both, 1, 2), flip(to_x, 0, 2), flip(to_y, 1, 0)
+    far_in = swap(far, "gz", 1)
+    (sums,) = call(add_kernel, [shard], [], 0, (keep, found[1], found[2], found[0]))
     sums, outside = tied(sums, near_in, far_in)
     sends = call(edges_kernel, [edge, edge], [], 0, (*gates, *outside))
     beside = swapped(*sends, "gy")
     (acc,) = call(
         field_kernel, [(lines, F32)], [cols, cols], conv_flops, (*gates, *outside, weight_bwd)
     )
-    wide = [("gy", 1 << k) for k in range(2, lax.axis_size("gy").bit_length() - 1)]
-    wide += [("gz", 1 << k) for k in range(1, lax.axis_size("gz").bit_length() - 1)]
-    for axis, bit in wide:
-        (sums,) = call(add_kernel, [shard], [], 0, (sums, flip(sums, axis, bit)))
+    bits = [(0, 1 << k) for k in range(2, lax.axis_size("gy").bit_length() - 1)]
+    bits += [(1 << k, 0) for k in range(1, lax.axis_size("gz").bit_length() - 1)]
+    while bits:
+        (z, y), *bits = bits
+        if bits:
+            (z2, y2), *bits = bits
+            found = flip(sums, z, y), flip(sums, z2, y2), flip(sums, z | z2, y | y2)
+            (sums,) = call(add_kernel, [shard], [], 0, (sums, *found))
+        else:
+            (sums,) = call(add_two_kernel, [shard], [], 0, (sums, flip(sums, z, y)))
     sums, beside = tied(sums, *beside)
+    found = flip(sums, 1, 2), flip(sums, 0, 2), flip(sums, 1, 0)
+    sums, (acc,) = tied(sums, acc)
     (sums,) = call(
-        functools.partial(join_kernel, axis="gz", bit=1), [((rows // 4, 128), BF16)], [], 0,
-        (sums, flip(sums, "gz", 1)),
-    )
-    sums, (acc,) = tied(sums, acc)
+        gather_kernel, [((rows // 2, 128), BF16)], [], 0, (sums, found[1], found[2], found[0])
+    )
     (field,) = call(
         field_edges_kernel, [((channels * plane_count * row_count, breadth), F32)], [edge_cols],
         conv_flops // 10, (*beside, acc, weight_bwd),
     )
-    (sums,) = call(
-        functools.partial(join_kernel, axis="gy", bit=2), [((rows // 2, 128), BF16)], [], 0,
-        (sums, flip(sums, "gy", 2)),
-    )
-    sums, (field,) = tied(sums, field)
+    other, (field,) = tied(flip(sums, 0, 1), field)
     grad_conv, grad_down = call(
         functools.partial(unpack_kernel, scale=grad_scale),
         [(conv_weight.shape, F32), (down_weight.shape, F32)], [((rows, 128), BF16)], 0,
-        (sums, flip(sums, "gy", 1)),
+        (sums, other),
     )
     section_out = section_out.reshape(out_channels, plane_count // 2, -1)
     return (section_out, field.reshape(features.shape), grad_conv, grad_down)

time: 53.3 us -> 57.9 us (1.086)
  starting transfers between devices: 17.7 us -> 27 us
  waiting for transfers between devices: 20.1 us -> 14.2 us
  local copies, waits for them, and re-layouts: 2.7 us -> 3.86 us
    ppermute x8 -> x11, waiting for transfers between devices: 18 us -> 7.37 us  [flip(): lax.ppermute(cells, ('gz', 'gy'), [(i, i ^ mask) for i in range(count)])]
    ppermute x8 -> x11, starting transfers between devices: 4.81 us -> 11.7 us  [flip(): lax.ppermute(cells, ('gz', 'gy'), [(i, i ^ mask) for i in range(count)])]
    ppermute x8 -> x10, waiting for transfers between devices: 2.13 us -> 6.81 us  [swap(): return lax.ppermute(cells, axis, pairs + [(b, a) for a, b in pairs])]
    ppermute x8 -> x10, starting transfers between devices: 12.9 us -> 15.3 us  [swap(): return lax.ppermute(cells, axis, pairs + [(b, a) for a, b in pairs])]
    unnamed x11, local copies, waits for them, and re-layouts: 2.18 us -> 3.36 us
    pallas_call x17 -> x14, Pallas kernels: 11.8 us -> 11.8 us  [call(): pl.pallas_call(kernel, out_shape=[jax.ShapeDtypeStruct(s, d) for s, d in...]
  transfers between devices with their start and end apart: 16 -> 21, of which waited for: 9 -> 9; matrix products, arithmetic and copies ran while one was open for 1% -> 1% of each run, Pallas kernels for 13% -> 12%
where the time goes in v6:
time: 57.9 us; the launch traced here: 57.7 us
  starting transfers between devices  27 us (47%)
  waiting for transfers between devices  14.2 us (25%)
  Pallas kernels  11.8 us (20%)
  local copies, waits for them, and re-layouts  3.86 us (7%)
  between operations  0.85 us (1%)
    ppermute x10, starting transfers between devices, swap(): return lax.ppermute(cells, axis, pairs + [(b, a) for a, b in pairs])  15.3 us
    pallas_call x14, Pallas kernels, call(): pl.pallas_call(kernel, out_shape=[jax.ShapeDtypeStruct(s, d) for s, d in...  11.8 us
    ppermute x11, starting transfers between devices, flip(): lax.ppermute(cells, ('gz', 'gy'), [(i, i ^ mask) for i in range(count)])  11.7 us
    ppermute x11, waiting for transfers between devices, flip(): lax.ppermute(cells, ('gz', 'gy'), [(i, i ^ mask) for i in range(count)])  7.37 us
    ppermute x10, waiting for transfers between devices, swap(): return lax.ppermute(cells, axis, pairs + [(b, a) for a, b in pairs])  6.81 us
    unnamed x11, local copies, waits for them, and re-layouts  3.36 us
  transfers between devices with their start and end apart: 21, of which 9 were waited for; matrix products, arithmetic and copies ran while one was open for 1% of the time, Pallas kernels for 12%

profile of v6, /device:TPU:0, one launch (start us, length us, event | category | flops | bytes accessed | tf_op | source)
XLA Modules:
  0.0 57.7 jit_solution(17323548959305217243)
XLA Ops:
  0.7 1.0 %copy-done.1 = bf16[64,2,8,128]{3,2,1,0:T(8,128)(2,1)S(1)} copy-done((bf16[64,2,8,128]{3,2,1,0:T(8,128)(2,1)S(1)}, bf16[64,2,8,128]{3,2,1,0:T(8,128)(2,1)}, u32[]{:S(2)}) %copy-start.1) | copy-done | bytes 262168
  1.6 0.2 shard_map.75
  1.9 3.0 %collective-permute-start.2 = (bf16[8,64,128]{2,1,0:T(8,128)(2,1)S(1)}, bf16[8,64,128]{2,1,0:T(8,128)(2,1)S(1)}, u32[]{:S(2)}, u32[]{:S(2)}) collective-permute-start(bf16[8,64,128]{2,1,0:T(8,128)(2,1)S(1)} %get-tuple-element.57.near), channel_id=1, source_target_pairs={{0,4},{8,12},{16,20},{24,28},{4,0},{12,8},{20,16},{28,24},{1,5},{9... | collective-permute-start | bytes 393224 | tf_op jit(solution)/shard_map/ppermute | solution.py:378
  4.9 3.5 %collective-permute-start.3 = (bf16[8,64,128]{2,1,0:T(8,128)(2,1)S(1)}, bf16[8,64,128]{2,1,0:T(8,128)(2,1)S(1)}, u32[]{:S(2)}, u32[]{:S(2)}) collective-permute-start(bf16[8,64,128]{2,1,0:T(8,128)(2,1)S(1)} %get-tuple-element.58.far), channel_id=1, source_target_pairs={{4,8},{12,16},{20,24},{28,0},{8,4},{16,12},{24,20},{0,28},{5,9},{1... | collective-permute-start | bytes 393224 | tf_op jit(solution)/shard_map/ppermute | solution.py:378
  8.4 0.0 collective-permute-start
  8.4 1.6 %collective-permute-start.1 = (bf16[2,64,128]{2,1,0:T(8,128)(2,1)S(1)}, bf16[2,64,128]{2,1,0:T(8,128)(2,1)S(1)}, u32[]{:S(2)}, u32[]{:S(2)}) collective-permute-start(bf16[2,64,128]{2,1,0:T(8,128)(2,1)S(1)} %get-tuple-element.54), channel_id=1, source_target_pairs={{1,2},{3,0},{2,1},{0,3},{5,6},{7,4},{6,5},{4,7},{9,10},{11,8},{10,... | collective-permute-start | bytes 98312 | tf_op jit(solution)/shard_map/ppermute | solution.py:378
  10.0 1.7 %collective-permute-done.1.far = bf16[2,64,128]{2,1,0:T(8,128)(2,1)S(1)} collective-permute-done((bf16[2,64,128]{2,1,0:T(8,128)(2,1)S(1)}, bf16[2,64,128]{2,1,0:T(8,128)(2,1)S(1)}, u32[]{:S(2)}, u32[]{:S(2)}) %collective-permute-start.1) | collective-permute-done | bytes 32800 | tf_op jit(solution)/shard_map/ppermute | solution.py:378
  11.8 0.1 collective-permute-start.4
  11.9 1.9 %collective-permute-start.5 = (bf16[2,64,128]{2,1,0:T(8,128)(2,1)S(1)}, bf16[2,64,128]{2,1,0:T(8,128)(2,1)S(1)}, u32[]{:S(2)}, u32[]{:S(2)}) collective-permute-start(bf16[2,64,128]{2,1,0:T(8,128)(2,1)S(1)} %get-tuple-element.66), channel_id=1, source_target_pairs={{4,8},{12,16},{20,24},{28,0},{8,4},{16,12},{24,20},{0,28},{5,9},{1... | collective-permute-start | bytes 98312 | tf_op jit(solution)/shard_map/ppermute | solution.py:378
  13.8 0.9 %copy-done.2 = bf16[2,2,128,128]{3,2,1,0:T(8,128)(2,1)S(1)} copy-done((bf16[2,2,128,128]{3,2,1,0:T(8,128)(2,1)S(1)}, bf16[2,2,128,128]{3,2,1,0:T(8,128)(2,1)}, u32[]{:S(2)}) %copy-start.2) | copy-done | bytes 131096
  14.7 0.8 %copy-done.4 = bf16[128,1,256]{2,0,1:T(8,128)(2,1)S(1)} copy-done((bf16[128,1,256]{2,0,1:T(8,128)(2,1)S(1)}, bf16[128,1,256]{2,0,1:T(8,128)(2,1)}, u32[]{:S(2)}) %copy-start.4) | copy-done | bytes 65560
  15.5 1.9 %shard_map.77 = (bf16[2,10,192,128]{3,2,1,0:T(8,128)(2,1)S(1)}, f32[2,8,64,128]{3,2,1,0:T(8,128)S(1)}, f32[2,8,64,128]{3,2,1,0:T(8,128)S(1)}) custom-call(bf16[8,64,128]{2,1,0:T(8,128)(2,1)S(1)} %get-tuple-element.57.near, bf16[8,64,128]{2,1,0:T(8,128)(2,1)S(1)} %get-tuple-element.58.far, bf16[3,3,64,192]{3,2,1,0:T(8,128)(2,1)S(1)} %copy-done, ...), custom_call_target="tpu_custom_call" | custom-call | flops 301989888 | bytes 2711552 | tf_op jit(solution)/shard_map/pallas_call | solution.py:20
  17.4 0.0 collective-permute-done.2.near
  17.4 0.0 collective-permute-done.3.far
  17.5 1.4 %shard_map.78 = (bf16[2,10,192,128]{3,2,1,0:T(8,128)(2,1)S(1)}, f32[2,8,64,128]{3,2,1,0:T(8,128)S(1)}) custom-call(bf16[8,64,128]{2,1,0:T(8,128)(2,1)S(1)} %collective-permute-done.2.near, bf16[8,64,128]{2,1,0:T(8,128)(2,1)S(1)} %collective-permute-done.3.far, bf16[3,3,64,192]{3,2,1,0:T(8,128)(2,1)S(1)} %copy-done, ...), custom_call_target="tpu_custom_call" | custom-call | flops 150994944 | bytes 2514944 | tf_op jit(solution)/shard_map/pallas_call | solution.py:20
  18.9 0.0 copy-start.3
  18.9 0.5 shard_map.79
  19.4 0.4 copy-done.3
  19.8 3.0 %shard_map.80 = (bf16[128,256]{1,0:T(8,128)(2,1)}, f32[704,128]{1,0:T(8,128)S(1)}, bf16[704,128]{1,0:T(8,128)(2,1)S(1)}) custom-call(bf16[2,10,192,128]{3,2,1,0:T(8,128)(2,1)S(1)} %get-tuple-element.59.inner, bf16[2,10,192,128]{3,2,1,0:T(8,128)(2,1)S(1)} %get-tuple-element.64.outer, bf16[4,2,192,128]{3,2,1,0:T(8,128)(2,1)S(1)} %get-tuple-element.69.edges, ...), custom_call_target="tpu_custom_call" | custom-call | flops 452984832 | bytes 3686400 | tf_op jit(solution)/shard_map/pallas_call | solution.py:20
  22.7 0.2 collective-permute-start.6
  23.0 0.6 %collective-permute-start.7 = (bf16[8,64,128]{2,1,0:T(8,128)(2,1)S(1)}, bf16[8,64,128]{2,1,0:T(8,128)(2,1)S(1)}, u32[]{:S(2)}, u32[]{:S(2)}) collective-permute-start(bf16[8,64,128]{2,1,0:T(8,128)(2,1)S(1)} %get-tuple-element.70.near), channel_id=1, source_target_pairs={{0,4},{8,12},{16,20},{24,28},{4,0},{12,8},{20,16},{28,24},{1,5},{9... | collective-permute-start | bytes 393224 | tf_op jit(solution)/shard_map/ppermute | solution.py:378
  23.6 5.1 %collective-permute-done.7.near_in = bf16[8,64,128]{2,1,0:T(8,128)(2,1)S(1)} collective-permute-done((bf16[8,64,128]{2,1,0:T(8,128)(2,1)S(1)}, bf16[8,64,128]{2,1,0:T(8,128)(2,1)S(1)}, u32[]{:S(2)}, u32[]{:S(2)}) %collective-permute-start.7) | collective-permute-done | bytes 131104 | tf_op jit(solution)/shard_map/ppermute | solution.py:378
  28.7 0.1 shard_map.81
  28.7 3.0 %collective-permute-start.11 = (bf16[8,64,128]{2,1,0:T(8,128)(2,1)S(1)}, bf16[8,64,128]{2,1,0:T(8,128)(2,1)S(1)}, u32[]{:S(2)}, u32[]{:S(2)}) collective-permute-start(bf16[8,64,128]{2,1,0:T(8,128)(2,1)S(1)} %get-tuple-element.83.far), channel_id=1, source_target_pairs={{4,8},{12,16},{20,24},{28,0},{8,4},{16,12},{24,20},{0,28},{5,9},{1... | collective-permute-start | bytes 393224 | tf_op jit(solution)/shard_map/ppermute | solution.py:378
  31.7 1.5 %collective-permute-start.8 = (bf16[176,128]{1,0:T(8,128)(2,1)S(1)}, bf16[176,128]{1,0:T(8,128)(2,1)S(1)}, u32[]{:S(2)}, u32[]{:S(2)}) collective-permute-start(bf16[176,128]{1,0:T(8,128)(2,1)S(1)} %get-tuple-element.79), channel_id=1, source_target_pairs={{0,2},{1,3},{2,0},{3,1},{4,6},{5,7},{6,4},{7,5},{8,10},{9,11},{10,... | collective-permute-start | bytes 135176 | tf_op jit(solution)/shard_map/ppermute | solution.py:385
  33.2 0.1 collective-permute-start.9
  33.3 1.9 %collective-permute-start.10 = (bf16[176,128]{1,0:T(8,128)(2,1)S(1)}, bf16[176,128]{1,0:T(8,128)(2,1)S(1)}, u32[]{:S(2)}, u32[]{:S(2)}) collective-permute-start(bf16[176,128]{1,0:T(8,128)(2,1)S(1)} %get-tuple-element.81), channel_id=1, source_target_pairs={{0,6},{1,7},{2,4},{3,5},{4,2},{5,3},{6,0},{7,1},{8,14},{9,15},{10,... | collective-permute-start | bytes 135176 | tf_op jit(solution)/shard_map/ppermute | solution.py:385
  35.2 0.7 %collective-permute-done.8.x = bf16[176,128]{1,0:T(8,128)(2,1)S(1)} collective-permute-done((bf16[176,128]{1,0:T(8,128)(2,1)S(1)}, bf16[176,128]{1,0:T(8,128)(2,1)S(1)}, u32[]{:S(2)}, u32[]{:S(2)}) %collective-permute-start.8) | collective-permute-done | bytes 45088 | tf_op jit(solution)/shard_map/ppermute | solution.py:385
  35.9 1.9 %collective-permute-done.9.y = bf16[176,128]{1,0:T(8,128)(2,1)S(1)} collective-permute-done((bf16[176,128]{1,0:T(8,128)(2,1)S(1)}, bf16[176,128]{1,0:T(8,128)(2,1)S(1)}, u32[]{:S(2)}, u32[]{:S(2)}) %collective-permute-start.9) | collective-permute-done | bytes 45088 | tf_op jit(solution)/shard_map/ppermute | solution.py:385
  37.8 0.5 collective-permute-done.10.both
  38.3 0.1 collective-permute-start.15
  38.4 1.5 %collective-permute-start.16 = (bf16[4,64,128]{2,1,0:T(8,128)(2,1)S(1)}, bf16[4,64,128]{2,1,0:T(8,128)(2,1)S(1)}, u32[]{:S(2)}, u32[]{:S(2)}) collective-permute-start(bf16[4,64,128]{2,1,0:T(8,128)(2,1)S(1)} %get-tuple-element.88), channel_id=1, source_target_pairs={{1,2},{3,0},{2,1},{0,3},{5,6},{7,4},{6,5},{4,7},{9,10},{11,8},{10,... | collective-permute-start | bytes 196616 | tf_op jit(solution)/shard_map/ppermute | solution.py:378
  39.9 2.0 %collective-permute-start.13 = (bf16[176,128]{1,0:T(8,128)(2,1)S(1)}, bf16[176,128]{1,0:T(8,128)(2,1)S(1)}, u32[]{:S(2)}, u32[]{:S(2)}) collective-permute-start(bf16[176,128]{1,0:T(8,128)(2,1)S(1)} %shard_map.82.own), channel_id=1, source_target_pairs={{0,16},{1,17},{2,18},{3,19},{4,20},{5,21},{6,22},{7,23},{8,24},{9,... | collective-permute-start | bytes 135176 | tf_op jit(solution)/shard_map/ppermute | solution.py:385
  41.9 2.4 %collective-permute-start.14 = (bf16[176,128]{1,0:T(8,128)(2,1)S(1)}, bf16[176,128]{1,0:T(8,128)(2,1)S(1)}, u32[]{:S(2)}, u32[]{:S(2)}) collective-permute-start(bf16[176,128]{1,0:T(8,128)(2,1)S(1)} %shard_map.82.own), channel_id=1, source_target_pairs={{0,24},{1,25},{2,26},{3,27},{4,28},{5,29},{6,30},{7,31},{8,16},{9,... | collective-permute-start | bytes 135176 | tf_op jit(solution)/shard_map/ppermute | solution.py:385
  44.3 0.3 copy.9
  44.6 0.8 %collective-permute-done.13.y = bf16[176,128]{1,0:T(8,128)(2,1)S(1)} collective-permute-done((bf16[176,128]{1,0:T(8,128)(2,1)S(1)}, bf16[176,128]{1,0:T(8,128)(2,1)S(1)}, u32[]{:S(2)}, u32[]{:S(2)}) %collective-permute-start.13) | collective-permute-done | bytes 45088 | tf_op jit(solution)/shard_map/ppermute | solution.py:385
  45.4 2.3 %collective-permute-done.14.both = bf16[176,128]{1,0:T(8,128)(2,1)S(1)} collective-permute-done((bf16[176,128]{1,0:T(8,128)(2,1)S(1)}, bf16[176,128]{1,0:T(8,128)(2,1)S(1)}, u32[]{:S(2)}, u32[]{:S(2)}) %collective-permute-start.14) | collective-permute-done | bytes 45088 | tf_op jit(solution)/shard_map/ppermute | solution.py:385
  47.8 1.6 %collective-permute-start.17 = (bf16[176,128]{1,0:T(8,128)(2,1)S(1)}, bf16[176,128]{1,0:T(8,128)(2,1)S(1)}, u32[]{:S(2)}, u32[]{:S(2)}) collective-permute-start(bf16[176,128]{1,0:T(8,128)(2,1)S(1)} %shard_map.83.own), channel_id=1, source_target_pairs={{0,2},{1,3},{2,0},{3,1},{4,6},{5,7},{6,4},{7,5},{8,10},{9,11},{10,... | collective-permute-start | bytes 135176 | tf_op jit(solution)/shard_map/ppermute | solution.py:385
  49.3 0.9 %collective-permute-start.18 = (bf16[176,128]{1,0:T(8,128)(2,1)S(1)}, bf16[176,128]{1,0:T(8,128)(2,1)S(1)}, u32[]{:S(2)}, u32[]{:S(2)}) collective-permute-start(bf16[176,128]{1,0:T(8,128)(2,1)S(1)} %shard_map.83.own), channel_id=1, source_target_pairs={{0,4},{1,5},{2,6},{3,7},{4,0},{5,1},{6,2},{7,3},{8,12},{9,13},{10,... | collective-permute-start | bytes 135176 | tf_op jit(solution)/shard_map/ppermute | solution.py:385
  50.3 1.1 %collective-permute-start.19 = (bf16[176,128]{1,0:T(8,128)(2,1)S(1)}, bf16[176,128]{1,0:T(8,128)(2,1)S(1)}, u32[]{:S(2)}, u32[]{:S(2)}) collective-permute-start(bf16[176,128]{1,0:T(8,128)(2,1)S(1)} %shard_map.83.own), channel_id=1, source_target_pairs={{0,6},{1,7},{2,4},{3,5},{4,2},{5,3},{6,0},{7,1},{8,14},{9,15},{10,... | collective-permute-start | bytes 135176 | tf_op jit(solution)/shard_map/ppermute | solution.py:385
  51.4 0.2 copy.10
  51.6 0.2 copy.11.w_ref
  51.9 2.3 %shard_map.85.acc_ref = f32[2,8,64,128]{3,2,1,0:T(8,128)S(1)} custom-call(bf16[8,64,128]{2,1,0:T(8,128)(2,1)S(1)} %get-tuple-element.70.near, bf16[8,64,128]{2,1,0:T(8,128)(2,1)S(1)} %get-tuple-element.83.far, bf16[8,64,128]{2,1,0:T(8,128)(2,1)S(1)} %collective-permute-done.7.near_in, bf16[8,64,128]{2,1,0:T(8,128)(2,1)S(1)} %collective-permute-done.11.far_in, ...), custom_call_target="tpu_custom_call" | custom-call | flops 452984832 | bytes 1269760 | tf_op jit(solution)/shard_map/pallas_call | solution.py:20
  54.2 1.1 %collective-permute-done.19.both = bf16[176,128]{1,0:T(8,128)(2,1)S(1)} collective-permute-done((bf16[176,128]{1,0:T(8,128)(2,1)S(1)}, bf16[176,128]{1,0:T(8,128)(2,1)S(1)}, u32[]{:S(2)}, u32[]{:S(2)}) %collective-permute-start.19) | collective-permute-done | bytes 45088 | tf_op jit(solution)/shard_map/ppermute | solution.py:385
  55.2 0.1 collective-permute-start.20
  55.3 1.3 %shard_map.87 = f32[1024,128]{1,0:T(8,128)} custom-call(bf16[4,64,128]{2,1,0:T(8,128)(2,1)S(1)} %collective-permute-done.15.near, bf16[4,64,128]{2,1,0:T(8,128)(2,1)S(1)} %collective-permute-done.16.far, f32[2,8,64,128]{3,2,1,0:T(8,128)S(1)} %shard_map.85.acc_ref, bf16[3,3,64,192]{3,2,1,0:T(8,128)(2,1)S(1)} %copy.11.w_ref), custom_call_target="tpu_custom_call" | custom-call | flops 45298484 | bytes 1400832 | tf_op jit(solution)/shard_map/pallas_call | solution.py:20
  56.7 0.1 collective-permute-done.20.other
  56.7 1.0 %shard_map.88 = (f32[3,3,64,192]{3,2,1,0:T(8,128)}, f32[2,2,128,128]{3,2,1,0:T(8,128)}) custom-call(bf16[704,128]{1,0:T(8,128)(2,1)S(1)} %shard_map.86.mine, bf16[704,128]{1,0:T(8,128)(2,1)S(1)} %collective-permute-done.20.other), custom_call_target="tpu_custom_call" | custom-call | bytes 1064960 | tf_op jit(solution)/shard_map/pallas_call | solution.py:20
  (22 shorter events, 0.2 us)
Async XLA Ops:
  0.6 13.1 %copy-start = (bf16[3,3,64,192]{3,2,1,0:T(8,128)(2,1)S(1)}, bf16[3,3,64,192]{3,2,1,0:T(8,128)(2,1)}, u32[]{:S(2)}) copy-start(bf16[3,3,64,192]{3,2,1,0:T(8,128)(2,1)} %w_ref.5) | copy-start | bytes 663556
  0.6 1.0 %copy-start.1 = (bf16[64,2,8,128]{3,2,1,0:T(8,128)(2,1)S(1)}, bf16[64,2,8,128]{3,2,1,0:T(8,128)(2,1)}, u32[]{:S(2)}) copy-start(bf16[64,2,8,128]{3,2,1,0:T(8,128)(2,1)} %f_ref.1) | copy-start | bytes 786436
  1.9 15.6 %collective-permute-start.2 = (bf16[8,64,128]{2,1,0:T(8,128)(2,1)S(1)}, bf16[8,64,128]{2,1,0:T(8,128)(2,1)S(1)}, u32[]{:S(2)}, u32[]{:S(2)}) collective-permute-start(bf16[8,64,128]{2,1,0:T(8,128)(2,1)S(1)} %get-tuple-element.57.near), channel_id=1, source_target_pairs={{0,4},{8,12},{16,20},{24,28},{4,0},{12,8},{20,16},{28,24},{1,5},{9... | collective-permute-start | bytes 393224 | tf_op jit(solution)/shard_map/ppermute | solution.py:378
  4.9 12.6 %collective-permute-start.3 = (bf16[8,64,128]{2,1,0:T(8,128)(2,1)S(1)}, bf16[8,64,128]{2,1,0:T(8,128)(2,1)S(1)}, u32[]{:S(2)}, u32[]{:S(2)}) collective-permute-start(bf16[8,64,128]{2,1,0:T(8,128)(2,1)S(1)} %get-tuple-element.58.far), channel_id=1, source_target_pairs={{4,8},{12,16},{20,24},{28,0},{8,4},{16,12},{24,20},{0,28},{5,9},{1... | collective-permute-start | bytes 393224 | tf_op jit(solution)/shard_map/ppermute | solution.py:378
  8.4 1.6 %collective-permute-start = (bf16[2,64,128]{2,1,0:T(8,128)(2,1)S(1)}, bf16[2,64,128]{2,1,0:T(8,128)(2,1)S(1)}, u32[]{:S(2)}, u32[]{:S(2)}) collective-permute-start(bf16[2,64,128]{2,1,0:T(8,128)(2,1)S(1)} %get-tuple-element.53), channel_id=1, source_target_pairs={{0,1},{2,3},{1,0},{3,2},{4,5},{6,7},{5,4},{7,6},{8,9},{10,11},{9,8... | collective-permute-start | bytes 98312 | tf_op jit(solution)/shard_map/ppermute | solution.py:378
  8.4 3.3 %collective-permute-start.1 = (bf16[2,64,128]{2,1,0:T(8,128)(2,1)S(1)}, bf16[2,64,128]{2,1,0:T(8,128)(2,1)S(1)}, u32[]{:S(2)}, u32[]{:S(2)}) collective-permute-start(bf16[2,64,128]{2,1,0:T(8,128)(2,1)S(1)} %get-tuple-element.54), channel_id=1, source_target_pairs={{1,2},{3,0},{2,1},{0,3},{5,6},{7,4},{6,5},{4,7},{9,10},{11,8},{10,... | collective-permute-start | bytes 98312 | tf_op jit(solution)/shard_map/ppermute | solution.py:378
  11.8 7.0 %collective-permute-start.4 = (bf16[2,64,128]{2,1,0:T(8,128)(2,1)S(1)}, bf16[2,64,128]{2,1,0:T(8,128)(2,1)S(1)}, u32[]{:S(2)}, u32[]{:S(2)}) collective-permute-start(bf16[2,64,128]{2,1,0:T(8,128)(2,1)S(1)} %get-tuple-element.65), channel_id=1, source_target_pairs={{0,4},{8,12},{16,20},{24,28},{4,0},{12,8},{20,16},{28,24},{1,5},{9... | collective-permute-start | bytes 98312 | tf_op jit(solution)/shard_map/ppermute | solution.py:378
  11.9 7.0 %collective-permute-start.5 = (bf16[2,64,128]{2,1,0:T(8,128)(2,1)S(1)}, bf16[2,64,128]{2,1,0:T(8,128)(2,1)S(1)}, u32[]{:S(2)}, u32[]{:S(2)}) collective-permute-start(bf16[2,64,128]{2,1,0:T(8,128)(2,1)S(1)} %get-tuple-element.66), channel_id=1, source_target_pairs={{4,8},{12,16},{20,24},{28,0},{8,4},{16,12},{24,20},{0,28},{5,9},{1... | collective-permute-start | bytes 98312 | tf_op jit(solution)/shard_map/ppermute | solution.py:378
  13.8 0.9 %copy-start.2 = (bf16[2,2,128,128]{3,2,1,0:T(8,128)(2,1)S(1)}, bf16[2,2,128,128]{3,2,1,0:T(8,128)(2,1)}, u32[]{:S(2)}) copy-start(bf16[2,2,128,128]{3,2,1,0:T(8,128)(2,1)} %d_ref.3) | copy-start | bytes 393220
  14.7 0.8 %copy-start.4 = (bf16[128,1,256]{2,0,1:T(8,128)(2,1)S(1)}, bf16[128,1,256]{2,0,1:T(8,128)(2,1)}, u32[]{:S(2)}) copy-start(bf16[128,1,256]{2,0,1:T(8,128)(2,1)} %param.7) | copy-start | bytes 196612
  18.9 0.9 %copy-start.3 = (bf16[2,2,128,128]{3,2,1,0:T(8,128)(2,1)S(1)}, bf16[2,2,128,128]{3,2,1,0:T(8,128)(2,1)}, u32[]{:S(2)}) copy-start(bf16[2,2,128,128]{3,2,1,0:T(8,128)(2,1)} %d_ref.3) | copy-start | bytes 393220
  22.7 5.9 %collective-permute-start.6 = (bf16[704,128]{1,0:T(8,128)(2,1)S(1)}, bf16[704,128]{1,0:T(8,128)(2,1)S(1)}, u32[]{:S(2)}, u32[]{:S(2)}) collective-permute-start(bf16[704,128]{1,0:T(8,128)(2,1)S(1)} %get-tuple-element.75), channel_id=1, source_target_pairs={{0,1},{1,0},{2,3},{3,2},{4,5},{5,4},{6,7},{7,6},{8,9},{9,8},{10,11... | collective-permute-start | bytes 540680 | tf_op jit(solution)/shard_map/ppermute | solution.py:385
  23.0 5.7 %collective-permute-start.7 = (bf16[8,64,128]{2,1,0:T(8,128)(2,1)S(1)}, bf16[8,64,128]{2,1,0:T(8,128)(2,1)S(1)}, u32[]{:S(2)}, u32[]{:S(2)}) collective-permute-start(bf16[8,64,128]{2,1,0:T(8,128)(2,1)S(1)} %get-tuple-element.70.near), channel_id=1, source_target_pairs={{0,4},{8,12},{16,20},{24,28},{4,0},{12,8},{20,16},{28,24},{1,5},{9... | collective-permute-start | bytes 393224 | tf_op jit(solution)/shard_map/ppermute | solution.py:378
  28.7 9.6 %collective-permute-start.11 = (bf16[8,64,128]{2,1,0:T(8,128)(2,1)S(1)}, bf16[8,64,128]{2,1,0:T(8,128)(2,1)S(1)}, u32[]{:S(2)}, u32[]{:S(2)}) collective-permute-start(bf16[8,64,128]{2,1,0:T(8,128)(2,1)S(1)} %get-tuple-element.83.far), channel_id=1, source_target_pairs={{4,8},{12,16},{20,24},{28,0},{8,4},{16,12},{24,20},{0,28},{5,9},{1... | collective-permute-start | bytes 393224 | tf_op jit(solution)/shard_map/ppermute | solution.py:378
  31.7 4.2 %collective-permute-start.8 = (bf16[176,128]{1,0:T(8,128)(2,1)S(1)}, bf16[176,128]{1,0:T(8,128)(2,1)S(1)}, u32[]{:S(2)}, u32[]{:S(2)}) collective-permute-start(bf16[176,128]{1,0:T(8,128)(2,1)S(1)} %get-tuple-element.79), channel_id=1, source_target_pairs={{0,2},{1,3},{2,0},{3,1},{4,6},{5,7},{6,4},{7,5},{8,10},{9,11},{10,... | collective-permute-start | bytes 135176 | tf_op jit(solution)/shard_map/ppermute | solution.py:385
  33.2 4.6 %collective-permute-start.9 = (bf16[176,128]{1,0:T(8,128)(2,1)S(1)}, bf16[176,128]{1,0:T(8,128)(2,1)S(1)}, u32[]{:S(2)}, u32[]{:S(2)}) collective-permute-start(bf16[176,128]{1,0:T(8,128)(2,1)S(1)} %get-tuple-element.80), channel_id=1, source_target_pairs={{0,4},{1,5},{2,6},{3,7},{4,0},{5,1},{6,2},{7,3},{8,12},{9,13},{10,... | collective-permute-start | bytes 135176 | tf_op jit(solution)/shard_map/ppermute | solution.py:385
  33.3 5.0 %collective-permute-start.10 = (bf16[176,128]{1,0:T(8,128)(2,1)S(1)}, bf16[176,128]{1,0:T(8,128)(2,1)S(1)}, u32[]{:S(2)}, u32[]{:S(2)}) collective-permute-start(bf16[176,128]{1,0:T(8,128)(2,1)S(1)} %get-tuple-element.81), channel_id=1, source_target_pairs={{0,6},{1,7},{2,4},{3,5},{4,2},{5,3},{6,0},{7,1},{8,14},{9,15},{10,... | collective-permute-start | bytes 135176 | tf_op jit(solution)/shard_map/ppermute | solution.py:385
  38.3 9.4 %collective-permute-start.15 = (bf16[4,64,128]{2,1,0:T(8,128)(2,1)S(1)}, bf16[4,64,128]{2,1,0:T(8,128)(2,1)S(1)}, u32[]{:S(2)}, u32[]{:S(2)}) collective-permute-start(bf16[4,64,128]{2,1,0:T(8,128)(2,1)S(1)} %get-tuple-element.87), channel_id=1, source_target_pairs={{0,1},{2,3},{1,0},{3,2},{4,5},{6,7},{5,4},{7,6},{8,9},{10,11},{9,8... | collective-permute-start | bytes 196616 | tf_op jit(solution)/shard_map/ppermute | solution.py:378
  38.4 9.3 %collective-permute-start.16 = (bf16[4,64,128]{2,1,0:T(8,128)(2,1)S(1)}, bf16[4,64,128]{2,1,0:T(8,128)(2,1)S(1)}, u32[]{:S(2)}, u32[]{:S(2)}) collective-permute-start(bf16[4,64,128]{2,1,0:T(8,128)(2,1)S(1)} %get-tuple-element.88), channel_id=1, source_target_pairs={{1,2},{3,0},{2,1},{0,3},{5,6},{7,4},{6,5},{4,7},{9,10},{11,8},{10,... | collective-permute-start | bytes 196616 | tf_op jit(solution)/shard_map/ppermute | solution.py:378
  39.9 4.7 %collective-permute-start.12 = (bf16[176,128]{1,0:T(8,128)(2,1)S(1)}, bf16[176,128]{1,0:T(8,128)(2,1)S(1)}, u32[]{:S(2)}, u32[]{:S(2)}) collective-permute-start(bf16[176,128]{1,0:T(8,128)(2,1)S(1)} %shard_map.82.own), channel_id=1, source_target_pairs={{0,8},{1,9},{2,10},{3,11},{4,12},{5,13},{6,14},{7,15},{8,0},{9,1},... | collective-permute-start | bytes 135176 | tf_op jit(solution)/shard_map/ppermute | solution.py:385
  39.9 5.5 %collective-permute-start.13 = (bf16[176,128]{1,0:T(8,128)(2,1)S(1)}, bf16[176,128]{1,0:T(8,128)(2,1)S(1)}, u32[]{:S(2)}, u32[]{:S(2)}) collective-permute-start(bf16[176,128]{1,0:T(8,128)(2,1)S(1)} %shard_map.82.own), channel_id=1, source_target_pairs={{0,16},{1,17},{2,18},{3,19},{4,20},{5,21},{6,22},{7,23},{8,24},{9,... | collective-permute-start | bytes 135176 | tf_op jit(solution)/shard_map/ppermute | solution.py:385
  41.9 5.8 %collective-permute-start.14 = (bf16[176,128]{1,0:T(8,128)(2,1)S(1)}, bf16[176,128]{1,0:T(8,128)(2,1)S(1)}, u32[]{:S(2)}, u32[]{:S(2)}) collective-permute-start(bf16[176,128]{1,0:T(8,128)(2,1)S(1)} %shard_map.82.own), channel_id=1, source_target_pairs={{0,24},{1,25},{2,26},{3,27},{4,28},{5,29},{6,30},{7,31},{8,16},{9,... | collective-permute-start | bytes 135176 | tf_op jit(solution)/shard_map/ppermute | solution.py:385
  47.8 6.4 %collective-permute-start.17 = (bf16[176,128]{1,0:T(8,128)(2,1)S(1)}, bf16[176,128]{1,0:T(8,128)(2,1)S(1)}, u32[]{:S(2)}, u32[]{:S(2)}) collective-permute-start(bf16[176,128]{1,0:T(8,128)(2,1)S(1)} %shard_map.83.own), channel_id=1, source_target_pairs={{0,2},{1,3},{2,0},{3,1},{4,6},{5,7},{6,4},{7,5},{8,10},{9,11},{10,... | collective-permute-start | bytes 135176 | tf_op jit(solution)/shard_map/ppermute | solution.py:385
  49.3 4.8 %collective-permute-start.18 = (bf16[176,128]{1,0:T(8,128)(2,1)S(1)}, bf16[176,128]{1,0:T(8,128)(2,1)S(1)}, u32[]{:S(2)}, u32[]{:S(2)}) collective-permute-start(bf16[176,128]{1,0:T(8,128)(2,1)S(1)} %shard_map.83.own), channel_id=1, source_target_pairs={{0,4},{1,5},{2,6},{3,7},{4,0},{5,1},{6,2},{7,3},{8,12},{9,13},{10,... | collective-permute-start | bytes 135176 | tf_op jit(solution)/shard_map/ppermute | solution.py:385
  50.3 4.9 %collective-permute-start.19 = (bf16[176,128]{1,0:T(8,128)(2,1)S(1)}, bf16[176,128]{1,0:T(8,128)(2,1)S(1)}, u32[]{:S(2)}, u32[]{:S(2)}) collective-permute-start(bf16[176,128]{1,0:T(8,128)(2,1)S(1)} %shard_map.83.own), channel_id=1, source_target_pairs={{0,6},{1,7},{2,4},{3,5},{4,2},{5,3},{6,0},{7,1},{8,14},{9,15},{10,... | collective-permute-start | bytes 135176 | tf_op jit(solution)/shard_map/ppermute | solution.py:385
  55.2 1.5 %collective-permute-start.20 = (bf16[704,128]{1,0:T(8,128)(2,1)S(1)}, bf16[704,128]{1,0:T(8,128)(2,1)S(1)}, u32[]{:S(2)}, u32[]{:S(2)}) collective-permute-start(bf16[704,128]{1,0:T(8,128)(2,1)S(1)} %shard_map.86.mine), channel_id=1, source_target_pairs={{0,1},{1,0},{2,3},{3,2},{4,5},{5,4},{6,7},{7,6},{8,9},{9,8},{10,11... | collective-permute-start | bytes 540680 | tf_op jit(solution)/shard_map/ppermute | solution.py:385

commit v7 on v5

--- a/solution.py
+++ b/solution.py
@@ -195,7 +195,32 @@
     gate(rows - 1, sides[1])
 
 
-def weight_grad_kernel(inner, outer, edges, near, far, h_ref, d_ref, cot_ref, out_ref, keep, send, packed):
+def coarse_hidden(h_ref, a, b):
+    rows, channels, breadth = h_ref.shape[1:]
+    source = lax.broadcasted_iota(jnp.int32, (2 * breadth, 2 * breadth), 0)
+    target = lax.broadcasted_iota(jnp.int32, (2 * breadth, 2 * breadth), 1)
+    wanted = 2 * (target % breadth) + target // breadth
+    pick = jnp.where(source == wanted, 1.0, 0.0).astype(BF16)
+    pairs = []
+    for pair in range(rows // 4):
+        both = jnp.concatenate([h_ref[a, 4 * pair + b], h_ref[a, 4 * pair + 2 + b]], axis=1)
+        pairs.append(dot(both, pick).astype(BF16))
+    return jnp.concatenate(
+        [jnp.concatenate([x[:, e * breadth : (e + 1) * breadth] for x in pairs], axis=1) for e in range(2)],
+        axis=0,
+    )
+
+
+def section_kernel(h_ref, d_ref, out_ref):
+    coarse = None
+    for a in range(2):
+        for b in range(2):
+            term = dot(d_ref[a, b], coarse_hidden(h_ref, a, b))
+            coarse = term if coarse is None else coarse + term
+    out_ref[...] = coarse.astype(BF16)
+
+
+def weight_grad_kernel(inner, outer, edges, near, far, h_ref, cot_ref, keep, send, packed):
     rows, channels, breadth = near.shape
     across = (((1,), (1,)), ((), ()))
     even = is_even("gz")
@@ -225,28 +250,13 @@
             mix = jnp.where(lane < channels, rest[0 : channels // 2], rest[channels // 2 :])
             packed[base + channels : base + 3 * channels // 2] = mix
     base = 9 * 3 * channels // 2
-    source = lax.broadcasted_iota(jnp.int32, (2 * breadth, 2 * breadth), 0)
-    target = lax.broadcasted_iota(jnp.int32, (2 * breadth, 2 * breadth), 1)
-    wanted = 2 * (target % breadth) + target // breadth
-    pick = jnp.where(source == wanted, 1.0, 0.0).astype(BF16)
-    coarse = None
+    height = cot_ref.shape[0]
     for a in range(2):
         for b in range(2):
-            pairs = []
-            for pair in range(rows // 4):
-                both = jnp.concatenate([h_ref[a, 4 * pair + b], h_ref[a, 4 * pair + 2 + b]], axis=1)
-                pairs.append(jnp.dot(both, pick, preferred_element_type=F32).astype(BF16))
-            hidden = jnp.concatenate(
-                [jnp.concatenate([x[:, e * breadth : (e + 1) * breadth] for x in pairs], axis=1) for e in range(2)],
-                axis=0,
-            )
-            term = jnp.dot(d_ref[a, b], hidden, preferred_element_type=F32)
-            coarse = term if coarse is None else coarse + term
-            down = lax.dot_general(cot_ref[...], hidden, across, preferred_element_type=F32)
-            at = base + (2 * a + b) * d_ref.shape[2]
-            packed[at : at + d_ref.shape[2]] = down
-    out_ref[...] = coarse.astype(BF16)
-    end = base + 4 * d_ref.shape[2]
+            down = lax.dot_general(cot_ref[...], coarse_hidden(h_ref, a, b), across, preferred_element_type=F32)
+            at = base + (2 * a + b) * height
+            packed[at : at + height] = down
+    end = base + 4 * height
     if end < packed.shape[0]:
         packed[end:] = jnp.zeros((packed.shape[0] - end, packed.shape[1]), F32)
     half = packed.shape[0] // 2
@@ -267,20 +277,21 @@
     send[...] = packed[part(1 - side, half)].astype(BF16)
 
 
-def halve_kernel(mine, other, keep, send, total, *, axis, bit):
-    total[...] = mine[...] + other[...].astype(F32)
-    split(total, keep, send, total.shape[0] // 2, axis, bit)
-
-
-def add_kernel(x, y, out):
-    out[...] = (x[...].astype(F32) + y[...].astype(F32)).astype(BF16)
-
-
-def join_kernel(mine, other, out, *, axis, bit):
-    rows = mine.shape[0]
-    side = side_of(axis, bit)
-    out[part(side, rows)] = mine[...]
-    out[part(1 - side, rows)] = other[...]
+def add_kernel(mine, other, out):
+    total = mine[...] + other[...].astype(F32)
+    out[...] = total.reshape(out.shape).astype(BF16)
+
+
+def total_kernel(terms, out):
+    count = terms.shape[0]
+    for core in range(2):
+        total = None
+        for s in range(core, count, 2):
+            term = terms[s].astype(F32)
+            total = term if total is None else total + term
+        total = total.astype(BF16)
+        for s in range(core, count, 2):
+            out[s] = total
 
 
 def field_kernel(near, far, near_in, far_in, w_ref, acc_ref, inner, outer):
@@ -314,13 +325,16 @@
 
 
 def unpack_kernel(mine, other, conv_ref, down_ref, sums_ref, *, scale):
-    join_kernel(mine, other, sums_ref, axis="gy", bit=1)
+    half = sums_ref.shape[0] // 2
+    side = side_of("gy", 1)
+    sums_ref[part(side, half)] = mine[...].astype(F32).reshape(half, sums_ref.shape[1])
+    sums_ref[part(1 - side, half)] = other[...].astype(F32).reshape(half, sums_ref.shape[1])
     channels = conv_ref.shape[2]
     for a in range(3):
         for b in range(3):
             base = (a * 3 + b) * 3 * channels // 2
-            conv_ref[a, b, :, 0 : 2 * channels] = sums_ref[base : base + channels].astype(F32) * scale
-            rest = sums_ref[base + channels : base + 3 * channels // 2].astype(F32) * scale
+            conv_ref[a, b, :, 0 : 2 * channels] = sums_ref[base : base + channels]* scale
+            rest = sums_ref[base + channels : base + 3 * channels // 2]* scale
             conv_ref[a, b, 0 : channels // 2, 2 * channels :] = rest[:, 0:channels]
             conv_ref[a, b, channels // 2 :, 2 * channels :] = rest[:, channels:]
     base = 9 * 3 * channels // 2
@@ -328,7 +342,7 @@
     for a in range(2):
         for b in range(2):
             at = base + (2 * a + b) * height
-            down_ref[a, b] = sums_ref[at : at + height].astype(F32) * scale
+            down_ref[a, b] = sums_ref[at : at + height]* scale
 
 
 def swap(cells, axis, low):
@@ -387,56 +401,38 @@
     gates = (near, far)
 
     used = 27 * channels * channels // 128 + 4 * out_channels
-    rows = -(-used // 128) * 128
-    section_out, keep, send = call(
-        weight_grad_kernel,
-        [((out_channels, cot.shape[1]), BF16), ((rows // 2, 128), F32), ((rows // 2, 128), BF16)],
-        [((rows, 128), F32)], conv_flops,
-        (inner, outer, edges, *gates, hidden, down_weight, cot),
+    share = -(-used // (16 * count)) * 8
+    half = share * count
+    parts = ((count, share, 128), BF16)
+    keep, send = call(
+        weight_grad_kernel, [((half, 128), F32), ((half, 128), BF16)], [((2 * half, 128), F32)], conv_flops,
+        (inner, outer, edges, *gates, hidden, cot),
+    )
+    exchange = functools.partial(
+        lax.all_to_all, axis_name=("gz", "gy"), split_axis=0, concat_axis=0, tiled=True
     )
     keep, gates = tied(keep, *gates)
     near, far = gates
-    near_in = swap(near, "gz", 0)
-    for level, (axis, bit) in enumerate((("gy", 2), ("gz", 1))):
-        size = rows >> (level + 2)
-        mine, got = keep, flip(send, *(("gy", 1), ("gy", 2))[level])
-        keep, send = call(
-            functools.partial(halve_kernel, axis=axis, bit=bit),
-            [((size, 128), F32), ((size, 128), BF16)], [((2 * size, 128), F32)], 0, (mine, got),
-        )
-        if level == 0:
-            keep, (far,) = tied(keep, far)
-            far_in = swap(far, "gz", 1)
-    shard = ((rows // 8, 128), BF16)
-    (sums,) = call(add_kernel, [shard], [], 0, (keep, flip(send, "gz", 1)))
-    sums, outside = tied(sums, near_in, far_in)
-    sends = call(edges_kernel, [edge, edge], [], 0, (*gates, *outside))
-    beside = swapped(*sends, "gy")
+    outside = swap(near, "gz", 0), swap(far, "gz", 1)
+    (terms,) = call(add_kernel, [parts], [], 0, (keep, flip(send, "gy", 1)))
+    terms, (hidden,) = tied(terms, hidden)
+    (section_out,) = call(
+        section_kernel, [((out_channels, cot.shape[1]), BF16)], [], conv_flops // 10, (hidden, down_weight)
+    )
+    beside = swapped(*call(edges_kernel, [edge, edge], [], 0, (*gates, *outside)), "gy")
+    terms, beside = tied(exchange(terms), *beside)
+    (sums,) = call(total_kernel, [parts], [], 0, (terms,))
     (acc,) = call(
         field_kernel, [(lines, F32)], [cols, cols], conv_flops, (*gates, *outside, weight_bwd)
     )
-    wide = [("gy", 1 << k) for k in range(2, lax.axis_size("gy").bit_length() - 1)]
-    wide += [("gz", 1 << k) for k in range(1, lax.axis_size("gz").bit_length() - 1)]
-    for axis, bit in wide:
-        (sums,) = call(add_kernel, [shard], [], 0, (sums, flip(sums, axis, bit)))
-    sums, beside = tied(sums, *beside)
-    (sums,) = call(
-        functools.partial(join_kernel, axis="gz", bit=1), [((rows // 4, 128), BF16)], [], 0,
-        (sums, flip(sums, "gz", 1)),
-    )
-    sums, (acc,) = tied(sums, acc)
     (field,) = call(
         field_edges_kernel, [((channels * plane_count * row_count, breadth), F32)], [edge_cols],
         conv_flops // 10, (*beside, acc, weight_bwd),
     )
-    (sums,) = call(
-        functools.partial(join_kernel, axis="gy", bit=2), [((rows // 2, 128), BF16)], [], 0,
-        (sums, flip(sums, "gy", 2)),
-    )
-    sums, (field,) = tied(sums, field)
+    sums, (field,) = tied(exchange(sums), field)
     grad_conv, grad_down = call(
         functools.partial(unpack_kernel, scale=grad_scale),
-        [(conv_weight.shape, F32), (down_weight.shape, F32)], [((rows, 128), BF16)], 0,
+        [(conv_weight.shape, F32), (down_weight.shape, F32)], [((2 * half, 128), F32)], 0,
         (sums, flip(sums, "gy", 1)),
     )
     section_out = section_out.reshape(out_channels, plane_count // 2, -1)

time: 53.3 us -> 58.6 us (1.099)
  starting transfers between devices: 17.7 us -> 24.4 us
  waiting for transfers between devices: 20.1 us -> 16.6 us
  Pallas kernels: 11.8 us -> 13.8 us
    ppermute x8 -> x2, waiting for transfers between devices: 18 us -> 1.07 us  [flip(): lax.ppermute(cells, axis, [(i, i ^ bit) for i in range(lax.axis_size(axis...]
    ppermute x8, waiting for transfers between devices: 2.13 us -> 11 us  [swap(): return lax.ppermute(cells, axis, pairs + [(b, a) for a, b in pairs])]
    all_to_all x0 -> x2, starting transfers between devices: none -> 8.34 us  [the longest x1 4.84 us: body(): terms, beside = tied(exchange(terms), *beside)]
    all_to_all x0 -> x2, waiting for transfers between devices: none -> 4.48 us  [the longest x1 4.48 us: body(): sums, (field,) = tied(exchange(sums), field)]
    ppermute x8 -> x2, starting transfers between devices: 4.81 us -> 1.06 us  [flip(): lax.ppermute(cells, axis, [(i, i ^ bit) for i in range(lax.axis_size(axis...]
    ppermute x8, starting transfers between devices: 12.9 us -> 15 us  [swap(): return lax.ppermute(cells, axis, pairs + [(b, a) for a, b in pairs])]
    pallas_call x17 -> x13, Pallas kernels: 11.8 us -> 13.8 us  [call(): pl.pallas_call(kernel, out_shape=[jax.ShapeDtypeStruct(s, d) for s, d in...]
  transfers between devices with their start and end apart: 16 -> 12, of which waited for: 9 -> 7; matrix products, arithmetic and copies ran while one was open for 1% -> 1% of each run, Pallas kernels for 13% -> 14%
where the time goes in v7:
time: 58.6 us; the launch traced here: 58.3 us
  starting transfers between devices  24.4 us (42%)
  waiting for transfers between devices  16.6 us (28%)
  Pallas kernels  13.8 us (24%)
  local copies, waits for them, and re-layouts  2.69 us (5%)
  between operations  0.77 us (1%)
    ppermute x8, starting transfers between devices, swap(): return lax.ppermute(cells, axis, pairs + [(b, a) for a, b in pairs])  15 us
    pallas_call x13, Pallas kernels, call(): pl.pallas_call(kernel, out_shape=[jax.ShapeDtypeStruct(s, d) for s, d in...  13.8 us
    ppermute x8, waiting for transfers between devices, swap(): return lax.ppermute(cells, axis, pairs + [(b, a) for a, b in pairs])  11 us
    all_to_all x1, starting transfers between devices, body(): terms, beside = tied(exchange(terms), *beside)  4.84 us
    all_to_all x1, waiting for transfers between devices, body(): sums, (field,) = tied(exchange(sums), field)  4.48 us
    all_to_all x1, starting transfers between devices, body(): sums, (field,) = tied(exchange(sums), field)  3.5 us
    unnamed x11, local copies, waits for them, and re-layouts  2.18 us
  transfers between devices with their start and end apart: 12, of which 7 were waited for; matrix products, arithmetic and copies ran while one was open for 1% of the time, Pallas kernels for 14%

profile of v7, /device:TPU:0, one launch (start us, length us, event | category | flops | bytes accessed | tf_op | source)
XLA Modules:
  0.0 58.3 jit_solution(12559985967296131160)
XLA Ops:
  0.6 0.0 copy-start.2
  0.6 0.9 %copy-done.2 = bf16[64,2,8,128]{3,2,1,0:T(8,128)(2,1)S(1)} copy-done((bf16[64,2,8,128]{3,2,1,0:T(8,128)(2,1)S(1)}, bf16[64,2,8,128]{3,2,1,0:T(8,128)(2,1)}, u32[]{:S(2)}) %copy-start.2) | copy-done | bytes 262168
  1.6 0.0 copy-start.3
  1.6 0.0 copy-start.4
  1.6 0.2 shard_map.75
  1.8 3.0 %collective-permute-start = (bf16[8,64,128]{2,1,0:T(8,128)(2,1)S(1)}, bf16[8,64,128]{2,1,0:T(8,128)(2,1)S(1)}, u32[]{:S(2)}, u32[]{:S(2)}) collective-permute-start(bf16[8,64,128]{2,1,0:T(8,128)(2,1)S(1)} %get-tuple-element.36.near), channel_id=1, source_target_pairs={{0,4},{8,12},{16,20},{24,28},{4,0},{12,8},{20,16},{28,24},{1,5},{9... | collective-permute-start | bytes 393224 | tf_op jit(solution)/shard_map/ppermute | solution.py:351
  4.8 3.5 %collective-permute-start.1 = (bf16[8,64,128]{2,1,0:T(8,128)(2,1)S(1)}, bf16[8,64,128]{2,1,0:T(8,128)(2,1)S(1)}, u32[]{:S(2)}, u32[]{:S(2)}) collective-permute-start(bf16[8,64,128]{2,1,0:T(8,128)(2,1)S(1)} %get-tuple-element.37.far), channel_id=1, source_target_pairs={{4,8},{12,16},{20,24},{28,0},{8,4},{16,12},{24,20},{0,28},{5,9},{1... | collective-permute-start | bytes 393224 | tf_op jit(solution)/shard_map/ppermute | solution.py:351
  8.4 0.0 copy-done.3
  8.4 0.0 copy-done.4
  8.4 0.0 copy-start
  8.4 1.0 %copy-done = bf16[3,3,64,192]{3,2,1,0:T(8,128)(2,1)S(1)} copy-done((bf16[3,3,64,192]{3,2,1,0:T(8,128)(2,1)S(1)}, bf16[3,3,64,192]{3,2,1,0:T(8,128)(2,1)}, u32[]{:S(2)}) %copy-start) | copy-done | bytes 221208
  9.3 1.9 %shard_map.76 = (bf16[2,10,192,128]{3,2,1,0:T(8,128)(2,1)S(1)}, f32[2,8,64,128]{3,2,1,0:T(8,128)S(1)}, f32[2,8,64,128]{3,2,1,0:T(8,128)S(1)}) custom-call(bf16[8,64,128]{2,1,0:T(8,128)(2,1)S(1)} %get-tuple-element.36.near, bf16[8,64,128]{2,1,0:T(8,128)(2,1)S(1)} %get-tuple-element.37.far, bf16[3,3,64,192]{3,2,1,0:T(8,128)(2,1)S(1)} %copy-done, ...), custom_call_target="tpu_custom_call" | custom-call | flops 301989888 | bytes 2711552 | tf_op jit(solution)/shard_map/pallas_call | solution.py:20
  11.3 0.0 copy-start.1
  11.3 0.0 collective-permute-done.near.near_in
  11.3 1.2 %collective-permute-done.1.far.far_in = bf16[8,64,128]{2,1,0:T(8,128)(2,1)S(1)} collective-permute-done((bf16[8,64,128]{2,1,0:T(8,128)(2,1)S(1)}, bf16[8,64,128]{2,1,0:T(8,128)(2,1)S(1)}, u32[]{:S(2)}, u32[]{:S(2)}) %collective-permute-start.1) | collective-permute-done | bytes 131104 | tf_op jit(solution)/shard_map/ppermute | solution.py:351
  12.5 0.1 collective-permute-start.2
  12.6 1.6 %collective-permute-start.3 = (bf16[4,64,128]{2,1,0:T(8,128)(2,1)S(1)}, bf16[4,64,128]{2,1,0:T(8,128)(2,1)S(1)}, u32[]{:S(2)}, u32[]{:S(2)}) collective-permute-start(bf16[4,64,128]{2,1,0:T(8,128)(2,1)S(1)} %get-tuple-element.45), channel_id=1, source_target_pairs={{1,2},{3,0},{2,1},{0,3},{5,6},{7,4},{6,5},{4,7},{9,10},{11,8},{10,... | collective-permute-start | bytes 196616 | tf_op jit(solution)/shard_map/ppermute | solution.py:351
  14.2 0.0 copy-done.1
  14.2 1.4 %shard_map.77 = (bf16[2,10,192,128]{3,2,1,0:T(8,128)(2,1)S(1)}, f32[2,8,64,128]{3,2,1,0:T(8,128)S(1)}) custom-call(bf16[8,64,128]{2,1,0:T(8,128)(2,1)S(1)} %collective-permute-done.near.near_in, bf16[8,64,128]{2,1,0:T(8,128)(2,1)S(1)} %collective-permute-done.1.far.far_in, bf16[3,3,64,192]{3,2,1,0:T(8,128)(2,1)S(1)} %copy-done.1, ...), custom_call_target="tpu_custom_call" | custom-call | flops 150994944 | bytes 2514944 | tf_op jit(solution)/shard_map/pallas_call | solution.py:20
  15.6 0.0 collective-permute-done.2.near
  15.6 0.9 %collective-permute-done.3.far = bf16[4,64,128]{2,1,0:T(8,128)(2,1)S(1)} collective-permute-done((bf16[4,64,128]{2,1,0:T(8,128)(2,1)S(1)}, bf16[4,64,128]{2,1,0:T(8,128)(2,1)S(1)}, u32[]{:S(2)}, u32[]{:S(2)}) %collective-permute-start.3) | collective-permute-done | bytes 65568 | tf_op jit(solution)/shard_map/ppermute | solution.py:351
  16.5 0.5 shard_map.79
  17.0 2.3 %shard_map.80 = (f32[768,128]{1,0:T(8,128)S(1)}, bf16[768,128]{1,0:T(8,128)(2,1)S(1)}) custom-call(bf16[2,10,192,128]{3,2,1,0:T(8,128)(2,1)S(1)} %get-tuple-element.38.inner, bf16[2,10,192,128]{3,2,1,0:T(8,128)(2,1)S(1)} %get-tuple-element.43.outer, bf16[4,2,192,128]{3,2,1,0:T(8,128)(2,1)S(1)} %get-tuple-element.48.edges, ...), custom_call_target="tpu_custom_call" | custom-call | flops 452984832 | bytes 3538944 | tf_op jit(solution)/shard_map/pallas_call | solution.py:20
  19.4 0.5 collective-permute-start.4
  19.8 1.1 %collective-permute-done.4.other = bf16[768,128]{1,0:T(8,128)(2,1)S(1)} collective-permute-done((bf16[768,128]{1,0:T(8,128)(2,1)S(1)}, bf16[768,128]{1,0:T(8,128)(2,1)S(1)}, u32[]{:S(2)}, u32[]{:S(2)}) %collective-permute-start.4) | collective-permute-done | bytes 196640 | tf_op jit(solution)/shard_map/ppermute | solution.py:355
  20.9 0.7 %shard_map.81 = bf16[32,24,128]{2,1,0:T(8,128)(2,1)} custom-call(f32[768,128]{1,0:T(8,128)S(1)} %get-tuple-element.53.mine, bf16[768,128]{1,0:T(8,128)(2,1)S(1)} %collective-permute-done.4.other), custom_call_target="tpu_custom_call" | custom-call | bytes 786432 | tf_op jit(solution)/shard_map/pallas_call | solution.py:20
  21.6 4.8 %all-to-all-start = ((bf16[32,24,128]{2,1,0:T(8,128)(2,1)}), bf16[32,24,128]{2,1,0:T(8,128)(2,1)S(1)}, u32[]{:S(2)}, u32[]{:S(2)}) async-start(bf16[32,24,128]{2,1,0:T(8,128)(2,1)} %shard_map.81), calls=%async_computation | async-start | bytes 393216 | tf_op jit(solution)/shard_map/all_to_all | solution.py:423
  26.5 1.8 %collective-permute-start.5 = (bf16[8,64,128]{2,1,0:T(8,128)(2,1)S(1)}, bf16[8,64,128]{2,1,0:T(8,128)(2,1)S(1)}, u32[]{:S(2)}, u32[]{:S(2)}) collective-permute-start(bf16[8,64,128]{2,1,0:T(8,128)(2,1)S(1)} %get-tuple-element.57.near), channel_id=1, source_target_pairs={{0,4},{8,12},{16,20},{24,28},{4,0},{12,8},{20,16},{28,24},{1,5},{9... | collective-permute-start | bytes 393224 | tf_op jit(solution)/shard_map/ppermute | solution.py:351
  28.3 3.3 %collective-permute-start.6 = (bf16[8,64,128]{2,1,0:T(8,128)(2,1)S(1)}, bf16[8,64,128]{2,1,0:T(8,128)(2,1)S(1)}, u32[]{:S(2)}, u32[]{:S(2)}) collective-permute-start(bf16[8,64,128]{2,1,0:T(8,128)(2,1)S(1)} %get-tuple-element.58.far), channel_id=1, source_target_pairs={{4,8},{12,16},{20,24},{28,0},{8,4},{16,12},{24,20},{0,28},{5,9},{1... | collective-permute-start | bytes 393224 | tf_op jit(solution)/shard_map/ppermute | solution.py:351
  31.6 4.2 %collective-permute-done.5.near_in = bf16[8,64,128]{2,1,0:T(8,128)(2,1)S(1)} collective-permute-done((bf16[8,64,128]{2,1,0:T(8,128)(2,1)S(1)}, bf16[8,64,128]{2,1,0:T(8,128)(2,1)S(1)}, u32[]{:S(2)}, u32[]{:S(2)}) %collective-permute-start.5) | collective-permute-done | bytes 131104 | tf_op jit(solution)/shard_map/ppermute | solution.py:351
  35.8 2.3 %collective-permute-done.6.far_in = bf16[8,64,128]{2,1,0:T(8,128)(2,1)S(1)} collective-permute-done((bf16[8,64,128]{2,1,0:T(8,128)(2,1)S(1)}, bf16[8,64,128]{2,1,0:T(8,128)(2,1)S(1)}, u32[]{:S(2)}, u32[]{:S(2)}) %collective-permute-start.6) | collective-permute-done | bytes 131104 | tf_op jit(solution)/shard_map/ppermute | solution.py:351
  38.2 0.1 collective-permute-start.7
  38.3 1.5 %collective-permute-start.8 = (bf16[4,64,128]{2,1,0:T(8,128)(2,1)S(1)}, bf16[4,64,128]{2,1,0:T(8,128)(2,1)S(1)}, u32[]{:S(2)}, u32[]{:S(2)}) collective-permute-start(bf16[4,64,128]{2,1,0:T(8,128)(2,1)S(1)} %get-tuple-element.60), channel_id=1, source_target_pairs={{1,2},{3,0},{2,1},{0,3},{5,6},{7,4},{6,5},{4,7},{9,10},{11,8},{10,... | collective-permute-start | bytes 196616 | tf_op jit(solution)/shard_map/ppermute | solution.py:351
  39.8 0.0 collective-permute-done.7.near
  39.8 2.4 %collective-permute-done.8.far = bf16[4,64,128]{2,1,0:T(8,128)(2,1)S(1)} collective-permute-done((bf16[4,64,128]{2,1,0:T(8,128)(2,1)S(1)}, bf16[4,64,128]{2,1,0:T(8,128)(2,1)S(1)}, u32[]{:S(2)}, u32[]{:S(2)}) %collective-permute-start.8) | collective-permute-done | bytes 65568 | tf_op jit(solution)/shard_map/ppermute | solution.py:351
  42.2 0.0 all-to-all-done.terms
  42.2 0.7 %shard_map.84 = bf16[32,24,128]{2,1,0:T(8,128)(2,1)} custom-call(bf16[32,24,128]{2,1,0:T(8,128)(2,1)S(1)} %all-to-all-done.terms), custom_call_target="tpu_custom_call" | custom-call | bytes 393216 | tf_op jit(solution)/shard_map/pallas_call | solution.py:20
  42.9 3.5 %all-to-all-start.1 = ((bf16[32,24,128]{2,1,0:T(8,128)(2,1)}), bf16[32,24,128]{2,1,0:T(8,128)(2,1)S(1)}, u32[]{:S(2)}, u32[]{:S(2)}) async-start(bf16[32,24,128]{2,1,0:T(8,128)(2,1)} %shard_map.84), calls=%async_computation.1 | async-start | bytes 393216 | tf_op jit(solution)/shard_map/all_to_all | solution.py:432
  46.4 0.3 copy.9
  46.7 0.2 copy.10
  46.9 0.2 copy.11.w_ref
  47.2 2.3 %shard_map.85.acc_ref = f32[2,8,64,128]{3,2,1,0:T(8,128)S(1)} custom-call(bf16[8,64,128]{2,1,0:T(8,128)(2,1)S(1)} %get-tuple-element.57.near, bf16[8,64,128]{2,1,0:T(8,128)(2,1)S(1)} %get-tuple-element.58.far, bf16[8,64,128]{2,1,0:T(8,128)(2,1)S(1)} %collective-permute-done.5.near_in, bf16[8,64,128]{2,1,0:T(8,128)(2,1)S(1)} %collective-permute-done.6.far_in, ...), custom_call_target="tpu_custom_call" | custom-call | flops 452984832 | bytes 1269760 | tf_op jit(solution)/shard_map/pallas_call | solution.py:20
  49.5 1.3 %shard_map.86 = f32[1024,128]{1,0:T(8,128)} custom-call(bf16[4,64,128]{2,1,0:T(8,128)(2,1)S(1)} %collective-permute-done.7.near, bf16[4,64,128]{2,1,0:T(8,128)(2,1)S(1)} %collective-permute-done.8.far, f32[2,8,64,128]{3,2,1,0:T(8,128)S(1)} %shard_map.85.acc_ref, bf16[3,3,64,192]{3,2,1,0:T(8,128)(2,1)S(1)} %copy.11.w_ref), custom_call_target="tpu_custom_call" | custom-call | flops 45298484 | bytes 1400832 | tf_op jit(solution)/shard_map/pallas_call | solution.py:20
  50.8 4.5 %all-to-all-done.1.mine = bf16[32,24,128]{2,1,0:T(8,128)(2,1)S(1)} async-done(((bf16[32,24,128]{2,1,0:T(8,128)(2,1)}), bf16[32,24,128]{2,1,0:T(8,128)(2,1)S(1)}, u32[]{:S(2)}, u32[]{:S(2)}) %all-to-all-start.1) | async-done | bytes 196640 | tf_op jit(solution)/shard_map/all_to_all | solution.py:432
  55.3 0.6 %collective-permute-start.9 = (bf16[32,24,128]{2,1,0:T(8,128)(2,1)S(1)}, bf16[32,24,128]{2,1,0:T(8,128)(2,1)S(1)}, u32[]{:S(2)}, u32[]{:S(2)}) collective-permute-start(bf16[32,24,128]{2,1,0:T(8,128)(2,1)S(1)} %all-to-all-done.1.mine), channel_id=1, source_target_pairs={{0,1},{1,0},{2,3},{3,2},{4,5},{5,4},{6,7},{7,6},{8,9},{9,8},{10,11... | collective-permute-start | bytes 589832 | tf_op jit(solution)/shard_map/ppermute | solution.py:355
  55.9 1.4 %shard_map.82 = bf16[128,256]{1,0:T(8,128)(2,1)} custom-call(bf16[2,8,64,128]{3,2,1,0:T(8,128)(2,1)S(1)} %get-tuple-element.55.h_ref, bf16[2,2,128,128]{3,2,1,0:T(8,128)(2,1)S(1)} %copy-done.3), custom_call_target="tpu_custom_call" | custom-call | flops 45298484 | bytes 458752 | tf_op jit(solution)/shard_map/pallas_call | solution.py:20
  57.3 0.0 collective-permute-done.9.other
  57.3 1.0 %shard_map.87 = (f32[3,3,64,192]{3,2,1,0:T(8,128)}, f32[2,2,128,128]{3,2,1,0:T(8,128)}) custom-call(bf16[32,24,128]{2,1,0:T(8,128)(2,1)S(1)} %all-to-all-done.1.mine, bf16[32,24,128]{2,1,0:T(8,128)(2,1)S(1)} %collective-permute-done.9.other), custom_call_target="tpu_custom_call" | custom-call | bytes 1097728 | tf_op jit(solution)/shard_map/pallas_call | solution.py:20
  (3 shorter events, 0.1 us)
Async XLA Ops:
  0.6 1.0 %copy-start.2 = (bf16[64,2,8,128]{3,2,1,0:T(8,128)(2,1)S(1)}, bf16[64,2,8,128]{3,2,1,0:T(8,128)(2,1)}, u32[]{:S(2)}) copy-start(bf16[64,2,8,128]{3,2,1,0:T(8,128)(2,1)} %f_ref.1) | copy-start | bytes 786436
  1.6 6.8 %copy-start.3 = (bf16[2,2,128,128]{3,2,1,0:T(8,128)(2,1)S(1)}, bf16[2,2,128,128]{3,2,1,0:T(8,128)(2,1)}, u32[]{:S(2)}) copy-start(bf16[2,2,128,128]{3,2,1,0:T(8,128)(2,1)} %d_ref.3) | copy-start | bytes 393220
  1.6 6.8 %copy-start.4 = (bf16[128,1,256]{2,0,1:T(8,128)(2,1)S(1)}, bf16[128,1,256]{2,0,1:T(8,128)(2,1)}, u32[]{:S(2)}) copy-start(bf16[128,1,256]{2,0,1:T(8,128)(2,1)} %param.7) | copy-start | bytes 196612
  1.8 9.5 %collective-permute-start = (bf16[8,64,128]{2,1,0:T(8,128)(2,1)S(1)}, bf16[8,64,128]{2,1,0:T(8,128)(2,1)S(1)}, u32[]{:S(2)}, u32[]{:S(2)}) collective-permute-start(bf16[8,64,128]{2,1,0:T(8,128)(2,1)S(1)} %get-tuple-element.36.near), channel_id=1, source_target_pairs={{0,4},{8,12},{16,20},{24,28},{4,0},{12,8},{20,16},{28,24},{1,5},{9... | collective-permute-start | bytes 393224 | tf_op jit(solution)/shard_map/ppermute | solution.py:351
  4.8 7.7 %collective-permute-start.1 = (bf16[8,64,128]{2,1,0:T(8,128)(2,1)S(1)}, bf16[8,64,128]{2,1,0:T(8,128)(2,1)S(1)}, u32[]{:S(2)}, u32[]{:S(2)}) collective-permute-start(bf16[8,64,128]{2,1,0:T(8,128)(2,1)S(1)} %get-tuple-element.37.far), channel_id=1, source_target_pairs={{4,8},{12,16},{20,24},{28,0},{8,4},{16,12},{24,20},{0,28},{5,9},{1... | collective-permute-start | bytes 393224 | tf_op jit(solution)/shard_map/ppermute | solution.py:351
  8.4 1.0 %copy-start = (bf16[3,3,64,192]{3,2,1,0:T(8,128)(2,1)S(1)}, bf16[3,3,64,192]{3,2,1,0:T(8,128)(2,1)}, u32[]{:S(2)}) copy-start(bf16[3,3,64,192]{3,2,1,0:T(8,128)(2,1)} %w_ref.5) | copy-start | bytes 663556
  11.3 3.0 %copy-start.1 = (bf16[3,3,64,192]{3,2,1,0:T(8,128)(2,1)S(1)}, bf16[3,3,64,192]{3,2,1,0:T(8,128)(2,1)}, u32[]{:S(2)}) copy-start(bf16[3,3,64,192]{3,2,1,0:T(8,128)(2,1)} %w_ref.5) | copy-start | bytes 663556
  12.5 3.1 %collective-permute-start.2 = (bf16[4,64,128]{2,1,0:T(8,128)(2,1)S(1)}, bf16[4,64,128]{2,1,0:T(8,128)(2,1)S(1)}, u32[]{:S(2)}, u32[]{:S(2)}) collective-permute-start(bf16[4,64,128]{2,1,0:T(8,128)(2,1)S(1)} %get-tuple-element.44), channel_id=1, source_target_pairs={{0,1},{2,3},{1,0},{3,2},{4,5},{6,7},{5,4},{7,6},{8,9},{10,11},{9,8... | collective-permute-start | bytes 196616 | tf_op jit(solution)/shard_map/ppermute | solution.py:351
  12.6 3.9 %collective-permute-start.3 = (bf16[4,64,128]{2,1,0:T(8,128)(2,1)S(1)}, bf16[4,64,128]{2,1,0:T(8,128)(2,1)S(1)}, u32[]{:S(2)}, u32[]{:S(2)}) collective-permute-start(bf16[4,64,128]{2,1,0:T(8,128)(2,1)S(1)} %get-tuple-element.45), channel_id=1, source_target_pairs={{1,2},{3,0},{2,1},{0,3},{5,6},{7,4},{6,5},{4,7},{9,10},{11,8},{10,... | collective-permute-start | bytes 196616 | tf_op jit(solution)/shard_map/ppermute | solution.py:351
  19.4 1.5 %collective-permute-start.4 = (bf16[768,128]{1,0:T(8,128)(2,1)S(1)}, bf16[768,128]{1,0:T(8,128)(2,1)S(1)}, u32[]{:S(2)}, u32[]{:S(2)}) collective-permute-start(bf16[768,128]{1,0:T(8,128)(2,1)S(1)} %get-tuple-element.54), channel_id=1, source_target_pairs={{0,1},{1,0},{2,3},{3,2},{4,5},{5,4},{6,7},{7,6},{8,9},{9,8},{10,11... | collective-permute-start | bytes 589832 | tf_op jit(solution)/shard_map/ppermute | solution.py:355
  21.6 20.5 %all-to-all-start = ((bf16[32,24,128]{2,1,0:T(8,128)(2,1)}), bf16[32,24,128]{2,1,0:T(8,128)(2,1)S(1)}, u32[]{:S(2)}, u32[]{:S(2)}) async-start(bf16[32,24,128]{2,1,0:T(8,128)(2,1)} %shard_map.81), calls=%async_computation | async-start | bytes 393216 | tf_op jit(solution)/shard_map/all_to_all | solution.py:423
  26.5 9.4 %collective-permute-start.5 = (bf16[8,64,128]{2,1,0:T(8,128)(2,1)S(1)}, bf16[8,64,128]{2,1,0:T(8,128)(2,1)S(1)}, u32[]{:S(2)}, u32[]{:S(2)}) collective-permute-start(bf16[8,64,128]{2,1,0:T(8,128)(2,1)S(1)} %get-tuple-element.57.near), channel_id=1, source_target_pairs={{0,4},{8,12},{16,20},{24,28},{4,0},{12,8},{20,16},{28,24},{1,5},{9... | collective-permute-start | bytes 393224 | tf_op jit(solution)/shard_map/ppermute | solution.py:351
  28.3 9.8 %collective-permute-start.6 = (bf16[8,64,128]{2,1,0:T(8,128)(2,1)S(1)}, bf16[8,64,128]{2,1,0:T(8,128)(2,1)S(1)}, u32[]{:S(2)}, u32[]{:S(2)}) collective-permute-start(bf16[8,64,128]{2,1,0:T(8,128)(2,1)S(1)} %get-tuple-element.58.far), channel_id=1, source_target_pairs={{4,8},{12,16},{20,24},{28,0},{8,4},{16,12},{24,20},{0,28},{5,9},{1... | collective-permute-start | bytes 393224 | tf_op jit(solution)/shard_map/ppermute | solution.py:351
  38.2 1.6 %collective-permute-start.7 = (bf16[4,64,128]{2,1,0:T(8,128)(2,1)S(1)}, bf16[4,64,128]{2,1,0:T(8,128)(2,1)S(1)}, u32[]{:S(2)}, u32[]{:S(2)}) collective-permute-start(bf16[4,64,128]{2,1,0:T(8,128)(2,1)S(1)} %get-tuple-element.59), channel_id=1, source_target_pairs={{0,1},{2,3},{1,0},{3,2},{4,5},{6,7},{5,4},{7,6},{8,9},{10,11},{9,8... | collective-permute-start | bytes 196616 | tf_op jit(solution)/shard_map/ppermute | solution.py:351
  38.3 3.9 %collective-permute-start.8 = (bf16[4,64,128]{2,1,0:T(8,128)(2,1)S(1)}, bf16[4,64,128]{2,1,0:T(8,128)(2,1)S(1)}, u32[]{:S(2)}, u32[]{:S(2)}) collective-permute-start(bf16[4,64,128]{2,1,0:T(8,128)(2,1)S(1)} %get-tuple-element.60), channel_id=1, source_target_pairs={{1,2},{3,0},{2,1},{0,3},{5,6},{7,4},{6,5},{4,7},{9,10},{11,8},{10,... | collective-permute-start | bytes 196616 | tf_op jit(solution)/shard_map/ppermute | solution.py:351
  42.9 12.4 %all-to-all-start.1 = ((bf16[32,24,128]{2,1,0:T(8,128)(2,1)}), bf16[32,24,128]{2,1,0:T(8,128)(2,1)S(1)}, u32[]{:S(2)}, u32[]{:S(2)}) async-start(bf16[32,24,128]{2,1,0:T(8,128)(2,1)} %shard_map.84), calls=%async_computation.1 | async-start | bytes 393216 | tf_op jit(solution)/shard_map/all_to_all | solution.py:432
  55.3 2.0 %collective-permute-start.9 = (bf16[32,24,128]{2,1,0:T(8,128)(2,1)S(1)}, bf16[32,24,128]{2,1,0:T(8,128)(2,1)S(1)}, u32[]{:S(2)}, u32[]{:S(2)}) collective-permute-start(bf16[32,24,128]{2,1,0:T(8,128)(2,1)S(1)} %all-to-all-done.1.mine), channel_id=1, source_target_pairs={{0,1},{1,0},{2,3},{3,2},{4,5},{5,4},{6,7},{7,6},{8,9},{9,8},{10,11... | collective-permute-start | bytes 589832 | tf_op jit(solution)/shard_map/ppermute | solution.py:355

commit v8 on v7

--- a/solution.py
+++ b/solution.py
@@ -220,7 +220,7 @@
     out_ref[...] = coarse.astype(BF16)
 
 
-def weight_grad_kernel(inner, outer, edges, near, far, h_ref, cot_ref, keep, send, packed):
+def weight_grad_kernel(inner, outer, edges, near, far, h_ref, cot_ref, keep0, keep1, send0, send1, packed):
     rows, channels, breadth = near.shape
     across = (((1,), (1,)), ((), ()))
     even = is_even("gz")
@@ -259,8 +259,10 @@
     end = base + 4 * height
     if end < packed.shape[0]:
         packed[end:] = jnp.zeros((packed.shape[0] - end, packed.shape[1]), F32)
-    half = packed.shape[0] // 2
-    split(packed, keep, send, half, "gy", 1)
+    rows0 = keep0.shape[0]
+    for keep, send, at in ((keep0, send0, slice(0, rows0)), (keep1, send1, slice(rows0, None))):
+        keep[...] = packed[at]
+        send[...] = packed[at].astype(BF16)
 
 
 def side_of(axis, bit):
@@ -271,27 +273,28 @@
     return pl.ds(pl.multiple_of(side * rows, 16), rows)
 
 
-def split(packed, keep, send, half, axis, bit):
+def halve_kernel(mine0, mine1, got0, got1, keep0, keep1, send0, send1, total0, total1, *, axis, bit):
     side = side_of(axis, bit)
-    keep[...] = packed[part(side, half)]
-    send[...] = packed[part(1 - side, half)].astype(BF16)
-
-
-def add_kernel(mine, other, out):
-    total = mine[...] + other[...].astype(F32)
-    out[...] = total.reshape(out.shape).astype(BF16)
-
-
-def total_kernel(terms, out):
-    count = terms.shape[0]
-    for core in range(2):
-        total = None
-        for s in range(core, count, 2):
-            term = terms[s].astype(F32)
-            total = term if total is None else total + term
-        total = total.astype(BF16)
-        for s in range(core, count, 2):
-            out[s] = total
+    for mine, got, keep, send, total in (
+        (mine0, got0, keep0, send0, total0), (mine1, got1, keep1, send1, total1)
+    ):
+        total[...] = mine[...] + got[...].astype(F32)
+        half = keep.shape[0]
+        keep[...] = total[part(side, half)]
+        send[...] = total[part(1 - side, half)].astype(BF16)
+
+
+def add_kernel(mine0, mine1, got0, got1, out0, out1):
+    out0[...] = (mine0[...].astype(F32) + got0[...].astype(F32)).astype(BF16)
+    out1[...] = (mine1[...].astype(F32) + got1[...].astype(F32)).astype(BF16)
+
+
+def join_kernel(mine0, mine1, got0, got1, out0, out1, *, axis, bit):
+    side = side_of(axis, bit)
+    for mine, got, out in ((mine0, got0, out0), (mine1, got1, out1)):
+        rows = mine.shape[0]
+        out[part(side, rows)] = mine[...]
+        out[part(1 - side, rows)] = got[...]
 
 
 def field_kernel(near, far, near_in, far_in, w_ref, acc_ref, inner, outer):
@@ -324,17 +327,17 @@
             out_ref[pl.ds(z * rows + y, channels, stride=2 * rows), :] = line
 
 
-def unpack_kernel(mine, other, conv_ref, down_ref, sums_ref, *, scale):
-    half = sums_ref.shape[0] // 2
-    side = side_of("gy", 1)
-    sums_ref[part(side, half)] = mine[...].astype(F32).reshape(half, sums_ref.shape[1])
-    sums_ref[part(1 - side, half)] = other[...].astype(F32).reshape(half, sums_ref.shape[1])
+def unpack_kernel(mine0, mine1, got0, got1, conv_ref, down_ref, sums_ref, *, scale):
+    even = is_even("gy")
+    rows0 = mine0.shape[0]
+    sums_ref[0:rows0] = choose(even, mine0[...], got0[...])
+    sums_ref[rows0:] = choose(even, got1[...], mine1[...])
     channels = conv_ref.shape[2]
     for a in range(3):
         for b in range(3):
             base = (a * 3 + b) * 3 * channels // 2
-            conv_ref[a, b, :, 0 : 2 * channels] = sums_ref[base : base + channels]* scale
-            rest = sums_ref[base + channels : base + 3 * channels // 2]* scale
+            conv_ref[a, b, :, 0 : 2 * channels] = sums_ref[base : base + channels].astype(F32) * scale
+            rest = sums_ref[base + channels : base + 3 * channels // 2].astype(F32) * scale
             conv_ref[a, b, 0 : channels // 2, 2 * channels :] = rest[:, 0:channels]
             conv_ref[a, b, channels // 2 :, 2 * channels :] = rest[:, channels:]
     base = 9 * 3 * channels // 2
@@ -342,7 +345,7 @@
     for a in range(2):
         for b in range(2):
             at = base + (2 * a + b) * height
-            down_ref[a, b] = sums_ref[at : at + height]* scale
+            down_ref[a, b] = sums_ref[at : at + height].astype(F32) * scale
 
 
 def swap(cells, axis, low):
@@ -351,8 +354,22 @@
     return lax.ppermute(cells, axis, pairs + [(b, a) for a, b in pairs])
 
 
-def flip(cells, axis, bit):
-    return lax.ppermute(cells, axis, [(i, i ^ bit) for i in range(lax.axis_size(axis))])
+def flip(pair, axis, bit):
+    row = lax.axis_size("gy")
+    mask = bit * row if axis == "gz" else bit
+    found = []
+    for core, cells in enumerate(pair):
+        devices = [i for i in range(lax.axis_size("gz") * row) if i % 2 == core]
+        found.append(lax.ppermute(cells, ("gz", "gy"), [(i, i ^ mask) for i in devices]))
+    return found
+
+
+def across(pair, sources):
+    count = lax.axis_size("gy")
+    return [
+        lax.ppermute(cells, "gy", [(i, i ^ 1) for i in range(count) if i % 2 == core])
+        for core, cells in zip(sources, pair)
+    ]
 
 
 def tied(first, *others):
@@ -401,39 +418,70 @@
     gates = (near, far)
 
     used = 27 * channels * channels // 128 + 4 * out_channels
-    share = -(-used // (16 * count)) * 8
-    half = share * count
-    parts = ((count, share, 128), BF16)
-    keep, send = call(
-        weight_grad_kernel, [((half, 128), F32), ((half, 128), BF16)], [((2 * half, 128), F32)], conv_flops,
+    total = -(-used // 64)
+    sizes = [64 * (total // 3), 64 * (total - total // 3)]
+
+    def both(shrink, kind):
+        return [((size // shrink, 128), kind) for size in sizes]
+
+    found = call(
+        weight_grad_kernel, [*both(1, F32), *both(1, BF16)], [((sum(sizes), 128), F32)], conv_flops,
         (inner, outer, edges, *gates, hidden, cot),
     )
-    exchange = functools.partial(
-        lax.all_to_all, axis_name=("gz", "gy"), split_axis=0, concat_axis=0, tiled=True
-    )
-    keep, gates = tied(keep, *gates)
+    keep, send = list(found[:2]), found[2:]
+    keep[0], (hidden, *gates) = tied(keep[0], hidden, *gates)
     near, far = gates
-    outside = swap(near, "gz", 0), swap(far, "gz", 1)
-    (terms,) = call(add_kernel, [parts], [], 0, (keep, flip(send, "gy", 1)))
-    terms, (hidden,) = tied(terms, hidden)
-    (section_out,) = call(
-        section_kernel, [((out_channels, cot.shape[1]), BF16)], [], conv_flops // 10, (hidden, down_weight)
-    )
-    beside = swapped(*call(edges_kernel, [edge, edge], [], 0, (*gates, *outside)), "gy")
-    terms, beside = tied(exchange(terms), *beside)
-    (sums,) = call(total_kernel, [parts], [], 0, (terms,))
+    near_in = swap(near, "gz", 0)
+    got = across(send, (1, 0))
+    for level, (axis, bit) in enumerate((("gy", 2), ("gz", 2))):
+        shrink = 2 << level
+        found = call(
+            functools.partial(halve_kernel, axis=axis, bit=bit),
+            [*both(shrink, F32), *both(shrink, BF16)], both(shrink // 2, F32), 0, (*keep, *got),
+        )
+        keep, send = list(found[:2]), found[2:]
+        if level == 0:
+            keep[0], (far,) = tied(keep[0], far)
+            far_in = swap(far, "gz", 1)
+            (section_out,) = call(
+                section_kernel, [((out_channels, cot.shape[1]), BF16)], [], conv_flops // 10,
+                (hidden, down_weight),
+            )
+        got = flip(send, axis, bit)
+    sums = list(call(add_kernel, both(4, BF16), [], 0, (*keep, *got)))
+    sums[0], outside = tied(sums[0], near_in, far_in)
+    sends = call(edges_kernel, [edge, edge], [], 0, (*gates, *outside))
+    beside = swapped(*sends, "gy")
     (acc,) = call(
         field_kernel, [(lines, F32)], [cols, cols], conv_flops, (*gates, *outside, weight_bwd)
     )
+    bits = [("gz", 1)]
+    bits += [("gy", 1 << k) for k in range(2, lax.axis_size("gy").bit_length() - 1)]
+    bits += [("gz", 1 << k) for k in range(2, lax.axis_size("gz").bit_length() - 1)]
+    for axis, bit in bits:
+        sums = list(call(add_kernel, both(4, BF16), [], 0, (*sums, *flip(sums, axis, bit))))
+    sums[0], (*beside, section_out) = tied(sums[0], *beside, section_out)
+    sums = list(
+        call(
+            functools.partial(join_kernel, axis="gz", bit=2), both(2, BF16), [], 0,
+            (*sums, *flip(sums, "gz", 2)),
+        )
+    )
+    sums[0], (acc,) = tied(sums[0], acc)
     (field,) = call(
         field_edges_kernel, [((channels * plane_count * row_count, breadth), F32)], [edge_cols],
         conv_flops // 10, (*beside, acc, weight_bwd),
     )
-    sums, (field,) = tied(exchange(sums), field)
+    sums = call(
+        functools.partial(join_kernel, axis="gy", bit=2), both(1, BF16), [], 0,
+        (*sums, *flip(sums, "gy", 2)),
+    )
+    got = across(sums, (0, 1))
+    got[0], (field,) = tied(got[0], field)
     grad_conv, grad_down = call(
         functools.partial(unpack_kernel, scale=grad_scale),
-        [(conv_weight.shape, F32), (down_weight.shape, F32)], [((2 * half, 128), F32)], 0,
-        (sums, flip(sums, "gy", 1)),
+        [(conv_weight.shape, F32), (down_weight.shape, F32)], [((sum(sizes), 128), BF16)], 0,
+        (*sums, *got),
     )
     section_out = section_out.reshape(out_channels, plane_count // 2, -1)
     return (section_out, field.reshape(features.shape), grad_conv, grad_down)

time: 58.6 us -> 79 us (1.35)
  starting transfers between devices: 24.4 us -> 40.3 us
  waiting for transfers between devices: 16.6 us -> 21.9 us
  Pallas kernels: 13.8 us -> 12.7 us
    ppermute x2 -> x16, starting transfers between devices: 1.06 us -> 27.3 us  [the longest x12 19.3 us: flip(): lax.ppermute(cells, ('gz', 'gy'), [(i, i ^ mask) for i in devices])]
    ppermute x2 -> x16, waiting for transfers between devices: 1.07 us -> 19.8 us  [the longest x12 17.9 us: flip(): lax.ppermute(cells, ('gz', 'gy'), [(i, i ^ mask) for i in devices])]
    ppermute x8, waiting for transfers between devices: 11 us -> 2.13 us  [swap(): return lax.ppermute(cells, axis, pairs + [(b, a) for a, b in pairs])]
    all_to_all x2 -> x0, starting transfers between devices: 8.34 us -> none  [the longest x1 4.84 us: body(): terms, beside = tied(exchange(terms), *beside)]
    all_to_all x2 -> x0, waiting for transfers between devices: 4.48 us -> none  [the longest x1 4.48 us: body(): sums, (field,) = tied(exchange(sums), field)]
    ppermute x8, starting transfers between devices: 15 us -> 13 us  [swap(): return lax.ppermute(cells, axis, pairs + [(b, a) for a, b in pairs])]
    pallas_call x13 -> x18, Pallas kernels: 13.8 us -> 12.7 us  [call(): pl.pallas_call(kernel, out_shape=[jax.ShapeDtypeStruct(s, d) for s, d in...]
  transfers between devices with their start and end apart: 12 -> 24, of which waited for: 7 -> 8; matrix products, arithmetic and copies ran while one was open for 1% -> 1% of each run, Pallas kernels for 14% -> 11%
where the time goes in v8:
time: 79 us; the launch traced here: 78.6 us
  starting transfers between devices  40.3 us (51%)
  waiting for transfers between devices  21.9 us (28%)
  Pallas kernels  12.7 us (16%)
  local copies, waits for them, and re-layouts  2.7 us (3%)
  between operations  0.95 us (1%)
    ppermute x12, starting transfers between devices, flip(): lax.ppermute(cells, ('gz', 'gy'), [(i, i ^ mask) for i in devices])  19.3 us
    ppermute x12, waiting for transfers between devices, flip(): lax.ppermute(cells, ('gz', 'gy'), [(i, i ^ mask) for i in devices])  17.9 us
    ppermute x8, starting transfers between devices, swap(): return lax.ppermute(cells, axis, pairs + [(b, a) for a, b in pairs])  13 us
    pallas_call x18, Pallas kernels, call(): pl.pallas_call(kernel, out_shape=[jax.ShapeDtypeStruct(s, d) for s, d in...  12.7 us
    ppermute x4, starting transfers between devices, across(): lax.ppermute(cells, 'gy', [(i, i ^ 1) for i in range(count) if i % 2 == c...  7.96 us
    unnamed x11, local copies, waits for them, and re-layouts  2.18 us
    ppermute x8, waiting for transfers between devices, swap(): return lax.ppermute(cells, axis, pairs + [(b, a) for a, b in pairs])  2.13 us
    ppermute x4, waiting for transfers between devices, across(): lax.ppermute(cells, 'gy', [(i, i ^ 1) for i in range(count) if i % 2 == c...  1.93 us
  transfers between devices with their start and end apart: 24, of which 8 were waited for; matrix products, arithmetic and copies ran while one was open for 1% of the time, Pallas kernels for 11%

profile of v8, /device:TPU:0, one launch (start us, length us, event | category | flops | bytes accessed | tf_op | source)
XLA Modules:
  0.0 78.6 jit_solution(15064377929033293655)
XLA Ops:
  0.6 0.9 %copy-done.2 = bf16[64,2,8,128]{3,2,1,0:T(8,128)(2,1)S(1)} copy-done((bf16[64,2,8,128]{3,2,1,0:T(8,128)(2,1)S(1)}, bf16[64,2,8,128]{3,2,1,0:T(8,128)(2,1)}, u32[]{:S(2)}) %copy-start.2) | copy-done | bytes 262168
  1.6 0.2 shard_map.75
  1.8 3.0 %collective-permute-start = (bf16[8,64,128]{2,1,0:T(8,128)(2,1)S(1)}, bf16[8,64,128]{2,1,0:T(8,128)(2,1)S(1)}, u32[]{:S(2)}, u32[]{:S(2)}) collective-permute-start(bf16[8,64,128]{2,1,0:T(8,128)(2,1)S(1)} %get-tuple-element.63.near), channel_id=1, source_target_pairs={{0,4},{8,12},{16,20},{24,28},{4,0},{12,8},{20,16},{28,24},{1,5},{9... | collective-permute-start | bytes 393224 | tf_op jit(solution)/shard_map/ppermute | solution.py:354
  4.8 3.5 %collective-permute-start.1 = (bf16[8,64,128]{2,1,0:T(8,128)(2,1)S(1)}, bf16[8,64,128]{2,1,0:T(8,128)(2,1)S(1)}, u32[]{:S(2)}, u32[]{:S(2)}) collective-permute-start(bf16[8,64,128]{2,1,0:T(8,128)(2,1)S(1)} %get-tuple-element.64.far), channel_id=1, source_target_pairs={{4,8},{12,16},{20,24},{28,0},{8,4},{16,12},{24,20},{0,28},{5,9},{1... | collective-permute-start | bytes 393224 | tf_op jit(solution)/shard_map/ppermute | solution.py:354
  8.4 1.0 %copy-done = bf16[3,3,64,192]{3,2,1,0:T(8,128)(2,1)S(1)} copy-done((bf16[3,3,64,192]{3,2,1,0:T(8,128)(2,1)S(1)}, bf16[3,3,64,192]{3,2,1,0:T(8,128)(2,1)}, u32[]{:S(2)}) %copy-start) | copy-done | bytes 221208
  9.3 1.9 %shard_map.76 = (bf16[2,10,192,128]{3,2,1,0:T(8,128)(2,1)S(1)}, f32[2,8,64,128]{3,2,1,0:T(8,128)S(1)}, f32[2,8,64,128]{3,2,1,0:T(8,128)S(1)}) custom-call(bf16[8,64,128]{2,1,0:T(8,128)(2,1)S(1)} %get-tuple-element.63.near, bf16[8,64,128]{2,1,0:T(8,128)(2,1)S(1)} %get-tuple-element.64.far, bf16[3,3,64,192]{3,2,1,0:T(8,128)(2,1)S(1)} %copy-done, ...), custom_call_target="tpu_custom_call" | custom-call | flops 301989888 | bytes 2711552 | tf_op jit(solution)/shard_map/pallas_call | solution.py:20
  11.3 1.2 %collective-permute-done.1.far.far_in = bf16[8,64,128]{2,1,0:T(8,128)(2,1)S(1)} collective-permute-done((bf16[8,64,128]{2,1,0:T(8,128)(2,1)S(1)}, bf16[8,64,128]{2,1,0:T(8,128)(2,1)S(1)}, u32[]{:S(2)}, u32[]{:S(2)}) %collective-permute-start.1) | collective-permute-done | bytes 131104 | tf_op jit(solution)/shard_map/ppermute | solution.py:354
  12.5 0.1 collective-permute-start.2
  12.6 1.6 %collective-permute-start.3 = (bf16[4,64,128]{2,1,0:T(8,128)(2,1)S(1)}, bf16[4,64,128]{2,1,0:T(8,128)(2,1)S(1)}, u32[]{:S(2)}, u32[]{:S(2)}) collective-permute-start(bf16[4,64,128]{2,1,0:T(8,128)(2,1)S(1)} %get-tuple-element.72), channel_id=1, source_target_pairs={{1,2},{3,0},{2,1},{0,3},{5,6},{7,4},{6,5},{4,7},{9,10},{11,8},{10,... | collective-permute-start | bytes 196616 | tf_op jit(solution)/shard_map/ppermute | solution.py:354
  14.2 1.4 %shard_map.77 = (bf16[2,10,192,128]{3,2,1,0:T(8,128)(2,1)S(1)}, f32[2,8,64,128]{3,2,1,0:T(8,128)S(1)}) custom-call(bf16[8,64,128]{2,1,0:T(8,128)(2,1)S(1)} %collective-permute-done.near.near_in, bf16[8,64,128]{2,1,0:T(8,128)(2,1)S(1)} %collective-permute-done.1.far.far_in, bf16[3,3,64,192]{3,2,1,0:T(8,128)(2,1)S(1)} %copy-done.1, ...), custom_call_target="tpu_custom_call" | custom-call | flops 150994944 | bytes 2514944 | tf_op jit(solution)/shard_map/pallas_call | solution.py:20
  15.6 0.9 %collective-permute-done.3.far = bf16[4,64,128]{2,1,0:T(8,128)(2,1)S(1)} collective-permute-done((bf16[4,64,128]{2,1,0:T(8,128)(2,1)S(1)}, bf16[4,64,128]{2,1,0:T(8,128)(2,1)S(1)}, u32[]{:S(2)}, u32[]{:S(2)}) %collective-permute-start.3) | collective-permute-done | bytes 65568 | tf_op jit(solution)/shard_map/ppermute | solution.py:354
  16.5 0.5 shard_map.79
  17.0 2.3 %shard_map.80 = (f32[448,128]{1,0:T(8,128)S(1)}, f32[960,128]{1,0:T(8,128)S(1)}, bf16[448,128]{1,0:T(8,128)(2,1)S(1)}, bf16[960,128]{1,0:T(8,128)(2,1)S(1)}) custom-call(bf16[2,10,192,128]{3,2,1,0:T(8,128)(2,1)S(1)} %get-tuple-element.65.inner, bf16[2,10,192,128]{3,2,1,0:T(8,128)(2,1)S(1)} %get-tuple-element.70.outer, ...), custom_call_target="tpu_custom_call" | custom-call | flops 452984832 | bytes 4030464 | tf_op jit(solution)/shard_map/pallas_call | solution.py:20
  19.3 2.3 %collective-permute-start.5 = (bf16[960,128]{1,0:T(8,128)(2,1)S(1)}, bf16[960,128]{1,0:T(8,128)(2,1)S(1)}, u32[]{:S(2)}, u32[]{:S(2)}) collective-permute-start(bf16[960,128]{1,0:T(8,128)(2,1)S(1)} %get-tuple-element.83), channel_id=1, source_target_pairs={{0,1},{2,3},{4,5},{6,7},{8,9},{10,11},{12,13},{14,15},{16,17},{18,... | collective-permute-start | bytes 737288 | tf_op jit(solution)/shard_map/ppermute | solution.py:370
  21.6 1.3 %collective-permute-start.4 = (bf16[448,128]{1,0:T(8,128)(2,1)S(1)}, bf16[448,128]{1,0:T(8,128)(2,1)S(1)}, u32[]{:S(2)}, u32[]{:S(2)}) collective-permute-start(bf16[448,128]{1,0:T(8,128)(2,1)S(1)} %get-tuple-element.82), channel_id=1, source_target_pairs={{1,0},{3,2},{5,4},{7,6},{9,8},{11,10},{13,12},{15,14},{17,16},{19,... | collective-permute-start | bytes 344072 | tf_op jit(solution)/shard_map/ppermute | solution.py:370
  22.9 1.9 %collective-permute-done.4.got0 = bf16[448,128]{1,0:T(8,128)(2,1)S(1)} collective-permute-done((bf16[448,128]{1,0:T(8,128)(2,1)S(1)}, bf16[448,128]{1,0:T(8,128)(2,1)S(1)}, u32[]{:S(2)}, u32[]{:S(2)}) %collective-permute-start.4) | collective-permute-done | bytes 114720 | tf_op jit(solution)/shard_map/ppermute | solution.py:370
  24.9 0.1 shard_map.81
  25.0 0.7 collective-permute-start.7
  25.7 3.4 %collective-permute-start.6 = (bf16[224,128]{1,0:T(8,128)(2,1)S(1)}, bf16[224,128]{1,0:T(8,128)(2,1)S(1)}, u32[]{:S(2)}, u32[]{:S(2)}) collective-permute-start(bf16[224,128]{1,0:T(8,128)(2,1)S(1)} %get-tuple-element.88), channel_id=1, source_target_pairs={{0,2},{2,0},{4,6},{6,4},{8,10},{10,8},{12,14},{14,12},{16,18},{18,... | collective-permute-start | bytes 172040 | tf_op jit(solution)/shard_map/ppermute | solution.py:363
  29.1 0.5 collective-permute-start.10
  29.5 3.5 %collective-permute-start.11 = (bf16[8,64,128]{2,1,0:T(8,128)(2,1)S(1)}, bf16[8,64,128]{2,1,0:T(8,128)(2,1)S(1)}, u32[]{:S(2)}, u32[]{:S(2)}) collective-permute-start(bf16[8,64,128]{2,1,0:T(8,128)(2,1)S(1)} %get-tuple-element.96.far), channel_id=1, source_target_pairs={{4,8},{12,16},{20,24},{28,0},{8,4},{16,12},{24,20},{0,28},{5,9},{1... | collective-permute-start | bytes 393224 | tf_op jit(solution)/shard_map/ppermute | solution.py:354
  33.1 0.1 shard_map.82
  33.1 0.7 collective-permute-start.9
  33.8 1.9 %collective-permute-start.8 = (bf16[112,128]{1,0:T(8,128)(2,1)S(1)}, bf16[112,128]{1,0:T(8,128)(2,1)S(1)}, u32[]{:S(2)}, u32[]{:S(2)}) collective-permute-start(bf16[112,128]{1,0:T(8,128)(2,1)S(1)} %get-tuple-element.92), channel_id=1, source_target_pairs={{0,8},{2,10},{4,12},{6,14},{8,0},{10,2},{12,4},{14,6},{16,24},{18,... | collective-permute-start | bytes 86024 | tf_op jit(solution)/shard_map/ppermute | solution.py:363
  35.7 3.8 %collective-permute-done.8.got0 = bf16[112,128]{1,0:T(8,128)(2,1)S(1)} collective-permute-done((bf16[112,128]{1,0:T(8,128)(2,1)S(1)}, bf16[112,128]{1,0:T(8,128)(2,1)S(1)}, u32[]{:S(2)}, u32[]{:S(2)}) %collective-permute-start.8) | collective-permute-done | bytes 28704 | tf_op jit(solution)/shard_map/ppermute | solution.py:363
  39.6 0.7 collective-permute-start.13
  40.3 1.9 %collective-permute-start.12 = (bf16[112,128]{1,0:T(8,128)(2,1)S(1)}, bf16[112,128]{1,0:T(8,128)(2,1)S(1)}, u32[]{:S(2)}, u32[]{:S(2)}) collective-permute-start(bf16[112,128]{1,0:T(8,128)(2,1)S(1)} %get-tuple-element.97.mine0), channel_id=1, source_target_pairs={{0,4},{2,6},{4,0},{6,2},{8,12},{10,14},{12,8},{14,10},{16,20},{18,... | collective-permute-start | bytes 86024 | tf_op jit(solution)/shard_map/ppermute | solution.py:363
  42.2 3.8 %collective-permute-done.12.got0 = bf16[112,128]{1,0:T(8,128)(2,1)S(1)} collective-permute-done((bf16[112,128]{1,0:T(8,128)(2,1)S(1)}, bf16[112,128]{1,0:T(8,128)(2,1)S(1)}, u32[]{:S(2)}, u32[]{:S(2)}) %collective-permute-start.12) | collective-permute-done | bytes 28704 | tf_op jit(solution)/shard_map/ppermute | solution.py:363
  46.1 0.7 collective-permute-start.15
  46.8 0.1 collective-permute-start.16
  46.9 0.7 collective-permute-start.17
  47.5 2.9 %collective-permute-start.14 = (bf16[112,128]{1,0:T(8,128)(2,1)S(1)}, bf16[112,128]{1,0:T(8,128)(2,1)S(1)}, u32[]{:S(2)}, u32[]{:S(2)}) collective-permute-start(bf16[112,128]{1,0:T(8,128)(2,1)S(1)} %get-tuple-element.99.mine0), channel_id=1, source_target_pairs={{0,16},{2,18},{4,20},{6,22},{8,24},{10,26},{12,28},{14,30},{16,0},... | collective-permute-start | bytes 86024 | tf_op jit(solution)/shard_map/ppermute | solution.py:363
  50.5 3.8 %collective-permute-done.14.got0 = bf16[112,128]{1,0:T(8,128)(2,1)S(1)} collective-permute-done((bf16[112,128]{1,0:T(8,128)(2,1)S(1)}, bf16[112,128]{1,0:T(8,128)(2,1)S(1)}, u32[]{:S(2)}, u32[]{:S(2)}) %collective-permute-start.14) | collective-permute-done | bytes 28704 | tf_op jit(solution)/shard_map/ppermute | solution.py:363
  54.3 0.7 collective-permute-start.19
  55.0 1.4 %shard_map.87 = bf16[128,256]{1,0:T(8,128)(2,1)} custom-call(bf16[2,8,64,128]{3,2,1,0:T(8,128)(2,1)S(1)} %get-tuple-element.106.h_ref, bf16[2,2,128,128]{3,2,1,0:T(8,128)(2,1)S(1)} %copy-done.3), custom_call_target="tpu_custom_call" | custom-call | flops 45298484 | bytes 458752 | tf_op jit(solution)/shard_map/pallas_call | solution.py:20
  56.4 1.9 %collective-permute-start.18 = (bf16[112,128]{1,0:T(8,128)(2,1)S(1)}, bf16[112,128]{1,0:T(8,128)(2,1)S(1)}, u32[]{:S(2)}, u32[]{:S(2)}) collective-permute-start(bf16[112,128]{1,0:T(8,128)(2,1)S(1)} %get-tuple-element.108.mine0), channel_id=1, source_target_pairs={{0,8},{2,10},{4,12},{6,14},{8,0},{10,2},{12,4},{14,6},{16,24},{18,... | collective-permute-start | bytes 86024 | tf_op jit(solution)/shard_map/ppermute | solution.py:363
  58.3 0.3 copy.9
  58.6 3.6 %collective-permute-done.18.got0 = bf16[112,128]{1,0:T(8,128)(2,1)S(1)} collective-permute-done((bf16[112,128]{1,0:T(8,128)(2,1)S(1)}, bf16[112,128]{1,0:T(8,128)(2,1)S(1)}, u32[]{:S(2)}, u32[]{:S(2)}) %collective-permute-start.18) | collective-permute-done | bytes 28704 | tf_op jit(solution)/shard_map/ppermute | solution.py:363
  62.2 0.7 collective-permute-start.21
  62.9 0.3 copy.10
  63.2 0.2 copy.11.w_ref
  63.4 2.3 %shard_map.89.acc_ref = f32[2,8,64,128]{3,2,1,0:T(8,128)S(1)} custom-call(bf16[8,64,128]{2,1,0:T(8,128)(2,1)S(1)} %get-tuple-element.95.near, bf16[8,64,128]{2,1,0:T(8,128)(2,1)S(1)} %get-tuple-element.96.far, bf16[8,64,128]{2,1,0:T(8,128)(2,1)S(1)} %collective-permute-done.10.near_in, bf16[8,64,128]{2,1,0:T(8,128)(2,1)S(1)} %collective-permute-done.11.far_in, ...), custom_call_target="tpu_custom_call" | custom-call | flops 452984832 | bytes 1269760 | tf_op jit(solution)/shard_map/pallas_call | solution.py:20
  65.7 3.3 %collective-permute-start.20 = (bf16[224,128]{1,0:T(8,128)(2,1)S(1)}, bf16[224,128]{1,0:T(8,128)(2,1)S(1)}, u32[]{:S(2)}, u32[]{:S(2)}) collective-permute-start(bf16[224,128]{1,0:T(8,128)(2,1)S(1)} %get-tuple-element.111.mine0), channel_id=1, source_target_pairs={{0,2},{2,0},{4,6},{6,4},{8,10},{10,8},{12,14},{14,12},{16,18},{18,... | collective-permute-start | bytes 172040 | tf_op jit(solution)/shard_map/ppermute | solution.py:363
  69.0 2.8 %collective-permute-done.20.got0 = bf16[224,128]{1,0:T(8,128)(2,1)S(1)} collective-permute-done((bf16[224,128]{1,0:T(8,128)(2,1)S(1)}, bf16[224,128]{1,0:T(8,128)(2,1)S(1)}, u32[]{:S(2)}, u32[]{:S(2)}) %collective-permute-start.20) | collective-permute-done | bytes 57376 | tf_op jit(solution)/shard_map/ppermute | solution.py:363
  71.8 1.3 %collective-permute-start.23 = (bf16[960,128]{1,0:T(8,128)(2,1)S(1)}, bf16[960,128]{1,0:T(8,128)(2,1)S(1)}, u32[]{:S(2)}, u32[]{:S(2)}) collective-permute-start(bf16[960,128]{1,0:T(8,128)(2,1)S(1)} %get-tuple-element.118.mine1), channel_id=1, source_target_pairs={{1,0},{3,2},{5,4},{7,6},{9,8},{11,10},{13,12},{15,14},{17,16},{19,... | collective-permute-start | bytes 737288 | tf_op jit(solution)/shard_map/ppermute | solution.py:370
  73.1 3.0 %collective-permute-start.22 = (bf16[448,128]{1,0:T(8,128)(2,1)S(1)}, bf16[448,128]{1,0:T(8,128)(2,1)S(1)}, u32[]{:S(2)}, u32[]{:S(2)}) collective-permute-start(bf16[448,128]{1,0:T(8,128)(2,1)S(1)} %get-tuple-element.113.mine0), channel_id=1, source_target_pairs={{0,1},{2,3},{4,5},{6,7},{8,9},{10,11},{12,13},{14,15},{16,17},{18,... | collective-permute-start | bytes 344072 | tf_op jit(solution)/shard_map/ppermute | solution.py:370
  76.2 1.3 %shard_map.91 = f32[1024,128]{1,0:T(8,128)} custom-call(bf16[4,64,128]{2,1,0:T(8,128)(2,1)S(1)} %collective-permute-done.16.near, bf16[4,64,128]{2,1,0:T(8,128)(2,1)S(1)} %collective-permute-done.17.far, f32[2,8,64,128]{3,2,1,0:T(8,128)S(1)} %shard_map.89.acc_ref, bf16[3,3,64,192]{3,2,1,0:T(8,128)(2,1)S(1)} %copy.11.w_ref), custom_call_target="tpu_custom_call" | custom-call | flops 45298484 | bytes 1400832 | tf_op jit(solution)/shard_map/pallas_call | solution.py:20
  77.5 1.0 %shard_map.92 = (f32[3,3,64,192]{3,2,1,0:T(8,128)}, f32[2,2,128,128]{3,2,1,0:T(8,128)}) custom-call(bf16[448,128]{1,0:T(8,128)(2,1)S(1)} %get-tuple-element.113.mine0, bf16[960,128]{1,0:T(8,128)(2,1)S(1)} %get-tuple-element.118.mine1, bf16[448,128]{1,0:T(8,128)(2,1)S(1)} %collective-permute-done.22.got0, bf16[960,128]{1,0:T(8,128)(2,1)S(1)} %collective-permute-done.23.got1), custom_call_target="tpu_custom_call" | custom-call | bytes 1425408 | tf_op jit(solution)/shard_map/pallas_call | solution.py:20
  (32 shorter events, 0.3 us)
Async XLA Ops:
  0.6 1.0 %copy-start.2 = (bf16[64,2,8,128]{3,2,1,0:T(8,128)(2,1)S(1)}, bf16[64,2,8,128]{3,2,1,0:T(8,128)(2,1)}, u32[]{:S(2)}) copy-start(bf16[64,2,8,128]{3,2,1,0:T(8,128)(2,1)} %f_ref.1) | copy-start | bytes 786436
  1.6 6.8 %copy-start.3 = (bf16[2,2,128,128]{3,2,1,0:T(8,128)(2,1)S(1)}, bf16[2,2,128,128]{3,2,1,0:T(8,128)(2,1)}, u32[]{:S(2)}) copy-start(bf16[2,2,128,128]{3,2,1,0:T(8,128)(2,1)} %d_ref.3) | copy-start | bytes 393220
  1.6 6.8 %copy-start.4 = (bf16[128,1,256]{2,0,1:T(8,128)(2,1)S(1)}, bf16[128,1,256]{2,0,1:T(8,128)(2,1)}, u32[]{:S(2)}) copy-start(bf16[128,1,256]{2,0,1:T(8,128)(2,1)} %param.7) | copy-start | bytes 196612
  1.8 9.5 %collective-permute-start = (bf16[8,64,128]{2,1,0:T(8,128)(2,1)S(1)}, bf16[8,64,128]{2,1,0:T(8,128)(2,1)S(1)}, u32[]{:S(2)}, u32[]{:S(2)}) collective-permute-start(bf16[8,64,128]{2,1,0:T(8,128)(2,1)S(1)} %get-tuple-element.63.near), channel_id=1, source_target_pairs={{0,4},{8,12},{16,20},{24,28},{4,0},{12,8},{20,16},{28,24},{1,5},{9... | collective-permute-start | bytes 393224 | tf_op jit(solution)/shard_map/ppermute | solution.py:354
  4.8 7.7 %collective-permute-start.1 = (bf16[8,64,128]{2,1,0:T(8,128)(2,1)S(1)}, bf16[8,64,128]{2,1,0:T(8,128)(2,1)S(1)}, u32[]{:S(2)}, u32[]{:S(2)}) collective-permute-start(bf16[8,64,128]{2,1,0:T(8,128)(2,1)S(1)} %get-tuple-element.64.far), channel_id=1, source_target_pairs={{4,8},{12,16},{20,24},{28,0},{8,4},{16,12},{24,20},{0,28},{5,9},{1... | collective-permute-start | bytes 393224 | tf_op jit(solution)/shard_map/ppermute | solution.py:354
  8.4 1.0 %copy-start = (bf16[3,3,64,192]{3,2,1,0:T(8,128)(2,1)S(1)}, bf16[3,3,64,192]{3,2,1,0:T(8,128)(2,1)}, u32[]{:S(2)}) copy-start(bf16[3,3,64,192]{3,2,1,0:T(8,128)(2,1)} %w_ref.5) | copy-start | bytes 663556
  11.3 3.0 %copy-start.1 = (bf16[3,3,64,192]{3,2,1,0:T(8,128)(2,1)S(1)}, bf16[3,3,64,192]{3,2,1,0:T(8,128)(2,1)}, u32[]{:S(2)}) copy-start(bf16[3,3,64,192]{3,2,1,0:T(8,128)(2,1)} %w_ref.5) | copy-start | bytes 663556
  12.5 3.1 %collective-permute-start.2 = (bf16[4,64,128]{2,1,0:T(8,128)(2,1)S(1)}, bf16[4,64,128]{2,1,0:T(8,128)(2,1)S(1)}, u32[]{:S(2)}, u32[]{:S(2)}) collective-permute-start(bf16[4,64,128]{2,1,0:T(8,128)(2,1)S(1)} %get-tuple-element.71), channel_id=1, source_target_pairs={{0,1},{2,3},{1,0},{3,2},{4,5},{6,7},{5,4},{7,6},{8,9},{10,11},{9,8... | collective-permute-start | bytes 196616 | tf_op jit(solution)/shard_map/ppermute | solution.py:354
  12.6 3.9 %collective-permute-start.3 = (bf16[4,64,128]{2,1,0:T(8,128)(2,1)S(1)}, bf16[4,64,128]{2,1,0:T(8,128)(2,1)S(1)}, u32[]{:S(2)}, u32[]{:S(2)}) collective-permute-start(bf16[4,64,128]{2,1,0:T(8,128)(2,1)S(1)} %get-tuple-element.72), channel_id=1, source_target_pairs={{1,2},{3,0},{2,1},{0,3},{5,6},{7,4},{6,5},{4,7},{9,10},{11,8},{10,... | collective-permute-start | bytes 196616 | tf_op jit(solution)/shard_map/ppermute | solution.py:354
  19.3 5.6 %collective-permute-start.5 = (bf16[960,128]{1,0:T(8,128)(2,1)S(1)}, bf16[960,128]{1,0:T(8,128)(2,1)S(1)}, u32[]{:S(2)}, u32[]{:S(2)}) collective-permute-start(bf16[960,128]{1,0:T(8,128)(2,1)S(1)} %get-tuple-element.83), channel_id=1, source_target_pairs={{0,1},{2,3},{4,5},{6,7},{8,9},{10,11},{12,13},{14,15},{16,17},{18,... | collective-permute-start | bytes 737288 | tf_op jit(solution)/shard_map/ppermute | solution.py:370
  21.6 3.2 %collective-permute-start.4 = (bf16[448,128]{1,0:T(8,128)(2,1)S(1)}, bf16[448,128]{1,0:T(8,128)(2,1)S(1)}, u32[]{:S(2)}, u32[]{:S(2)}) collective-permute-start(bf16[448,128]{1,0:T(8,128)(2,1)S(1)} %get-tuple-element.82), channel_id=1, source_target_pairs={{1,0},{3,2},{5,4},{7,6},{9,8},{11,10},{13,12},{15,14},{17,16},{19,... | collective-permute-start | bytes 344072 | tf_op jit(solution)/shard_map/ppermute | solution.py:370
  25.0 8.1 %collective-permute-start.7 = (bf16[480,128]{1,0:T(8,128)(2,1)S(1)}, bf16[480,128]{1,0:T(8,128)(2,1)S(1)}, u32[]{:S(2)}, u32[]{:S(2)}) collective-permute-start(bf16[480,128]{1,0:T(8,128)(2,1)S(1)} %get-tuple-element.89), channel_id=1, source_target_pairs={{1,3},{3,1},{5,7},{7,5},{9,11},{11,9},{13,15},{15,13},{17,19},{19,... | collective-permute-start | bytes 368648 | tf_op jit(solution)/shard_map/ppermute | solution.py:363
  25.7 7.4 %collective-permute-start.6 = (bf16[224,128]{1,0:T(8,128)(2,1)S(1)}, bf16[224,128]{1,0:T(8,128)(2,1)S(1)}, u32[]{:S(2)}, u32[]{:S(2)}) collective-permute-start(bf16[224,128]{1,0:T(8,128)(2,1)S(1)} %get-tuple-element.88), channel_id=1, source_target_pairs={{0,2},{2,0},{4,6},{6,4},{8,10},{10,8},{12,14},{14,12},{16,18},{18,... | collective-permute-start | bytes 172040 | tf_op jit(solution)/shard_map/ppermute | solution.py:363
  29.1 11.2 %collective-permute-start.10 = (bf16[8,64,128]{2,1,0:T(8,128)(2,1)S(1)}, bf16[8,64,128]{2,1,0:T(8,128)(2,1)S(1)}, u32[]{:S(2)}, u32[]{:S(2)}) collective-permute-start(bf16[8,64,128]{2,1,0:T(8,128)(2,1)S(1)} %get-tuple-element.95.near), channel_id=1, source_target_pairs={{0,4},{8,12},{16,20},{24,28},{4,0},{12,8},{20,16},{28,24},{1,5},{9... | collective-permute-start | bytes 393224 | tf_op jit(solution)/shard_map/ppermute | solution.py:354
  29.5 10.8 %collective-permute-start.11 = (bf16[8,64,128]{2,1,0:T(8,128)(2,1)S(1)}, bf16[8,64,128]{2,1,0:T(8,128)(2,1)S(1)}, u32[]{:S(2)}, u32[]{:S(2)}) collective-permute-start(bf16[8,64,128]{2,1,0:T(8,128)(2,1)S(1)} %get-tuple-element.96.far), channel_id=1, source_target_pairs={{4,8},{12,16},{20,24},{28,0},{8,4},{16,12},{24,20},{0,28},{5,9},{1... | collective-permute-start | bytes 393224 | tf_op jit(solution)/shard_map/ppermute | solution.py:354
  33.1 6.4 %collective-permute-start.9 = (bf16[240,128]{1,0:T(8,128)(2,1)S(1)}, bf16[240,128]{1,0:T(8,128)(2,1)S(1)}, u32[]{:S(2)}, u32[]{:S(2)}) collective-permute-start(bf16[240,128]{1,0:T(8,128)(2,1)S(1)} %get-tuple-element.93), channel_id=1, source_target_pairs={{1,9},{3,11},{5,13},{7,15},{9,1},{11,3},{13,5},{15,7},{17,25},{19,... | collective-permute-start | bytes 184328 | tf_op jit(solution)/shard_map/ppermute | solution.py:363
  33.8 5.8 %collective-permute-start.8 = (bf16[112,128]{1,0:T(8,128)(2,1)S(1)}, bf16[112,128]{1,0:T(8,128)(2,1)S(1)}, u32[]{:S(2)}, u32[]{:S(2)}) collective-permute-start(bf16[112,128]{1,0:T(8,128)(2,1)S(1)} %get-tuple-element.92), channel_id=1, source_target_pairs={{0,8},{2,10},{4,12},{6,14},{8,0},{10,2},{12,4},{14,6},{16,24},{18,... | collective-permute-start | bytes 86024 | tf_op jit(solution)/shard_map/ppermute | solution.py:363
  39.6 6.5 %collective-permute-start.13 = (bf16[240,128]{1,0:T(8,128)(2,1)S(1)}, bf16[240,128]{1,0:T(8,128)(2,1)S(1)}, u32[]{:S(2)}, u32[]{:S(2)}) collective-permute-start(bf16[240,128]{1,0:T(8,128)(2,1)S(1)} %get-tuple-element.98.mine1), channel_id=1, source_target_pairs={{1,5},{3,7},{5,1},{7,3},{9,13},{11,15},{13,9},{15,11},{17,21},{19,... | collective-permute-start | bytes 184328 | tf_op jit(solution)/shard_map/ppermute | solution.py:363
  40.3 5.8 %collective-permute-start.12 = (bf16[112,128]{1,0:T(8,128)(2,1)S(1)}, bf16[112,128]{1,0:T(8,128)(2,1)S(1)}, u32[]{:S(2)}, u32[]{:S(2)}) collective-permute-start(bf16[112,128]{1,0:T(8,128)(2,1)S(1)} %get-tuple-element.97.mine0), channel_id=1, source_target_pairs={{0,4},{2,6},{4,0},{6,2},{8,12},{10,14},{12,8},{14,10},{16,20},{18,... | collective-permute-start | bytes 86024 | tf_op jit(solution)/shard_map/ppermute | solution.py:363
  46.1 8.2 %collective-permute-start.15 = (bf16[240,128]{1,0:T(8,128)(2,1)S(1)}, bf16[240,128]{1,0:T(8,128)(2,1)S(1)}, u32[]{:S(2)}, u32[]{:S(2)}) collective-permute-start(bf16[240,128]{1,0:T(8,128)(2,1)S(1)} %get-tuple-element.100.mine1), channel_id=1, source_target_pairs={{1,17},{3,19},{5,21},{7,23},{9,25},{11,27},{13,29},{15,31},{17,1},... | collective-permute-start | bytes 184328 | tf_op jit(solution)/shard_map/ppermute | solution.py:363
  46.8 9.6 %collective-permute-start.16 = (bf16[4,64,128]{2,1,0:T(8,128)(2,1)S(1)}, bf16[4,64,128]{2,1,0:T(8,128)(2,1)S(1)}, u32[]{:S(2)}, u32[]{:S(2)}) collective-permute-start(bf16[4,64,128]{2,1,0:T(8,128)(2,1)S(1)} %get-tuple-element.104), channel_id=1, source_target_pairs={{0,1},{2,3},{1,0},{3,2},{4,5},{6,7},{5,4},{7,6},{8,9},{10,11},{9,8... | collective-permute-start | bytes 196616 | tf_op jit(solution)/shard_map/ppermute | solution.py:354
  46.9 9.5 %collective-permute-start.17 = (bf16[4,64,128]{2,1,0:T(8,128)(2,1)S(1)}, bf16[4,64,128]{2,1,0:T(8,128)(2,1)S(1)}, u32[]{:S(2)}, u32[]{:S(2)}) collective-permute-start(bf16[4,64,128]{2,1,0:T(8,128)(2,1)S(1)} %get-tuple-element.105), channel_id=1, source_target_pairs={{1,2},{3,0},{2,1},{0,3},{5,6},{7,4},{6,5},{4,7},{9,10},{11,8},{10,... | collective-permute-start | bytes 196616 | tf_op jit(solution)/shard_map/ppermute | solution.py:354
  47.5 6.8 %collective-permute-start.14 = (bf16[112,128]{1,0:T(8,128)(2,1)S(1)}, bf16[112,128]{1,0:T(8,128)(2,1)S(1)}, u32[]{:S(2)}, u32[]{:S(2)}) collective-permute-start(bf16[112,128]{1,0:T(8,128)(2,1)S(1)} %get-tuple-element.99.mine0), channel_id=1, source_target_pairs={{0,16},{2,18},{4,20},{6,22},{8,24},{10,26},{12,28},{14,30},{16,0},... | collective-permute-start | bytes 86024 | tf_op jit(solution)/shard_map/ppermute | solution.py:363
  54.3 7.8 %collective-permute-start.19 = (bf16[240,128]{1,0:T(8,128)(2,1)S(1)}, bf16[240,128]{1,0:T(8,128)(2,1)S(1)}, u32[]{:S(2)}, u32[]{:S(2)}) collective-permute-start(bf16[240,128]{1,0:T(8,128)(2,1)S(1)} %get-tuple-element.109.mine1), channel_id=1, source_target_pairs={{1,9},{3,11},{5,13},{7,15},{9,1},{11,3},{13,5},{15,7},{17,25},{19,... | collective-permute-start | bytes 184328 | tf_op jit(solution)/shard_map/ppermute | solution.py:363
  56.4 5.8 %collective-permute-start.18 = (bf16[112,128]{1,0:T(8,128)(2,1)S(1)}, bf16[112,128]{1,0:T(8,128)(2,1)S(1)}, u32[]{:S(2)}, u32[]{:S(2)}) collective-permute-start(bf16[112,128]{1,0:T(8,128)(2,1)S(1)} %get-tuple-element.108.mine0), channel_id=1, source_target_pairs={{0,8},{2,10},{4,12},{6,14},{8,0},{10,2},{12,4},{14,6},{16,24},{18,... | collective-permute-start | bytes 86024 | tf_op jit(solution)/shard_map/ppermute | solution.py:363
  62.2 9.6 %collective-permute-start.21 = (bf16[480,128]{1,0:T(8,128)(2,1)S(1)}, bf16[480,128]{1,0:T(8,128)(2,1)S(1)}, u32[]{:S(2)}, u32[]{:S(2)}) collective-permute-start(bf16[480,128]{1,0:T(8,128)(2,1)S(1)} %get-tuple-element.112.mine1), channel_id=1, source_target_pairs={{1,3},{3,1},{5,7},{7,5},{9,11},{11,9},{13,15},{15,13},{17,19},{19,... | collective-permute-start | bytes 368648 | tf_op jit(solution)/shard_map/ppermute | solution.py:363
  65.7 6.1 %collective-permute-start.20 = (bf16[224,128]{1,0:T(8,128)(2,1)S(1)}, bf16[224,128]{1,0:T(8,128)(2,1)S(1)}, u32[]{:S(2)}, u32[]{:S(2)}) collective-permute-start(bf16[224,128]{1,0:T(8,128)(2,1)S(1)} %get-tuple-element.111.mine0), channel_id=1, source_target_pairs={{0,2},{2,0},{4,6},{6,4},{8,10},{10,8},{12,14},{14,12},{16,18},{18,... | collective-permute-start | bytes 172040 | tf_op jit(solution)/shard_map/ppermute | solution.py:363
  71.8 5.7 %collective-permute-start.23 = (bf16[960,128]{1,0:T(8,128)(2,1)S(1)}, bf16[960,128]{1,0:T(8,128)(2,1)S(1)}, u32[]{:S(2)}, u32[]{:S(2)}) collective-permute-start(bf16[960,128]{1,0:T(8,128)(2,1)S(1)} %get-tuple-element.118.mine1), channel_id=1, source_target_pairs={{1,0},{3,2},{5,4},{7,6},{9,8},{11,10},{13,12},{15,14},{17,16},{19,... | collective-permute-start | bytes 737288 | tf_op jit(solution)/shard_map/ppermute | solution.py:370
  73.1 4.4 %collective-permute-start.22 = (bf16[448,128]{1,0:T(8,128)(2,1)S(1)}, bf16[448,128]{1,0:T(8,128)(2,1)S(1)}, u32[]{:S(2)}, u32[]{:S(2)}) collective-permute-start(bf16[448,128]{1,0:T(8,128)(2,1)S(1)} %get-tuple-element.113.mine0), channel_id=1, source_target_pairs={{0,1},{2,3},{4,5},{6,7},{8,9},{10,11},{12,13},{14,15},{16,17},{18,... | collective-permute-start | bytes 344072 | tf_op jit(solution)/shard_map/ppermute | solution.py:370

commit v9 on v5

--- a/solution.py
+++ b/solution.py
@@ -195,7 +195,32 @@
     gate(rows - 1, sides[1])
 
 
-def weight_grad_kernel(inner, outer, edges, near, far, h_ref, d_ref, cot_ref, out_ref, keep, send, packed):
+def coarse_hidden(h_ref, a, b):
+    rows, channels, breadth = h_ref.shape[1:]
+    source = lax.broadcasted_iota(jnp.int32, (2 * breadth, 2 * breadth), 0)
+    target = lax.broadcasted_iota(jnp.int32, (2 * breadth, 2 * breadth), 1)
+    wanted = 2 * (target % breadth) + target // breadth
+    pick = jnp.where(source == wanted, 1.0, 0.0).astype(BF16)
+    pairs = []
+    for pair in range(rows // 4):
+        both = jnp.concatenate([h_ref[a, 4 * pair + b], h_ref[a, 4 * pair + 2 + b]], axis=1)
+        pairs.append(dot(both, pick).astype(BF16))
+    return jnp.concatenate(
+        [jnp.concatenate([x[:, e * breadth : (e + 1) * breadth] for x in pairs], axis=1) for e in range(2)],
+        axis=0,
+    )
+
+
+def section_kernel(h_ref, d_ref, out_ref):
+    coarse = None
+    for a in range(2):
+        for b in range(2):
+            term = dot(d_ref[a, b], coarse_hidden(h_ref, a, b))
+            coarse = term if coarse is None else coarse + term
+    out_ref[...] = coarse.astype(BF16)
+
+
+def weight_grad_kernel(inner, outer, edges, near, far, h_ref, cot_ref, keep, send, packed):
     rows, channels, breadth = near.shape
     across = (((1,), (1,)), ((), ()))
     even = is_even("gz")
@@ -225,28 +250,13 @@
             mix = jnp.where(lane < channels, rest[0 : channels // 2], rest[channels // 2 :])
             packed[base + channels : base + 3 * channels // 2] = mix
     base = 9 * 3 * channels // 2
-    source = lax.broadcasted_iota(jnp.int32, (2 * breadth, 2 * breadth), 0)
-    target = lax.broadcasted_iota(jnp.int32, (2 * breadth, 2 * breadth), 1)
-    wanted = 2 * (target % breadth) + target // breadth
-    pick = jnp.where(source == wanted, 1.0, 0.0).astype(BF16)
-    coarse = None
+    height = cot_ref.shape[0]
     for a in range(2):
         for b in range(2):
-            pairs = []
-            for pair in range(rows // 4):
-                both = jnp.concatenate([h_ref[a, 4 * pair + b], h_ref[a, 4 * pair + 2 + b]], axis=1)
-                pairs.append(jnp.dot(both, pick, preferred_element_type=F32).astype(BF16))
-            hidden = jnp.concatenate(
-                [jnp.concatenate([x[:, e * breadth : (e + 1) * breadth] for x in pairs], axis=1) for e in range(2)],
-                axis=0,
-            )
-            term = jnp.dot(d_ref[a, b], hidden, preferred_element_type=F32)
-            coarse = term if coarse is None else coarse + term
-            down = lax.dot_general(cot_ref[...], hidden, across, preferred_element_type=F32)
-            at = base + (2 * a + b) * d_ref.shape[2]
-            packed[at : at + d_ref.shape[2]] = down
-    out_ref[...] = coarse.astype(BF16)
-    end = base + 4 * d_ref.shape[2]
+            down = lax.dot_general(cot_ref[...], coarse_hidden(h_ref, a, b), across, preferred_element_type=F32)
+            at = base + (2 * a + b) * height
+            packed[at : at + height] = down
+    end = base + 4 * height
     if end < packed.shape[0]:
         packed[end:] = jnp.zeros((packed.shape[0] - end, packed.shape[1]), F32)
     half = packed.shape[0] // 2
@@ -388,16 +398,14 @@
 
     used = 27 * channels * channels // 128 + 4 * out_channels
     rows = -(-used // 128) * 128
-    section_out, keep, send = call(
-        weight_grad_kernel,
-        [((out_channels, cot.shape[1]), BF16), ((rows // 2, 128), F32), ((rows // 2, 128), BF16)],
-        [((rows, 128), F32)], conv_flops,
-        (inner, outer, edges, *gates, hidden, down_weight, cot),
+    keep, send = call(
+        weight_grad_kernel, [((rows // 2, 128), F32), ((rows // 2, 128), BF16)], [((rows, 128), F32)],
+        conv_flops, (inner, outer, edges, *gates, hidden, cot),
     )
     keep, gates = tied(keep, *gates)
     near, far = gates
     near_in = swap(near, "gz", 0)
-    for level, (axis, bit) in enumerate((("gy", 2), ("gz", 1))):
+    for level, (axis, bit) in enumerate((("gy", 2), ("gz", 2))):
         size = rows >> (level + 2)
         mine, got = keep, flip(send, *(("gy", 1), ("gy", 2))[level])
         keep, send = call(
@@ -405,10 +413,15 @@
             [((size, 128), F32), ((size, 128), BF16)], [((2 * size, 128), F32)], 0, (mine, got),
         )
         if level == 0:
-            keep, (far,) = tied(keep, far)
+            keep, (far, hidden) = tied(keep, far, hidden)
             far_in = swap(far, "gz", 1)
+            (section_out,) = call(
+                section_kernel, [((out_channels, cot.shape[1]), BF16)], [], conv_flops // 10,
+                (hidden, down_weight),
+            )
     shard = ((rows // 8, 128), BF16)
-    (sums,) = call(add_kernel, [shard], [], 0, (keep, flip(send, "gz", 1)))
+    (sums,) = call(add_kernel, [shard], [], 0, (keep, flip(send, "gz", 2)))
+    (sums,) = call(add_kernel, [shard], [], 0, (sums, flip(sums, "gz", 1)))
     sums, outside = tied(sums, near_in, far_in)
     sends = call(edges_kernel, [edge, edge], [], 0, (*gates, *outside))
     beside = swapped(*sends, "gy")
@@ -416,15 +429,15 @@
         field_kernel, [(lines, F32)], [cols, cols], conv_flops, (*gates, *outside, weight_bwd)
     )
     wide = [("gy", 1 << k) for k in range(2, lax.axis_size("gy").bit_length() - 1)]
-    wide += [("gz", 1 << k) for k in range(1, lax.axis_size("gz").bit_length() - 1)]
+    wide += [("gz", 1 << k) for k in range(2, lax.axis_size("gz").bit_length() - 1)]
     for axis, bit in wide:
         (sums,) = call(add_kernel, [shard], [], 0, (sums, flip(sums, axis, bit)))
-    sums, beside = tied(sums, *beside)
+    sums, (section_out,) = tied(sums, section_out)
     (sums,) = call(
-        functools.partial(join_kernel, axis="gz", bit=1), [((rows // 4, 128), BF16)], [], 0,
-        (sums, flip(sums, "gz", 1)),
-    )
-    sums, (acc,) = tied(sums, acc)
+        functools.partial(join_kernel, axis="gz", bit=2), [((rows // 4, 128), BF16)], [], 0,
+        (sums, flip(sums, "gz", 2)),
+    )
+    sums, (acc, *beside) = tied(sums, acc, *beside)
     (field,) = call(
         field_edges_kernel, [((channels * plane_count * row_count, breadth), F32)], [edge_cols],
         conv_flops // 10, (*beside, acc, weight_bwd),

time: 53.3 us -> 52 us (0.976)
  waiting for transfers between devices: 20.1 us -> 13.4 us
  starting transfers between devices: 17.7 us -> 22.3 us
  Pallas kernels: 11.8 us -> 12.6 us
    ppermute x8, waiting for transfers between devices: 18 us -> 11.3 us  [flip(): lax.ppermute(cells, axis, [(i, i ^ bit) for i in range(lax.axis_size(axis...]
    ppermute x8, starting transfers between devices: 4.81 us -> 9.41 us  [flip(): lax.ppermute(cells, axis, [(i, i ^ bit) for i in range(lax.axis_size(axis...]
    pallas_call x17 -> x18, Pallas kernels: 11.8 us -> 12.6 us  [call(): pl.pallas_call(kernel, out_shape=[jax.ShapeDtypeStruct(s, d) for s, d in...]
  transfers between devices with their start and end apart: 16 -> 16, of which waited for: 9 -> 8; matrix products, arithmetic and copies ran while one was open for 1% -> 2% of each run, Pallas kernels for 13% -> 16%
where the time goes in v9:
time: 52 us; the launch traced here: 51.8 us
  starting transfers between devices  22.3 us (43%)
  waiting for transfers between devices  13.4 us (26%)
  Pallas kernels  12.6 us (24%)
  local copies, waits for them, and re-layouts  2.7 us (5%)
  between operations  0.84 us (2%)
    ppermute x8, starting transfers between devices, swap(): return lax.ppermute(cells, axis, pairs + [(b, a) for a, b in pairs])  12.9 us
    pallas_call x18, Pallas kernels, call(): pl.pallas_call(kernel, out_shape=[jax.ShapeDtypeStruct(s, d) for s, d in...  12.6 us
    ppermute x8, waiting for transfers between devices, flip(): lax.ppermute(cells, axis, [(i, i ^ bit) for i in range(lax.axis_size(axis...  11.3 us
    ppermute x8, starting transfers between devices, flip(): lax.ppermute(cells, axis, [(i, i ^ bit) for i in range(lax.axis_size(axis...  9.41 us
    unnamed x11, local copies, waits for them, and re-layouts  2.18 us
    ppermute x8, waiting for transfers between devices, swap(): return lax.ppermute(cells, axis, pairs + [(b, a) for a, b in pairs])  2.13 us
  transfers between devices with their start and end apart: 16, of which 8 were waited for; matrix products, arithmetic and copies ran while one was open for 2% of the time, Pallas kernels for 16%

profile of v9, /device:TPU:0, one launch (start us, length us, event | category | flops | bytes accessed | tf_op | source)
XLA Modules:
  0.0 51.8 jit_solution(17050641490582569315)
XLA Ops:
  0.6 0.9 %copy-done.2 = bf16[64,2,8,128]{3,2,1,0:T(8,128)(2,1)S(1)} copy-done((bf16[64,2,8,128]{3,2,1,0:T(8,128)(2,1)S(1)}, bf16[64,2,8,128]{3,2,1,0:T(8,128)(2,1)}, u32[]{:S(2)}) %copy-start.2) | copy-done | bytes 262168
  1.6 0.2 shard_map.75
  1.8 3.0 %collective-permute-start = (bf16[8,64,128]{2,1,0:T(8,128)(2,1)S(1)}, bf16[8,64,128]{2,1,0:T(8,128)(2,1)S(1)}, u32[]{:S(2)}, u32[]{:S(2)}) collective-permute-start(bf16[8,64,128]{2,1,0:T(8,128)(2,1)S(1)} %get-tuple-element.47.near), channel_id=1, source_target_pairs={{0,4},{8,12},{16,20},{24,28},{4,0},{12,8},{20,16},{28,24},{1,5},{9... | collective-permute-start | bytes 393224 | tf_op jit(solution)/shard_map/ppermute | solution.py:347
  4.8 3.5 %collective-permute-start.1 = (bf16[8,64,128]{2,1,0:T(8,128)(2,1)S(1)}, bf16[8,64,128]{2,1,0:T(8,128)(2,1)S(1)}, u32[]{:S(2)}, u32[]{:S(2)}) collective-permute-start(bf16[8,64,128]{2,1,0:T(8,128)(2,1)S(1)} %get-tuple-element.48.far), channel_id=1, source_target_pairs={{4,8},{12,16},{20,24},{28,0},{8,4},{16,12},{24,20},{0,28},{5,9},{1... | collective-permute-start | bytes 393224 | tf_op jit(solution)/shard_map/ppermute | solution.py:347
  8.4 1.0 %copy-done = bf16[3,3,64,192]{3,2,1,0:T(8,128)(2,1)S(1)} copy-done((bf16[3,3,64,192]{3,2,1,0:T(8,128)(2,1)S(1)}, bf16[3,3,64,192]{3,2,1,0:T(8,128)(2,1)}, u32[]{:S(2)}) %copy-start) | copy-done | bytes 221208
  9.3 1.9 %shard_map.76 = (bf16[2,10,192,128]{3,2,1,0:T(8,128)(2,1)S(1)}, f32[2,8,64,128]{3,2,1,0:T(8,128)S(1)}, f32[2,8,64,128]{3,2,1,0:T(8,128)S(1)}) custom-call(bf16[8,64,128]{2,1,0:T(8,128)(2,1)S(1)} %get-tuple-element.47.near, bf16[8,64,128]{2,1,0:T(8,128)(2,1)S(1)} %get-tuple-element.48.far, bf16[3,3,64,192]{3,2,1,0:T(8,128)(2,1)S(1)} %copy-done, ...), custom_call_target="tpu_custom_call" | custom-call | flops 301989888 | bytes 2711552 | tf_op jit(solution)/shard_map/pallas_call | solution.py:20
  11.3 0.0 copy-start.1
  11.3 0.0 collective-permute-done.near.near_in
  11.3 1.2 %collective-permute-done.1.far.far_in = bf16[8,64,128]{2,1,0:T(8,128)(2,1)S(1)} collective-permute-done((bf16[8,64,128]{2,1,0:T(8,128)(2,1)S(1)}, bf16[8,64,128]{2,1,0:T(8,128)(2,1)S(1)}, u32[]{:S(2)}, u32[]{:S(2)}) %collective-permute-start.1) | collective-permute-done | bytes 131104 | tf_op jit(solution)/shard_map/ppermute | solution.py:347
  12.5 0.1 collective-permute-start.2
  12.6 1.6 %collective-permute-start.3 = (bf16[4,64,128]{2,1,0:T(8,128)(2,1)S(1)}, bf16[4,64,128]{2,1,0:T(8,128)(2,1)S(1)}, u32[]{:S(2)}, u32[]{:S(2)}) collective-permute-start(bf16[4,64,128]{2,1,0:T(8,128)(2,1)S(1)} %get-tuple-element.56), channel_id=1, source_target_pairs={{1,2},{3,0},{2,1},{0,3},{5,6},{7,4},{6,5},{4,7},{9,10},{11,8},{10,... | collective-permute-start | bytes 196616 | tf_op jit(solution)/shard_map/ppermute | solution.py:347
  14.2 1.4 %shard_map.77 = (bf16[2,10,192,128]{3,2,1,0:T(8,128)(2,1)S(1)}, f32[2,8,64,128]{3,2,1,0:T(8,128)S(1)}) custom-call(bf16[8,64,128]{2,1,0:T(8,128)(2,1)S(1)} %collective-permute-done.near.near_in, bf16[8,64,128]{2,1,0:T(8,128)(2,1)S(1)} %collective-permute-done.1.far.far_in, bf16[3,3,64,192]{3,2,1,0:T(8,128)(2,1)S(1)} %copy-done.1, ...), custom_call_target="tpu_custom_call" | custom-call | flops 150994944 | bytes 2514944 | tf_op jit(solution)/shard_map/pallas_call | solution.py:20
  15.6 0.0 collective-permute-done.2.near
  15.6 0.9 %collective-permute-done.3.far = bf16[4,64,128]{2,1,0:T(8,128)(2,1)S(1)} collective-permute-done((bf16[4,64,128]{2,1,0:T(8,128)(2,1)S(1)}, bf16[4,64,128]{2,1,0:T(8,128)(2,1)S(1)}, u32[]{:S(2)}, u32[]{:S(2)}) %collective-permute-start.3) | collective-permute-done | bytes 65568 | tf_op jit(solution)/shard_map/ppermute | solution.py:347
  16.5 0.5 %shard_map.79 = (bf16[4,2,192,128]{3,2,1,0:T(8,128)(2,1)S(1)}, bf16[8,64,128]{2,1,0:T(8,128)(2,1)S(1)}, bf16[8,64,128]{2,1,0:T(8,128)(2,1)S(1)}, bf16[2,8,64,128]{3,2,1,0:T(8,128)(2,1)S(1)}) custom-call(bf16[4,64,128]{2,1,0:T(8,128)(2,1)S(1)} %collective-permute-done.2.near, bf16[4,64,128]{2,1,0:T(8,128)(2,1)S(1)} %collective-permute-done.3.far, ...), custom_call_target="tpu_custom_call" | custom-call | flops 45298484 | bytes 2318336 | tf_op jit(solution)/shard_map/pallas_call | solution.py:20
  17.0 2.3 %shard_map.80 = (f32[704,128]{1,0:T(8,128)S(1)}, bf16[704,128]{1,0:T(8,128)(2,1)S(1)}) custom-call(bf16[2,10,192,128]{3,2,1,0:T(8,128)(2,1)S(1)} %get-tuple-element.49.inner, bf16[2,10,192,128]{3,2,1,0:T(8,128)(2,1)S(1)} %get-tuple-element.54.outer, bf16[4,2,192,128]{3,2,1,0:T(8,128)(2,1)S(1)} %get-tuple-element.59.edges, ...), custom_call_target="tpu_custom_call" | custom-call | flops 452984832 | bytes 3489792 | tf_op jit(solution)/shard_map/pallas_call | solution.py:20
  19.4 0.5 collective-permute-start.4
  19.8 1.0 %collective-permute-done.4.other = bf16[704,128]{1,0:T(8,128)(2,1)S(1)} collective-permute-done((bf16[704,128]{1,0:T(8,128)(2,1)S(1)}, bf16[704,128]{1,0:T(8,128)(2,1)S(1)}, u32[]{:S(2)}, u32[]{:S(2)}) %collective-permute-start.4) | collective-permute-done | bytes 180256 | tf_op jit(solution)/shard_map/ppermute | solution.py:351
  20.9 0.1 shard_map.81
  20.9 1.6 %collective-permute-start.5 = (bf16[352,128]{1,0:T(8,128)(2,1)S(1)}, bf16[352,128]{1,0:T(8,128)(2,1)S(1)}, u32[]{:S(2)}, u32[]{:S(2)}) collective-permute-start(bf16[352,128]{1,0:T(8,128)(2,1)S(1)} %get-tuple-element.69), channel_id=1, source_target_pairs={{0,2},{1,3},{2,0},{3,1},{4,6},{5,7},{6,4},{7,5},{8,10},{9,11},{10,... | collective-permute-start | bytes 270344 | tf_op jit(solution)/shard_map/ppermute | solution.py:351
  22.5 0.4 collective-permute-start.8
  22.9 3.5 %collective-permute-start.9 = (bf16[8,64,128]{2,1,0:T(8,128)(2,1)S(1)}, bf16[8,64,128]{2,1,0:T(8,128)(2,1)S(1)}, u32[]{:S(2)}, u32[]{:S(2)}) collective-permute-start(bf16[8,64,128]{2,1,0:T(8,128)(2,1)S(1)} %get-tuple-element.73.far), channel_id=1, source_target_pairs={{4,8},{12,16},{20,24},{28,0},{8,4},{16,12},{24,20},{0,28},{5,9},{1... | collective-permute-start | bytes 393224 | tf_op jit(solution)/shard_map/ppermute | solution.py:347
  26.4 0.0 collective-permute-done.5.other
  26.5 0.1 collective-permute-start.6
  26.6 4.0 %collective-permute-done.6.y = bf16[176,128]{1,0:T(8,128)(2,1)S(1)} collective-permute-done((bf16[176,128]{1,0:T(8,128)(2,1)S(1)}, bf16[176,128]{1,0:T(8,128)(2,1)S(1)}, u32[]{:S(2)}, u32[]{:S(2)}) %collective-permute-start.6) | collective-permute-done | bytes 45088 | tf_op jit(solution)/shard_map/ppermute | solution.py:351
  30.6 1.8 %collective-permute-start.7 = (bf16[176,128]{1,0:T(8,128)(2,1)S(1)}, bf16[176,128]{1,0:T(8,128)(2,1)S(1)}, u32[]{:S(2)}, u32[]{:S(2)}) collective-permute-start(bf16[176,128]{1,0:T(8,128)(2,1)S(1)} %shard_map.83.x), channel_id=1, source_target_pairs={{0,4},{4,0},{8,12},{12,8},{16,20},{20,16},{24,28},{28,24},{1,5},{5... | collective-permute-start | bytes 135176 | tf_op jit(solution)/shard_map/ppermute | solution.py:351
  32.4 2.3 %collective-permute-done.7.y = bf16[176,128]{1,0:T(8,128)(2,1)S(1)} collective-permute-done((bf16[176,128]{1,0:T(8,128)(2,1)S(1)}, bf16[176,128]{1,0:T(8,128)(2,1)S(1)}, u32[]{:S(2)}, u32[]{:S(2)}) %collective-permute-start.7) | collective-permute-done | bytes 45088 | tf_op jit(solution)/shard_map/ppermute | solution.py:351
  34.7 0.0 collective-permute-done.8.near_in
  34.7 0.0 collective-permute-done.9.far_in
  34.8 2.0 %collective-permute-start.10 = (bf16[176,128]{1,0:T(8,128)(2,1)S(1)}, bf16[176,128]{1,0:T(8,128)(2,1)S(1)}, u32[]{:S(2)}, u32[]{:S(2)}) collective-permute-start(bf16[176,128]{1,0:T(8,128)(2,1)S(1)} %shard_map.84.x), channel_id=1, source_target_pairs={{0,16},{4,20},{8,24},{12,28},{16,0},{20,4},{24,8},{28,12},{1,17},{... | collective-permute-start | bytes 135176 | tf_op jit(solution)/shard_map/ppermute | solution.py:351
  36.7 0.3 copy.9
  37.0 1.4 %shard_map.86 = bf16[128,256]{1,0:T(8,128)(2,1)} custom-call(bf16[2,8,64,128]{3,2,1,0:T(8,128)(2,1)S(1)} %get-tuple-element.75.h_ref, bf16[2,2,128,128]{3,2,1,0:T(8,128)(2,1)S(1)} %copy-done.3), custom_call_target="tpu_custom_call" | custom-call | flops 45298484 | bytes 458752 | tf_op jit(solution)/shard_map/pallas_call | solution.py:20
  38.4 0.1 collective-permute-start.12
  38.5 0.7 %collective-permute-start.13 = (bf16[4,64,128]{2,1,0:T(8,128)(2,1)S(1)}, bf16[4,64,128]{2,1,0:T(8,128)(2,1)S(1)}, u32[]{:S(2)}, u32[]{:S(2)}) collective-permute-start(bf16[4,64,128]{2,1,0:T(8,128)(2,1)S(1)} %get-tuple-element.81), channel_id=1, source_target_pairs={{1,2},{3,0},{2,1},{0,3},{5,6},{7,4},{6,5},{4,7},{9,10},{11,8},{10,... | collective-permute-start | bytes 196616 | tf_op jit(solution)/shard_map/ppermute | solution.py:347
  39.2 0.6 %collective-permute-done.10.y = bf16[176,128]{1,0:T(8,128)(2,1)S(1)} collective-permute-done((bf16[176,128]{1,0:T(8,128)(2,1)S(1)}, bf16[176,128]{1,0:T(8,128)(2,1)S(1)}, u32[]{:S(2)}, u32[]{:S(2)}) %collective-permute-start.10) | collective-permute-done | bytes 45088 | tf_op jit(solution)/shard_map/ppermute | solution.py:351
  39.8 2.1 %collective-permute-start.11 = (bf16[176,128]{1,0:T(8,128)(2,1)S(1)}, bf16[176,128]{1,0:T(8,128)(2,1)S(1)}, u32[]{:S(2)}, u32[]{:S(2)}) collective-permute-start(bf16[176,128]{1,0:T(8,128)(2,1)S(1)} %shard_map.85.mine), channel_id=1, source_target_pairs={{0,8},{4,12},{8,0},{12,4},{16,24},{20,28},{24,16},{28,20},{1,9},{5... | collective-permute-start | bytes 135176 | tf_op jit(solution)/shard_map/ppermute | solution.py:351
  41.9 0.3 copy.10
  42.1 0.2 copy.11.w_ref
  42.4 2.3 %shard_map.88.acc_ref = f32[2,8,64,128]{3,2,1,0:T(8,128)S(1)} custom-call(bf16[8,64,128]{2,1,0:T(8,128)(2,1)S(1)} %get-tuple-element.72.near, bf16[8,64,128]{2,1,0:T(8,128)(2,1)S(1)} %get-tuple-element.73.far, bf16[8,64,128]{2,1,0:T(8,128)(2,1)S(1)} %collective-permute-done.8.near_in, bf16[8,64,128]{2,1,0:T(8,128)(2,1)S(1)} %collective-permute-done.9.far_in, ...), custom_call_target="tpu_custom_call" | custom-call | flops 452984832 | bytes 1269760 | tf_op jit(solution)/shard_map/pallas_call | solution.py:20
  44.7 0.0 collective-permute-done.11.other
  44.7 0.0 collective-permute-done.12.near
  44.7 0.0 collective-permute-done.13.far
  44.7 1.4 %collective-permute-start.14 = (bf16[352,128]{1,0:T(8,128)(2,1)S(1)}, bf16[352,128]{1,0:T(8,128)(2,1)S(1)}, u32[]{:S(2)}, u32[]{:S(2)}) collective-permute-start(bf16[352,128]{1,0:T(8,128)(2,1)S(1)} %shard_map.87.mine), channel_id=1, source_target_pairs={{0,2},{1,3},{2,0},{3,1},{4,6},{5,7},{6,4},{7,5},{8,10},{9,11},{10,... | collective-permute-start | bytes 270344 | tf_op jit(solution)/shard_map/ppermute | solution.py:351
  46.1 1.3 %shard_map.91 = f32[1024,128]{1,0:T(8,128)} custom-call(bf16[4,64,128]{2,1,0:T(8,128)(2,1)S(1)} %collective-permute-done.12.near, bf16[4,64,128]{2,1,0:T(8,128)(2,1)S(1)} %collective-permute-done.13.far, f32[2,8,64,128]{3,2,1,0:T(8,128)S(1)} %shard_map.88.acc_ref, bf16[3,3,64,192]{3,2,1,0:T(8,128)(2,1)S(1)} %copy.11.w_ref), custom_call_target="tpu_custom_call" | custom-call | flops 45298484 | bytes 1400832 | tf_op jit(solution)/shard_map/pallas_call | solution.py:20
  47.5 1.9 %collective-permute-done.14.other = bf16[352,128]{1,0:T(8,128)(2,1)S(1)} collective-permute-done((bf16[352,128]{1,0:T(8,128)(2,1)S(1)}, bf16[352,128]{1,0:T(8,128)(2,1)S(1)}, u32[]{:S(2)}, u32[]{:S(2)}) %collective-permute-start.14) | collective-permute-done | bytes 90144 | tf_op jit(solution)/shard_map/ppermute | solution.py:351
  49.4 0.1 collective-permute-start.15
  49.4 1.4 %collective-permute-done.15.other = bf16[704,128]{1,0:T(8,128)(2,1)S(1)} collective-permute-done((bf16[704,128]{1,0:T(8,128)(2,1)S(1)}, bf16[704,128]{1,0:T(8,128)(2,1)S(1)}, u32[]{:S(2)}, u32[]{:S(2)}) %collective-permute-start.15) | collective-permute-done | bytes 180256 | tf_op jit(solution)/shard_map/ppermute | solution.py:351
  50.9 1.0 %shard_map.92 = (f32[3,3,64,192]{3,2,1,0:T(8,128)}, f32[2,2,128,128]{3,2,1,0:T(8,128)}) custom-call(bf16[704,128]{1,0:T(8,128)(2,1)S(1)} %shard_map.90.mine, bf16[704,128]{1,0:T(8,128)(2,1)S(1)} %collective-permute-done.15.other), custom_call_target="tpu_custom_call" | custom-call | bytes 1064960 | tf_op jit(solution)/shard_map/pallas_call | solution.py:20
  (16 shorter events, 0.2 us)
Async XLA Ops:
  0.6 1.0 %copy-start.2 = (bf16[64,2,8,128]{3,2,1,0:T(8,128)(2,1)S(1)}, bf16[64,2,8,128]{3,2,1,0:T(8,128)(2,1)}, u32[]{:S(2)}) copy-start(bf16[64,2,8,128]{3,2,1,0:T(8,128)(2,1)} %f_ref.1) | copy-start | bytes 786436
  1.6 6.8 %copy-start.3 = (bf16[2,2,128,128]{3,2,1,0:T(8,128)(2,1)S(1)}, bf16[2,2,128,128]{3,2,1,0:T(8,128)(2,1)}, u32[]{:S(2)}) copy-start(bf16[2,2,128,128]{3,2,1,0:T(8,128)(2,1)} %d_ref.3) | copy-start | bytes 393220
  1.6 6.8 %copy-start.4 = (bf16[128,1,256]{2,0,1:T(8,128)(2,1)S(1)}, bf16[128,1,256]{2,0,1:T(8,128)(2,1)}, u32[]{:S(2)}) copy-start(bf16[128,1,256]{2,0,1:T(8,128)(2,1)} %param.7) | copy-start | bytes 196612
  1.8 9.5 %collective-permute-start = (bf16[8,64,128]{2,1,0:T(8,128)(2,1)S(1)}, bf16[8,64,128]{2,1,0:T(8,128)(2,1)S(1)}, u32[]{:S(2)}, u32[]{:S(2)}) collective-permute-start(bf16[8,64,128]{2,1,0:T(8,128)(2,1)S(1)} %get-tuple-element.47.near), channel_id=1, source_target_pairs={{0,4},{8,12},{16,20},{24,28},{4,0},{12,8},{20,16},{28,24},{1,5},{9... | collective-permute-start | bytes 393224 | tf_op jit(solution)/shard_map/ppermute | solution.py:347
  4.8 7.7 %collective-permute-start.1 = (bf16[8,64,128]{2,1,0:T(8,128)(2,1)S(1)}, bf16[8,64,128]{2,1,0:T(8,128)(2,1)S(1)}, u32[]{:S(2)}, u32[]{:S(2)}) collective-permute-start(bf16[8,64,128]{2,1,0:T(8,128)(2,1)S(1)} %get-tuple-element.48.far), channel_id=1, source_target_pairs={{4,8},{12,16},{20,24},{28,0},{8,4},{16,12},{24,20},{0,28},{5,9},{1... | collective-permute-start | bytes 393224 | tf_op jit(solution)/shard_map/ppermute | solution.py:347
  8.4 1.0 %copy-start = (bf16[3,3,64,192]{3,2,1,0:T(8,128)(2,1)S(1)}, bf16[3,3,64,192]{3,2,1,0:T(8,128)(2,1)}, u32[]{:S(2)}) copy-start(bf16[3,3,64,192]{3,2,1,0:T(8,128)(2,1)} %w_ref.5) | copy-start | bytes 663556
  11.3 3.0 %copy-start.1 = (bf16[3,3,64,192]{3,2,1,0:T(8,128)(2,1)S(1)}, bf16[3,3,64,192]{3,2,1,0:T(8,128)(2,1)}, u32[]{:S(2)}) copy-start(bf16[3,3,64,192]{3,2,1,0:T(8,128)(2,1)} %w_ref.5) | copy-start | bytes 663556
  12.5 3.1 %collective-permute-start.2 = (bf16[4,64,128]{2,1,0:T(8,128)(2,1)S(1)}, bf16[4,64,128]{2,1,0:T(8,128)(2,1)S(1)}, u32[]{:S(2)}, u32[]{:S(2)}) collective-permute-start(bf16[4,64,128]{2,1,0:T(8,128)(2,1)S(1)} %get-tuple-element.55), channel_id=1, source_target_pairs={{0,1},{2,3},{1,0},{3,2},{4,5},{6,7},{5,4},{7,6},{8,9},{10,11},{9,8... | collective-permute-start | bytes 196616 | tf_op jit(solution)/shard_map/ppermute | solution.py:347
  12.6 3.9 %collective-permute-start.3 = (bf16[4,64,128]{2,1,0:T(8,128)(2,1)S(1)}, bf16[4,64,128]{2,1,0:T(8,128)(2,1)S(1)}, u32[]{:S(2)}, u32[]{:S(2)}) collective-permute-start(bf16[4,64,128]{2,1,0:T(8,128)(2,1)S(1)} %get-tuple-element.56), channel_id=1, source_target_pairs={{1,2},{3,0},{2,1},{0,3},{5,6},{7,4},{6,5},{4,7},{9,10},{11,8},{10,... | collective-permute-start | bytes 196616 | tf_op jit(solution)/shard_map/ppermute | solution.py:347
  19.4 1.5 %collective-permute-start.4 = (bf16[704,128]{1,0:T(8,128)(2,1)S(1)}, bf16[704,128]{1,0:T(8,128)(2,1)S(1)}, u32[]{:S(2)}, u32[]{:S(2)}) collective-permute-start(bf16[704,128]{1,0:T(8,128)(2,1)S(1)} %get-tuple-element.65), channel_id=1, source_target_pairs={{0,1},{1,0},{2,3},{3,2},{4,5},{5,4},{6,7},{7,6},{8,9},{9,8},{10,11... | collective-permute-start | bytes 540680 | tf_op jit(solution)/shard_map/ppermute | solution.py:351
  20.9 5.5 %collective-permute-start.5 = (bf16[352,128]{1,0:T(8,128)(2,1)S(1)}, bf16[352,128]{1,0:T(8,128)(2,1)S(1)}, u32[]{:S(2)}, u32[]{:S(2)}) collective-permute-start(bf16[352,128]{1,0:T(8,128)(2,1)S(1)} %get-tuple-element.69), channel_id=1, source_target_pairs={{0,2},{1,3},{2,0},{3,1},{4,6},{5,7},{6,4},{7,5},{8,10},{9,11},{10,... | collective-permute-start | bytes 270344 | tf_op jit(solution)/shard_map/ppermute | solution.py:351
  22.5 12.2 %collective-permute-start.8 = (bf16[8,64,128]{2,1,0:T(8,128)(2,1)S(1)}, bf16[8,64,128]{2,1,0:T(8,128)(2,1)S(1)}, u32[]{:S(2)}, u32[]{:S(2)}) collective-permute-start(bf16[8,64,128]{2,1,0:T(8,128)(2,1)S(1)} %get-tuple-element.72.near), channel_id=1, source_target_pairs={{0,4},{8,12},{16,20},{24,28},{4,0},{12,8},{20,16},{28,24},{1,5},{9... | collective-permute-start | bytes 393224 | tf_op jit(solution)/shard_map/ppermute | solution.py:347
  22.9 11.8 %collective-permute-start.9 = (bf16[8,64,128]{2,1,0:T(8,128)(2,1)S(1)}, bf16[8,64,128]{2,1,0:T(8,128)(2,1)S(1)}, u32[]{:S(2)}, u32[]{:S(2)}) collective-permute-start(bf16[8,64,128]{2,1,0:T(8,128)(2,1)S(1)} %get-tuple-element.73.far), channel_id=1, source_target_pairs={{4,8},{12,16},{20,24},{28,0},{8,4},{16,12},{24,20},{0,28},{5,9},{1... | collective-permute-start | bytes 393224 | tf_op jit(solution)/shard_map/ppermute | solution.py:347
  26.5 4.1 %collective-permute-start.6 = (bf16[176,128]{1,0:T(8,128)(2,1)S(1)}, bf16[176,128]{1,0:T(8,128)(2,1)S(1)}, u32[]{:S(2)}, u32[]{:S(2)}) collective-permute-start(bf16[176,128]{1,0:T(8,128)(2,1)S(1)} %get-tuple-element.71), channel_id=1, source_target_pairs={{0,8},{4,12},{8,0},{12,4},{16,24},{20,28},{24,16},{28,20},{1,9},{5... | collective-permute-start | bytes 135176 | tf_op jit(solution)/shard_map/ppermute | solution.py:351
  30.6 4.1 %collective-permute-start.7 = (bf16[176,128]{1,0:T(8,128)(2,1)S(1)}, bf16[176,128]{1,0:T(8,128)(2,1)S(1)}, u32[]{:S(2)}, u32[]{:S(2)}) collective-permute-start(bf16[176,128]{1,0:T(8,128)(2,1)S(1)} %shard_map.83.x), channel_id=1, source_target_pairs={{0,4},{4,0},{8,12},{12,8},{16,20},{20,16},{24,28},{28,24},{1,5},{5... | collective-permute-start | bytes 135176 | tf_op jit(solution)/shard_map/ppermute | solution.py:351
  34.8 5.0 %collective-permute-start.10 = (bf16[176,128]{1,0:T(8,128)(2,1)S(1)}, bf16[176,128]{1,0:T(8,128)(2,1)S(1)}, u32[]{:S(2)}, u32[]{:S(2)}) collective-permute-start(bf16[176,128]{1,0:T(8,128)(2,1)S(1)} %shard_map.84.x), channel_id=1, source_target_pairs={{0,16},{4,20},{8,24},{12,28},{16,0},{20,4},{24,8},{28,12},{1,17},{... | collective-permute-start | bytes 135176 | tf_op jit(solution)/shard_map/ppermute | solution.py:351
  38.4 6.3 %collective-permute-start.12 = (bf16[4,64,128]{2,1,0:T(8,128)(2,1)S(1)}, bf16[4,64,128]{2,1,0:T(8,128)(2,1)S(1)}, u32[]{:S(2)}, u32[]{:S(2)}) collective-permute-start(bf16[4,64,128]{2,1,0:T(8,128)(2,1)S(1)} %get-tuple-element.80), channel_id=1, source_target_pairs={{0,1},{2,3},{1,0},{3,2},{4,5},{6,7},{5,4},{7,6},{8,9},{10,11},{9,8... | collective-permute-start | bytes 196616 | tf_op jit(solution)/shard_map/ppermute | solution.py:347
  38.5 6.2 %collective-permute-start.13 = (bf16[4,64,128]{2,1,0:T(8,128)(2,1)S(1)}, bf16[4,64,128]{2,1,0:T(8,128)(2,1)S(1)}, u32[]{:S(2)}, u32[]{:S(2)}) collective-permute-start(bf16[4,64,128]{2,1,0:T(8,128)(2,1)S(1)} %get-tuple-element.81), channel_id=1, source_target_pairs={{1,2},{3,0},{2,1},{0,3},{5,6},{7,4},{6,5},{4,7},{9,10},{11,8},{10,... | collective-permute-start | bytes 196616 | tf_op jit(solution)/shard_map/ppermute | solution.py:347
  39.8 4.9 %collective-permute-start.11 = (bf16[176,128]{1,0:T(8,128)(2,1)S(1)}, bf16[176,128]{1,0:T(8,128)(2,1)S(1)}, u32[]{:S(2)}, u32[]{:S(2)}) collective-permute-start(bf16[176,128]{1,0:T(8,128)(2,1)S(1)} %shard_map.85.mine), channel_id=1, source_target_pairs={{0,8},{4,12},{8,0},{12,4},{16,24},{20,28},{24,16},{28,20},{1,9},{5... | collective-permute-start | bytes 135176 | tf_op jit(solution)/shard_map/ppermute | solution.py:351
  44.7 4.6 %collective-permute-start.14 = (bf16[352,128]{1,0:T(8,128)(2,1)S(1)}, bf16[352,128]{1,0:T(8,128)(2,1)S(1)}, u32[]{:S(2)}, u32[]{:S(2)}) collective-permute-start(bf16[352,128]{1,0:T(8,128)(2,1)S(1)} %shard_map.87.mine), channel_id=1, source_target_pairs={{0,2},{1,3},{2,0},{3,1},{4,6},{5,7},{6,4},{7,5},{8,10},{9,11},{10,... | collective-permute-start | bytes 270344 | tf_op jit(solution)/shard_map/ppermute | solution.py:351
  49.4 1.5 %collective-permute-start.15 = (bf16[704,128]{1,0:T(8,128)(2,1)S(1)}, bf16[704,128]{1,0:T(8,128)(2,1)S(1)}, u32[]{:S(2)}, u32[]{:S(2)}) collective-permute-start(bf16[704,128]{1,0:T(8,128)(2,1)S(1)} %shard_map.90.mine), channel_id=1, source_target_pairs={{0,1},{1,0},{2,3},{3,2},{4,5},{5,4},{6,7},{7,6},{8,9},{9,8},{10,11... | collective-permute-start | bytes 540680 | tf_op jit(solution)/shard_map/ppermute | solution.py:351

commit v10 on v9

--- a/solution.py
+++ b/solution.py
@@ -259,27 +259,34 @@
     end = base + 4 * height
     if end < packed.shape[0]:
         packed[end:] = jnp.zeros((packed.shape[0] - end, packed.shape[1]), F32)
-    half = packed.shape[0] // 2
-    split(packed, keep, send, half, "gy", 1)
+    split(packed, keep, send, owned_half())
 
 
 def side_of(axis, bit):
     return lax.rem(lax.axis_index(axis) // bit, 2)
 
 
+def owned_half():
+    total = 0
+    for axis in ("gz", "gy"):
+        for k in range(lax.axis_size(axis).bit_length() - 1):
+            total = total + side_of(axis, 1 << k)
+    return lax.rem(total, 2)
+
+
 def part(side, rows):
     return pl.ds(pl.multiple_of(side * rows, 16), rows)
 
 
-def split(packed, keep, send, half, axis, bit):
-    side = side_of(axis, bit)
+def split(packed, keep, send, side):
+    half = keep.shape[0]
     keep[...] = packed[part(side, half)]
     send[...] = packed[part(1 - side, half)].astype(BF16)
 
 
 def halve_kernel(mine, other, keep, send, total, *, axis, bit):
     total[...] = mine[...] + other[...].astype(F32)
-    split(total, keep, send, total.shape[0] // 2, axis, bit)
+    split(total, keep, send, side_of(axis, bit))
 
 
 def add_kernel(x, y, out):
@@ -287,8 +294,11 @@
 
 
 def join_kernel(mine, other, out, *, axis, bit):
+    join(mine, other, out, side_of(axis, bit))
+
+
+def join(mine, other, out, side):
     rows = mine.shape[0]
-    side = side_of(axis, bit)
     out[part(side, rows)] = mine[...]
     out[part(1 - side, rows)] = other[...]
 
@@ -324,7 +334,7 @@
 
 
 def unpack_kernel(mine, other, conv_ref, down_ref, sums_ref, *, scale):
-    join_kernel(mine, other, sums_ref, axis="gy", bit=1)
+    join(mine, other, sums_ref, owned_half())
     channels = conv_ref.shape[2]
     for a in range(3):
         for b in range(3):
@@ -348,7 +358,9 @@
 
 
 def flip(cells, axis, bit):
-    return lax.ppermute(cells, axis, [(i, i ^ bit) for i in range(lax.axis_size(axis))])
+    row = lax.axis_size("gy")
+    mask = bit * row | 1 if axis == "gz" else bit | 1
+    return lax.ppermute(cells, ("gz", "gy"), [(i, i ^ mask) for i in range(lax.axis_size("gz") * row)])
 
 
 def tied(first, *others):

time: 52 us -> 51.1 us (0.983)
  waiting for transfers between devices: 13.4 us -> 11.8 us
  starting transfers between devices: 22.3 us -> 23 us
    ppermute x8, waiting for transfers between devices: 11.3 us -> 9.69 us  [flip(): lax.ppermute(cells, ('gz', 'gy'), [(i, i ^ mask) for i in range(lax.axis_...]
    ppermute x8, starting transfers between devices: 9.41 us -> 10.1 us  [flip(): lax.ppermute(cells, ('gz', 'gy'), [(i, i ^ mask) for i in range(lax.axis_...]
  transfers between devices with their start and end apart: 16 -> 16, of which waited for: 8 -> 7; matrix products, arithmetic and copies ran while one was open for 2% -> 2% of each run, Pallas kernels for 16% -> 16%
where the time goes in v10:
time: 51.1 us; the launch traced here: 51 us
  starting transfers between devices  23 us (45%)
  Pallas kernels  12.6 us (25%)
  waiting for transfers between devices  11.8 us (23%)
  local copies, waits for them, and re-layouts  2.7 us (5%)
  between operations  0.83 us (2%)
    ppermute x8, starting transfers between devices, swap(): return lax.ppermute(cells, axis, pairs + [(b, a) for a, b in pairs])  12.9 us
    pallas_call x18, Pallas kernels, call(): pl.pallas_call(kernel, out_shape=[jax.ShapeDtypeStruct(s, d) for s, d in...  12.6 us
    ppermute x8, starting transfers between devices, flip(): lax.ppermute(cells, ('gz', 'gy'), [(i, i ^ mask) for i in range(lax.axis_...  10.1 us
    ppermute x8, waiting for transfers between devices, flip(): lax.ppermute(cells, ('gz', 'gy'), [(i, i ^ mask) for i in range(lax.axis_...  9.69 us
    unnamed x11, local copies, waits for them, and re-layouts  2.18 us
    ppermute x8, waiting for transfers between devices, swap(): return lax.ppermute(cells, axis, pairs + [(b, a) for a, b in pairs])  2.13 us
  transfers between devices with their start and end apart: 16, of which 7 were waited for; matrix products, arithmetic and copies ran while one was open for 2% of the time, Pallas kernels for 16%

profile of v10, /device:TPU:0, one launch (start us, length us, event | category | flops | bytes accessed | tf_op | source)
XLA Modules:
  0.0 51.0 jit_solution(14281991939002953317)
XLA Ops:
  0.6 0.9 %copy-done.2 = bf16[64,2,8,128]{3,2,1,0:T(8,128)(2,1)S(1)} copy-done((bf16[64,2,8,128]{3,2,1,0:T(8,128)(2,1)S(1)}, bf16[64,2,8,128]{3,2,1,0:T(8,128)(2,1)}, u32[]{:S(2)}) %copy-start.2) | copy-done | bytes 262168
  1.6 0.2 shard_map.75
  1.8 3.0 %collective-permute-start = (bf16[8,64,128]{2,1,0:T(8,128)(2,1)S(1)}, bf16[8,64,128]{2,1,0:T(8,128)(2,1)S(1)}, u32[]{:S(2)}, u32[]{:S(2)}) collective-permute-start(bf16[8,64,128]{2,1,0:T(8,128)(2,1)S(1)} %get-tuple-element.47.near), channel_id=1, source_target_pairs={{0,4},{8,12},{16,20},{24,28},{4,0},{12,8},{20,16},{28,24},{1,5},{9... | collective-permute-start | bytes 393224 | tf_op jit(solution)/shard_map/ppermute | solution.py:357
  4.8 3.5 %collective-permute-start.1 = (bf16[8,64,128]{2,1,0:T(8,128)(2,1)S(1)}, bf16[8,64,128]{2,1,0:T(8,128)(2,1)S(1)}, u32[]{:S(2)}, u32[]{:S(2)}) collective-permute-start(bf16[8,64,128]{2,1,0:T(8,128)(2,1)S(1)} %get-tuple-element.48.far), channel_id=1, source_target_pairs={{4,8},{12,16},{20,24},{28,0},{8,4},{16,12},{24,20},{0,28},{5,9},{1... | collective-permute-start | bytes 393224 | tf_op jit(solution)/shard_map/ppermute | solution.py:357
  8.4 1.0 %copy-done = bf16[3,3,64,192]{3,2,1,0:T(8,128)(2,1)S(1)} copy-done((bf16[3,3,64,192]{3,2,1,0:T(8,128)(2,1)S(1)}, bf16[3,3,64,192]{3,2,1,0:T(8,128)(2,1)}, u32[]{:S(2)}) %copy-start) | copy-done | bytes 221208
  9.3 1.9 %shard_map.76 = (bf16[2,10,192,128]{3,2,1,0:T(8,128)(2,1)S(1)}, f32[2,8,64,128]{3,2,1,0:T(8,128)S(1)}, f32[2,8,64,128]{3,2,1,0:T(8,128)S(1)}) custom-call(bf16[8,64,128]{2,1,0:T(8,128)(2,1)S(1)} %get-tuple-element.47.near, bf16[8,64,128]{2,1,0:T(8,128)(2,1)S(1)} %get-tuple-element.48.far, bf16[3,3,64,192]{3,2,1,0:T(8,128)(2,1)S(1)} %copy-done, ...), custom_call_target="tpu_custom_call" | custom-call | flops 301989888 | bytes 2711552 | tf_op jit(solution)/shard_map/pallas_call | solution.py:20
  11.3 0.0 copy-start.1
  11.3 0.0 collective-permute-done.near.near_in
  11.3 1.2 %collective-permute-done.1.far.far_in = bf16[8,64,128]{2,1,0:T(8,128)(2,1)S(1)} collective-permute-done((bf16[8,64,128]{2,1,0:T(8,128)(2,1)S(1)}, bf16[8,64,128]{2,1,0:T(8,128)(2,1)S(1)}, u32[]{:S(2)}, u32[]{:S(2)}) %collective-permute-start.1) | collective-permute-done | bytes 131104 | tf_op jit(solution)/shard_map/ppermute | solution.py:357
  12.5 0.1 collective-permute-start.2
  12.6 1.6 %collective-permute-start.3 = (bf16[4,64,128]{2,1,0:T(8,128)(2,1)S(1)}, bf16[4,64,128]{2,1,0:T(8,128)(2,1)S(1)}, u32[]{:S(2)}, u32[]{:S(2)}) collective-permute-start(bf16[4,64,128]{2,1,0:T(8,128)(2,1)S(1)} %get-tuple-element.56), channel_id=1, source_target_pairs={{1,2},{3,0},{2,1},{0,3},{5,6},{7,4},{6,5},{4,7},{9,10},{11,8},{10,... | collective-permute-start | bytes 196616 | tf_op jit(solution)/shard_map/ppermute | solution.py:357
  14.2 1.4 %shard_map.77 = (bf16[2,10,192,128]{3,2,1,0:T(8,128)(2,1)S(1)}, f32[2,8,64,128]{3,2,1,0:T(8,128)S(1)}) custom-call(bf16[8,64,128]{2,1,0:T(8,128)(2,1)S(1)} %collective-permute-done.near.near_in, bf16[8,64,128]{2,1,0:T(8,128)(2,1)S(1)} %collective-permute-done.1.far.far_in, bf16[3,3,64,192]{3,2,1,0:T(8,128)(2,1)S(1)} %copy-done.1, ...), custom_call_target="tpu_custom_call" | custom-call | flops 150994944 | bytes 2514944 | tf_op jit(solution)/shard_map/pallas_call | solution.py:20
  15.6 0.0 collective-permute-done.2.near
  15.6 0.9 %collective-permute-done.3.far = bf16[4,64,128]{2,1,0:T(8,128)(2,1)S(1)} collective-permute-done((bf16[4,64,128]{2,1,0:T(8,128)(2,1)S(1)}, bf16[4,64,128]{2,1,0:T(8,128)(2,1)S(1)}, u32[]{:S(2)}, u32[]{:S(2)}) %collective-permute-start.3) | collective-permute-done | bytes 65568 | tf_op jit(solution)/shard_map/ppermute | solution.py:357
  16.5 0.5 %shard_map.79 = (bf16[4,2,192,128]{3,2,1,0:T(8,128)(2,1)S(1)}, bf16[8,64,128]{2,1,0:T(8,128)(2,1)S(1)}, bf16[8,64,128]{2,1,0:T(8,128)(2,1)S(1)}, bf16[2,8,64,128]{3,2,1,0:T(8,128)(2,1)S(1)}) custom-call(bf16[4,64,128]{2,1,0:T(8,128)(2,1)S(1)} %collective-permute-done.2.near, bf16[4,64,128]{2,1,0:T(8,128)(2,1)S(1)} %collective-permute-done.3.far, ...), custom_call_target="tpu_custom_call" | custom-call | flops 45298484 | bytes 2318336 | tf_op jit(solution)/shard_map/pallas_call | solution.py:20
  17.0 2.3 %shard_map.80 = (f32[704,128]{1,0:T(8,128)S(1)}, bf16[704,128]{1,0:T(8,128)(2,1)S(1)}) custom-call(bf16[2,10,192,128]{3,2,1,0:T(8,128)(2,1)S(1)} %get-tuple-element.49.inner, bf16[2,10,192,128]{3,2,1,0:T(8,128)(2,1)S(1)} %get-tuple-element.54.outer, bf16[4,2,192,128]{3,2,1,0:T(8,128)(2,1)S(1)} %get-tuple-element.59.edges, ...), custom_call_target="tpu_custom_call" | custom-call | flops 452984832 | bytes 3489792 | tf_op jit(solution)/shard_map/pallas_call | solution.py:20
  19.4 0.5 collective-permute-start.4
  19.8 1.0 %collective-permute-done.4.other = bf16[704,128]{1,0:T(8,128)(2,1)S(1)} collective-permute-done((bf16[704,128]{1,0:T(8,128)(2,1)S(1)}, bf16[704,128]{1,0:T(8,128)(2,1)S(1)}, u32[]{:S(2)}, u32[]{:S(2)}) %collective-permute-start.4) | collective-permute-done | bytes 180256 | tf_op jit(solution)/shard_map/ppermute | solution.py:363
  20.9 0.1 shard_map.81
  20.9 1.5 %collective-permute-start.5 = (bf16[352,128]{1,0:T(8,128)(2,1)S(1)}, bf16[352,128]{1,0:T(8,128)(2,1)S(1)}, u32[]{:S(2)}, u32[]{:S(2)}) collective-permute-start(bf16[352,128]{1,0:T(8,128)(2,1)S(1)} %get-tuple-element.69), channel_id=1, source_target_pairs={{0,3},{1,2},{2,1},{3,0},{4,7},{5,6},{6,5},{7,4},{8,11},{9,10},{10,... | collective-permute-start | bytes 270344 | tf_op jit(solution)/shard_map/ppermute | solution.py:363
  22.5 0.4 collective-permute-start.8
  22.9 3.5 %collective-permute-start.9 = (bf16[8,64,128]{2,1,0:T(8,128)(2,1)S(1)}, bf16[8,64,128]{2,1,0:T(8,128)(2,1)S(1)}, u32[]{:S(2)}, u32[]{:S(2)}) collective-permute-start(bf16[8,64,128]{2,1,0:T(8,128)(2,1)S(1)} %get-tuple-element.73.far), channel_id=1, source_target_pairs={{4,8},{12,16},{20,24},{28,0},{8,4},{16,12},{24,20},{0,28},{5,9},{1... | collective-permute-start | bytes 393224 | tf_op jit(solution)/shard_map/ppermute | solution.py:357
  26.4 0.0 collective-permute-done.5.other
  26.4 0.1 collective-permute-start.6
  26.5 3.7 %collective-permute-done.6.y = bf16[176,128]{1,0:T(8,128)(2,1)S(1)} collective-permute-done((bf16[176,128]{1,0:T(8,128)(2,1)S(1)}, bf16[176,128]{1,0:T(8,128)(2,1)S(1)}, u32[]{:S(2)}, u32[]{:S(2)}) %collective-permute-start.6) | collective-permute-done | bytes 45088 | tf_op jit(solution)/shard_map/ppermute | solution.py:363
  30.2 1.9 %collective-permute-start.7 = (bf16[176,128]{1,0:T(8,128)(2,1)S(1)}, bf16[176,128]{1,0:T(8,128)(2,1)S(1)}, u32[]{:S(2)}, u32[]{:S(2)}) collective-permute-start(bf16[176,128]{1,0:T(8,128)(2,1)S(1)} %shard_map.83.x), channel_id=1, source_target_pairs={{0,5},{1,4},{2,7},{3,6},{4,1},{5,0},{6,3},{7,2},{8,13},{9,12},{10,... | collective-permute-start | bytes 135176 | tf_op jit(solution)/shard_map/ppermute | solution.py:363
  32.1 1.8 %collective-permute-done.7.y = bf16[176,128]{1,0:T(8,128)(2,1)S(1)} collective-permute-done((bf16[176,128]{1,0:T(8,128)(2,1)S(1)}, bf16[176,128]{1,0:T(8,128)(2,1)S(1)}, u32[]{:S(2)}, u32[]{:S(2)}) %collective-permute-start.7) | collective-permute-done | bytes 45088 | tf_op jit(solution)/shard_map/ppermute | solution.py:363
  33.9 0.0 collective-permute-done.8.near_in
  33.9 0.0 collective-permute-done.9.far_in
  33.9 2.4 %collective-permute-start.10 = (bf16[176,128]{1,0:T(8,128)(2,1)S(1)}, bf16[176,128]{1,0:T(8,128)(2,1)S(1)}, u32[]{:S(2)}, u32[]{:S(2)}) collective-permute-start(bf16[176,128]{1,0:T(8,128)(2,1)S(1)} %shard_map.84.x), channel_id=1, source_target_pairs={{0,17},{1,16},{2,19},{3,18},{4,21},{5,20},{6,23},{7,22},{8,25},{9,... | collective-permute-start | bytes 135176 | tf_op jit(solution)/shard_map/ppermute | solution.py:363
  36.3 0.3 copy.9
  36.6 1.4 %shard_map.86 = bf16[128,256]{1,0:T(8,128)(2,1)} custom-call(bf16[2,8,64,128]{3,2,1,0:T(8,128)(2,1)S(1)} %get-tuple-element.75.h_ref, bf16[2,2,128,128]{3,2,1,0:T(8,128)(2,1)S(1)} %copy-done.3), custom_call_target="tpu_custom_call" | custom-call | flops 45298484 | bytes 458752 | tf_op jit(solution)/shard_map/pallas_call | solution.py:20
  38.0 0.5 collective-permute-start.12
  38.5 0.3 collective-permute-start.13
  38.7 0.0 collective-permute-done.10.y
  38.8 2.1 %collective-permute-start.11 = (bf16[176,128]{1,0:T(8,128)(2,1)S(1)}, bf16[176,128]{1,0:T(8,128)(2,1)S(1)}, u32[]{:S(2)}, u32[]{:S(2)}) collective-permute-start(bf16[176,128]{1,0:T(8,128)(2,1)S(1)} %shard_map.85.mine), channel_id=1, source_target_pairs={{0,9},{1,8},{2,11},{3,10},{4,13},{5,12},{6,15},{7,14},{8,1},{9,0},... | collective-permute-start | bytes 135176 | tf_op jit(solution)/shard_map/ppermute | solution.py:363
  40.9 0.3 copy.10
  41.2 0.2 copy.11.w_ref
  41.4 2.3 %shard_map.88.acc_ref = f32[2,8,64,128]{3,2,1,0:T(8,128)S(1)} custom-call(bf16[8,64,128]{2,1,0:T(8,128)(2,1)S(1)} %get-tuple-element.72.near, bf16[8,64,128]{2,1,0:T(8,128)(2,1)S(1)} %get-tuple-element.73.far, bf16[8,64,128]{2,1,0:T(8,128)(2,1)S(1)} %collective-permute-done.8.near_in, bf16[8,64,128]{2,1,0:T(8,128)(2,1)S(1)} %collective-permute-done.9.far_in, ...), custom_call_target="tpu_custom_call" | custom-call | flops 452984832 | bytes 1269760 | tf_op jit(solution)/shard_map/pallas_call | solution.py:20
  43.7 0.0 collective-permute-done.11.other
  43.8 0.0 collective-permute-done.12.near
  43.8 0.0 collective-permute-done.13.far
  43.8 1.4 %collective-permute-start.14 = (bf16[352,128]{1,0:T(8,128)(2,1)S(1)}, bf16[352,128]{1,0:T(8,128)(2,1)S(1)}, u32[]{:S(2)}, u32[]{:S(2)}) collective-permute-start(bf16[352,128]{1,0:T(8,128)(2,1)S(1)} %shard_map.87.mine), channel_id=1, source_target_pairs={{0,3},{1,2},{2,1},{3,0},{4,7},{5,6},{6,5},{7,4},{8,11},{9,10},{10,... | collective-permute-start | bytes 270344 | tf_op jit(solution)/shard_map/ppermute | solution.py:363
  45.2 1.3 %shard_map.91 = f32[1024,128]{1,0:T(8,128)} custom-call(bf16[4,64,128]{2,1,0:T(8,128)(2,1)S(1)} %collective-permute-done.12.near, bf16[4,64,128]{2,1,0:T(8,128)(2,1)S(1)} %collective-permute-done.13.far, f32[2,8,64,128]{3,2,1,0:T(8,128)S(1)} %shard_map.88.acc_ref, bf16[3,3,64,192]{3,2,1,0:T(8,128)(2,1)S(1)} %copy.11.w_ref), custom_call_target="tpu_custom_call" | custom-call | flops 45298484 | bytes 1400832 | tf_op jit(solution)/shard_map/pallas_call | solution.py:20
  46.5 1.9 %collective-permute-done.14.other = bf16[352,128]{1,0:T(8,128)(2,1)S(1)} collective-permute-done((bf16[352,128]{1,0:T(8,128)(2,1)S(1)}, bf16[352,128]{1,0:T(8,128)(2,1)S(1)}, u32[]{:S(2)}, u32[]{:S(2)}) %collective-permute-start.14) | collective-permute-done | bytes 90144 | tf_op jit(solution)/shard_map/ppermute | solution.py:363
  48.5 0.2 collective-permute-start.15
  48.7 1.3 %collective-permute-done.15.other = bf16[704,128]{1,0:T(8,128)(2,1)S(1)} collective-permute-done((bf16[704,128]{1,0:T(8,128)(2,1)S(1)}, bf16[704,128]{1,0:T(8,128)(2,1)S(1)}, u32[]{:S(2)}, u32[]{:S(2)}) %collective-permute-start.15) | collective-permute-done | bytes 180256 | tf_op jit(solution)/shard_map/ppermute | solution.py:363
  50.0 1.0 %shard_map.92 = (f32[3,3,64,192]{3,2,1,0:T(8,128)}, f32[2,2,128,128]{3,2,1,0:T(8,128)}) custom-call(bf16[704,128]{1,0:T(8,128)(2,1)S(1)} %shard_map.90.mine, bf16[704,128]{1,0:T(8,128)(2,1)S(1)} %collective-permute-done.15.other), custom_call_target="tpu_custom_call" | custom-call | bytes 1064960 | tf_op jit(solution)/shard_map/pallas_call | solution.py:20
  (16 shorter events, 0.2 us)
Async XLA Ops:
  0.6 1.0 %copy-start.2 = (bf16[64,2,8,128]{3,2,1,0:T(8,128)(2,1)S(1)}, bf16[64,2,8,128]{3,2,1,0:T(8,128)(2,1)}, u32[]{:S(2)}) copy-start(bf16[64,2,8,128]{3,2,1,0:T(8,128)(2,1)} %f_ref.1) | copy-start | bytes 786436
  1.6 6.8 %copy-start.3 = (bf16[2,2,128,128]{3,2,1,0:T(8,128)(2,1)S(1)}, bf16[2,2,128,128]{3,2,1,0:T(8,128)(2,1)}, u32[]{:S(2)}) copy-start(bf16[2,2,128,128]{3,2,1,0:T(8,128)(2,1)} %d_ref.3) | copy-start | bytes 393220
  1.6 6.8 %copy-start.4 = (bf16[128,1,256]{2,0,1:T(8,128)(2,1)S(1)}, bf16[128,1,256]{2,0,1:T(8,128)(2,1)}, u32[]{:S(2)}) copy-start(bf16[128,1,256]{2,0,1:T(8,128)(2,1)} %param.7) | copy-start | bytes 196612
  1.8 9.5 %collective-permute-start = (bf16[8,64,128]{2,1,0:T(8,128)(2,1)S(1)}, bf16[8,64,128]{2,1,0:T(8,128)(2,1)S(1)}, u32[]{:S(2)}, u32[]{:S(2)}) collective-permute-start(bf16[8,64,128]{2,1,0:T(8,128)(2,1)S(1)} %get-tuple-element.47.near), channel_id=1, source_target_pairs={{0,4},{8,12},{16,20},{24,28},{4,0},{12,8},{20,16},{28,24},{1,5},{9... | collective-permute-start | bytes 393224 | tf_op jit(solution)/shard_map/ppermute | solution.py:357
  4.8 7.7 %collective-permute-start.1 = (bf16[8,64,128]{2,1,0:T(8,128)(2,1)S(1)}, bf16[8,64,128]{2,1,0:T(8,128)(2,1)S(1)}, u32[]{:S(2)}, u32[]{:S(2)}) collective-permute-start(bf16[8,64,128]{2,1,0:T(8,128)(2,1)S(1)} %get-tuple-element.48.far), channel_id=1, source_target_pairs={{4,8},{12,16},{20,24},{28,0},{8,4},{16,12},{24,20},{0,28},{5,9},{1... | collective-permute-start | bytes 393224 | tf_op jit(solution)/shard_map/ppermute | solution.py:357
  8.4 1.0 %copy-start = (bf16[3,3,64,192]{3,2,1,0:T(8,128)(2,1)S(1)}, bf16[3,3,64,192]{3,2,1,0:T(8,128)(2,1)}, u32[]{:S(2)}) copy-start(bf16[3,3,64,192]{3,2,1,0:T(8,128)(2,1)} %w_ref.5) | copy-start | bytes 663556
  11.3 3.0 %copy-start.1 = (bf16[3,3,64,192]{3,2,1,0:T(8,128)(2,1)S(1)}, bf16[3,3,64,192]{3,2,1,0:T(8,128)(2,1)}, u32[]{:S(2)}) copy-start(bf16[3,3,64,192]{3,2,1,0:T(8,128)(2,1)} %w_ref.5) | copy-start | bytes 663556
  12.5 3.1 %collective-permute-start.2 = (bf16[4,64,128]{2,1,0:T(8,128)(2,1)S(1)}, bf16[4,64,128]{2,1,0:T(8,128)(2,1)S(1)}, u32[]{:S(2)}, u32[]{:S(2)}) collective-permute-start(bf16[4,64,128]{2,1,0:T(8,128)(2,1)S(1)} %get-tuple-element.55), channel_id=1, source_target_pairs={{0,1},{2,3},{1,0},{3,2},{4,5},{6,7},{5,4},{7,6},{8,9},{10,11},{9,8... | collective-permute-start | bytes 196616 | tf_op jit(solution)/shard_map/ppermute | solution.py:357
  12.6 3.9 %collective-permute-start.3 = (bf16[4,64,128]{2,1,0:T(8,128)(2,1)S(1)}, bf16[4,64,128]{2,1,0:T(8,128)(2,1)S(1)}, u32[]{:S(2)}, u32[]{:S(2)}) collective-permute-start(bf16[4,64,128]{2,1,0:T(8,128)(2,1)S(1)} %get-tuple-element.56), channel_id=1, source_target_pairs={{1,2},{3,0},{2,1},{0,3},{5,6},{7,4},{6,5},{4,7},{9,10},{11,8},{10,... | collective-permute-start | bytes 196616 | tf_op jit(solution)/shard_map/ppermute | solution.py:357
  19.4 1.5 %collective-permute-start.4 = (bf16[704,128]{1,0:T(8,128)(2,1)S(1)}, bf16[704,128]{1,0:T(8,128)(2,1)S(1)}, u32[]{:S(2)}, u32[]{:S(2)}) collective-permute-start(bf16[704,128]{1,0:T(8,128)(2,1)S(1)} %get-tuple-element.65), channel_id=1, source_target_pairs={{0,1},{1,0},{2,3},{3,2},{4,5},{5,4},{6,7},{7,6},{8,9},{9,8},{10,11... | collective-permute-start | bytes 540680 | tf_op jit(solution)/shard_map/ppermute | solution.py:363
  20.9 5.4 %collective-permute-start.5 = (bf16[352,128]{1,0:T(8,128)(2,1)S(1)}, bf16[352,128]{1,0:T(8,128)(2,1)S(1)}, u32[]{:S(2)}, u32[]{:S(2)}) collective-permute-start(bf16[352,128]{1,0:T(8,128)(2,1)S(1)} %get-tuple-element.69), channel_id=1, source_target_pairs={{0,3},{1,2},{2,1},{3,0},{4,7},{5,6},{6,5},{7,4},{8,11},{9,10},{10,... | collective-permute-start | bytes 270344 | tf_op jit(solution)/shard_map/ppermute | solution.py:363
  22.5 11.4 %collective-permute-start.8 = (bf16[8,64,128]{2,1,0:T(8,128)(2,1)S(1)}, bf16[8,64,128]{2,1,0:T(8,128)(2,1)S(1)}, u32[]{:S(2)}, u32[]{:S(2)}) collective-permute-start(bf16[8,64,128]{2,1,0:T(8,128)(2,1)S(1)} %get-tuple-element.72.near), channel_id=1, source_target_pairs={{0,4},{8,12},{16,20},{24,28},{4,0},{12,8},{20,16},{28,24},{1,5},{9... | collective-permute-start | bytes 393224 | tf_op jit(solution)/shard_map/ppermute | solution.py:357
  22.9 11.0 %collective-permute-start.9 = (bf16[8,64,128]{2,1,0:T(8,128)(2,1)S(1)}, bf16[8,64,128]{2,1,0:T(8,128)(2,1)S(1)}, u32[]{:S(2)}, u32[]{:S(2)}) collective-permute-start(bf16[8,64,128]{2,1,0:T(8,128)(2,1)S(1)} %get-tuple-element.73.far), channel_id=1, source_target_pairs={{4,8},{12,16},{20,24},{28,0},{8,4},{16,12},{24,20},{0,28},{5,9},{1... | collective-permute-start | bytes 393224 | tf_op jit(solution)/shard_map/ppermute | solution.py:357
  26.4 3.8 %collective-permute-start.6 = (bf16[176,128]{1,0:T(8,128)(2,1)S(1)}, bf16[176,128]{1,0:T(8,128)(2,1)S(1)}, u32[]{:S(2)}, u32[]{:S(2)}) collective-permute-start(bf16[176,128]{1,0:T(8,128)(2,1)S(1)} %get-tuple-element.71), channel_id=1, source_target_pairs={{0,9},{1,8},{2,11},{3,10},{4,13},{5,12},{6,15},{7,14},{8,1},{9,0},... | collective-permute-start | bytes 135176 | tf_op jit(solution)/shard_map/ppermute | solution.py:363
  30.2 3.6 %collective-permute-start.7 = (bf16[176,128]{1,0:T(8,128)(2,1)S(1)}, bf16[176,128]{1,0:T(8,128)(2,1)S(1)}, u32[]{:S(2)}, u32[]{:S(2)}) collective-permute-start(bf16[176,128]{1,0:T(8,128)(2,1)S(1)} %shard_map.83.x), channel_id=1, source_target_pairs={{0,5},{1,4},{2,7},{3,6},{4,1},{5,0},{6,3},{7,2},{8,13},{9,12},{10,... | collective-permute-start | bytes 135176 | tf_op jit(solution)/shard_map/ppermute | solution.py:363
  33.9 4.8 %collective-permute-start.10 = (bf16[176,128]{1,0:T(8,128)(2,1)S(1)}, bf16[176,128]{1,0:T(8,128)(2,1)S(1)}, u32[]{:S(2)}, u32[]{:S(2)}) collective-permute-start(bf16[176,128]{1,0:T(8,128)(2,1)S(1)} %shard_map.84.x), channel_id=1, source_target_pairs={{0,17},{1,16},{2,19},{3,18},{4,21},{5,20},{6,23},{7,22},{8,25},{9,... | collective-permute-start | bytes 135176 | tf_op jit(solution)/shard_map/ppermute | solution.py:363
  38.0 5.7 %collective-permute-start.12 = (bf16[4,64,128]{2,1,0:T(8,128)(2,1)S(1)}, bf16[4,64,128]{2,1,0:T(8,128)(2,1)S(1)}, u32[]{:S(2)}, u32[]{:S(2)}) collective-permute-start(bf16[4,64,128]{2,1,0:T(8,128)(2,1)S(1)} %get-tuple-element.80), channel_id=1, source_target_pairs={{0,1},{2,3},{1,0},{3,2},{4,5},{6,7},{5,4},{7,6},{8,9},{10,11},{9,8... | collective-permute-start | bytes 196616 | tf_op jit(solution)/shard_map/ppermute | solution.py:357
  38.5 5.3 %collective-permute-start.13 = (bf16[4,64,128]{2,1,0:T(8,128)(2,1)S(1)}, bf16[4,64,128]{2,1,0:T(8,128)(2,1)S(1)}, u32[]{:S(2)}, u32[]{:S(2)}) collective-permute-start(bf16[4,64,128]{2,1,0:T(8,128)(2,1)S(1)} %get-tuple-element.81), channel_id=1, source_target_pairs={{1,2},{3,0},{2,1},{0,3},{5,6},{7,4},{6,5},{4,7},{9,10},{11,8},{10,... | collective-permute-start | bytes 196616 | tf_op jit(solution)/shard_map/ppermute | solution.py:357
  38.8 5.0 %collective-permute-start.11 = (bf16[176,128]{1,0:T(8,128)(2,1)S(1)}, bf16[176,128]{1,0:T(8,128)(2,1)S(1)}, u32[]{:S(2)}, u32[]{:S(2)}) collective-permute-start(bf16[176,128]{1,0:T(8,128)(2,1)S(1)} %shard_map.85.mine), channel_id=1, source_target_pairs={{0,9},{1,8},{2,11},{3,10},{4,13},{5,12},{6,15},{7,14},{8,1},{9,0},... | collective-permute-start | bytes 135176 | tf_op jit(solution)/shard_map/ppermute | solution.py:363
  43.8 4.7 %collective-permute-start.14 = (bf16[352,128]{1,0:T(8,128)(2,1)S(1)}, bf16[352,128]{1,0:T(8,128)(2,1)S(1)}, u32[]{:S(2)}, u32[]{:S(2)}) collective-permute-start(bf16[352,128]{1,0:T(8,128)(2,1)S(1)} %shard_map.87.mine), channel_id=1, source_target_pairs={{0,3},{1,2},{2,1},{3,0},{4,7},{5,6},{6,5},{7,4},{8,11},{9,10},{10,... | collective-permute-start | bytes 270344 | tf_op jit(solution)/shard_map/ppermute | solution.py:363
  48.5 1.5 %collective-permute-start.15 = (bf16[704,128]{1,0:T(8,128)(2,1)S(1)}, bf16[704,128]{1,0:T(8,128)(2,1)S(1)}, u32[]{:S(2)}, u32[]{:S(2)}) collective-permute-start(bf16[704,128]{1,0:T(8,128)(2,1)S(1)} %shard_map.90.mine), channel_id=1, source_target_pairs={{0,1},{1,0},{2,3},{3,2},{4,5},{5,4},{6,7},{7,6},{8,9},{9,8},{10,11... | collective-permute-start | bytes 540680 | tf_op jit(solution)/shard_map/ppermute | solution.py:363

commit v11 on v10

--- a/solution.py
+++ b/solution.py
@@ -416,7 +416,7 @@
     )
     keep, gates = tied(keep, *gates)
     near, far = gates
-    near_in = swap(near, "gz", 0)
+    near_in, far_in = swap(near, "gz", 0), swap(far, "gz", 1)
     for level, (axis, bit) in enumerate((("gy", 2), ("gz", 2))):
         size = rows >> (level + 2)
         mine, got = keep, flip(send, *(("gy", 1), ("gy", 2))[level])
@@ -425,16 +425,15 @@
             [((size, 128), F32), ((size, 128), BF16)], [((2 * size, 128), F32)], 0, (mine, got),
         )
         if level == 0:
-            keep, (far, hidden) = tied(keep, far, hidden)
-            far_in = swap(far, "gz", 1)
+            keep, (hidden,) = tied(keep, hidden)
             (section_out,) = call(
                 section_kernel, [((out_channels, cot.shape[1]), BF16)], [], conv_flops // 10,
                 (hidden, down_weight),
             )
     shard = ((rows // 8, 128), BF16)
+    send, outside = tied(send, near_in, far_in)
     (sums,) = call(add_kernel, [shard], [], 0, (keep, flip(send, "gz", 2)))
     (sums,) = call(add_kernel, [shard], [], 0, (sums, flip(sums, "gz", 1)))
-    sums, outside = tied(sums, near_in, far_in)
     sends = call(edges_kernel, [edge, edge], [], 0, (*gates, *outside))
     beside = swapped(*sends, "gy")
     (acc,) = call(

time: 51.1 us -> 52.4 us (1.025)
  waiting for transfers between devices: 11.8 us -> 18.6 us
  starting transfers between devices: 23 us -> 17.5 us
    ppermute x8, waiting for transfers between devices: 9.69 us -> 16.4 us  [flip(): lax.ppermute(cells, ('gz', 'gy'), [(i, i ^ mask) for i in range(lax.axis_...]
    ppermute x8, starting transfers between devices: 10.1 us -> 3.67 us  [flip(): lax.ppermute(cells, ('gz', 'gy'), [(i, i ^ mask) for i in range(lax.axis_...]
    ppermute x8, starting transfers between devices: 12.9 us -> 13.9 us  [swap(): return lax.ppermute(cells, axis, pairs + [(b, a) for a, b in pairs])]
  transfers between devices with their start and end apart: 16 -> 16, of which waited for: 7 -> 9; matrix products, arithmetic and copies ran while one was open for 2% -> 1% of each run, Pallas kernels for 16% -> 16%
where the time goes in v11:
time: 52.4 us; the launch traced here: 52.2 us
  waiting for transfers between devices  18.6 us (35%)
  starting transfers between devices  17.5 us (33%)
  Pallas kernels  12.6 us (24%)
  local copies, waits for them, and re-layouts  2.7 us (5%)
  between operations  0.82 us (2%)
    ppermute x8, waiting for transfers between devices, flip(): lax.ppermute(cells, ('gz', 'gy'), [(i, i ^ mask) for i in range(lax.axis_...  16.4 us
    ppermute x8, starting transfers between devices, swap(): return lax.ppermute(cells, axis, pairs + [(b, a) for a, b in pairs])  13.9 us
    pallas_call x18, Pallas kernels, call(): pl.pallas_call(kernel, out_shape=[jax.ShapeDtypeStruct(s, d) for s, d in...  12.6 us
    ppermute x8, starting transfers between devices, flip(): lax.ppermute(cells, ('gz', 'gy'), [(i, i ^ mask) for i in range(lax.axis_...  3.67 us
    unnamed x11, local copies, waits for them, and re-layouts  2.18 us
    ppermute x8, waiting for transfers between devices, swap(): return lax.ppermute(cells, axis, pairs + [(b, a) for a, b in pairs])  2.13 us
  transfers between devices with their start and end apart: 16, of which 9 were waited for; matrix products, arithmetic and copies ran while one was open for 1% of the time, Pallas kernels for 16%

profile of v11, /device:TPU:0, one launch (start us, length us, event | category | flops | bytes accessed | tf_op | source)
XLA Modules:
  0.0 52.2 jit_solution(17862450900109656843)
XLA Ops:
  0.6 0.9 %copy-done.2 = bf16[64,2,8,128]{3,2,1,0:T(8,128)(2,1)S(1)} copy-done((bf16[64,2,8,128]{3,2,1,0:T(8,128)(2,1)S(1)}, bf16[64,2,8,128]{3,2,1,0:T(8,128)(2,1)}, u32[]{:S(2)}) %copy-start.2) | copy-done | bytes 262168
  1.6 0.2 shard_map.75
  1.8 3.0 %collective-permute-start = (bf16[8,64,128]{2,1,0:T(8,128)(2,1)S(1)}, bf16[8,64,128]{2,1,0:T(8,128)(2,1)S(1)}, u32[]{:S(2)}, u32[]{:S(2)}) collective-permute-start(bf16[8,64,128]{2,1,0:T(8,128)(2,1)S(1)} %get-tuple-element.46.near), channel_id=1, source_target_pairs={{0,4},{8,12},{16,20},{24,28},{4,0},{12,8},{20,16},{28,24},{1,5},{9... | collective-permute-start | bytes 393224 | tf_op jit(solution)/shard_map/ppermute | solution.py:357
  4.8 3.5 %collective-permute-start.1 = (bf16[8,64,128]{2,1,0:T(8,128)(2,1)S(1)}, bf16[8,64,128]{2,1,0:T(8,128)(2,1)S(1)}, u32[]{:S(2)}, u32[]{:S(2)}) collective-permute-start(bf16[8,64,128]{2,1,0:T(8,128)(2,1)S(1)} %get-tuple-element.47.far), channel_id=1, source_target_pairs={{4,8},{12,16},{20,24},{28,0},{8,4},{16,12},{24,20},{0,28},{5,9},{1... | collective-permute-start | bytes 393224 | tf_op jit(solution)/shard_map/ppermute | solution.py:357
  8.4 1.0 %copy-done = bf16[3,3,64,192]{3,2,1,0:T(8,128)(2,1)S(1)} copy-done((bf16[3,3,64,192]{3,2,1,0:T(8,128)(2,1)S(1)}, bf16[3,3,64,192]{3,2,1,0:T(8,128)(2,1)}, u32[]{:S(2)}) %copy-start) | copy-done | bytes 221208
  9.3 1.9 %shard_map.76 = (bf16[2,10,192,128]{3,2,1,0:T(8,128)(2,1)S(1)}, f32[2,8,64,128]{3,2,1,0:T(8,128)S(1)}, f32[2,8,64,128]{3,2,1,0:T(8,128)S(1)}) custom-call(bf16[8,64,128]{2,1,0:T(8,128)(2,1)S(1)} %get-tuple-element.46.near, bf16[8,64,128]{2,1,0:T(8,128)(2,1)S(1)} %get-tuple-element.47.far, bf16[3,3,64,192]{3,2,1,0:T(8,128)(2,1)S(1)} %copy-done, ...), custom_call_target="tpu_custom_call" | custom-call | flops 301989888 | bytes 2711552 | tf_op jit(solution)/shard_map/pallas_call | solution.py:20
  11.3 0.0 copy-start.1
  11.3 0.0 collective-permute-done.near.near_in
  11.3 1.2 %collective-permute-done.1.far.far_in = bf16[8,64,128]{2,1,0:T(8,128)(2,1)S(1)} collective-permute-done((bf16[8,64,128]{2,1,0:T(8,128)(2,1)S(1)}, bf16[8,64,128]{2,1,0:T(8,128)(2,1)S(1)}, u32[]{:S(2)}, u32[]{:S(2)}) %collective-permute-start.1) | collective-permute-done | bytes 131104 | tf_op jit(solution)/shard_map/ppermute | solution.py:357
  12.5 0.1 collective-permute-start.2
  12.6 1.6 %collective-permute-start.3 = (bf16[4,64,128]{2,1,0:T(8,128)(2,1)S(1)}, bf16[4,64,128]{2,1,0:T(8,128)(2,1)S(1)}, u32[]{:S(2)}, u32[]{:S(2)}) collective-permute-start(bf16[4,64,128]{2,1,0:T(8,128)(2,1)S(1)} %get-tuple-element.55), channel_id=1, source_target_pairs={{1,2},{3,0},{2,1},{0,3},{5,6},{7,4},{6,5},{4,7},{9,10},{11,8},{10,... | collective-permute-start | bytes 196616 | tf_op jit(solution)/shard_map/ppermute | solution.py:357
  14.2 1.4 %shard_map.77 = (bf16[2,10,192,128]{3,2,1,0:T(8,128)(2,1)S(1)}, f32[2,8,64,128]{3,2,1,0:T(8,128)S(1)}) custom-call(bf16[8,64,128]{2,1,0:T(8,128)(2,1)S(1)} %collective-permute-done.near.near_in, bf16[8,64,128]{2,1,0:T(8,128)(2,1)S(1)} %collective-permute-done.1.far.far_in, bf16[3,3,64,192]{3,2,1,0:T(8,128)(2,1)S(1)} %copy-done.1, ...), custom_call_target="tpu_custom_call" | custom-call | flops 150994944 | bytes 2514944 | tf_op jit(solution)/shard_map/pallas_call | solution.py:20
  15.6 0.0 collective-permute-done.2.near
  15.6 0.9 %collective-permute-done.3.far = bf16[4,64,128]{2,1,0:T(8,128)(2,1)S(1)} collective-permute-done((bf16[4,64,128]{2,1,0:T(8,128)(2,1)S(1)}, bf16[4,64,128]{2,1,0:T(8,128)(2,1)S(1)}, u32[]{:S(2)}, u32[]{:S(2)}) %collective-permute-start.3) | collective-permute-done | bytes 65568 | tf_op jit(solution)/shard_map/ppermute | solution.py:357
  16.5 0.5 %shard_map.79 = (bf16[4,2,192,128]{3,2,1,0:T(8,128)(2,1)S(1)}, bf16[8,64,128]{2,1,0:T(8,128)(2,1)S(1)}, bf16[8,64,128]{2,1,0:T(8,128)(2,1)S(1)}, bf16[2,8,64,128]{3,2,1,0:T(8,128)(2,1)S(1)}) custom-call(bf16[4,64,128]{2,1,0:T(8,128)(2,1)S(1)} %collective-permute-done.2.near, bf16[4,64,128]{2,1,0:T(8,128)(2,1)S(1)} %collective-permute-done.3.far, ...), custom_call_target="tpu_custom_call" | custom-call | flops 45298484 | bytes 2318336 | tf_op jit(solution)/shard_map/pallas_call | solution.py:20
  17.0 2.3 %shard_map.80 = (f32[704,128]{1,0:T(8,128)S(1)}, bf16[704,128]{1,0:T(8,128)(2,1)S(1)}) custom-call(bf16[2,10,192,128]{3,2,1,0:T(8,128)(2,1)S(1)} %get-tuple-element.48.inner, bf16[2,10,192,128]{3,2,1,0:T(8,128)(2,1)S(1)} %get-tuple-element.53.outer, bf16[4,2,192,128]{3,2,1,0:T(8,128)(2,1)S(1)} %get-tuple-element.58.edges, ...), custom_call_target="tpu_custom_call" | custom-call | flops 452984832 | bytes 3489792 | tf_op jit(solution)/shard_map/pallas_call | solution.py:20
  19.4 0.5 collective-permute-start.4
  19.8 0.4 collective-permute-start.6
  20.2 3.6 %collective-permute-start.7 = (bf16[8,64,128]{2,1,0:T(8,128)(2,1)S(1)}, bf16[8,64,128]{2,1,0:T(8,128)(2,1)S(1)}, u32[]{:S(2)}, u32[]{:S(2)}) collective-permute-start(bf16[8,64,128]{2,1,0:T(8,128)(2,1)S(1)} %get-tuple-element.71.far), channel_id=1, source_target_pairs={{4,8},{12,16},{20,24},{28,0},{8,4},{16,12},{24,20},{0,28},{5,9},{1... | collective-permute-start | bytes 393224 | tf_op jit(solution)/shard_map/ppermute | solution.py:357
  23.8 0.0 collective-permute-done.4.other
  23.8 0.1 shard_map.81
  23.8 0.7 %collective-permute-start.5 = (bf16[352,128]{1,0:T(8,128)(2,1)S(1)}, bf16[352,128]{1,0:T(8,128)(2,1)S(1)}, u32[]{:S(2)}, u32[]{:S(2)}) collective-permute-start(bf16[352,128]{1,0:T(8,128)(2,1)S(1)} %get-tuple-element.67), channel_id=1, source_target_pairs={{0,3},{1,2},{2,1},{3,0},{4,7},{5,6},{6,5},{7,4},{8,11},{9,10},{10,... | collective-permute-start | bytes 270344 | tf_op jit(solution)/shard_map/ppermute | solution.py:363
  24.5 4.3 %collective-permute-done.5.other = bf16[352,128]{1,0:T(8,128)(2,1)S(1)} collective-permute-done((bf16[352,128]{1,0:T(8,128)(2,1)S(1)}, bf16[352,128]{1,0:T(8,128)(2,1)S(1)}, u32[]{:S(2)}, u32[]{:S(2)}) %collective-permute-start.5) | collective-permute-done | bytes 90144 | tf_op jit(solution)/shard_map/ppermute | solution.py:363
  28.8 0.0 collective-permute-done.6.near_in
  28.8 0.0 collective-permute-done.7.far_in
  28.9 0.1 collective-permute-start.8
  28.9 3.6 %collective-permute-done.8.y = bf16[176,128]{1,0:T(8,128)(2,1)S(1)} collective-permute-done((bf16[176,128]{1,0:T(8,128)(2,1)S(1)}, bf16[176,128]{1,0:T(8,128)(2,1)S(1)}, u32[]{:S(2)}, u32[]{:S(2)}) %collective-permute-start.8) | collective-permute-done | bytes 45088 | tf_op jit(solution)/shard_map/ppermute | solution.py:363
  32.6 0.1 collective-permute-start.9
  32.7 3.6 %collective-permute-done.9.y = bf16[176,128]{1,0:T(8,128)(2,1)S(1)} collective-permute-done((bf16[176,128]{1,0:T(8,128)(2,1)S(1)}, bf16[176,128]{1,0:T(8,128)(2,1)S(1)}, u32[]{:S(2)}, u32[]{:S(2)}) %collective-permute-start.9) | collective-permute-done | bytes 45088 | tf_op jit(solution)/shard_map/ppermute | solution.py:363
  36.3 0.6 %collective-permute-start.10 = (bf16[176,128]{1,0:T(8,128)(2,1)S(1)}, bf16[176,128]{1,0:T(8,128)(2,1)S(1)}, u32[]{:S(2)}, u32[]{:S(2)}) collective-permute-start(bf16[176,128]{1,0:T(8,128)(2,1)S(1)} %shard_map.84.x), channel_id=1, source_target_pairs={{0,17},{1,16},{2,19},{3,18},{4,21},{5,20},{6,23},{7,22},{8,25},{9,... | collective-permute-start | bytes 135176 | tf_op jit(solution)/shard_map/ppermute | solution.py:363
  37.0 0.3 copy.9
  37.2 1.4 %shard_map.86 = bf16[128,256]{1,0:T(8,128)(2,1)} custom-call(bf16[2,8,64,128]{3,2,1,0:T(8,128)(2,1)S(1)} %get-tuple-element.73.h_ref, bf16[2,2,128,128]{3,2,1,0:T(8,128)(2,1)S(1)} %copy-done.3), custom_call_target="tpu_custom_call" | custom-call | flops 45298484 | bytes 458752 | tf_op jit(solution)/shard_map/pallas_call | solution.py:20
  38.6 0.5 collective-permute-start.12
  39.1 1.2 %collective-permute-start.13 = (bf16[4,64,128]{2,1,0:T(8,128)(2,1)S(1)}, bf16[4,64,128]{2,1,0:T(8,128)(2,1)S(1)}, u32[]{:S(2)}, u32[]{:S(2)}) collective-permute-start(bf16[4,64,128]{2,1,0:T(8,128)(2,1)S(1)} %get-tuple-element.79), channel_id=1, source_target_pairs={{1,2},{3,0},{2,1},{0,3},{5,6},{7,4},{6,5},{4,7},{9,10},{11,8},{10,... | collective-permute-start | bytes 196616 | tf_op jit(solution)/shard_map/ppermute | solution.py:357
  40.3 0.9 %collective-permute-done.10.y = bf16[176,128]{1,0:T(8,128)(2,1)S(1)} collective-permute-done((bf16[176,128]{1,0:T(8,128)(2,1)S(1)}, bf16[176,128]{1,0:T(8,128)(2,1)S(1)}, u32[]{:S(2)}, u32[]{:S(2)}) %collective-permute-start.10) | collective-permute-done | bytes 45088 | tf_op jit(solution)/shard_map/ppermute | solution.py:363
  41.2 0.5 collective-permute-start.11
  41.8 0.3 copy.10
  42.0 0.2 copy.11.w_ref
  42.3 2.3 %shard_map.88.acc_ref = f32[2,8,64,128]{3,2,1,0:T(8,128)S(1)} custom-call(bf16[8,64,128]{2,1,0:T(8,128)(2,1)S(1)} %get-tuple-element.70.near, bf16[8,64,128]{2,1,0:T(8,128)(2,1)S(1)} %get-tuple-element.71.far, bf16[8,64,128]{2,1,0:T(8,128)(2,1)S(1)} %collective-permute-done.6.near_in, bf16[8,64,128]{2,1,0:T(8,128)(2,1)S(1)} %collective-permute-done.7.far_in, ...), custom_call_target="tpu_custom_call" | custom-call | flops 452984832 | bytes 1269760 | tf_op jit(solution)/shard_map/pallas_call | solution.py:20
  44.6 0.4 collective-permute-done.11.other
  45.0 0.0 collective-permute-done.12.near
  45.0 0.0 collective-permute-done.13.far
  45.0 1.0 %collective-permute-start.14 = (bf16[352,128]{1,0:T(8,128)(2,1)S(1)}, bf16[352,128]{1,0:T(8,128)(2,1)S(1)}, u32[]{:S(2)}, u32[]{:S(2)}) collective-permute-start(bf16[352,128]{1,0:T(8,128)(2,1)S(1)} %shard_map.87.mine), channel_id=1, source_target_pairs={{0,3},{1,2},{2,1},{3,0},{4,7},{5,6},{6,5},{7,4},{8,11},{9,10},{10,... | collective-permute-start | bytes 270344 | tf_op jit(solution)/shard_map/ppermute | solution.py:363
  46.0 1.3 %shard_map.91 = f32[1024,128]{1,0:T(8,128)} custom-call(bf16[4,64,128]{2,1,0:T(8,128)(2,1)S(1)} %collective-permute-done.12.near, bf16[4,64,128]{2,1,0:T(8,128)(2,1)S(1)} %collective-permute-done.13.far, f32[2,8,64,128]{3,2,1,0:T(8,128)S(1)} %shard_map.88.acc_ref, bf16[3,3,64,192]{3,2,1,0:T(8,128)(2,1)S(1)} %copy.11.w_ref), custom_call_target="tpu_custom_call" | custom-call | flops 45298484 | bytes 1400832 | tf_op jit(solution)/shard_map/pallas_call | solution.py:20
  47.3 2.3 %collective-permute-done.14.other = bf16[352,128]{1,0:T(8,128)(2,1)S(1)} collective-permute-done((bf16[352,128]{1,0:T(8,128)(2,1)S(1)}, bf16[352,128]{1,0:T(8,128)(2,1)S(1)}, u32[]{:S(2)}, u32[]{:S(2)}) %collective-permute-start.14) | collective-permute-done | bytes 90144 | tf_op jit(solution)/shard_map/ppermute | solution.py:363
  49.7 0.2 collective-permute-start.15
  49.9 1.3 %collective-permute-done.15.other = bf16[704,128]{1,0:T(8,128)(2,1)S(1)} collective-permute-done((bf16[704,128]{1,0:T(8,128)(2,1)S(1)}, bf16[704,128]{1,0:T(8,128)(2,1)S(1)}, u32[]{:S(2)}, u32[]{:S(2)}) %collective-permute-start.15) | collective-permute-done | bytes 180256 | tf_op jit(solution)/shard_map/ppermute | solution.py:363
  51.2 1.0 %shard_map.92 = (f32[3,3,64,192]{3,2,1,0:T(8,128)}, f32[2,2,128,128]{3,2,1,0:T(8,128)}) custom-call(bf16[704,128]{1,0:T(8,128)(2,1)S(1)} %shard_map.90.mine, bf16[704,128]{1,0:T(8,128)(2,1)S(1)} %collective-permute-done.15.other), custom_call_target="tpu_custom_call" | custom-call | bytes 1064960 | tf_op jit(solution)/shard_map/pallas_call | solution.py:20
  (16 shorter events, 0.2 us)
Async XLA Ops:
  0.6 1.0 %copy-start.2 = (bf16[64,2,8,128]{3,2,1,0:T(8,128)(2,1)S(1)}, bf16[64,2,8,128]{3,2,1,0:T(8,128)(2,1)}, u32[]{:S(2)}) copy-start(bf16[64,2,8,128]{3,2,1,0:T(8,128)(2,1)} %f_ref.1) | copy-start | bytes 786436
  1.6 6.8 %copy-start.3 = (bf16[2,2,128,128]{3,2,1,0:T(8,128)(2,1)S(1)}, bf16[2,2,128,128]{3,2,1,0:T(8,128)(2,1)}, u32[]{:S(2)}) copy-start(bf16[2,2,128,128]{3,2,1,0:T(8,128)(2,1)} %d_ref.3) | copy-start | bytes 393220
  1.6 6.8 %copy-start.4 = (bf16[128,1,256]{2,0,1:T(8,128)(2,1)S(1)}, bf16[128,1,256]{2,0,1:T(8,128)(2,1)}, u32[]{:S(2)}) copy-start(bf16[128,1,256]{2,0,1:T(8,128)(2,1)} %param.7) | copy-start | bytes 196612
  1.8 9.5 %collective-permute-start = (bf16[8,64,128]{2,1,0:T(8,128)(2,1)S(1)}, bf16[8,64,128]{2,1,0:T(8,128)(2,1)S(1)}, u32[]{:S(2)}, u32[]{:S(2)}) collective-permute-start(bf16[8,64,128]{2,1,0:T(8,128)(2,1)S(1)} %get-tuple-element.46.near), channel_id=1, source_target_pairs={{0,4},{8,12},{16,20},{24,28},{4,0},{12,8},{20,16},{28,24},{1,5},{9... | collective-permute-start | bytes 393224 | tf_op jit(solution)/shard_map/ppermute | solution.py:357
  4.8 7.7 %collective-permute-start.1 = (bf16[8,64,128]{2,1,0:T(8,128)(2,1)S(1)}, bf16[8,64,128]{2,1,0:T(8,128)(2,1)S(1)}, u32[]{:S(2)}, u32[]{:S(2)}) collective-permute-start(bf16[8,64,128]{2,1,0:T(8,128)(2,1)S(1)} %get-tuple-element.47.far), channel_id=1, source_target_pairs={{4,8},{12,16},{20,24},{28,0},{8,4},{16,12},{24,20},{0,28},{5,9},{1... | collective-permute-start | bytes 393224 | tf_op jit(solution)/shard_map/ppermute | solution.py:357
  8.4 1.0 %copy-start = (bf16[3,3,64,192]{3,2,1,0:T(8,128)(2,1)S(1)}, bf16[3,3,64,192]{3,2,1,0:T(8,128)(2,1)}, u32[]{:S(2)}) copy-start(bf16[3,3,64,192]{3,2,1,0:T(8,128)(2,1)} %w_ref.5) | copy-start | bytes 663556
  11.3 3.0 %copy-start.1 = (bf16[3,3,64,192]{3,2,1,0:T(8,128)(2,1)S(1)}, bf16[3,3,64,192]{3,2,1,0:T(8,128)(2,1)}, u32[]{:S(2)}) copy-start(bf16[3,3,64,192]{3,2,1,0:T(8,128)(2,1)} %w_ref.5) | copy-start | bytes 663556
  12.5 3.1 %collective-permute-start.2 = (bf16[4,64,128]{2,1,0:T(8,128)(2,1)S(1)}, bf16[4,64,128]{2,1,0:T(8,128)(2,1)S(1)}, u32[]{:S(2)}, u32[]{:S(2)}) collective-permute-start(bf16[4,64,128]{2,1,0:T(8,128)(2,1)S(1)} %get-tuple-element.54), channel_id=1, source_target_pairs={{0,1},{2,3},{1,0},{3,2},{4,5},{6,7},{5,4},{7,6},{8,9},{10,11},{9,8... | collective-permute-start | bytes 196616 | tf_op jit(solution)/shard_map/ppermute | solution.py:357
  12.6 3.9 %collective-permute-start.3 = (bf16[4,64,128]{2,1,0:T(8,128)(2,1)S(1)}, bf16[4,64,128]{2,1,0:T(8,128)(2,1)S(1)}, u32[]{:S(2)}, u32[]{:S(2)}) collective-permute-start(bf16[4,64,128]{2,1,0:T(8,128)(2,1)S(1)} %get-tuple-element.55), channel_id=1, source_target_pairs={{1,2},{3,0},{2,1},{0,3},{5,6},{7,4},{6,5},{4,7},{9,10},{11,8},{10,... | collective-permute-start | bytes 196616 | tf_op jit(solution)/shard_map/ppermute | solution.py:357
  19.4 4.4 %collective-permute-start.4 = (bf16[704,128]{1,0:T(8,128)(2,1)S(1)}, bf16[704,128]{1,0:T(8,128)(2,1)S(1)}, u32[]{:S(2)}, u32[]{:S(2)}) collective-permute-start(bf16[704,128]{1,0:T(8,128)(2,1)S(1)} %get-tuple-element.64), channel_id=1, source_target_pairs={{0,1},{1,0},{2,3},{3,2},{4,5},{5,4},{6,7},{7,6},{8,9},{9,8},{10,11... | collective-permute-start | bytes 540680 | tf_op jit(solution)/shard_map/ppermute | solution.py:363
  19.8 9.0 %collective-permute-start.6 = (bf16[8,64,128]{2,1,0:T(8,128)(2,1)S(1)}, bf16[8,64,128]{2,1,0:T(8,128)(2,1)S(1)}, u32[]{:S(2)}, u32[]{:S(2)}) collective-permute-start(bf16[8,64,128]{2,1,0:T(8,128)(2,1)S(1)} %get-tuple-element.70.near), channel_id=1, source_target_pairs={{0,4},{8,12},{16,20},{24,28},{4,0},{12,8},{20,16},{28,24},{1,5},{9... | collective-permute-start | bytes 393224 | tf_op jit(solution)/shard_map/ppermute | solution.py:357
  20.2 8.7 %collective-permute-start.7 = (bf16[8,64,128]{2,1,0:T(8,128)(2,1)S(1)}, bf16[8,64,128]{2,1,0:T(8,128)(2,1)S(1)}, u32[]{:S(2)}, u32[]{:S(2)}) collective-permute-start(bf16[8,64,128]{2,1,0:T(8,128)(2,1)S(1)} %get-tuple-element.71.far), channel_id=1, source_target_pairs={{4,8},{12,16},{20,24},{28,0},{8,4},{16,12},{24,20},{0,28},{5,9},{1... | collective-permute-start | bytes 393224 | tf_op jit(solution)/shard_map/ppermute | solution.py:357
  23.8 5.0 %collective-permute-start.5 = (bf16[352,128]{1,0:T(8,128)(2,1)S(1)}, bf16[352,128]{1,0:T(8,128)(2,1)S(1)}, u32[]{:S(2)}, u32[]{:S(2)}) collective-permute-start(bf16[352,128]{1,0:T(8,128)(2,1)S(1)} %get-tuple-element.67), channel_id=1, source_target_pairs={{0,3},{1,2},{2,1},{3,0},{4,7},{5,6},{6,5},{7,4},{8,11},{9,10},{10,... | collective-permute-start | bytes 270344 | tf_op jit(solution)/shard_map/ppermute | solution.py:363
  28.9 3.7 %collective-permute-start.8 = (bf16[176,128]{1,0:T(8,128)(2,1)S(1)}, bf16[176,128]{1,0:T(8,128)(2,1)S(1)}, u32[]{:S(2)}, u32[]{:S(2)}) collective-permute-start(bf16[176,128]{1,0:T(8,128)(2,1)S(1)} %get-tuple-element.72), channel_id=1, source_target_pairs={{0,9},{1,8},{2,11},{3,10},{4,13},{5,12},{6,15},{7,14},{8,1},{9,0},... | collective-permute-start | bytes 135176 | tf_op jit(solution)/shard_map/ppermute | solution.py:363
  32.6 3.7 %collective-permute-start.9 = (bf16[176,128]{1,0:T(8,128)(2,1)S(1)}, bf16[176,128]{1,0:T(8,128)(2,1)S(1)}, u32[]{:S(2)}, u32[]{:S(2)}) collective-permute-start(bf16[176,128]{1,0:T(8,128)(2,1)S(1)} %shard_map.83.x), channel_id=1, source_target_pairs={{0,5},{1,4},{2,7},{3,6},{4,1},{5,0},{6,3},{7,2},{8,13},{9,12},{10,... | collective-permute-start | bytes 135176 | tf_op jit(solution)/shard_map/ppermute | solution.py:363
  36.3 4.9 %collective-permute-start.10 = (bf16[176,128]{1,0:T(8,128)(2,1)S(1)}, bf16[176,128]{1,0:T(8,128)(2,1)S(1)}, u32[]{:S(2)}, u32[]{:S(2)}) collective-permute-start(bf16[176,128]{1,0:T(8,128)(2,1)S(1)} %shard_map.84.x), channel_id=1, source_target_pairs={{0,17},{1,16},{2,19},{3,18},{4,21},{5,20},{6,23},{7,22},{8,25},{9,... | collective-permute-start | bytes 135176 | tf_op jit(solution)/shard_map/ppermute | solution.py:363
  38.6 6.3 %collective-permute-start.12 = (bf16[4,64,128]{2,1,0:T(8,128)(2,1)S(1)}, bf16[4,64,128]{2,1,0:T(8,128)(2,1)S(1)}, u32[]{:S(2)}, u32[]{:S(2)}) collective-permute-start(bf16[4,64,128]{2,1,0:T(8,128)(2,1)S(1)} %get-tuple-element.78), channel_id=1, source_target_pairs={{0,1},{2,3},{1,0},{3,2},{4,5},{6,7},{5,4},{7,6},{8,9},{10,11},{9,8... | collective-permute-start | bytes 196616 | tf_op jit(solution)/shard_map/ppermute | solution.py:357
  39.1 5.9 %collective-permute-start.13 = (bf16[4,64,128]{2,1,0:T(8,128)(2,1)S(1)}, bf16[4,64,128]{2,1,0:T(8,128)(2,1)S(1)}, u32[]{:S(2)}, u32[]{:S(2)}) collective-permute-start(bf16[4,64,128]{2,1,0:T(8,128)(2,1)S(1)} %get-tuple-element.79), channel_id=1, source_target_pairs={{1,2},{3,0},{2,1},{0,3},{5,6},{7,4},{6,5},{4,7},{9,10},{11,8},{10,... | collective-permute-start | bytes 196616 | tf_op jit(solution)/shard_map/ppermute | solution.py:357
  41.2 3.7 %collective-permute-start.11 = (bf16[176,128]{1,0:T(8,128)(2,1)S(1)}, bf16[176,128]{1,0:T(8,128)(2,1)S(1)}, u32[]{:S(2)}, u32[]{:S(2)}) collective-permute-start(bf16[176,128]{1,0:T(8,128)(2,1)S(1)} %shard_map.85.mine), channel_id=1, source_target_pairs={{0,9},{1,8},{2,11},{3,10},{4,13},{5,12},{6,15},{7,14},{8,1},{9,0},... | collective-permute-start | bytes 135176 | tf_op jit(solution)/shard_map/ppermute | solution.py:363
  45.0 4.7 %collective-permute-start.14 = (bf16[352,128]{1,0:T(8,128)(2,1)S(1)}, bf16[352,128]{1,0:T(8,128)(2,1)S(1)}, u32[]{:S(2)}, u32[]{:S(2)}) collective-permute-start(bf16[352,128]{1,0:T(8,128)(2,1)S(1)} %shard_map.87.mine), channel_id=1, source_target_pairs={{0,3},{1,2},{2,1},{3,0},{4,7},{5,6},{6,5},{7,4},{8,11},{9,10},{10,... | collective-permute-start | bytes 270344 | tf_op jit(solution)/shard_map/ppermute | solution.py:363
  49.7 1.5 %collective-permute-start.15 = (bf16[704,128]{1,0:T(8,128)(2,1)S(1)}, bf16[704,128]{1,0:T(8,128)(2,1)S(1)}, u32[]{:S(2)}, u32[]{:S(2)}) collective-permute-start(bf16[704,128]{1,0:T(8,128)(2,1)S(1)} %shard_map.90.mine), channel_id=1, source_target_pairs={{0,1},{1,0},{2,3},{3,2},{4,5},{5,4},{6,7},{7,6},{8,9},{9,8},{10,11... | collective-permute-start | bytes 540680 | tf_op jit(solution)/shard_map/ppermute | solution.py:363

commit v12 on v11

--- a/solution.py
+++ b/solution.py
@@ -414,9 +414,6 @@
         weight_grad_kernel, [((rows // 2, 128), F32), ((rows // 2, 128), BF16)], [((rows, 128), F32)],
         conv_flops, (inner, outer, edges, *gates, hidden, cot),
     )
-    keep, gates = tied(keep, *gates)
-    near, far = gates
-    near_in, far_in = swap(near, "gz", 0), swap(far, "gz", 1)
     for level, (axis, bit) in enumerate((("gy", 2), ("gz", 2))):
         size = rows >> (level + 2)
         mine, got = keep, flip(send, *(("gy", 1), ("gy", 2))[level])
@@ -425,43 +422,43 @@
             [((size, 128), F32), ((size, 128), BF16)], [((2 * size, 128), F32)], 0, (mine, got),
         )
         if level == 0:
-            keep, (hidden,) = tied(keep, hidden)
+            keep, (hidden, *gates) = tied(keep, hidden, *gates)
             (section_out,) = call(
                 section_kernel, [((out_channels, cot.shape[1]), BF16)], [], conv_flops // 10,
                 (hidden, down_weight),
             )
     shard = ((rows // 8, 128), BF16)
-    send, outside = tied(send, near_in, far_in)
     (sums,) = call(add_kernel, [shard], [], 0, (keep, flip(send, "gz", 2)))
+    sums, (section_out, *gates) = tied(sums, section_out, *gates)
+    outside = swapped(*gates, "gz")
     (sums,) = call(add_kernel, [shard], [], 0, (sums, flip(sums, "gz", 1)))
-    sends = call(edges_kernel, [edge, edge], [], 0, (*gates, *outside))
-    beside = swapped(*sends, "gy")
-    (acc,) = call(
-        field_kernel, [(lines, F32)], [cols, cols], conv_flops, (*gates, *outside, weight_bwd)
-    )
     wide = [("gy", 1 << k) for k in range(2, lax.axis_size("gy").bit_length() - 1)]
     wide += [("gz", 1 << k) for k in range(2, lax.axis_size("gz").bit_length() - 1)]
     for axis, bit in wide:
         (sums,) = call(add_kernel, [shard], [], 0, (sums, flip(sums, axis, bit)))
-    sums, (section_out,) = tied(sums, section_out)
     (sums,) = call(
         functools.partial(join_kernel, axis="gz", bit=2), [((rows // 4, 128), BF16)], [], 0,
         (sums, flip(sums, "gz", 2)),
+    )
+    sums, outside = tied(sums, *outside)
+    beside = swapped(*call(edges_kernel, [edge, edge], [], 0, (*gates, *outside)), "gy")
+    (acc,) = call(
+        field_kernel, [(lines, F32)], [cols, cols], conv_flops, (*gates, *outside, weight_bwd)
+    )
+    (sums,) = call(
+        functools.partial(join_kernel, axis="gy", bit=2), [((rows // 2, 128), BF16)], [], 0,
+        (sums, flip(sums, "gy", 2)),
     )
     sums, (acc, *beside) = tied(sums, acc, *beside)
     (field,) = call(
         field_edges_kernel, [((channels * plane_count * row_count, breadth), F32)], [edge_cols],
         conv_flops // 10, (*beside, acc, weight_bwd),
     )
-    (sums,) = call(
-        functools.partial(join_kernel, axis="gy", bit=2), [((rows // 2, 128), BF16)], [], 0,
-        (sums, flip(sums, "gy", 2)),
-    )
-    sums, (field,) = tied(sums, field)
+    other, (field,) = tied(flip(sums, "gy", 1), field)
     grad_conv, grad_down = call(
         functools.partial(unpack_kernel, scale=grad_scale),
         [(conv_weight.shape, F32), (down_weight.shape, F32)], [((rows, 128), BF16)], 0,
-        (sums, flip(sums, "gy", 1)),
+        (sums, other),
     )
     section_out = section_out.reshape(out_channels, plane_count // 2, -1)
     return (section_out, field.reshape(features.shape), grad_conv, grad_down)

time: 52.4 us -> 52.7 us (level)
  starting transfers between devices: 17.5 us -> 19 us
  waiting for transfers between devices: 18.6 us -> 17.4 us
    ppermute x8, waiting for transfers between devices: 16.4 us -> 13.9 us  [flip(): lax.ppermute(cells, ('gz', 'gy'), [(i, i ^ mask) for i in range(lax.axis_...]
    ppermute x8, waiting for transfers between devices: 2.13 us -> 3.44 us  [swap(): return lax.ppermute(cells, axis, pairs + [(b, a) for a, b in pairs])]
    ppermute x8, starting transfers between devices: 3.67 us -> 4.83 us  [flip(): lax.ppermute(cells, ('gz', 'gy'), [(i, i ^ mask) for i in range(lax.axis_...]
  transfers between devices with their start and end apart: 16 -> 16, of which waited for: 9 -> 8; matrix products, arithmetic and copies ran while one was open for 1% -> 1% of each run, Pallas kernels for 16% -> 16%
where the time goes in v12:
time: 52.7 us; the launch traced here: 52.5 us
  starting transfers between devices  19 us (36%)
  waiting for transfers between devices  17.4 us (33%)
  Pallas kernels  12.6 us (24%)
  local copies, waits for them, and re-layouts  2.7 us (5%)
  between operations  0.81 us (2%)
    ppermute x8, starting transfers between devices, swap(): return lax.ppermute(cells, axis, pairs + [(b, a) for a, b in pairs])  14.2 us
    ppermute x8, waiting for transfers between devices, flip(): lax.ppermute(cells, ('gz', 'gy'), [(i, i ^ mask) for i in range(lax.axis_...  13.9 us
    pallas_call x18, Pallas kernels, call(): pl.pallas_call(kernel, out_shape=[jax.ShapeDtypeStruct(s, d) for s, d in...  12.6 us
    ppermute x8, starting transfers between devices, flip(): lax.ppermute(cells, ('gz', 'gy'), [(i, i ^ mask) for i in range(lax.axis_...  4.83 us
    ppermute x8, waiting for transfers between devices, swap(): return lax.ppermute(cells, axis, pairs + [(b, a) for a, b in pairs])  3.44 us
    unnamed x11, local copies, waits for them, and re-layouts  2.18 us
  transfers between devices with their start and end apart: 16, of which 8 were waited for; matrix products, arithmetic and copies ran while one was open for 1% of the time, Pallas kernels for 16%

profile of v12, /device:TPU:0, one launch (start us, length us, event | category | flops | bytes accessed | tf_op | source)
XLA Modules:
  0.0 52.5 jit_solution(12781402049524394734)
XLA Ops:
  0.6 0.9 %copy-done.2 = bf16[64,2,8,128]{3,2,1,0:T(8,128)(2,1)S(1)} copy-done((bf16[64,2,8,128]{3,2,1,0:T(8,128)(2,1)S(1)}, bf16[64,2,8,128]{3,2,1,0:T(8,128)(2,1)}, u32[]{:S(2)}) %copy-start.2) | copy-done | bytes 262168
  1.6 0.2 shard_map.75
  1.8 3.0 %collective-permute-start = (bf16[8,64,128]{2,1,0:T(8,128)(2,1)S(1)}, bf16[8,64,128]{2,1,0:T(8,128)(2,1)S(1)}, u32[]{:S(2)}, u32[]{:S(2)}) collective-permute-start(bf16[8,64,128]{2,1,0:T(8,128)(2,1)S(1)} %get-tuple-element.47.near), channel_id=1, source_target_pairs={{0,4},{8,12},{16,20},{24,28},{4,0},{12,8},{20,16},{28,24},{1,5},{9... | collective-permute-start | bytes 393224 | tf_op jit(solution)/shard_map/ppermute | solution.py:357
  4.8 3.5 %collective-permute-start.1 = (bf16[8,64,128]{2,1,0:T(8,128)(2,1)S(1)}, bf16[8,64,128]{2,1,0:T(8,128)(2,1)S(1)}, u32[]{:S(2)}, u32[]{:S(2)}) collective-permute-start(bf16[8,64,128]{2,1,0:T(8,128)(2,1)S(1)} %get-tuple-element.48.far), channel_id=1, source_target_pairs={{4,8},{12,16},{20,24},{28,0},{8,4},{16,12},{24,20},{0,28},{5,9},{1... | collective-permute-start | bytes 393224 | tf_op jit(solution)/shard_map/ppermute | solution.py:357
  8.4 1.0 %copy-done = bf16[3,3,64,192]{3,2,1,0:T(8,128)(2,1)S(1)} copy-done((bf16[3,3,64,192]{3,2,1,0:T(8,128)(2,1)S(1)}, bf16[3,3,64,192]{3,2,1,0:T(8,128)(2,1)}, u32[]{:S(2)}) %copy-start) | copy-done | bytes 221208
  9.3 1.9 %shard_map.76 = (bf16[2,10,192,128]{3,2,1,0:T(8,128)(2,1)S(1)}, f32[2,8,64,128]{3,2,1,0:T(8,128)S(1)}, f32[2,8,64,128]{3,2,1,0:T(8,128)S(1)}) custom-call(bf16[8,64,128]{2,1,0:T(8,128)(2,1)S(1)} %get-tuple-element.47.near, bf16[8,64,128]{2,1,0:T(8,128)(2,1)S(1)} %get-tuple-element.48.far, bf16[3,3,64,192]{3,2,1,0:T(8,128)(2,1)S(1)} %copy-done, ...), custom_call_target="tpu_custom_call" | custom-call | flops 301989888 | bytes 2711552 | tf_op jit(solution)/shard_map/pallas_call | solution.py:20
  11.3 0.0 copy-start.1
  11.3 0.0 collective-permute-done.near.near_in
  11.3 1.2 %collective-permute-done.1.far.far_in = bf16[8,64,128]{2,1,0:T(8,128)(2,1)S(1)} collective-permute-done((bf16[8,64,128]{2,1,0:T(8,128)(2,1)S(1)}, bf16[8,64,128]{2,1,0:T(8,128)(2,1)S(1)}, u32[]{:S(2)}, u32[]{:S(2)}) %collective-permute-start.1) | collective-permute-done | bytes 131104 | tf_op jit(solution)/shard_map/ppermute | solution.py:357
  12.5 0.1 collective-permute-start.2
  12.6 1.6 %collective-permute-start.3 = (bf16[4,64,128]{2,1,0:T(8,128)(2,1)S(1)}, bf16[4,64,128]{2,1,0:T(8,128)(2,1)S(1)}, u32[]{:S(2)}, u32[]{:S(2)}) collective-permute-start(bf16[4,64,128]{2,1,0:T(8,128)(2,1)S(1)} %get-tuple-element.56), channel_id=1, source_target_pairs={{1,2},{3,0},{2,1},{0,3},{5,6},{7,4},{6,5},{4,7},{9,10},{11,8},{10,... | collective-permute-start | bytes 196616 | tf_op jit(solution)/shard_map/ppermute | solution.py:357
  14.2 1.4 %shard_map.77 = (bf16[2,10,192,128]{3,2,1,0:T(8,128)(2,1)S(1)}, f32[2,8,64,128]{3,2,1,0:T(8,128)S(1)}) custom-call(bf16[8,64,128]{2,1,0:T(8,128)(2,1)S(1)} %collective-permute-done.near.near_in, bf16[8,64,128]{2,1,0:T(8,128)(2,1)S(1)} %collective-permute-done.1.far.far_in, bf16[3,3,64,192]{3,2,1,0:T(8,128)(2,1)S(1)} %copy-done.1, ...), custom_call_target="tpu_custom_call" | custom-call | flops 150994944 | bytes 2514944 | tf_op jit(solution)/shard_map/pallas_call | solution.py:20
  15.6 0.0 collective-permute-done.2.near
  15.6 0.9 %collective-permute-done.3.far = bf16[4,64,128]{2,1,0:T(8,128)(2,1)S(1)} collective-permute-done((bf16[4,64,128]{2,1,0:T(8,128)(2,1)S(1)}, bf16[4,64,128]{2,1,0:T(8,128)(2,1)S(1)}, u32[]{:S(2)}, u32[]{:S(2)}) %collective-permute-start.3) | collective-permute-done | bytes 65568 | tf_op jit(solution)/shard_map/ppermute | solution.py:357
  16.5 0.5 %shard_map.79 = (bf16[4,2,192,128]{3,2,1,0:T(8,128)(2,1)S(1)}, bf16[8,64,128]{2,1,0:T(8,128)(2,1)S(1)}, bf16[8,64,128]{2,1,0:T(8,128)(2,1)S(1)}, bf16[2,8,64,128]{3,2,1,0:T(8,128)(2,1)S(1)}) custom-call(bf16[4,64,128]{2,1,0:T(8,128)(2,1)S(1)} %collective-permute-done.2.near, bf16[4,64,128]{2,1,0:T(8,128)(2,1)S(1)} %collective-permute-done.3.far, ...), custom_call_target="tpu_custom_call" | custom-call | flops 45298484 | bytes 2318336 | tf_op jit(solution)/shard_map/pallas_call | solution.py:20
  17.0 2.3 %shard_map.80 = (f32[704,128]{1,0:T(8,128)S(1)}, bf16[704,128]{1,0:T(8,128)(2,1)S(1)}) custom-call(bf16[2,10,192,128]{3,2,1,0:T(8,128)(2,1)S(1)} %get-tuple-element.49.inner, bf16[2,10,192,128]{3,2,1,0:T(8,128)(2,1)S(1)} %get-tuple-element.54.outer, bf16[4,2,192,128]{3,2,1,0:T(8,128)(2,1)S(1)} %get-tuple-element.59.edges, ...), custom_call_target="tpu_custom_call" | custom-call | flops 452984832 | bytes 3489792 | tf_op jit(solution)/shard_map/pallas_call | solution.py:20
  19.4 0.5 collective-permute-start.4
  19.8 1.0 %collective-permute-done.4.other = bf16[704,128]{1,0:T(8,128)(2,1)S(1)} collective-permute-done((bf16[704,128]{1,0:T(8,128)(2,1)S(1)}, bf16[704,128]{1,0:T(8,128)(2,1)S(1)}, u32[]{:S(2)}, u32[]{:S(2)}) %collective-permute-start.4) | collective-permute-done | bytes 180256 | tf_op jit(solution)/shard_map/ppermute | solution.py:363
  20.9 0.1 shard_map.81
  20.9 1.5 %collective-permute-start.5 = (bf16[352,128]{1,0:T(8,128)(2,1)S(1)}, bf16[352,128]{1,0:T(8,128)(2,1)S(1)}, u32[]{:S(2)}, u32[]{:S(2)}) collective-permute-start(bf16[352,128]{1,0:T(8,128)(2,1)S(1)} %get-tuple-element.67), channel_id=1, source_target_pairs={{0,3},{1,2},{2,1},{3,0},{4,7},{5,6},{6,5},{7,4},{8,11},{9,10},{10,... | collective-permute-start | bytes 270344 | tf_op jit(solution)/shard_map/ppermute | solution.py:363
  22.5 3.0 %collective-permute-done.5.other = bf16[352,128]{1,0:T(8,128)(2,1)S(1)} collective-permute-done((bf16[352,128]{1,0:T(8,128)(2,1)S(1)}, bf16[352,128]{1,0:T(8,128)(2,1)S(1)}, u32[]{:S(2)}, u32[]{:S(2)}) %collective-permute-start.5) | collective-permute-done | bytes 90144 | tf_op jit(solution)/shard_map/ppermute | solution.py:363
  25.5 0.4 collective-permute-start.6
  25.9 1.4 %shard_map.84 = bf16[128,256]{1,0:T(8,128)(2,1)} custom-call(bf16[2,8,64,128]{3,2,1,0:T(8,128)(2,1)S(1)} %get-tuple-element.70.h_ref, bf16[2,2,128,128]{3,2,1,0:T(8,128)(2,1)S(1)} %copy-done.3), custom_call_target="tpu_custom_call" | custom-call | flops 45298484 | bytes 458752 | tf_op jit(solution)/shard_map/pallas_call | solution.py:20
  27.3 1.8 %collective-permute-done.6.y = bf16[176,128]{1,0:T(8,128)(2,1)S(1)} collective-permute-done((bf16[176,128]{1,0:T(8,128)(2,1)S(1)}, bf16[176,128]{1,0:T(8,128)(2,1)S(1)}, u32[]{:S(2)}, u32[]{:S(2)}) %collective-permute-start.6) | collective-permute-done | bytes 45088 | tf_op jit(solution)/shard_map/ppermute | solution.py:363
  29.1 0.2 collective-permute-start.7
  29.4 1.7 %collective-permute-start.10 = (bf16[8,64,128]{2,1,0:T(8,128)(2,1)S(1)}, bf16[8,64,128]{2,1,0:T(8,128)(2,1)S(1)}, u32[]{:S(2)}, u32[]{:S(2)}) collective-permute-start(bf16[8,64,128]{2,1,0:T(8,128)(2,1)S(1)} %get-tuple-element.75.near), channel_id=1, source_target_pairs={{0,4},{8,12},{16,20},{24,28},{4,0},{12,8},{20,16},{28,24},{1,5},{9... | collective-permute-start | bytes 393224 | tf_op jit(solution)/shard_map/ppermute | solution.py:357
  31.1 3.5 %collective-permute-start.11 = (bf16[8,64,128]{2,1,0:T(8,128)(2,1)S(1)}, bf16[8,64,128]{2,1,0:T(8,128)(2,1)S(1)}, u32[]{:S(2)}, u32[]{:S(2)}) collective-permute-start(bf16[8,64,128]{2,1,0:T(8,128)(2,1)S(1)} %get-tuple-element.76.far), channel_id=1, source_target_pairs={{4,8},{12,16},{20,24},{28,0},{8,4},{16,12},{24,20},{0,28},{5,9},{1... | collective-permute-start | bytes 393224 | tf_op jit(solution)/shard_map/ppermute | solution.py:357
  34.6 0.0 collective-permute-done.7.y
  34.6 0.1 collective-permute-start.8
  34.7 5.2 %collective-permute-done.8.y = bf16[176,128]{1,0:T(8,128)(2,1)S(1)} collective-permute-done((bf16[176,128]{1,0:T(8,128)(2,1)S(1)}, bf16[176,128]{1,0:T(8,128)(2,1)S(1)}, u32[]{:S(2)}, u32[]{:S(2)}) %collective-permute-start.8) | collective-permute-done | bytes 45088 | tf_op jit(solution)/shard_map/ppermute | solution.py:363
  39.9 0.8 %collective-permute-start.9 = (bf16[176,128]{1,0:T(8,128)(2,1)S(1)}, bf16[176,128]{1,0:T(8,128)(2,1)S(1)}, u32[]{:S(2)}, u32[]{:S(2)}) collective-permute-start(bf16[176,128]{1,0:T(8,128)(2,1)S(1)} %shard_map.86.mine), channel_id=1, source_target_pairs={{0,9},{1,8},{2,11},{3,10},{4,13},{5,12},{6,15},{7,14},{8,1},{9,0},... | collective-permute-start | bytes 135176 | tf_op jit(solution)/shard_map/ppermute | solution.py:363
  40.7 0.3 copy.9
  41.0 2.8 %collective-permute-done.9.other = bf16[176,128]{1,0:T(8,128)(2,1)S(1)} collective-permute-done((bf16[176,128]{1,0:T(8,128)(2,1)S(1)}, bf16[176,128]{1,0:T(8,128)(2,1)S(1)}, u32[]{:S(2)}, u32[]{:S(2)}) %collective-permute-start.9) | collective-permute-done | bytes 45088 | tf_op jit(solution)/shard_map/ppermute | solution.py:363
  43.8 0.0 collective-permute-done.10.near_in
  43.8 0.0 collective-permute-done.11.far_in
  43.8 1.3 %collective-permute-start.12 = (bf16[352,128]{1,0:T(8,128)(2,1)S(1)}, bf16[352,128]{1,0:T(8,128)(2,1)S(1)}, u32[]{:S(2)}, u32[]{:S(2)}) collective-permute-start(bf16[352,128]{1,0:T(8,128)(2,1)S(1)} %shard_map.87.mine), channel_id=1, source_target_pairs={{0,3},{1,2},{2,1},{3,0},{4,7},{5,6},{6,5},{7,4},{8,11},{9,10},{10,... | collective-permute-start | bytes 270344 | tf_op jit(solution)/shard_map/ppermute | solution.py:363
  45.1 0.5 collective-permute-start.13
  45.6 0.3 collective-permute-start.14
  45.9 0.3 copy.10
  46.1 0.2 copy.11.w_ref
  46.4 2.3 %shard_map.89.acc_ref = f32[2,8,64,128]{3,2,1,0:T(8,128)S(1)} custom-call(bf16[8,64,128]{2,1,0:T(8,128)(2,1)S(1)} %get-tuple-element.75.near, bf16[8,64,128]{2,1,0:T(8,128)(2,1)S(1)} %get-tuple-element.76.far, bf16[8,64,128]{2,1,0:T(8,128)(2,1)S(1)} %collective-permute-done.10.near_in, bf16[8,64,128]{2,1,0:T(8,128)(2,1)S(1)} %collective-permute-done.11.far_in, ...), custom_call_target="tpu_custom_call" | custom-call | flops 452984832 | bytes 1269760 | tf_op jit(solution)/shard_map/pallas_call | solution.py:20
  48.6 0.0 collective-permute-done.12.other
  48.7 0.0 collective-permute-done.13.near
  48.7 1.3 %collective-permute-done.14.far = bf16[4,64,128]{2,1,0:T(8,128)(2,1)S(1)} collective-permute-done((bf16[4,64,128]{2,1,0:T(8,128)(2,1)S(1)}, bf16[4,64,128]{2,1,0:T(8,128)(2,1)S(1)}, u32[]{:S(2)}, u32[]{:S(2)}) %collective-permute-start.14) | collective-permute-done | bytes 65568 | tf_op jit(solution)/shard_map/ppermute | solution.py:357
  50.0 0.1 collective-permute-start.15
  50.1 1.3 %shard_map.91 = f32[1024,128]{1,0:T(8,128)} custom-call(bf16[4,64,128]{2,1,0:T(8,128)(2,1)S(1)} %collective-permute-done.13.near, bf16[4,64,128]{2,1,0:T(8,128)(2,1)S(1)} %collective-permute-done.14.far, f32[2,8,64,128]{3,2,1,0:T(8,128)S(1)} %shard_map.89.acc_ref, bf16[3,3,64,192]{3,2,1,0:T(8,128)(2,1)S(1)} %copy.11.w_ref), custom_call_target="tpu_custom_call" | custom-call | flops 45298484 | bytes 1400832 | tf_op jit(solution)/shard_map/pallas_call | solution.py:20
  51.5 0.0 collective-permute-done.15.other
  51.5 1.0 %shard_map.92 = (f32[3,3,64,192]{3,2,1,0:T(8,128)}, f32[2,2,128,128]{3,2,1,0:T(8,128)}) custom-call(bf16[704,128]{1,0:T(8,128)(2,1)S(1)} %shard_map.88.mine, bf16[704,128]{1,0:T(8,128)(2,1)S(1)} %collective-permute-done.15.other), custom_call_target="tpu_custom_call" | custom-call | bytes 1064960 | tf_op jit(solution)/shard_map/pallas_call | solution.py:20
  (16 shorter events, 0.2 us)
Async XLA Ops:
  0.6 1.0 %copy-start.2 = (bf16[64,2,8,128]{3,2,1,0:T(8,128)(2,1)S(1)}, bf16[64,2,8,128]{3,2,1,0:T(8,128)(2,1)}, u32[]{:S(2)}) copy-start(bf16[64,2,8,128]{3,2,1,0:T(8,128)(2,1)} %f_ref.1) | copy-start | bytes 786436
  1.6 6.8 %copy-start.3 = (bf16[2,2,128,128]{3,2,1,0:T(8,128)(2,1)S(1)}, bf16[2,2,128,128]{3,2,1,0:T(8,128)(2,1)}, u32[]{:S(2)}) copy-start(bf16[2,2,128,128]{3,2,1,0:T(8,128)(2,1)} %d_ref.3) | copy-start | bytes 393220
  1.6 6.8 %copy-start.4 = (bf16[128,1,256]{2,0,1:T(8,128)(2,1)S(1)}, bf16[128,1,256]{2,0,1:T(8,128)(2,1)}, u32[]{:S(2)}) copy-start(bf16[128,1,256]{2,0,1:T(8,128)(2,1)} %param.7) | copy-start | bytes 196612
  1.8 9.5 %collective-permute-start = (bf16[8,64,128]{2,1,0:T(8,128)(2,1)S(1)}, bf16[8,64,128]{2,1,0:T(8,128)(2,1)S(1)}, u32[]{:S(2)}, u32[]{:S(2)}) collective-permute-start(bf16[8,64,128]{2,1,0:T(8,128)(2,1)S(1)} %get-tuple-element.47.near), channel_id=1, source_target_pairs={{0,4},{8,12},{16,20},{24,28},{4,0},{12,8},{20,16},{28,24},{1,5},{9... | collective-permute-start | bytes 393224 | tf_op jit(solution)/shard_map/ppermute | solution.py:357
  4.8 7.7 %collective-permute-start.1 = (bf16[8,64,128]{2,1,0:T(8,128)(2,1)S(1)}, bf16[8,64,128]{2,1,0:T(8,128)(2,1)S(1)}, u32[]{:S(2)}, u32[]{:S(2)}) collective-permute-start(bf16[8,64,128]{2,1,0:T(8,128)(2,1)S(1)} %get-tuple-element.48.far), channel_id=1, source_target_pairs={{4,8},{12,16},{20,24},{28,0},{8,4},{16,12},{24,20},{0,28},{5,9},{1... | collective-permute-start | bytes 393224 | tf_op jit(solution)/shard_map/ppermute | solution.py:357
  8.4 1.0 %copy-start = (bf16[3,3,64,192]{3,2,1,0:T(8,128)(2,1)S(1)}, bf16[3,3,64,192]{3,2,1,0:T(8,128)(2,1)}, u32[]{:S(2)}) copy-start(bf16[3,3,64,192]{3,2,1,0:T(8,128)(2,1)} %w_ref.5) | copy-start | bytes 663556
  11.3 3.0 %copy-start.1 = (bf16[3,3,64,192]{3,2,1,0:T(8,128)(2,1)S(1)}, bf16[3,3,64,192]{3,2,1,0:T(8,128)(2,1)}, u32[]{:S(2)}) copy-start(bf16[3,3,64,192]{3,2,1,0:T(8,128)(2,1)} %w_ref.5) | copy-start | bytes 663556
  12.5 3.1 %collective-permute-start.2 = (bf16[4,64,128]{2,1,0:T(8,128)(2,1)S(1)}, bf16[4,64,128]{2,1,0:T(8,128)(2,1)S(1)}, u32[]{:S(2)}, u32[]{:S(2)}) collective-permute-start(bf16[4,64,128]{2,1,0:T(8,128)(2,1)S(1)} %get-tuple-element.55), channel_id=1, source_target_pairs={{0,1},{2,3},{1,0},{3,2},{4,5},{6,7},{5,4},{7,6},{8,9},{10,11},{9,8... | collective-permute-start | bytes 196616 | tf_op jit(solution)/shard_map/ppermute | solution.py:357
  12.6 3.9 %collective-permute-start.3 = (bf16[4,64,128]{2,1,0:T(8,128)(2,1)S(1)}, bf16[4,64,128]{2,1,0:T(8,128)(2,1)S(1)}, u32[]{:S(2)}, u32[]{:S(2)}) collective-permute-start(bf16[4,64,128]{2,1,0:T(8,128)(2,1)S(1)} %get-tuple-element.56), channel_id=1, source_target_pairs={{1,2},{3,0},{2,1},{0,3},{5,6},{7,4},{6,5},{4,7},{9,10},{11,8},{10,... | collective-permute-start | bytes 196616 | tf_op jit(solution)/shard_map/ppermute | solution.py:357
  19.4 1.5 %collective-permute-start.4 = (bf16[704,128]{1,0:T(8,128)(2,1)S(1)}, bf16[704,128]{1,0:T(8,128)(2,1)S(1)}, u32[]{:S(2)}, u32[]{:S(2)}) collective-permute-start(bf16[704,128]{1,0:T(8,128)(2,1)S(1)} %get-tuple-element.64), channel_id=1, source_target_pairs={{0,1},{1,0},{2,3},{3,2},{4,5},{5,4},{6,7},{7,6},{8,9},{9,8},{10,11... | collective-permute-start | bytes 540680 | tf_op jit(solution)/shard_map/ppermute | solution.py:363
  20.9 4.5 %collective-permute-start.5 = (bf16[352,128]{1,0:T(8,128)(2,1)S(1)}, bf16[352,128]{1,0:T(8,128)(2,1)S(1)}, u32[]{:S(2)}, u32[]{:S(2)}) collective-permute-start(bf16[352,128]{1,0:T(8,128)(2,1)S(1)} %get-tuple-element.67), channel_id=1, source_target_pairs={{0,3},{1,2},{2,1},{3,0},{4,7},{5,6},{6,5},{7,4},{8,11},{9,10},{10,... | collective-permute-start | bytes 270344 | tf_op jit(solution)/shard_map/ppermute | solution.py:363
  25.5 3.6 %collective-permute-start.6 = (bf16[176,128]{1,0:T(8,128)(2,1)S(1)}, bf16[176,128]{1,0:T(8,128)(2,1)S(1)}, u32[]{:S(2)}, u32[]{:S(2)}) collective-permute-start(bf16[176,128]{1,0:T(8,128)(2,1)S(1)} %get-tuple-element.69), channel_id=1, source_target_pairs={{0,9},{1,8},{2,11},{3,10},{4,13},{5,12},{6,15},{7,14},{8,1},{9,0},... | collective-permute-start | bytes 135176 | tf_op jit(solution)/shard_map/ppermute | solution.py:363
  29.1 5.4 %collective-permute-start.7 = (bf16[176,128]{1,0:T(8,128)(2,1)S(1)}, bf16[176,128]{1,0:T(8,128)(2,1)S(1)}, u32[]{:S(2)}, u32[]{:S(2)}) collective-permute-start(bf16[176,128]{1,0:T(8,128)(2,1)S(1)} %shard_map.83.x), channel_id=1, source_target_pairs={{0,5},{1,4},{2,7},{3,6},{4,1},{5,0},{6,3},{7,2},{8,13},{9,12},{10,... | collective-permute-start | bytes 135176 | tf_op jit(solution)/shard_map/ppermute | solution.py:363
  29.4 14.4 %collective-permute-start.10 = (bf16[8,64,128]{2,1,0:T(8,128)(2,1)S(1)}, bf16[8,64,128]{2,1,0:T(8,128)(2,1)S(1)}, u32[]{:S(2)}, u32[]{:S(2)}) collective-permute-start(bf16[8,64,128]{2,1,0:T(8,128)(2,1)S(1)} %get-tuple-element.75.near), channel_id=1, source_target_pairs={{0,4},{8,12},{16,20},{24,28},{4,0},{12,8},{20,16},{28,24},{1,5},{9... | collective-permute-start | bytes 393224 | tf_op jit(solution)/shard_map/ppermute | solution.py:357
  31.1 12.7 %collective-permute-start.11 = (bf16[8,64,128]{2,1,0:T(8,128)(2,1)S(1)}, bf16[8,64,128]{2,1,0:T(8,128)(2,1)S(1)}, u32[]{:S(2)}, u32[]{:S(2)}) collective-permute-start(bf16[8,64,128]{2,1,0:T(8,128)(2,1)S(1)} %get-tuple-element.76.far), channel_id=1, source_target_pairs={{4,8},{12,16},{20,24},{28,0},{8,4},{16,12},{24,20},{0,28},{5,9},{1... | collective-permute-start | bytes 393224 | tf_op jit(solution)/shard_map/ppermute | solution.py:357
  34.6 5.3 %collective-permute-start.8 = (bf16[176,128]{1,0:T(8,128)(2,1)S(1)}, bf16[176,128]{1,0:T(8,128)(2,1)S(1)}, u32[]{:S(2)}, u32[]{:S(2)}) collective-permute-start(bf16[176,128]{1,0:T(8,128)(2,1)S(1)} %shard_map.85.x), channel_id=1, source_target_pairs={{0,17},{1,16},{2,19},{3,18},{4,21},{5,20},{6,23},{7,22},{8,25},{9,... | collective-permute-start | bytes 135176 | tf_op jit(solution)/shard_map/ppermute | solution.py:363
  39.9 3.8 %collective-permute-start.9 = (bf16[176,128]{1,0:T(8,128)(2,1)S(1)}, bf16[176,128]{1,0:T(8,128)(2,1)S(1)}, u32[]{:S(2)}, u32[]{:S(2)}) collective-permute-start(bf16[176,128]{1,0:T(8,128)(2,1)S(1)} %shard_map.86.mine), channel_id=1, source_target_pairs={{0,9},{1,8},{2,11},{3,10},{4,13},{5,12},{6,15},{7,14},{8,1},{9,0},... | collective-permute-start | bytes 135176 | tf_op jit(solution)/shard_map/ppermute | solution.py:363
  43.8 4.9 %collective-permute-start.12 = (bf16[352,128]{1,0:T(8,128)(2,1)S(1)}, bf16[352,128]{1,0:T(8,128)(2,1)S(1)}, u32[]{:S(2)}, u32[]{:S(2)}) collective-permute-start(bf16[352,128]{1,0:T(8,128)(2,1)S(1)} %shard_map.87.mine), channel_id=1, source_target_pairs={{0,3},{1,2},{2,1},{3,0},{4,7},{5,6},{6,5},{7,4},{8,11},{9,10},{10,... | collective-permute-start | bytes 270344 | tf_op jit(solution)/shard_map/ppermute | solution.py:363
  45.1 3.6 %collective-permute-start.13 = (bf16[4,64,128]{2,1,0:T(8,128)(2,1)S(1)}, bf16[4,64,128]{2,1,0:T(8,128)(2,1)S(1)}, u32[]{:S(2)}, u32[]{:S(2)}) collective-permute-start(bf16[4,64,128]{2,1,0:T(8,128)(2,1)S(1)} %get-tuple-element.80), channel_id=1, source_target_pairs={{0,1},{2,3},{1,0},{3,2},{4,5},{6,7},{5,4},{7,6},{8,9},{10,11},{9,8... | collective-permute-start | bytes 196616 | tf_op jit(solution)/shard_map/ppermute | solution.py:357
  45.6 4.4 %collective-permute-start.14 = (bf16[4,64,128]{2,1,0:T(8,128)(2,1)S(1)}, bf16[4,64,128]{2,1,0:T(8,128)(2,1)S(1)}, u32[]{:S(2)}, u32[]{:S(2)}) collective-permute-start(bf16[4,64,128]{2,1,0:T(8,128)(2,1)S(1)} %get-tuple-element.81), channel_id=1, source_target_pairs={{1,2},{3,0},{2,1},{0,3},{5,6},{7,4},{6,5},{4,7},{9,10},{11,8},{10,... | collective-permute-start | bytes 196616 | tf_op jit(solution)/shard_map/ppermute | solution.py:357
  50.0 1.5 %collective-permute-start.15 = (bf16[704,128]{1,0:T(8,128)(2,1)S(1)}, bf16[704,128]{1,0:T(8,128)(2,1)S(1)}, u32[]{:S(2)}, u32[]{:S(2)}) collective-permute-start(bf16[704,128]{1,0:T(8,128)(2,1)S(1)} %shard_map.88.mine), channel_id=1, source_target_pairs={{0,1},{1,0},{2,3},{3,2},{4,5},{5,4},{6,7},{7,6},{8,9},{9,8},{10,11... | collective-permute-start | bytes 540680 | tf_op jit(solution)/shard_map/ppermute | solution.py:363

commit v13 on v11

--- a/solution.py
+++ b/solution.py
@@ -416,7 +416,7 @@
     )
     keep, gates = tied(keep, *gates)
     near, far = gates
-    near_in, far_in = swap(near, "gz", 0), swap(far, "gz", 1)
+    far_in = swap(far, "gz", 1)
     for level, (axis, bit) in enumerate((("gy", 2), ("gz", 2))):
         size = rows >> (level + 2)
         mine, got = keep, flip(send, *(("gy", 1), ("gy", 2))[level])
@@ -430,10 +430,12 @@
                 section_kernel, [((out_channels, cot.shape[1]), BF16)], [], conv_flops // 10,
                 (hidden, down_weight),
             )
+    keep, (near,) = tied(keep, near)
+    near_in = swap(near, "gz", 0)
     shard = ((rows // 8, 128), BF16)
-    send, outside = tied(send, near_in, far_in)
     (sums,) = call(add_kernel, [shard], [], 0, (keep, flip(send, "gz", 2)))
     (sums,) = call(add_kernel, [shard], [], 0, (sums, flip(sums, "gz", 1)))
+    sums, outside = tied(sums, near_in, far_in)
     sends = call(edges_kernel, [edge, edge], [], 0, (*gates, *outside))
     beside = swapped(*sends, "gy")
     (acc,) = call(

time: 52.4 us -> 51 us (0.973)
  waiting for transfers between devices: 18.6 us -> 11.1 us
  starting transfers between devices: 17.5 us -> 23.5 us
    ppermute x8, waiting for transfers between devices: 16.4 us -> 9.02 us  [flip(): lax.ppermute(cells, ('gz', 'gy'), [(i, i ^ mask) for i in range(lax.axis_...]
    ppermute x8, starting transfers between devices: 3.67 us -> 10.2 us  [flip(): lax.ppermute(cells, ('gz', 'gy'), [(i, i ^ mask) for i in range(lax.axis_...]
  transfers between devices with their start and end apart: 16 -> 16, of which waited for: 9 -> 7; matrix products, arithmetic and copies ran while one was open for 1% -> 2% of each run, Pallas kernels for 16% -> 17%
where the time goes in v13:
time: 51 us; the launch traced here: 50.8 us
  starting transfers between devices  23.5 us (46%)
  Pallas kernels  12.6 us (25%)
  waiting for transfers between devices  11.1 us (22%)
  local copies, waits for them, and re-layouts  2.7 us (5%)
  between operations  0.82 us (2%)
    ppermute x8, starting transfers between devices, swap(): return lax.ppermute(cells, axis, pairs + [(b, a) for a, b in pairs])  13.4 us
    pallas_call x18, Pallas kernels, call(): pl.pallas_call(kernel, out_shape=[jax.ShapeDtypeStruct(s, d) for s, d in...  12.6 us
    ppermute x8, starting transfers between devices, flip(): lax.ppermute(cells, ('gz', 'gy'), [(i, i ^ mask) for i in range(lax.axis_...  10.2 us
    ppermute x8, waiting for transfers between devices, flip(): lax.ppermute(cells, ('gz', 'gy'), [(i, i ^ mask) for i in range(lax.axis_...  9.02 us
    unnamed x11, local copies, waits for them, and re-layouts  2.18 us
    ppermute x8, waiting for transfers between devices, swap(): return lax.ppermute(cells, axis, pairs + [(b, a) for a, b in pairs])  2.13 us
  transfers between devices with their start and end apart: 16, of which 7 were waited for; matrix products, arithmetic and copies ran while one was open for 2% of the time, Pallas kernels for 17%

profile of v13, /device:TPU:0, one launch (start us, length us, event | category | flops | bytes accessed | tf_op | source)
XLA Modules:
  0.0 50.8 jit_solution(14759940224829994306)
XLA Ops:
  0.6 0.9 %copy-done.2 = bf16[64,2,8,128]{3,2,1,0:T(8,128)(2,1)S(1)} copy-done((bf16[64,2,8,128]{3,2,1,0:T(8,128)(2,1)S(1)}, bf16[64,2,8,128]{3,2,1,0:T(8,128)(2,1)}, u32[]{:S(2)}) %copy-start.2) | copy-done | bytes 262168
  1.6 0.2 shard_map.75
  1.8 3.0 %collective-permute-start = (bf16[8,64,128]{2,1,0:T(8,128)(2,1)S(1)}, bf16[8,64,128]{2,1,0:T(8,128)(2,1)S(1)}, u32[]{:S(2)}, u32[]{:S(2)}) collective-permute-start(bf16[8,64,128]{2,1,0:T(8,128)(2,1)S(1)} %get-tuple-element.48.near), channel_id=1, source_target_pairs={{0,4},{8,12},{16,20},{24,28},{4,0},{12,8},{20,16},{28,24},{1,5},{9... | collective-permute-start | bytes 393224 | tf_op jit(solution)/shard_map/ppermute | solution.py:357
  4.8 3.5 %collective-permute-start.1 = (bf16[8,64,128]{2,1,0:T(8,128)(2,1)S(1)}, bf16[8,64,128]{2,1,0:T(8,128)(2,1)S(1)}, u32[]{:S(2)}, u32[]{:S(2)}) collective-permute-start(bf16[8,64,128]{2,1,0:T(8,128)(2,1)S(1)} %get-tuple-element.49.far), channel_id=1, source_target_pairs={{4,8},{12,16},{20,24},{28,0},{8,4},{16,12},{24,20},{0,28},{5,9},{1... | collective-permute-start | bytes 393224 | tf_op jit(solution)/shard_map/ppermute | solution.py:357
  8.4 1.0 %copy-done = bf16[3,3,64,192]{3,2,1,0:T(8,128)(2,1)S(1)} copy-done((bf16[3,3,64,192]{3,2,1,0:T(8,128)(2,1)S(1)}, bf16[3,3,64,192]{3,2,1,0:T(8,128)(2,1)}, u32[]{:S(2)}) %copy-start) | copy-done | bytes 221208
  9.3 1.9 %shard_map.76 = (bf16[2,10,192,128]{3,2,1,0:T(8,128)(2,1)S(1)}, f32[2,8,64,128]{3,2,1,0:T(8,128)S(1)}, f32[2,8,64,128]{3,2,1,0:T(8,128)S(1)}) custom-call(bf16[8,64,128]{2,1,0:T(8,128)(2,1)S(1)} %get-tuple-element.48.near, bf16[8,64,128]{2,1,0:T(8,128)(2,1)S(1)} %get-tuple-element.49.far, bf16[3,3,64,192]{3,2,1,0:T(8,128)(2,1)S(1)} %copy-done, ...), custom_call_target="tpu_custom_call" | custom-call | flops 301989888 | bytes 2711552 | tf_op jit(solution)/shard_map/pallas_call | solution.py:20
  11.3 0.0 copy-start.1
  11.3 0.0 collective-permute-done.near.near_in
  11.3 1.2 %collective-permute-done.1.far.far_in = bf16[8,64,128]{2,1,0:T(8,128)(2,1)S(1)} collective-permute-done((bf16[8,64,128]{2,1,0:T(8,128)(2,1)S(1)}, bf16[8,64,128]{2,1,0:T(8,128)(2,1)S(1)}, u32[]{:S(2)}, u32[]{:S(2)}) %collective-permute-start.1) | collective-permute-done | bytes 131104 | tf_op jit(solution)/shard_map/ppermute | solution.py:357
  12.5 0.1 collective-permute-start.2
  12.6 1.6 %collective-permute-start.3 = (bf16[4,64,128]{2,1,0:T(8,128)(2,1)S(1)}, bf16[4,64,128]{2,1,0:T(8,128)(2,1)S(1)}, u32[]{:S(2)}, u32[]{:S(2)}) collective-permute-start(bf16[4,64,128]{2,1,0:T(8,128)(2,1)S(1)} %get-tuple-element.57), channel_id=1, source_target_pairs={{1,2},{3,0},{2,1},{0,3},{5,6},{7,4},{6,5},{4,7},{9,10},{11,8},{10,... | collective-permute-start | bytes 196616 | tf_op jit(solution)/shard_map/ppermute | solution.py:357
  14.2 1.4 %shard_map.77 = (bf16[2,10,192,128]{3,2,1,0:T(8,128)(2,1)S(1)}, f32[2,8,64,128]{3,2,1,0:T(8,128)S(1)}) custom-call(bf16[8,64,128]{2,1,0:T(8,128)(2,1)S(1)} %collective-permute-done.near.near_in, bf16[8,64,128]{2,1,0:T(8,128)(2,1)S(1)} %collective-permute-done.1.far.far_in, bf16[3,3,64,192]{3,2,1,0:T(8,128)(2,1)S(1)} %copy-done.1, ...), custom_call_target="tpu_custom_call" | custom-call | flops 150994944 | bytes 2514944 | tf_op jit(solution)/shard_map/pallas_call | solution.py:20
  15.6 0.0 collective-permute-done.2.near
  15.6 0.9 %collective-permute-done.3.far = bf16[4,64,128]{2,1,0:T(8,128)(2,1)S(1)} collective-permute-done((bf16[4,64,128]{2,1,0:T(8,128)(2,1)S(1)}, bf16[4,64,128]{2,1,0:T(8,128)(2,1)S(1)}, u32[]{:S(2)}, u32[]{:S(2)}) %collective-permute-start.3) | collective-permute-done | bytes 65568 | tf_op jit(solution)/shard_map/ppermute | solution.py:357
  16.5 0.5 %shard_map.79 = (bf16[4,2,192,128]{3,2,1,0:T(8,128)(2,1)S(1)}, bf16[8,64,128]{2,1,0:T(8,128)(2,1)S(1)}, bf16[8,64,128]{2,1,0:T(8,128)(2,1)S(1)}, bf16[2,8,64,128]{3,2,1,0:T(8,128)(2,1)S(1)}) custom-call(bf16[4,64,128]{2,1,0:T(8,128)(2,1)S(1)} %collective-permute-done.2.near, bf16[4,64,128]{2,1,0:T(8,128)(2,1)S(1)} %collective-permute-done.3.far, ...), custom_call_target="tpu_custom_call" | custom-call | flops 45298484 | bytes 2318336 | tf_op jit(solution)/shard_map/pallas_call | solution.py:20
  17.0 2.3 %shard_map.80 = (f32[704,128]{1,0:T(8,128)S(1)}, bf16[704,128]{1,0:T(8,128)(2,1)S(1)}) custom-call(bf16[2,10,192,128]{3,2,1,0:T(8,128)(2,1)S(1)} %get-tuple-element.50.inner, bf16[2,10,192,128]{3,2,1,0:T(8,128)(2,1)S(1)} %get-tuple-element.55.outer, bf16[4,2,192,128]{3,2,1,0:T(8,128)(2,1)S(1)} %get-tuple-element.60.edges, ...), custom_call_target="tpu_custom_call" | custom-call | flops 452984832 | bytes 3489792 | tf_op jit(solution)/shard_map/pallas_call | solution.py:20
  19.4 0.5 collective-permute-start.4
  19.8 1.0 %collective-permute-done.4.other = bf16[704,128]{1,0:T(8,128)(2,1)S(1)} collective-permute-done((bf16[704,128]{1,0:T(8,128)(2,1)S(1)}, bf16[704,128]{1,0:T(8,128)(2,1)S(1)}, u32[]{:S(2)}, u32[]{:S(2)}) %collective-permute-start.4) | collective-permute-done | bytes 180256 | tf_op jit(solution)/shard_map/ppermute | solution.py:363
  20.9 0.1 shard_map.81
  20.9 1.5 %collective-permute-start.5 = (bf16[352,128]{1,0:T(8,128)(2,1)S(1)}, bf16[352,128]{1,0:T(8,128)(2,1)S(1)}, u32[]{:S(2)}, u32[]{:S(2)}) collective-permute-start(bf16[352,128]{1,0:T(8,128)(2,1)S(1)} %get-tuple-element.69), channel_id=1, source_target_pairs={{0,3},{1,2},{2,1},{3,0},{4,7},{5,6},{6,5},{7,4},{8,11},{9,10},{10,... | collective-permute-start | bytes 270344 | tf_op jit(solution)/shard_map/ppermute | solution.py:363
  22.5 3.5 %collective-permute-start.9 = (bf16[8,64,128]{2,1,0:T(8,128)(2,1)S(1)}, bf16[8,64,128]{2,1,0:T(8,128)(2,1)S(1)}, u32[]{:S(2)}, u32[]{:S(2)}) collective-permute-start(bf16[8,64,128]{2,1,0:T(8,128)(2,1)S(1)} %get-tuple-element.75.far), channel_id=1, source_target_pairs={{4,8},{12,16},{20,24},{28,0},{8,4},{16,12},{24,20},{0,28},{5,9},{1... | collective-permute-start | bytes 393224 | tf_op jit(solution)/shard_map/ppermute | solution.py:357
  26.0 0.0 collective-permute-done.5.other
  26.1 0.1 collective-permute-start.8
  26.1 1.0 %collective-permute-start.6 = (bf16[176,128]{1,0:T(8,128)(2,1)S(1)}, bf16[176,128]{1,0:T(8,128)(2,1)S(1)}, u32[]{:S(2)}, u32[]{:S(2)}) collective-permute-start(bf16[176,128]{1,0:T(8,128)(2,1)S(1)} %get-tuple-element.73), channel_id=1, source_target_pairs={{0,9},{1,8},{2,11},{3,10},{4,13},{5,12},{6,15},{7,14},{8,1},{9,0},... | collective-permute-start | bytes 135176 | tf_op jit(solution)/shard_map/ppermute | solution.py:363
  27.1 2.9 %collective-permute-done.6.y = bf16[176,128]{1,0:T(8,128)(2,1)S(1)} collective-permute-done((bf16[176,128]{1,0:T(8,128)(2,1)S(1)}, bf16[176,128]{1,0:T(8,128)(2,1)S(1)}, u32[]{:S(2)}, u32[]{:S(2)}) %collective-permute-start.6) | collective-permute-done | bytes 45088 | tf_op jit(solution)/shard_map/ppermute | solution.py:363
  30.1 1.9 %collective-permute-start.7 = (bf16[176,128]{1,0:T(8,128)(2,1)S(1)}, bf16[176,128]{1,0:T(8,128)(2,1)S(1)}, u32[]{:S(2)}, u32[]{:S(2)}) collective-permute-start(bf16[176,128]{1,0:T(8,128)(2,1)S(1)} %shard_map.83.x), channel_id=1, source_target_pairs={{0,5},{1,4},{2,7},{3,6},{4,1},{5,0},{6,3},{7,2},{8,13},{9,12},{10,... | collective-permute-start | bytes 135176 | tf_op jit(solution)/shard_map/ppermute | solution.py:363
  32.1 2.0 %collective-permute-done.7.y = bf16[176,128]{1,0:T(8,128)(2,1)S(1)} collective-permute-done((bf16[176,128]{1,0:T(8,128)(2,1)S(1)}, bf16[176,128]{1,0:T(8,128)(2,1)S(1)}, u32[]{:S(2)}, u32[]{:S(2)}) %collective-permute-start.7) | collective-permute-done | bytes 45088 | tf_op jit(solution)/shard_map/ppermute | solution.py:363
  34.1 0.0 collective-permute-done.9.far_in
  34.1 0.0 collective-permute-done.8.near_in
  34.1 2.0 %collective-permute-start.10 = (bf16[176,128]{1,0:T(8,128)(2,1)S(1)}, bf16[176,128]{1,0:T(8,128)(2,1)S(1)}, u32[]{:S(2)}, u32[]{:S(2)}) collective-permute-start(bf16[176,128]{1,0:T(8,128)(2,1)S(1)} %shard_map.84.x), channel_id=1, source_target_pairs={{0,17},{1,16},{2,19},{3,18},{4,21},{5,20},{6,23},{7,22},{8,25},{9,... | collective-permute-start | bytes 135176 | tf_op jit(solution)/shard_map/ppermute | solution.py:363
  36.1 0.3 copy.9
  36.3 1.4 %shard_map.86 = bf16[128,256]{1,0:T(8,128)(2,1)} custom-call(bf16[2,8,64,128]{3,2,1,0:T(8,128)(2,1)S(1)} %get-tuple-element.77.h_ref, bf16[2,2,128,128]{3,2,1,0:T(8,128)(2,1)S(1)} %copy-done.3), custom_call_target="tpu_custom_call" | custom-call | flops 45298484 | bytes 458752 | tf_op jit(solution)/shard_map/pallas_call | solution.py:20
  37.8 0.5 collective-permute-start.12
  38.2 1.0 %collective-permute-start.13 = (bf16[4,64,128]{2,1,0:T(8,128)(2,1)S(1)}, bf16[4,64,128]{2,1,0:T(8,128)(2,1)S(1)}, u32[]{:S(2)}, u32[]{:S(2)}) collective-permute-start(bf16[4,64,128]{2,1,0:T(8,128)(2,1)S(1)} %get-tuple-element.83), channel_id=1, source_target_pairs={{1,2},{3,0},{2,1},{0,3},{5,6},{7,4},{6,5},{4,7},{9,10},{11,8},{10,... | collective-permute-start | bytes 196616 | tf_op jit(solution)/shard_map/ppermute | solution.py:357
  39.2 0.0 collective-permute-done.10.y
  39.2 1.6 %collective-permute-start.11 = (bf16[176,128]{1,0:T(8,128)(2,1)S(1)}, bf16[176,128]{1,0:T(8,128)(2,1)S(1)}, u32[]{:S(2)}, u32[]{:S(2)}) collective-permute-start(bf16[176,128]{1,0:T(8,128)(2,1)S(1)} %shard_map.85.mine), channel_id=1, source_target_pairs={{0,9},{1,8},{2,11},{3,10},{4,13},{5,12},{6,15},{7,14},{8,1},{9,0},... | collective-permute-start | bytes 135176 | tf_op jit(solution)/shard_map/ppermute | solution.py:363
  40.9 0.3 copy.10
  41.1 0.2 copy.11.w_ref
  41.4 2.3 %shard_map.88.acc_ref = f32[2,8,64,128]{3,2,1,0:T(8,128)S(1)} custom-call(bf16[8,64,128]{2,1,0:T(8,128)(2,1)S(1)} %get-tuple-element.74.near, bf16[8,64,128]{2,1,0:T(8,128)(2,1)S(1)} %get-tuple-element.75.far, bf16[8,64,128]{2,1,0:T(8,128)(2,1)S(1)} %collective-permute-done.8.near_in, bf16[8,64,128]{2,1,0:T(8,128)(2,1)S(1)} %collective-permute-done.9.far_in, ...), custom_call_target="tpu_custom_call" | custom-call | flops 452984832 | bytes 1269760 | tf_op jit(solution)/shard_map/pallas_call | solution.py:20
  43.6 0.0 collective-permute-done.11.other
  43.7 0.0 collective-permute-done.12.near
  43.7 0.0 collective-permute-done.13.far
  43.7 1.4 %collective-permute-start.14 = (bf16[352,128]{1,0:T(8,128)(2,1)S(1)}, bf16[352,128]{1,0:T(8,128)(2,1)S(1)}, u32[]{:S(2)}, u32[]{:S(2)}) collective-permute-start(bf16[352,128]{1,0:T(8,128)(2,1)S(1)} %shard_map.87.mine), channel_id=1, source_target_pairs={{0,3},{1,2},{2,1},{3,0},{4,7},{5,6},{6,5},{7,4},{8,11},{9,10},{10,... | collective-permute-start | bytes 270344 | tf_op jit(solution)/shard_map/ppermute | solution.py:363
  45.1 1.3 %shard_map.91 = f32[1024,128]{1,0:T(8,128)} custom-call(bf16[4,64,128]{2,1,0:T(8,128)(2,1)S(1)} %collective-permute-done.12.near, bf16[4,64,128]{2,1,0:T(8,128)(2,1)S(1)} %collective-permute-done.13.far, f32[2,8,64,128]{3,2,1,0:T(8,128)S(1)} %shard_map.88.acc_ref, bf16[3,3,64,192]{3,2,1,0:T(8,128)(2,1)S(1)} %copy.11.w_ref), custom_call_target="tpu_custom_call" | custom-call | flops 45298484 | bytes 1400832 | tf_op jit(solution)/shard_map/pallas_call | solution.py:20
  46.4 1.8 %collective-permute-done.14.other = bf16[352,128]{1,0:T(8,128)(2,1)S(1)} collective-permute-done((bf16[352,128]{1,0:T(8,128)(2,1)S(1)}, bf16[352,128]{1,0:T(8,128)(2,1)S(1)}, u32[]{:S(2)}, u32[]{:S(2)}) %collective-permute-start.14) | collective-permute-done | bytes 90144 | tf_op jit(solution)/shard_map/ppermute | solution.py:363
  48.3 0.3 collective-permute-start.15
  48.6 1.2 %collective-permute-done.15.other = bf16[704,128]{1,0:T(8,128)(2,1)S(1)} collective-permute-done((bf16[704,128]{1,0:T(8,128)(2,1)S(1)}, bf16[704,128]{1,0:T(8,128)(2,1)S(1)}, u32[]{:S(2)}, u32[]{:S(2)}) %collective-permute-start.15) | collective-permute-done | bytes 180256 | tf_op jit(solution)/shard_map/ppermute | solution.py:363
  49.8 1.0 %shard_map.92 = (f32[3,3,64,192]{3,2,1,0:T(8,128)}, f32[2,2,128,128]{3,2,1,0:T(8,128)}) custom-call(bf16[704,128]{1,0:T(8,128)(2,1)S(1)} %shard_map.90.mine, bf16[704,128]{1,0:T(8,128)(2,1)S(1)} %collective-permute-done.15.other), custom_call_target="tpu_custom_call" | custom-call | bytes 1064960 | tf_op jit(solution)/shard_map/pallas_call | solution.py:20
  (16 shorter events, 0.2 us)
Async XLA Ops:
  0.6 1.0 %copy-start.2 = (bf16[64,2,8,128]{3,2,1,0:T(8,128)(2,1)S(1)}, bf16[64,2,8,128]{3,2,1,0:T(8,128)(2,1)}, u32[]{:S(2)}) copy-start(bf16[64,2,8,128]{3,2,1,0:T(8,128)(2,1)} %f_ref.1) | copy-start | bytes 786436
  1.6 6.8 %copy-start.3 = (bf16[2,2,128,128]{3,2,1,0:T(8,128)(2,1)S(1)}, bf16[2,2,128,128]{3,2,1,0:T(8,128)(2,1)}, u32[]{:S(2)}) copy-start(bf16[2,2,128,128]{3,2,1,0:T(8,128)(2,1)} %d_ref.3) | copy-start | bytes 393220
  1.6 6.8 %copy-start.4 = (bf16[128,1,256]{2,0,1:T(8,128)(2,1)S(1)}, bf16[128,1,256]{2,0,1:T(8,128)(2,1)}, u32[]{:S(2)}) copy-start(bf16[128,1,256]{2,0,1:T(8,128)(2,1)} %param.7) | copy-start | bytes 196612
  1.8 9.5 %collective-permute-start = (bf16[8,64,128]{2,1,0:T(8,128)(2,1)S(1)}, bf16[8,64,128]{2,1,0:T(8,128)(2,1)S(1)}, u32[]{:S(2)}, u32[]{:S(2)}) collective-permute-start(bf16[8,64,128]{2,1,0:T(8,128)(2,1)S(1)} %get-tuple-element.48.near), channel_id=1, source_target_pairs={{0,4},{8,12},{16,20},{24,28},{4,0},{12,8},{20,16},{28,24},{1,5},{9... | collective-permute-start | bytes 393224 | tf_op jit(solution)/shard_map/ppermute | solution.py:357
  4.8 7.7 %collective-permute-start.1 = (bf16[8,64,128]{2,1,0:T(8,128)(2,1)S(1)}, bf16[8,64,128]{2,1,0:T(8,128)(2,1)S(1)}, u32[]{:S(2)}, u32[]{:S(2)}) collective-permute-start(bf16[8,64,128]{2,1,0:T(8,128)(2,1)S(1)} %get-tuple-element.49.far), channel_id=1, source_target_pairs={{4,8},{12,16},{20,24},{28,0},{8,4},{16,12},{24,20},{0,28},{5,9},{1... | collective-permute-start | bytes 393224 | tf_op jit(solution)/shard_map/ppermute | solution.py:357
  8.4 1.0 %copy-start = (bf16[3,3,64,192]{3,2,1,0:T(8,128)(2,1)S(1)}, bf16[3,3,64,192]{3,2,1,0:T(8,128)(2,1)}, u32[]{:S(2)}) copy-start(bf16[3,3,64,192]{3,2,1,0:T(8,128)(2,1)} %w_ref.5) | copy-start | bytes 663556
  11.3 3.0 %copy-start.1 = (bf16[3,3,64,192]{3,2,1,0:T(8,128)(2,1)S(1)}, bf16[3,3,64,192]{3,2,1,0:T(8,128)(2,1)}, u32[]{:S(2)}) copy-start(bf16[3,3,64,192]{3,2,1,0:T(8,128)(2,1)} %w_ref.5) | copy-start | bytes 663556
  12.5 3.1 %collective-permute-start.2 = (bf16[4,64,128]{2,1,0:T(8,128)(2,1)S(1)}, bf16[4,64,128]{2,1,0:T(8,128)(2,1)S(1)}, u32[]{:S(2)}, u32[]{:S(2)}) collective-permute-start(bf16[4,64,128]{2,1,0:T(8,128)(2,1)S(1)} %get-tuple-element.56), channel_id=1, source_target_pairs={{0,1},{2,3},{1,0},{3,2},{4,5},{6,7},{5,4},{7,6},{8,9},{10,11},{9,8... | collective-permute-start | bytes 196616 | tf_op jit(solution)/shard_map/ppermute | solution.py:357
  12.6 3.9 %collective-permute-start.3 = (bf16[4,64,128]{2,1,0:T(8,128)(2,1)S(1)}, bf16[4,64,128]{2,1,0:T(8,128)(2,1)S(1)}, u32[]{:S(2)}, u32[]{:S(2)}) collective-permute-start(bf16[4,64,128]{2,1,0:T(8,128)(2,1)S(1)} %get-tuple-element.57), channel_id=1, source_target_pairs={{1,2},{3,0},{2,1},{0,3},{5,6},{7,4},{6,5},{4,7},{9,10},{11,8},{10,... | collective-permute-start | bytes 196616 | tf_op jit(solution)/shard_map/ppermute | solution.py:357
  19.4 1.5 %collective-permute-start.4 = (bf16[704,128]{1,0:T(8,128)(2,1)S(1)}, bf16[704,128]{1,0:T(8,128)(2,1)S(1)}, u32[]{:S(2)}, u32[]{:S(2)}) collective-permute-start(bf16[704,128]{1,0:T(8,128)(2,1)S(1)} %get-tuple-element.66), channel_id=1, source_target_pairs={{0,1},{1,0},{2,3},{3,2},{4,5},{5,4},{6,7},{7,6},{8,9},{9,8},{10,11... | collective-permute-start | bytes 540680 | tf_op jit(solution)/shard_map/ppermute | solution.py:363
  20.9 5.1 %collective-permute-start.5 = (bf16[352,128]{1,0:T(8,128)(2,1)S(1)}, bf16[352,128]{1,0:T(8,128)(2,1)S(1)}, u32[]{:S(2)}, u32[]{:S(2)}) collective-permute-start(bf16[352,128]{1,0:T(8,128)(2,1)S(1)} %get-tuple-element.69), channel_id=1, source_target_pairs={{0,3},{1,2},{2,1},{3,0},{4,7},{5,6},{6,5},{7,4},{8,11},{9,10},{10,... | collective-permute-start | bytes 270344 | tf_op jit(solution)/shard_map/ppermute | solution.py:363
  22.5 11.6 %collective-permute-start.9 = (bf16[8,64,128]{2,1,0:T(8,128)(2,1)S(1)}, bf16[8,64,128]{2,1,0:T(8,128)(2,1)S(1)}, u32[]{:S(2)}, u32[]{:S(2)}) collective-permute-start(bf16[8,64,128]{2,1,0:T(8,128)(2,1)S(1)} %get-tuple-element.75.far), channel_id=1, source_target_pairs={{4,8},{12,16},{20,24},{28,0},{8,4},{16,12},{24,20},{0,28},{5,9},{1... | collective-permute-start | bytes 393224 | tf_op jit(solution)/shard_map/ppermute | solution.py:357
  26.1 8.0 %collective-permute-start.8 = (bf16[8,64,128]{2,1,0:T(8,128)(2,1)S(1)}, bf16[8,64,128]{2,1,0:T(8,128)(2,1)S(1)}, u32[]{:S(2)}, u32[]{:S(2)}) collective-permute-start(bf16[8,64,128]{2,1,0:T(8,128)(2,1)S(1)} %get-tuple-element.74.near), channel_id=1, source_target_pairs={{0,4},{8,12},{16,20},{24,28},{4,0},{12,8},{20,16},{28,24},{1,5},{9... | collective-permute-start | bytes 393224 | tf_op jit(solution)/shard_map/ppermute | solution.py:357
  26.1 4.0 %collective-permute-start.6 = (bf16[176,128]{1,0:T(8,128)(2,1)S(1)}, bf16[176,128]{1,0:T(8,128)(2,1)S(1)}, u32[]{:S(2)}, u32[]{:S(2)}) collective-permute-start(bf16[176,128]{1,0:T(8,128)(2,1)S(1)} %get-tuple-element.73), channel_id=1, source_target_pairs={{0,9},{1,8},{2,11},{3,10},{4,13},{5,12},{6,15},{7,14},{8,1},{9,0},... | collective-permute-start | bytes 135176 | tf_op jit(solution)/shard_map/ppermute | solution.py:363
  30.1 3.9 %collective-permute-start.7 = (bf16[176,128]{1,0:T(8,128)(2,1)S(1)}, bf16[176,128]{1,0:T(8,128)(2,1)S(1)}, u32[]{:S(2)}, u32[]{:S(2)}) collective-permute-start(bf16[176,128]{1,0:T(8,128)(2,1)S(1)} %shard_map.83.x), channel_id=1, source_target_pairs={{0,5},{1,4},{2,7},{3,6},{4,1},{5,0},{6,3},{7,2},{8,13},{9,12},{10,... | collective-permute-start | bytes 135176 | tf_op jit(solution)/shard_map/ppermute | solution.py:363
  34.1 5.1 %collective-permute-start.10 = (bf16[176,128]{1,0:T(8,128)(2,1)S(1)}, bf16[176,128]{1,0:T(8,128)(2,1)S(1)}, u32[]{:S(2)}, u32[]{:S(2)}) collective-permute-start(bf16[176,128]{1,0:T(8,128)(2,1)S(1)} %shard_map.84.x), channel_id=1, source_target_pairs={{0,17},{1,16},{2,19},{3,18},{4,21},{5,20},{6,23},{7,22},{8,25},{9,... | collective-permute-start | bytes 135176 | tf_op jit(solution)/shard_map/ppermute | solution.py:363
  37.8 5.9 %collective-permute-start.12 = (bf16[4,64,128]{2,1,0:T(8,128)(2,1)S(1)}, bf16[4,64,128]{2,1,0:T(8,128)(2,1)S(1)}, u32[]{:S(2)}, u32[]{:S(2)}) collective-permute-start(bf16[4,64,128]{2,1,0:T(8,128)(2,1)S(1)} %get-tuple-element.82), channel_id=1, source_target_pairs={{0,1},{2,3},{1,0},{3,2},{4,5},{6,7},{5,4},{7,6},{8,9},{10,11},{9,8... | collective-permute-start | bytes 196616 | tf_op jit(solution)/shard_map/ppermute | solution.py:357
  38.2 5.5 %collective-permute-start.13 = (bf16[4,64,128]{2,1,0:T(8,128)(2,1)S(1)}, bf16[4,64,128]{2,1,0:T(8,128)(2,1)S(1)}, u32[]{:S(2)}, u32[]{:S(2)}) collective-permute-start(bf16[4,64,128]{2,1,0:T(8,128)(2,1)S(1)} %get-tuple-element.83), channel_id=1, source_target_pairs={{1,2},{3,0},{2,1},{0,3},{5,6},{7,4},{6,5},{4,7},{9,10},{11,8},{10,... | collective-permute-start | bytes 196616 | tf_op jit(solution)/shard_map/ppermute | solution.py:357
  39.2 4.4 %collective-permute-start.11 = (bf16[176,128]{1,0:T(8,128)(2,1)S(1)}, bf16[176,128]{1,0:T(8,128)(2,1)S(1)}, u32[]{:S(2)}, u32[]{:S(2)}) collective-permute-start(bf16[176,128]{1,0:T(8,128)(2,1)S(1)} %shard_map.85.mine), channel_id=1, source_target_pairs={{0,9},{1,8},{2,11},{3,10},{4,13},{5,12},{6,15},{7,14},{8,1},{9,0},... | collective-permute-start | bytes 135176 | tf_op jit(solution)/shard_map/ppermute | solution.py:363
  43.7 4.6 %collective-permute-start.14 = (bf16[352,128]{1,0:T(8,128)(2,1)S(1)}, bf16[352,128]{1,0:T(8,128)(2,1)S(1)}, u32[]{:S(2)}, u32[]{:S(2)}) collective-permute-start(bf16[352,128]{1,0:T(8,128)(2,1)S(1)} %shard_map.87.mine), channel_id=1, source_target_pairs={{0,3},{1,2},{2,1},{3,0},{4,7},{5,6},{6,5},{7,4},{8,11},{9,10},{10,... | collective-permute-start | bytes 270344 | tf_op jit(solution)/shard_map/ppermute | solution.py:363
  48.3 1.5 %collective-permute-start.15 = (bf16[704,128]{1,0:T(8,128)(2,1)S(1)}, bf16[704,128]{1,0:T(8,128)(2,1)S(1)}, u32[]{:S(2)}, u32[]{:S(2)}) collective-permute-start(bf16[704,128]{1,0:T(8,128)(2,1)S(1)} %shard_map.90.mine), channel_id=1, source_target_pairs={{0,1},{1,0},{2,3},{3,2},{4,5},{5,4},{6,7},{7,6},{8,9},{9,8},{10,11... | collective-permute-start | bytes 540680 | tf_op jit(solution)/shard_map/ppermute | solution.py:363

commit v14 on v13

--- a/solution.py
+++ b/solution.py
@@ -36,7 +36,7 @@
     return jnp.where(jnp.broadcast_to(cond, yes.shape), yes, no)
 
 
-def lines_kernel(f_ref, near_ref, far_ref, wide):
+def lines_kernel(f_ref, far_ref, near_ref, wide):
     channels, planes, rows, breadth = f_ref.shape
     wide[...] = f_ref[...].astype(F32).reshape(channels * planes * rows, breadth)
     even = is_even("gz")
@@ -369,7 +369,8 @@
 
 
 def swapped(near, far, axis):
-    return swap(near, axis, 0), swap(far, axis, 1)
+    far = swap(far, axis, 1)
+    return swap(near, axis, 0), far
 
 
 def body(features, conv_weight, down_weight, cotangent):
@@ -387,16 +388,17 @@
     lines = (plane_count, row_count, channels, breadth)
     conv_flops = 2 * 27 * channels * channels * plane_count * row_count * breadth
 
-    own = call(
+    far, near = call(
         lines_kernel, [plane, plane], [((channels * plane_count * row_count, breadth), F32)], 0, (features,)
     )
+    own = (near, far)
     outside = swapped(*own, "gz")
     inner, acc, hidden_grad = call(
         inner_kernel, [cols, (lines, F32), (lines, F32)],
         [((out_channels, row_count // 2 * breadth), BF16)],
         2 * conv_flops // 3, (*own, conv_weight, down_weight, cot),
     )
-    near, far, acc = lax.optimization_barrier((*outside, acc))
+    acc, far, near = lax.optimization_barrier((acc, outside[1], outside[0]))
     outside = (near, far)
     beside = swapped(*call(edges_kernel, [edge, edge], [], 0, (*own, *outside)), "gy")
     outer, acc = call(

time: 51 us -> 52.7 us (1.033)
  waiting for transfers between devices: 11.1 us -> 17.9 us
  starting transfers between devices: 23.5 us -> 18.5 us
    ppermute x8, waiting for transfers between devices: 9.02 us -> 13.6 us  [flip(): lax.ppermute(cells, ('gz', 'gy'), [(i, i ^ mask) for i in range(lax.axis_...]
    ppermute x8, starting transfers between devices: 10.2 us -> 7.16 us  [flip(): lax.ppermute(cells, ('gz', 'gy'), [(i, i ^ mask) for i in range(lax.axis_...]
    ppermute x8, waiting for transfers between devices: 2.13 us -> 4.32 us  [swap(): return lax.ppermute(cells, axis, pairs + [(b, a) for a, b in pairs])]
    ppermute x8, starting transfers between devices: 13.4 us -> 11.3 us  [swap(): return lax.ppermute(cells, axis, pairs + [(b, a) for a, b in pairs])]
  transfers between devices with their start and end apart: 16 -> 16, of which waited for: 7 -> 11; matrix products, arithmetic and copies ran while one was open for 2% -> 1% of each run, Pallas kernels for 17% -> 16%
where the time goes in v14:
time: 52.7 us; the launch traced here: 52.5 us
  starting transfers between devices  18.5 us (35%)
  waiting for transfers between devices  17.9 us (34%)
  Pallas kernels  12.6 us (24%)
  local copies, waits for them, and re-layouts  2.7 us (5%)
  between operations  0.82 us (2%)
    ppermute x8, waiting for transfers between devices, flip(): lax.ppermute(cells, ('gz', 'gy'), [(i, i ^ mask) for i in range(lax.axis_...  13.6 us
    pallas_call x18, Pallas kernels, call(): pl.pallas_call(kernel, out_shape=[jax.ShapeDtypeStruct(s, d) for s, d in...  12.6 us
    ppermute x8, starting transfers between devices, swap(): return lax.ppermute(cells, axis, pairs + [(b, a) for a, b in pairs])  11.3 us
    ppermute x8, starting transfers between devices, flip(): lax.ppermute(cells, ('gz', 'gy'), [(i, i ^ mask) for i in range(lax.axis_...  7.16 us
    ppermute x8, waiting for transfers between devices, swap(): return lax.ppermute(cells, axis, pairs + [(b, a) for a, b in pairs])  4.32 us
    unnamed x11, local copies, waits for them, and re-layouts  2.17 us
  transfers between devices with their start and end apart: 16, of which 11 were waited for; matrix products, arithmetic and copies ran while one was open for 1% of the time, Pallas kernels for 16%

profile of v14, /device:TPU:0, one launch (start us, length us, event | category | flops | bytes accessed | tf_op | source)
XLA Modules:
  0.0 52.5 jit_solution(10233922913866105333)
XLA Ops:
  0.6 0.9 %copy-done.2 = bf16[64,2,8,128]{3,2,1,0:T(8,128)(2,1)S(1)} copy-done((bf16[64,2,8,128]{3,2,1,0:T(8,128)(2,1)S(1)}, bf16[64,2,8,128]{3,2,1,0:T(8,128)(2,1)}, u32[]{:S(2)}) %copy-start.2) | copy-done | bytes 262168
  1.6 0.2 shard_map.75
  1.8 6.1 %collective-permute-start = (bf16[8,64,128]{2,1,0:T(8,128)(2,1)S(1)}, bf16[8,64,128]{2,1,0:T(8,128)(2,1)S(1)}, u32[]{:S(2)}, u32[]{:S(2)}) collective-permute-start(bf16[8,64,128]{2,1,0:T(8,128)(2,1)S(1)} %get-tuple-element.49.far), channel_id=1, source_target_pairs={{4,8},{12,16},{20,24},{28,0},{8,4},{16,12},{24,20},{0,28},{5,9},{1... | collective-permute-start | bytes 393224 | tf_op jit(solution)/shard_map/ppermute | solution.py:357
  7.9 0.0 collective-permute-start.1
  7.9 0.0 copy-start
  7.9 1.0 %copy-done = bf16[3,3,64,192]{3,2,1,0:T(8,128)(2,1)S(1)} copy-done((bf16[3,3,64,192]{3,2,1,0:T(8,128)(2,1)S(1)}, bf16[3,3,64,192]{3,2,1,0:T(8,128)(2,1)}, u32[]{:S(2)}) %copy-start) | copy-done | bytes 221208
  8.8 1.9 %shard_map.76 = (bf16[2,10,192,128]{3,2,1,0:T(8,128)(2,1)S(1)}, f32[2,8,64,128]{3,2,1,0:T(8,128)S(1)}, f32[2,8,64,128]{3,2,1,0:T(8,128)S(1)}) custom-call(bf16[8,64,128]{2,1,0:T(8,128)(2,1)S(1)} %get-tuple-element.48.near, bf16[8,64,128]{2,1,0:T(8,128)(2,1)S(1)} %get-tuple-element.49.far, bf16[3,3,64,192]{3,2,1,0:T(8,128)(2,1)S(1)} %copy-done, ...), custom_call_target="tpu_custom_call" | custom-call | flops 301989888 | bytes 2711552 | tf_op jit(solution)/shard_map/pallas_call | solution.py:20
  10.7 0.0 copy-start.1
  10.8 0.7 %collective-permute-done.far.far_in = bf16[8,64,128]{2,1,0:T(8,128)(2,1)S(1)} collective-permute-done((bf16[8,64,128]{2,1,0:T(8,128)(2,1)S(1)}, bf16[8,64,128]{2,1,0:T(8,128)(2,1)S(1)}, u32[]{:S(2)}, u32[]{:S(2)}) %collective-permute-start) | collective-permute-done | bytes 131104 | tf_op jit(solution)/shard_map/ppermute | solution.py:357
  11.5 2.7 %collective-permute-done.1.near.near_in = bf16[8,64,128]{2,1,0:T(8,128)(2,1)S(1)} collective-permute-done((bf16[8,64,128]{2,1,0:T(8,128)(2,1)S(1)}, bf16[8,64,128]{2,1,0:T(8,128)(2,1)S(1)}, u32[]{:S(2)}, u32[]{:S(2)}) %collective-permute-start.1) | collective-permute-done | bytes 131104 | tf_op jit(solution)/shard_map/ppermute | solution.py:357
  14.2 0.1 collective-permute-start.2
  14.3 1.6 %collective-permute-start.3 = (bf16[4,64,128]{2,1,0:T(8,128)(2,1)S(1)}, bf16[4,64,128]{2,1,0:T(8,128)(2,1)S(1)}, u32[]{:S(2)}, u32[]{:S(2)}) collective-permute-start(bf16[4,64,128]{2,1,0:T(8,128)(2,1)S(1)} %get-tuple-element.57), channel_id=1, source_target_pairs={{1,2},{3,0},{2,1},{0,3},{5,6},{7,4},{6,5},{4,7},{9,10},{11,8},{10,... | collective-permute-start | bytes 196616 | tf_op jit(solution)/shard_map/ppermute | solution.py:357
  15.9 1.4 %shard_map.77 = (bf16[2,10,192,128]{3,2,1,0:T(8,128)(2,1)S(1)}, f32[2,8,64,128]{3,2,1,0:T(8,128)S(1)}) custom-call(bf16[8,64,128]{2,1,0:T(8,128)(2,1)S(1)} %collective-permute-done.1.near.near_in, bf16[8,64,128]{2,1,0:T(8,128)(2,1)S(1)} %collective-permute-done.far.far_in, bf16[3,3,64,192]{3,2,1,0:T(8,128)(2,1)S(1)} %copy-done.1, ...), custom_call_target="tpu_custom_call" | custom-call | flops 150994944 | bytes 2514944 | tf_op jit(solution)/shard_map/pallas_call | solution.py:20
  17.3 0.0 collective-permute-done.2.near
  17.3 0.9 %collective-permute-done.3.far = bf16[4,64,128]{2,1,0:T(8,128)(2,1)S(1)} collective-permute-done((bf16[4,64,128]{2,1,0:T(8,128)(2,1)S(1)}, bf16[4,64,128]{2,1,0:T(8,128)(2,1)S(1)}, u32[]{:S(2)}, u32[]{:S(2)}) %collective-permute-start.3) | collective-permute-done | bytes 65568 | tf_op jit(solution)/shard_map/ppermute | solution.py:357
  18.2 0.5 %shard_map.79 = (bf16[4,2,192,128]{3,2,1,0:T(8,128)(2,1)S(1)}, bf16[8,64,128]{2,1,0:T(8,128)(2,1)S(1)}, bf16[8,64,128]{2,1,0:T(8,128)(2,1)S(1)}, bf16[2,8,64,128]{3,2,1,0:T(8,128)(2,1)S(1)}) custom-call(bf16[4,64,128]{2,1,0:T(8,128)(2,1)S(1)} %collective-permute-done.2.near, bf16[4,64,128]{2,1,0:T(8,128)(2,1)S(1)} %collective-permute-done.3.far, ...), custom_call_target="tpu_custom_call" | custom-call | flops 45298484 | bytes 2318336 | tf_op jit(solution)/shard_map/pallas_call | solution.py:20
  18.7 2.3 %shard_map.80 = (f32[704,128]{1,0:T(8,128)S(1)}, bf16[704,128]{1,0:T(8,128)(2,1)S(1)}) custom-call(bf16[2,10,192,128]{3,2,1,0:T(8,128)(2,1)S(1)} %get-tuple-element.50.inner, bf16[2,10,192,128]{3,2,1,0:T(8,128)(2,1)S(1)} %get-tuple-element.55.outer, bf16[4,2,192,128]{3,2,1,0:T(8,128)(2,1)S(1)} %get-tuple-element.60.edges, ...), custom_call_target="tpu_custom_call" | custom-call | flops 452984832 | bytes 3489792 | tf_op jit(solution)/shard_map/pallas_call | solution.py:20
  21.0 0.5 collective-permute-start.4
  21.5 1.0 %collective-permute-done.4.other = bf16[704,128]{1,0:T(8,128)(2,1)S(1)} collective-permute-done((bf16[704,128]{1,0:T(8,128)(2,1)S(1)}, bf16[704,128]{1,0:T(8,128)(2,1)S(1)}, u32[]{:S(2)}, u32[]{:S(2)}) %collective-permute-start.4) | collective-permute-done | bytes 180256 | tf_op jit(solution)/shard_map/ppermute | solution.py:363
  22.5 0.1 shard_map.81
  22.6 1.5 %collective-permute-start.5 = (bf16[352,128]{1,0:T(8,128)(2,1)S(1)}, bf16[352,128]{1,0:T(8,128)(2,1)S(1)}, u32[]{:S(2)}, u32[]{:S(2)}) collective-permute-start(bf16[352,128]{1,0:T(8,128)(2,1)S(1)} %get-tuple-element.69), channel_id=1, source_target_pairs={{0,3},{1,2},{2,1},{3,0},{4,7},{5,6},{6,5},{7,4},{8,11},{9,10},{10,... | collective-permute-start | bytes 270344 | tf_op jit(solution)/shard_map/ppermute | solution.py:363
  24.1 1.8 %collective-permute-start.9 = (bf16[8,64,128]{2,1,0:T(8,128)(2,1)S(1)}, bf16[8,64,128]{2,1,0:T(8,128)(2,1)S(1)}, u32[]{:S(2)}, u32[]{:S(2)}) collective-permute-start(bf16[8,64,128]{2,1,0:T(8,128)(2,1)S(1)} %get-tuple-element.75.far), channel_id=1, source_target_pairs={{4,8},{12,16},{20,24},{28,0},{8,4},{16,12},{24,20},{0,28},{5,9},{1... | collective-permute-start | bytes 393224 | tf_op jit(solution)/shard_map/ppermute | solution.py:357
  26.0 1.2 %collective-permute-done.5.other = bf16[352,128]{1,0:T(8,128)(2,1)S(1)} collective-permute-done((bf16[352,128]{1,0:T(8,128)(2,1)S(1)}, bf16[352,128]{1,0:T(8,128)(2,1)S(1)}, u32[]{:S(2)}, u32[]{:S(2)}) %collective-permute-start.5) | collective-permute-done | bytes 90144 | tf_op jit(solution)/shard_map/ppermute | solution.py:363
  27.2 0.1 collective-permute-start.8
  27.3 0.8 %collective-permute-start.6 = (bf16[176,128]{1,0:T(8,128)(2,1)S(1)}, bf16[176,128]{1,0:T(8,128)(2,1)S(1)}, u32[]{:S(2)}, u32[]{:S(2)}) collective-permute-start(bf16[176,128]{1,0:T(8,128)(2,1)S(1)} %get-tuple-element.73), channel_id=1, source_target_pairs={{0,9},{1,8},{2,11},{3,10},{4,13},{5,12},{6,15},{7,14},{8,1},{9,0},... | collective-permute-start | bytes 135176 | tf_op jit(solution)/shard_map/ppermute | solution.py:363
  28.0 2.8 %collective-permute-done.6.y = bf16[176,128]{1,0:T(8,128)(2,1)S(1)} collective-permute-done((bf16[176,128]{1,0:T(8,128)(2,1)S(1)}, bf16[176,128]{1,0:T(8,128)(2,1)S(1)}, u32[]{:S(2)}, u32[]{:S(2)}) %collective-permute-start.6) | collective-permute-done | bytes 45088 | tf_op jit(solution)/shard_map/ppermute | solution.py:363
  30.9 2.8 %collective-permute-start.7 = (bf16[176,128]{1,0:T(8,128)(2,1)S(1)}, bf16[176,128]{1,0:T(8,128)(2,1)S(1)}, u32[]{:S(2)}, u32[]{:S(2)}) collective-permute-start(bf16[176,128]{1,0:T(8,128)(2,1)S(1)} %shard_map.83.x), channel_id=1, source_target_pairs={{0,5},{1,4},{2,7},{3,6},{4,1},{5,0},{6,3},{7,2},{8,13},{9,12},{10,... | collective-permute-start | bytes 135176 | tf_op jit(solution)/shard_map/ppermute | solution.py:363
  33.7 2.0 %collective-permute-done.7.y = bf16[176,128]{1,0:T(8,128)(2,1)S(1)} collective-permute-done((bf16[176,128]{1,0:T(8,128)(2,1)S(1)}, bf16[176,128]{1,0:T(8,128)(2,1)S(1)}, u32[]{:S(2)}, u32[]{:S(2)}) %collective-permute-start.7) | collective-permute-done | bytes 45088 | tf_op jit(solution)/shard_map/ppermute | solution.py:363
  35.8 0.0 collective-permute-done.9.far_in
  35.8 0.0 collective-permute-done.8.near_in
  35.8 1.0 %collective-permute-start.10 = (bf16[176,128]{1,0:T(8,128)(2,1)S(1)}, bf16[176,128]{1,0:T(8,128)(2,1)S(1)}, u32[]{:S(2)}, u32[]{:S(2)}) collective-permute-start(bf16[176,128]{1,0:T(8,128)(2,1)S(1)} %shard_map.84.x), channel_id=1, source_target_pairs={{0,17},{1,16},{2,19},{3,18},{4,21},{5,20},{6,23},{7,22},{8,25},{9,... | collective-permute-start | bytes 135176 | tf_op jit(solution)/shard_map/ppermute | solution.py:363
  36.8 0.3 copy.9
  37.0 1.4 %shard_map.86 = bf16[128,256]{1,0:T(8,128)(2,1)} custom-call(bf16[2,8,64,128]{3,2,1,0:T(8,128)(2,1)S(1)} %get-tuple-element.77.h_ref, bf16[2,2,128,128]{3,2,1,0:T(8,128)(2,1)S(1)} %copy-done.3), custom_call_target="tpu_custom_call" | custom-call | flops 45298484 | bytes 458752 | tf_op jit(solution)/shard_map/pallas_call | solution.py:20
  38.5 0.3 collective-permute-start.12
  38.7 1.4 %collective-permute-start.13 = (bf16[4,64,128]{2,1,0:T(8,128)(2,1)S(1)}, bf16[4,64,128]{2,1,0:T(8,128)(2,1)S(1)}, u32[]{:S(2)}, u32[]{:S(2)}) collective-permute-start(bf16[4,64,128]{2,1,0:T(8,128)(2,1)S(1)} %get-tuple-element.83), channel_id=1, source_target_pairs={{1,2},{3,0},{2,1},{0,3},{5,6},{7,4},{6,5},{4,7},{9,10},{11,8},{10,... | collective-permute-start | bytes 196616 | tf_op jit(solution)/shard_map/ppermute | solution.py:357
  40.1 1.4 %collective-permute-done.10.y = bf16[176,128]{1,0:T(8,128)(2,1)S(1)} collective-permute-done((bf16[176,128]{1,0:T(8,128)(2,1)S(1)}, bf16[176,128]{1,0:T(8,128)(2,1)S(1)}, u32[]{:S(2)}, u32[]{:S(2)}) %collective-permute-start.10) | collective-permute-done | bytes 45088 | tf_op jit(solution)/shard_map/ppermute | solution.py:363
  41.5 0.1 collective-permute-start.11
  41.7 0.3 copy.10
  41.9 0.2 copy.11.w_ref
  42.2 2.3 %shard_map.88.acc_ref = f32[2,8,64,128]{3,2,1,0:T(8,128)S(1)} custom-call(bf16[8,64,128]{2,1,0:T(8,128)(2,1)S(1)} %get-tuple-element.74.near, bf16[8,64,128]{2,1,0:T(8,128)(2,1)S(1)} %get-tuple-element.75.far, bf16[8,64,128]{2,1,0:T(8,128)(2,1)S(1)} %collective-permute-done.8.near_in, bf16[8,64,128]{2,1,0:T(8,128)(2,1)S(1)} %collective-permute-done.9.far_in, ...), custom_call_target="tpu_custom_call" | custom-call | flops 452984832 | bytes 1269760 | tf_op jit(solution)/shard_map/pallas_call | solution.py:20
  44.4 0.8 %collective-permute-done.11.other = bf16[176,128]{1,0:T(8,128)(2,1)S(1)} collective-permute-done((bf16[176,128]{1,0:T(8,128)(2,1)S(1)}, bf16[176,128]{1,0:T(8,128)(2,1)S(1)}, u32[]{:S(2)}, u32[]{:S(2)}) %collective-permute-start.11) | collective-permute-done | bytes 45088 | tf_op jit(solution)/shard_map/ppermute | solution.py:363
  45.3 0.0 collective-permute-done.12.near
  45.3 0.3 collective-permute-start.14
  45.6 1.3 %shard_map.91 = f32[1024,128]{1,0:T(8,128)} custom-call(bf16[4,64,128]{2,1,0:T(8,128)(2,1)S(1)} %collective-permute-done.12.near, bf16[4,64,128]{2,1,0:T(8,128)(2,1)S(1)} %collective-permute-done.13.far, f32[2,8,64,128]{3,2,1,0:T(8,128)S(1)} %shard_map.88.acc_ref, bf16[3,3,64,192]{3,2,1,0:T(8,128)(2,1)S(1)} %copy.11.w_ref), custom_call_target="tpu_custom_call" | custom-call | flops 45298484 | bytes 1400832 | tf_op jit(solution)/shard_map/pallas_call | solution.py:20
  47.0 3.0 %collective-permute-done.14.other = bf16[352,128]{1,0:T(8,128)(2,1)S(1)} collective-permute-done((bf16[352,128]{1,0:T(8,128)(2,1)S(1)}, bf16[352,128]{1,0:T(8,128)(2,1)S(1)}, u32[]{:S(2)}, u32[]{:S(2)}) %collective-permute-start.14) | collective-permute-done | bytes 90144 | tf_op jit(solution)/shard_map/ppermute | solution.py:363
  50.0 0.2 collective-permute-start.15
  50.2 1.3 %collective-permute-done.15.other = bf16[704,128]{1,0:T(8,128)(2,1)S(1)} collective-permute-done((bf16[704,128]{1,0:T(8,128)(2,1)S(1)}, bf16[704,128]{1,0:T(8,128)(2,1)S(1)}, u32[]{:S(2)}, u32[]{:S(2)}) %collective-permute-start.15) | collective-permute-done | bytes 180256 | tf_op jit(solution)/shard_map/ppermute | solution.py:363
  51.5 1.0 %shard_map.92 = (f32[3,3,64,192]{3,2,1,0:T(8,128)}, f32[2,2,128,128]{3,2,1,0:T(8,128)}) custom-call(bf16[704,128]{1,0:T(8,128)(2,1)S(1)} %shard_map.90.mine, bf16[704,128]{1,0:T(8,128)(2,1)S(1)} %collective-permute-done.15.other), custom_call_target="tpu_custom_call" | custom-call | bytes 1064960 | tf_op jit(solution)/shard_map/pallas_call | solution.py:20
  (16 shorter events, 0.2 us)
Async XLA Ops:
  0.6 1.0 %copy-start.2 = (bf16[64,2,8,128]{3,2,1,0:T(8,128)(2,1)S(1)}, bf16[64,2,8,128]{3,2,1,0:T(8,128)(2,1)}, u32[]{:S(2)}) copy-start(bf16[64,2,8,128]{3,2,1,0:T(8,128)(2,1)} %f_ref.1) | copy-start | bytes 786436
  1.6 6.3 %copy-start.3 = (bf16[2,2,128,128]{3,2,1,0:T(8,128)(2,1)S(1)}, bf16[2,2,128,128]{3,2,1,0:T(8,128)(2,1)}, u32[]{:S(2)}) copy-start(bf16[2,2,128,128]{3,2,1,0:T(8,128)(2,1)} %d_ref.3) | copy-start | bytes 393220
  1.6 6.3 %copy-start.4 = (bf16[128,1,256]{2,0,1:T(8,128)(2,1)S(1)}, bf16[128,1,256]{2,0,1:T(8,128)(2,1)}, u32[]{:S(2)}) copy-start(bf16[128,1,256]{2,0,1:T(8,128)(2,1)} %param.7) | copy-start | bytes 196612
  1.8 9.7 %collective-permute-start = (bf16[8,64,128]{2,1,0:T(8,128)(2,1)S(1)}, bf16[8,64,128]{2,1,0:T(8,128)(2,1)S(1)}, u32[]{:S(2)}, u32[]{:S(2)}) collective-permute-start(bf16[8,64,128]{2,1,0:T(8,128)(2,1)S(1)} %get-tuple-element.49.far), channel_id=1, source_target_pairs={{4,8},{12,16},{20,24},{28,0},{8,4},{16,12},{24,20},{0,28},{5,9},{1... | collective-permute-start | bytes 393224 | tf_op jit(solution)/shard_map/ppermute | solution.py:357
  7.9 6.3 %collective-permute-start.1 = (bf16[8,64,128]{2,1,0:T(8,128)(2,1)S(1)}, bf16[8,64,128]{2,1,0:T(8,128)(2,1)S(1)}, u32[]{:S(2)}, u32[]{:S(2)}) collective-permute-start(bf16[8,64,128]{2,1,0:T(8,128)(2,1)S(1)} %get-tuple-element.48.near), channel_id=1, source_target_pairs={{0,4},{8,12},{16,20},{24,28},{4,0},{12,8},{20,16},{28,24},{1,5},{9... | collective-permute-start | bytes 393224 | tf_op jit(solution)/shard_map/ppermute | solution.py:357
  7.9 1.0 %copy-start = (bf16[3,3,64,192]{3,2,1,0:T(8,128)(2,1)S(1)}, bf16[3,3,64,192]{3,2,1,0:T(8,128)(2,1)}, u32[]{:S(2)}) copy-start(bf16[3,3,64,192]{3,2,1,0:T(8,128)(2,1)} %w_ref.5) | copy-start | bytes 663556
  10.7 5.2 %copy-start.1 = (bf16[3,3,64,192]{3,2,1,0:T(8,128)(2,1)S(1)}, bf16[3,3,64,192]{3,2,1,0:T(8,128)(2,1)}, u32[]{:S(2)}) copy-start(bf16[3,3,64,192]{3,2,1,0:T(8,128)(2,1)} %w_ref.5) | copy-start | bytes 663556
  14.2 3.1 %collective-permute-start.2 = (bf16[4,64,128]{2,1,0:T(8,128)(2,1)S(1)}, bf16[4,64,128]{2,1,0:T(8,128)(2,1)S(1)}, u32[]{:S(2)}, u32[]{:S(2)}) collective-permute-start(bf16[4,64,128]{2,1,0:T(8,128)(2,1)S(1)} %get-tuple-element.56), channel_id=1, source_target_pairs={{0,1},{2,3},{1,0},{3,2},{4,5},{6,7},{5,4},{7,6},{8,9},{10,11},{9,8... | collective-permute-start | bytes 196616 | tf_op jit(solution)/shard_map/ppermute | solution.py:357
  14.3 3.9 %collective-permute-start.3 = (bf16[4,64,128]{2,1,0:T(8,128)(2,1)S(1)}, bf16[4,64,128]{2,1,0:T(8,128)(2,1)S(1)}, u32[]{:S(2)}, u32[]{:S(2)}) collective-permute-start(bf16[4,64,128]{2,1,0:T(8,128)(2,1)S(1)} %get-tuple-element.57), channel_id=1, source_target_pairs={{1,2},{3,0},{2,1},{0,3},{5,6},{7,4},{6,5},{4,7},{9,10},{11,8},{10,... | collective-permute-start | bytes 196616 | tf_op jit(solution)/shard_map/ppermute | solution.py:357
  21.0 1.5 %collective-permute-start.4 = (bf16[704,128]{1,0:T(8,128)(2,1)S(1)}, bf16[704,128]{1,0:T(8,128)(2,1)S(1)}, u32[]{:S(2)}, u32[]{:S(2)}) collective-permute-start(bf16[704,128]{1,0:T(8,128)(2,1)S(1)} %get-tuple-element.66), channel_id=1, source_target_pairs={{0,1},{1,0},{2,3},{3,2},{4,5},{5,4},{6,7},{7,6},{8,9},{9,8},{10,11... | collective-permute-start | bytes 540680 | tf_op jit(solution)/shard_map/ppermute | solution.py:363
  22.6 4.5 %collective-permute-start.5 = (bf16[352,128]{1,0:T(8,128)(2,1)S(1)}, bf16[352,128]{1,0:T(8,128)(2,1)S(1)}, u32[]{:S(2)}, u32[]{:S(2)}) collective-permute-start(bf16[352,128]{1,0:T(8,128)(2,1)S(1)} %get-tuple-element.69), channel_id=1, source_target_pairs={{0,3},{1,2},{2,1},{3,0},{4,7},{5,6},{6,5},{7,4},{8,11},{9,10},{10,... | collective-permute-start | bytes 270344 | tf_op jit(solution)/shard_map/ppermute | solution.py:363
  24.1 11.6 %collective-permute-start.9 = (bf16[8,64,128]{2,1,0:T(8,128)(2,1)S(1)}, bf16[8,64,128]{2,1,0:T(8,128)(2,1)S(1)}, u32[]{:S(2)}, u32[]{:S(2)}) collective-permute-start(bf16[8,64,128]{2,1,0:T(8,128)(2,1)S(1)} %get-tuple-element.75.far), channel_id=1, source_target_pairs={{4,8},{12,16},{20,24},{28,0},{8,4},{16,12},{24,20},{0,28},{5,9},{1... | collective-permute-start | bytes 393224 | tf_op jit(solution)/shard_map/ppermute | solution.py:357
  27.2 8.6 %collective-permute-start.8 = (bf16[8,64,128]{2,1,0:T(8,128)(2,1)S(1)}, bf16[8,64,128]{2,1,0:T(8,128)(2,1)S(1)}, u32[]{:S(2)}, u32[]{:S(2)}) collective-permute-start(bf16[8,64,128]{2,1,0:T(8,128)(2,1)S(1)} %get-tuple-element.74.near), channel_id=1, source_target_pairs={{0,4},{8,12},{16,20},{24,28},{4,0},{12,8},{20,16},{28,24},{1,5},{9... | collective-permute-start | bytes 393224 | tf_op jit(solution)/shard_map/ppermute | solution.py:357
  27.3 3.6 %collective-permute-start.6 = (bf16[176,128]{1,0:T(8,128)(2,1)S(1)}, bf16[176,128]{1,0:T(8,128)(2,1)S(1)}, u32[]{:S(2)}, u32[]{:S(2)}) collective-permute-start(bf16[176,128]{1,0:T(8,128)(2,1)S(1)} %get-tuple-element.73), channel_id=1, source_target_pairs={{0,9},{1,8},{2,11},{3,10},{4,13},{5,12},{6,15},{7,14},{8,1},{9,0},... | collective-permute-start | bytes 135176 | tf_op jit(solution)/shard_map/ppermute | solution.py:363
  30.9 4.9 %collective-permute-start.7 = (bf16[176,128]{1,0:T(8,128)(2,1)S(1)}, bf16[176,128]{1,0:T(8,128)(2,1)S(1)}, u32[]{:S(2)}, u32[]{:S(2)}) collective-permute-start(bf16[176,128]{1,0:T(8,128)(2,1)S(1)} %shard_map.83.x), channel_id=1, source_target_pairs={{0,5},{1,4},{2,7},{3,6},{4,1},{5,0},{6,3},{7,2},{8,13},{9,12},{10,... | collective-permute-start | bytes 135176 | tf_op jit(solution)/shard_map/ppermute | solution.py:363
  35.8 5.7 %collective-permute-start.10 = (bf16[176,128]{1,0:T(8,128)(2,1)S(1)}, bf16[176,128]{1,0:T(8,128)(2,1)S(1)}, u32[]{:S(2)}, u32[]{:S(2)}) collective-permute-start(bf16[176,128]{1,0:T(8,128)(2,1)S(1)} %shard_map.84.x), channel_id=1, source_target_pairs={{0,17},{1,16},{2,19},{3,18},{4,21},{5,20},{6,23},{7,22},{8,25},{9,... | collective-permute-start | bytes 135176 | tf_op jit(solution)/shard_map/ppermute | solution.py:363
  38.5 6.8 %collective-permute-start.12 = (bf16[4,64,128]{2,1,0:T(8,128)(2,1)S(1)}, bf16[4,64,128]{2,1,0:T(8,128)(2,1)S(1)}, u32[]{:S(2)}, u32[]{:S(2)}) collective-permute-start(bf16[4,64,128]{2,1,0:T(8,128)(2,1)S(1)} %get-tuple-element.82), channel_id=1, source_target_pairs={{0,1},{2,3},{1,0},{3,2},{4,5},{6,7},{5,4},{7,6},{8,9},{10,11},{9,8... | collective-permute-start | bytes 196616 | tf_op jit(solution)/shard_map/ppermute | solution.py:357
  38.7 6.6 %collective-permute-start.13 = (bf16[4,64,128]{2,1,0:T(8,128)(2,1)S(1)}, bf16[4,64,128]{2,1,0:T(8,128)(2,1)S(1)}, u32[]{:S(2)}, u32[]{:S(2)}) collective-permute-start(bf16[4,64,128]{2,1,0:T(8,128)(2,1)S(1)} %get-tuple-element.83), channel_id=1, source_target_pairs={{1,2},{3,0},{2,1},{0,3},{5,6},{7,4},{6,5},{4,7},{9,10},{11,8},{10,... | collective-permute-start | bytes 196616 | tf_op jit(solution)/shard_map/ppermute | solution.py:357
  41.5 3.7 %collective-permute-start.11 = (bf16[176,128]{1,0:T(8,128)(2,1)S(1)}, bf16[176,128]{1,0:T(8,128)(2,1)S(1)}, u32[]{:S(2)}, u32[]{:S(2)}) collective-permute-start(bf16[176,128]{1,0:T(8,128)(2,1)S(1)} %shard_map.85.mine), channel_id=1, source_target_pairs={{0,9},{1,8},{2,11},{3,10},{4,13},{5,12},{6,15},{7,14},{8,1},{9,0},... | collective-permute-start | bytes 135176 | tf_op jit(solution)/shard_map/ppermute | solution.py:363
  45.3 4.7 %collective-permute-start.14 = (bf16[352,128]{1,0:T(8,128)(2,1)S(1)}, bf16[352,128]{1,0:T(8,128)(2,1)S(1)}, u32[]{:S(2)}, u32[]{:S(2)}) collective-permute-start(bf16[352,128]{1,0:T(8,128)(2,1)S(1)} %shard_map.87.mine), channel_id=1, source_target_pairs={{0,3},{1,2},{2,1},{3,0},{4,7},{5,6},{6,5},{7,4},{8,11},{9,10},{10,... | collective-permute-start | bytes 270344 | tf_op jit(solution)/shard_map/ppermute | solution.py:363
  50.0 1.5 %collective-permute-start.15 = (bf16[704,128]{1,0:T(8,128)(2,1)S(1)}, bf16[704,128]{1,0:T(8,128)(2,1)S(1)}, u32[]{:S(2)}, u32[]{:S(2)}) collective-permute-start(bf16[704,128]{1,0:T(8,128)(2,1)S(1)} %shard_map.90.mine), channel_id=1, source_target_pairs={{0,1},{1,0},{2,3},{3,2},{4,5},{5,4},{6,7},{7,6},{8,9},{9,8},{10,11... | collective-permute-start | bytes 540680 | tf_op jit(solution)/shard_map/ppermute | solution.py:363

commit v15 on v13

--- a/solution.py
+++ b/solution.py
@@ -417,7 +417,7 @@
     keep, gates = tied(keep, *gates)
     near, far = gates
     far_in = swap(far, "gz", 1)
-    for level, (axis, bit) in enumerate((("gy", 2), ("gz", 2))):
+    for level, (axis, bit) in enumerate((("gy", 2), ("gz", 1))):
         size = rows >> (level + 2)
         mine, got = keep, flip(send, *(("gy", 1), ("gy", 2))[level])
         keep, send = call(
@@ -430,25 +430,23 @@
                 section_kernel, [((out_channels, cot.shape[1]), BF16)], [], conv_flops // 10,
                 (hidden, down_weight),
             )
-    keep, (near,) = tied(keep, near)
-    near_in = swap(near, "gz", 0)
     shard = ((rows // 8, 128), BF16)
-    (sums,) = call(add_kernel, [shard], [], 0, (keep, flip(send, "gz", 2)))
-    (sums,) = call(add_kernel, [shard], [], 0, (sums, flip(sums, "gz", 1)))
-    sums, outside = tied(sums, near_in, far_in)
+    (sums,) = call(add_kernel, [shard], [], 0, (keep, flip(send, "gz", 1)))
+    sums, (near, far_in) = tied(sums, near, far_in)
+    outside = (swap(near, "gz", 0), far_in)
     sends = call(edges_kernel, [edge, edge], [], 0, (*gates, *outside))
     beside = swapped(*sends, "gy")
     (acc,) = call(
         field_kernel, [(lines, F32)], [cols, cols], conv_flops, (*gates, *outside, weight_bwd)
     )
     wide = [("gy", 1 << k) for k in range(2, lax.axis_size("gy").bit_length() - 1)]
-    wide += [("gz", 1 << k) for k in range(2, lax.axis_size("gz").bit_length() - 1)]
+    wide += [("gz", 1 << k) for k in range(1, lax.axis_size("gz").bit_length() - 1)]
     for axis, bit in wide:
         (sums,) = call(add_kernel, [shard], [], 0, (sums, flip(sums, axis, bit)))
     sums, (section_out,) = tied(sums, section_out)
     (sums,) = call(
-        functools.partial(join_kernel, axis="gz", bit=2), [((rows // 4, 128), BF16)], [], 0,
-        (sums, flip(sums, "gz", 2)),
+        functools.partial(join_kernel, axis="gz", bit=1), [((rows // 4, 128), BF16)], [], 0,
+        (sums, flip(sums, "gz", 1)),
     )
     sums, (acc, *beside) = tied(sums, acc, *beside)
     (field,) = call(

time: 51 us -> 54.5 us (1.069)
  waiting for transfers between devices: 11.1 us -> 17.6 us
  starting transfers between devices: 23.5 us -> 20.6 us
    ppermute x8, waiting for transfers between devices: 9.02 us -> 14.6 us  [flip(): lax.ppermute(cells, ('gz', 'gy'), [(i, i ^ mask) for i in range(lax.axis_...]
    ppermute x8, starting transfers between devices: 10.2 us -> 7.86 us  [flip(): lax.ppermute(cells, ('gz', 'gy'), [(i, i ^ mask) for i in range(lax.axis_...]
    ppermute x8, waiting for transfers between devices: 2.13 us -> 3 us  [swap(): return lax.ppermute(cells, axis, pairs + [(b, a) for a, b in pairs])]
    ppermute x8, starting transfers between devices: 13.4 us -> 12.7 us  [swap(): return lax.ppermute(cells, axis, pairs + [(b, a) for a, b in pairs])]
  transfers between devices with their start and end apart: 16 -> 16, of which waited for: 7 -> 9; matrix products, arithmetic and copies ran while one was open for 2% -> 1% of each run, Pallas kernels for 17% -> 15%
where the time goes in v15:
time: 54.5 us; the launch traced here: 54.3 us
  starting transfers between devices  20.6 us (38%)
  waiting for transfers between devices  17.6 us (32%)
  Pallas kernels  12.6 us (23%)
  local copies, waits for them, and re-layouts  2.7 us (5%)
  between operations  0.83 us (2%)
    ppermute x8, waiting for transfers between devices, flip(): lax.ppermute(cells, ('gz', 'gy'), [(i, i ^ mask) for i in range(lax.axis_...  14.6 us
    ppermute x8, starting transfers between devices, swap(): return lax.ppermute(cells, axis, pairs + [(b, a) for a, b in pairs])  12.7 us
    pallas_call x18, Pallas kernels, call(): pl.pallas_call(kernel, out_shape=[jax.ShapeDtypeStruct(s, d) for s, d in...  12.6 us
    ppermute x8, starting transfers between devices, flip(): lax.ppermute(cells, ('gz', 'gy'), [(i, i ^ mask) for i in range(lax.axis_...  7.86 us
    ppermute x8, waiting for transfers between devices, swap(): return lax.ppermute(cells, axis, pairs + [(b, a) for a, b in pairs])  3 us
    unnamed x11, local copies, waits for them, and re-layouts  2.18 us
  transfers between devices with their start and end apart: 16, of which 9 were waited for; matrix products, arithmetic and copies ran while one was open for 1% of the time, Pallas kernels for 15%

profile of v15, /device:TPU:0, one launch (start us, length us, event | category | flops | bytes accessed | tf_op | source)
XLA Modules:
  0.0 54.3 jit_solution(8936776925944524549)
XLA Ops:
  0.6 0.9 %copy-done.2 = bf16[64,2,8,128]{3,2,1,0:T(8,128)(2,1)S(1)} copy-done((bf16[64,2,8,128]{3,2,1,0:T(8,128)(2,1)S(1)}, bf16[64,2,8,128]{3,2,1,0:T(8,128)(2,1)}, u32[]{:S(2)}) %copy-start.2) | copy-done | bytes 262168
  1.6 0.2 shard_map.75
  1.8 3.0 %collective-permute-start = (bf16[8,64,128]{2,1,0:T(8,128)(2,1)S(1)}, bf16[8,64,128]{2,1,0:T(8,128)(2,1)S(1)}, u32[]{:S(2)}, u32[]{:S(2)}) collective-permute-start(bf16[8,64,128]{2,1,0:T(8,128)(2,1)S(1)} %get-tuple-element.46.near), channel_id=1, source_target_pairs={{0,4},{8,12},{16,20},{24,28},{4,0},{12,8},{20,16},{28,24},{1,5},{9... | collective-permute-start | bytes 393224 | tf_op jit(solution)/shard_map/ppermute | solution.py:357
  4.8 3.5 %collective-permute-start.1 = (bf16[8,64,128]{2,1,0:T(8,128)(2,1)S(1)}, bf16[8,64,128]{2,1,0:T(8,128)(2,1)S(1)}, u32[]{:S(2)}, u32[]{:S(2)}) collective-permute-start(bf16[8,64,128]{2,1,0:T(8,128)(2,1)S(1)} %get-tuple-element.47.far), channel_id=1, source_target_pairs={{4,8},{12,16},{20,24},{28,0},{8,4},{16,12},{24,20},{0,28},{5,9},{1... | collective-permute-start | bytes 393224 | tf_op jit(solution)/shard_map/ppermute | solution.py:357
  8.4 1.0 %copy-done = bf16[3,3,64,192]{3,2,1,0:T(8,128)(2,1)S(1)} copy-done((bf16[3,3,64,192]{3,2,1,0:T(8,128)(2,1)S(1)}, bf16[3,3,64,192]{3,2,1,0:T(8,128)(2,1)}, u32[]{:S(2)}) %copy-start) | copy-done | bytes 221208
  9.3 1.9 %shard_map.76 = (bf16[2,10,192,128]{3,2,1,0:T(8,128)(2,1)S(1)}, f32[2,8,64,128]{3,2,1,0:T(8,128)S(1)}, f32[2,8,64,128]{3,2,1,0:T(8,128)S(1)}) custom-call(bf16[8,64,128]{2,1,0:T(8,128)(2,1)S(1)} %get-tuple-element.46.near, bf16[8,64,128]{2,1,0:T(8,128)(2,1)S(1)} %get-tuple-element.47.far, bf16[3,3,64,192]{3,2,1,0:T(8,128)(2,1)S(1)} %copy-done, ...), custom_call_target="tpu_custom_call" | custom-call | flops 301989888 | bytes 2711552 | tf_op jit(solution)/shard_map/pallas_call | solution.py:20
  11.3 0.0 copy-start.1
  11.3 0.0 collective-permute-done.near.near_in
  11.3 1.2 %collective-permute-done.1.far.far_in = bf16[8,64,128]{2,1,0:T(8,128)(2,1)S(1)} collective-permute-done((bf16[8,64,128]{2,1,0:T(8,128)(2,1)S(1)}, bf16[8,64,128]{2,1,0:T(8,128)(2,1)S(1)}, u32[]{:S(2)}, u32[]{:S(2)}) %collective-permute-start.1) | collective-permute-done | bytes 131104 | tf_op jit(solution)/shard_map/ppermute | solution.py:357
  12.5 0.1 collective-permute-start.2
  12.6 1.6 %collective-permute-start.3 = (bf16[4,64,128]{2,1,0:T(8,128)(2,1)S(1)}, bf16[4,64,128]{2,1,0:T(8,128)(2,1)S(1)}, u32[]{:S(2)}, u32[]{:S(2)}) collective-permute-start(bf16[4,64,128]{2,1,0:T(8,128)(2,1)S(1)} %get-tuple-element.55), channel_id=1, source_target_pairs={{1,2},{3,0},{2,1},{0,3},{5,6},{7,4},{6,5},{4,7},{9,10},{11,8},{10,... | collective-permute-start | bytes 196616 | tf_op jit(solution)/shard_map/ppermute | solution.py:357
  14.2 1.4 %shard_map.77 = (bf16[2,10,192,128]{3,2,1,0:T(8,128)(2,1)S(1)}, f32[2,8,64,128]{3,2,1,0:T(8,128)S(1)}) custom-call(bf16[8,64,128]{2,1,0:T(8,128)(2,1)S(1)} %collective-permute-done.near.near_in, bf16[8,64,128]{2,1,0:T(8,128)(2,1)S(1)} %collective-permute-done.1.far.far_in, bf16[3,3,64,192]{3,2,1,0:T(8,128)(2,1)S(1)} %copy-done.1, ...), custom_call_target="tpu_custom_call" | custom-call | flops 150994944 | bytes 2514944 | tf_op jit(solution)/shard_map/pallas_call | solution.py:20
  15.6 0.0 collective-permute-done.2.near
  15.6 0.9 %collective-permute-done.3.far = bf16[4,64,128]{2,1,0:T(8,128)(2,1)S(1)} collective-permute-done((bf16[4,64,128]{2,1,0:T(8,128)(2,1)S(1)}, bf16[4,64,128]{2,1,0:T(8,128)(2,1)S(1)}, u32[]{:S(2)}, u32[]{:S(2)}) %collective-permute-start.3) | collective-permute-done | bytes 65568 | tf_op jit(solution)/shard_map/ppermute | solution.py:357
  16.5 0.5 shard_map.79
  17.0 2.3 %shard_map.80 = (f32[704,128]{1,0:T(8,128)S(1)}, bf16[704,128]{1,0:T(8,128)(2,1)S(1)}) custom-call(bf16[2,10,192,128]{3,2,1,0:T(8,128)(2,1)S(1)} %get-tuple-element.48.inner, bf16[2,10,192,128]{3,2,1,0:T(8,128)(2,1)S(1)} %get-tuple-element.53.outer, bf16[4,2,192,128]{3,2,1,0:T(8,128)(2,1)S(1)} %get-tuple-element.58.edges, ...), custom_call_target="tpu_custom_call" | custom-call | flops 452984832 | bytes 3489792 | tf_op jit(solution)/shard_map/pallas_call | solution.py:20
  19.4 0.5 collective-permute-start.4
  19.8 1.0 %collective-permute-done.4.other = bf16[704,128]{1,0:T(8,128)(2,1)S(1)} collective-permute-done((bf16[704,128]{1,0:T(8,128)(2,1)S(1)}, bf16[704,128]{1,0:T(8,128)(2,1)S(1)}, u32[]{:S(2)}, u32[]{:S(2)}) %collective-permute-start.4) | collective-permute-done | bytes 180256 | tf_op jit(solution)/shard_map/ppermute | solution.py:363
  20.9 0.1 shard_map.81
  20.9 1.5 %collective-permute-start.5 = (bf16[352,128]{1,0:T(8,128)(2,1)S(1)}, bf16[352,128]{1,0:T(8,128)(2,1)S(1)}, u32[]{:S(2)}, u32[]{:S(2)}) collective-permute-start(bf16[352,128]{1,0:T(8,128)(2,1)S(1)} %get-tuple-element.67), channel_id=1, source_target_pairs={{0,3},{1,2},{2,1},{3,0},{4,7},{5,6},{6,5},{7,4},{8,11},{9,10},{10,... | collective-permute-start | bytes 270344 | tf_op jit(solution)/shard_map/ppermute | solution.py:363
  22.5 3.5 %collective-permute-start.7 = (bf16[8,64,128]{2,1,0:T(8,128)(2,1)S(1)}, bf16[8,64,128]{2,1,0:T(8,128)(2,1)S(1)}, u32[]{:S(2)}, u32[]{:S(2)}) collective-permute-start(bf16[8,64,128]{2,1,0:T(8,128)(2,1)S(1)} %get-tuple-element.71.far), channel_id=1, source_target_pairs={{4,8},{12,16},{20,24},{28,0},{8,4},{16,12},{24,20},{0,28},{5,9},{1... | collective-permute-start | bytes 393224 | tf_op jit(solution)/shard_map/ppermute | solution.py:357
  26.0 0.0 collective-permute-done.5.other
  26.1 0.1 collective-permute-start.6
  26.1 5.6 %collective-permute-done.6.y = bf16[176,128]{1,0:T(8,128)(2,1)S(1)} collective-permute-done((bf16[176,128]{1,0:T(8,128)(2,1)S(1)}, bf16[176,128]{1,0:T(8,128)(2,1)S(1)}, u32[]{:S(2)}, u32[]{:S(2)}) %collective-permute-start.6) | collective-permute-done | bytes 45088 | tf_op jit(solution)/shard_map/ppermute | solution.py:363
  31.7 0.0 collective-permute-done.7.far_in
  31.7 0.1 collective-permute-start.11
  31.8 0.1 collective-permute-start.8
  31.9 3.6 %collective-permute-done.8.y = bf16[176,128]{1,0:T(8,128)(2,1)S(1)} collective-permute-done((bf16[176,128]{1,0:T(8,128)(2,1)S(1)}, bf16[176,128]{1,0:T(8,128)(2,1)S(1)}, u32[]{:S(2)}, u32[]{:S(2)}) %collective-permute-start.8) | collective-permute-done | bytes 45088 | tf_op jit(solution)/shard_map/ppermute | solution.py:363
  35.5 2.4 %collective-permute-start.9 = (bf16[176,128]{1,0:T(8,128)(2,1)S(1)}, bf16[176,128]{1,0:T(8,128)(2,1)S(1)}, u32[]{:S(2)}, u32[]{:S(2)}) collective-permute-start(bf16[176,128]{1,0:T(8,128)(2,1)S(1)} %shard_map.84.x), channel_id=1, source_target_pairs={{0,17},{1,16},{2,19},{3,18},{4,21},{5,20},{6,23},{7,22},{8,25},{9,... | collective-permute-start | bytes 135176 | tf_op jit(solution)/shard_map/ppermute | solution.py:363
  37.9 0.3 copy.9
  38.2 1.4 %shard_map.86 = bf16[128,256]{1,0:T(8,128)(2,1)} custom-call(bf16[2,8,64,128]{3,2,1,0:T(8,128)(2,1)S(1)} %get-tuple-element.73.h_ref, bf16[2,2,128,128]{3,2,1,0:T(8,128)(2,1)S(1)} %copy-done.3), custom_call_target="tpu_custom_call" | custom-call | flops 45298484 | bytes 458752 | tf_op jit(solution)/shard_map/pallas_call | solution.py:20
  39.6 0.4 collective-permute-done.9.y
  40.0 2.6 %collective-permute-start.10 = (bf16[176,128]{1,0:T(8,128)(2,1)S(1)}, bf16[176,128]{1,0:T(8,128)(2,1)S(1)}, u32[]{:S(2)}, u32[]{:S(2)}) collective-permute-start(bf16[176,128]{1,0:T(8,128)(2,1)S(1)} %shard_map.85.mine), channel_id=1, source_target_pairs={{0,5},{1,4},{2,7},{3,6},{4,1},{5,0},{6,3},{7,2},{8,13},{9,12},{10,... | collective-permute-start | bytes 135176 | tf_op jit(solution)/shard_map/ppermute | solution.py:363
  42.5 0.0 collective-permute-done.11.near_in
  42.6 0.5 collective-permute-start.12
  43.0 0.4 collective-permute-start.13
  43.4 0.3 copy.10
  43.7 0.2 copy.11.w_ref
  43.9 2.3 %shard_map.88.acc_ref = f32[2,8,64,128]{3,2,1,0:T(8,128)S(1)} custom-call(bf16[8,64,128]{2,1,0:T(8,128)(2,1)S(1)} %get-tuple-element.76.near, bf16[8,64,128]{2,1,0:T(8,128)(2,1)S(1)} %get-tuple-element.71.far, bf16[8,64,128]{2,1,0:T(8,128)(2,1)S(1)} %collective-permute-done.11.near_in, bf16[8,64,128]{2,1,0:T(8,128)(2,1)S(1)} %collective-permute-done.7.far_in, ...), custom_call_target="tpu_custom_call" | custom-call | flops 452984832 | bytes 1269760 | tf_op jit(solution)/shard_map/pallas_call | solution.py:20
  46.2 0.0 collective-permute-done.10.other
  46.3 0.0 collective-permute-done.12.near
  46.3 0.9 %collective-permute-done.13.far = bf16[4,64,128]{2,1,0:T(8,128)(2,1)S(1)} collective-permute-done((bf16[4,64,128]{2,1,0:T(8,128)(2,1)S(1)}, bf16[4,64,128]{2,1,0:T(8,128)(2,1)S(1)}, u32[]{:S(2)}, u32[]{:S(2)}) %collective-permute-start.13) | collective-permute-done | bytes 65568 | tf_op jit(solution)/shard_map/ppermute | solution.py:357
  47.1 0.6 %collective-permute-start.14 = (bf16[352,128]{1,0:T(8,128)(2,1)S(1)}, bf16[352,128]{1,0:T(8,128)(2,1)S(1)}, u32[]{:S(2)}, u32[]{:S(2)}) collective-permute-start(bf16[352,128]{1,0:T(8,128)(2,1)S(1)} %shard_map.87.mine), channel_id=1, source_target_pairs={{0,3},{1,2},{2,1},{3,0},{4,7},{5,6},{6,5},{7,4},{8,11},{9,10},{10,... | collective-permute-start | bytes 270344 | tf_op jit(solution)/shard_map/ppermute | solution.py:363
  47.7 1.3 %shard_map.91 = f32[1024,128]{1,0:T(8,128)} custom-call(bf16[4,64,128]{2,1,0:T(8,128)(2,1)S(1)} %collective-permute-done.12.near, bf16[4,64,128]{2,1,0:T(8,128)(2,1)S(1)} %collective-permute-done.13.far, f32[2,8,64,128]{3,2,1,0:T(8,128)S(1)} %shard_map.88.acc_ref, bf16[3,3,64,192]{3,2,1,0:T(8,128)(2,1)S(1)} %copy.11.w_ref), custom_call_target="tpu_custom_call" | custom-call | flops 45298484 | bytes 1400832 | tf_op jit(solution)/shard_map/pallas_call | solution.py:20
  49.1 2.7 %collective-permute-done.14.other = bf16[352,128]{1,0:T(8,128)(2,1)S(1)} collective-permute-done((bf16[352,128]{1,0:T(8,128)(2,1)S(1)}, bf16[352,128]{1,0:T(8,128)(2,1)S(1)}, u32[]{:S(2)}, u32[]{:S(2)}) %collective-permute-start.14) | collective-permute-done | bytes 90144 | tf_op jit(solution)/shard_map/ppermute | solution.py:363
  51.8 0.2 collective-permute-start.15
  52.0 1.3 %collective-permute-done.15.other = bf16[704,128]{1,0:T(8,128)(2,1)S(1)} collective-permute-done((bf16[704,128]{1,0:T(8,128)(2,1)S(1)}, bf16[704,128]{1,0:T(8,128)(2,1)S(1)}, u32[]{:S(2)}, u32[]{:S(2)}) %collective-permute-start.15) | collective-permute-done | bytes 180256 | tf_op jit(solution)/shard_map/ppermute | solution.py:363
  53.3 1.0 %shard_map.92 = (f32[3,3,64,192]{3,2,1,0:T(8,128)}, f32[2,2,128,128]{3,2,1,0:T(8,128)}) custom-call(bf16[704,128]{1,0:T(8,128)(2,1)S(1)} %shard_map.90.mine, bf16[704,128]{1,0:T(8,128)(2,1)S(1)} %collective-permute-done.15.other), custom_call_target="tpu_custom_call" | custom-call | bytes 1064960 | tf_op jit(solution)/shard_map/pallas_call | solution.py:20
  (16 shorter events, 0.2 us)
Async XLA Ops:
  0.6 1.0 %copy-start.2 = (bf16[64,2,8,128]{3,2,1,0:T(8,128)(2,1)S(1)}, bf16[64,2,8,128]{3,2,1,0:T(8,128)(2,1)}, u32[]{:S(2)}) copy-start(bf16[64,2,8,128]{3,2,1,0:T(8,128)(2,1)} %f_ref.1) | copy-start | bytes 786436
  1.6 6.8 %copy-start.3 = (bf16[2,2,128,128]{3,2,1,0:T(8,128)(2,1)S(1)}, bf16[2,2,128,128]{3,2,1,0:T(8,128)(2,1)}, u32[]{:S(2)}) copy-start(bf16[2,2,128,128]{3,2,1,0:T(8,128)(2,1)} %d_ref.3) | copy-start | bytes 393220
  1.6 6.8 %copy-start.4 = (bf16[128,1,256]{2,0,1:T(8,128)(2,1)S(1)}, bf16[128,1,256]{2,0,1:T(8,128)(2,1)}, u32[]{:S(2)}) copy-start(bf16[128,1,256]{2,0,1:T(8,128)(2,1)} %param.7) | copy-start | bytes 196612
  1.8 9.5 %collective-permute-start = (bf16[8,64,128]{2,1,0:T(8,128)(2,1)S(1)}, bf16[8,64,128]{2,1,0:T(8,128)(2,1)S(1)}, u32[]{:S(2)}, u32[]{:S(2)}) collective-permute-start(bf16[8,64,128]{2,1,0:T(8,128)(2,1)S(1)} %get-tuple-element.46.near), channel_id=1, source_target_pairs={{0,4},{8,12},{16,20},{24,28},{4,0},{12,8},{20,16},{28,24},{1,5},{9... | collective-permute-start | bytes 393224 | tf_op jit(solution)/shard_map/ppermute | solution.py:357
  4.8 7.7 %collective-permute-start.1 = (bf16[8,64,128]{2,1,0:T(8,128)(2,1)S(1)}, bf16[8,64,128]{2,1,0:T(8,128)(2,1)S(1)}, u32[]{:S(2)}, u32[]{:S(2)}) collective-permute-start(bf16[8,64,128]{2,1,0:T(8,128)(2,1)S(1)} %get-tuple-element.47.far), channel_id=1, source_target_pairs={{4,8},{12,16},{20,24},{28,0},{8,4},{16,12},{24,20},{0,28},{5,9},{1... | collective-permute-start | bytes 393224 | tf_op jit(solution)/shard_map/ppermute | solution.py:357
  8.4 1.0 %copy-start = (bf16[3,3,64,192]{3,2,1,0:T(8,128)(2,1)S(1)}, bf16[3,3,64,192]{3,2,1,0:T(8,128)(2,1)}, u32[]{:S(2)}) copy-start(bf16[3,3,64,192]{3,2,1,0:T(8,128)(2,1)} %w_ref.5) | copy-start | bytes 663556
  11.3 3.0 %copy-start.1 = (bf16[3,3,64,192]{3,2,1,0:T(8,128)(2,1)S(1)}, bf16[3,3,64,192]{3,2,1,0:T(8,128)(2,1)}, u32[]{:S(2)}) copy-start(bf16[3,3,64,192]{3,2,1,0:T(8,128)(2,1)} %w_ref.5) | copy-start | bytes 663556
  12.5 3.1 %collective-permute-start.2 = (bf16[4,64,128]{2,1,0:T(8,128)(2,1)S(1)}, bf16[4,64,128]{2,1,0:T(8,128)(2,1)S(1)}, u32[]{:S(2)}, u32[]{:S(2)}) collective-permute-start(bf16[4,64,128]{2,1,0:T(8,128)(2,1)S(1)} %get-tuple-element.54), channel_id=1, source_target_pairs={{0,1},{2,3},{1,0},{3,2},{4,5},{6,7},{5,4},{7,6},{8,9},{10,11},{9,8... | collective-permute-start | bytes 196616 | tf_op jit(solution)/shard_map/ppermute | solution.py:357
  12.6 3.9 %collective-permute-start.3 = (bf16[4,64,128]{2,1,0:T(8,128)(2,1)S(1)}, bf16[4,64,128]{2,1,0:T(8,128)(2,1)S(1)}, u32[]{:S(2)}, u32[]{:S(2)}) collective-permute-start(bf16[4,64,128]{2,1,0:T(8,128)(2,1)S(1)} %get-tuple-element.55), channel_id=1, source_target_pairs={{1,2},{3,0},{2,1},{0,3},{5,6},{7,4},{6,5},{4,7},{9,10},{11,8},{10,... | collective-permute-start | bytes 196616 | tf_op jit(solution)/shard_map/ppermute | solution.py:357
  19.4 1.5 %collective-permute-start.4 = (bf16[704,128]{1,0:T(8,128)(2,1)S(1)}, bf16[704,128]{1,0:T(8,128)(2,1)S(1)}, u32[]{:S(2)}, u32[]{:S(2)}) collective-permute-start(bf16[704,128]{1,0:T(8,128)(2,1)S(1)} %get-tuple-element.64), channel_id=1, source_target_pairs={{0,1},{1,0},{2,3},{3,2},{4,5},{5,4},{6,7},{7,6},{8,9},{9,8},{10,11... | collective-permute-start | bytes 540680 | tf_op jit(solution)/shard_map/ppermute | solution.py:363
  20.9 5.1 %collective-permute-start.5 = (bf16[352,128]{1,0:T(8,128)(2,1)S(1)}, bf16[352,128]{1,0:T(8,128)(2,1)S(1)}, u32[]{:S(2)}, u32[]{:S(2)}) collective-permute-start(bf16[352,128]{1,0:T(8,128)(2,1)S(1)} %get-tuple-element.67), channel_id=1, source_target_pairs={{0,3},{1,2},{2,1},{3,0},{4,7},{5,6},{6,5},{7,4},{8,11},{9,10},{10,... | collective-permute-start | bytes 270344 | tf_op jit(solution)/shard_map/ppermute | solution.py:363
  22.5 9.2 %collective-permute-start.7 = (bf16[8,64,128]{2,1,0:T(8,128)(2,1)S(1)}, bf16[8,64,128]{2,1,0:T(8,128)(2,1)S(1)}, u32[]{:S(2)}, u32[]{:S(2)}) collective-permute-start(bf16[8,64,128]{2,1,0:T(8,128)(2,1)S(1)} %get-tuple-element.71.far), channel_id=1, source_target_pairs={{4,8},{12,16},{20,24},{28,0},{8,4},{16,12},{24,20},{0,28},{5,9},{1... | collective-permute-start | bytes 393224 | tf_op jit(solution)/shard_map/ppermute | solution.py:357
  26.1 5.6 %collective-permute-start.6 = (bf16[176,128]{1,0:T(8,128)(2,1)S(1)}, bf16[176,128]{1,0:T(8,128)(2,1)S(1)}, u32[]{:S(2)}, u32[]{:S(2)}) collective-permute-start(bf16[176,128]{1,0:T(8,128)(2,1)S(1)} %get-tuple-element.69), channel_id=1, source_target_pairs={{0,5},{1,4},{2,7},{3,6},{4,1},{5,0},{6,3},{7,2},{8,13},{9,12},{10,... | collective-permute-start | bytes 135176 | tf_op jit(solution)/shard_map/ppermute | solution.py:363
  31.7 10.8 %collective-permute-start.11 = (bf16[8,64,128]{2,1,0:T(8,128)(2,1)S(1)}, bf16[8,64,128]{2,1,0:T(8,128)(2,1)S(1)}, u32[]{:S(2)}, u32[]{:S(2)}) collective-permute-start(bf16[8,64,128]{2,1,0:T(8,128)(2,1)S(1)} %get-tuple-element.76.near), channel_id=1, source_target_pairs={{0,4},{8,12},{16,20},{24,28},{4,0},{12,8},{20,16},{28,24},{1,5},{9... | collective-permute-start | bytes 393224 | tf_op jit(solution)/shard_map/ppermute | solution.py:357
  31.8 3.7 %collective-permute-start.8 = (bf16[176,128]{1,0:T(8,128)(2,1)S(1)}, bf16[176,128]{1,0:T(8,128)(2,1)S(1)}, u32[]{:S(2)}, u32[]{:S(2)}) collective-permute-start(bf16[176,128]{1,0:T(8,128)(2,1)S(1)} %shard_map.83.x), channel_id=1, source_target_pairs={{0,9},{1,8},{2,11},{3,10},{4,13},{5,12},{6,15},{7,14},{8,1},{9,0},... | collective-permute-start | bytes 135176 | tf_op jit(solution)/shard_map/ppermute | solution.py:363
  35.5 4.4 %collective-permute-start.9 = (bf16[176,128]{1,0:T(8,128)(2,1)S(1)}, bf16[176,128]{1,0:T(8,128)(2,1)S(1)}, u32[]{:S(2)}, u32[]{:S(2)}) collective-permute-start(bf16[176,128]{1,0:T(8,128)(2,1)S(1)} %shard_map.84.x), channel_id=1, source_target_pairs={{0,17},{1,16},{2,19},{3,18},{4,21},{5,20},{6,23},{7,22},{8,25},{9,... | collective-permute-start | bytes 135176 | tf_op jit(solution)/shard_map/ppermute | solution.py:363
  40.0 6.2 %collective-permute-start.10 = (bf16[176,128]{1,0:T(8,128)(2,1)S(1)}, bf16[176,128]{1,0:T(8,128)(2,1)S(1)}, u32[]{:S(2)}, u32[]{:S(2)}) collective-permute-start(bf16[176,128]{1,0:T(8,128)(2,1)S(1)} %shard_map.85.mine), channel_id=1, source_target_pairs={{0,5},{1,4},{2,7},{3,6},{4,1},{5,0},{6,3},{7,2},{8,13},{9,12},{10,... | collective-permute-start | bytes 135176 | tf_op jit(solution)/shard_map/ppermute | solution.py:363
  42.6 3.7 %collective-permute-start.12 = (bf16[4,64,128]{2,1,0:T(8,128)(2,1)S(1)}, bf16[4,64,128]{2,1,0:T(8,128)(2,1)S(1)}, u32[]{:S(2)}, u32[]{:S(2)}) collective-permute-start(bf16[4,64,128]{2,1,0:T(8,128)(2,1)S(1)} %get-tuple-element.78), channel_id=1, source_target_pairs={{0,1},{2,3},{1,0},{3,2},{4,5},{6,7},{5,4},{7,6},{8,9},{10,11},{9,8... | collective-permute-start | bytes 196616 | tf_op jit(solution)/shard_map/ppermute | solution.py:357
  43.0 4.1 %collective-permute-start.13 = (bf16[4,64,128]{2,1,0:T(8,128)(2,1)S(1)}, bf16[4,64,128]{2,1,0:T(8,128)(2,1)S(1)}, u32[]{:S(2)}, u32[]{:S(2)}) collective-permute-start(bf16[4,64,128]{2,1,0:T(8,128)(2,1)S(1)} %get-tuple-element.79), channel_id=1, source_target_pairs={{1,2},{3,0},{2,1},{0,3},{5,6},{7,4},{6,5},{4,7},{9,10},{11,8},{10,... | collective-permute-start | bytes 196616 | tf_op jit(solution)/shard_map/ppermute | solution.py:357
  47.1 4.6 %collective-permute-start.14 = (bf16[352,128]{1,0:T(8,128)(2,1)S(1)}, bf16[352,128]{1,0:T(8,128)(2,1)S(1)}, u32[]{:S(2)}, u32[]{:S(2)}) collective-permute-start(bf16[352,128]{1,0:T(8,128)(2,1)S(1)} %shard_map.87.mine), channel_id=1, source_target_pairs={{0,3},{1,2},{2,1},{3,0},{4,7},{5,6},{6,5},{7,4},{8,11},{9,10},{10,... | collective-permute-start | bytes 270344 | tf_op jit(solution)/shard_map/ppermute | solution.py:363
  51.8 1.5 %collective-permute-start.15 = (bf16[704,128]{1,0:T(8,128)(2,1)S(1)}, bf16[704,128]{1,0:T(8,128)(2,1)S(1)}, u32[]{:S(2)}, u32[]{:S(2)}) collective-permute-start(bf16[704,128]{1,0:T(8,128)(2,1)S(1)} %shard_map.90.mine), channel_id=1, source_target_pairs={{0,1},{1,0},{2,3},{3,2},{4,5},{5,4},{6,7},{7,6},{8,9},{9,8},{10,11... | collective-permute-start | bytes 540680 | tf_op jit(solution)/shard_map/ppermute | solution.py:363

commit v16 on v10

--- a/solution.py
+++ b/solution.py
@@ -417,9 +417,9 @@
     keep, gates = tied(keep, *gates)
     near, far = gates
     near_in = swap(near, "gz", 0)
-    for level, (axis, bit) in enumerate((("gy", 2), ("gz", 2))):
+    for level, (axis, bit) in enumerate((("gz", 2), ("gy", 2))):
         size = rows >> (level + 2)
-        mine, got = keep, flip(send, *(("gy", 1), ("gy", 2))[level])
+        mine, got = keep, flip(send, *(("gy", 1), ("gz", 2))[level])
         keep, send = call(
             functools.partial(halve_kernel, axis=axis, bit=bit),
             [((size, 128), F32), ((size, 128), BF16)], [((2 * size, 128), F32)], 0, (mine, got),
@@ -432,7 +432,7 @@
                 (hidden, down_weight),
             )
     shard = ((rows // 8, 128), BF16)
-    (sums,) = call(add_kernel, [shard], [], 0, (keep, flip(send, "gz", 2)))
+    (sums,) = call(add_kernel, [shard], [], 0, (keep, flip(send, "gy", 2)))
     (sums,) = call(add_kernel, [shard], [], 0, (sums, flip(sums, "gz", 1)))
     sums, outside = tied(sums, near_in, far_in)
     sends = call(edges_kernel, [edge, edge], [], 0, (*gates, *outside))
@@ -446,8 +446,8 @@
         (sums,) = call(add_kernel, [shard], [], 0, (sums, flip(sums, axis, bit)))
     sums, (section_out,) = tied(sums, section_out)
     (sums,) = call(
-        functools.partial(join_kernel, axis="gz", bit=2), [((rows // 4, 128), BF16)], [], 0,
-        (sums, flip(sums, "gz", 2)),
+        functools.partial(join_kernel, axis="gy", bit=2), [((rows // 4, 128), BF16)], [], 0,
+        (sums, flip(sums, "gy", 2)),
     )
     sums, (acc, *beside) = tied(sums, acc, *beside)
     (field,) = call(
@@ -455,8 +455,8 @@
         conv_flops // 10, (*beside, acc, weight_bwd),
     )
     (sums,) = call(
-        functools.partial(join_kernel, axis="gy", bit=2), [((rows // 2, 128), BF16)], [], 0,
-        (sums, flip(sums, "gy", 2)),
+        functools.partial(join_kernel, axis="gz", bit=2), [((rows // 2, 128), BF16)], [], 0,
+        (sums, flip(sums, "gz", 2)),
     )
     sums, (field,) = tied(sums, field)
     grad_conv, grad_down = call(

time: 51.1 us -> 49.9 us (0.977)
  starting transfers between devices: 23 us -> 20.3 us
  waiting for transfers between devices: 11.8 us -> 13.4 us
    ppermute x8, starting transfers between devices: 10.1 us -> 6.39 us  [flip(): lax.ppermute(cells, ('gz', 'gy'), [(i, i ^ mask) for i in range(lax.axis_...]
    ppermute x8, waiting for transfers between devices: 9.69 us -> 11.2 us  [flip(): lax.ppermute(cells, ('gz', 'gy'), [(i, i ^ mask) for i in range(lax.axis_...]
    ppermute x8, starting transfers between devices: 12.9 us -> 13.9 us  [swap(): return lax.ppermute(cells, axis, pairs + [(b, a) for a, b in pairs])]
  transfers between devices with their start and end apart: 16 -> 16, of which waited for: 7 -> 10; matrix products, arithmetic and copies ran while one was open for 2% -> 2% of each run, Pallas kernels for 16% -> 17%
where the time goes in v16:
time: 49.9 us; the launch traced here: 49.7 us
  starting transfers between devices  20.3 us (41%)
  waiting for transfers between devices  13.4 us (27%)
  Pallas kernels  12.6 us (25%)
  local copies, waits for them, and re-layouts  2.7 us (5%)
  between operations  0.81 us (2%)
    ppermute x8, starting transfers between devices, swap(): return lax.ppermute(cells, axis, pairs + [(b, a) for a, b in pairs])  13.9 us
    pallas_call x18, Pallas kernels, call(): pl.pallas_call(kernel, out_shape=[jax.ShapeDtypeStruct(s, d) for s, d in...  12.6 us
    ppermute x8, waiting for transfers between devices, flip(): lax.ppermute(cells, ('gz', 'gy'), [(i, i ^ mask) for i in range(lax.axis_...  11.2 us
    ppermute x8, starting transfers between devices, flip(): lax.ppermute(cells, ('gz', 'gy'), [(i, i ^ mask) for i in range(lax.axis_...  6.39 us
    unnamed x11, local copies, waits for them, and re-layouts  2.18 us
    ppermute x8, waiting for transfers between devices, swap(): return lax.ppermute(cells, axis, pairs + [(b, a) for a, b in pairs])  2.13 us
  transfers between devices with their start and end apart: 16, of which 10 were waited for; matrix products, arithmetic and copies ran while one was open for 2% of the time, Pallas kernels for 17%

profile of v16, /device:TPU:0, one launch (start us, length us, event | category | flops | bytes accessed | tf_op | source)
XLA Modules:
  0.0 49.7 jit_solution(13086119644624945647)
XLA Ops:
  0.6 0.9 %copy-done.2 = bf16[64,2,8,128]{3,2,1,0:T(8,128)(2,1)S(1)} copy-done((bf16[64,2,8,128]{3,2,1,0:T(8,128)(2,1)S(1)}, bf16[64,2,8,128]{3,2,1,0:T(8,128)(2,1)}, u32[]{:S(2)}) %copy-start.2) | copy-done | bytes 262168
  1.6 0.2 shard_map.75
  1.8 3.0 %collective-permute-start = (bf16[8,64,128]{2,1,0:T(8,128)(2,1)S(1)}, bf16[8,64,128]{2,1,0:T(8,128)(2,1)S(1)}, u32[]{:S(2)}, u32[]{:S(2)}) collective-permute-start(bf16[8,64,128]{2,1,0:T(8,128)(2,1)S(1)} %get-tuple-element.47.near), channel_id=1, source_target_pairs={{0,4},{8,12},{16,20},{24,28},{4,0},{12,8},{20,16},{28,24},{1,5},{9... | collective-permute-start | bytes 393224 | tf_op jit(solution)/shard_map/ppermute | solution.py:357
  4.8 3.5 %collective-permute-start.1 = (bf16[8,64,128]{2,1,0:T(8,128)(2,1)S(1)}, bf16[8,64,128]{2,1,0:T(8,128)(2,1)S(1)}, u32[]{:S(2)}, u32[]{:S(2)}) collective-permute-start(bf16[8,64,128]{2,1,0:T(8,128)(2,1)S(1)} %get-tuple-element.48.far), channel_id=1, source_target_pairs={{4,8},{12,16},{20,24},{28,0},{8,4},{16,12},{24,20},{0,28},{5,9},{1... | collective-permute-start | bytes 393224 | tf_op jit(solution)/shard_map/ppermute | solution.py:357
  8.4 1.0 %copy-done = bf16[3,3,64,192]{3,2,1,0:T(8,128)(2,1)S(1)} copy-done((bf16[3,3,64,192]{3,2,1,0:T(8,128)(2,1)S(1)}, bf16[3,3,64,192]{3,2,1,0:T(8,128)(2,1)}, u32[]{:S(2)}) %copy-start) | copy-done | bytes 221208
  9.3 1.9 %shard_map.76 = (bf16[2,10,192,128]{3,2,1,0:T(8,128)(2,1)S(1)}, f32[2,8,64,128]{3,2,1,0:T(8,128)S(1)}, f32[2,8,64,128]{3,2,1,0:T(8,128)S(1)}) custom-call(bf16[8,64,128]{2,1,0:T(8,128)(2,1)S(1)} %get-tuple-element.47.near, bf16[8,64,128]{2,1,0:T(8,128)(2,1)S(1)} %get-tuple-element.48.far, bf16[3,3,64,192]{3,2,1,0:T(8,128)(2,1)S(1)} %copy-done, ...), custom_call_target="tpu_custom_call" | custom-call | flops 301989888 | bytes 2711552 | tf_op jit(solution)/shard_map/pallas_call | solution.py:20
  11.3 0.0 copy-start.1
  11.3 0.0 collective-permute-done.near.near_in
  11.3 1.2 %collective-permute-done.1.far.far_in = bf16[8,64,128]{2,1,0:T(8,128)(2,1)S(1)} collective-permute-done((bf16[8,64,128]{2,1,0:T(8,128)(2,1)S(1)}, bf16[8,64,128]{2,1,0:T(8,128)(2,1)S(1)}, u32[]{:S(2)}, u32[]{:S(2)}) %collective-permute-start.1) | collective-permute-done | bytes 131104 | tf_op jit(solution)/shard_map/ppermute | solution.py:357
  12.5 0.1 collective-permute-start.2
  12.6 1.6 %collective-permute-start.3 = (bf16[4,64,128]{2,1,0:T(8,128)(2,1)S(1)}, bf16[4,64,128]{2,1,0:T(8,128)(2,1)S(1)}, u32[]{:S(2)}, u32[]{:S(2)}) collective-permute-start(bf16[4,64,128]{2,1,0:T(8,128)(2,1)S(1)} %get-tuple-element.56), channel_id=1, source_target_pairs={{1,2},{3,0},{2,1},{0,3},{5,6},{7,4},{6,5},{4,7},{9,10},{11,8},{10,... | collective-permute-start | bytes 196616 | tf_op jit(solution)/shard_map/ppermute | solution.py:357
  14.2 1.4 %shard_map.77 = (bf16[2,10,192,128]{3,2,1,0:T(8,128)(2,1)S(1)}, f32[2,8,64,128]{3,2,1,0:T(8,128)S(1)}) custom-call(bf16[8,64,128]{2,1,0:T(8,128)(2,1)S(1)} %collective-permute-done.near.near_in, bf16[8,64,128]{2,1,0:T(8,128)(2,1)S(1)} %collective-permute-done.1.far.far_in, bf16[3,3,64,192]{3,2,1,0:T(8,128)(2,1)S(1)} %copy-done.1, ...), custom_call_target="tpu_custom_call" | custom-call | flops 150994944 | bytes 2514944 | tf_op jit(solution)/shard_map/pallas_call | solution.py:20
  15.6 0.0 collective-permute-done.2.near
  15.6 0.9 %collective-permute-done.3.far = bf16[4,64,128]{2,1,0:T(8,128)(2,1)S(1)} collective-permute-done((bf16[4,64,128]{2,1,0:T(8,128)(2,1)S(1)}, bf16[4,64,128]{2,1,0:T(8,128)(2,1)S(1)}, u32[]{:S(2)}, u32[]{:S(2)}) %collective-permute-start.3) | collective-permute-done | bytes 65568 | tf_op jit(solution)/shard_map/ppermute | solution.py:357
  16.5 0.5 %shard_map.79 = (bf16[4,2,192,128]{3,2,1,0:T(8,128)(2,1)S(1)}, bf16[8,64,128]{2,1,0:T(8,128)(2,1)S(1)}, bf16[8,64,128]{2,1,0:T(8,128)(2,1)S(1)}, bf16[2,8,64,128]{3,2,1,0:T(8,128)(2,1)S(1)}) custom-call(bf16[4,64,128]{2,1,0:T(8,128)(2,1)S(1)} %collective-permute-done.2.near, bf16[4,64,128]{2,1,0:T(8,128)(2,1)S(1)} %collective-permute-done.3.far, ...), custom_call_target="tpu_custom_call" | custom-call | flops 45298484 | bytes 2318336 | tf_op jit(solution)/shard_map/pallas_call | solution.py:20
  17.0 2.3 %shard_map.80 = (f32[704,128]{1,0:T(8,128)S(1)}, bf16[704,128]{1,0:T(8,128)(2,1)S(1)}) custom-call(bf16[2,10,192,128]{3,2,1,0:T(8,128)(2,1)S(1)} %get-tuple-element.49.inner, bf16[2,10,192,128]{3,2,1,0:T(8,128)(2,1)S(1)} %get-tuple-element.54.outer, bf16[4,2,192,128]{3,2,1,0:T(8,128)(2,1)S(1)} %get-tuple-element.59.edges, ...), custom_call_target="tpu_custom_call" | custom-call | flops 452984832 | bytes 3489792 | tf_op jit(solution)/shard_map/pallas_call | solution.py:20
  19.4 0.5 collective-permute-start.4
  19.8 1.0 %collective-permute-done.4.other = bf16[704,128]{1,0:T(8,128)(2,1)S(1)} collective-permute-done((bf16[704,128]{1,0:T(8,128)(2,1)S(1)}, bf16[704,128]{1,0:T(8,128)(2,1)S(1)}, u32[]{:S(2)}, u32[]{:S(2)}) %collective-permute-start.4) | collective-permute-done | bytes 180256 | tf_op jit(solution)/shard_map/ppermute | solution.py:363
  20.9 0.1 shard_map.81
  20.9 0.5 collective-permute-start.5
  21.4 1.5 %collective-permute-start.8 = (bf16[8,64,128]{2,1,0:T(8,128)(2,1)S(1)}, bf16[8,64,128]{2,1,0:T(8,128)(2,1)S(1)}, u32[]{:S(2)}, u32[]{:S(2)}) collective-permute-start(bf16[8,64,128]{2,1,0:T(8,128)(2,1)S(1)} %get-tuple-element.72.near), channel_id=1, source_target_pairs={{0,4},{8,12},{16,20},{24,28},{4,0},{12,8},{20,16},{28,24},{1,5},{9... | collective-permute-start | bytes 393224 | tf_op jit(solution)/shard_map/ppermute | solution.py:357
  22.9 2.4 %collective-permute-start.9 = (bf16[8,64,128]{2,1,0:T(8,128)(2,1)S(1)}, bf16[8,64,128]{2,1,0:T(8,128)(2,1)S(1)}, u32[]{:S(2)}, u32[]{:S(2)}) collective-permute-start(bf16[8,64,128]{2,1,0:T(8,128)(2,1)S(1)} %get-tuple-element.73.far), channel_id=1, source_target_pairs={{4,8},{12,16},{20,24},{28,0},{8,4},{16,12},{24,20},{0,28},{5,9},{1... | collective-permute-start | bytes 393224 | tf_op jit(solution)/shard_map/ppermute | solution.py:357
  25.4 0.1 collective-permute-done.5.other
  25.5 2.2 %collective-permute-start.6 = (bf16[176,128]{1,0:T(8,128)(2,1)S(1)}, bf16[176,128]{1,0:T(8,128)(2,1)S(1)}, u32[]{:S(2)}, u32[]{:S(2)}) collective-permute-start(bf16[176,128]{1,0:T(8,128)(2,1)S(1)} %get-tuple-element.71), channel_id=1, source_target_pairs={{0,3},{1,2},{2,1},{3,0},{4,7},{5,6},{6,5},{7,4},{8,11},{9,10},{10,... | collective-permute-start | bytes 135176 | tf_op jit(solution)/shard_map/ppermute | solution.py:363
  27.7 1.7 %collective-permute-done.6.y = bf16[176,128]{1,0:T(8,128)(2,1)S(1)} collective-permute-done((bf16[176,128]{1,0:T(8,128)(2,1)S(1)}, bf16[176,128]{1,0:T(8,128)(2,1)S(1)}, u32[]{:S(2)}, u32[]{:S(2)}) %collective-permute-start.6) | collective-permute-done | bytes 45088 | tf_op jit(solution)/shard_map/ppermute | solution.py:363
  29.5 0.3 collective-permute-start.7
  29.7 3.3 %collective-permute-done.7.y = bf16[176,128]{1,0:T(8,128)(2,1)S(1)} collective-permute-done((bf16[176,128]{1,0:T(8,128)(2,1)S(1)}, bf16[176,128]{1,0:T(8,128)(2,1)S(1)}, u32[]{:S(2)}, u32[]{:S(2)}) %collective-permute-start.7) | collective-permute-done | bytes 45088 | tf_op jit(solution)/shard_map/ppermute | solution.py:363
  33.0 0.0 collective-permute-done.8.near_in
  33.0 0.0 collective-permute-done.9.far_in
  33.0 1.3 %collective-permute-start.10 = (bf16[176,128]{1,0:T(8,128)(2,1)S(1)}, bf16[176,128]{1,0:T(8,128)(2,1)S(1)}, u32[]{:S(2)}, u32[]{:S(2)}) collective-permute-start(bf16[176,128]{1,0:T(8,128)(2,1)S(1)} %shard_map.84.x), channel_id=1, source_target_pairs={{0,17},{1,16},{2,19},{3,18},{4,21},{5,20},{6,23},{7,22},{8,25},{9,... | collective-permute-start | bytes 135176 | tf_op jit(solution)/shard_map/ppermute | solution.py:363
  34.4 0.3 copy.9
  34.6 1.4 %shard_map.86 = bf16[128,256]{1,0:T(8,128)(2,1)} custom-call(bf16[2,8,64,128]{3,2,1,0:T(8,128)(2,1)S(1)} %get-tuple-element.75.h_ref, bf16[2,2,128,128]{3,2,1,0:T(8,128)(2,1)S(1)} %copy-done.3), custom_call_target="tpu_custom_call" | custom-call | flops 45298484 | bytes 458752 | tf_op jit(solution)/shard_map/pallas_call | solution.py:20
  36.1 0.1 collective-permute-start.12
  36.2 1.6 %collective-permute-start.13 = (bf16[4,64,128]{2,1,0:T(8,128)(2,1)S(1)}, bf16[4,64,128]{2,1,0:T(8,128)(2,1)S(1)}, u32[]{:S(2)}, u32[]{:S(2)}) collective-permute-start(bf16[4,64,128]{2,1,0:T(8,128)(2,1)S(1)} %get-tuple-element.81), channel_id=1, source_target_pairs={{1,2},{3,0},{2,1},{0,3},{5,6},{7,4},{6,5},{4,7},{9,10},{11,8},{10,... | collective-permute-start | bytes 196616 | tf_op jit(solution)/shard_map/ppermute | solution.py:357
  37.7 1.0 %collective-permute-done.10.y = bf16[176,128]{1,0:T(8,128)(2,1)S(1)} collective-permute-done((bf16[176,128]{1,0:T(8,128)(2,1)S(1)}, bf16[176,128]{1,0:T(8,128)(2,1)S(1)}, u32[]{:S(2)}, u32[]{:S(2)}) %collective-permute-start.10) | collective-permute-done | bytes 45088 | tf_op jit(solution)/shard_map/ppermute | solution.py:363
  38.8 0.8 %collective-permute-start.11 = (bf16[176,128]{1,0:T(8,128)(2,1)S(1)}, bf16[176,128]{1,0:T(8,128)(2,1)S(1)}, u32[]{:S(2)}, u32[]{:S(2)}) collective-permute-start(bf16[176,128]{1,0:T(8,128)(2,1)S(1)} %shard_map.85.mine), channel_id=1, source_target_pairs={{0,3},{1,2},{2,1},{3,0},{4,7},{5,6},{6,5},{7,4},{8,11},{9,10},{10,... | collective-permute-start | bytes 135176 | tf_op jit(solution)/shard_map/ppermute | solution.py:363
  39.6 0.3 copy.10
  39.9 0.2 copy.11.w_ref
  40.1 2.3 %shard_map.88.acc_ref = f32[2,8,64,128]{3,2,1,0:T(8,128)S(1)} custom-call(bf16[8,64,128]{2,1,0:T(8,128)(2,1)S(1)} %get-tuple-element.72.near, bf16[8,64,128]{2,1,0:T(8,128)(2,1)S(1)} %get-tuple-element.73.far, bf16[8,64,128]{2,1,0:T(8,128)(2,1)S(1)} %collective-permute-done.8.near_in, bf16[8,64,128]{2,1,0:T(8,128)(2,1)S(1)} %collective-permute-done.9.far_in, ...), custom_call_target="tpu_custom_call" | custom-call | flops 452984832 | bytes 1269760 | tf_op jit(solution)/shard_map/pallas_call | solution.py:20
  42.4 0.1 collective-permute-done.11.other
  42.5 0.0 collective-permute-done.12.near
  42.5 0.0 collective-permute-done.13.far
  42.5 0.6 %collective-permute-start.14 = (bf16[352,128]{1,0:T(8,128)(2,1)S(1)}, bf16[352,128]{1,0:T(8,128)(2,1)S(1)}, u32[]{:S(2)}, u32[]{:S(2)}) collective-permute-start(bf16[352,128]{1,0:T(8,128)(2,1)S(1)} %shard_map.87.mine), channel_id=1, source_target_pairs={{0,9},{1,8},{2,11},{3,10},{4,13},{5,12},{6,15},{7,14},{8,1},{9,0},... | collective-permute-start | bytes 270344 | tf_op jit(solution)/shard_map/ppermute | solution.py:363
  43.2 1.3 %shard_map.91 = f32[1024,128]{1,0:T(8,128)} custom-call(bf16[4,64,128]{2,1,0:T(8,128)(2,1)S(1)} %collective-permute-done.12.near, bf16[4,64,128]{2,1,0:T(8,128)(2,1)S(1)} %collective-permute-done.13.far, f32[2,8,64,128]{3,2,1,0:T(8,128)S(1)} %shard_map.88.acc_ref, bf16[3,3,64,192]{3,2,1,0:T(8,128)(2,1)S(1)} %copy.11.w_ref), custom_call_target="tpu_custom_call" | custom-call | flops 45298484 | bytes 1400832 | tf_op jit(solution)/shard_map/pallas_call | solution.py:20
  44.5 2.7 %collective-permute-done.14.other = bf16[352,128]{1,0:T(8,128)(2,1)S(1)} collective-permute-done((bf16[352,128]{1,0:T(8,128)(2,1)S(1)}, bf16[352,128]{1,0:T(8,128)(2,1)S(1)}, u32[]{:S(2)}, u32[]{:S(2)}) %collective-permute-start.14) | collective-permute-done | bytes 90144 | tf_op jit(solution)/shard_map/ppermute | solution.py:363
  47.2 0.2 collective-permute-start.15
  47.4 1.3 %collective-permute-done.15.other = bf16[704,128]{1,0:T(8,128)(2,1)S(1)} collective-permute-done((bf16[704,128]{1,0:T(8,128)(2,1)S(1)}, bf16[704,128]{1,0:T(8,128)(2,1)S(1)}, u32[]{:S(2)}, u32[]{:S(2)}) %collective-permute-start.15) | collective-permute-done | bytes 180256 | tf_op jit(solution)/shard_map/ppermute | solution.py:363
  48.7 1.0 %shard_map.92 = (f32[3,3,64,192]{3,2,1,0:T(8,128)}, f32[2,2,128,128]{3,2,1,0:T(8,128)}) custom-call(bf16[704,128]{1,0:T(8,128)(2,1)S(1)} %shard_map.90.mine, bf16[704,128]{1,0:T(8,128)(2,1)S(1)} %collective-permute-done.15.other), custom_call_target="tpu_custom_call" | custom-call | bytes 1064960 | tf_op jit(solution)/shard_map/pallas_call | solution.py:20
  (16 shorter events, 0.2 us)
Async XLA Ops:
  0.6 1.0 %copy-start.2 = (bf16[64,2,8,128]{3,2,1,0:T(8,128)(2,1)S(1)}, bf16[64,2,8,128]{3,2,1,0:T(8,128)(2,1)}, u32[]{:S(2)}) copy-start(bf16[64,2,8,128]{3,2,1,0:T(8,128)(2,1)} %f_ref.1) | copy-start | bytes 786436
  1.6 6.8 %copy-start.3 = (bf16[2,2,128,128]{3,2,1,0:T(8,128)(2,1)S(1)}, bf16[2,2,128,128]{3,2,1,0:T(8,128)(2,1)}, u32[]{:S(2)}) copy-start(bf16[2,2,128,128]{3,2,1,0:T(8,128)(2,1)} %d_ref.3) | copy-start | bytes 393220
  1.6 6.8 %copy-start.4 = (bf16[128,1,256]{2,0,1:T(8,128)(2,1)S(1)}, bf16[128,1,256]{2,0,1:T(8,128)(2,1)}, u32[]{:S(2)}) copy-start(bf16[128,1,256]{2,0,1:T(8,128)(2,1)} %param.7) | copy-start | bytes 196612
  1.8 9.5 %collective-permute-start = (bf16[8,64,128]{2,1,0:T(8,128)(2,1)S(1)}, bf16[8,64,128]{2,1,0:T(8,128)(2,1)S(1)}, u32[]{:S(2)}, u32[]{:S(2)}) collective-permute-start(bf16[8,64,128]{2,1,0:T(8,128)(2,1)S(1)} %get-tuple-element.47.near), channel_id=1, source_target_pairs={{0,4},{8,12},{16,20},{24,28},{4,0},{12,8},{20,16},{28,24},{1,5},{9... | collective-permute-start | bytes 393224 | tf_op jit(solution)/shard_map/ppermute | solution.py:357
  4.8 7.7 %collective-permute-start.1 = (bf16[8,64,128]{2,1,0:T(8,128)(2,1)S(1)}, bf16[8,64,128]{2,1,0:T(8,128)(2,1)S(1)}, u32[]{:S(2)}, u32[]{:S(2)}) collective-permute-start(bf16[8,64,128]{2,1,0:T(8,128)(2,1)S(1)} %get-tuple-element.48.far), channel_id=1, source_target_pairs={{4,8},{12,16},{20,24},{28,0},{8,4},{16,12},{24,20},{0,28},{5,9},{1... | collective-permute-start | bytes 393224 | tf_op jit(solution)/shard_map/ppermute | solution.py:357
  8.4 1.0 %copy-start = (bf16[3,3,64,192]{3,2,1,0:T(8,128)(2,1)S(1)}, bf16[3,3,64,192]{3,2,1,0:T(8,128)(2,1)}, u32[]{:S(2)}) copy-start(bf16[3,3,64,192]{3,2,1,0:T(8,128)(2,1)} %w_ref.5) | copy-start | bytes 663556
  11.3 3.0 %copy-start.1 = (bf16[3,3,64,192]{3,2,1,0:T(8,128)(2,1)S(1)}, bf16[3,3,64,192]{3,2,1,0:T(8,128)(2,1)}, u32[]{:S(2)}) copy-start(bf16[3,3,64,192]{3,2,1,0:T(8,128)(2,1)} %w_ref.5) | copy-start | bytes 663556
  12.5 3.1 %collective-permute-start.2 = (bf16[4,64,128]{2,1,0:T(8,128)(2,1)S(1)}, bf16[4,64,128]{2,1,0:T(8,128)(2,1)S(1)}, u32[]{:S(2)}, u32[]{:S(2)}) collective-permute-start(bf16[4,64,128]{2,1,0:T(8,128)(2,1)S(1)} %get-tuple-element.55), channel_id=1, source_target_pairs={{0,1},{2,3},{1,0},{3,2},{4,5},{6,7},{5,4},{7,6},{8,9},{10,11},{9,8... | collective-permute-start | bytes 196616 | tf_op jit(solution)/shard_map/ppermute | solution.py:357
  12.6 3.9 %collective-permute-start.3 = (bf16[4,64,128]{2,1,0:T(8,128)(2,1)S(1)}, bf16[4,64,128]{2,1,0:T(8,128)(2,1)S(1)}, u32[]{:S(2)}, u32[]{:S(2)}) collective-permute-start(bf16[4,64,128]{2,1,0:T(8,128)(2,1)S(1)} %get-tuple-element.56), channel_id=1, source_target_pairs={{1,2},{3,0},{2,1},{0,3},{5,6},{7,4},{6,5},{4,7},{9,10},{11,8},{10,... | collective-permute-start | bytes 196616 | tf_op jit(solution)/shard_map/ppermute | solution.py:357
  19.4 1.5 %collective-permute-start.4 = (bf16[704,128]{1,0:T(8,128)(2,1)S(1)}, bf16[704,128]{1,0:T(8,128)(2,1)S(1)}, u32[]{:S(2)}, u32[]{:S(2)}) collective-permute-start(bf16[704,128]{1,0:T(8,128)(2,1)S(1)} %get-tuple-element.65), channel_id=1, source_target_pairs={{0,1},{1,0},{2,3},{3,2},{4,5},{5,4},{6,7},{7,6},{8,9},{9,8},{10,11... | collective-permute-start | bytes 540680 | tf_op jit(solution)/shard_map/ppermute | solution.py:363
  20.9 4.5 %collective-permute-start.5 = (bf16[352,128]{1,0:T(8,128)(2,1)S(1)}, bf16[352,128]{1,0:T(8,128)(2,1)S(1)}, u32[]{:S(2)}, u32[]{:S(2)}) collective-permute-start(bf16[352,128]{1,0:T(8,128)(2,1)S(1)} %get-tuple-element.69), channel_id=1, source_target_pairs={{0,9},{1,8},{2,11},{3,10},{4,13},{5,12},{6,15},{7,14},{8,1},{9,0},... | collective-permute-start | bytes 270344 | tf_op jit(solution)/shard_map/ppermute | solution.py:363
  21.4 11.6 %collective-permute-start.8 = (bf16[8,64,128]{2,1,0:T(8,128)(2,1)S(1)}, bf16[8,64,128]{2,1,0:T(8,128)(2,1)S(1)}, u32[]{:S(2)}, u32[]{:S(2)}) collective-permute-start(bf16[8,64,128]{2,1,0:T(8,128)(2,1)S(1)} %get-tuple-element.72.near), channel_id=1, source_target_pairs={{0,4},{8,12},{16,20},{24,28},{4,0},{12,8},{20,16},{28,24},{1,5},{9... | collective-permute-start | bytes 393224 | tf_op jit(solution)/shard_map/ppermute | solution.py:357
  22.9 10.1 %collective-permute-start.9 = (bf16[8,64,128]{2,1,0:T(8,128)(2,1)S(1)}, bf16[8,64,128]{2,1,0:T(8,128)(2,1)S(1)}, u32[]{:S(2)}, u32[]{:S(2)}) collective-permute-start(bf16[8,64,128]{2,1,0:T(8,128)(2,1)S(1)} %get-tuple-element.73.far), channel_id=1, source_target_pairs={{4,8},{12,16},{20,24},{28,0},{8,4},{16,12},{24,20},{0,28},{5,9},{1... | collective-permute-start | bytes 393224 | tf_op jit(solution)/shard_map/ppermute | solution.py:357
  25.5 3.9 %collective-permute-start.6 = (bf16[176,128]{1,0:T(8,128)(2,1)S(1)}, bf16[176,128]{1,0:T(8,128)(2,1)S(1)}, u32[]{:S(2)}, u32[]{:S(2)}) collective-permute-start(bf16[176,128]{1,0:T(8,128)(2,1)S(1)} %get-tuple-element.71), channel_id=1, source_target_pairs={{0,3},{1,2},{2,1},{3,0},{4,7},{5,6},{6,5},{7,4},{8,11},{9,10},{10,... | collective-permute-start | bytes 135176 | tf_op jit(solution)/shard_map/ppermute | solution.py:363
  29.5 3.5 %collective-permute-start.7 = (bf16[176,128]{1,0:T(8,128)(2,1)S(1)}, bf16[176,128]{1,0:T(8,128)(2,1)S(1)}, u32[]{:S(2)}, u32[]{:S(2)}) collective-permute-start(bf16[176,128]{1,0:T(8,128)(2,1)S(1)} %shard_map.83.x), channel_id=1, source_target_pairs={{0,5},{1,4},{2,7},{3,6},{4,1},{5,0},{6,3},{7,2},{8,13},{9,12},{10,... | collective-permute-start | bytes 135176 | tf_op jit(solution)/shard_map/ppermute | solution.py:363
  33.0 5.7 %collective-permute-start.10 = (bf16[176,128]{1,0:T(8,128)(2,1)S(1)}, bf16[176,128]{1,0:T(8,128)(2,1)S(1)}, u32[]{:S(2)}, u32[]{:S(2)}) collective-permute-start(bf16[176,128]{1,0:T(8,128)(2,1)S(1)} %shard_map.84.x), channel_id=1, source_target_pairs={{0,17},{1,16},{2,19},{3,18},{4,21},{5,20},{6,23},{7,22},{8,25},{9,... | collective-permute-start | bytes 135176 | tf_op jit(solution)/shard_map/ppermute | solution.py:363
  36.1 6.4 %collective-permute-start.12 = (bf16[4,64,128]{2,1,0:T(8,128)(2,1)S(1)}, bf16[4,64,128]{2,1,0:T(8,128)(2,1)S(1)}, u32[]{:S(2)}, u32[]{:S(2)}) collective-permute-start(bf16[4,64,128]{2,1,0:T(8,128)(2,1)S(1)} %get-tuple-element.80), channel_id=1, source_target_pairs={{0,1},{2,3},{1,0},{3,2},{4,5},{6,7},{5,4},{7,6},{8,9},{10,11},{9,8... | collective-permute-start | bytes 196616 | tf_op jit(solution)/shard_map/ppermute | solution.py:357
  36.2 6.4 %collective-permute-start.13 = (bf16[4,64,128]{2,1,0:T(8,128)(2,1)S(1)}, bf16[4,64,128]{2,1,0:T(8,128)(2,1)S(1)}, u32[]{:S(2)}, u32[]{:S(2)}) collective-permute-start(bf16[4,64,128]{2,1,0:T(8,128)(2,1)S(1)} %get-tuple-element.81), channel_id=1, source_target_pairs={{1,2},{3,0},{2,1},{0,3},{5,6},{7,4},{6,5},{4,7},{9,10},{11,8},{10,... | collective-permute-start | bytes 196616 | tf_op jit(solution)/shard_map/ppermute | solution.py:357
  38.8 3.7 %collective-permute-start.11 = (bf16[176,128]{1,0:T(8,128)(2,1)S(1)}, bf16[176,128]{1,0:T(8,128)(2,1)S(1)}, u32[]{:S(2)}, u32[]{:S(2)}) collective-permute-start(bf16[176,128]{1,0:T(8,128)(2,1)S(1)} %shard_map.85.mine), channel_id=1, source_target_pairs={{0,3},{1,2},{2,1},{3,0},{4,7},{5,6},{6,5},{7,4},{8,11},{9,10},{10,... | collective-permute-start | bytes 135176 | tf_op jit(solution)/shard_map/ppermute | solution.py:363
  42.5 4.7 %collective-permute-start.14 = (bf16[352,128]{1,0:T(8,128)(2,1)S(1)}, bf16[352,128]{1,0:T(8,128)(2,1)S(1)}, u32[]{:S(2)}, u32[]{:S(2)}) collective-permute-start(bf16[352,128]{1,0:T(8,128)(2,1)S(1)} %shard_map.87.mine), channel_id=1, source_target_pairs={{0,9},{1,8},{2,11},{3,10},{4,13},{5,12},{6,15},{7,14},{8,1},{9,0},... | collective-permute-start | bytes 270344 | tf_op jit(solution)/shard_map/ppermute | solution.py:363
  47.2 1.5 %collective-permute-start.15 = (bf16[704,128]{1,0:T(8,128)(2,1)S(1)}, bf16[704,128]{1,0:T(8,128)(2,1)S(1)}, u32[]{:S(2)}, u32[]{:S(2)}) collective-permute-start(bf16[704,128]{1,0:T(8,128)(2,1)S(1)} %shard_map.90.mine), channel_id=1, source_target_pairs={{0,1},{1,0},{2,3},{3,2},{4,5},{5,4},{6,7},{7,6},{8,9},{9,8},{10,11... | collective-permute-start | bytes 540680 | tf_op jit(solution)/shard_map/ppermute | solution.py:363

commit v17 on v16

--- a/solution.py
+++ b/solution.py
@@ -159,65 +159,73 @@
     lax.fori_loop(0, rows // 2, step, 0)
 
 
-def outer_kernel(near, far, w_ref, acc_ref, cols, out_ref):
+def gated(preact, grad):
+    sig = 1.0 / (1.0 + jnp.exp(-preact))
+    return (preact * sig).astype(BF16), (grad * sig * (1.0 + preact * (1.0 - sig))).astype(BF16)
+
+
+def outer_kernel(near, far, w_ref, acc_ref, grad_ref, cols, side_ref, near_ref, far_ref, h_ref):
     rows, channels, breadth = near.shape
     fill_columns(cols, near, far)
-
-    def step(t, carry):
-        y = 2 * t
-        for z, lines in enumerate(outer_terms(cols, w_ref, y)):
-            for b in range(2):
-                out_ref[z, y + b] = acc_ref[z, y + b] + lines[:, b * breadth : (b + 1) * breadth]
-        return carry
-
-    lax.fori_loop(0, rows // 2, step, 0)
-
-
-def gate_kernel(near, far, acc_ref, grad_ref, w_ref, edges, near_ref, far_ref, h_ref):
-    rows, channels, breadth = acc_ref.shape[1:]
+    even = is_even("gz")
+    for y in range(0, rows, 2):
+        outer = outer_terms(cols, w_ref, y)
+        for b in range(2):
+            found = []
+            for z in range(2):
+                preact = acc_ref[z, y + b] + outer[z][:, b * breadth : (b + 1) * breadth]
+                if y + b in (0, rows - 1):
+                    side_ref[z, b] = preact
+                else:
+                    h_ref[z, y + b], gate = gated(preact, grad_ref[z, y + b])
+                    found.append(gate)
+            if len(found) > 0:
+                near_ref[y + b] = choose(even, found[1], found[0])
+                far_ref[y + b] = choose(even, found[0], found[1])
+
+
+def gate_kernel(near, far, side_ref, near_in, far_in, h_in, grad_ref, w_ref, edges, near_ref, far_ref, h_ref):
+    rows = near_in.shape[0]
     fill_edges(edges, near, far)
-    sides = [edge_terms(edges, w_ref, side) for side in range(2)]
     even = is_even("gz")
-
-    def gate(y, extra):
+    for side, y in enumerate((0, rows - 1)):
+        terms = edge_terms(edges, w_ref, side)
         found = []
         for z in range(2):
-            preact = acc_ref[z, y] if extra is None else acc_ref[z, y] + extra[z]
-            sig = 1.0 / (1.0 + jnp.exp(-preact))
-            h_ref[z, y] = (preact * sig).astype(BF16)
-            found.append((grad_ref[z, y] * sig * (1.0 + preact * (1.0 - sig))).astype(BF16))
+            h_ref[z, y], gate = gated(side_ref[z, side] + terms[z], grad_ref[z, y])
+            found.append(gate)
         near_ref[y] = choose(even, found[1], found[0])
         far_ref[y] = choose(even, found[0], found[1])
-
-    gate(0, sides[0])
     for y in range(1, rows - 1):
-        gate(y, None)
-    gate(rows - 1, sides[1])
-
-
-def coarse_hidden(h_ref, a, b):
+        near_ref[y] = near_in[y]
+        far_ref[y] = far_in[y]
+        for z in range(2):
+            h_ref[z, y] = h_in[z, y]
+
+
+def coarse_hidden(h_ref):
     rows, channels, breadth = h_ref.shape[1:]
     source = lax.broadcasted_iota(jnp.int32, (2 * breadth, 2 * breadth), 0)
     target = lax.broadcasted_iota(jnp.int32, (2 * breadth, 2 * breadth), 1)
     wanted = 2 * (target % breadth) + target // breadth
     pick = jnp.where(source == wanted, 1.0, 0.0).astype(BF16)
-    pairs = []
-    for pair in range(rows // 4):
-        both = jnp.concatenate([h_ref[a, 4 * pair + b], h_ref[a, 4 * pair + 2 + b]], axis=1)
-        pairs.append(dot(both, pick).astype(BF16))
-    return jnp.concatenate(
-        [jnp.concatenate([x[:, e * breadth : (e + 1) * breadth] for x in pairs], axis=1) for e in range(2)],
-        axis=0,
-    )
+    pairs = rows // 4
+    both = [
+        jnp.concatenate([h_ref[a, 4 * pair + b], h_ref[a, 4 * pair + 2 + b]], axis=1)
+        for a in range(2) for b in range(2) for pair in range(pairs)
+    ]
+    picked = dot(jnp.concatenate(both, axis=0), pick).astype(BF16)
+    blocks = []
+    for tap in range(4):
+        parts = [picked[(tap * pairs + pair) * channels : (tap * pairs + pair + 1) * channels] for pair in range(pairs)]
+        for e in range(2):
+            blocks.append(jnp.concatenate([x[:, e * breadth : (e + 1) * breadth] for x in parts], axis=1))
+    return jnp.concatenate(blocks, axis=0)
 
 
 def section_kernel(h_ref, d_ref, out_ref):
-    coarse = None
-    for a in range(2):
-        for b in range(2):
-            term = dot(d_ref[a, b], coarse_hidden(h_ref, a, b))
-            coarse = term if coarse is None else coarse + term
-    out_ref[...] = coarse.astype(BF16)
+    down = jnp.concatenate([d_ref[a, b] for a in range(2) for b in range(2)], axis=1)
+    out_ref[...] = dot(down, coarse_hidden(h_ref)).astype(BF16)
 
 
 def weight_grad_kernel(inner, outer, edges, near, far, h_ref, cot_ref, keep, send, packed):
@@ -226,24 +234,31 @@
     even = is_even("gz")
     low = [choose(even, far[y], near[y]) for y in range(rows)]
     high = [choose(even, near[y], far[y]) for y in range(rows)]
-    gates = jnp.concatenate([jnp.concatenate(low, axis=1), jnp.concatenate(high, axis=1)], axis=0)
+    nothing = jnp.zeros((channels, breadth), BF16)
+
+    def shifted(lines):
+        return jnp.concatenate(
+            [jnp.concatenate([nothing] * b + lines + [nothing] * (2 - b), axis=1) for b in range(3)], axis=0
+        )
+
+    low, high = shifted(low), shifted(high)
+    both = jnp.concatenate([low, high], axis=0)
 
     def columns(p, q):
         if q in (0, rows + 1):
             return edges[p, 0 if q == 0 else 1]
         return inner[p - 1, q] if p in (1, 2) else outer[p // 3, q]
 
+    parts = []
+    for p in range(4):
+        lines = jnp.concatenate([columns(p, q) for q in range(rows + 2)], axis=1)
+        lhs = low if p == 0 else high if p == 3 else both
+        parts.append(lax.dot_general(lhs, lines, across, preferred_element_type=F32))
     lane = lax.broadcasted_iota(jnp.int32, (channels // 2, breadth), 1)
-    for b in range(3):
-        parts = []
-        for p in range(4):
-            across_rows = jnp.concatenate([columns(p, y + b) for y in range(rows)], axis=1)
-            lhs = gates[0:channels] if p == 0 else gates[channels:] if p == 3 else gates
-            parts.append(lax.dot_general(lhs, across_rows, across, preferred_element_type=F32))
-        for a in range(3):
-            low = parts[a][0:channels]
-            high = parts[a + 1] if a == 2 else parts[a + 1][channels:]
-            total = low + high
+    for a in range(3):
+        for b in range(3):
+            at = b * channels + (0 if a == 2 else 3 * channels)
+            total = parts[a][b * channels : (b + 1) * channels] + parts[a + 1][at : at + channels]
             base = (a * 3 + b) * 3 * channels // 2
             packed[base : base + channels] = total[:, 0:breadth]
             rest = jnp.concatenate([total[:, breadth:], total[:, breadth:]], axis=1)
@@ -251,11 +266,9 @@
             packed[base + channels : base + 3 * channels // 2] = mix
     base = 9 * 3 * channels // 2
     height = cot_ref.shape[0]
-    for a in range(2):
-        for b in range(2):
-            down = lax.dot_general(cot_ref[...], coarse_hidden(h_ref, a, b), across, preferred_element_type=F32)
-            at = base + (2 * a + b) * height
-            packed[at : at + height] = down
+    down = lax.dot_general(cot_ref[...], coarse_hidden(h_ref), across, preferred_element_type=F32)
+    for tap in range(4):
+        packed[base + tap * height : base + (tap + 1) * height] = down[:, tap * breadth : (tap + 1) * breadth]
     end = base + 4 * height
     if end < packed.shape[0]:
         packed[end:] = jnp.zeros((packed.shape[0] - end, packed.shape[1]), F32)
@@ -399,12 +412,13 @@
     near, far, acc = lax.optimization_barrier((*outside, acc))
     outside = (near, far)
     beside = swapped(*call(edges_kernel, [edge, edge], [], 0, (*own, *outside)), "gy")
-    outer, acc = call(
-        outer_kernel, [cols, (lines, F32)], [], conv_flops // 3, (*outside, conv_weight, acc)
+    outer, *inside = call(
+        outer_kernel, [cols, ((plane_count, 2, channels, breadth), F32), plane, plane, (lines, BF16)], [],
+        conv_flops // 3, (*outside, conv_weight, acc, hidden_grad),
     )
     edges, near, far, hidden = call(
         gate_kernel, [edge_cols, plane, plane, (lines, BF16)], [], conv_flops // 10,
-        (*beside, acc, hidden_grad, conv_weight),
+        (*beside, *inside, hidden_grad, conv_weight),
     )
     gates = (near, far)
 

time: 49.9 us -> 48.7 us (0.976)
  Pallas kernels: 12.6 us -> 10.7 us
  waiting for transfers between devices: 13.4 us -> 14.3 us
    pallas_call x18, Pallas kernels: 12.6 us -> 10.7 us  [call(): pl.pallas_call(kernel, out_shape=[jax.ShapeDtypeStruct(s, d) for s, d in...]
    ppermute x8, waiting for transfers between devices: 11.2 us -> 11.8 us  [flip(): lax.ppermute(cells, ('gz', 'gy'), [(i, i ^ mask) for i in range(lax.axis_...]
  transfers between devices with their start and end apart: 16 -> 16, of which waited for: 10 -> 10; matrix products, arithmetic and copies ran while one was open for 2% -> 2% of each run, Pallas kernels for 17% -> 16%
where the time goes in v17:
time: 48.7 us; the launch traced here: 48.5 us
  starting transfers between devices  20 us (41%)
  waiting for transfers between devices  14.3 us (29%)
  Pallas kernels  10.7 us (22%)
  local copies, waits for them, and re-layouts  2.7 us (6%)
  between operations  0.8 us (2%)
    ppermute x8, starting transfers between devices, swap(): return lax.ppermute(cells, axis, pairs + [(b, a) for a, b in pairs])  13.9 us
    ppermute x8, waiting for transfers between devices, flip(): lax.ppermute(cells, ('gz', 'gy'), [(i, i ^ mask) for i in range(lax.axis_...  11.8 us
    pallas_call x18, Pallas kernels, call(): pl.pallas_call(kernel, out_shape=[jax.ShapeDtypeStruct(s, d) for s, d in...  10.7 us
    ppermute x8, starting transfers between devices, flip(): lax.ppermute(cells, ('gz', 'gy'), [(i, i ^ mask) for i in range(lax.axis_...  6.14 us
    ppermute x8, waiting for transfers between devices, swap(): return lax.ppermute(cells, axis, pairs + [(b, a) for a, b in pairs])  2.47 us
    unnamed x11, local copies, waits for them, and re-layouts  2.18 us
  transfers between devices with their start and end apart: 16, of which 10 were waited for; matrix products, arithmetic and copies ran while one was open for 2% of the time, Pallas kernels for 16%

profile of v17, /device:TPU:0, one launch (start us, length us, event | category | flops | bytes accessed | tf_op | source)
XLA Modules:
  0.0 48.5 jit_solution(9856896385188762100)
XLA Ops:
  0.6 0.9 %copy-done.2 = bf16[64,2,8,128]{3,2,1,0:T(8,128)(2,1)S(1)} copy-done((bf16[64,2,8,128]{3,2,1,0:T(8,128)(2,1)S(1)}, bf16[64,2,8,128]{3,2,1,0:T(8,128)(2,1)}, u32[]{:S(2)}) %copy-start.2) | copy-done | bytes 262168
  1.6 0.2 shard_map.75
  1.8 3.0 %collective-permute-start = (bf16[8,64,128]{2,1,0:T(8,128)(2,1)S(1)}, bf16[8,64,128]{2,1,0:T(8,128)(2,1)S(1)}, u32[]{:S(2)}, u32[]{:S(2)}) collective-permute-start(bf16[8,64,128]{2,1,0:T(8,128)(2,1)S(1)} %get-tuple-element.50.near), channel_id=1, source_target_pairs={{0,4},{8,12},{16,20},{24,28},{4,0},{12,8},{20,16},{28,24},{1,5},{9... | collective-permute-start | bytes 393224 | tf_op jit(solution)/shard_map/ppermute | solution.py:370
  4.8 3.5 %collective-permute-start.1 = (bf16[8,64,128]{2,1,0:T(8,128)(2,1)S(1)}, bf16[8,64,128]{2,1,0:T(8,128)(2,1)S(1)}, u32[]{:S(2)}, u32[]{:S(2)}) collective-permute-start(bf16[8,64,128]{2,1,0:T(8,128)(2,1)S(1)} %get-tuple-element.51.far), channel_id=1, source_target_pairs={{4,8},{12,16},{20,24},{28,0},{8,4},{16,12},{24,20},{0,28},{5,9},{1... | collective-permute-start | bytes 393224 | tf_op jit(solution)/shard_map/ppermute | solution.py:370
  8.4 1.0 %copy-done = bf16[3,3,64,192]{3,2,1,0:T(8,128)(2,1)S(1)} copy-done((bf16[3,3,64,192]{3,2,1,0:T(8,128)(2,1)S(1)}, bf16[3,3,64,192]{3,2,1,0:T(8,128)(2,1)}, u32[]{:S(2)}) %copy-start) | copy-done | bytes 221208
  9.3 1.9 %shard_map.76 = (bf16[2,10,192,128]{3,2,1,0:T(8,128)(2,1)S(1)}, f32[2,8,64,128]{3,2,1,0:T(8,128)S(1)}, f32[2,8,64,128]{3,2,1,0:T(8,128)S(1)}) custom-call(bf16[8,64,128]{2,1,0:T(8,128)(2,1)S(1)} %get-tuple-element.50.near, bf16[8,64,128]{2,1,0:T(8,128)(2,1)S(1)} %get-tuple-element.51.far, bf16[3,3,64,192]{3,2,1,0:T(8,128)(2,1)S(1)} %copy-done, ...), custom_call_target="tpu_custom_call" | custom-call | flops 301989888 | bytes 2711552 | tf_op jit(solution)/shard_map/pallas_call | solution.py:20
  11.3 0.0 copy-start.1
  11.3 0.0 collective-permute-done.near.near_in
  11.3 1.2 %collective-permute-done.1.far.far_in = bf16[8,64,128]{2,1,0:T(8,128)(2,1)S(1)} collective-permute-done((bf16[8,64,128]{2,1,0:T(8,128)(2,1)S(1)}, bf16[8,64,128]{2,1,0:T(8,128)(2,1)S(1)}, u32[]{:S(2)}, u32[]{:S(2)}) %collective-permute-start.1) | collective-permute-done | bytes 131104 | tf_op jit(solution)/shard_map/ppermute | solution.py:370
  12.5 0.1 collective-permute-start.2
  12.6 1.6 %collective-permute-start.3 = (bf16[4,64,128]{2,1,0:T(8,128)(2,1)S(1)}, bf16[4,64,128]{2,1,0:T(8,128)(2,1)S(1)}, u32[]{:S(2)}, u32[]{:S(2)}) collective-permute-start(bf16[4,64,128]{2,1,0:T(8,128)(2,1)S(1)} %get-tuple-element.60), channel_id=1, source_target_pairs={{1,2},{3,0},{2,1},{0,3},{5,6},{7,4},{6,5},{4,7},{9,10},{11,8},{10,... | collective-permute-start | bytes 196616 | tf_op jit(solution)/shard_map/ppermute | solution.py:370
  14.2 1.0 %shard_map.77 = (bf16[2,10,192,128]{3,2,1,0:T(8,128)(2,1)S(1)}, f32[2,2,64,128]{3,2,1,0:T(8,128)S(1)}, bf16[8,64,128]{2,1,0:T(8,128)(2,1)S(1)}, bf16[8,64,128]{2...) custom-call(bf16[8,64,128]{2,1,0:T(8,128)(2,1)S(1)} %collective-permute-done.near.near_in, ...), custom_call_target="tpu_custom_call" | custom-call | flops 150994944 | bytes 3170304 | tf_op jit(solution)/shard_map/pallas_call | solution.py:20
  15.2 0.0 collective-permute-done.2.near
  15.3 1.2 %collective-permute-done.3.far = bf16[4,64,128]{2,1,0:T(8,128)(2,1)S(1)} collective-permute-done((bf16[4,64,128]{2,1,0:T(8,128)(2,1)S(1)}, bf16[4,64,128]{2,1,0:T(8,128)(2,1)S(1)}, u32[]{:S(2)}, u32[]{:S(2)}) %collective-permute-start.3) | collective-permute-done | bytes 65568 | tf_op jit(solution)/shard_map/ppermute | solution.py:370
  16.5 0.4 shard_map.79
  16.9 1.2 %shard_map.80 = (f32[704,128]{1,0:T(8,128)S(1)}, bf16[704,128]{1,0:T(8,128)(2,1)S(1)}) custom-call(bf16[2,10,192,128]{3,2,1,0:T(8,128)(2,1)S(1)} %get-tuple-element.52.inner, bf16[2,10,192,128]{3,2,1,0:T(8,128)(2,1)S(1)} %get-tuple-element.58.outer, bf16[4,2,192,128]{3,2,1,0:T(8,128)(2,1)S(1)} %get-tuple-element.65.edges, ...), custom_call_target="tpu_custom_call" | custom-call | flops 452984832 | bytes 3489792 | tf_op jit(solution)/shard_map/pallas_call | solution.py:20
  18.1 0.5 collective-permute-start.4
  18.6 1.0 %collective-permute-done.4.other = bf16[704,128]{1,0:T(8,128)(2,1)S(1)} collective-permute-done((bf16[704,128]{1,0:T(8,128)(2,1)S(1)}, bf16[704,128]{1,0:T(8,128)(2,1)S(1)}, u32[]{:S(2)}, u32[]{:S(2)}) %collective-permute-start.4) | collective-permute-done | bytes 180256 | tf_op jit(solution)/shard_map/ppermute | solution.py:376
  19.6 0.1 shard_map.81
  19.7 0.5 collective-permute-start.5
  20.2 1.5 %collective-permute-start.8 = (bf16[8,64,128]{2,1,0:T(8,128)(2,1)S(1)}, bf16[8,64,128]{2,1,0:T(8,128)(2,1)S(1)}, u32[]{:S(2)}, u32[]{:S(2)}) collective-permute-start(bf16[8,64,128]{2,1,0:T(8,128)(2,1)S(1)} %get-tuple-element.78.near), channel_id=1, source_target_pairs={{0,4},{8,12},{16,20},{24,28},{4,0},{12,8},{20,16},{28,24},{1,5},{9... | collective-permute-start | bytes 393224 | tf_op jit(solution)/shard_map/ppermute | solution.py:370
  21.7 2.4 %collective-permute-start.9 = (bf16[8,64,128]{2,1,0:T(8,128)(2,1)S(1)}, bf16[8,64,128]{2,1,0:T(8,128)(2,1)S(1)}, u32[]{:S(2)}, u32[]{:S(2)}) collective-permute-start(bf16[8,64,128]{2,1,0:T(8,128)(2,1)S(1)} %get-tuple-element.79.far), channel_id=1, source_target_pairs={{4,8},{12,16},{20,24},{28,0},{8,4},{16,12},{24,20},{0,28},{5,9},{1... | collective-permute-start | bytes 393224 | tf_op jit(solution)/shard_map/ppermute | solution.py:370
  24.1 0.1 collective-permute-done.5.other
  24.3 2.2 %collective-permute-start.6 = (bf16[176,128]{1,0:T(8,128)(2,1)S(1)}, bf16[176,128]{1,0:T(8,128)(2,1)S(1)}, u32[]{:S(2)}, u32[]{:S(2)}) collective-permute-start(bf16[176,128]{1,0:T(8,128)(2,1)S(1)} %get-tuple-element.77), channel_id=1, source_target_pairs={{0,3},{1,2},{2,1},{3,0},{4,7},{5,6},{6,5},{7,4},{8,11},{9,10},{10,... | collective-permute-start | bytes 135176 | tf_op jit(solution)/shard_map/ppermute | solution.py:376
  26.5 1.7 %collective-permute-done.6.y = bf16[176,128]{1,0:T(8,128)(2,1)S(1)} collective-permute-done((bf16[176,128]{1,0:T(8,128)(2,1)S(1)}, bf16[176,128]{1,0:T(8,128)(2,1)S(1)}, u32[]{:S(2)}, u32[]{:S(2)}) %collective-permute-start.6) | collective-permute-done | bytes 45088 | tf_op jit(solution)/shard_map/ppermute | solution.py:376
  28.2 0.3 collective-permute-start.7
  28.5 3.3 %collective-permute-done.7.y = bf16[176,128]{1,0:T(8,128)(2,1)S(1)} collective-permute-done((bf16[176,128]{1,0:T(8,128)(2,1)S(1)}, bf16[176,128]{1,0:T(8,128)(2,1)S(1)}, u32[]{:S(2)}, u32[]{:S(2)}) %collective-permute-start.7) | collective-permute-done | bytes 45088 | tf_op jit(solution)/shard_map/ppermute | solution.py:376
  31.8 0.0 collective-permute-done.8.near_in
  31.8 0.0 collective-permute-done.9.far_in
  31.8 1.3 %collective-permute-start.10 = (bf16[176,128]{1,0:T(8,128)(2,1)S(1)}, bf16[176,128]{1,0:T(8,128)(2,1)S(1)}, u32[]{:S(2)}, u32[]{:S(2)}) collective-permute-start(bf16[176,128]{1,0:T(8,128)(2,1)S(1)} %shard_map.84.x), channel_id=1, source_target_pairs={{0,17},{1,16},{2,19},{3,18},{4,21},{5,20},{6,23},{7,22},{8,25},{9,... | collective-permute-start | bytes 135176 | tf_op jit(solution)/shard_map/ppermute | solution.py:376
  33.1 0.3 copy.9
  33.4 1.1 %shard_map.86 = bf16[128,256]{1,0:T(8,128)(2,1)} custom-call(bf16[2,8,64,128]{3,2,1,0:T(8,128)(2,1)S(1)} %get-tuple-element.81.h_ref, bf16[2,2,128,128]{3,2,1,0:T(8,128)(2,1)S(1)} %copy-done.3), custom_call_target="tpu_custom_call" | custom-call | flops 45298484 | bytes 458752 | tf_op jit(solution)/shard_map/pallas_call | solution.py:20
  34.5 0.1 collective-permute-start.12
  34.6 1.6 %collective-permute-start.13 = (bf16[4,64,128]{2,1,0:T(8,128)(2,1)S(1)}, bf16[4,64,128]{2,1,0:T(8,128)(2,1)S(1)}, u32[]{:S(2)}, u32[]{:S(2)}) collective-permute-start(bf16[4,64,128]{2,1,0:T(8,128)(2,1)S(1)} %get-tuple-element.87), channel_id=1, source_target_pairs={{1,2},{3,0},{2,1},{0,3},{5,6},{7,4},{6,5},{4,7},{9,10},{11,8},{10,... | collective-permute-start | bytes 196616 | tf_op jit(solution)/shard_map/ppermute | solution.py:370
  36.2 1.3 %collective-permute-done.10.y = bf16[176,128]{1,0:T(8,128)(2,1)S(1)} collective-permute-done((bf16[176,128]{1,0:T(8,128)(2,1)S(1)}, bf16[176,128]{1,0:T(8,128)(2,1)S(1)}, u32[]{:S(2)}, u32[]{:S(2)}) %collective-permute-start.10) | collective-permute-done | bytes 45088 | tf_op jit(solution)/shard_map/ppermute | solution.py:376
  37.5 0.8 %collective-permute-start.11 = (bf16[176,128]{1,0:T(8,128)(2,1)S(1)}, bf16[176,128]{1,0:T(8,128)(2,1)S(1)}, u32[]{:S(2)}, u32[]{:S(2)}) collective-permute-start(bf16[176,128]{1,0:T(8,128)(2,1)S(1)} %shard_map.85.mine), channel_id=1, source_target_pairs={{0,3},{1,2},{2,1},{3,0},{4,7},{5,6},{6,5},{7,4},{8,11},{9,10},{10,... | collective-permute-start | bytes 135176 | tf_op jit(solution)/shard_map/ppermute | solution.py:376
  38.4 0.3 copy.10
  38.7 0.2 copy.11.w_ref
  38.9 2.3 %shard_map.88.acc_ref = f32[2,8,64,128]{3,2,1,0:T(8,128)S(1)} custom-call(bf16[8,64,128]{2,1,0:T(8,128)(2,1)S(1)} %get-tuple-element.78.near, bf16[8,64,128]{2,1,0:T(8,128)(2,1)S(1)} %get-tuple-element.79.far, bf16[8,64,128]{2,1,0:T(8,128)(2,1)S(1)} %collective-permute-done.8.near_in, bf16[8,64,128]{2,1,0:T(8,128)(2,1)S(1)} %collective-permute-done.9.far_in, ...), custom_call_target="tpu_custom_call" | custom-call | flops 452984832 | bytes 1269760 | tf_op jit(solution)/shard_map/pallas_call | solution.py:20
  41.2 0.1 collective-permute-done.11.other
  41.3 0.0 collective-permute-done.12.near
  41.3 0.0 collective-permute-done.13.far
  41.3 0.4 collective-permute-start.14
  41.6 1.3 %shard_map.91 = f32[1024,128]{1,0:T(8,128)} custom-call(bf16[4,64,128]{2,1,0:T(8,128)(2,1)S(1)} %collective-permute-done.12.near, bf16[4,64,128]{2,1,0:T(8,128)(2,1)S(1)} %collective-permute-done.13.far, f32[2,8,64,128]{3,2,1,0:T(8,128)S(1)} %shard_map.88.acc_ref, bf16[3,3,64,192]{3,2,1,0:T(8,128)(2,1)S(1)} %copy.11.w_ref), custom_call_target="tpu_custom_call" | custom-call | flops 45298484 | bytes 1400832 | tf_op jit(solution)/shard_map/pallas_call | solution.py:20
  43.0 3.0 %collective-permute-done.14.other = bf16[352,128]{1,0:T(8,128)(2,1)S(1)} collective-permute-done((bf16[352,128]{1,0:T(8,128)(2,1)S(1)}, bf16[352,128]{1,0:T(8,128)(2,1)S(1)}, u32[]{:S(2)}, u32[]{:S(2)}) %collective-permute-start.14) | collective-permute-done | bytes 90144 | tf_op jit(solution)/shard_map/ppermute | solution.py:376
  46.0 0.2 collective-permute-start.15
  46.2 1.3 %collective-permute-done.15.other = bf16[704,128]{1,0:T(8,128)(2,1)S(1)} collective-permute-done((bf16[704,128]{1,0:T(8,128)(2,1)S(1)}, bf16[704,128]{1,0:T(8,128)(2,1)S(1)}, u32[]{:S(2)}, u32[]{:S(2)}) %collective-permute-start.15) | collective-permute-done | bytes 180256 | tf_op jit(solution)/shard_map/ppermute | solution.py:376
  47.5 1.0 %shard_map.92 = (f32[3,3,64,192]{3,2,1,0:T(8,128)}, f32[2,2,128,128]{3,2,1,0:T(8,128)}) custom-call(bf16[704,128]{1,0:T(8,128)(2,1)S(1)} %shard_map.90.mine, bf16[704,128]{1,0:T(8,128)(2,1)S(1)} %collective-permute-done.15.other), custom_call_target="tpu_custom_call" | custom-call | bytes 1064960 | tf_op jit(solution)/shard_map/pallas_call | solution.py:20
  (16 shorter events, 0.2 us)
Async XLA Ops:
  0.6 1.0 %copy-start.2 = (bf16[64,2,8,128]{3,2,1,0:T(8,128)(2,1)S(1)}, bf16[64,2,8,128]{3,2,1,0:T(8,128)(2,1)}, u32[]{:S(2)}) copy-start(bf16[64,2,8,128]{3,2,1,0:T(8,128)(2,1)} %f_ref.1) | copy-start | bytes 786436
  1.6 6.8 %copy-start.3 = (bf16[2,2,128,128]{3,2,1,0:T(8,128)(2,1)S(1)}, bf16[2,2,128,128]{3,2,1,0:T(8,128)(2,1)}, u32[]{:S(2)}) copy-start(bf16[2,2,128,128]{3,2,1,0:T(8,128)(2,1)} %d_ref.3) | copy-start | bytes 393220
  1.6 6.8 %copy-start.4 = (bf16[128,1,256]{2,0,1:T(8,128)(2,1)S(1)}, bf16[128,1,256]{2,0,1:T(8,128)(2,1)}, u32[]{:S(2)}) copy-start(bf16[128,1,256]{2,0,1:T(8,128)(2,1)} %param.7) | copy-start | bytes 196612
  1.8 9.5 %collective-permute-start = (bf16[8,64,128]{2,1,0:T(8,128)(2,1)S(1)}, bf16[8,64,128]{2,1,0:T(8,128)(2,1)S(1)}, u32[]{:S(2)}, u32[]{:S(2)}) collective-permute-start(bf16[8,64,128]{2,1,0:T(8,128)(2,1)S(1)} %get-tuple-element.50.near), channel_id=1, source_target_pairs={{0,4},{8,12},{16,20},{24,28},{4,0},{12,8},{20,16},{28,24},{1,5},{9... | collective-permute-start | bytes 393224 | tf_op jit(solution)/shard_map/ppermute | solution.py:370
  4.8 7.7 %collective-permute-start.1 = (bf16[8,64,128]{2,1,0:T(8,128)(2,1)S(1)}, bf16[8,64,128]{2,1,0:T(8,128)(2,1)S(1)}, u32[]{:S(2)}, u32[]{:S(2)}) collective-permute-start(bf16[8,64,128]{2,1,0:T(8,128)(2,1)S(1)} %get-tuple-element.51.far), channel_id=1, source_target_pairs={{4,8},{12,16},{20,24},{28,0},{8,4},{16,12},{24,20},{0,28},{5,9},{1... | collective-permute-start | bytes 393224 | tf_op jit(solution)/shard_map/ppermute | solution.py:370
  8.4 1.0 %copy-start = (bf16[3,3,64,192]{3,2,1,0:T(8,128)(2,1)S(1)}, bf16[3,3,64,192]{3,2,1,0:T(8,128)(2,1)}, u32[]{:S(2)}) copy-start(bf16[3,3,64,192]{3,2,1,0:T(8,128)(2,1)} %w_ref.5) | copy-start | bytes 663556
  11.3 3.0 %copy-start.1 = (bf16[3,3,64,192]{3,2,1,0:T(8,128)(2,1)S(1)}, bf16[3,3,64,192]{3,2,1,0:T(8,128)(2,1)}, u32[]{:S(2)}) copy-start(bf16[3,3,64,192]{3,2,1,0:T(8,128)(2,1)} %w_ref.5) | copy-start | bytes 663556
  12.5 2.7 %collective-permute-start.2 = (bf16[4,64,128]{2,1,0:T(8,128)(2,1)S(1)}, bf16[4,64,128]{2,1,0:T(8,128)(2,1)S(1)}, u32[]{:S(2)}, u32[]{:S(2)}) collective-permute-start(bf16[4,64,128]{2,1,0:T(8,128)(2,1)S(1)} %get-tuple-element.59), channel_id=1, source_target_pairs={{0,1},{2,3},{1,0},{3,2},{4,5},{6,7},{5,4},{7,6},{8,9},{10,11},{9,8... | collective-permute-start | bytes 196616 | tf_op jit(solution)/shard_map/ppermute | solution.py:370
  12.6 3.9 %collective-permute-start.3 = (bf16[4,64,128]{2,1,0:T(8,128)(2,1)S(1)}, bf16[4,64,128]{2,1,0:T(8,128)(2,1)S(1)}, u32[]{:S(2)}, u32[]{:S(2)}) collective-permute-start(bf16[4,64,128]{2,1,0:T(8,128)(2,1)S(1)} %get-tuple-element.60), channel_id=1, source_target_pairs={{1,2},{3,0},{2,1},{0,3},{5,6},{7,4},{6,5},{4,7},{9,10},{11,8},{10,... | collective-permute-start | bytes 196616 | tf_op jit(solution)/shard_map/ppermute | solution.py:370
  18.1 1.5 %collective-permute-start.4 = (bf16[704,128]{1,0:T(8,128)(2,1)S(1)}, bf16[704,128]{1,0:T(8,128)(2,1)S(1)}, u32[]{:S(2)}, u32[]{:S(2)}) collective-permute-start(bf16[704,128]{1,0:T(8,128)(2,1)S(1)} %get-tuple-element.71), channel_id=1, source_target_pairs={{0,1},{1,0},{2,3},{3,2},{4,5},{5,4},{6,7},{7,6},{8,9},{9,8},{10,11... | collective-permute-start | bytes 540680 | tf_op jit(solution)/shard_map/ppermute | solution.py:376
  19.7 4.5 %collective-permute-start.5 = (bf16[352,128]{1,0:T(8,128)(2,1)S(1)}, bf16[352,128]{1,0:T(8,128)(2,1)S(1)}, u32[]{:S(2)}, u32[]{:S(2)}) collective-permute-start(bf16[352,128]{1,0:T(8,128)(2,1)S(1)} %get-tuple-element.75), channel_id=1, source_target_pairs={{0,9},{1,8},{2,11},{3,10},{4,13},{5,12},{6,15},{7,14},{8,1},{9,0},... | collective-permute-start | bytes 270344 | tf_op jit(solution)/shard_map/ppermute | solution.py:376
  20.2 11.6 %collective-permute-start.8 = (bf16[8,64,128]{2,1,0:T(8,128)(2,1)S(1)}, bf16[8,64,128]{2,1,0:T(8,128)(2,1)S(1)}, u32[]{:S(2)}, u32[]{:S(2)}) collective-permute-start(bf16[8,64,128]{2,1,0:T(8,128)(2,1)S(1)} %get-tuple-element.78.near), channel_id=1, source_target_pairs={{0,4},{8,12},{16,20},{24,28},{4,0},{12,8},{20,16},{28,24},{1,5},{9... | collective-permute-start | bytes 393224 | tf_op jit(solution)/shard_map/ppermute | solution.py:370
  21.7 10.1 %collective-permute-start.9 = (bf16[8,64,128]{2,1,0:T(8,128)(2,1)S(1)}, bf16[8,64,128]{2,1,0:T(8,128)(2,1)S(1)}, u32[]{:S(2)}, u32[]{:S(2)}) collective-permute-start(bf16[8,64,128]{2,1,0:T(8,128)(2,1)S(1)} %get-tuple-element.79.far), channel_id=1, source_target_pairs={{4,8},{12,16},{20,24},{28,0},{8,4},{16,12},{24,20},{0,28},{5,9},{1... | collective-permute-start | bytes 393224 | tf_op jit(solution)/shard_map/ppermute | solution.py:370
  24.3 3.9 %collective-permute-start.6 = (bf16[176,128]{1,0:T(8,128)(2,1)S(1)}, bf16[176,128]{1,0:T(8,128)(2,1)S(1)}, u32[]{:S(2)}, u32[]{:S(2)}) collective-permute-start(bf16[176,128]{1,0:T(8,128)(2,1)S(1)} %get-tuple-element.77), channel_id=1, source_target_pairs={{0,3},{1,2},{2,1},{3,0},{4,7},{5,6},{6,5},{7,4},{8,11},{9,10},{10,... | collective-permute-start | bytes 135176 | tf_op jit(solution)/shard_map/ppermute | solution.py:376
  28.2 3.5 %collective-permute-start.7 = (bf16[176,128]{1,0:T(8,128)(2,1)S(1)}, bf16[176,128]{1,0:T(8,128)(2,1)S(1)}, u32[]{:S(2)}, u32[]{:S(2)}) collective-permute-start(bf16[176,128]{1,0:T(8,128)(2,1)S(1)} %shard_map.83.x), channel_id=1, source_target_pairs={{0,5},{1,4},{2,7},{3,6},{4,1},{5,0},{6,3},{7,2},{8,13},{9,12},{10,... | collective-permute-start | bytes 135176 | tf_op jit(solution)/shard_map/ppermute | solution.py:376
  31.8 5.7 %collective-permute-start.10 = (bf16[176,128]{1,0:T(8,128)(2,1)S(1)}, bf16[176,128]{1,0:T(8,128)(2,1)S(1)}, u32[]{:S(2)}, u32[]{:S(2)}) collective-permute-start(bf16[176,128]{1,0:T(8,128)(2,1)S(1)} %shard_map.84.x), channel_id=1, source_target_pairs={{0,17},{1,16},{2,19},{3,18},{4,21},{5,20},{6,23},{7,22},{8,25},{9,... | collective-permute-start | bytes 135176 | tf_op jit(solution)/shard_map/ppermute | solution.py:376
  34.5 6.7 %collective-permute-start.12 = (bf16[4,64,128]{2,1,0:T(8,128)(2,1)S(1)}, bf16[4,64,128]{2,1,0:T(8,128)(2,1)S(1)}, u32[]{:S(2)}, u32[]{:S(2)}) collective-permute-start(bf16[4,64,128]{2,1,0:T(8,128)(2,1)S(1)} %get-tuple-element.86), channel_id=1, source_target_pairs={{0,1},{2,3},{1,0},{3,2},{4,5},{6,7},{5,4},{7,6},{8,9},{10,11},{9,8... | collective-permute-start | bytes 196616 | tf_op jit(solution)/shard_map/ppermute | solution.py:370
  34.6 6.6 %collective-permute-start.13 = (bf16[4,64,128]{2,1,0:T(8,128)(2,1)S(1)}, bf16[4,64,128]{2,1,0:T(8,128)(2,1)S(1)}, u32[]{:S(2)}, u32[]{:S(2)}) collective-permute-start(bf16[4,64,128]{2,1,0:T(8,128)(2,1)S(1)} %get-tuple-element.87), channel_id=1, source_target_pairs={{1,2},{3,0},{2,1},{0,3},{5,6},{7,4},{6,5},{4,7},{9,10},{11,8},{10,... | collective-permute-start | bytes 196616 | tf_op jit(solution)/shard_map/ppermute | solution.py:370
  37.5 3.7 %collective-permute-start.11 = (bf16[176,128]{1,0:T(8,128)(2,1)S(1)}, bf16[176,128]{1,0:T(8,128)(2,1)S(1)}, u32[]{:S(2)}, u32[]{:S(2)}) collective-permute-start(bf16[176,128]{1,0:T(8,128)(2,1)S(1)} %shard_map.85.mine), channel_id=1, source_target_pairs={{0,3},{1,2},{2,1},{3,0},{4,7},{5,6},{6,5},{7,4},{8,11},{9,10},{10,... | collective-permute-start | bytes 135176 | tf_op jit(solution)/shard_map/ppermute | solution.py:376
  41.3 4.7 %collective-permute-start.14 = (bf16[352,128]{1,0:T(8,128)(2,1)S(1)}, bf16[352,128]{1,0:T(8,128)(2,1)S(1)}, u32[]{:S(2)}, u32[]{:S(2)}) collective-permute-start(bf16[352,128]{1,0:T(8,128)(2,1)S(1)} %shard_map.87.mine), channel_id=1, source_target_pairs={{0,9},{1,8},{2,11},{3,10},{4,13},{5,12},{6,15},{7,14},{8,1},{9,0},... | collective-permute-start | bytes 270344 | tf_op jit(solution)/shard_map/ppermute | solution.py:376
  46.0 1.5 %collective-permute-start.15 = (bf16[704,128]{1,0:T(8,128)(2,1)S(1)}, bf16[704,128]{1,0:T(8,128)(2,1)S(1)}, u32[]{:S(2)}, u32[]{:S(2)}) collective-permute-start(bf16[704,128]{1,0:T(8,128)(2,1)S(1)} %shard_map.90.mine), channel_id=1, source_target_pairs={{0,1},{1,0},{2,3},{3,2},{4,5},{5,4},{6,7},{7,6},{8,9},{9,8},{10,11... | collective-permute-start | bytes 540680 | tf_op jit(solution)/shard_map/ppermute | solution.py:376

commit v18 on v17

--- a/solution.py
+++ b/solution.py
@@ -36,16 +36,31 @@
     return jnp.where(jnp.broadcast_to(cond, yes.shape), yes, no)
 
 
-def lines_kernel(f_ref, near_ref, far_ref, wide):
+def lines_kernel(f_ref, near_ref, far_ref, near_row, far_row, wide):
     channels, planes, rows, breadth = f_ref.shape
     wide[...] = f_ref[...].astype(F32).reshape(channels * planes * rows, breadth)
     even = is_even("gz")
+    ends = {}
     for y in range(rows):
-        low, high = (
+        low, high = ends[y] = [
             wide[pl.ds(z * rows + y, channels, stride=planes * rows), :].astype(BF16) for z in range(2)
-        )
+        ]
         near_ref[y] = choose(even, high, low)
         far_ref[y] = choose(even, low, high)
+    even_y = is_even("gy")
+    for z in range(2):
+        near_row[z] = choose(even_y, ends[rows - 1][z], ends[0][z])
+        far_row[z] = choose(even_y, ends[0][z], ends[rows - 1][z])
+
+
+def outer_rows_kernel(near_in, far_in, near_ref, far_ref):
+    rows = near_in.shape[0]
+    even_z, even_y = is_even("gz"), is_even("gy")
+    for p, (one, other) in enumerate(((far_in, near_in), (near_in, far_in))):
+        first = choose(even_z, one[0], other[0])
+        last = choose(even_z, one[rows - 1], other[rows - 1])
+        near_ref[p] = choose(even_y, last, first)
+        far_ref[p] = choose(even_y, first, last)
 
 
 def edges_kernel(near, far, near_in, far_in, near_ref, far_ref):
@@ -72,7 +87,7 @@
     cols[p, q, 2 * channels : 3 * channels] = pltpu.roll(wide, line.shape[1] - 1, 1).astype(BF16)
 
 
-def fill_columns(cols, near, far):
+def fill_columns(cols, near, far, near_row=None, far_row=None):
     rows = near.shape[0]
     even = is_even("gz")
 
@@ -82,16 +97,19 @@
         return carry
 
     lax.fori_loop(0, rows, step, 0, unroll=2)
+    if near_row is not None:
+        fill_rows(cols, near_row, far_row, 0, rows + 1)
+        return
     for p in range(2):
         for q in (0, rows + 1):
             cols[p, q] = jnp.zeros(cols.shape[2:], BF16)
 
 
-def fill_edges(cols, near, far):
+def fill_rows(cols, near, far, below, above):
     even = is_even("gy")
-    for p in range(4):
-        put_columns(cols, p, 0, choose(even, far[p], near[p]))
-        put_columns(cols, p, 1, choose(even, near[p], far[p]))
+    for p in range(near.shape[0]):
+        put_columns(cols, p, below, choose(even, far[p], near[p]))
+        put_columns(cols, p, above, choose(even, near[p], far[p]))
 
 
 def dot(lhs, rhs):
@@ -132,9 +150,9 @@
     return acc[half:] + dot(w_ref[0, b], edges[0, side]), acc[:half] + dot(w_ref[2, b], edges[3, side])
 
 
-def inner_kernel(near, far, w_ref, d_ref, cot_ref, cols, acc_ref, grad_ref, up):
+def inner_kernel(near, far, near_row, far_row, w_ref, d_ref, cot_ref, cols, acc_ref, grad_ref, up):
     rows, channels, breadth = near.shape
-    fill_columns(cols, near, far)
+    fill_columns(cols, near, far, near_row, far_row)
     source = lax.broadcasted_iota(jnp.int32, (breadth, 2 * breadth), 0)
     target = lax.broadcasted_iota(jnp.int32, (breadth, 2 * breadth), 1)
     spread = jnp.where(source == target // 2, 1.0, 0.0).astype(BF16)
@@ -186,10 +204,10 @@
 
 def gate_kernel(near, far, side_ref, near_in, far_in, h_in, grad_ref, w_ref, edges, near_ref, far_ref, h_ref):
     rows = near_in.shape[0]
-    fill_edges(edges, near, far)
+    fill_rows(edges, near, far, 0, 1)
     even = is_even("gz")
     for side, y in enumerate((0, rows - 1)):
-        terms = edge_terms(edges, w_ref, side)
+        terms = [dot(w_ref[2 * z, 2 * side], edges[z, side]) for z in range(2)]
         found = []
         for z in range(2):
             h_ref[z, y], gate = gated(side_ref[z, side] + terms[z], grad_ref[z, y])
@@ -245,9 +263,9 @@
     both = jnp.concatenate([low, high], axis=0)
 
     def columns(p, q):
-        if q in (0, rows + 1):
-            return edges[p, 0 if q == 0 else 1]
-        return inner[p - 1, q] if p in (1, 2) else outer[p // 3, q]
+        if p in (1, 2):
+            return inner[p - 1, q]
+        return edges[p // 3, q // (rows + 1)] if q in (0, rows + 1) else outer[p // 3, q]
 
     parts = []
     for p in range(4):
@@ -336,7 +354,7 @@
 
 def field_edges_kernel(near, far, acc_ref, w_ref, out_ref, edges):
     rows, channels, breadth = acc_ref.shape[1:]
-    fill_edges(edges, near, far)
+    fill_rows(edges, near, far, 0, 1)
     sides = [edge_terms(edges, w_ref, side) for side in range(2)]
     for z in range(2):
         for y in range(rows):
@@ -400,24 +418,27 @@
     lines = (plane_count, row_count, channels, breadth)
     conv_flops = 2 * 27 * channels * channels * plane_count * row_count * breadth
 
-    own = call(
-        lines_kernel, [plane, plane], [((channels * plane_count * row_count, breadth), F32)], 0, (features,)
+    pair = ((plane_count, channels, breadth), BF16)
+    *own, near_row, far_row = call(
+        lines_kernel, [plane, plane, pair, pair],
+        [((channels * plane_count * row_count, breadth), F32)], 0, (features,),
     )
     outside = swapped(*own, "gz")
+    beside = swapped(near_row, far_row, "gy")
     inner, acc, hidden_grad = call(
         inner_kernel, [cols, (lines, F32), (lines, F32)],
         [((out_channels, row_count // 2 * breadth), BF16)],
-        2 * conv_flops // 3, (*own, conv_weight, down_weight, cot),
+        2 * conv_flops // 3, (*own, *beside, conv_weight, down_weight, cot),
     )
     near, far, acc = lax.optimization_barrier((*outside, acc))
     outside = (near, far)
-    beside = swapped(*call(edges_kernel, [edge, edge], [], 0, (*own, *outside)), "gy")
+    beside = swapped(*call(outer_rows_kernel, [pair, pair], [], 0, outside), "gy")
     outer, *inside = call(
         outer_kernel, [cols, ((plane_count, 2, channels, breadth), F32), plane, plane, (lines, BF16)], [],
         conv_flops // 3, (*outside, conv_weight, acc, hidden_grad),
     )
     edges, near, far, hidden = call(
-        gate_kernel, [edge_cols, plane, plane, (lines, BF16)], [], conv_flops // 10,
+        gate_kernel, [((plane_count, 2, 3 * channels, breadth), BF16), plane, plane, (lines, BF16)], [], conv_flops // 10,
         (*beside, *inside, hidden_grad, conv_weight),
     )
     gates = (near, far)

time: 48.7 us -> 50.9 us (1.045)
  waiting for transfers between devices: 14.3 us -> 17.5 us
  starting transfers between devices: 20 us -> 19.1 us
    ppermute x8, waiting for transfers between devices: 11.8 us -> 14.5 us  [flip(): lax.ppermute(cells, ('gz', 'gy'), [(i, i ^ mask) for i in range(lax.axis_...]
    ppermute x8, starting transfers between devices: 6.14 us -> 4.43 us  [flip(): lax.ppermute(cells, ('gz', 'gy'), [(i, i ^ mask) for i in range(lax.axis_...]
    ppermute x8 -> x10, starting transfers between devices: 13.9 us -> 14.7 us  [swap(): return lax.ppermute(cells, axis, pairs + [(b, a) for a, b in pairs])]
    ppermute x8 -> x10, waiting for transfers between devices: 2.47 us -> 2.96 us  [swap(): return lax.ppermute(cells, axis, pairs + [(b, a) for a, b in pairs])]
  transfers between devices with their start and end apart: 16 -> 18, of which waited for: 10 -> 9; matrix products, arithmetic and copies ran while one was open for 2% -> 2% of each run, Pallas kernels for 16% -> 15%
where the time goes in v18:
time: 50.9 us; the launch traced here: 50.7 us
  starting transfers between devices  19.1 us (38%)
  waiting for transfers between devices  17.5 us (34%)
  Pallas kernels  10.6 us (21%)
  local copies, waits for them, and re-layouts  2.7 us (5%)
  between operations  0.84 us (2%)
    ppermute x10, starting transfers between devices, swap(): return lax.ppermute(cells, axis, pairs + [(b, a) for a, b in pairs])  14.7 us
    ppermute x8, waiting for transfers between devices, flip(): lax.ppermute(cells, ('gz', 'gy'), [(i, i ^ mask) for i in range(lax.axis_...  14.5 us
    pallas_call x18, Pallas kernels, call(): pl.pallas_call(kernel, out_shape=[jax.ShapeDtypeStruct(s, d) for s, d in...  10.6 us
    ppermute x8, starting transfers between devices, flip(): lax.ppermute(cells, ('gz', 'gy'), [(i, i ^ mask) for i in range(lax.axis_...  4.43 us
    ppermute x10, waiting for transfers between devices, swap(): return lax.ppermute(cells, axis, pairs + [(b, a) for a, b in pairs])  2.96 us
    unnamed x11, local copies, waits for them, and re-layouts  2.18 us
  transfers between devices with their start and end apart: 18, of which 9 were waited for; matrix products, arithmetic and copies ran while one was open for 2% of the time, Pallas kernels for 15%

profile of v18, /device:TPU:0, one launch (start us, length us, event | category | flops | bytes accessed | tf_op | source)
XLA Modules:
  0.0 50.7 jit_solution(51105333401789943)
XLA Ops:
  0.6 0.9 %copy-done.2 = bf16[64,2,8,128]{3,2,1,0:T(8,128)(2,1)S(1)} copy-done((bf16[64,2,8,128]{3,2,1,0:T(8,128)(2,1)S(1)}, bf16[64,2,8,128]{3,2,1,0:T(8,128)(2,1)}, u32[]{:S(2)}) %copy-start.2) | copy-done | bytes 262168
  1.6 0.2 shard_map.75
  1.8 3.0 %collective-permute-start.2 = (bf16[8,64,128]{2,1,0:T(8,128)(2,1)S(1)}, bf16[8,64,128]{2,1,0:T(8,128)(2,1)S(1)}, u32[]{:S(2)}, u32[]{:S(2)}) collective-permute-start(bf16[8,64,128]{2,1,0:T(8,128)(2,1)S(1)} %get-tuple-element.52.near), channel_id=1, source_target_pairs={{0,4},{8,12},{16,20},{24,28},{4,0},{12,8},{20,16},{28,24},{1,5},{9... | collective-permute-start | bytes 393224 | tf_op jit(solution)/shard_map/ppermute | solution.py:388
  4.8 3.5 %collective-permute-start.3 = (bf16[8,64,128]{2,1,0:T(8,128)(2,1)S(1)}, bf16[8,64,128]{2,1,0:T(8,128)(2,1)S(1)}, u32[]{:S(2)}, u32[]{:S(2)}) collective-permute-start(bf16[8,64,128]{2,1,0:T(8,128)(2,1)S(1)} %get-tuple-element.53.far), channel_id=1, source_target_pairs={{4,8},{12,16},{20,24},{28,0},{8,4},{16,12},{24,20},{0,28},{5,9},{1... | collective-permute-start | bytes 393224 | tf_op jit(solution)/shard_map/ppermute | solution.py:388
  8.4 0.0 collective-permute-start
  8.4 1.6 %collective-permute-start.1 = (bf16[2,64,128]{2,1,0:T(8,128)(2,1)S(1)}, bf16[2,64,128]{2,1,0:T(8,128)(2,1)S(1)}, u32[]{:S(2)}, u32[]{:S(2)}) collective-permute-start(bf16[2,64,128]{2,1,0:T(8,128)(2,1)S(1)} %get-tuple-element.55), channel_id=1, source_target_pairs={{1,2},{3,0},{2,1},{0,3},{5,6},{7,4},{6,5},{4,7},{9,10},{11,8},{10,... | collective-permute-start | bytes 98312 | tf_op jit(solution)/shard_map/ppermute | solution.py:388
  10.0 1.7 %collective-permute-done.1.far_row = bf16[2,64,128]{2,1,0:T(8,128)(2,1)S(1)} collective-permute-done((bf16[2,64,128]{2,1,0:T(8,128)(2,1)S(1)}, bf16[2,64,128]{2,1,0:T(8,128)(2,1)S(1)}, u32[]{:S(2)}, u32[]{:S(2)}) %collective-permute-start.1) | collective-permute-done | bytes 32800 | tf_op jit(solution)/shard_map/ppermute | solution.py:388
  11.7 1.0 %copy-done = bf16[3,3,64,192]{3,2,1,0:T(8,128)(2,1)S(1)} copy-done((bf16[3,3,64,192]{3,2,1,0:T(8,128)(2,1)S(1)}, bf16[3,3,64,192]{3,2,1,0:T(8,128)(2,1)}, u32[]{:S(2)}) %copy-start) | copy-done | bytes 221208
  12.7 1.9 %shard_map.76 = (bf16[2,10,192,128]{3,2,1,0:T(8,128)(2,1)S(1)}, f32[2,8,64,128]{3,2,1,0:T(8,128)S(1)}, f32[2,8,64,128]{3,2,1,0:T(8,128)S(1)}) custom-call(bf16[8,64,128]{2,1,0:T(8,128)(2,1)S(1)} %get-tuple-element.52.near, bf16[8,64,128]{2,1,0:T(8,128)(2,1)S(1)} %get-tuple-element.53.far, bf16[2,64,128]{2,1,0:T(8,128)(2,1)S(1)} %collective-permute-done.near_row, ...), custom_call_target="tpu_custom_call" | custom-call | flops 301989888 | bytes 2777088 | tf_op jit(solution)/shard_map/pallas_call | solution.py:20
  14.6 0.0 collective-permute-done.2.near.near_in
  14.6 0.0 collective-permute-done.3.far.far_in
  14.7 0.9 %collective-permute-start.4 = (bf16[2,64,128]{2,1,0:T(8,128)(2,1)S(1)}, bf16[2,64,128]{2,1,0:T(8,128)(2,1)S(1)}, u32[]{:S(2)}, u32[]{:S(2)}) collective-permute-start(bf16[2,64,128]{2,1,0:T(8,128)(2,1)S(1)} %get-tuple-element.63), channel_id=1, source_target_pairs={{0,1},{2,3},{1,0},{3,2},{4,5},{6,7},{5,4},{7,6},{8,9},{10,11},{9,8... | collective-permute-start | bytes 98312 | tf_op jit(solution)/shard_map/ppermute | solution.py:388
  15.5 1.2 %collective-permute-start.5 = (bf16[2,64,128]{2,1,0:T(8,128)(2,1)S(1)}, bf16[2,64,128]{2,1,0:T(8,128)(2,1)S(1)}, u32[]{:S(2)}, u32[]{:S(2)}) collective-permute-start(bf16[2,64,128]{2,1,0:T(8,128)(2,1)S(1)} %get-tuple-element.64), channel_id=1, source_target_pairs={{1,2},{3,0},{2,1},{0,3},{5,6},{7,4},{6,5},{4,7},{9,10},{11,8},{10,... | collective-permute-start | bytes 98312 | tf_op jit(solution)/shard_map/ppermute | solution.py:388
  16.7 1.0 %shard_map.77 = (bf16[2,10,192,128]{3,2,1,0:T(8,128)(2,1)S(1)}, f32[2,2,64,128]{3,2,1,0:T(8,128)S(1)}, bf16[8,64,128]{2,1,0:T(8,128)(2,1)S(1)}, bf16[8,64,128]{2...) custom-call(bf16[8,64,128]{2,1,0:T(8,128)(2,1)S(1)} %collective-permute-done.2.near.near_in, ...), custom_call_target="tpu_custom_call" | custom-call | flops 150994944 | bytes 3170304 | tf_op jit(solution)/shard_map/pallas_call | solution.py:20
  17.7 0.0 collective-permute-done.4.near
  17.7 1.2 %collective-permute-done.5.far = bf16[2,64,128]{2,1,0:T(8,128)(2,1)S(1)} collective-permute-done((bf16[2,64,128]{2,1,0:T(8,128)(2,1)S(1)}, bf16[2,64,128]{2,1,0:T(8,128)(2,1)S(1)}, u32[]{:S(2)}, u32[]{:S(2)}) %collective-permute-start.5) | collective-permute-done | bytes 32800 | tf_op jit(solution)/shard_map/ppermute | solution.py:388
  18.9 0.3 shard_map.79
  19.3 1.2 %shard_map.80 = (f32[704,128]{1,0:T(8,128)S(1)}, bf16[704,128]{1,0:T(8,128)(2,1)S(1)}) custom-call(bf16[2,10,192,128]{3,2,1,0:T(8,128)(2,1)S(1)} %get-tuple-element.56.inner, bf16[2,10,192,128]{3,2,1,0:T(8,128)(2,1)S(1)} %get-tuple-element.62.outer, bf16[2,2,192,128]{3,2,1,0:T(8,128)(2,1)S(1)} %get-tuple-element.69.edges, ...), custom_call_target="tpu_custom_call" | custom-call | flops 452984832 | bytes 3293184 | tf_op jit(solution)/shard_map/pallas_call | solution.py:20
  20.5 0.2 collective-permute-start.6
  20.7 1.3 %collective-permute-done.6.other = bf16[704,128]{1,0:T(8,128)(2,1)S(1)} collective-permute-done((bf16[704,128]{1,0:T(8,128)(2,1)S(1)}, bf16[704,128]{1,0:T(8,128)(2,1)S(1)}, u32[]{:S(2)}, u32[]{:S(2)}) %collective-permute-start.6) | collective-permute-done | bytes 180256 | tf_op jit(solution)/shard_map/ppermute | solution.py:394
  22.0 0.1 shard_map.81
  22.0 0.1 collective-permute-start.7
  22.1 0.8 %collective-permute-start.10 = (bf16[8,64,128]{2,1,0:T(8,128)(2,1)S(1)}, bf16[8,64,128]{2,1,0:T(8,128)(2,1)S(1)}, u32[]{:S(2)}, u32[]{:S(2)}) collective-permute-start(bf16[8,64,128]{2,1,0:T(8,128)(2,1)S(1)} %get-tuple-element.82.near), channel_id=1, source_target_pairs={{0,4},{8,12},{16,20},{24,28},{4,0},{12,8},{20,16},{28,24},{1,5},{9... | collective-permute-start | bytes 393224 | tf_op jit(solution)/shard_map/ppermute | solution.py:388
  22.9 1.9 %collective-permute-start.11 = (bf16[8,64,128]{2,1,0:T(8,128)(2,1)S(1)}, bf16[8,64,128]{2,1,0:T(8,128)(2,1)S(1)}, u32[]{:S(2)}, u32[]{:S(2)}) collective-permute-start(bf16[8,64,128]{2,1,0:T(8,128)(2,1)S(1)} %get-tuple-element.83.far), channel_id=1, source_target_pairs={{4,8},{12,16},{20,24},{28,0},{8,4},{16,12},{24,20},{0,28},{5,9},{1... | collective-permute-start | bytes 393224 | tf_op jit(solution)/shard_map/ppermute | solution.py:388
  24.9 1.8 %collective-permute-done.7.other = bf16[352,128]{1,0:T(8,128)(2,1)S(1)} collective-permute-done((bf16[352,128]{1,0:T(8,128)(2,1)S(1)}, bf16[352,128]{1,0:T(8,128)(2,1)S(1)}, u32[]{:S(2)}, u32[]{:S(2)}) %collective-permute-start.7) | collective-permute-done | bytes 90144 | tf_op jit(solution)/shard_map/ppermute | solution.py:394
  26.7 1.9 %collective-permute-start.8 = (bf16[176,128]{1,0:T(8,128)(2,1)S(1)}, bf16[176,128]{1,0:T(8,128)(2,1)S(1)}, u32[]{:S(2)}, u32[]{:S(2)}) collective-permute-start(bf16[176,128]{1,0:T(8,128)(2,1)S(1)} %get-tuple-element.81), channel_id=1, source_target_pairs={{0,3},{1,2},{2,1},{3,0},{4,7},{5,6},{6,5},{7,4},{8,11},{9,10},{10,... | collective-permute-start | bytes 135176 | tf_op jit(solution)/shard_map/ppermute | solution.py:394
  28.7 1.7 %collective-permute-done.8.y = bf16[176,128]{1,0:T(8,128)(2,1)S(1)} collective-permute-done((bf16[176,128]{1,0:T(8,128)(2,1)S(1)}, bf16[176,128]{1,0:T(8,128)(2,1)S(1)}, u32[]{:S(2)}, u32[]{:S(2)}) %collective-permute-start.8) | collective-permute-done | bytes 45088 | tf_op jit(solution)/shard_map/ppermute | solution.py:394
  30.4 0.1 collective-permute-start.9
  30.5 3.5 %collective-permute-done.9.y = bf16[176,128]{1,0:T(8,128)(2,1)S(1)} collective-permute-done((bf16[176,128]{1,0:T(8,128)(2,1)S(1)}, bf16[176,128]{1,0:T(8,128)(2,1)S(1)}, u32[]{:S(2)}, u32[]{:S(2)}) %collective-permute-start.9) | collective-permute-done | bytes 45088 | tf_op jit(solution)/shard_map/ppermute | solution.py:394
  34.0 0.0 collective-permute-done.10.near_in
  34.0 0.0 collective-permute-done.11.far_in
  34.0 0.4 collective-permute-start.12
  34.4 0.3 copy.9
  34.7 1.1 %shard_map.86 = bf16[128,256]{1,0:T(8,128)(2,1)} custom-call(bf16[2,8,64,128]{3,2,1,0:T(8,128)(2,1)S(1)} %get-tuple-element.85.h_ref, bf16[2,2,128,128]{3,2,1,0:T(8,128)(2,1)S(1)} %copy-done.3), custom_call_target="tpu_custom_call" | custom-call | flops 45298484 | bytes 458752 | tf_op jit(solution)/shard_map/pallas_call | solution.py:20
  35.8 0.5 %collective-permute-start.14 = (bf16[4,64,128]{2,1,0:T(8,128)(2,1)S(1)}, bf16[4,64,128]{2,1,0:T(8,128)(2,1)S(1)}, u32[]{:S(2)}, u32[]{:S(2)}) collective-permute-start(bf16[4,64,128]{2,1,0:T(8,128)(2,1)S(1)} %get-tuple-element.90), channel_id=1, source_target_pairs={{0,1},{2,3},{1,0},{3,2},{4,5},{6,7},{5,4},{7,6},{8,9},{10,11},{9,8... | collective-permute-start | bytes 196616 | tf_op jit(solution)/shard_map/ppermute | solution.py:388
  36.4 1.2 %collective-permute-start.15 = (bf16[4,64,128]{2,1,0:T(8,128)(2,1)S(1)}, bf16[4,64,128]{2,1,0:T(8,128)(2,1)S(1)}, u32[]{:S(2)}, u32[]{:S(2)}) collective-permute-start(bf16[4,64,128]{2,1,0:T(8,128)(2,1)S(1)} %get-tuple-element.91), channel_id=1, source_target_pairs={{1,2},{3,0},{2,1},{0,3},{5,6},{7,4},{6,5},{4,7},{9,10},{11,8},{10,... | collective-permute-start | bytes 196616 | tf_op jit(solution)/shard_map/ppermute | solution.py:388
  37.5 2.1 %collective-permute-done.12.y = bf16[176,128]{1,0:T(8,128)(2,1)S(1)} collective-permute-done((bf16[176,128]{1,0:T(8,128)(2,1)S(1)}, bf16[176,128]{1,0:T(8,128)(2,1)S(1)}, u32[]{:S(2)}, u32[]{:S(2)}) %collective-permute-start.12) | collective-permute-done | bytes 45088 | tf_op jit(solution)/shard_map/ppermute | solution.py:394
  39.7 1.2 %collective-permute-start.13 = (bf16[176,128]{1,0:T(8,128)(2,1)S(1)}, bf16[176,128]{1,0:T(8,128)(2,1)S(1)}, u32[]{:S(2)}, u32[]{:S(2)}) collective-permute-start(bf16[176,128]{1,0:T(8,128)(2,1)S(1)} %shard_map.85.mine), channel_id=1, source_target_pairs={{0,3},{1,2},{2,1},{3,0},{4,7},{5,6},{6,5},{7,4},{8,11},{9,10},{10,... | collective-permute-start | bytes 135176 | tf_op jit(solution)/shard_map/ppermute | solution.py:394
  40.9 0.3 copy.10
  41.2 0.2 copy.11.w_ref
  41.4 2.3 %shard_map.88.acc_ref = f32[2,8,64,128]{3,2,1,0:T(8,128)S(1)} custom-call(bf16[8,64,128]{2,1,0:T(8,128)(2,1)S(1)} %get-tuple-element.82.near, bf16[8,64,128]{2,1,0:T(8,128)(2,1)S(1)} %get-tuple-element.83.far, bf16[8,64,128]{2,1,0:T(8,128)(2,1)S(1)} %collective-permute-done.10.near_in, bf16[8,64,128]{2,1,0:T(8,128)(2,1)S(1)} %collective-permute-done.11.far_in, ...), custom_call_target="tpu_custom_call" | custom-call | flops 452984832 | bytes 1269760 | tf_op jit(solution)/shard_map/pallas_call | solution.py:20
  43.8 0.0 collective-permute-done.14.near
  43.8 0.1 collective-permute-start.16
  43.9 1.3 %shard_map.91 = f32[1024,128]{1,0:T(8,128)} custom-call(bf16[4,64,128]{2,1,0:T(8,128)(2,1)S(1)} %collective-permute-done.14.near, bf16[4,64,128]{2,1,0:T(8,128)(2,1)S(1)} %collective-permute-done.15.far, f32[2,8,64,128]{3,2,1,0:T(8,128)S(1)} %shard_map.88.acc_ref, bf16[3,3,64,192]{3,2,1,0:T(8,128)(2,1)S(1)} %copy.11.w_ref), custom_call_target="tpu_custom_call" | custom-call | flops 45298484 | bytes 1400832 | tf_op jit(solution)/shard_map/pallas_call | solution.py:20
  45.2 3.0 %collective-permute-done.16.other = bf16[352,128]{1,0:T(8,128)(2,1)S(1)} collective-permute-done((bf16[352,128]{1,0:T(8,128)(2,1)S(1)}, bf16[352,128]{1,0:T(8,128)(2,1)S(1)}, u32[]{:S(2)}, u32[]{:S(2)}) %collective-permute-start.16) | collective-permute-done | bytes 90144 | tf_op jit(solution)/shard_map/ppermute | solution.py:394
  48.2 0.4 collective-permute-start.17
  48.7 1.0 %collective-permute-done.17.other = bf16[704,128]{1,0:T(8,128)(2,1)S(1)} collective-permute-done((bf16[704,128]{1,0:T(8,128)(2,1)S(1)}, bf16[704,128]{1,0:T(8,128)(2,1)S(1)}, u32[]{:S(2)}, u32[]{:S(2)}) %collective-permute-start.17) | collective-permute-done | bytes 180256 | tf_op jit(solution)/shard_map/ppermute | solution.py:394
  49.7 1.0 %shard_map.92 = (f32[3,3,64,192]{3,2,1,0:T(8,128)}, f32[2,2,128,128]{3,2,1,0:T(8,128)}) custom-call(bf16[704,128]{1,0:T(8,128)(2,1)S(1)} %shard_map.90.mine, bf16[704,128]{1,0:T(8,128)(2,1)S(1)} %collective-permute-done.17.other), custom_call_target="tpu_custom_call" | custom-call | bytes 1064960 | tf_op jit(solution)/shard_map/pallas_call | solution.py:20
  (20 shorter events, 0.2 us)
Async XLA Ops:
  0.6 1.0 %copy-start.2 = (bf16[64,2,8,128]{3,2,1,0:T(8,128)(2,1)S(1)}, bf16[64,2,8,128]{3,2,1,0:T(8,128)(2,1)}, u32[]{:S(2)}) copy-start(bf16[64,2,8,128]{3,2,1,0:T(8,128)(2,1)} %f_ref.1) | copy-start | bytes 786436
  1.6 10.1 %copy-start.3 = (bf16[2,2,128,128]{3,2,1,0:T(8,128)(2,1)S(1)}, bf16[2,2,128,128]{3,2,1,0:T(8,128)(2,1)}, u32[]{:S(2)}) copy-start(bf16[2,2,128,128]{3,2,1,0:T(8,128)(2,1)} %d_ref.3) | copy-start | bytes 393220
  1.6 10.1 %copy-start.4 = (bf16[128,1,256]{2,0,1:T(8,128)(2,1)S(1)}, bf16[128,1,256]{2,0,1:T(8,128)(2,1)}, u32[]{:S(2)}) copy-start(bf16[128,1,256]{2,0,1:T(8,128)(2,1)} %param.7) | copy-start | bytes 196612
  1.8 12.8 %collective-permute-start.2 = (bf16[8,64,128]{2,1,0:T(8,128)(2,1)S(1)}, bf16[8,64,128]{2,1,0:T(8,128)(2,1)S(1)}, u32[]{:S(2)}, u32[]{:S(2)}) collective-permute-start(bf16[8,64,128]{2,1,0:T(8,128)(2,1)S(1)} %get-tuple-element.52.near), channel_id=1, source_target_pairs={{0,4},{8,12},{16,20},{24,28},{4,0},{12,8},{20,16},{28,24},{1,5},{9... | collective-permute-start | bytes 393224 | tf_op jit(solution)/shard_map/ppermute | solution.py:388
  4.8 9.8 %collective-permute-start.3 = (bf16[8,64,128]{2,1,0:T(8,128)(2,1)S(1)}, bf16[8,64,128]{2,1,0:T(8,128)(2,1)S(1)}, u32[]{:S(2)}, u32[]{:S(2)}) collective-permute-start(bf16[8,64,128]{2,1,0:T(8,128)(2,1)S(1)} %get-tuple-element.53.far), channel_id=1, source_target_pairs={{4,8},{12,16},{20,24},{28,0},{8,4},{16,12},{24,20},{0,28},{5,9},{1... | collective-permute-start | bytes 393224 | tf_op jit(solution)/shard_map/ppermute | solution.py:388
  8.4 1.6 %collective-permute-start = (bf16[2,64,128]{2,1,0:T(8,128)(2,1)S(1)}, bf16[2,64,128]{2,1,0:T(8,128)(2,1)S(1)}, u32[]{:S(2)}, u32[]{:S(2)}) collective-permute-start(bf16[2,64,128]{2,1,0:T(8,128)(2,1)S(1)} %get-tuple-element.54), channel_id=1, source_target_pairs={{0,1},{2,3},{1,0},{3,2},{4,5},{6,7},{5,4},{7,6},{8,9},{10,11},{9,8... | collective-permute-start | bytes 98312 | tf_op jit(solution)/shard_map/ppermute | solution.py:388
  8.4 3.3 %collective-permute-start.1 = (bf16[2,64,128]{2,1,0:T(8,128)(2,1)S(1)}, bf16[2,64,128]{2,1,0:T(8,128)(2,1)S(1)}, u32[]{:S(2)}, u32[]{:S(2)}) collective-permute-start(bf16[2,64,128]{2,1,0:T(8,128)(2,1)S(1)} %get-tuple-element.55), channel_id=1, source_target_pairs={{1,2},{3,0},{2,1},{0,3},{5,6},{7,4},{6,5},{4,7},{9,10},{11,8},{10,... | collective-permute-start | bytes 98312 | tf_op jit(solution)/shard_map/ppermute | solution.py:388
  11.7 1.0 %copy-start = (bf16[3,3,64,192]{3,2,1,0:T(8,128)(2,1)S(1)}, bf16[3,3,64,192]{3,2,1,0:T(8,128)(2,1)}, u32[]{:S(2)}) copy-start(bf16[3,3,64,192]{3,2,1,0:T(8,128)(2,1)} %w_ref.5) | copy-start | bytes 663556
  12.7 4.0 %copy-start.1 = (bf16[3,3,64,192]{3,2,1,0:T(8,128)(2,1)S(1)}, bf16[3,3,64,192]{3,2,1,0:T(8,128)(2,1)}, u32[]{:S(2)}) copy-start(bf16[3,3,64,192]{3,2,1,0:T(8,128)(2,1)} %w_ref.5) | copy-start | bytes 663556
  14.7 3.1 %collective-permute-start.4 = (bf16[2,64,128]{2,1,0:T(8,128)(2,1)S(1)}, bf16[2,64,128]{2,1,0:T(8,128)(2,1)S(1)}, u32[]{:S(2)}, u32[]{:S(2)}) collective-permute-start(bf16[2,64,128]{2,1,0:T(8,128)(2,1)S(1)} %get-tuple-element.63), channel_id=1, source_target_pairs={{0,1},{2,3},{1,0},{3,2},{4,5},{6,7},{5,4},{7,6},{8,9},{10,11},{9,8... | collective-permute-start | bytes 98312 | tf_op jit(solution)/shard_map/ppermute | solution.py:388
  15.5 3.4 %collective-permute-start.5 = (bf16[2,64,128]{2,1,0:T(8,128)(2,1)S(1)}, bf16[2,64,128]{2,1,0:T(8,128)(2,1)S(1)}, u32[]{:S(2)}, u32[]{:S(2)}) collective-permute-start(bf16[2,64,128]{2,1,0:T(8,128)(2,1)S(1)} %get-tuple-element.64), channel_id=1, source_target_pairs={{1,2},{3,0},{2,1},{0,3},{5,6},{7,4},{6,5},{4,7},{9,10},{11,8},{10,... | collective-permute-start | bytes 98312 | tf_op jit(solution)/shard_map/ppermute | solution.py:388
  20.5 1.5 %collective-permute-start.6 = (bf16[704,128]{1,0:T(8,128)(2,1)S(1)}, bf16[704,128]{1,0:T(8,128)(2,1)S(1)}, u32[]{:S(2)}, u32[]{:S(2)}) collective-permute-start(bf16[704,128]{1,0:T(8,128)(2,1)S(1)} %get-tuple-element.75), channel_id=1, source_target_pairs={{0,1},{1,0},{2,3},{3,2},{4,5},{5,4},{6,7},{7,6},{8,9},{9,8},{10,11... | collective-permute-start | bytes 540680 | tf_op jit(solution)/shard_map/ppermute | solution.py:394
  22.0 4.7 %collective-permute-start.7 = (bf16[352,128]{1,0:T(8,128)(2,1)S(1)}, bf16[352,128]{1,0:T(8,128)(2,1)S(1)}, u32[]{:S(2)}, u32[]{:S(2)}) collective-permute-start(bf16[352,128]{1,0:T(8,128)(2,1)S(1)} %get-tuple-element.79), channel_id=1, source_target_pairs={{0,9},{1,8},{2,11},{3,10},{4,13},{5,12},{6,15},{7,14},{8,1},{9,0},... | collective-permute-start | bytes 270344 | tf_op jit(solution)/shard_map/ppermute | solution.py:394
  22.1 11.8 %collective-permute-start.10 = (bf16[8,64,128]{2,1,0:T(8,128)(2,1)S(1)}, bf16[8,64,128]{2,1,0:T(8,128)(2,1)S(1)}, u32[]{:S(2)}, u32[]{:S(2)}) collective-permute-start(bf16[8,64,128]{2,1,0:T(8,128)(2,1)S(1)} %get-tuple-element.82.near), channel_id=1, source_target_pairs={{0,4},{8,12},{16,20},{24,28},{4,0},{12,8},{20,16},{28,24},{1,5},{9... | collective-permute-start | bytes 393224 | tf_op jit(solution)/shard_map/ppermute | solution.py:388
  22.9 11.0 %collective-permute-start.11 = (bf16[8,64,128]{2,1,0:T(8,128)(2,1)S(1)}, bf16[8,64,128]{2,1,0:T(8,128)(2,1)S(1)}, u32[]{:S(2)}, u32[]{:S(2)}) collective-permute-start(bf16[8,64,128]{2,1,0:T(8,128)(2,1)S(1)} %get-tuple-element.83.far), channel_id=1, source_target_pairs={{4,8},{12,16},{20,24},{28,0},{8,4},{16,12},{24,20},{0,28},{5,9},{1... | collective-permute-start | bytes 393224 | tf_op jit(solution)/shard_map/ppermute | solution.py:388
  26.7 3.7 %collective-permute-start.8 = (bf16[176,128]{1,0:T(8,128)(2,1)S(1)}, bf16[176,128]{1,0:T(8,128)(2,1)S(1)}, u32[]{:S(2)}, u32[]{:S(2)}) collective-permute-start(bf16[176,128]{1,0:T(8,128)(2,1)S(1)} %get-tuple-element.81), channel_id=1, source_target_pairs={{0,3},{1,2},{2,1},{3,0},{4,7},{5,6},{6,5},{7,4},{8,11},{9,10},{10,... | collective-permute-start | bytes 135176 | tf_op jit(solution)/shard_map/ppermute | solution.py:394
  30.4 3.5 %collective-permute-start.9 = (bf16[176,128]{1,0:T(8,128)(2,1)S(1)}, bf16[176,128]{1,0:T(8,128)(2,1)S(1)}, u32[]{:S(2)}, u32[]{:S(2)}) collective-permute-start(bf16[176,128]{1,0:T(8,128)(2,1)S(1)} %shard_map.83.x), channel_id=1, source_target_pairs={{0,5},{1,4},{2,7},{3,6},{4,1},{5,0},{6,3},{7,2},{8,13},{9,12},{10,... | collective-permute-start | bytes 135176 | tf_op jit(solution)/shard_map/ppermute | solution.py:394
  34.0 5.6 %collective-permute-start.12 = (bf16[176,128]{1,0:T(8,128)(2,1)S(1)}, bf16[176,128]{1,0:T(8,128)(2,1)S(1)}, u32[]{:S(2)}, u32[]{:S(2)}) collective-permute-start(bf16[176,128]{1,0:T(8,128)(2,1)S(1)} %shard_map.84.x), channel_id=1, source_target_pairs={{0,17},{1,16},{2,19},{3,18},{4,21},{5,20},{6,23},{7,22},{8,25},{9,... | collective-permute-start | bytes 135176 | tf_op jit(solution)/shard_map/ppermute | solution.py:394
  35.8 7.9 %collective-permute-start.14 = (bf16[4,64,128]{2,1,0:T(8,128)(2,1)S(1)}, bf16[4,64,128]{2,1,0:T(8,128)(2,1)S(1)}, u32[]{:S(2)}, u32[]{:S(2)}) collective-permute-start(bf16[4,64,128]{2,1,0:T(8,128)(2,1)S(1)} %get-tuple-element.90), channel_id=1, source_target_pairs={{0,1},{2,3},{1,0},{3,2},{4,5},{6,7},{5,4},{7,6},{8,9},{10,11},{9,8... | collective-permute-start | bytes 196616 | tf_op jit(solution)/shard_map/ppermute | solution.py:388
  36.4 7.4 %collective-permute-start.15 = (bf16[4,64,128]{2,1,0:T(8,128)(2,1)S(1)}, bf16[4,64,128]{2,1,0:T(8,128)(2,1)S(1)}, u32[]{:S(2)}, u32[]{:S(2)}) collective-permute-start(bf16[4,64,128]{2,1,0:T(8,128)(2,1)S(1)} %get-tuple-element.91), channel_id=1, source_target_pairs={{1,2},{3,0},{2,1},{0,3},{5,6},{7,4},{6,5},{4,7},{9,10},{11,8},{10,... | collective-permute-start | bytes 196616 | tf_op jit(solution)/shard_map/ppermute | solution.py:388
  39.7 4.1 %collective-permute-start.13 = (bf16[176,128]{1,0:T(8,128)(2,1)S(1)}, bf16[176,128]{1,0:T(8,128)(2,1)S(1)}, u32[]{:S(2)}, u32[]{:S(2)}) collective-permute-start(bf16[176,128]{1,0:T(8,128)(2,1)S(1)} %shard_map.85.mine), channel_id=1, source_target_pairs={{0,3},{1,2},{2,1},{3,0},{4,7},{5,6},{6,5},{7,4},{8,11},{9,10},{10,... | collective-permute-start | bytes 135176 | tf_op jit(solution)/shard_map/ppermute | solution.py:394
  43.8 4.4 %collective-permute-start.16 = (bf16[352,128]{1,0:T(8,128)(2,1)S(1)}, bf16[352,128]{1,0:T(8,128)(2,1)S(1)}, u32[]{:S(2)}, u32[]{:S(2)}) collective-permute-start(bf16[352,128]{1,0:T(8,128)(2,1)S(1)} %shard_map.87.mine), channel_id=1, source_target_pairs={{0,9},{1,8},{2,11},{3,10},{4,13},{5,12},{6,15},{7,14},{8,1},{9,0},... | collective-permute-start | bytes 270344 | tf_op jit(solution)/shard_map/ppermute | solution.py:394
  48.2 1.5 %collective-permute-start.17 = (bf16[704,128]{1,0:T(8,128)(2,1)S(1)}, bf16[704,128]{1,0:T(8,128)(2,1)S(1)}, u32[]{:S(2)}, u32[]{:S(2)}) collective-permute-start(bf16[704,128]{1,0:T(8,128)(2,1)S(1)} %shard_map.90.mine), channel_id=1, source_target_pairs={{0,1},{1,0},{2,3},{3,2},{4,5},{5,4},{6,7},{7,6},{8,9},{9,8},{10,11... | collective-permute-start | bytes 540680 | tf_op jit(solution)/shard_map/ppermute | solution.py:394

commit v19 on v17

--- a/solution.py
+++ b/solution.py
@@ -409,7 +409,7 @@
         [((out_channels, row_count // 2 * breadth), BF16)],
         2 * conv_flops // 3, (*own, conv_weight, down_weight, cot),
     )
-    near, far, acc = lax.optimization_barrier((*outside, acc))
+    near, far, acc, weight_bwd = lax.optimization_barrier((*outside, acc, weight_bwd))
     outside = (near, far)
     beside = swapped(*call(edges_kernel, [edge, edge], [], 0, (*own, *outside)), "gy")
     outer, *inside = call(

time: 48.7 us -> 48.7 us (level)
  local copies, waits for them, and re-layouts: 2.7 us -> 3.39 us
    ppermute x8, waiting for transfers between devices: 2.47 us -> 1.27 us  [swap(): return lax.ppermute(cells, axis, pairs + [(b, a) for a, b in pairs])]
    ppermute x8, waiting for transfers between devices: 11.8 us -> 12.6 us  [flip(): lax.ppermute(cells, ('gz', 'gy'), [(i, i ^ mask) for i in range(lax.axis_...]
    unnamed x11 -> x9, local copies, waits for them, and re-layouts: 2.18 us -> 2.88 us
  transfers between devices with their start and end apart: 16 -> 16, of which waited for: 10 -> 9; matrix products, arithmetic and copies ran while one was open for 2% -> 4% of each run, Pallas kernels for 16% -> 16%
where the time goes in v19:
time: 48.7 us; the launch traced here: 48.5 us
  starting transfers between devices  19.6 us (40%)
  waiting for transfers between devices  13.9 us (29%)
  Pallas kernels  10.7 us (22%)
  local copies, waits for them, and re-layouts  3.39 us (7%)
  between operations  0.83 us (2%)
    ppermute x8, starting transfers between devices, swap(): return lax.ppermute(cells, axis, pairs + [(b, a) for a, b in pairs])  13.9 us
    ppermute x8, waiting for transfers between devices, flip(): lax.ppermute(cells, ('gz', 'gy'), [(i, i ^ mask) for i in range(lax.axis_...  12.6 us
    pallas_call x18, Pallas kernels, call(): pl.pallas_call(kernel, out_shape=[jax.ShapeDtypeStruct(s, d) for s, d in...  10.7 us
    ppermute x8, starting transfers between devices, flip(): lax.ppermute(cells, ('gz', 'gy'), [(i, i ^ mask) for i in range(lax.axis_...  5.75 us
    unnamed x9, local copies, waits for them, and re-layouts  2.88 us
    ppermute x8, waiting for transfers between devices, swap(): return lax.ppermute(cells, axis, pairs + [(b, a) for a, b in pairs])  1.27 us
  transfers between devices with their start and end apart: 16, of which 9 were waited for; matrix products, arithmetic and copies ran while one was open for 4% of the time, Pallas kernels for 16%

profile of v19, /device:TPU:0, one launch (start us, length us, event | category | flops | bytes accessed | tf_op | source)
XLA Modules:
  0.0 48.5 jit_solution(16696022108709227532)
XLA Ops:
  0.6 0.9 %copy-done.1 = bf16[64,2,8,128]{3,2,1,0:T(8,128)(2,1)S(1)} copy-done((bf16[64,2,8,128]{3,2,1,0:T(8,128)(2,1)S(1)}, bf16[64,2,8,128]{3,2,1,0:T(8,128)(2,1)}, u32[]{:S(2)}) %copy-start.1) | copy-done | bytes 262168
  1.6 0.2 shard_map.75
  1.8 3.0 %collective-permute-start = (bf16[8,64,128]{2,1,0:T(8,128)(2,1)S(1)}, bf16[8,64,128]{2,1,0:T(8,128)(2,1)S(1)}, u32[]{:S(2)}, u32[]{:S(2)}) collective-permute-start(bf16[8,64,128]{2,1,0:T(8,128)(2,1)S(1)} %get-tuple-element.51.near), channel_id=1, source_target_pairs={{0,4},{8,12},{16,20},{24,28},{4,0},{12,8},{20,16},{28,24},{1,5},{9... | collective-permute-start | bytes 393224 | tf_op jit(solution)/shard_map/ppermute | solution.py:370
  4.8 3.5 %collective-permute-start.1 = (bf16[8,64,128]{2,1,0:T(8,128)(2,1)S(1)}, bf16[8,64,128]{2,1,0:T(8,128)(2,1)S(1)}, u32[]{:S(2)}, u32[]{:S(2)}) collective-permute-start(bf16[8,64,128]{2,1,0:T(8,128)(2,1)S(1)} %get-tuple-element.52.far), channel_id=1, source_target_pairs={{4,8},{12,16},{20,24},{28,0},{8,4},{16,12},{24,20},{0,28},{5,9},{1... | collective-permute-start | bytes 393224 | tf_op jit(solution)/shard_map/ppermute | solution.py:370
  8.4 1.2 %copy.9 = bf16[3,3,64,192]{2,3,1,0:T(8,128)(2,1)S(1)} copy(bf16[3,3,64,192]{3,2,1,0:T(8,128)(2,1)} %w_ref.5) | data formatting | bytes 442368 | tf_op args[1]
  9.6 0.0 copy-start
  9.6 0.0 copy-start.2
  9.7 0.0 copy-start.3
  9.7 0.2 copy.10
  9.9 0.7 %copy-done = bf16[3,3,64,192]{3,2,1,0:T(8,128)(2,1)S(1)} copy-done((bf16[3,3,64,192]{3,2,1,0:T(8,128)(2,1)S(1)}, bf16[3,3,64,192]{3,2,1,0:T(8,128)(2,1)}, u32[]{:S(2)}) %copy-start) | copy-done | bytes 221208
  10.6 0.0 copy-done.2
  10.6 1.9 %shard_map.76 = (bf16[2,10,192,128]{3,2,1,0:T(8,128)(2,1)S(1)}, f32[2,8,64,128]{3,2,1,0:T(8,128)S(1)}, f32[2,8,64,128]{3,2,1,0:T(8,128)S(1)}) custom-call(bf16[8,64,128]{2,1,0:T(8,128)(2,1)S(1)} %get-tuple-element.51.near, bf16[8,64,128]{2,1,0:T(8,128)(2,1)S(1)} %get-tuple-element.52.far, bf16[3,3,64,192]{3,2,1,0:T(8,128)(2,1)S(1)} %copy-done, ...), custom_call_target="tpu_custom_call" | custom-call | flops 301989888 | bytes 2711552 | tf_op jit(solution)/shard_map/pallas_call | solution.py:20
  12.5 0.0 collective-permute-done.near.near_in
  12.6 0.1 collective-permute-start.2
  12.7 1.6 %collective-permute-start.3 = (bf16[4,64,128]{2,1,0:T(8,128)(2,1)S(1)}, bf16[4,64,128]{2,1,0:T(8,128)(2,1)S(1)}, u32[]{:S(2)}, u32[]{:S(2)}) collective-permute-start(bf16[4,64,128]{2,1,0:T(8,128)(2,1)S(1)} %get-tuple-element.61), channel_id=1, source_target_pairs={{1,2},{3,0},{2,1},{0,3},{5,6},{7,4},{6,5},{4,7},{9,10},{11,8},{10,... | collective-permute-start | bytes 196616 | tf_op jit(solution)/shard_map/ppermute | solution.py:370
  14.3 1.0 %shard_map.77 = (bf16[2,10,192,128]{3,2,1,0:T(8,128)(2,1)S(1)}, f32[2,2,64,128]{3,2,1,0:T(8,128)S(1)}, bf16[8,64,128]{2,1,0:T(8,128)(2,1)S(1)}, bf16[8,64,128]{2...) custom-call(bf16[8,64,128]{2,1,0:T(8,128)(2,1)S(1)} %collective-permute-done.near.near_in, ...), custom_call_target="tpu_custom_call" | custom-call | flops 150994944 | bytes 3170304 | tf_op jit(solution)/shard_map/pallas_call | solution.py:20
  15.3 0.0 collective-permute-done.2.near
  15.3 1.2 %collective-permute-done.3.far = bf16[4,64,128]{2,1,0:T(8,128)(2,1)S(1)} collective-permute-done((bf16[4,64,128]{2,1,0:T(8,128)(2,1)S(1)}, bf16[4,64,128]{2,1,0:T(8,128)(2,1)S(1)}, u32[]{:S(2)}, u32[]{:S(2)}) %collective-permute-start.3) | collective-permute-done | bytes 65568 | tf_op jit(solution)/shard_map/ppermute | solution.py:370
  16.6 0.4 shard_map.79
  17.0 1.2 %shard_map.80 = (f32[704,128]{1,0:T(8,128)S(1)}, bf16[704,128]{1,0:T(8,128)(2,1)S(1)}) custom-call(bf16[2,10,192,128]{3,2,1,0:T(8,128)(2,1)S(1)} %get-tuple-element.53.inner, bf16[2,10,192,128]{3,2,1,0:T(8,128)(2,1)S(1)} %get-tuple-element.59.outer, bf16[4,2,192,128]{3,2,1,0:T(8,128)(2,1)S(1)} %get-tuple-element.66.edges, ...), custom_call_target="tpu_custom_call" | custom-call | flops 452984832 | bytes 3489792 | tf_op jit(solution)/shard_map/pallas_call | solution.py:20
  18.2 0.5 collective-permute-start.4
  18.7 1.0 %collective-permute-done.4.other = bf16[704,128]{1,0:T(8,128)(2,1)S(1)} collective-permute-done((bf16[704,128]{1,0:T(8,128)(2,1)S(1)}, bf16[704,128]{1,0:T(8,128)(2,1)S(1)}, u32[]{:S(2)}, u32[]{:S(2)}) %collective-permute-start.4) | collective-permute-done | bytes 180256 | tf_op jit(solution)/shard_map/ppermute | solution.py:376
  19.7 0.1 shard_map.81
  19.8 0.4 collective-permute-start.5
  20.2 1.5 %collective-permute-start.8 = (bf16[8,64,128]{2,1,0:T(8,128)(2,1)S(1)}, bf16[8,64,128]{2,1,0:T(8,128)(2,1)S(1)}, u32[]{:S(2)}, u32[]{:S(2)}) collective-permute-start(bf16[8,64,128]{2,1,0:T(8,128)(2,1)S(1)} %get-tuple-element.79.near), channel_id=1, source_target_pairs={{0,4},{8,12},{16,20},{24,28},{4,0},{12,8},{20,16},{28,24},{1,5},{9... | collective-permute-start | bytes 393224 | tf_op jit(solution)/shard_map/ppermute | solution.py:370
  21.7 2.4 %collective-permute-start.9 = (bf16[8,64,128]{2,1,0:T(8,128)(2,1)S(1)}, bf16[8,64,128]{2,1,0:T(8,128)(2,1)S(1)}, u32[]{:S(2)}, u32[]{:S(2)}) collective-permute-start(bf16[8,64,128]{2,1,0:T(8,128)(2,1)S(1)} %get-tuple-element.80.far), channel_id=1, source_target_pairs={{4,8},{12,16},{20,24},{28,0},{8,4},{16,12},{24,20},{0,28},{5,9},{1... | collective-permute-start | bytes 393224 | tf_op jit(solution)/shard_map/ppermute | solution.py:370
  24.1 0.2 collective-permute-done.5.other
  24.3 2.2 %collective-permute-start.6 = (bf16[176,128]{1,0:T(8,128)(2,1)S(1)}, bf16[176,128]{1,0:T(8,128)(2,1)S(1)}, u32[]{:S(2)}, u32[]{:S(2)}) collective-permute-start(bf16[176,128]{1,0:T(8,128)(2,1)S(1)} %get-tuple-element.78), channel_id=1, source_target_pairs={{0,3},{1,2},{2,1},{3,0},{4,7},{5,6},{6,5},{7,4},{8,11},{9,10},{10,... | collective-permute-start | bytes 135176 | tf_op jit(solution)/shard_map/ppermute | solution.py:376
  26.6 1.7 %collective-permute-done.6.y = bf16[176,128]{1,0:T(8,128)(2,1)S(1)} collective-permute-done((bf16[176,128]{1,0:T(8,128)(2,1)S(1)}, bf16[176,128]{1,0:T(8,128)(2,1)S(1)}, u32[]{:S(2)}, u32[]{:S(2)}) %collective-permute-start.6) | collective-permute-done | bytes 45088 | tf_op jit(solution)/shard_map/ppermute | solution.py:376
  28.3 0.2 collective-permute-start.7
  28.5 3.3 %collective-permute-done.7.y = bf16[176,128]{1,0:T(8,128)(2,1)S(1)} collective-permute-done((bf16[176,128]{1,0:T(8,128)(2,1)S(1)}, bf16[176,128]{1,0:T(8,128)(2,1)S(1)}, u32[]{:S(2)}, u32[]{:S(2)}) %collective-permute-start.7) | collective-permute-done | bytes 45088 | tf_op jit(solution)/shard_map/ppermute | solution.py:376
  31.9 0.0 collective-permute-done.8.near_in
  31.9 1.2 %collective-permute-start.10 = (bf16[176,128]{1,0:T(8,128)(2,1)S(1)}, bf16[176,128]{1,0:T(8,128)(2,1)S(1)}, u32[]{:S(2)}, u32[]{:S(2)}) collective-permute-start(bf16[176,128]{1,0:T(8,128)(2,1)S(1)} %shard_map.84.x), channel_id=1, source_target_pairs={{0,17},{1,16},{2,19},{3,18},{4,21},{5,20},{6,23},{7,22},{8,25},{9,... | collective-permute-start | bytes 135176 | tf_op jit(solution)/shard_map/ppermute | solution.py:376
  33.2 0.1 collective-permute-start.12
  33.3 1.6 %collective-permute-start.13 = (bf16[4,64,128]{2,1,0:T(8,128)(2,1)S(1)}, bf16[4,64,128]{2,1,0:T(8,128)(2,1)S(1)}, u32[]{:S(2)}, u32[]{:S(2)}) collective-permute-start(bf16[4,64,128]{2,1,0:T(8,128)(2,1)S(1)} %get-tuple-element.89), channel_id=1, source_target_pairs={{1,2},{3,0},{2,1},{0,3},{5,6},{7,4},{6,5},{4,7},{9,10},{11,8},{10,... | collective-permute-start | bytes 196616 | tf_op jit(solution)/shard_map/ppermute | solution.py:370
  34.8 1.1 %shard_map.86 = bf16[128,256]{1,0:T(8,128)(2,1)} custom-call(bf16[2,8,64,128]{3,2,1,0:T(8,128)(2,1)S(1)} %get-tuple-element.82.h_ref, bf16[2,2,128,128]{3,2,1,0:T(8,128)(2,1)S(1)} %copy-done.2), custom_call_target="tpu_custom_call" | custom-call | flops 45298484 | bytes 458752 | tf_op jit(solution)/shard_map/pallas_call | solution.py:20
  35.9 1.5 %collective-permute-done.10.y = bf16[176,128]{1,0:T(8,128)(2,1)S(1)} collective-permute-done((bf16[176,128]{1,0:T(8,128)(2,1)S(1)}, bf16[176,128]{1,0:T(8,128)(2,1)S(1)}, u32[]{:S(2)}, u32[]{:S(2)}) %collective-permute-start.10) | collective-permute-done | bytes 45088 | tf_op jit(solution)/shard_map/ppermute | solution.py:376
  37.5 0.9 %collective-permute-start.11 = (bf16[176,128]{1,0:T(8,128)(2,1)S(1)}, bf16[176,128]{1,0:T(8,128)(2,1)S(1)}, u32[]{:S(2)}, u32[]{:S(2)}) collective-permute-start(bf16[176,128]{1,0:T(8,128)(2,1)S(1)} %shard_map.85.mine), channel_id=1, source_target_pairs={{0,3},{1,2},{2,1},{3,0},{4,7},{5,6},{6,5},{7,4},{8,11},{9,10},{10,... | collective-permute-start | bytes 135176 | tf_op jit(solution)/shard_map/ppermute | solution.py:376
  38.4 0.2 copy.11.w_ref
  38.7 2.3 %shard_map.88.acc_ref = f32[2,8,64,128]{3,2,1,0:T(8,128)S(1)} custom-call(bf16[8,64,128]{2,1,0:T(8,128)(2,1)S(1)} %get-tuple-element.79.near, bf16[8,64,128]{2,1,0:T(8,128)(2,1)S(1)} %get-tuple-element.80.far, bf16[8,64,128]{2,1,0:T(8,128)(2,1)S(1)} %collective-permute-done.8.near_in, bf16[8,64,128]{2,1,0:T(8,128)(2,1)S(1)} %collective-permute-done.9.far_in, ...), custom_call_target="tpu_custom_call" | custom-call | flops 452984832 | bytes 1269760 | tf_op jit(solution)/shard_map/pallas_call | solution.py:20
  40.9 0.3 collective-permute-done.11.other
  41.2 0.0 collective-permute-done.13.far
  41.2 0.1 collective-permute-start.14
  41.4 1.3 %shard_map.91 = f32[1024,128]{1,0:T(8,128)} custom-call(bf16[4,64,128]{2,1,0:T(8,128)(2,1)S(1)} %collective-permute-done.12.near, bf16[4,64,128]{2,1,0:T(8,128)(2,1)S(1)} %collective-permute-done.13.far, f32[2,8,64,128]{3,2,1,0:T(8,128)S(1)} %shard_map.88.acc_ref, bf16[3,3,64,192]{3,2,1,0:T(8,128)(2,1)S(1)} %copy.11.w_ref), custom_call_target="tpu_custom_call" | custom-call | flops 45298484 | bytes 1400832 | tf_op jit(solution)/shard_map/pallas_call | solution.py:20
  42.7 3.2 %collective-permute-done.14.other = bf16[352,128]{1,0:T(8,128)(2,1)S(1)} collective-permute-done((bf16[352,128]{1,0:T(8,128)(2,1)S(1)}, bf16[352,128]{1,0:T(8,128)(2,1)S(1)}, u32[]{:S(2)}, u32[]{:S(2)}) %collective-permute-start.14) | collective-permute-done | bytes 90144 | tf_op jit(solution)/shard_map/ppermute | solution.py:376
  46.0 0.2 collective-permute-start.15
  46.2 1.3 %collective-permute-done.15.other = bf16[704,128]{1,0:T(8,128)(2,1)S(1)} collective-permute-done((bf16[704,128]{1,0:T(8,128)(2,1)S(1)}, bf16[704,128]{1,0:T(8,128)(2,1)S(1)}, u32[]{:S(2)}, u32[]{:S(2)}) %collective-permute-start.15) | collective-permute-done | bytes 180256 | tf_op jit(solution)/shard_map/ppermute | solution.py:376
  47.4 1.0 %shard_map.92 = (f32[3,3,64,192]{3,2,1,0:T(8,128)}, f32[2,2,128,128]{3,2,1,0:T(8,128)}) custom-call(bf16[704,128]{1,0:T(8,128)(2,1)S(1)} %shard_map.90.mine, bf16[704,128]{1,0:T(8,128)(2,1)S(1)} %collective-permute-done.15.other), custom_call_target="tpu_custom_call" | custom-call | bytes 1064960 | tf_op jit(solution)/shard_map/pallas_call | solution.py:20
  (14 shorter events, 0.2 us)
Async XLA Ops:
  0.6 1.0 %copy-start.1 = (bf16[64,2,8,128]{3,2,1,0:T(8,128)(2,1)S(1)}, bf16[64,2,8,128]{3,2,1,0:T(8,128)(2,1)}, u32[]{:S(2)}) copy-start(bf16[64,2,8,128]{3,2,1,0:T(8,128)(2,1)} %f_ref.1) | copy-start | bytes 786436
  1.8 10.7 %collective-permute-start = (bf16[8,64,128]{2,1,0:T(8,128)(2,1)S(1)}, bf16[8,64,128]{2,1,0:T(8,128)(2,1)S(1)}, u32[]{:S(2)}, u32[]{:S(2)}) collective-permute-start(bf16[8,64,128]{2,1,0:T(8,128)(2,1)S(1)} %get-tuple-element.51.near), channel_id=1, source_target_pairs={{0,4},{8,12},{16,20},{24,28},{4,0},{12,8},{20,16},{28,24},{1,5},{9... | collective-permute-start | bytes 393224 | tf_op jit(solution)/shard_map/ppermute | solution.py:370
  4.8 7.7 %collective-permute-start.1 = (bf16[8,64,128]{2,1,0:T(8,128)(2,1)S(1)}, bf16[8,64,128]{2,1,0:T(8,128)(2,1)S(1)}, u32[]{:S(2)}, u32[]{:S(2)}) collective-permute-start(bf16[8,64,128]{2,1,0:T(8,128)(2,1)S(1)} %get-tuple-element.52.far), channel_id=1, source_target_pairs={{4,8},{12,16},{20,24},{28,0},{8,4},{16,12},{24,20},{0,28},{5,9},{1... | collective-permute-start | bytes 393224 | tf_op jit(solution)/shard_map/ppermute | solution.py:370
  9.6 1.0 %copy-start = (bf16[3,3,64,192]{3,2,1,0:T(8,128)(2,1)S(1)}, bf16[3,3,64,192]{3,2,1,0:T(8,128)(2,1)}, u32[]{:S(2)}) copy-start(bf16[3,3,64,192]{3,2,1,0:T(8,128)(2,1)} %w_ref.5) | copy-start | bytes 663556
  9.6 1.0 %copy-start.2 = (bf16[2,2,128,128]{3,2,1,0:T(8,128)(2,1)S(1)}, bf16[2,2,128,128]{3,2,1,0:T(8,128)(2,1)}, u32[]{:S(2)}) copy-start(bf16[2,2,128,128]{3,2,1,0:T(8,128)(2,1)} %d_ref.3) | copy-start | bytes 393220
  9.7 1.0 %copy-start.3 = (bf16[128,1,256]{2,0,1:T(8,128)(2,1)S(1)}, bf16[128,1,256]{2,0,1:T(8,128)(2,1)}, u32[]{:S(2)}) copy-start(bf16[128,1,256]{2,0,1:T(8,128)(2,1)} %param.7) | copy-start | bytes 196612
  12.6 2.7 %collective-permute-start.2 = (bf16[4,64,128]{2,1,0:T(8,128)(2,1)S(1)}, bf16[4,64,128]{2,1,0:T(8,128)(2,1)S(1)}, u32[]{:S(2)}, u32[]{:S(2)}) collective-permute-start(bf16[4,64,128]{2,1,0:T(8,128)(2,1)S(1)} %get-tuple-element.60), channel_id=1, source_target_pairs={{0,1},{2,3},{1,0},{3,2},{4,5},{6,7},{5,4},{7,6},{8,9},{10,11},{9,8... | collective-permute-start | bytes 196616 | tf_op jit(solution)/shard_map/ppermute | solution.py:370
  12.7 3.9 %collective-permute-start.3 = (bf16[4,64,128]{2,1,0:T(8,128)(2,1)S(1)}, bf16[4,64,128]{2,1,0:T(8,128)(2,1)S(1)}, u32[]{:S(2)}, u32[]{:S(2)}) collective-permute-start(bf16[4,64,128]{2,1,0:T(8,128)(2,1)S(1)} %get-tuple-element.61), channel_id=1, source_target_pairs={{1,2},{3,0},{2,1},{0,3},{5,6},{7,4},{6,5},{4,7},{9,10},{11,8},{10,... | collective-permute-start | bytes 196616 | tf_op jit(solution)/shard_map/ppermute | solution.py:370
  18.2 1.5 %collective-permute-start.4 = (bf16[704,128]{1,0:T(8,128)(2,1)S(1)}, bf16[704,128]{1,0:T(8,128)(2,1)S(1)}, u32[]{:S(2)}, u32[]{:S(2)}) collective-permute-start(bf16[704,128]{1,0:T(8,128)(2,1)S(1)} %get-tuple-element.72), channel_id=1, source_target_pairs={{0,1},{1,0},{2,3},{3,2},{4,5},{5,4},{6,7},{7,6},{8,9},{9,8},{10,11... | collective-permute-start | bytes 540680 | tf_op jit(solution)/shard_map/ppermute | solution.py:376
  19.8 4.5 %collective-permute-start.5 = (bf16[352,128]{1,0:T(8,128)(2,1)S(1)}, bf16[352,128]{1,0:T(8,128)(2,1)S(1)}, u32[]{:S(2)}, u32[]{:S(2)}) collective-permute-start(bf16[352,128]{1,0:T(8,128)(2,1)S(1)} %get-tuple-element.76), channel_id=1, source_target_pairs={{0,9},{1,8},{2,11},{3,10},{4,13},{5,12},{6,15},{7,14},{8,1},{9,0},... | collective-permute-start | bytes 270344 | tf_op jit(solution)/shard_map/ppermute | solution.py:376
  20.2 11.7 %collective-permute-start.8 = (bf16[8,64,128]{2,1,0:T(8,128)(2,1)S(1)}, bf16[8,64,128]{2,1,0:T(8,128)(2,1)S(1)}, u32[]{:S(2)}, u32[]{:S(2)}) collective-permute-start(bf16[8,64,128]{2,1,0:T(8,128)(2,1)S(1)} %get-tuple-element.79.near), channel_id=1, source_target_pairs={{0,4},{8,12},{16,20},{24,28},{4,0},{12,8},{20,16},{28,24},{1,5},{9... | collective-permute-start | bytes 393224 | tf_op jit(solution)/shard_map/ppermute | solution.py:370
  21.7 10.2 %collective-permute-start.9 = (bf16[8,64,128]{2,1,0:T(8,128)(2,1)S(1)}, bf16[8,64,128]{2,1,0:T(8,128)(2,1)S(1)}, u32[]{:S(2)}, u32[]{:S(2)}) collective-permute-start(bf16[8,64,128]{2,1,0:T(8,128)(2,1)S(1)} %get-tuple-element.80.far), channel_id=1, source_target_pairs={{4,8},{12,16},{20,24},{28,0},{8,4},{16,12},{24,20},{0,28},{5,9},{1... | collective-permute-start | bytes 393224 | tf_op jit(solution)/shard_map/ppermute | solution.py:370
  24.3 3.9 %collective-permute-start.6 = (bf16[176,128]{1,0:T(8,128)(2,1)S(1)}, bf16[176,128]{1,0:T(8,128)(2,1)S(1)}, u32[]{:S(2)}, u32[]{:S(2)}) collective-permute-start(bf16[176,128]{1,0:T(8,128)(2,1)S(1)} %get-tuple-element.78), channel_id=1, source_target_pairs={{0,3},{1,2},{2,1},{3,0},{4,7},{5,6},{6,5},{7,4},{8,11},{9,10},{10,... | collective-permute-start | bytes 135176 | tf_op jit(solution)/shard_map/ppermute | solution.py:376
  28.3 3.5 %collective-permute-start.7 = (bf16[176,128]{1,0:T(8,128)(2,1)S(1)}, bf16[176,128]{1,0:T(8,128)(2,1)S(1)}, u32[]{:S(2)}, u32[]{:S(2)}) collective-permute-start(bf16[176,128]{1,0:T(8,128)(2,1)S(1)} %shard_map.83.x), channel_id=1, source_target_pairs={{0,5},{1,4},{2,7},{3,6},{4,1},{5,0},{6,3},{7,2},{8,13},{9,12},{10,... | collective-permute-start | bytes 135176 | tf_op jit(solution)/shard_map/ppermute | solution.py:376
  31.9 5.6 %collective-permute-start.10 = (bf16[176,128]{1,0:T(8,128)(2,1)S(1)}, bf16[176,128]{1,0:T(8,128)(2,1)S(1)}, u32[]{:S(2)}, u32[]{:S(2)}) collective-permute-start(bf16[176,128]{1,0:T(8,128)(2,1)S(1)} %shard_map.84.x), channel_id=1, source_target_pairs={{0,17},{1,16},{2,19},{3,18},{4,21},{5,20},{6,23},{7,22},{8,25},{9,... | collective-permute-start | bytes 135176 | tf_op jit(solution)/shard_map/ppermute | solution.py:376
  33.2 8.1 %collective-permute-start.12 = (bf16[4,64,128]{2,1,0:T(8,128)(2,1)S(1)}, bf16[4,64,128]{2,1,0:T(8,128)(2,1)S(1)}, u32[]{:S(2)}, u32[]{:S(2)}) collective-permute-start(bf16[4,64,128]{2,1,0:T(8,128)(2,1)S(1)} %get-tuple-element.88), channel_id=1, source_target_pairs={{0,1},{2,3},{1,0},{3,2},{4,5},{6,7},{5,4},{7,6},{8,9},{10,11},{9,8... | collective-permute-start | bytes 196616 | tf_op jit(solution)/shard_map/ppermute | solution.py:370
  33.3 8.0 %collective-permute-start.13 = (bf16[4,64,128]{2,1,0:T(8,128)(2,1)S(1)}, bf16[4,64,128]{2,1,0:T(8,128)(2,1)S(1)}, u32[]{:S(2)}, u32[]{:S(2)}) collective-permute-start(bf16[4,64,128]{2,1,0:T(8,128)(2,1)S(1)} %get-tuple-element.89), channel_id=1, source_target_pairs={{1,2},{3,0},{2,1},{0,3},{5,6},{7,4},{6,5},{4,7},{9,10},{11,8},{10,... | collective-permute-start | bytes 196616 | tf_op jit(solution)/shard_map/ppermute | solution.py:370
  37.5 3.7 %collective-permute-start.11 = (bf16[176,128]{1,0:T(8,128)(2,1)S(1)}, bf16[176,128]{1,0:T(8,128)(2,1)S(1)}, u32[]{:S(2)}, u32[]{:S(2)}) collective-permute-start(bf16[176,128]{1,0:T(8,128)(2,1)S(1)} %shard_map.85.mine), channel_id=1, source_target_pairs={{0,3},{1,2},{2,1},{3,0},{4,7},{5,6},{6,5},{7,4},{8,11},{9,10},{10,... | collective-permute-start | bytes 135176 | tf_op jit(solution)/shard_map/ppermute | solution.py:376
  41.2 4.7 %collective-permute-start.14 = (bf16[352,128]{1,0:T(8,128)(2,1)S(1)}, bf16[352,128]{1,0:T(8,128)(2,1)S(1)}, u32[]{:S(2)}, u32[]{:S(2)}) collective-permute-start(bf16[352,128]{1,0:T(8,128)(2,1)S(1)} %shard_map.87.mine), channel_id=1, source_target_pairs={{0,9},{1,8},{2,11},{3,10},{4,13},{5,12},{6,15},{7,14},{8,1},{9,0},... | collective-permute-start | bytes 270344 | tf_op jit(solution)/shard_map/ppermute | solution.py:376
  46.0 1.5 %collective-permute-start.15 = (bf16[704,128]{1,0:T(8,128)(2,1)S(1)}, bf16[704,128]{1,0:T(8,128)(2,1)S(1)}, u32[]{:S(2)}, u32[]{:S(2)}) collective-permute-start(bf16[704,128]{1,0:T(8,128)(2,1)S(1)} %shard_map.90.mine), channel_id=1, source_target_pairs={{0,1},{1,0},{2,3},{3,2},{4,5},{5,4},{6,7},{7,6},{8,9},{9,8},{10,11... | collective-permute-start | bytes 540680 | tf_op jit(solution)/shard_map/ppermute | solution.py:376

commit v20 on v19

--- a/solution.py
+++ b/solution.py
@@ -412,6 +412,8 @@
     near, far, acc, weight_bwd = lax.optimization_barrier((*outside, acc, weight_bwd))
     outside = (near, far)
     beside = swapped(*call(edges_kernel, [edge, edge], [], 0, (*own, *outside)), "gy")
+    far, near = lax.optimization_barrier((beside[1], beside[0]))
+    beside = (near, far)
     outer, *inside = call(
         outer_kernel, [cols, ((plane_count, 2, channels, breadth), F32), plane, plane, (lines, BF16)], [],
         conv_flops // 3, (*outside, conv_weight, acc, hidden_grad),

time: 48.7 us -> 48.8 us (level)
  waiting for transfers between devices: 13.9 us -> 15.3 us
  starting transfers between devices: 19.6 us -> 18.4 us
    ppermute x8, waiting for transfers between devices: 12.6 us -> 13.5 us  [flip(): lax.ppermute(cells, ('gz', 'gy'), [(i, i ^ mask) for i in range(lax.axis_...]
    ppermute x8, starting transfers between devices: 13.9 us -> 13.2 us  [swap(): return lax.ppermute(cells, axis, pairs + [(b, a) for a, b in pairs])]
    ppermute x8, starting transfers between devices: 5.75 us -> 5.22 us  [flip(): lax.ppermute(cells, ('gz', 'gy'), [(i, i ^ mask) for i in range(lax.axis_...]
where the time goes in v20:
time: 48.8 us; the launch traced here: 48.6 us
  starting transfers between devices  18.4 us (38%)
  waiting for transfers between devices  15.3 us (31%)
  Pallas kernels  10.7 us (22%)
  local copies, waits for them, and re-layouts  3.39 us (7%)
  between operations  0.83 us (2%)
    ppermute x8, waiting for transfers between devices, flip(): lax.ppermute(cells, ('gz', 'gy'), [(i, i ^ mask) for i in range(lax.axis_...  13.5 us
    ppermute x8, starting transfers between devices, swap(): return lax.ppermute(cells, axis, pairs + [(b, a) for a, b in pairs])  13.2 us
    pallas_call x18, Pallas kernels, call(): pl.pallas_call(kernel, out_shape=[jax.ShapeDtypeStruct(s, d) for s, d in...  10.7 us
    ppermute x8, starting transfers between devices, flip(): lax.ppermute(cells, ('gz', 'gy'), [(i, i ^ mask) for i in range(lax.axis_...  5.22 us
    unnamed x9, local copies, waits for them, and re-layouts  2.88 us
    ppermute x8, waiting for transfers between devices, swap(): return lax.ppermute(cells, axis, pairs + [(b, a) for a, b in pairs])  1.73 us
  transfers between devices with their start and end apart: 16, of which 9 were waited for; matrix products, arithmetic and copies ran while one was open for 4% of the time, Pallas kernels for 16%

profile of v20, /device:TPU:0, one launch (start us, length us, event | category | flops | bytes accessed | tf_op | source)
XLA Modules:
  0.0 48.6 jit_solution(13513361467842842577)
XLA Ops:
  0.6 0.9 %copy-done.1 = bf16[64,2,8,128]{3,2,1,0:T(8,128)(2,1)S(1)} copy-done((bf16[64,2,8,128]{3,2,1,0:T(8,128)(2,1)S(1)}, bf16[64,2,8,128]{3,2,1,0:T(8,128)(2,1)}, u32[]{:S(2)}) %copy-start.1) | copy-done | bytes 262168
  1.6 0.2 shard_map.75
  1.8 3.0 %collective-permute-start = (bf16[8,64,128]{2,1,0:T(8,128)(2,1)S(1)}, bf16[8,64,128]{2,1,0:T(8,128)(2,1)S(1)}, u32[]{:S(2)}, u32[]{:S(2)}) collective-permute-start(bf16[8,64,128]{2,1,0:T(8,128)(2,1)S(1)} %get-tuple-element.53.near), channel_id=1, source_target_pairs={{0,4},{8,12},{16,20},{24,28},{4,0},{12,8},{20,16},{28,24},{1,5},{9... | collective-permute-start | bytes 393224 | tf_op jit(solution)/shard_map/ppermute | solution.py:370
  4.8 3.5 %collective-permute-start.1 = (bf16[8,64,128]{2,1,0:T(8,128)(2,1)S(1)}, bf16[8,64,128]{2,1,0:T(8,128)(2,1)S(1)}, u32[]{:S(2)}, u32[]{:S(2)}) collective-permute-start(bf16[8,64,128]{2,1,0:T(8,128)(2,1)S(1)} %get-tuple-element.54.far), channel_id=1, source_target_pairs={{4,8},{12,16},{20,24},{28,0},{8,4},{16,12},{24,20},{0,28},{5,9},{1... | collective-permute-start | bytes 393224 | tf_op jit(solution)/shard_map/ppermute | solution.py:370
  8.4 1.2 %copy.9 = bf16[3,3,64,192]{2,3,1,0:T(8,128)(2,1)S(1)} copy(bf16[3,3,64,192]{3,2,1,0:T(8,128)(2,1)} %w_ref.5) | data formatting | bytes 442368 | tf_op args[1]
  9.6 0.0 copy-start
  9.6 0.0 copy-start.2
  9.7 0.0 copy-start.3
  9.7 0.2 copy.10
  9.9 0.7 %copy-done = bf16[3,3,64,192]{3,2,1,0:T(8,128)(2,1)S(1)} copy-done((bf16[3,3,64,192]{3,2,1,0:T(8,128)(2,1)S(1)}, bf16[3,3,64,192]{3,2,1,0:T(8,128)(2,1)}, u32[]{:S(2)}) %copy-start) | copy-done | bytes 221208
  10.6 0.0 copy-done.2
  10.6 1.9 %shard_map.76 = (bf16[2,10,192,128]{3,2,1,0:T(8,128)(2,1)S(1)}, f32[2,8,64,128]{3,2,1,0:T(8,128)S(1)}, f32[2,8,64,128]{3,2,1,0:T(8,128)S(1)}) custom-call(bf16[8,64,128]{2,1,0:T(8,128)(2,1)S(1)} %get-tuple-element.53.near, bf16[8,64,128]{2,1,0:T(8,128)(2,1)S(1)} %get-tuple-element.54.far, bf16[3,3,64,192]{3,2,1,0:T(8,128)(2,1)S(1)} %copy-done, ...), custom_call_target="tpu_custom_call" | custom-call | flops 301989888 | bytes 2711552 | tf_op jit(solution)/shard_map/pallas_call | solution.py:20
  12.5 0.0 collective-permute-done.near.near_in
  12.5 0.0 collective-permute-done.1.far.far_in
  12.6 0.4 collective-permute-start.2
  13.0 1.2 %collective-permute-start.3 = (bf16[4,64,128]{2,1,0:T(8,128)(2,1)S(1)}, bf16[4,64,128]{2,1,0:T(8,128)(2,1)S(1)}, u32[]{:S(2)}, u32[]{:S(2)}) collective-permute-start(bf16[4,64,128]{2,1,0:T(8,128)(2,1)S(1)} %get-tuple-element.63), channel_id=1, source_target_pairs={{0,1},{2,3},{1,0},{3,2},{4,5},{6,7},{5,4},{7,6},{8,9},{10,11},{9,8... | collective-permute-start | bytes 196616 | tf_op jit(solution)/shard_map/ppermute | solution.py:370
  14.3 1.0 %shard_map.77 = (bf16[2,10,192,128]{3,2,1,0:T(8,128)(2,1)S(1)}, f32[2,2,64,128]{3,2,1,0:T(8,128)S(1)}, bf16[8,64,128]{2,1,0:T(8,128)(2,1)S(1)}, bf16[8,64,128]{2...) custom-call(bf16[8,64,128]{2,1,0:T(8,128)(2,1)S(1)} %collective-permute-done.near.near_in, ...), custom_call_target="tpu_custom_call" | custom-call | flops 150994944 | bytes 3170304 | tf_op jit(solution)/shard_map/pallas_call | solution.py:20
  15.3 1.7 %collective-permute-done.2.far = bf16[4,64,128]{2,1,0:T(8,128)(2,1)S(1)} collective-permute-done((bf16[4,64,128]{2,1,0:T(8,128)(2,1)S(1)}, bf16[4,64,128]{2,1,0:T(8,128)(2,1)S(1)}, u32[]{:S(2)}, u32[]{:S(2)}) %collective-permute-start.2) | collective-permute-done | bytes 65568 | tf_op jit(solution)/shard_map/ppermute | solution.py:370
  17.0 0.0 collective-permute-done.3.near
  17.0 0.4 shard_map.79
  17.4 1.2 %shard_map.80 = (f32[704,128]{1,0:T(8,128)S(1)}, bf16[704,128]{1,0:T(8,128)(2,1)S(1)}) custom-call(bf16[2,10,192,128]{3,2,1,0:T(8,128)(2,1)S(1)} %get-tuple-element.55.inner, bf16[2,10,192,128]{3,2,1,0:T(8,128)(2,1)S(1)} %get-tuple-element.61.outer, bf16[4,2,192,128]{3,2,1,0:T(8,128)(2,1)S(1)} %get-tuple-element.70.edges, ...), custom_call_target="tpu_custom_call" | custom-call | flops 452984832 | bytes 3489792 | tf_op jit(solution)/shard_map/pallas_call | solution.py:20
  18.7 0.2 collective-permute-start.4
  18.8 1.3 %collective-permute-done.4.other = bf16[704,128]{1,0:T(8,128)(2,1)S(1)} collective-permute-done((bf16[704,128]{1,0:T(8,128)(2,1)S(1)}, bf16[704,128]{1,0:T(8,128)(2,1)S(1)}, u32[]{:S(2)}, u32[]{:S(2)}) %collective-permute-start.4) | collective-permute-done | bytes 180256 | tf_op jit(solution)/shard_map/ppermute | solution.py:376
  20.1 0.1 shard_map.81
  20.2 0.2 collective-permute-start.5
  20.4 1.5 %collective-permute-start.8 = (bf16[8,64,128]{2,1,0:T(8,128)(2,1)S(1)}, bf16[8,64,128]{2,1,0:T(8,128)(2,1)S(1)}, u32[]{:S(2)}, u32[]{:S(2)}) collective-permute-start(bf16[8,64,128]{2,1,0:T(8,128)(2,1)S(1)} %get-tuple-element.83.near), channel_id=1, source_target_pairs={{0,4},{8,12},{16,20},{24,28},{4,0},{12,8},{20,16},{28,24},{1,5},{9... | collective-permute-start | bytes 393224 | tf_op jit(solution)/shard_map/ppermute | solution.py:370
  21.9 2.4 %collective-permute-start.9 = (bf16[8,64,128]{2,1,0:T(8,128)(2,1)S(1)}, bf16[8,64,128]{2,1,0:T(8,128)(2,1)S(1)}, u32[]{:S(2)}, u32[]{:S(2)}) collective-permute-start(bf16[8,64,128]{2,1,0:T(8,128)(2,1)S(1)} %get-tuple-element.84.far), channel_id=1, source_target_pairs={{4,8},{12,16},{20,24},{28,0},{8,4},{16,12},{24,20},{0,28},{5,9},{1... | collective-permute-start | bytes 393224 | tf_op jit(solution)/shard_map/ppermute | solution.py:370
  24.3 0.5 %collective-permute-done.5.other = bf16[352,128]{1,0:T(8,128)(2,1)S(1)} collective-permute-done((bf16[352,128]{1,0:T(8,128)(2,1)S(1)}, bf16[352,128]{1,0:T(8,128)(2,1)S(1)}, u32[]{:S(2)}, u32[]{:S(2)}) %collective-permute-start.5) | collective-permute-done | bytes 90144 | tf_op jit(solution)/shard_map/ppermute | solution.py:376
  24.9 1.4 %collective-permute-start.6 = (bf16[176,128]{1,0:T(8,128)(2,1)S(1)}, bf16[176,128]{1,0:T(8,128)(2,1)S(1)}, u32[]{:S(2)}, u32[]{:S(2)}) collective-permute-start(bf16[176,128]{1,0:T(8,128)(2,1)S(1)} %get-tuple-element.82), channel_id=1, source_target_pairs={{0,3},{1,2},{2,1},{3,0},{4,7},{5,6},{6,5},{7,4},{8,11},{9,10},{10,... | collective-permute-start | bytes 135176 | tf_op jit(solution)/shard_map/ppermute | solution.py:376
  26.3 2.1 %collective-permute-done.6.y = bf16[176,128]{1,0:T(8,128)(2,1)S(1)} collective-permute-done((bf16[176,128]{1,0:T(8,128)(2,1)S(1)}, bf16[176,128]{1,0:T(8,128)(2,1)S(1)}, u32[]{:S(2)}, u32[]{:S(2)}) %collective-permute-start.6) | collective-permute-done | bytes 45088 | tf_op jit(solution)/shard_map/ppermute | solution.py:376
  28.5 0.7 %collective-permute-start.7 = (bf16[176,128]{1,0:T(8,128)(2,1)S(1)}, bf16[176,128]{1,0:T(8,128)(2,1)S(1)}, u32[]{:S(2)}, u32[]{:S(2)}) collective-permute-start(bf16[176,128]{1,0:T(8,128)(2,1)S(1)} %shard_map.83.x), channel_id=1, source_target_pairs={{0,5},{1,4},{2,7},{3,6},{4,1},{5,0},{6,3},{7,2},{8,13},{9,12},{10,... | collective-permute-start | bytes 135176 | tf_op jit(solution)/shard_map/ppermute | solution.py:376
  29.2 2.8 %collective-permute-done.7.y = bf16[176,128]{1,0:T(8,128)(2,1)S(1)} collective-permute-done((bf16[176,128]{1,0:T(8,128)(2,1)S(1)}, bf16[176,128]{1,0:T(8,128)(2,1)S(1)}, u32[]{:S(2)}, u32[]{:S(2)}) %collective-permute-start.7) | collective-permute-done | bytes 45088 | tf_op jit(solution)/shard_map/ppermute | solution.py:376
  32.0 0.0 collective-permute-done.8.near_in
  32.0 1.8 %collective-permute-start.10 = (bf16[176,128]{1,0:T(8,128)(2,1)S(1)}, bf16[176,128]{1,0:T(8,128)(2,1)S(1)}, u32[]{:S(2)}, u32[]{:S(2)}) collective-permute-start(bf16[176,128]{1,0:T(8,128)(2,1)S(1)} %shard_map.84.x), channel_id=1, source_target_pairs={{0,17},{1,16},{2,19},{3,18},{4,21},{5,20},{6,23},{7,22},{8,25},{9,... | collective-permute-start | bytes 135176 | tf_op jit(solution)/shard_map/ppermute | solution.py:376
  33.9 0.1 collective-permute-start.12
  33.9 1.0 %collective-permute-start.13 = (bf16[4,64,128]{2,1,0:T(8,128)(2,1)S(1)}, bf16[4,64,128]{2,1,0:T(8,128)(2,1)S(1)}, u32[]{:S(2)}, u32[]{:S(2)}) collective-permute-start(bf16[4,64,128]{2,1,0:T(8,128)(2,1)S(1)} %get-tuple-element.93), channel_id=1, source_target_pairs={{1,2},{3,0},{2,1},{0,3},{5,6},{7,4},{6,5},{4,7},{9,10},{11,8},{10,... | collective-permute-start | bytes 196616 | tf_op jit(solution)/shard_map/ppermute | solution.py:370
  34.9 1.1 %shard_map.86 = bf16[128,256]{1,0:T(8,128)(2,1)} custom-call(bf16[2,8,64,128]{3,2,1,0:T(8,128)(2,1)S(1)} %get-tuple-element.86.h_ref, bf16[2,2,128,128]{3,2,1,0:T(8,128)(2,1)S(1)} %copy-done.2), custom_call_target="tpu_custom_call" | custom-call | flops 45298484 | bytes 458752 | tf_op jit(solution)/shard_map/pallas_call | solution.py:20
  36.0 1.7 %collective-permute-done.10.y = bf16[176,128]{1,0:T(8,128)(2,1)S(1)} collective-permute-done((bf16[176,128]{1,0:T(8,128)(2,1)S(1)}, bf16[176,128]{1,0:T(8,128)(2,1)S(1)}, u32[]{:S(2)}, u32[]{:S(2)}) %collective-permute-start.10) | collective-permute-done | bytes 45088 | tf_op jit(solution)/shard_map/ppermute | solution.py:376
  37.7 0.7 %collective-permute-start.11 = (bf16[176,128]{1,0:T(8,128)(2,1)S(1)}, bf16[176,128]{1,0:T(8,128)(2,1)S(1)}, u32[]{:S(2)}, u32[]{:S(2)}) collective-permute-start(bf16[176,128]{1,0:T(8,128)(2,1)S(1)} %shard_map.85.mine), channel_id=1, source_target_pairs={{0,3},{1,2},{2,1},{3,0},{4,7},{5,6},{6,5},{7,4},{8,11},{9,10},{10,... | collective-permute-start | bytes 135176 | tf_op jit(solution)/shard_map/ppermute | solution.py:376
  38.4 0.2 copy.11.w_ref
  38.6 2.3 %shard_map.88.acc_ref = f32[2,8,64,128]{3,2,1,0:T(8,128)S(1)} custom-call(bf16[8,64,128]{2,1,0:T(8,128)(2,1)S(1)} %get-tuple-element.83.near, bf16[8,64,128]{2,1,0:T(8,128)(2,1)S(1)} %get-tuple-element.84.far, bf16[8,64,128]{2,1,0:T(8,128)(2,1)S(1)} %collective-permute-done.8.near_in, bf16[8,64,128]{2,1,0:T(8,128)(2,1)S(1)} %collective-permute-done.9.far_in, ...), custom_call_target="tpu_custom_call" | custom-call | flops 452984832 | bytes 1269760 | tf_op jit(solution)/shard_map/pallas_call | solution.py:20
  40.9 0.5 %collective-permute-done.11.other = bf16[176,128]{1,0:T(8,128)(2,1)S(1)} collective-permute-done((bf16[176,128]{1,0:T(8,128)(2,1)S(1)}, bf16[176,128]{1,0:T(8,128)(2,1)S(1)}, u32[]{:S(2)}, u32[]{:S(2)}) %collective-permute-start.11) | collective-permute-done | bytes 45088 | tf_op jit(solution)/shard_map/ppermute | solution.py:376
  41.4 0.1 collective-permute-start.14
  41.5 1.3 %shard_map.91 = f32[1024,128]{1,0:T(8,128)} custom-call(bf16[4,64,128]{2,1,0:T(8,128)(2,1)S(1)} %collective-permute-done.12.near, bf16[4,64,128]{2,1,0:T(8,128)(2,1)S(1)} %collective-permute-done.13.far, f32[2,8,64,128]{3,2,1,0:T(8,128)S(1)} %shard_map.88.acc_ref, bf16[3,3,64,192]{3,2,1,0:T(8,128)(2,1)S(1)} %copy.11.w_ref), custom_call_target="tpu_custom_call" | custom-call | flops 45298484 | bytes 1400832 | tf_op jit(solution)/shard_map/pallas_call | solution.py:20
  42.8 3.3 %collective-permute-done.14.other = bf16[352,128]{1,0:T(8,128)(2,1)S(1)} collective-permute-done((bf16[352,128]{1,0:T(8,128)(2,1)S(1)}, bf16[352,128]{1,0:T(8,128)(2,1)S(1)}, u32[]{:S(2)}, u32[]{:S(2)}) %collective-permute-start.14) | collective-permute-done | bytes 90144 | tf_op jit(solution)/shard_map/ppermute | solution.py:376
  46.1 0.2 collective-permute-start.15
  46.3 1.3 %collective-permute-done.15.other = bf16[704,128]{1,0:T(8,128)(2,1)S(1)} collective-permute-done((bf16[704,128]{1,0:T(8,128)(2,1)S(1)}, bf16[704,128]{1,0:T(8,128)(2,1)S(1)}, u32[]{:S(2)}, u32[]{:S(2)}) %collective-permute-start.15) | collective-permute-done | bytes 180256 | tf_op jit(solution)/shard_map/ppermute | solution.py:376
  47.6 1.0 %shard_map.92 = (f32[3,3,64,192]{3,2,1,0:T(8,128)}, f32[2,2,128,128]{3,2,1,0:T(8,128)}) custom-call(bf16[704,128]{1,0:T(8,128)(2,1)S(1)} %shard_map.90.mine, bf16[704,128]{1,0:T(8,128)(2,1)S(1)} %collective-permute-done.15.other), custom_call_target="tpu_custom_call" | custom-call | bytes 1064960 | tf_op jit(solution)/shard_map/pallas_call | solution.py:20
  (14 shorter events, 0.2 us)
Async XLA Ops:
  0.6 1.0 %copy-start.1 = (bf16[64,2,8,128]{3,2,1,0:T(8,128)(2,1)S(1)}, bf16[64,2,8,128]{3,2,1,0:T(8,128)(2,1)}, u32[]{:S(2)}) copy-start(bf16[64,2,8,128]{3,2,1,0:T(8,128)(2,1)} %f_ref.1) | copy-start | bytes 786436
  1.8 10.7 %collective-permute-start = (bf16[8,64,128]{2,1,0:T(8,128)(2,1)S(1)}, bf16[8,64,128]{2,1,0:T(8,128)(2,1)S(1)}, u32[]{:S(2)}, u32[]{:S(2)}) collective-permute-start(bf16[8,64,128]{2,1,0:T(8,128)(2,1)S(1)} %get-tuple-element.53.near), channel_id=1, source_target_pairs={{0,4},{8,12},{16,20},{24,28},{4,0},{12,8},{20,16},{28,24},{1,5},{9... | collective-permute-start | bytes 393224 | tf_op jit(solution)/shard_map/ppermute | solution.py:370
  4.8 7.7 %collective-permute-start.1 = (bf16[8,64,128]{2,1,0:T(8,128)(2,1)S(1)}, bf16[8,64,128]{2,1,0:T(8,128)(2,1)S(1)}, u32[]{:S(2)}, u32[]{:S(2)}) collective-permute-start(bf16[8,64,128]{2,1,0:T(8,128)(2,1)S(1)} %get-tuple-element.54.far), channel_id=1, source_target_pairs={{4,8},{12,16},{20,24},{28,0},{8,4},{16,12},{24,20},{0,28},{5,9},{1... | collective-permute-start | bytes 393224 | tf_op jit(solution)/shard_map/ppermute | solution.py:370
  9.6 1.0 %copy-start = (bf16[3,3,64,192]{3,2,1,0:T(8,128)(2,1)S(1)}, bf16[3,3,64,192]{3,2,1,0:T(8,128)(2,1)}, u32[]{:S(2)}) copy-start(bf16[3,3,64,192]{3,2,1,0:T(8,128)(2,1)} %w_ref.5) | copy-start | bytes 663556
  9.6 1.0 %copy-start.2 = (bf16[2,2,128,128]{3,2,1,0:T(8,128)(2,1)S(1)}, bf16[2,2,128,128]{3,2,1,0:T(8,128)(2,1)}, u32[]{:S(2)}) copy-start(bf16[2,2,128,128]{3,2,1,0:T(8,128)(2,1)} %d_ref.3) | copy-start | bytes 393220
  9.7 1.0 %copy-start.3 = (bf16[128,1,256]{2,0,1:T(8,128)(2,1)S(1)}, bf16[128,1,256]{2,0,1:T(8,128)(2,1)}, u32[]{:S(2)}) copy-start(bf16[128,1,256]{2,0,1:T(8,128)(2,1)} %param.7) | copy-start | bytes 196612
  12.6 4.4 %collective-permute-start.2 = (bf16[4,64,128]{2,1,0:T(8,128)(2,1)S(1)}, bf16[4,64,128]{2,1,0:T(8,128)(2,1)S(1)}, u32[]{:S(2)}, u32[]{:S(2)}) collective-permute-start(bf16[4,64,128]{2,1,0:T(8,128)(2,1)S(1)} %get-tuple-element.62), channel_id=1, source_target_pairs={{1,2},{3,0},{2,1},{0,3},{5,6},{7,4},{6,5},{4,7},{9,10},{11,8},{10,... | collective-permute-start | bytes 196616 | tf_op jit(solution)/shard_map/ppermute | solution.py:370
  13.0 4.0 %collective-permute-start.3 = (bf16[4,64,128]{2,1,0:T(8,128)(2,1)S(1)}, bf16[4,64,128]{2,1,0:T(8,128)(2,1)S(1)}, u32[]{:S(2)}, u32[]{:S(2)}) collective-permute-start(bf16[4,64,128]{2,1,0:T(8,128)(2,1)S(1)} %get-tuple-element.63), channel_id=1, source_target_pairs={{0,1},{2,3},{1,0},{3,2},{4,5},{6,7},{5,4},{7,6},{8,9},{10,11},{9,8... | collective-permute-start | bytes 196616 | tf_op jit(solution)/shard_map/ppermute | solution.py:370
  18.7 1.5 %collective-permute-start.4 = (bf16[704,128]{1,0:T(8,128)(2,1)S(1)}, bf16[704,128]{1,0:T(8,128)(2,1)S(1)}, u32[]{:S(2)}, u32[]{:S(2)}) collective-permute-start(bf16[704,128]{1,0:T(8,128)(2,1)S(1)} %get-tuple-element.76), channel_id=1, source_target_pairs={{0,1},{1,0},{2,3},{3,2},{4,5},{5,4},{6,7},{7,6},{8,9},{9,8},{10,11... | collective-permute-start | bytes 540680 | tf_op jit(solution)/shard_map/ppermute | solution.py:376
  20.2 4.7 %collective-permute-start.5 = (bf16[352,128]{1,0:T(8,128)(2,1)S(1)}, bf16[352,128]{1,0:T(8,128)(2,1)S(1)}, u32[]{:S(2)}, u32[]{:S(2)}) collective-permute-start(bf16[352,128]{1,0:T(8,128)(2,1)S(1)} %get-tuple-element.80), channel_id=1, source_target_pairs={{0,9},{1,8},{2,11},{3,10},{4,13},{5,12},{6,15},{7,14},{8,1},{9,0},... | collective-permute-start | bytes 270344 | tf_op jit(solution)/shard_map/ppermute | solution.py:376
  20.4 11.6 %collective-permute-start.8 = (bf16[8,64,128]{2,1,0:T(8,128)(2,1)S(1)}, bf16[8,64,128]{2,1,0:T(8,128)(2,1)S(1)}, u32[]{:S(2)}, u32[]{:S(2)}) collective-permute-start(bf16[8,64,128]{2,1,0:T(8,128)(2,1)S(1)} %get-tuple-element.83.near), channel_id=1, source_target_pairs={{0,4},{8,12},{16,20},{24,28},{4,0},{12,8},{20,16},{28,24},{1,5},{9... | collective-permute-start | bytes 393224 | tf_op jit(solution)/shard_map/ppermute | solution.py:370
  21.9 10.1 %collective-permute-start.9 = (bf16[8,64,128]{2,1,0:T(8,128)(2,1)S(1)}, bf16[8,64,128]{2,1,0:T(8,128)(2,1)S(1)}, u32[]{:S(2)}, u32[]{:S(2)}) collective-permute-start(bf16[8,64,128]{2,1,0:T(8,128)(2,1)S(1)} %get-tuple-element.84.far), channel_id=1, source_target_pairs={{4,8},{12,16},{20,24},{28,0},{8,4},{16,12},{24,20},{0,28},{5,9},{1... | collective-permute-start | bytes 393224 | tf_op jit(solution)/shard_map/ppermute | solution.py:370
  24.9 3.5 %collective-permute-start.6 = (bf16[176,128]{1,0:T(8,128)(2,1)S(1)}, bf16[176,128]{1,0:T(8,128)(2,1)S(1)}, u32[]{:S(2)}, u32[]{:S(2)}) collective-permute-start(bf16[176,128]{1,0:T(8,128)(2,1)S(1)} %get-tuple-element.82), channel_id=1, source_target_pairs={{0,3},{1,2},{2,1},{3,0},{4,7},{5,6},{6,5},{7,4},{8,11},{9,10},{10,... | collective-permute-start | bytes 135176 | tf_op jit(solution)/shard_map/ppermute | solution.py:376
  28.5 3.5 %collective-permute-start.7 = (bf16[176,128]{1,0:T(8,128)(2,1)S(1)}, bf16[176,128]{1,0:T(8,128)(2,1)S(1)}, u32[]{:S(2)}, u32[]{:S(2)}) collective-permute-start(bf16[176,128]{1,0:T(8,128)(2,1)S(1)} %shard_map.83.x), channel_id=1, source_target_pairs={{0,5},{1,4},{2,7},{3,6},{4,1},{5,0},{6,3},{7,2},{8,13},{9,12},{10,... | collective-permute-start | bytes 135176 | tf_op jit(solution)/shard_map/ppermute | solution.py:376
  32.0 5.6 %collective-permute-start.10 = (bf16[176,128]{1,0:T(8,128)(2,1)S(1)}, bf16[176,128]{1,0:T(8,128)(2,1)S(1)}, u32[]{:S(2)}, u32[]{:S(2)}) collective-permute-start(bf16[176,128]{1,0:T(8,128)(2,1)S(1)} %shard_map.84.x), channel_id=1, source_target_pairs={{0,17},{1,16},{2,19},{3,18},{4,21},{5,20},{6,23},{7,22},{8,25},{9,... | collective-permute-start | bytes 135176 | tf_op jit(solution)/shard_map/ppermute | solution.py:376
  33.9 7.6 %collective-permute-start.12 = (bf16[4,64,128]{2,1,0:T(8,128)(2,1)S(1)}, bf16[4,64,128]{2,1,0:T(8,128)(2,1)S(1)}, u32[]{:S(2)}, u32[]{:S(2)}) collective-permute-start(bf16[4,64,128]{2,1,0:T(8,128)(2,1)S(1)} %get-tuple-element.92), channel_id=1, source_target_pairs={{0,1},{2,3},{1,0},{3,2},{4,5},{6,7},{5,4},{7,6},{8,9},{10,11},{9,8... | collective-permute-start | bytes 196616 | tf_op jit(solution)/shard_map/ppermute | solution.py:370
  33.9 7.5 %collective-permute-start.13 = (bf16[4,64,128]{2,1,0:T(8,128)(2,1)S(1)}, bf16[4,64,128]{2,1,0:T(8,128)(2,1)S(1)}, u32[]{:S(2)}, u32[]{:S(2)}) collective-permute-start(bf16[4,64,128]{2,1,0:T(8,128)(2,1)S(1)} %get-tuple-element.93), channel_id=1, source_target_pairs={{1,2},{3,0},{2,1},{0,3},{5,6},{7,4},{6,5},{4,7},{9,10},{11,8},{10,... | collective-permute-start | bytes 196616 | tf_op jit(solution)/shard_map/ppermute | solution.py:370
  37.7 3.7 %collective-permute-start.11 = (bf16[176,128]{1,0:T(8,128)(2,1)S(1)}, bf16[176,128]{1,0:T(8,128)(2,1)S(1)}, u32[]{:S(2)}, u32[]{:S(2)}) collective-permute-start(bf16[176,128]{1,0:T(8,128)(2,1)S(1)} %shard_map.85.mine), channel_id=1, source_target_pairs={{0,3},{1,2},{2,1},{3,0},{4,7},{5,6},{6,5},{7,4},{8,11},{9,10},{10,... | collective-permute-start | bytes 135176 | tf_op jit(solution)/shard_map/ppermute | solution.py:376
  41.4 4.7 %collective-permute-start.14 = (bf16[352,128]{1,0:T(8,128)(2,1)S(1)}, bf16[352,128]{1,0:T(8,128)(2,1)S(1)}, u32[]{:S(2)}, u32[]{:S(2)}) collective-permute-start(bf16[352,128]{1,0:T(8,128)(2,1)S(1)} %shard_map.87.mine), channel_id=1, source_target_pairs={{0,9},{1,8},{2,11},{3,10},{4,13},{5,12},{6,15},{7,14},{8,1},{9,0},... | collective-permute-start | bytes 270344 | tf_op jit(solution)/shard_map/ppermute | solution.py:376
  46.1 1.5 %collective-permute-start.15 = (bf16[704,128]{1,0:T(8,128)(2,1)S(1)}, bf16[704,128]{1,0:T(8,128)(2,1)S(1)}, u32[]{:S(2)}, u32[]{:S(2)}) collective-permute-start(bf16[704,128]{1,0:T(8,128)(2,1)S(1)} %shard_map.90.mine), channel_id=1, source_target_pairs={{0,1},{1,0},{2,3},{3,2},{4,5},{5,4},{6,7},{7,6},{8,9},{9,8},{10,11... | collective-permute-start | bytes 540680 | tf_op jit(solution)/shard_map/ppermute | solution.py:376

commit v21 on v18

--- a/solution.py
+++ b/solution.py
@@ -51,6 +51,10 @@
     for z in range(2):
         near_row[z] = choose(even_y, ends[rows - 1][z], ends[0][z])
         far_row[z] = choose(even_y, ends[0][z], ends[rows - 1][z])
+
+
+def copy_kernel(x, out):
+    out[...] = x[...]
 
 
 def outer_rows_kernel(near_in, far_in, near_ref, far_ref):
@@ -408,6 +412,7 @@
     out_channels = down_weight.shape[2]
     count = lax.axis_size("gz") * lax.axis_size("gy")
     grad_scale = 1.0 / math.sqrt(plane_count * row_count * breadth * count)
+    (conv_weight,) = call(copy_kernel, [(conv_weight.shape, BF16)], [], 0, (conv_weight,))
     turned = conv_weight.reshape(3, 3, channels, 3, channels)[::-1, ::-1, :, ::-1]
     weight_bwd = turned.transpose(0, 1, 4, 3, 2).reshape(3, 3, channels, 3 * channels)
     cot = cotangent.reshape(out_channels, -1)
@@ -433,6 +438,8 @@
     near, far, acc = lax.optimization_barrier((*outside, acc))
     outside = (near, far)
     beside = swapped(*call(outer_rows_kernel, [pair, pair], [], 0, outside), "gy")
+    far, near = lax.optimization_barrier((beside[1], beside[0]))
+    beside = (near, far)
     outer, *inside = call(
         outer_kernel, [cols, ((plane_count, 2, channels, breadth), F32), plane, plane, (lines, BF16)], [],
         conv_flops // 3, (*outside, conv_weight, acc, hidden_grad),

time: 50.9 us -> 49.3 us (0.969)
  waiting for transfers between devices: 17.5 us -> 15.3 us
    ppermute x10, waiting for transfers between devices: 2.96 us -> 1.32 us  [swap(): return lax.ppermute(cells, axis, pairs + [(b, a) for a, b in pairs])]
    ppermute x8, waiting for transfers between devices: 14.5 us -> 14 us  [flip(): lax.ppermute(cells, ('gz', 'gy'), [(i, i ^ mask) for i in range(lax.axis_...]
    unnamed x11 -> x8, local copies, waits for them, and re-layouts: 2.18 us -> 2.04 us
    pallas_call x18 -> x19, Pallas kernels: 10.6 us -> 10.7 us  [call(): pl.pallas_call(kernel, out_shape=[jax.ShapeDtypeStruct(s, d) for s, d in...]
  transfers between devices with their start and end apart: 18 -> 18, of which waited for: 9 -> 9; matrix products, arithmetic and copies ran while one was open for 2% -> 2% of each run, Pallas kernels for 15% -> 16%
where the time goes in v21:
time: 49.3 us; the launch traced here: 49.1 us
  starting transfers between devices  19.5 us (40%)
  waiting for transfers between devices  15.3 us (31%)
  Pallas kernels  10.7 us (22%)
  local copies, waits for them, and re-layouts  2.82 us (6%)
  between operations  0.84 us (2%)
    ppermute x10, starting transfers between devices, swap(): return lax.ppermute(cells, axis, pairs + [(b, a) for a, b in pairs])  14.6 us
    ppermute x8, waiting for transfers between devices, flip(): lax.ppermute(cells, ('gz', 'gy'), [(i, i ^ mask) for i in range(lax.axis_...  14 us
    pallas_call x19, Pallas kernels, call(): pl.pallas_call(kernel, out_shape=[jax.ShapeDtypeStruct(s, d) for s, d in...  10.7 us
    ppermute x8, starting transfers between devices, flip(): lax.ppermute(cells, ('gz', 'gy'), [(i, i ^ mask) for i in range(lax.axis_...  4.86 us
    unnamed x8, local copies, waits for them, and re-layouts  2.04 us
    ppermute x10, waiting for transfers between devices, swap(): return lax.ppermute(cells, axis, pairs + [(b, a) for a, b in pairs])  1.32 us
  transfers between devices with their start and end apart: 18, of which 9 were waited for; matrix products, arithmetic and copies ran while one was open for 2% of the time, Pallas kernels for 16%

profile of v21, /device:TPU:0, one launch (start us, length us, event | category | flops | bytes accessed | tf_op | source)
XLA Modules:
  0.0 49.1 jit_solution(7616995054398551635)
XLA Ops:
  0.6 0.9 %copy-done.1 = bf16[64,2,8,128]{3,2,1,0:T(8,128)(2,1)S(1)} copy-done((bf16[64,2,8,128]{3,2,1,0:T(8,128)(2,1)S(1)}, bf16[64,2,8,128]{3,2,1,0:T(8,128)(2,1)}, u32[]{:S(2)}) %copy-start.1) | copy-done | bytes 262168
  1.6 0.2 shard_map.75
  1.8 3.0 %collective-permute-start.2 = (bf16[8,64,128]{2,1,0:T(8,128)(2,1)S(1)}, bf16[8,64,128]{2,1,0:T(8,128)(2,1)S(1)}, u32[]{:S(2)}, u32[]{:S(2)}) collective-permute-start(bf16[8,64,128]{2,1,0:T(8,128)(2,1)S(1)} %get-tuple-element.54.near), channel_id=1, source_target_pairs={{0,4},{8,12},{16,20},{24,28},{4,0},{12,8},{20,16},{28,24},{1,5},{9... | collective-permute-start | bytes 393224 | tf_op jit(solution)/shard_map/ppermute | solution.py:392
  4.8 3.5 %collective-permute-start.3 = (bf16[8,64,128]{2,1,0:T(8,128)(2,1)S(1)}, bf16[8,64,128]{2,1,0:T(8,128)(2,1)S(1)}, u32[]{:S(2)}, u32[]{:S(2)}) collective-permute-start(bf16[8,64,128]{2,1,0:T(8,128)(2,1)S(1)} %get-tuple-element.55.far), channel_id=1, source_target_pairs={{4,8},{12,16},{20,24},{28,0},{8,4},{16,12},{24,20},{0,28},{5,9},{1... | collective-permute-start | bytes 393224 | tf_op jit(solution)/shard_map/ppermute | solution.py:392
  8.4 1.6 %collective-permute-start.1 = (bf16[2,64,128]{2,1,0:T(8,128)(2,1)S(1)}, bf16[2,64,128]{2,1,0:T(8,128)(2,1)S(1)}, u32[]{:S(2)}, u32[]{:S(2)}) collective-permute-start(bf16[2,64,128]{2,1,0:T(8,128)(2,1)S(1)} %get-tuple-element.57), channel_id=1, source_target_pairs={{1,2},{3,0},{2,1},{0,3},{5,6},{7,4},{6,5},{4,7},{9,10},{11,8},{10,... | collective-permute-start | bytes 98312 | tf_op jit(solution)/shard_map/ppermute | solution.py:392
  10.0 1.0 %copy-done = bf16[3,3,64,192]{3,2,1,0:T(8,128)(2,1)S(1)} copy-done((bf16[3,3,64,192]{3,2,1,0:T(8,128)(2,1)S(1)}, bf16[3,3,64,192]{3,2,1,0:T(8,128)(2,1)}, u32[]{:S(2)}) %copy-start) | copy-done | bytes 221208
  11.0 0.7 %collective-permute-done.1.far_row = bf16[2,64,128]{2,1,0:T(8,128)(2,1)S(1)} collective-permute-done((bf16[2,64,128]{2,1,0:T(8,128)(2,1)S(1)}, bf16[2,64,128]{2,1,0:T(8,128)(2,1)S(1)}, u32[]{:S(2)}, u32[]{:S(2)}) %collective-permute-start.1) | collective-permute-done | bytes 32800 | tf_op jit(solution)/shard_map/ppermute | solution.py:392
  11.7 0.1 copy-done.2
  11.8 1.9 %shard_map.77 = (bf16[2,10,192,128]{3,2,1,0:T(8,128)(2,1)S(1)}, f32[2,8,64,128]{3,2,1,0:T(8,128)S(1)}, f32[2,8,64,128]{3,2,1,0:T(8,128)S(1)}) custom-call(bf16[8,64,128]{2,1,0:T(8,128)(2,1)S(1)} %get-tuple-element.54.near, bf16[8,64,128]{2,1,0:T(8,128)(2,1)S(1)} %get-tuple-element.55.far, bf16[2,64,128]{2,1,0:T(8,128)(2,1)S(1)} %collective-permute-done.near_row, ...), custom_call_target="tpu_custom_call" | custom-call | flops 301989888 | bytes 2777088 | tf_op jit(solution)/shard_map/pallas_call | solution.py:20
  13.8 0.0 collective-permute-done.3.far.far_in
  13.8 1.8 %collective-permute-start.4 = (bf16[2,64,128]{2,1,0:T(8,128)(2,1)S(1)}, bf16[2,64,128]{2,1,0:T(8,128)(2,1)S(1)}, u32[]{:S(2)}, u32[]{:S(2)}) collective-permute-start(bf16[2,64,128]{2,1,0:T(8,128)(2,1)S(1)} %get-tuple-element.65), channel_id=1, source_target_pairs={{1,2},{3,0},{2,1},{0,3},{5,6},{7,4},{6,5},{4,7},{9,10},{11,8},{10,... | collective-permute-start | bytes 98312 | tf_op jit(solution)/shard_map/ppermute | solution.py:392
  15.7 0.0 collective-permute-start.5
  15.7 1.0 %shard_map.78 = (bf16[2,10,192,128]{3,2,1,0:T(8,128)(2,1)S(1)}, f32[2,2,64,128]{3,2,1,0:T(8,128)S(1)}, bf16[8,64,128]{2,1,0:T(8,128)(2,1)S(1)}, bf16[8,64,128]{2...) custom-call(bf16[8,64,128]{2,1,0:T(8,128)(2,1)S(1)} %collective-permute-done.2.near.near_in, ...), custom_call_target="tpu_custom_call" | custom-call | flops 150994944 | bytes 3170304 | tf_op jit(solution)/shard_map/pallas_call | solution.py:20
  16.7 0.6 %collective-permute-done.4.far = bf16[2,64,128]{2,1,0:T(8,128)(2,1)S(1)} collective-permute-done((bf16[2,64,128]{2,1,0:T(8,128)(2,1)S(1)}, bf16[2,64,128]{2,1,0:T(8,128)(2,1)S(1)}, u32[]{:S(2)}, u32[]{:S(2)}) %collective-permute-start.4) | collective-permute-done | bytes 32800 | tf_op jit(solution)/shard_map/ppermute | solution.py:392
  17.3 0.0 collective-permute-done.5.near
  17.3 0.3 shard_map.80
  17.6 1.2 %shard_map.81 = (f32[704,128]{1,0:T(8,128)S(1)}, bf16[704,128]{1,0:T(8,128)(2,1)S(1)}) custom-call(bf16[2,10,192,128]{3,2,1,0:T(8,128)(2,1)S(1)} %get-tuple-element.58.inner, bf16[2,10,192,128]{3,2,1,0:T(8,128)(2,1)S(1)} %get-tuple-element.64.outer, bf16[2,2,192,128]{3,2,1,0:T(8,128)(2,1)S(1)} %get-tuple-element.73.edges, ...), custom_call_target="tpu_custom_call" | custom-call | flops 452984832 | bytes 3293184 | tf_op jit(solution)/shard_map/pallas_call | solution.py:20
  18.8 0.7 %collective-permute-start.6 = (bf16[704,128]{1,0:T(8,128)(2,1)S(1)}, bf16[704,128]{1,0:T(8,128)(2,1)S(1)}, u32[]{:S(2)}, u32[]{:S(2)}) collective-permute-start(bf16[704,128]{1,0:T(8,128)(2,1)S(1)} %get-tuple-element.79), channel_id=1, source_target_pairs={{0,1},{1,0},{2,3},{3,2},{4,5},{5,4},{6,7},{7,6},{8,9},{9,8},{10,11... | collective-permute-start | bytes 540680 | tf_op jit(solution)/shard_map/ppermute | solution.py:398
  19.5 1.0 %collective-permute-done.6.other = bf16[704,128]{1,0:T(8,128)(2,1)S(1)} collective-permute-done((bf16[704,128]{1,0:T(8,128)(2,1)S(1)}, bf16[704,128]{1,0:T(8,128)(2,1)S(1)}, u32[]{:S(2)}, u32[]{:S(2)}) %collective-permute-start.6) | collective-permute-done | bytes 180256 | tf_op jit(solution)/shard_map/ppermute | solution.py:398
  20.6 0.1 shard_map.82
  20.6 0.1 collective-permute-start.7
  20.7 1.0 %collective-permute-start.10 = (bf16[8,64,128]{2,1,0:T(8,128)(2,1)S(1)}, bf16[8,64,128]{2,1,0:T(8,128)(2,1)S(1)}, u32[]{:S(2)}, u32[]{:S(2)}) collective-permute-start(bf16[8,64,128]{2,1,0:T(8,128)(2,1)S(1)} %get-tuple-element.86.near), channel_id=1, source_target_pairs={{0,4},{8,12},{16,20},{24,28},{4,0},{12,8},{20,16},{28,24},{1,5},{9... | collective-permute-start | bytes 393224 | tf_op jit(solution)/shard_map/ppermute | solution.py:392
  21.7 1.9 %collective-permute-start.11 = (bf16[8,64,128]{2,1,0:T(8,128)(2,1)S(1)}, bf16[8,64,128]{2,1,0:T(8,128)(2,1)S(1)}, u32[]{:S(2)}, u32[]{:S(2)}) collective-permute-start(bf16[8,64,128]{2,1,0:T(8,128)(2,1)S(1)} %get-tuple-element.87.far), channel_id=1, source_target_pairs={{4,8},{12,16},{20,24},{28,0},{8,4},{16,12},{24,20},{0,28},{5,9},{1... | collective-permute-start | bytes 393224 | tf_op jit(solution)/shard_map/ppermute | solution.py:392
  23.7 1.5 %collective-permute-done.7.other = bf16[352,128]{1,0:T(8,128)(2,1)S(1)} collective-permute-done((bf16[352,128]{1,0:T(8,128)(2,1)S(1)}, bf16[352,128]{1,0:T(8,128)(2,1)S(1)}, u32[]{:S(2)}, u32[]{:S(2)}) %collective-permute-start.7) | collective-permute-done | bytes 90144 | tf_op jit(solution)/shard_map/ppermute | solution.py:398
  25.2 2.2 %collective-permute-start.8 = (bf16[176,128]{1,0:T(8,128)(2,1)S(1)}, bf16[176,128]{1,0:T(8,128)(2,1)S(1)}, u32[]{:S(2)}, u32[]{:S(2)}) collective-permute-start(bf16[176,128]{1,0:T(8,128)(2,1)S(1)} %get-tuple-element.85), channel_id=1, source_target_pairs={{0,3},{1,2},{2,1},{3,0},{4,7},{5,6},{6,5},{7,4},{8,11},{9,10},{10,... | collective-permute-start | bytes 135176 | tf_op jit(solution)/shard_map/ppermute | solution.py:398
  27.4 1.7 %collective-permute-done.8.y = bf16[176,128]{1,0:T(8,128)(2,1)S(1)} collective-permute-done((bf16[176,128]{1,0:T(8,128)(2,1)S(1)}, bf16[176,128]{1,0:T(8,128)(2,1)S(1)}, u32[]{:S(2)}, u32[]{:S(2)}) %collective-permute-start.8) | collective-permute-done | bytes 45088 | tf_op jit(solution)/shard_map/ppermute | solution.py:398
  29.2 0.1 collective-permute-start.9
  29.2 3.5 %collective-permute-done.9.y = bf16[176,128]{1,0:T(8,128)(2,1)S(1)} collective-permute-done((bf16[176,128]{1,0:T(8,128)(2,1)S(1)}, bf16[176,128]{1,0:T(8,128)(2,1)S(1)}, u32[]{:S(2)}, u32[]{:S(2)}) %collective-permute-start.9) | collective-permute-done | bytes 45088 | tf_op jit(solution)/shard_map/ppermute | solution.py:398
  32.7 0.0 collective-permute-done.10.near_in
  32.7 0.0 collective-permute-done.11.far_in
  32.7 0.4 collective-permute-start.12
  33.1 0.3 copy.9
  33.4 1.1 %shard_map.87 = bf16[128,256]{1,0:T(8,128)(2,1)} custom-call(bf16[2,8,64,128]{3,2,1,0:T(8,128)(2,1)S(1)} %get-tuple-element.89.h_ref, bf16[2,2,128,128]{3,2,1,0:T(8,128)(2,1)S(1)} %copy-done.2), custom_call_target="tpu_custom_call" | custom-call | flops 45298484 | bytes 458752 | tf_op jit(solution)/shard_map/pallas_call | solution.py:20
  34.5 0.4 collective-permute-start.14
  35.0 1.2 %collective-permute-start.15 = (bf16[4,64,128]{2,1,0:T(8,128)(2,1)S(1)}, bf16[4,64,128]{2,1,0:T(8,128)(2,1)S(1)}, u32[]{:S(2)}, u32[]{:S(2)}) collective-permute-start(bf16[4,64,128]{2,1,0:T(8,128)(2,1)S(1)} %get-tuple-element.95), channel_id=1, source_target_pairs={{1,2},{3,0},{2,1},{0,3},{5,6},{7,4},{6,5},{4,7},{9,10},{11,8},{10,... | collective-permute-start | bytes 196616 | tf_op jit(solution)/shard_map/ppermute | solution.py:392
  36.2 2.0 %collective-permute-done.12.y = bf16[176,128]{1,0:T(8,128)(2,1)S(1)} collective-permute-done((bf16[176,128]{1,0:T(8,128)(2,1)S(1)}, bf16[176,128]{1,0:T(8,128)(2,1)S(1)}, u32[]{:S(2)}, u32[]{:S(2)}) %collective-permute-start.12) | collective-permute-done | bytes 45088 | tf_op jit(solution)/shard_map/ppermute | solution.py:398
  38.2 1.0 %collective-permute-start.13 = (bf16[176,128]{1,0:T(8,128)(2,1)S(1)}, bf16[176,128]{1,0:T(8,128)(2,1)S(1)}, u32[]{:S(2)}, u32[]{:S(2)}) collective-permute-start(bf16[176,128]{1,0:T(8,128)(2,1)S(1)} %shard_map.86.mine), channel_id=1, source_target_pairs={{0,3},{1,2},{2,1},{3,0},{4,7},{5,6},{6,5},{7,4},{8,11},{9,10},{10,... | collective-permute-start | bytes 135176 | tf_op jit(solution)/shard_map/ppermute | solution.py:398
  39.2 0.3 copy.10
  39.5 0.2 copy.11.w_ref
  39.7 2.3 %shard_map.89.acc_ref = f32[2,8,64,128]{3,2,1,0:T(8,128)S(1)} custom-call(bf16[8,64,128]{2,1,0:T(8,128)(2,1)S(1)} %get-tuple-element.86.near, bf16[8,64,128]{2,1,0:T(8,128)(2,1)S(1)} %get-tuple-element.87.far, bf16[8,64,128]{2,1,0:T(8,128)(2,1)S(1)} %collective-permute-done.10.near_in, bf16[8,64,128]{2,1,0:T(8,128)(2,1)S(1)} %collective-permute-done.11.far_in, ...), custom_call_target="tpu_custom_call" | custom-call | flops 452984832 | bytes 1269760 | tf_op jit(solution)/shard_map/pallas_call | solution.py:20
  42.0 0.0 collective-permute-done.13.other
  42.1 0.0 collective-permute-done.15.far
  42.1 0.1 collective-permute-start.16
  42.2 1.3 %shard_map.92 = f32[1024,128]{1,0:T(8,128)} custom-call(bf16[4,64,128]{2,1,0:T(8,128)(2,1)S(1)} %collective-permute-done.14.near, bf16[4,64,128]{2,1,0:T(8,128)(2,1)S(1)} %collective-permute-done.15.far, f32[2,8,64,128]{3,2,1,0:T(8,128)S(1)} %shard_map.89.acc_ref, bf16[3,3,64,192]{3,2,1,0:T(8,128)(2,1)S(1)} %copy.11.w_ref), custom_call_target="tpu_custom_call" | custom-call | flops 45298484 | bytes 1400832 | tf_op jit(solution)/shard_map/pallas_call | solution.py:20
  43.5 3.1 %collective-permute-done.16.other = bf16[352,128]{1,0:T(8,128)(2,1)S(1)} collective-permute-done((bf16[352,128]{1,0:T(8,128)(2,1)S(1)}, bf16[352,128]{1,0:T(8,128)(2,1)S(1)}, u32[]{:S(2)}, u32[]{:S(2)}) %collective-permute-start.16) | collective-permute-done | bytes 90144 | tf_op jit(solution)/shard_map/ppermute | solution.py:398
  46.7 0.4 collective-permute-start.17
  47.0 1.1 %collective-permute-done.17.other = bf16[704,128]{1,0:T(8,128)(2,1)S(1)} collective-permute-done((bf16[704,128]{1,0:T(8,128)(2,1)S(1)}, bf16[704,128]{1,0:T(8,128)(2,1)S(1)}, u32[]{:S(2)}, u32[]{:S(2)}) %collective-permute-start.17) | collective-permute-done | bytes 180256 | tf_op jit(solution)/shard_map/ppermute | solution.py:398
  48.1 1.0 %shard_map.93 = (f32[3,3,64,192]{3,2,1,0:T(8,128)}, f32[2,2,128,128]{3,2,1,0:T(8,128)}) custom-call(bf16[704,128]{1,0:T(8,128)(2,1)S(1)} %shard_map.91.mine, bf16[704,128]{1,0:T(8,128)(2,1)S(1)} %collective-permute-done.17.other), custom_call_target="tpu_custom_call" | custom-call | bytes 1064960 | tf_op jit(solution)/shard_map/pallas_call | solution.py:20
  (19 shorter events, 0.3 us)
Async XLA Ops:
  0.6 1.0 %copy-start.1 = (bf16[64,2,8,128]{3,2,1,0:T(8,128)(2,1)S(1)}, bf16[64,2,8,128]{3,2,1,0:T(8,128)(2,1)}, u32[]{:S(2)}) copy-start(bf16[64,2,8,128]{3,2,1,0:T(8,128)(2,1)} %f_ref.1) | copy-start | bytes 786436
  1.8 12.0 %collective-permute-start.2 = (bf16[8,64,128]{2,1,0:T(8,128)(2,1)S(1)}, bf16[8,64,128]{2,1,0:T(8,128)(2,1)S(1)}, u32[]{:S(2)}, u32[]{:S(2)}) collective-permute-start(bf16[8,64,128]{2,1,0:T(8,128)(2,1)S(1)} %get-tuple-element.54.near), channel_id=1, source_target_pairs={{0,4},{8,12},{16,20},{24,28},{4,0},{12,8},{20,16},{28,24},{1,5},{9... | collective-permute-start | bytes 393224 | tf_op jit(solution)/shard_map/ppermute | solution.py:392
  4.8 8.9 %collective-permute-start.3 = (bf16[8,64,128]{2,1,0:T(8,128)(2,1)S(1)}, bf16[8,64,128]{2,1,0:T(8,128)(2,1)S(1)}, u32[]{:S(2)}, u32[]{:S(2)}) collective-permute-start(bf16[8,64,128]{2,1,0:T(8,128)(2,1)S(1)} %get-tuple-element.55.far), channel_id=1, source_target_pairs={{4,8},{12,16},{20,24},{28,0},{8,4},{16,12},{24,20},{0,28},{5,9},{1... | collective-permute-start | bytes 393224 | tf_op jit(solution)/shard_map/ppermute | solution.py:392
  8.4 2.6 %collective-permute-start = (bf16[2,64,128]{2,1,0:T(8,128)(2,1)S(1)}, bf16[2,64,128]{2,1,0:T(8,128)(2,1)S(1)}, u32[]{:S(2)}, u32[]{:S(2)}) collective-permute-start(bf16[2,64,128]{2,1,0:T(8,128)(2,1)S(1)} %get-tuple-element.56), channel_id=1, source_target_pairs={{0,1},{2,3},{1,0},{3,2},{4,5},{6,7},{5,4},{7,6},{8,9},{10,11},{9,8... | collective-permute-start | bytes 98312 | tf_op jit(solution)/shard_map/ppermute | solution.py:392
  8.4 3.3 %collective-permute-start.1 = (bf16[2,64,128]{2,1,0:T(8,128)(2,1)S(1)}, bf16[2,64,128]{2,1,0:T(8,128)(2,1)S(1)}, u32[]{:S(2)}, u32[]{:S(2)}) collective-permute-start(bf16[2,64,128]{2,1,0:T(8,128)(2,1)S(1)} %get-tuple-element.57), channel_id=1, source_target_pairs={{1,2},{3,0},{2,1},{0,3},{5,6},{7,4},{6,5},{4,7},{9,10},{11,8},{10,... | collective-permute-start | bytes 98312 | tf_op jit(solution)/shard_map/ppermute | solution.py:392
  10.0 1.0 %copy-start = (bf16[3,3,64,192]{3,2,1,0:T(8,128)(2,1)S(1)}, bf16[3,3,64,192]{3,2,1,0:T(8,128)(2,1)}, u32[]{:S(2)}) copy-start(bf16[3,3,64,192]{3,2,1,0:T(8,128)(2,1)} %x.1) | copy-start | bytes 663556
  10.9 0.9 %copy-start.2 = (bf16[2,2,128,128]{3,2,1,0:T(8,128)(2,1)S(1)}, bf16[2,2,128,128]{3,2,1,0:T(8,128)(2,1)}, u32[]{:S(2)}) copy-start(bf16[2,2,128,128]{3,2,1,0:T(8,128)(2,1)} %d_ref.3) | copy-start | bytes 393220
  10.9 0.9 %copy-start.3 = (bf16[128,1,256]{2,0,1:T(8,128)(2,1)S(1)}, bf16[128,1,256]{2,0,1:T(8,128)(2,1)}, u32[]{:S(2)}) copy-start(bf16[128,1,256]{2,0,1:T(8,128)(2,1)} %param.7) | copy-start | bytes 196612
  13.8 3.4 %collective-permute-start.4 = (bf16[2,64,128]{2,1,0:T(8,128)(2,1)S(1)}, bf16[2,64,128]{2,1,0:T(8,128)(2,1)S(1)}, u32[]{:S(2)}, u32[]{:S(2)}) collective-permute-start(bf16[2,64,128]{2,1,0:T(8,128)(2,1)S(1)} %get-tuple-element.65), channel_id=1, source_target_pairs={{1,2},{3,0},{2,1},{0,3},{5,6},{7,4},{6,5},{4,7},{9,10},{11,8},{10,... | collective-permute-start | bytes 98312 | tf_op jit(solution)/shard_map/ppermute | solution.py:392
  15.7 1.6 %collective-permute-start.5 = (bf16[2,64,128]{2,1,0:T(8,128)(2,1)S(1)}, bf16[2,64,128]{2,1,0:T(8,128)(2,1)S(1)}, u32[]{:S(2)}, u32[]{:S(2)}) collective-permute-start(bf16[2,64,128]{2,1,0:T(8,128)(2,1)S(1)} %get-tuple-element.66), channel_id=1, source_target_pairs={{0,1},{2,3},{1,0},{3,2},{4,5},{6,7},{5,4},{7,6},{8,9},{10,11},{9,8... | collective-permute-start | bytes 98312 | tf_op jit(solution)/shard_map/ppermute | solution.py:392
  18.8 1.8 %collective-permute-start.6 = (bf16[704,128]{1,0:T(8,128)(2,1)S(1)}, bf16[704,128]{1,0:T(8,128)(2,1)S(1)}, u32[]{:S(2)}, u32[]{:S(2)}) collective-permute-start(bf16[704,128]{1,0:T(8,128)(2,1)S(1)} %get-tuple-element.79), channel_id=1, source_target_pairs={{0,1},{1,0},{2,3},{3,2},{4,5},{5,4},{6,7},{7,6},{8,9},{9,8},{10,11... | collective-permute-start | bytes 540680 | tf_op jit(solution)/shard_map/ppermute | solution.py:398
  20.6 4.5 %collective-permute-start.7 = (bf16[352,128]{1,0:T(8,128)(2,1)S(1)}, bf16[352,128]{1,0:T(8,128)(2,1)S(1)}, u32[]{:S(2)}, u32[]{:S(2)}) collective-permute-start(bf16[352,128]{1,0:T(8,128)(2,1)S(1)} %get-tuple-element.83), channel_id=1, source_target_pairs={{0,9},{1,8},{2,11},{3,10},{4,13},{5,12},{6,15},{7,14},{8,1},{9,0},... | collective-permute-start | bytes 270344 | tf_op jit(solution)/shard_map/ppermute | solution.py:398
  20.7 12.0 %collective-permute-start.10 = (bf16[8,64,128]{2,1,0:T(8,128)(2,1)S(1)}, bf16[8,64,128]{2,1,0:T(8,128)(2,1)S(1)}, u32[]{:S(2)}, u32[]{:S(2)}) collective-permute-start(bf16[8,64,128]{2,1,0:T(8,128)(2,1)S(1)} %get-tuple-element.86.near), channel_id=1, source_target_pairs={{0,4},{8,12},{16,20},{24,28},{4,0},{12,8},{20,16},{28,24},{1,5},{9... | collective-permute-start | bytes 393224 | tf_op jit(solution)/shard_map/ppermute | solution.py:392
  21.7 11.0 %collective-permute-start.11 = (bf16[8,64,128]{2,1,0:T(8,128)(2,1)S(1)}, bf16[8,64,128]{2,1,0:T(8,128)(2,1)S(1)}, u32[]{:S(2)}, u32[]{:S(2)}) collective-permute-start(bf16[8,64,128]{2,1,0:T(8,128)(2,1)S(1)} %get-tuple-element.87.far), channel_id=1, source_target_pairs={{4,8},{12,16},{20,24},{28,0},{8,4},{16,12},{24,20},{0,28},{5,9},{1... | collective-permute-start | bytes 393224 | tf_op jit(solution)/shard_map/ppermute | solution.py:392
  25.2 3.9 %collective-permute-start.8 = (bf16[176,128]{1,0:T(8,128)(2,1)S(1)}, bf16[176,128]{1,0:T(8,128)(2,1)S(1)}, u32[]{:S(2)}, u32[]{:S(2)}) collective-permute-start(bf16[176,128]{1,0:T(8,128)(2,1)S(1)} %get-tuple-element.85), channel_id=1, source_target_pairs={{0,3},{1,2},{2,1},{3,0},{4,7},{5,6},{6,5},{7,4},{8,11},{9,10},{10,... | collective-permute-start | bytes 135176 | tf_op jit(solution)/shard_map/ppermute | solution.py:398
  29.2 3.5 %collective-permute-start.9 = (bf16[176,128]{1,0:T(8,128)(2,1)S(1)}, bf16[176,128]{1,0:T(8,128)(2,1)S(1)}, u32[]{:S(2)}, u32[]{:S(2)}) collective-permute-start(bf16[176,128]{1,0:T(8,128)(2,1)S(1)} %shard_map.84.x), channel_id=1, source_target_pairs={{0,5},{1,4},{2,7},{3,6},{4,1},{5,0},{6,3},{7,2},{8,13},{9,12},{10,... | collective-permute-start | bytes 135176 | tf_op jit(solution)/shard_map/ppermute | solution.py:398
  32.7 5.5 %collective-permute-start.12 = (bf16[176,128]{1,0:T(8,128)(2,1)S(1)}, bf16[176,128]{1,0:T(8,128)(2,1)S(1)}, u32[]{:S(2)}, u32[]{:S(2)}) collective-permute-start(bf16[176,128]{1,0:T(8,128)(2,1)S(1)} %shard_map.85.x), channel_id=1, source_target_pairs={{0,17},{1,16},{2,19},{3,18},{4,21},{5,20},{6,23},{7,22},{8,25},{9,... | collective-permute-start | bytes 135176 | tf_op jit(solution)/shard_map/ppermute | solution.py:398
  34.5 7.6 %collective-permute-start.14 = (bf16[4,64,128]{2,1,0:T(8,128)(2,1)S(1)}, bf16[4,64,128]{2,1,0:T(8,128)(2,1)S(1)}, u32[]{:S(2)}, u32[]{:S(2)}) collective-permute-start(bf16[4,64,128]{2,1,0:T(8,128)(2,1)S(1)} %get-tuple-element.94), channel_id=1, source_target_pairs={{0,1},{2,3},{1,0},{3,2},{4,5},{6,7},{5,4},{7,6},{8,9},{10,11},{9,8... | collective-permute-start | bytes 196616 | tf_op jit(solution)/shard_map/ppermute | solution.py:392
  35.0 7.1 %collective-permute-start.15 = (bf16[4,64,128]{2,1,0:T(8,128)(2,1)S(1)}, bf16[4,64,128]{2,1,0:T(8,128)(2,1)S(1)}, u32[]{:S(2)}, u32[]{:S(2)}) collective-permute-start(bf16[4,64,128]{2,1,0:T(8,128)(2,1)S(1)} %get-tuple-element.95), channel_id=1, source_target_pairs={{1,2},{3,0},{2,1},{0,3},{5,6},{7,4},{6,5},{4,7},{9,10},{11,8},{10,... | collective-permute-start | bytes 196616 | tf_op jit(solution)/shard_map/ppermute | solution.py:392
  38.2 3.8 %collective-permute-start.13 = (bf16[176,128]{1,0:T(8,128)(2,1)S(1)}, bf16[176,128]{1,0:T(8,128)(2,1)S(1)}, u32[]{:S(2)}, u32[]{:S(2)}) collective-permute-start(bf16[176,128]{1,0:T(8,128)(2,1)S(1)} %shard_map.86.mine), channel_id=1, source_target_pairs={{0,3},{1,2},{2,1},{3,0},{4,7},{5,6},{6,5},{7,4},{8,11},{9,10},{10,... | collective-permute-start | bytes 135176 | tf_op jit(solution)/shard_map/ppermute | solution.py:398
  42.1 4.5 %collective-permute-start.16 = (bf16[352,128]{1,0:T(8,128)(2,1)S(1)}, bf16[352,128]{1,0:T(8,128)(2,1)S(1)}, u32[]{:S(2)}, u32[]{:S(2)}) collective-permute-start(bf16[352,128]{1,0:T(8,128)(2,1)S(1)} %shard_map.88.mine), channel_id=1, source_target_pairs={{0,9},{1,8},{2,11},{3,10},{4,13},{5,12},{6,15},{7,14},{8,1},{9,0},... | collective-permute-start | bytes 270344 | tf_op jit(solution)/shard_map/ppermute | solution.py:398
  46.7 1.5 %collective-permute-start.17 = (bf16[704,128]{1,0:T(8,128)(2,1)S(1)}, bf16[704,128]{1,0:T(8,128)(2,1)S(1)}, u32[]{:S(2)}, u32[]{:S(2)}) collective-permute-start(bf16[704,128]{1,0:T(8,128)(2,1)S(1)} %shard_map.91.mine), channel_id=1, source_target_pairs={{0,1},{1,0},{2,3},{3,2},{4,5},{5,4},{6,7},{7,6},{8,9},{9,8},{10,11... | collective-permute-start | bytes 540680 | tf_op jit(solution)/shard_map/ppermute | solution.py:398

commit v22 on v21

--- a/solution.py
+++ b/solution.py
@@ -91,7 +91,7 @@
     cols[p, q, 2 * channels : 3 * channels] = pltpu.roll(wide, line.shape[1] - 1, 1).astype(BF16)
 
 
-def fill_columns(cols, near, far, near_row=None, far_row=None):
+def fill_columns(cols, near, far):
     rows = near.shape[0]
     even = is_even("gz")
 
@@ -101,19 +101,16 @@
         return carry
 
     lax.fori_loop(0, rows, step, 0, unroll=2)
-    if near_row is not None:
-        fill_rows(cols, near_row, far_row, 0, rows + 1)
-        return
     for p in range(2):
         for q in (0, rows + 1):
             cols[p, q] = jnp.zeros(cols.shape[2:], BF16)
 
 
-def fill_rows(cols, near, far, below, above):
+def fill_rows(cols, near, far):
     even = is_even("gy")
     for p in range(near.shape[0]):
-        put_columns(cols, p, below, choose(even, far[p], near[p]))
-        put_columns(cols, p, above, choose(even, near[p], far[p]))
+        put_columns(cols, p, 0, choose(even, far[p], near[p]))
+        put_columns(cols, p, 1, choose(even, near[p], far[p]))
 
 
 def dot(lhs, rhs):
@@ -154,9 +151,9 @@
     return acc[half:] + dot(w_ref[0, b], edges[0, side]), acc[:half] + dot(w_ref[2, b], edges[3, side])
 
 
-def inner_kernel(near, far, near_row, far_row, w_ref, d_ref, cot_ref, cols, acc_ref, grad_ref, up):
+def inner_kernel(near, far, w_ref, d_ref, cot_ref, cols, acc_ref, grad_ref, up):
     rows, channels, breadth = near.shape
-    fill_columns(cols, near, far, near_row, far_row)
+    fill_columns(cols, near, far)
     source = lax.broadcasted_iota(jnp.int32, (breadth, 2 * breadth), 0)
     target = lax.broadcasted_iota(jnp.int32, (breadth, 2 * breadth), 1)
     spread = jnp.where(source == target // 2, 1.0, 0.0).astype(BF16)
@@ -186,9 +183,16 @@
     return (preact * sig).astype(BF16), (grad * sig * (1.0 + preact * (1.0 - sig))).astype(BF16)
 
 
-def outer_kernel(near, far, w_ref, acc_ref, grad_ref, cols, side_ref, near_ref, far_ref, h_ref):
+def outer_kernel(
+    near, far, near_row, far_row, w_ref, acc_ref, grad_ref, cols, edges, side_ref, near_ref, far_ref, h_ref
+):
     rows, channels, breadth = near.shape
     fill_columns(cols, near, far)
+    fill_rows(edges, near_row, far_row)
+    beside = []
+    for side in range(2):
+        terms = dot(taps(w_ref, 2 * side, 0, 2), edges[0, side]) + dot(taps(w_ref, 2 * side, 1, 3), edges[1, side])
+        beside.append((terms[channels:], terms[:channels]))
     even = is_even("gz")
     for y in range(0, rows, 2):
         outer = outer_terms(cols, w_ref, y)
@@ -197,7 +201,7 @@
             for z in range(2):
                 preact = acc_ref[z, y + b] + outer[z][:, b * breadth : (b + 1) * breadth]
                 if y + b in (0, rows - 1):
-                    side_ref[z, b] = preact
+                    side_ref[z, b] = preact + beside[b][z]
                 else:
                     h_ref[z, y + b], gate = gated(preact, grad_ref[z, y + b])
                     found.append(gate)
@@ -208,7 +212,7 @@
 
 def gate_kernel(near, far, side_ref, near_in, far_in, h_in, grad_ref, w_ref, edges, near_ref, far_ref, h_ref):
     rows = near_in.shape[0]
-    fill_rows(edges, near, far, 0, 1)
+    fill_rows(edges, near, far)
     even = is_even("gz")
     for side, y in enumerate((0, rows - 1)):
         terms = [dot(w_ref[2 * z, 2 * side], edges[z, side]) for z in range(2)]
@@ -250,7 +254,7 @@
     out_ref[...] = dot(down, coarse_hidden(h_ref)).astype(BF16)
 
 
-def weight_grad_kernel(inner, outer, edges, near, far, h_ref, cot_ref, keep, send, packed):
+def weight_grad_kernel(inner, outer, own_edges, edges, near, far, h_ref, cot_ref, keep, send, packed):
     rows, channels, breadth = near.shape
     across = (((1,), (1,)), ((), ()))
     even = is_even("gz")
@@ -267,9 +271,8 @@
     both = jnp.concatenate([low, high], axis=0)
 
     def columns(p, q):
-        if p in (1, 2):
-            return inner[p - 1, q]
-        return edges[p // 3, q // (rows + 1)] if q in (0, rows + 1) else outer[p // 3, q]
+        planes, rows_beside, at = (inner, own_edges, p - 1) if p in (1, 2) else (outer, edges, p // 3)
+        return rows_beside[at, q // (rows + 1)] if q in (0, rows + 1) else planes[at, q]
 
     parts = []
     for p in range(4):
@@ -358,7 +361,7 @@
 
 def field_edges_kernel(near, far, acc_ref, w_ref, out_ref, edges):
     rows, channels, breadth = acc_ref.shape[1:]
-    fill_rows(edges, near, far, 0, 1)
+    fill_rows(edges, near, far)
     sides = [edge_terms(edges, w_ref, side) for side in range(2)]
     for z in range(2):
         for y in range(rows):
@@ -433,19 +436,21 @@
     inner, acc, hidden_grad = call(
         inner_kernel, [cols, (lines, F32), (lines, F32)],
         [((out_channels, row_count // 2 * breadth), BF16)],
-        2 * conv_flops // 3, (*own, *beside, conv_weight, down_weight, cot),
-    )
-    near, far, acc = lax.optimization_barrier((*outside, acc))
-    outside = (near, far)
+        2 * conv_flops // 3, (*own, conv_weight, down_weight, cot),
+    )
+    near, far, near_row, far_row, acc = lax.optimization_barrier((*outside, *beside, acc))
+    outside, own_rows = (near, far), (near_row, far_row)
     beside = swapped(*call(outer_rows_kernel, [pair, pair], [], 0, outside), "gy")
     far, near = lax.optimization_barrier((beside[1], beside[0]))
     beside = (near, far)
-    outer, *inside = call(
-        outer_kernel, [cols, ((plane_count, 2, channels, breadth), F32), plane, plane, (lines, BF16)], [],
-        conv_flops // 3, (*outside, conv_weight, acc, hidden_grad),
+    rows_cols = ((plane_count, 2, 3 * channels, breadth), BF16)
+    outer, own_edges, *inside = call(
+        outer_kernel,
+        [cols, rows_cols, ((plane_count, 2, channels, breadth), F32), plane, plane, (lines, BF16)], [],
+        conv_flops // 3, (*outside, *own_rows, conv_weight, acc, hidden_grad),
     )
     edges, near, far, hidden = call(
-        gate_kernel, [((plane_count, 2, 3 * channels, breadth), BF16), plane, plane, (lines, BF16)], [], conv_flops // 10,
+        gate_kernel, [rows_cols, plane, plane, (lines, BF16)], [], conv_flops // 10,
         (*beside, *inside, hidden_grad, conv_weight),
     )
     gates = (near, far)
@@ -454,7 +459,7 @@
     rows = -(-used // 128) * 128
     keep, send = call(
         weight_grad_kernel, [((rows // 2, 128), F32), ((rows // 2, 128), BF16)], [((rows, 128), F32)],
-        conv_flops, (inner, outer, edges, *gates, hidden, cot),
+        conv_flops, (inner, outer, own_edges, edges, *gates, hidden, cot),
     )
     keep, gates = tied(keep, *gates)
     near, far = gates

time: 49.3 us -> 49.3 us (level)
  starting transfers between devices: 19.5 us -> 15.7 us
  waiting for transfers between devices: 15.3 us -> 18.2 us
  local copies, waits for them, and re-layouts: 2.82 us -> 3.57 us
    ppermute x8, waiting for transfers between devices: 14 us -> 16.5 us  [flip(): lax.ppermute(cells, ('gz', 'gy'), [(i, i ^ mask) for i in range(lax.axis_...]
    ppermute x8, starting transfers between devices: 4.86 us -> 2.48 us  [flip(): lax.ppermute(cells, ('gz', 'gy'), [(i, i ^ mask) for i in range(lax.axis_...]
    ppermute x10, starting transfers between devices: 14.6 us -> 13.2 us  [swap(): return lax.ppermute(cells, axis, pairs + [(b, a) for a, b in pairs])]
    unnamed x8, local copies, waits for them, and re-layouts: 2.04 us -> 2.79 us
where the time goes in v22:
time: 49.3 us; the launch traced here: 49.1 us
  waiting for transfers between devices  18.2 us (37%)
  starting transfers between devices  15.7 us (32%)
  Pallas kernels  10.8 us (22%)
  local copies, waits for them, and re-layouts  3.57 us (7%)
  between operations  0.83 us (2%)
    ppermute x8, waiting for transfers between devices, flip(): lax.ppermute(cells, ('gz', 'gy'), [(i, i ^ mask) for i in range(lax.axis_...  16.5 us
    ppermute x10, starting transfers between devices, swap(): return lax.ppermute(cells, axis, pairs + [(b, a) for a, b in pairs])  13.2 us
    pallas_call x19, Pallas kernels, call(): pl.pallas_call(kernel, out_shape=[jax.ShapeDtypeStruct(s, d) for s, d in...  10.8 us
    unnamed x8, local copies, waits for them, and re-layouts  2.79 us
    ppermute x8, starting transfers between devices, flip(): lax.ppermute(cells, ('gz', 'gy'), [(i, i ^ mask) for i in range(lax.axis_...  2.48 us
    ppermute x10, waiting for transfers between devices, swap(): return lax.ppermute(cells, axis, pairs + [(b, a) for a, b in pairs])  1.73 us
  transfers between devices with their start and end apart: 18, of which 9 were waited for; matrix products, arithmetic and copies ran while one was open for 2% of the time, Pallas kernels for 16%

profile of v22, /device:TPU:0, one launch (start us, length us, event | category | flops | bytes accessed | tf_op | source)
XLA Modules:
  0.0 49.1 jit_solution(13567984400491164082)
XLA Ops:
  0.6 0.9 %copy-done.1 = bf16[64,2,8,128]{3,2,1,0:T(8,128)(2,1)S(1)} copy-done((bf16[64,2,8,128]{3,2,1,0:T(8,128)(2,1)S(1)}, bf16[64,2,8,128]{3,2,1,0:T(8,128)(2,1)}, u32[]{:S(2)}) %copy-start.1) | copy-done | bytes 262168
  1.6 0.2 shard_map.75
  1.8 3.0 %collective-permute-start = (bf16[8,64,128]{2,1,0:T(8,128)(2,1)S(1)}, bf16[8,64,128]{2,1,0:T(8,128)(2,1)S(1)}, u32[]{:S(2)}, u32[]{:S(2)}) collective-permute-start(bf16[8,64,128]{2,1,0:T(8,128)(2,1)S(1)} %get-tuple-element.57.near), channel_id=1, source_target_pairs={{0,4},{8,12},{16,20},{24,28},{4,0},{12,8},{20,16},{28,24},{1,5},{9... | collective-permute-start | bytes 393224 | tf_op jit(solution)/shard_map/ppermute | solution.py:395
  4.8 3.5 %collective-permute-start.1 = (bf16[8,64,128]{2,1,0:T(8,128)(2,1)S(1)}, bf16[8,64,128]{2,1,0:T(8,128)(2,1)S(1)}, u32[]{:S(2)}, u32[]{:S(2)}) collective-permute-start(bf16[8,64,128]{2,1,0:T(8,128)(2,1)S(1)} %get-tuple-element.58.far), channel_id=1, source_target_pairs={{4,8},{12,16},{20,24},{28,0},{8,4},{16,12},{24,20},{0,28},{5,9},{1... | collective-permute-start | bytes 393224 | tf_op jit(solution)/shard_map/ppermute | solution.py:395
  8.4 0.0 collective-permute-start.2
  8.4 1.6 %collective-permute-start.3 = (bf16[2,64,128]{2,1,0:T(8,128)(2,1)S(1)}, bf16[2,64,128]{2,1,0:T(8,128)(2,1)S(1)}, u32[]{:S(2)}, u32[]{:S(2)}) collective-permute-start(bf16[2,64,128]{2,1,0:T(8,128)(2,1)S(1)} %get-tuple-element.61), channel_id=1, source_target_pairs={{1,2},{3,0},{2,1},{0,3},{5,6},{7,4},{6,5},{4,7},{9,10},{11,8},{10,... | collective-permute-start | bytes 98312 | tf_op jit(solution)/shard_map/ppermute | solution.py:395
  10.0 1.0 %copy-done = bf16[3,3,64,192]{3,2,1,0:T(8,128)(2,1)S(1)} copy-done((bf16[3,3,64,192]{3,2,1,0:T(8,128)(2,1)S(1)}, bf16[3,3,64,192]{3,2,1,0:T(8,128)(2,1)}, u32[]{:S(2)}) %copy-start) | copy-done | bytes 221208
  11.0 0.9 %copy-done.2 = bf16[2,2,128,128]{3,2,1,0:T(8,128)(2,1)S(1)} copy-done((bf16[2,2,128,128]{3,2,1,0:T(8,128)(2,1)S(1)}, bf16[2,2,128,128]{3,2,1,0:T(8,128)(2,1)}, u32[]{:S(2)}) %copy-start.2) | copy-done | bytes 131096
  11.8 1.9 %shard_map.77 = (bf16[2,10,192,128]{3,2,1,0:T(8,128)(2,1)S(1)}, f32[2,8,64,128]{3,2,1,0:T(8,128)S(1)}, f32[2,8,64,128]{3,2,1,0:T(8,128)S(1)}) custom-call(bf16[8,64,128]{2,1,0:T(8,128)(2,1)S(1)} %get-tuple-element.57.near, bf16[8,64,128]{2,1,0:T(8,128)(2,1)S(1)} %get-tuple-element.58.far, bf16[3,3,64,192]{3,2,1,0:T(8,128)(2,1)S(1)} %shard_map.76.w_ref, ...), custom_call_target="tpu_custom_call" | custom-call | flops 301989888 | bytes 2711552 | tf_op jit(solution)/shard_map/pallas_call | solution.py:20
  13.8 0.0 collective-permute-done.2.near_row
  13.8 0.0 collective-permute-done.near.near_in
  13.8 0.0 collective-permute-done.1.far.far_in
  13.8 0.2 collective-permute-start.4
  14.0 0.5 %collective-permute-start.5 = (bf16[2,64,128]{2,1,0:T(8,128)(2,1)S(1)}, bf16[2,64,128]{2,1,0:T(8,128)(2,1)S(1)}, u32[]{:S(2)}, u32[]{:S(2)}) collective-permute-start(bf16[2,64,128]{2,1,0:T(8,128)(2,1)S(1)} %get-tuple-element.72), channel_id=1, source_target_pairs={{0,1},{2,3},{1,0},{3,2},{4,5},{6,7},{5,4},{7,6},{8,9},{10,11},{9,8... | collective-permute-start | bytes 98312 | tf_op jit(solution)/shard_map/ppermute | solution.py:395
  14.6 1.2 %shard_map.78 = (bf16[2,10,192,128]{3,2,1,0:T(8,128)(2,1)S(1)}, bf16[2,2,192,128]{3,2,1,0:T(8,128)(2,1)S(1)}, f32[2,2,64,128]{3,2,1,0:T(8,128)S(1)}, bf16[8,64,1...) custom-call(bf16[8,64,128]{2,1,0:T(8,128)(2,1)S(1)} %collective-permute-done.near.near_in,, ...), custom_call_target="tpu_custom_call" | custom-call | flops 150994944 | bytes 3432448 | tf_op jit(solution)/shard_map/pallas_call | solution.py:20
  15.7 1.7 %collective-permute-done.4.far = bf16[2,64,128]{2,1,0:T(8,128)(2,1)S(1)} collective-permute-done((bf16[2,64,128]{2,1,0:T(8,128)(2,1)S(1)}, bf16[2,64,128]{2,1,0:T(8,128)(2,1)S(1)}, u32[]{:S(2)}, u32[]{:S(2)}) %collective-permute-start.4) | collective-permute-done | bytes 32800 | tf_op jit(solution)/shard_map/ppermute | solution.py:395
  17.4 0.3 shard_map.80
  17.8 1.2 %shard_map.81 = (f32[704,128]{1,0:T(8,128)S(1)}, bf16[704,128]{1,0:T(8,128)(2,1)S(1)}) custom-call(bf16[2,10,192,128]{3,2,1,0:T(8,128)(2,1)S(1)} %get-tuple-element.59.inner, bf16[2,10,192,128]{3,2,1,0:T(8,128)(2,1)S(1)} %get-tuple-element.69.outer, bf16[2,2,192,128]{3,2,1,0:T(8,128)(2,1)S(1)} %get-tuple-element.70.own_edges, ...), custom_call_target="tpu_custom_call" | custom-call | flops 452984832 | bytes 3489792 | tf_op jit(solution)/shard_map/pallas_call | solution.py:20
  19.0 0.2 collective-permute-start.6
  19.2 1.3 %collective-permute-done.6.other = bf16[704,128]{1,0:T(8,128)(2,1)S(1)} collective-permute-done((bf16[704,128]{1,0:T(8,128)(2,1)S(1)}, bf16[704,128]{1,0:T(8,128)(2,1)S(1)}, u32[]{:S(2)}, u32[]{:S(2)}) %collective-permute-start.6) | collective-permute-done | bytes 180256 | tf_op jit(solution)/shard_map/ppermute | solution.py:401
  20.5 0.1 shard_map.82
  20.5 0.1 collective-permute-start.7
  20.6 0.8 %collective-permute-start.10 = (bf16[8,64,128]{2,1,0:T(8,128)(2,1)S(1)}, bf16[8,64,128]{2,1,0:T(8,128)(2,1)S(1)}, u32[]{:S(2)}, u32[]{:S(2)}) collective-permute-start(bf16[8,64,128]{2,1,0:T(8,128)(2,1)S(1)} %get-tuple-element.92.near), channel_id=1, source_target_pairs={{0,4},{8,12},{16,20},{24,28},{4,0},{12,8},{20,16},{28,24},{1,5},{9... | collective-permute-start | bytes 393224 | tf_op jit(solution)/shard_map/ppermute | solution.py:395
  21.4 2.1 %collective-permute-start.11 = (bf16[8,64,128]{2,1,0:T(8,128)(2,1)S(1)}, bf16[8,64,128]{2,1,0:T(8,128)(2,1)S(1)}, u32[]{:S(2)}, u32[]{:S(2)}) collective-permute-start(bf16[8,64,128]{2,1,0:T(8,128)(2,1)S(1)} %get-tuple-element.93.far), channel_id=1, source_target_pairs={{4,8},{12,16},{20,24},{28,0},{8,4},{16,12},{24,20},{0,28},{5,9},{1... | collective-permute-start | bytes 393224 | tf_op jit(solution)/shard_map/ppermute | solution.py:395
  23.5 1.6 %collective-permute-done.7.other = bf16[352,128]{1,0:T(8,128)(2,1)S(1)} collective-permute-done((bf16[352,128]{1,0:T(8,128)(2,1)S(1)}, bf16[352,128]{1,0:T(8,128)(2,1)S(1)}, u32[]{:S(2)}, u32[]{:S(2)}) %collective-permute-start.7) | collective-permute-done | bytes 90144 | tf_op jit(solution)/shard_map/ppermute | solution.py:401
  25.2 1.0 %collective-permute-start.8 = (bf16[176,128]{1,0:T(8,128)(2,1)S(1)}, bf16[176,128]{1,0:T(8,128)(2,1)S(1)}, u32[]{:S(2)}, u32[]{:S(2)}) collective-permute-start(bf16[176,128]{1,0:T(8,128)(2,1)S(1)} %get-tuple-element.91), channel_id=1, source_target_pairs={{0,3},{1,2},{2,1},{3,0},{4,7},{5,6},{6,5},{7,4},{8,11},{9,10},{10,... | collective-permute-start | bytes 135176 | tf_op jit(solution)/shard_map/ppermute | solution.py:401
  26.2 2.6 %collective-permute-done.8.y = bf16[176,128]{1,0:T(8,128)(2,1)S(1)} collective-permute-done((bf16[176,128]{1,0:T(8,128)(2,1)S(1)}, bf16[176,128]{1,0:T(8,128)(2,1)S(1)}, u32[]{:S(2)}, u32[]{:S(2)}) %collective-permute-start.8) | collective-permute-done | bytes 45088 | tf_op jit(solution)/shard_map/ppermute | solution.py:401
  28.8 0.1 collective-permute-start.9
  28.9 3.5 %collective-permute-done.9.y = bf16[176,128]{1,0:T(8,128)(2,1)S(1)} collective-permute-done((bf16[176,128]{1,0:T(8,128)(2,1)S(1)}, bf16[176,128]{1,0:T(8,128)(2,1)S(1)}, u32[]{:S(2)}, u32[]{:S(2)}) %collective-permute-start.9) | collective-permute-done | bytes 45088 | tf_op jit(solution)/shard_map/ppermute | solution.py:401
  32.3 0.0 collective-permute-done.11.far_in
  32.3 0.7 %collective-permute-start.12 = (bf16[176,128]{1,0:T(8,128)(2,1)S(1)}, bf16[176,128]{1,0:T(8,128)(2,1)S(1)}, u32[]{:S(2)}, u32[]{:S(2)}) collective-permute-start(bf16[176,128]{1,0:T(8,128)(2,1)S(1)} %shard_map.85.x), channel_id=1, source_target_pairs={{0,17},{1,16},{2,19},{3,18},{4,21},{5,20},{6,23},{7,22},{8,25},{9,... | collective-permute-start | bytes 135176 | tf_op jit(solution)/shard_map/ppermute | solution.py:401
  33.0 0.3 copy.9
  33.3 1.1 %shard_map.87 = bf16[128,256]{1,0:T(8,128)(2,1)} custom-call(bf16[2,8,64,128]{3,2,1,0:T(8,128)(2,1)S(1)} %get-tuple-element.95.h_ref, bf16[2,2,128,128]{3,2,1,0:T(8,128)(2,1)S(1)} %copy-done.2), custom_call_target="tpu_custom_call" | custom-call | flops 45298484 | bytes 458752 | tf_op jit(solution)/shard_map/pallas_call | solution.py:20
  34.4 0.4 collective-permute-start.14
  34.8 1.0 %collective-permute-start.15 = (bf16[4,64,128]{2,1,0:T(8,128)(2,1)S(1)}, bf16[4,64,128]{2,1,0:T(8,128)(2,1)S(1)}, u32[]{:S(2)}, u32[]{:S(2)}) collective-permute-start(bf16[4,64,128]{2,1,0:T(8,128)(2,1)S(1)} %get-tuple-element.101), channel_id=1, source_target_pairs={{1,2},{3,0},{2,1},{0,3},{5,6},{7,4},{6,5},{4,7},{9,10},{11,8},{10,... | collective-permute-start | bytes 196616 | tf_op jit(solution)/shard_map/ppermute | solution.py:395
  35.8 2.3 %collective-permute-done.12.y = bf16[176,128]{1,0:T(8,128)(2,1)S(1)} collective-permute-done((bf16[176,128]{1,0:T(8,128)(2,1)S(1)}, bf16[176,128]{1,0:T(8,128)(2,1)S(1)}, u32[]{:S(2)}, u32[]{:S(2)}) %collective-permute-start.12) | collective-permute-done | bytes 45088 | tf_op jit(solution)/shard_map/ppermute | solution.py:401
  38.1 0.3 collective-permute-start.13
  38.4 0.3 copy.10
  38.6 0.2 copy.11.w_ref
  38.9 2.3 %shard_map.89.acc_ref = f32[2,8,64,128]{3,2,1,0:T(8,128)S(1)} custom-call(bf16[8,64,128]{2,1,0:T(8,128)(2,1)S(1)} %get-tuple-element.92.near, bf16[8,64,128]{2,1,0:T(8,128)(2,1)S(1)} %get-tuple-element.93.far, bf16[8,64,128]{2,1,0:T(8,128)(2,1)S(1)} %collective-permute-done.10.near_in, bf16[8,64,128]{2,1,0:T(8,128)(2,1)S(1)} %collective-permute-done.11.far_in, ...), custom_call_target="tpu_custom_call" | custom-call | flops 452984832 | bytes 1269760 | tf_op jit(solution)/shard_map/pallas_call | solution.py:20
  41.2 0.6 %collective-permute-done.13.other = bf16[176,128]{1,0:T(8,128)(2,1)S(1)} collective-permute-done((bf16[176,128]{1,0:T(8,128)(2,1)S(1)}, bf16[176,128]{1,0:T(8,128)(2,1)S(1)}, u32[]{:S(2)}, u32[]{:S(2)}) %collective-permute-start.13) | collective-permute-done | bytes 45088 | tf_op jit(solution)/shard_map/ppermute | solution.py:401
  41.8 0.0 collective-permute-done.15.far
  41.8 0.1 collective-permute-start.16
  41.9 1.3 %shard_map.92 = f32[1024,128]{1,0:T(8,128)} custom-call(bf16[4,64,128]{2,1,0:T(8,128)(2,1)S(1)} %collective-permute-done.14.near, bf16[4,64,128]{2,1,0:T(8,128)(2,1)S(1)} %collective-permute-done.15.far, f32[2,8,64,128]{3,2,1,0:T(8,128)S(1)} %shard_map.89.acc_ref, bf16[3,3,64,192]{3,2,1,0:T(8,128)(2,1)S(1)} %copy.11.w_ref), custom_call_target="tpu_custom_call" | custom-call | flops 45298484 | bytes 1400832 | tf_op jit(solution)/shard_map/pallas_call | solution.py:20
  43.3 3.3 %collective-permute-done.16.other = bf16[352,128]{1,0:T(8,128)(2,1)S(1)} collective-permute-done((bf16[352,128]{1,0:T(8,128)(2,1)S(1)}, bf16[352,128]{1,0:T(8,128)(2,1)S(1)}, u32[]{:S(2)}, u32[]{:S(2)}) %collective-permute-start.16) | collective-permute-done | bytes 90144 | tf_op jit(solution)/shard_map/ppermute | solution.py:401
  46.6 0.2 collective-permute-start.17
  46.8 1.3 %collective-permute-done.17.other = bf16[704,128]{1,0:T(8,128)(2,1)S(1)} collective-permute-done((bf16[704,128]{1,0:T(8,128)(2,1)S(1)}, bf16[704,128]{1,0:T(8,128)(2,1)S(1)}, u32[]{:S(2)}, u32[]{:S(2)}) %collective-permute-start.17) | collective-permute-done | bytes 180256 | tf_op jit(solution)/shard_map/ppermute | solution.py:401
  48.1 1.0 %shard_map.93 = (f32[3,3,64,192]{3,2,1,0:T(8,128)}, f32[2,2,128,128]{3,2,1,0:T(8,128)}) custom-call(bf16[704,128]{1,0:T(8,128)(2,1)S(1)} %shard_map.91.mine, bf16[704,128]{1,0:T(8,128)(2,1)S(1)} %collective-permute-done.17.other), custom_call_target="tpu_custom_call" | custom-call | bytes 1064960 | tf_op jit(solution)/shard_map/pallas_call | solution.py:20
  (19 shorter events, 0.2 us)
Async XLA Ops:
  0.6 1.0 %copy-start.1 = (bf16[64,2,8,128]{3,2,1,0:T(8,128)(2,1)S(1)}, bf16[64,2,8,128]{3,2,1,0:T(8,128)(2,1)}, u32[]{:S(2)}) copy-start(bf16[64,2,8,128]{3,2,1,0:T(8,128)(2,1)} %f_ref.1) | copy-start | bytes 786436
  1.8 12.0 %collective-permute-start = (bf16[8,64,128]{2,1,0:T(8,128)(2,1)S(1)}, bf16[8,64,128]{2,1,0:T(8,128)(2,1)S(1)}, u32[]{:S(2)}, u32[]{:S(2)}) collective-permute-start(bf16[8,64,128]{2,1,0:T(8,128)(2,1)S(1)} %get-tuple-element.57.near), channel_id=1, source_target_pairs={{0,4},{8,12},{16,20},{24,28},{4,0},{12,8},{20,16},{28,24},{1,5},{9... | collective-permute-start | bytes 393224 | tf_op jit(solution)/shard_map/ppermute | solution.py:395
  4.8 9.0 %collective-permute-start.1 = (bf16[8,64,128]{2,1,0:T(8,128)(2,1)S(1)}, bf16[8,64,128]{2,1,0:T(8,128)(2,1)S(1)}, u32[]{:S(2)}, u32[]{:S(2)}) collective-permute-start(bf16[8,64,128]{2,1,0:T(8,128)(2,1)S(1)} %get-tuple-element.58.far), channel_id=1, source_target_pairs={{4,8},{12,16},{20,24},{28,0},{8,4},{16,12},{24,20},{0,28},{5,9},{1... | collective-permute-start | bytes 393224 | tf_op jit(solution)/shard_map/ppermute | solution.py:395
  8.4 5.4 %collective-permute-start.2 = (bf16[2,64,128]{2,1,0:T(8,128)(2,1)S(1)}, bf16[2,64,128]{2,1,0:T(8,128)(2,1)S(1)}, u32[]{:S(2)}, u32[]{:S(2)}) collective-permute-start(bf16[2,64,128]{2,1,0:T(8,128)(2,1)S(1)} %get-tuple-element.60), channel_id=1, source_target_pairs={{0,1},{2,3},{1,0},{3,2},{4,5},{6,7},{5,4},{7,6},{8,9},{10,11},{9,8... | collective-permute-start | bytes 98312 | tf_op jit(solution)/shard_map/ppermute | solution.py:395
  8.4 5.4 %collective-permute-start.3 = (bf16[2,64,128]{2,1,0:T(8,128)(2,1)S(1)}, bf16[2,64,128]{2,1,0:T(8,128)(2,1)S(1)}, u32[]{:S(2)}, u32[]{:S(2)}) collective-permute-start(bf16[2,64,128]{2,1,0:T(8,128)(2,1)S(1)} %get-tuple-element.61), channel_id=1, source_target_pairs={{1,2},{3,0},{2,1},{0,3},{5,6},{7,4},{6,5},{4,7},{9,10},{11,8},{10,... | collective-permute-start | bytes 98312 | tf_op jit(solution)/shard_map/ppermute | solution.py:395
  10.0 1.0 %copy-start = (bf16[3,3,64,192]{3,2,1,0:T(8,128)(2,1)S(1)}, bf16[3,3,64,192]{3,2,1,0:T(8,128)(2,1)}, u32[]{:S(2)}) copy-start(bf16[3,3,64,192]{3,2,1,0:T(8,128)(2,1)} %x.1) | copy-start | bytes 663556
  10.9 0.9 %copy-start.2 = (bf16[2,2,128,128]{3,2,1,0:T(8,128)(2,1)S(1)}, bf16[2,2,128,128]{3,2,1,0:T(8,128)(2,1)}, u32[]{:S(2)}) copy-start(bf16[2,2,128,128]{3,2,1,0:T(8,128)(2,1)} %d_ref.3) | copy-start | bytes 393220
  10.9 0.9 %copy-start.3 = (bf16[128,1,256]{2,0,1:T(8,128)(2,1)S(1)}, bf16[128,1,256]{2,0,1:T(8,128)(2,1)}, u32[]{:S(2)}) copy-start(bf16[128,1,256]{2,0,1:T(8,128)(2,1)} %param.7) | copy-start | bytes 196612
  13.8 3.6 %collective-permute-start.4 = (bf16[2,64,128]{2,1,0:T(8,128)(2,1)S(1)}, bf16[2,64,128]{2,1,0:T(8,128)(2,1)S(1)}, u32[]{:S(2)}, u32[]{:S(2)}) collective-permute-start(bf16[2,64,128]{2,1,0:T(8,128)(2,1)S(1)} %get-tuple-element.71), channel_id=1, source_target_pairs={{1,2},{3,0},{2,1},{0,3},{5,6},{7,4},{6,5},{4,7},{9,10},{11,8},{10,... | collective-permute-start | bytes 98312 | tf_op jit(solution)/shard_map/ppermute | solution.py:395
  14.0 3.4 %collective-permute-start.5 = (bf16[2,64,128]{2,1,0:T(8,128)(2,1)S(1)}, bf16[2,64,128]{2,1,0:T(8,128)(2,1)S(1)}, u32[]{:S(2)}, u32[]{:S(2)}) collective-permute-start(bf16[2,64,128]{2,1,0:T(8,128)(2,1)S(1)} %get-tuple-element.72), channel_id=1, source_target_pairs={{0,1},{2,3},{1,0},{3,2},{4,5},{6,7},{5,4},{7,6},{8,9},{10,11},{9,8... | collective-permute-start | bytes 98312 | tf_op jit(solution)/shard_map/ppermute | solution.py:395
  19.0 1.5 %collective-permute-start.6 = (bf16[704,128]{1,0:T(8,128)(2,1)S(1)}, bf16[704,128]{1,0:T(8,128)(2,1)S(1)}, u32[]{:S(2)}, u32[]{:S(2)}) collective-permute-start(bf16[704,128]{1,0:T(8,128)(2,1)S(1)} %get-tuple-element.85), channel_id=1, source_target_pairs={{0,1},{1,0},{2,3},{3,2},{4,5},{5,4},{6,7},{7,6},{8,9},{9,8},{10,11... | collective-permute-start | bytes 540680 | tf_op jit(solution)/shard_map/ppermute | solution.py:401
  20.5 4.7 %collective-permute-start.7 = (bf16[352,128]{1,0:T(8,128)(2,1)S(1)}, bf16[352,128]{1,0:T(8,128)(2,1)S(1)}, u32[]{:S(2)}, u32[]{:S(2)}) collective-permute-start(bf16[352,128]{1,0:T(8,128)(2,1)S(1)} %get-tuple-element.89), channel_id=1, source_target_pairs={{0,9},{1,8},{2,11},{3,10},{4,13},{5,12},{6,15},{7,14},{8,1},{9,0},... | collective-permute-start | bytes 270344 | tf_op jit(solution)/shard_map/ppermute | solution.py:401
  20.6 11.7 %collective-permute-start.10 = (bf16[8,64,128]{2,1,0:T(8,128)(2,1)S(1)}, bf16[8,64,128]{2,1,0:T(8,128)(2,1)S(1)}, u32[]{:S(2)}, u32[]{:S(2)}) collective-permute-start(bf16[8,64,128]{2,1,0:T(8,128)(2,1)S(1)} %get-tuple-element.92.near), channel_id=1, source_target_pairs={{0,4},{8,12},{16,20},{24,28},{4,0},{12,8},{20,16},{28,24},{1,5},{9... | collective-permute-start | bytes 393224 | tf_op jit(solution)/shard_map/ppermute | solution.py:395
  21.4 10.9 %collective-permute-start.11 = (bf16[8,64,128]{2,1,0:T(8,128)(2,1)S(1)}, bf16[8,64,128]{2,1,0:T(8,128)(2,1)S(1)}, u32[]{:S(2)}, u32[]{:S(2)}) collective-permute-start(bf16[8,64,128]{2,1,0:T(8,128)(2,1)S(1)} %get-tuple-element.93.far), channel_id=1, source_target_pairs={{4,8},{12,16},{20,24},{28,0},{8,4},{16,12},{24,20},{0,28},{5,9},{1... | collective-permute-start | bytes 393224 | tf_op jit(solution)/shard_map/ppermute | solution.py:395
  25.2 3.5 %collective-permute-start.8 = (bf16[176,128]{1,0:T(8,128)(2,1)S(1)}, bf16[176,128]{1,0:T(8,128)(2,1)S(1)}, u32[]{:S(2)}, u32[]{:S(2)}) collective-permute-start(bf16[176,128]{1,0:T(8,128)(2,1)S(1)} %get-tuple-element.91), channel_id=1, source_target_pairs={{0,3},{1,2},{2,1},{3,0},{4,7},{5,6},{6,5},{7,4},{8,11},{9,10},{10,... | collective-permute-start | bytes 135176 | tf_op jit(solution)/shard_map/ppermute | solution.py:401
  28.8 3.5 %collective-permute-start.9 = (bf16[176,128]{1,0:T(8,128)(2,1)S(1)}, bf16[176,128]{1,0:T(8,128)(2,1)S(1)}, u32[]{:S(2)}, u32[]{:S(2)}) collective-permute-start(bf16[176,128]{1,0:T(8,128)(2,1)S(1)} %shard_map.84.x), channel_id=1, source_target_pairs={{0,5},{1,4},{2,7},{3,6},{4,1},{5,0},{6,3},{7,2},{8,13},{9,12},{10,... | collective-permute-start | bytes 135176 | tf_op jit(solution)/shard_map/ppermute | solution.py:401
  32.3 5.7 %collective-permute-start.12 = (bf16[176,128]{1,0:T(8,128)(2,1)S(1)}, bf16[176,128]{1,0:T(8,128)(2,1)S(1)}, u32[]{:S(2)}, u32[]{:S(2)}) collective-permute-start(bf16[176,128]{1,0:T(8,128)(2,1)S(1)} %shard_map.85.x), channel_id=1, source_target_pairs={{0,17},{1,16},{2,19},{3,18},{4,21},{5,20},{6,23},{7,22},{8,25},{9,... | collective-permute-start | bytes 135176 | tf_op jit(solution)/shard_map/ppermute | solution.py:401
  34.4 7.4 %collective-permute-start.14 = (bf16[4,64,128]{2,1,0:T(8,128)(2,1)S(1)}, bf16[4,64,128]{2,1,0:T(8,128)(2,1)S(1)}, u32[]{:S(2)}, u32[]{:S(2)}) collective-permute-start(bf16[4,64,128]{2,1,0:T(8,128)(2,1)S(1)} %get-tuple-element.100), channel_id=1, source_target_pairs={{0,1},{2,3},{1,0},{3,2},{4,5},{6,7},{5,4},{7,6},{8,9},{10,11},{9,8... | collective-permute-start | bytes 196616 | tf_op jit(solution)/shard_map/ppermute | solution.py:395
  34.8 7.0 %collective-permute-start.15 = (bf16[4,64,128]{2,1,0:T(8,128)(2,1)S(1)}, bf16[4,64,128]{2,1,0:T(8,128)(2,1)S(1)}, u32[]{:S(2)}, u32[]{:S(2)}) collective-permute-start(bf16[4,64,128]{2,1,0:T(8,128)(2,1)S(1)} %get-tuple-element.101), channel_id=1, source_target_pairs={{1,2},{3,0},{2,1},{0,3},{5,6},{7,4},{6,5},{4,7},{9,10},{11,8},{10,... | collective-permute-start | bytes 196616 | tf_op jit(solution)/shard_map/ppermute | solution.py:395
  38.1 3.7 %collective-permute-start.13 = (bf16[176,128]{1,0:T(8,128)(2,1)S(1)}, bf16[176,128]{1,0:T(8,128)(2,1)S(1)}, u32[]{:S(2)}, u32[]{:S(2)}) collective-permute-start(bf16[176,128]{1,0:T(8,128)(2,1)S(1)} %shard_map.86.mine), channel_id=1, source_target_pairs={{0,3},{1,2},{2,1},{3,0},{4,7},{5,6},{6,5},{7,4},{8,11},{9,10},{10,... | collective-permute-start | bytes 135176 | tf_op jit(solution)/shard_map/ppermute | solution.py:401
  41.8 4.7 %collective-permute-start.16 = (bf16[352,128]{1,0:T(8,128)(2,1)S(1)}, bf16[352,128]{1,0:T(8,128)(2,1)S(1)}, u32[]{:S(2)}, u32[]{:S(2)}) collective-permute-start(bf16[352,128]{1,0:T(8,128)(2,1)S(1)} %shard_map.88.mine), channel_id=1, source_target_pairs={{0,9},{1,8},{2,11},{3,10},{4,13},{5,12},{6,15},{7,14},{8,1},{9,0},... | collective-permute-start | bytes 270344 | tf_op jit(solution)/shard_map/ppermute | solution.py:401
  46.6 1.5 %collective-permute-start.17 = (bf16[704,128]{1,0:T(8,128)(2,1)S(1)}, bf16[704,128]{1,0:T(8,128)(2,1)S(1)}, u32[]{:S(2)}, u32[]{:S(2)}) collective-permute-start(bf16[704,128]{1,0:T(8,128)(2,1)S(1)} %shard_map.91.mine), channel_id=1, source_target_pairs={{0,1},{1,0},{2,3},{3,2},{4,5},{5,4},{6,7},{7,6},{8,9},{9,8},{10,11... | collective-permute-start | bytes 540680 | tf_op jit(solution)/shard_map/ppermute | solution.py:401

commit v23 on v22

--- a/solution.py
+++ b/solution.py
@@ -53,8 +53,26 @@
         far_row[z] = choose(even_y, ends[0][z], ends[rows - 1][z])
 
 
-def copy_kernel(x, out):
-    out[...] = x[...]
+def fetch_kernel(*refs):
+    *both, sems = refs
+    count = len(both) // 2
+    copies = [pltpu.make_async_copy(both[k], both[count + k], sems.at[k]) for k in range(count)]
+    for copy in copies:
+        copy.start()
+    for copy in copies:
+        copy.wait()
+
+
+def fetch(*operands):
+    return pl.pallas_call(
+        fetch_kernel,
+        out_shape=[jax.ShapeDtypeStruct(x.shape, x.dtype) for x in operands],
+        in_specs=[pl.BlockSpec(memory_space=pltpu.HBM)] * len(operands),
+        out_specs=[pl.BlockSpec(memory_space=pltpu.VMEM)] * len(operands),
+        scratch_shapes=[pltpu.SemaphoreType.DMA((len(operands),))],
+        compiler_params=PARAMS,
+        cost_estimate=pl.CostEstimate(flops=0, bytes_accessed=2 * sum(x.size * 2 for x in operands), transcendentals=0),
+    )(*operands)
 
 
 def outer_rows_kernel(near_in, far_in, near_ref, far_ref):
@@ -415,10 +433,10 @@
     out_channels = down_weight.shape[2]
     count = lax.axis_size("gz") * lax.axis_size("gy")
     grad_scale = 1.0 / math.sqrt(plane_count * row_count * breadth * count)
-    (conv_weight,) = call(copy_kernel, [(conv_weight.shape, BF16)], [], 0, (conv_weight,))
+    cot = cotangent.reshape(out_channels, -1)
+    conv_weight, down_weight, cot = fetch(conv_weight, down_weight, cot)
     turned = conv_weight.reshape(3, 3, channels, 3, channels)[::-1, ::-1, :, ::-1]
     weight_bwd = turned.transpose(0, 1, 4, 3, 2).reshape(3, 3, channels, 3 * channels)
-    cot = cotangent.reshape(out_channels, -1)
     plane = ((row_count, channels, breadth), BF16)
     edge = ((plane_count + 2, channels, breadth), BF16)
     cols = ((plane_count, row_count + 2, 3 * channels, breadth), BF16)

time: 49.3 us -> 48.6 us (0.986)
  waiting for transfers between devices: 18.2 us -> 16.4 us
  starting transfers between devices: 15.7 us -> 17.4 us
  local copies, waits for them, and re-layouts: 3.57 us -> 2.69 us
    ppermute x8, waiting for transfers between devices: 16.5 us -> 14.9 us  [flip(): lax.ppermute(cells, ('gz', 'gy'), [(i, i ^ mask) for i in range(lax.axis_...]
    ppermute x8, starting transfers between devices: 2.48 us -> 3.43 us  [flip(): lax.ppermute(cells, ('gz', 'gy'), [(i, i ^ mask) for i in range(lax.axis_...]
    unnamed x8, local copies, waits for them, and re-layouts: 2.79 us -> 1.91 us
    ppermute x10, starting transfers between devices: 13.2 us -> 13.9 us  [swap(): return lax.ppermute(cells, axis, pairs + [(b, a) for a, b in pairs])]
    pallas_call x19 -> x18, Pallas kernels: 10.8 us -> 10.8 us  [call(): pl.pallas_call(kernel, out_shape=[jax.ShapeDtypeStruct(s, d) for s, d in...]
  transfers between devices with their start and end apart: 18 -> 18, of which waited for: 9 -> 9; matrix products, arithmetic and copies ran while one was open for 2% -> 2% of each run, Pallas kernels for 16% -> 17%
where the time goes in v23:
time: 48.6 us; the launch traced here: 48.4 us
  starting transfers between devices  17.4 us (36%)
  waiting for transfers between devices  16.4 us (34%)
  Pallas kernels  11.1 us (23%)
  local copies, waits for them, and re-layouts  2.69 us (6%)
  between operations  0.84 us (2%)
    ppermute x8, waiting for transfers between devices, flip(): lax.ppermute(cells, ('gz', 'gy'), [(i, i ^ mask) for i in range(lax.axis_...  14.9 us
    ppermute x10, starting transfers between devices, swap(): return lax.ppermute(cells, axis, pairs + [(b, a) for a, b in pairs])  13.9 us
    pallas_call x18, Pallas kernels, call(): pl.pallas_call(kernel, out_shape=[jax.ShapeDtypeStruct(s, d) for s, d in...  10.8 us
    ppermute x8, starting transfers between devices, flip(): lax.ppermute(cells, ('gz', 'gy'), [(i, i ^ mask) for i in range(lax.axis_...  3.43 us
    unnamed x8, local copies, waits for them, and re-layouts  1.91 us
    ppermute x10, waiting for transfers between devices, swap(): return lax.ppermute(cells, axis, pairs + [(b, a) for a, b in pairs])  1.54 us
  transfers between devices with their start and end apart: 18, of which 9 were waited for; matrix products, arithmetic and copies ran while one was open for 2% of the time, Pallas kernels for 17%

profile of v23, /device:TPU:0, one launch (start us, length us, event | category | flops | bytes accessed | tf_op | source)
XLA Modules:
  0.0 48.4 jit_solution(7783618933057623618)
XLA Ops:
  0.6 0.9 %copy-done.1 = bf16[64,2,8,128]{3,2,1,0:T(8,128)(2,1)S(1)} copy-done((bf16[64,2,8,128]{3,2,1,0:T(8,128)(2,1)S(1)}, bf16[64,2,8,128]{3,2,1,0:T(8,128)(2,1)}, u32[]{:S(2)}) %copy-start.1) | copy-done | bytes 262168
  1.6 0.2 shard_map.75
  1.8 3.0 %collective-permute-start = (bf16[8,64,128]{2,1,0:T(8,128)(2,1)S(1)}, bf16[8,64,128]{2,1,0:T(8,128)(2,1)S(1)}, u32[]{:S(2)}, u32[]{:S(2)}) collective-permute-start(bf16[8,64,128]{2,1,0:T(8,128)(2,1)S(1)} %get-tuple-element.60.near), channel_id=1, source_target_pairs={{0,4},{8,12},{16,20},{24,28},{4,0},{12,8},{20,16},{28,24},{1,5},{9... | collective-permute-start | bytes 393224 | tf_op jit(solution)/shard_map/ppermute | solution.py:413
  4.8 3.5 %collective-permute-start.1 = (bf16[8,64,128]{2,1,0:T(8,128)(2,1)S(1)}, bf16[8,64,128]{2,1,0:T(8,128)(2,1)S(1)}, u32[]{:S(2)}, u32[]{:S(2)}) collective-permute-start(bf16[8,64,128]{2,1,0:T(8,128)(2,1)S(1)} %get-tuple-element.61.far), channel_id=1, source_target_pairs={{4,8},{12,16},{20,24},{28,0},{8,4},{16,12},{24,20},{0,28},{5,9},{1... | collective-permute-start | bytes 393224 | tf_op jit(solution)/shard_map/ppermute | solution.py:413
  8.4 0.0 collective-permute-start.2
  8.4 1.6 %collective-permute-start.3 = (bf16[2,64,128]{2,1,0:T(8,128)(2,1)S(1)}, bf16[2,64,128]{2,1,0:T(8,128)(2,1)S(1)}, u32[]{:S(2)}, u32[]{:S(2)}) collective-permute-start(bf16[2,64,128]{2,1,0:T(8,128)(2,1)S(1)} %get-tuple-element.67), channel_id=1, source_target_pairs={{1,2},{3,0},{2,1},{0,3},{5,6},{7,4},{6,5},{4,7},{9,10},{11,8},{10,... | collective-permute-start | bytes 98312 | tf_op jit(solution)/shard_map/ppermute | solution.py:413
  10.0 1.0 %copy-done = bf16[3,3,64,192]{3,2,1,0:T(8,128)(2,1)S(1)} copy-done((bf16[3,3,64,192]{3,2,1,0:T(8,128)(2,1)S(1)}, bf16[3,3,64,192]{3,2,1,0:T(8,128)(2,1)}, u32[]{:S(2)}) %copy-start) | copy-done | bytes 221208
  11.0 0.3 shard_map.76
  11.3 1.9 %shard_map.77 = (bf16[2,10,192,128]{3,2,1,0:T(8,128)(2,1)S(1)}, f32[2,8,64,128]{3,2,1,0:T(8,128)S(1)}, f32[2,8,64,128]{3,2,1,0:T(8,128)S(1)}) custom-call(bf16[8,64,128]{2,1,0:T(8,128)(2,1)S(1)} %get-tuple-element.60.near, bf16[8,64,128]{2,1,0:T(8,128)(2,1)S(1)} %get-tuple-element.61.far, bf16[3,3,64,192]{3,2,1,0:T(8,128)(2,1)S(1)} %get-tuple-element.62.w_ref, ...), custom_call_target="tpu_custom_call" | custom-call | flops 301989888 | bytes 2711552 | tf_op jit(solution)/shard_map/pallas_call | solution.py:20
  13.2 0.0 collective-permute-done.3.far_row
  13.2 0.0 collective-permute-done.near.near_in
  13.3 0.4 collective-permute-start.4
  13.7 0.5 collective-permute-start.5
  14.2 1.2 %shard_map.78 = (bf16[2,10,192,128]{3,2,1,0:T(8,128)(2,1)S(1)}, bf16[2,2,192,128]{3,2,1,0:T(8,128)(2,1)S(1)}, f32[2,2,64,128]{3,2,1,0:T(8,128)S(1)}, bf16[8,64,1...) custom-call(bf16[8,64,128]{2,1,0:T(8,128)(2,1)S(1)} %collective-permute-done.near.near_in,, ...), custom_call_target="tpu_custom_call" | custom-call | flops 150994944 | bytes 3432448 | tf_op jit(solution)/shard_map/pallas_call | solution.py:20
  15.4 1.5 %collective-permute-done.4.far = bf16[2,64,128]{2,1,0:T(8,128)(2,1)S(1)} collective-permute-done((bf16[2,64,128]{2,1,0:T(8,128)(2,1)S(1)}, bf16[2,64,128]{2,1,0:T(8,128)(2,1)S(1)}, u32[]{:S(2)}, u32[]{:S(2)}) %collective-permute-start.4) | collective-permute-done | bytes 32800 | tf_op jit(solution)/shard_map/ppermute | solution.py:413
  16.9 0.3 shard_map.80
  17.2 1.2 %shard_map.81 = (f32[704,128]{1,0:T(8,128)S(1)}, bf16[704,128]{1,0:T(8,128)(2,1)S(1)}) custom-call(bf16[2,10,192,128]{3,2,1,0:T(8,128)(2,1)S(1)} %get-tuple-element.65.inner, bf16[2,10,192,128]{3,2,1,0:T(8,128)(2,1)S(1)} %get-tuple-element.75.outer, bf16[2,2,192,128]{3,2,1,0:T(8,128)(2,1)S(1)} %get-tuple-element.76.own_edges, ...), custom_call_target="tpu_custom_call" | custom-call | flops 452984832 | bytes 3489792 | tf_op jit(solution)/shard_map/pallas_call | solution.py:20
  18.4 0.2 collective-permute-start.6
  18.6 1.3 %collective-permute-done.6.other = bf16[704,128]{1,0:T(8,128)(2,1)S(1)} collective-permute-done((bf16[704,128]{1,0:T(8,128)(2,1)S(1)}, bf16[704,128]{1,0:T(8,128)(2,1)S(1)}, u32[]{:S(2)}, u32[]{:S(2)}) %collective-permute-start.6) | collective-permute-done | bytes 180256 | tf_op jit(solution)/shard_map/ppermute | solution.py:419
  19.9 0.1 shard_map.82
  20.0 0.1 collective-permute-start.7
  20.1 1.0 %collective-permute-start.10 = (bf16[8,64,128]{2,1,0:T(8,128)(2,1)S(1)}, bf16[8,64,128]{2,1,0:T(8,128)(2,1)S(1)}, u32[]{:S(2)}, u32[]{:S(2)}) collective-permute-start(bf16[8,64,128]{2,1,0:T(8,128)(2,1)S(1)} %get-tuple-element.98.near), channel_id=1, source_target_pairs={{0,4},{8,12},{16,20},{24,28},{4,0},{12,8},{20,16},{28,24},{1,5},{9... | collective-permute-start | bytes 393224 | tf_op jit(solution)/shard_map/ppermute | solution.py:413
  21.1 2.4 %collective-permute-start.11 = (bf16[8,64,128]{2,1,0:T(8,128)(2,1)S(1)}, bf16[8,64,128]{2,1,0:T(8,128)(2,1)S(1)}, u32[]{:S(2)}, u32[]{:S(2)}) collective-permute-start(bf16[8,64,128]{2,1,0:T(8,128)(2,1)S(1)} %get-tuple-element.99.far), channel_id=1, source_target_pairs={{4,8},{12,16},{20,24},{28,0},{8,4},{16,12},{24,20},{0,28},{5,9},{1... | collective-permute-start | bytes 393224 | tf_op jit(solution)/shard_map/ppermute | solution.py:413
  23.5 1.1 %collective-permute-done.7.other = bf16[352,128]{1,0:T(8,128)(2,1)S(1)} collective-permute-done((bf16[352,128]{1,0:T(8,128)(2,1)S(1)}, bf16[352,128]{1,0:T(8,128)(2,1)S(1)}, u32[]{:S(2)}, u32[]{:S(2)}) %collective-permute-start.7) | collective-permute-done | bytes 90144 | tf_op jit(solution)/shard_map/ppermute | solution.py:419
  24.7 1.1 %collective-permute-start.8 = (bf16[176,128]{1,0:T(8,128)(2,1)S(1)}, bf16[176,128]{1,0:T(8,128)(2,1)S(1)}, u32[]{:S(2)}, u32[]{:S(2)}) collective-permute-start(bf16[176,128]{1,0:T(8,128)(2,1)S(1)} %get-tuple-element.97), channel_id=1, source_target_pairs={{0,3},{1,2},{2,1},{3,0},{4,7},{5,6},{6,5},{7,4},{8,11},{9,10},{10,... | collective-permute-start | bytes 135176 | tf_op jit(solution)/shard_map/ppermute | solution.py:419
  25.8 2.4 %collective-permute-done.8.y = bf16[176,128]{1,0:T(8,128)(2,1)S(1)} collective-permute-done((bf16[176,128]{1,0:T(8,128)(2,1)S(1)}, bf16[176,128]{1,0:T(8,128)(2,1)S(1)}, u32[]{:S(2)}, u32[]{:S(2)}) %collective-permute-start.8) | collective-permute-done | bytes 45088 | tf_op jit(solution)/shard_map/ppermute | solution.py:419
  28.2 0.1 collective-permute-start.9
  28.4 3.4 %collective-permute-done.9.y = bf16[176,128]{1,0:T(8,128)(2,1)S(1)} collective-permute-done((bf16[176,128]{1,0:T(8,128)(2,1)S(1)}, bf16[176,128]{1,0:T(8,128)(2,1)S(1)}, u32[]{:S(2)}, u32[]{:S(2)}) %collective-permute-start.9) | collective-permute-done | bytes 45088 | tf_op jit(solution)/shard_map/ppermute | solution.py:419
  31.8 0.0 collective-permute-done.11.far_in
  31.8 1.2 %collective-permute-start.12 = (bf16[176,128]{1,0:T(8,128)(2,1)S(1)}, bf16[176,128]{1,0:T(8,128)(2,1)S(1)}, u32[]{:S(2)}, u32[]{:S(2)}) collective-permute-start(bf16[176,128]{1,0:T(8,128)(2,1)S(1)} %shard_map.85.x), channel_id=1, source_target_pairs={{0,17},{1,16},{2,19},{3,18},{4,21},{5,20},{6,23},{7,22},{8,25},{9,... | collective-permute-start | bytes 135176 | tf_op jit(solution)/shard_map/ppermute | solution.py:419
  33.0 0.3 copy.9
  33.3 1.1 %shard_map.87 = bf16[128,256]{1,0:T(8,128)(2,1)} custom-call(bf16[2,8,64,128]{3,2,1,0:T(8,128)(2,1)S(1)} %get-tuple-element.101.h_ref, bf16[2,2,128,128]{3,2,1,0:T(8,128)(2,1)S(1)} %get-tuple-element.63.d_ref), custom_call_target="tpu_custom_call" | custom-call | flops 45298484 | bytes 458752 | tf_op jit(solution)/shard_map/pallas_call | solution.py:20
  34.4 0.1 collective-permute-start.14
  34.5 1.3 %collective-permute-start.15 = (bf16[4,64,128]{2,1,0:T(8,128)(2,1)S(1)}, bf16[4,64,128]{2,1,0:T(8,128)(2,1)S(1)}, u32[]{:S(2)}, u32[]{:S(2)}) collective-permute-start(bf16[4,64,128]{2,1,0:T(8,128)(2,1)S(1)} %get-tuple-element.107), channel_id=1, source_target_pairs={{1,2},{3,0},{2,1},{0,3},{5,6},{7,4},{6,5},{4,7},{9,10},{11,8},{10,... | collective-permute-start | bytes 196616 | tf_op jit(solution)/shard_map/ppermute | solution.py:413
  35.8 1.6 %collective-permute-done.12.y = bf16[176,128]{1,0:T(8,128)(2,1)S(1)} collective-permute-done((bf16[176,128]{1,0:T(8,128)(2,1)S(1)}, bf16[176,128]{1,0:T(8,128)(2,1)S(1)}, u32[]{:S(2)}, u32[]{:S(2)}) %collective-permute-start.12) | collective-permute-done | bytes 45088 | tf_op jit(solution)/shard_map/ppermute | solution.py:419
  37.4 0.5 collective-permute-start.13
  37.9 0.3 copy.10
  38.2 0.2 copy.11.w_ref
  38.4 2.3 %shard_map.89.acc_ref = f32[2,8,64,128]{3,2,1,0:T(8,128)S(1)} custom-call(bf16[8,64,128]{2,1,0:T(8,128)(2,1)S(1)} %get-tuple-element.98.near, bf16[8,64,128]{2,1,0:T(8,128)(2,1)S(1)} %get-tuple-element.99.far, bf16[8,64,128]{2,1,0:T(8,128)(2,1)S(1)} %collective-permute-done.10.near_in, bf16[8,64,128]{2,1,0:T(8,128)(2,1)S(1)} %collective-permute-done.11.far_in, ...), custom_call_target="tpu_custom_call" | custom-call | flops 452984832 | bytes 1269760 | tf_op jit(solution)/shard_map/pallas_call | solution.py:20
  40.7 0.4 collective-permute-done.13.other
  41.2 0.0 collective-permute-done.14.near
  41.2 0.0 collective-permute-done.15.far
  41.2 0.1 collective-permute-start.16
  41.3 1.3 %shard_map.92 = f32[1024,128]{1,0:T(8,128)} custom-call(bf16[4,64,128]{2,1,0:T(8,128)(2,1)S(1)} %collective-permute-done.14.near, bf16[4,64,128]{2,1,0:T(8,128)(2,1)S(1)} %collective-permute-done.15.far, f32[2,8,64,128]{3,2,1,0:T(8,128)S(1)} %shard_map.89.acc_ref, bf16[3,3,64,192]{3,2,1,0:T(8,128)(2,1)S(1)} %copy.11.w_ref), custom_call_target="tpu_custom_call" | custom-call | flops 45298484 | bytes 1400832 | tf_op jit(solution)/shard_map/pallas_call | solution.py:20
  42.6 3.3 %collective-permute-done.16.other = bf16[352,128]{1,0:T(8,128)(2,1)S(1)} collective-permute-done((bf16[352,128]{1,0:T(8,128)(2,1)S(1)}, bf16[352,128]{1,0:T(8,128)(2,1)S(1)}, u32[]{:S(2)}, u32[]{:S(2)}) %collective-permute-start.16) | collective-permute-done | bytes 90144 | tf_op jit(solution)/shard_map/ppermute | solution.py:419
  45.9 0.2 collective-permute-start.17
  46.1 1.3 %collective-permute-done.17.other = bf16[704,128]{1,0:T(8,128)(2,1)S(1)} collective-permute-done((bf16[704,128]{1,0:T(8,128)(2,1)S(1)}, bf16[704,128]{1,0:T(8,128)(2,1)S(1)}, u32[]{:S(2)}, u32[]{:S(2)}) %collective-permute-start.17) | collective-permute-done | bytes 180256 | tf_op jit(solution)/shard_map/ppermute | solution.py:419
  47.4 1.0 %shard_map.93 = (f32[3,3,64,192]{3,2,1,0:T(8,128)}, f32[2,2,128,128]{3,2,1,0:T(8,128)}) custom-call(bf16[704,128]{1,0:T(8,128)(2,1)S(1)} %shard_map.91.mine, bf16[704,128]{1,0:T(8,128)(2,1)S(1)} %collective-permute-done.17.other), custom_call_target="tpu_custom_call" | custom-call | bytes 1064960 | tf_op jit(solution)/shard_map/pallas_call | solution.py:20
  (19 shorter events, 0.2 us)
Async XLA Ops:
  0.6 1.0 %copy-start.1 = (bf16[64,2,8,128]{3,2,1,0:T(8,128)(2,1)S(1)}, bf16[64,2,8,128]{3,2,1,0:T(8,128)(2,1)}, u32[]{:S(2)}) copy-start(bf16[64,2,8,128]{3,2,1,0:T(8,128)(2,1)} %f_ref.1) | copy-start | bytes 786436
  1.6 8.4 %copy-start.2 = (bf16[2,2,128,128]{3,2,1,0:T(8,128)(2,1)S(1)}, bf16[2,2,128,128]{3,2,1,0:T(8,128)(2,1)}, u32[]{:S(2)}) copy-start(bf16[2,2,128,128]{3,2,1,0:T(8,128)(2,1)} %refs_1_.1) | copy-start | bytes 393220
  1.6 8.4 %copy-start.3 = (bf16[128,1,256]{2,0,1:T(8,128)(2,1)S(1)}, bf16[128,1,256]{2,0,1:T(8,128)(2,1)}, u32[]{:S(2)}) copy-start(bf16[128,1,256]{2,0,1:T(8,128)(2,1)} %param.7) | copy-start | bytes 196612
  1.8 11.4 %collective-permute-start = (bf16[8,64,128]{2,1,0:T(8,128)(2,1)S(1)}, bf16[8,64,128]{2,1,0:T(8,128)(2,1)S(1)}, u32[]{:S(2)}, u32[]{:S(2)}) collective-permute-start(bf16[8,64,128]{2,1,0:T(8,128)(2,1)S(1)} %get-tuple-element.60.near), channel_id=1, source_target_pairs={{0,4},{8,12},{16,20},{24,28},{4,0},{12,8},{20,16},{28,24},{1,5},{9... | collective-permute-start | bytes 393224 | tf_op jit(solution)/shard_map/ppermute | solution.py:413
  4.8 8.4 %collective-permute-start.1 = (bf16[8,64,128]{2,1,0:T(8,128)(2,1)S(1)}, bf16[8,64,128]{2,1,0:T(8,128)(2,1)S(1)}, u32[]{:S(2)}, u32[]{:S(2)}) collective-permute-start(bf16[8,64,128]{2,1,0:T(8,128)(2,1)S(1)} %get-tuple-element.61.far), channel_id=1, source_target_pairs={{4,8},{12,16},{20,24},{28,0},{8,4},{16,12},{24,20},{0,28},{5,9},{1... | collective-permute-start | bytes 393224 | tf_op jit(solution)/shard_map/ppermute | solution.py:413
  8.4 4.8 %collective-permute-start.2 = (bf16[2,64,128]{2,1,0:T(8,128)(2,1)S(1)}, bf16[2,64,128]{2,1,0:T(8,128)(2,1)S(1)}, u32[]{:S(2)}, u32[]{:S(2)}) collective-permute-start(bf16[2,64,128]{2,1,0:T(8,128)(2,1)S(1)} %get-tuple-element.66), channel_id=1, source_target_pairs={{0,1},{2,3},{1,0},{3,2},{4,5},{6,7},{5,4},{7,6},{8,9},{10,11},{9,8... | collective-permute-start | bytes 98312 | tf_op jit(solution)/shard_map/ppermute | solution.py:413
  8.4 4.9 %collective-permute-start.3 = (bf16[2,64,128]{2,1,0:T(8,128)(2,1)S(1)}, bf16[2,64,128]{2,1,0:T(8,128)(2,1)S(1)}, u32[]{:S(2)}, u32[]{:S(2)}) collective-permute-start(bf16[2,64,128]{2,1,0:T(8,128)(2,1)S(1)} %get-tuple-element.67), channel_id=1, source_target_pairs={{1,2},{3,0},{2,1},{0,3},{5,6},{7,4},{6,5},{4,7},{9,10},{11,8},{10,... | collective-permute-start | bytes 98312 | tf_op jit(solution)/shard_map/ppermute | solution.py:413
  10.0 1.0 %copy-start = (bf16[3,3,64,192]{3,2,1,0:T(8,128)(2,1)S(1)}, bf16[3,3,64,192]{3,2,1,0:T(8,128)(2,1)}, u32[]{:S(2)}) copy-start(bf16[3,3,64,192]{3,2,1,0:T(8,128)(2,1)} %refs_0_.1) | copy-start | bytes 663556
  13.3 3.6 %collective-permute-start.4 = (bf16[2,64,128]{2,1,0:T(8,128)(2,1)S(1)}, bf16[2,64,128]{2,1,0:T(8,128)(2,1)S(1)}, u32[]{:S(2)}, u32[]{:S(2)}) collective-permute-start(bf16[2,64,128]{2,1,0:T(8,128)(2,1)S(1)} %get-tuple-element.77), channel_id=1, source_target_pairs={{1,2},{3,0},{2,1},{0,3},{5,6},{7,4},{6,5},{4,7},{9,10},{11,8},{10,... | collective-permute-start | bytes 98312 | tf_op jit(solution)/shard_map/ppermute | solution.py:413
  13.7 3.1 %collective-permute-start.5 = (bf16[2,64,128]{2,1,0:T(8,128)(2,1)S(1)}, bf16[2,64,128]{2,1,0:T(8,128)(2,1)S(1)}, u32[]{:S(2)}, u32[]{:S(2)}) collective-permute-start(bf16[2,64,128]{2,1,0:T(8,128)(2,1)S(1)} %get-tuple-element.78), channel_id=1, source_target_pairs={{0,1},{2,3},{1,0},{3,2},{4,5},{6,7},{5,4},{7,6},{8,9},{10,11},{9,8... | collective-permute-start | bytes 98312 | tf_op jit(solution)/shard_map/ppermute | solution.py:413
  18.4 1.5 %collective-permute-start.6 = (bf16[704,128]{1,0:T(8,128)(2,1)S(1)}, bf16[704,128]{1,0:T(8,128)(2,1)S(1)}, u32[]{:S(2)}, u32[]{:S(2)}) collective-permute-start(bf16[704,128]{1,0:T(8,128)(2,1)S(1)} %get-tuple-element.91), channel_id=1, source_target_pairs={{0,1},{1,0},{2,3},{3,2},{4,5},{5,4},{6,7},{7,6},{8,9},{9,8},{10,11... | collective-permute-start | bytes 540680 | tf_op jit(solution)/shard_map/ppermute | solution.py:419
  20.0 4.7 %collective-permute-start.7 = (bf16[352,128]{1,0:T(8,128)(2,1)S(1)}, bf16[352,128]{1,0:T(8,128)(2,1)S(1)}, u32[]{:S(2)}, u32[]{:S(2)}) collective-permute-start(bf16[352,128]{1,0:T(8,128)(2,1)S(1)} %get-tuple-element.95), channel_id=1, source_target_pairs={{0,9},{1,8},{2,11},{3,10},{4,13},{5,12},{6,15},{7,14},{8,1},{9,0},... | collective-permute-start | bytes 270344 | tf_op jit(solution)/shard_map/ppermute | solution.py:419
  20.1 11.7 %collective-permute-start.10 = (bf16[8,64,128]{2,1,0:T(8,128)(2,1)S(1)}, bf16[8,64,128]{2,1,0:T(8,128)(2,1)S(1)}, u32[]{:S(2)}, u32[]{:S(2)}) collective-permute-start(bf16[8,64,128]{2,1,0:T(8,128)(2,1)S(1)} %get-tuple-element.98.near), channel_id=1, source_target_pairs={{0,4},{8,12},{16,20},{24,28},{4,0},{12,8},{20,16},{28,24},{1,5},{9... | collective-permute-start | bytes 393224 | tf_op jit(solution)/shard_map/ppermute | solution.py:413
  21.1 10.7 %collective-permute-start.11 = (bf16[8,64,128]{2,1,0:T(8,128)(2,1)S(1)}, bf16[8,64,128]{2,1,0:T(8,128)(2,1)S(1)}, u32[]{:S(2)}, u32[]{:S(2)}) collective-permute-start(bf16[8,64,128]{2,1,0:T(8,128)(2,1)S(1)} %get-tuple-element.99.far), channel_id=1, source_target_pairs={{4,8},{12,16},{20,24},{28,0},{8,4},{16,12},{24,20},{0,28},{5,9},{1... | collective-permute-start | bytes 393224 | tf_op jit(solution)/shard_map/ppermute | solution.py:413
  24.7 3.5 %collective-permute-start.8 = (bf16[176,128]{1,0:T(8,128)(2,1)S(1)}, bf16[176,128]{1,0:T(8,128)(2,1)S(1)}, u32[]{:S(2)}, u32[]{:S(2)}) collective-permute-start(bf16[176,128]{1,0:T(8,128)(2,1)S(1)} %get-tuple-element.97), channel_id=1, source_target_pairs={{0,3},{1,2},{2,1},{3,0},{4,7},{5,6},{6,5},{7,4},{8,11},{9,10},{10,... | collective-permute-start | bytes 135176 | tf_op jit(solution)/shard_map/ppermute | solution.py:419
  28.2 3.5 %collective-permute-start.9 = (bf16[176,128]{1,0:T(8,128)(2,1)S(1)}, bf16[176,128]{1,0:T(8,128)(2,1)S(1)}, u32[]{:S(2)}, u32[]{:S(2)}) collective-permute-start(bf16[176,128]{1,0:T(8,128)(2,1)S(1)} %shard_map.84.x), channel_id=1, source_target_pairs={{0,5},{1,4},{2,7},{3,6},{4,1},{5,0},{6,3},{7,2},{8,13},{9,12},{10,... | collective-permute-start | bytes 135176 | tf_op jit(solution)/shard_map/ppermute | solution.py:419
  31.8 5.6 %collective-permute-start.12 = (bf16[176,128]{1,0:T(8,128)(2,1)S(1)}, bf16[176,128]{1,0:T(8,128)(2,1)S(1)}, u32[]{:S(2)}, u32[]{:S(2)}) collective-permute-start(bf16[176,128]{1,0:T(8,128)(2,1)S(1)} %shard_map.85.x), channel_id=1, source_target_pairs={{0,17},{1,16},{2,19},{3,18},{4,21},{5,20},{6,23},{7,22},{8,25},{9,... | collective-permute-start | bytes 135176 | tf_op jit(solution)/shard_map/ppermute | solution.py:419
  34.4 6.8 %collective-permute-start.14 = (bf16[4,64,128]{2,1,0:T(8,128)(2,1)S(1)}, bf16[4,64,128]{2,1,0:T(8,128)(2,1)S(1)}, u32[]{:S(2)}, u32[]{:S(2)}) collective-permute-start(bf16[4,64,128]{2,1,0:T(8,128)(2,1)S(1)} %get-tuple-element.106), channel_id=1, source_target_pairs={{0,1},{2,3},{1,0},{3,2},{4,5},{6,7},{5,4},{7,6},{8,9},{10,11},{9,8... | collective-permute-start | bytes 196616 | tf_op jit(solution)/shard_map/ppermute | solution.py:413
  34.5 6.7 %collective-permute-start.15 = (bf16[4,64,128]{2,1,0:T(8,128)(2,1)S(1)}, bf16[4,64,128]{2,1,0:T(8,128)(2,1)S(1)}, u32[]{:S(2)}, u32[]{:S(2)}) collective-permute-start(bf16[4,64,128]{2,1,0:T(8,128)(2,1)S(1)} %get-tuple-element.107), channel_id=1, source_target_pairs={{1,2},{3,0},{2,1},{0,3},{5,6},{7,4},{6,5},{4,7},{9,10},{11,8},{10,... | collective-permute-start | bytes 196616 | tf_op jit(solution)/shard_map/ppermute | solution.py:413
  37.4 3.7 %collective-permute-start.13 = (bf16[176,128]{1,0:T(8,128)(2,1)S(1)}, bf16[176,128]{1,0:T(8,128)(2,1)S(1)}, u32[]{:S(2)}, u32[]{:S(2)}) collective-permute-start(bf16[176,128]{1,0:T(8,128)(2,1)S(1)} %shard_map.86.mine), channel_id=1, source_target_pairs={{0,3},{1,2},{2,1},{3,0},{4,7},{5,6},{6,5},{7,4},{8,11},{9,10},{10,... | collective-permute-start | bytes 135176 | tf_op jit(solution)/shard_map/ppermute | solution.py:419
  41.2 4.7 %collective-permute-start.16 = (bf16[352,128]{1,0:T(8,128)(2,1)S(1)}, bf16[352,128]{1,0:T(8,128)(2,1)S(1)}, u32[]{:S(2)}, u32[]{:S(2)}) collective-permute-start(bf16[352,128]{1,0:T(8,128)(2,1)S(1)} %shard_map.88.mine), channel_id=1, source_target_pairs={{0,9},{1,8},{2,11},{3,10},{4,13},{5,12},{6,15},{7,14},{8,1},{9,0},... | collective-permute-start | bytes 270344 | tf_op jit(solution)/shard_map/ppermute | solution.py:419
  45.9 1.5 %collective-permute-start.17 = (bf16[704,128]{1,0:T(8,128)(2,1)S(1)}, bf16[704,128]{1,0:T(8,128)(2,1)S(1)}, u32[]{:S(2)}, u32[]{:S(2)}) collective-permute-start(bf16[704,128]{1,0:T(8,128)(2,1)S(1)} %shard_map.91.mine), channel_id=1, source_target_pairs={{0,1},{1,0},{2,3},{3,2},{4,5},{5,4},{6,7},{7,6},{8,9},{9,8},{10,11... | collective-permute-start | bytes 540680 | tf_op jit(solution)/shard_map/ppermute | solution.py:419

commit v24 on v23

--- a/solution.py
+++ b/solution.py
@@ -143,14 +143,29 @@
     return jnp.concatenate([cols[p, q], cols[p, q + 1]], axis=1)
 
 
-def inner_terms(cols, w_ref, y):
-    acc = None
-    for b in range(3):
-        for p in range(2):
-            term = dot(taps(w_ref, b, p, p + 2), window(cols, p, y + b))
-            acc = term if acc is None else acc + term
-    half = acc.shape[0] // 2
-    return acc[half:], acc[:half]
+def add_terms(acc, w_ref, inner, outer=None):
+    channels, breadth = acc.shape[2:]
+    acc[...] = jnp.zeros(acc.shape, F32)
+    stacks = [jnp.concatenate([taps(w_ref, b, p, p + 2) for b in range(3)], axis=0) for p in range(2)]
+    if outer is not None:
+        low, high = (jnp.concatenate([w_ref[a, b] for b in range(3)], axis=0) for a in (0, 2))
+
+    def step(t, carry):
+        q = 2 * t
+        own = dot(stacks[0], window(inner, 0, q)) + dot(stacks[1], window(inner, 1, q))
+        if outer is not None:
+            rest = [dot(low, window(outer, 0, q)), dot(high, window(outer, 1, q))]
+        for b in range(3):
+            for z in range(2):
+                at = (2 * b + 1 - z) * channels
+                block = own[at : at + channels]
+                if outer is not None:
+                    block = block + rest[z][b * channels : (b + 1) * channels]
+                for row in range(2):
+                    acc[z, q + row - b + 2] += block[:, row * breadth : (row + 1) * breadth]
+        return carry
+
+    lax.fori_loop(0, inner.shape[1] // 2, step, 0)
 
 
 def outer_terms(cols, w_ref, y):
@@ -185,15 +200,7 @@
             for t in range(rows // 2):
                 part = terms[:, t * breadth : (t + 1) * breadth]
                 grad_ref[a, 2 * t + b] = jnp.where(even, part[0:channels], part[channels:])
-
-    def step(t, carry):
-        y = 2 * t
-        for z, lines in enumerate(inner_terms(cols, w_ref, y)):
-            for b in range(2):
-                acc_ref[z, y + b] = lines[:, b * breadth : (b + 1) * breadth]
-        return carry
-
-    lax.fori_loop(0, rows // 2, step, 0)
+    add_terms(acc_ref, w_ref, cols)
 
 
 def gated(preact, grad):
@@ -217,7 +224,7 @@
         for b in range(2):
             found = []
             for z in range(2):
-                preact = acc_ref[z, y + b] + outer[z][:, b * breadth : (b + 1) * breadth]
+                preact = acc_ref[z, y + b + 2] + outer[z][:, b * breadth : (b + 1) * breadth]
                 if y + b in (0, rows - 1):
                     side_ref[z, b] = preact + beside[b][z]
                 else:
@@ -360,30 +367,19 @@
 
 
 def field_kernel(near, far, near_in, far_in, w_ref, acc_ref, inner, outer):
-    rows, channels, breadth = near.shape
     fill_columns(inner, near, far)
     fill_columns(outer, near_in, far_in)
-
-    def step(t, carry):
-        y = 2 * t
-        own = inner_terms(inner, w_ref, y)
-        rest = outer_terms(outer, w_ref, y)
-        for z in range(2):
-            total = own[z] + rest[z]
-            for b in range(2):
-                acc_ref[z, y + b] = total[:, b * breadth : (b + 1) * breadth]
-        return carry
-
-    lax.fori_loop(0, rows // 2, step, 0)
+    add_terms(acc_ref, w_ref, inner, outer)
 
 
 def field_edges_kernel(near, far, acc_ref, w_ref, out_ref, edges):
-    rows, channels, breadth = acc_ref.shape[1:]
+    channels = acc_ref.shape[2]
+    rows = acc_ref.shape[1] - 4
     fill_rows(edges, near, far)
     sides = [edge_terms(edges, w_ref, side) for side in range(2)]
     for z in range(2):
         for y in range(rows):
-            line = acc_ref[z, y]
+            line = acc_ref[z, y + 2]
             if y in (0, rows - 1):
                 line = line + sides[0 if y == 0 else 1][z]
             out_ref[pl.ds(z * rows + y, channels, stride=2 * rows), :] = line
@@ -442,6 +438,7 @@
     cols = ((plane_count, row_count + 2, 3 * channels, breadth), BF16)
     edge_cols = ((plane_count + 2, 2, 3 * channels, breadth), BF16)
     lines = (plane_count, row_count, channels, breadth)
+    sums_of = (plane_count, row_count + 4, channels, breadth)
     conv_flops = 2 * 27 * channels * channels * plane_count * row_count * breadth
 
     pair = ((plane_count, channels, breadth), BF16)
@@ -452,14 +449,14 @@
     outside = swapped(*own, "gz")
     beside = swapped(near_row, far_row, "gy")
     inner, acc, hidden_grad = call(
-        inner_kernel, [cols, (lines, F32), (lines, F32)],
+        inner_kernel, [cols, (sums_of, F32), (lines, F32)],
         [((out_channels, row_count // 2 * breadth), BF16)],
         2 * conv_flops // 3, (*own, conv_weight, down_weight, cot),
     )
     near, far, near_row, far_row, acc = lax.optimization_barrier((*outside, *beside, acc))
     outside, own_rows = (near, far), (near_row, far_row)
     beside = swapped(*call(outer_rows_kernel, [pair, pair], [], 0, outside), "gy")
-    far, near = lax.optimization_barrier((beside[1], beside[0]))
+    far, near, weight_bwd = lax.optimization_barrier((beside[1], beside[0], weight_bwd))
     beside = (near, far)
     rows_cols = ((plane_count, 2, 3 * channels, breadth), BF16)
     outer, own_edges, *inside = call(
@@ -503,7 +500,7 @@
     sends = call(edges_kernel, [edge, edge], [], 0, (*gates, *outside))
     beside = swapped(*sends, "gy")
     (acc,) = call(
-        field_kernel, [(lines, F32)], [cols, cols], conv_flops, (*gates, *outside, weight_bwd)
+        field_kernel, [(sums_of, F32)], [cols, cols], conv_flops, (*gates, *outside, weight_bwd)
     )
     wide = [("gy", 1 << k) for k in range(2, lax.axis_size("gy").bit_length() - 1)]
     wide += [("gz", 1 << k) for k in range(2, lax.axis_size("gz").bit_length() - 1)]

time: 48.6 us -> 51.3 us (1.056)
  local copies, waits for them, and re-layouts: 2.69 us -> 5.88 us
  waiting for transfers between devices: 16.4 us -> 14.6 us
  starting transfers between devices: 17.4 us -> 18.1 us
    transpose x2, local copies, waits for them, and re-layouts: 0.29 us -> 2.76 us  [body(): turned.transpose(0, 1, 4, 3, 2).reshape(3, 3, channels, 3 * channels)]
    ppermute x10, waiting for transfers between devices: 1.54 us -> 0.03 us  [swap(): return lax.ppermute(cells, axis, pairs + [(b, a) for a, b in pairs])]
    ppermute x8, starting transfers between devices: 3.43 us -> 4.5 us  [flip(): lax.ppermute(cells, ('gz', 'gy'), [(i, i ^ mask) for i in range(lax.axis_...]
    pallas_call x1, local copies, waits for them, and re-layouts: 0.26 us -> 0.97 us  [fetch(): pl.pallas_call(fetch_kernel, out_shape=[jax.ShapeDtypeStruct(x.shape, x.d...]
    pallas_call x18, Pallas kernels: 10.8 us -> 11.3 us  [call(): pl.pallas_call(kernel, out_shape=[jax.ShapeDtypeStruct(s, d) for s, d in...]
    unnamed x8 -> x12, local copies, waits for them, and re-layouts: 1.91 us -> 1.92 us
  transfers between devices with their start and end apart: 18 -> 18, of which waited for: 9 -> 7; matrix products, arithmetic and copies ran while one was open for 2% -> 8% of each run, Pallas kernels for 17% -> 17%
where the time goes in v24:
time: 51.3 us; the launch traced here: 51.1 us
  starting transfers between devices  18.1 us (35%)
  waiting for transfers between devices  14.6 us (28%)
  Pallas kernels  11.6 us (23%)
  local copies, waits for them, and re-layouts  5.88 us (11%)
  between operations  0.87 us (2%)
    ppermute x8, waiting for transfers between devices, flip(): lax.ppermute(cells, ('gz', 'gy'), [(i, i ^ mask) for i in range(lax.axis_...  14.5 us
    ppermute x10, starting transfers between devices, swap(): return lax.ppermute(cells, axis, pairs + [(b, a) for a, b in pairs])  13.6 us
    pallas_call x18, Pallas kernels, call(): pl.pallas_call(kernel, out_shape=[jax.ShapeDtypeStruct(s, d) for s, d in...  11.3 us
    ppermute x8, starting transfers between devices, flip(): lax.ppermute(cells, ('gz', 'gy'), [(i, i ^ mask) for i in range(lax.axis_...  4.5 us
    transpose x2, local copies, waits for them, and re-layouts, body(): turned.transpose(0, 1, 4, 3, 2).reshape(3, 3, channels, 3 * channels)  2.76 us
    unnamed x12, local copies, waits for them, and re-layouts  1.92 us
  transfers between devices with their start and end apart: 18, of which 7 were waited for; matrix products, arithmetic and copies ran while one was open for 8% of the time, Pallas kernels for 17%

profile of v24, /device:TPU:0, one launch (start us, length us, event | category | flops | bytes accessed | tf_op | source)
XLA Modules:
  0.0 51.1 jit_solution(14210808268280107476)
XLA Ops:
  0.6 0.9 %copy-done.1 = bf16[64,2,8,128]{3,2,1,0:T(8,128)(2,1)S(1)} copy-done((bf16[64,2,8,128]{3,2,1,0:T(8,128)(2,1)S(1)}, bf16[64,2,8,128]{3,2,1,0:T(8,128)(2,1)}, u32[]{:S(2)}) %copy-start.1) | copy-done | bytes 262168
  1.6 0.2 shard_map.75
  1.8 3.0 %collective-permute-start = (bf16[8,64,128]{2,1,0:T(8,128)(2,1)S(1)}, bf16[8,64,128]{2,1,0:T(8,128)(2,1)S(1)}, u32[]{:S(2)}, u32[]{:S(2)}) collective-permute-start(bf16[8,64,128]{2,1,0:T(8,128)(2,1)S(1)} %get-tuple-element.61.near), channel_id=1, source_target_pairs={{0,4},{8,12},{16,20},{24,28},{4,0},{12,8},{20,16},{28,24},{1,5},{9... | collective-permute-start | bytes 393224 | tf_op jit(solution)/shard_map/ppermute | solution.py:409
  4.8 3.5 %collective-permute-start.1 = (bf16[8,64,128]{2,1,0:T(8,128)(2,1)S(1)}, bf16[8,64,128]{2,1,0:T(8,128)(2,1)S(1)}, u32[]{:S(2)}, u32[]{:S(2)}) collective-permute-start(bf16[8,64,128]{2,1,0:T(8,128)(2,1)S(1)} %get-tuple-element.62.far), channel_id=1, source_target_pairs={{4,8},{12,16},{20,24},{28,0},{8,4},{16,12},{24,20},{0,28},{5,9},{1... | collective-permute-start | bytes 393224 | tf_op jit(solution)/shard_map/ppermute | solution.py:409
  8.4 0.0 collective-permute-start.2
  8.4 1.6 %collective-permute-start.3 = (bf16[2,64,128]{2,1,0:T(8,128)(2,1)S(1)}, bf16[2,64,128]{2,1,0:T(8,128)(2,1)S(1)}, u32[]{:S(2)}, u32[]{:S(2)}) collective-permute-start(bf16[2,64,128]{2,1,0:T(8,128)(2,1)S(1)} %get-tuple-element.68), channel_id=1, source_target_pairs={{1,2},{3,0},{2,1},{0,3},{5,6},{7,4},{6,5},{4,7},{9,10},{11,8},{10,... | collective-permute-start | bytes 98312 | tf_op jit(solution)/shard_map/ppermute | solution.py:409
  10.0 1.0 %copy-done = bf16[3,3,64,192]{3,2,1,0:T(8,128)(2,1)S(1)} copy-done((bf16[3,3,64,192]{3,2,1,0:T(8,128)(2,1)S(1)}, bf16[3,3,64,192]{3,2,1,0:T(8,128)(2,1)}, u32[]{:S(2)}) %copy-start) | copy-done | bytes 221208
  11.0 0.3 shard_map.76
  11.3 1.0 %copy.9 = bf16[3,3,64,192]{2,3,1,0:T(8,128)(2,1)} copy(bf16[3,3,64,192]{3,2,1,0:T(8,128)(2,1)S(1)} %get-tuple-element.63.w_ref) | data formatting | bytes 442368 | tf_op jit(solution)/shard_map/pallas_call | solution.py:67
  12.3 2.2 %shard_map.77 = (bf16[2,10,192,128]{3,2,1,0:T(8,128)(2,1)S(1)}, f32[2,12,64,128]{3,2,1,0:T(8,128)S(1)}, f32[2,8,64,128]{3,2,1,0:T(8,128)S(1)}) custom-call(bf16[8,64,128]{2,1,0:T(8,128)(2,1)S(1)} %get-tuple-element.61.near, bf16[8,64,128]{2,1,0:T(8,128)(2,1)S(1)} %get-tuple-element.62.far, bf16[3,3,64,192]{3,2,1,0:T(8,128)(2,1)S(1)} %get-tuple-element.63.w_ref, ...), custom_call_target="tpu_custom_call" | custom-call | flops 301989888 | bytes 2973696 | tf_op jit(solution)/shard_map/pallas_call | solution.py:20
  14.4 0.0 collective-permute-done.2.near_row
  14.5 0.0 collective-permute-done.3.far_row
  14.5 0.0 collective-permute-done.1.far.far_in
  14.5 0.2 collective-permute-start.4
  14.7 0.5 %collective-permute-start.5 = (bf16[2,64,128]{2,1,0:T(8,128)(2,1)S(1)}, bf16[2,64,128]{2,1,0:T(8,128)(2,1)S(1)}, u32[]{:S(2)}, u32[]{:S(2)}) collective-permute-start(bf16[2,64,128]{2,1,0:T(8,128)(2,1)S(1)} %get-tuple-element.79), channel_id=1, source_target_pairs={{0,1},{2,3},{1,0},{3,2},{4,5},{6,7},{5,4},{7,6},{8,9},{10,11},{9,8... | collective-permute-start | bytes 98312 | tf_op jit(solution)/shard_map/ppermute | solution.py:409
  15.2 0.8 %reverse_bitcast_fusion = bf16[3,3,64,3,64]{4,2,3,1,0:T(8,128)(2,1)} fusion(bf16[3,3,64,3,64]{2,4,3,1,0:T(8,128)(2,1)S(1)} %bitcast.9), kind=kLoop, calls=%fused_computation | loop fusion | bytes 442368 | tf_op jit(solution)/shard_map/transpose | solution.py:435
  16.0 2.0 %copy.10 = bf16[3,3,64,3,64]{2,4,3,1,0:T(8,128)(2,1)} copy(bf16[3,3,64,3,64]{4,2,3,1,0:T(8,128)(2,1)} %reverse_bitcast_fusion) | data formatting | bytes 442368 | tf_op jit(solution)/shard_map/transpose | solution.py:435
  18.0 1.2 %shard_map.78 = (bf16[2,10,192,128]{3,2,1,0:T(8,128)(2,1)S(1)}, bf16[2,2,192,128]{3,2,1,0:T(8,128)(2,1)S(1)}, f32[2,2,64,128]{3,2,1,0:T(8,128)S(1)}, bf16[8,64,1...) custom-call(bf16[8,64,128]{2,1,0:T(8,128)(2,1)S(1)} %collective-permute-done.near.near_in,, ...), custom_call_target="tpu_custom_call" | custom-call | flops 150994944 | bytes 3694592 | tf_op jit(solution)/shard_map/pallas_call | solution.py:20
  19.2 0.0 collective-permute-done.5.near
  19.2 0.3 shard_map.80
  19.5 1.2 %shard_map.81 = (f32[704,128]{1,0:T(8,128)S(1)}, bf16[704,128]{1,0:T(8,128)(2,1)S(1)}) custom-call(bf16[2,10,192,128]{3,2,1,0:T(8,128)(2,1)S(1)} %get-tuple-element.66.inner, bf16[2,10,192,128]{3,2,1,0:T(8,128)(2,1)S(1)} %get-tuple-element.76.outer, bf16[2,2,192,128]{3,2,1,0:T(8,128)(2,1)S(1)} %get-tuple-element.77.own_edges, ...), custom_call_target="tpu_custom_call" | custom-call | flops 452984832 | bytes 3489792 | tf_op jit(solution)/shard_map/pallas_call | solution.py:20
  20.7 0.1 collective-permute-start.6
  20.8 1.4 %collective-permute-done.6.other = bf16[704,128]{1,0:T(8,128)(2,1)S(1)} collective-permute-done((bf16[704,128]{1,0:T(8,128)(2,1)S(1)}, bf16[704,128]{1,0:T(8,128)(2,1)S(1)}, u32[]{:S(2)}, u32[]{:S(2)}) %collective-permute-start.6) | collective-permute-done | bytes 180256 | tf_op jit(solution)/shard_map/ppermute | solution.py:415
  22.2 0.1 shard_map.82
  22.3 0.1 collective-permute-start.7
  22.4 0.8 %collective-permute-start.10 = (bf16[8,64,128]{2,1,0:T(8,128)(2,1)S(1)}, bf16[8,64,128]{2,1,0:T(8,128)(2,1)S(1)}, u32[]{:S(2)}, u32[]{:S(2)}) collective-permute-start(bf16[8,64,128]{2,1,0:T(8,128)(2,1)S(1)} %get-tuple-element.99.near), channel_id=1, source_target_pairs={{0,4},{8,12},{16,20},{24,28},{4,0},{12,8},{20,16},{28,24},{1,5},{9... | collective-permute-start | bytes 393224 | tf_op jit(solution)/shard_map/ppermute | solution.py:409
  23.2 2.3 %collective-permute-start.11 = (bf16[8,64,128]{2,1,0:T(8,128)(2,1)S(1)}, bf16[8,64,128]{2,1,0:T(8,128)(2,1)S(1)}, u32[]{:S(2)}, u32[]{:S(2)}) collective-permute-start(bf16[8,64,128]{2,1,0:T(8,128)(2,1)S(1)} %get-tuple-element.100.far), channel_id=1, source_target_pairs={{4,8},{12,16},{20,24},{28,0},{8,4},{16,12},{24,20},{0,28},{5,9},{1... | collective-permute-start | bytes 393224 | tf_op jit(solution)/shard_map/ppermute | solution.py:409
  25.5 1.5 %collective-permute-done.7.other = bf16[352,128]{1,0:T(8,128)(2,1)S(1)} collective-permute-done((bf16[352,128]{1,0:T(8,128)(2,1)S(1)}, bf16[352,128]{1,0:T(8,128)(2,1)S(1)}, u32[]{:S(2)}, u32[]{:S(2)}) %collective-permute-start.7) | collective-permute-done | bytes 90144 | tf_op jit(solution)/shard_map/ppermute | solution.py:415
  27.0 1.9 %collective-permute-start.8 = (bf16[176,128]{1,0:T(8,128)(2,1)S(1)}, bf16[176,128]{1,0:T(8,128)(2,1)S(1)}, u32[]{:S(2)}, u32[]{:S(2)}) collective-permute-start(bf16[176,128]{1,0:T(8,128)(2,1)S(1)} %get-tuple-element.98), channel_id=1, source_target_pairs={{0,3},{1,2},{2,1},{3,0},{4,7},{5,6},{6,5},{7,4},{8,11},{9,10},{10,... | collective-permute-start | bytes 135176 | tf_op jit(solution)/shard_map/ppermute | solution.py:415
  28.9 1.7 %collective-permute-done.8.y = bf16[176,128]{1,0:T(8,128)(2,1)S(1)} collective-permute-done((bf16[176,128]{1,0:T(8,128)(2,1)S(1)}, bf16[176,128]{1,0:T(8,128)(2,1)S(1)}, u32[]{:S(2)}, u32[]{:S(2)}) %collective-permute-start.8) | collective-permute-done | bytes 45088 | tf_op jit(solution)/shard_map/ppermute | solution.py:415
  30.7 0.1 collective-permute-start.9
  30.7 3.5 %collective-permute-done.9.y = bf16[176,128]{1,0:T(8,128)(2,1)S(1)} collective-permute-done((bf16[176,128]{1,0:T(8,128)(2,1)S(1)}, bf16[176,128]{1,0:T(8,128)(2,1)S(1)}, u32[]{:S(2)}, u32[]{:S(2)}) %collective-permute-start.9) | collective-permute-done | bytes 45088 | tf_op jit(solution)/shard_map/ppermute | solution.py:415
  34.2 0.0 copy-start.4
  34.2 0.0 collective-permute-done.11.far_in
  34.2 0.7 %collective-permute-start.12 = (bf16[176,128]{1,0:T(8,128)(2,1)S(1)}, bf16[176,128]{1,0:T(8,128)(2,1)S(1)}, u32[]{:S(2)}, u32[]{:S(2)}) collective-permute-start(bf16[176,128]{1,0:T(8,128)(2,1)S(1)} %shard_map.85.x), channel_id=1, source_target_pairs={{0,17},{1,16},{2,19},{3,18},{4,21},{5,20},{6,23},{7,22},{8,25},{9,... | collective-permute-start | bytes 135176 | tf_op jit(solution)/shard_map/ppermute | solution.py:415
  35.0 0.3 collective-permute-start.14
  35.3 1.3 %collective-permute-start.15 = (bf16[4,64,128]{2,1,0:T(8,128)(2,1)S(1)}, bf16[4,64,128]{2,1,0:T(8,128)(2,1)S(1)}, u32[]{:S(2)}, u32[]{:S(2)}) collective-permute-start(bf16[4,64,128]{2,1,0:T(8,128)(2,1)S(1)} %get-tuple-element.109), channel_id=1, source_target_pairs={{1,2},{3,0},{2,1},{0,3},{5,6},{7,4},{6,5},{4,7},{9,10},{11,8},{10,... | collective-permute-start | bytes 196616 | tf_op jit(solution)/shard_map/ppermute | solution.py:409
  36.6 1.1 %shard_map.87 = bf16[128,256]{1,0:T(8,128)(2,1)} custom-call(bf16[2,8,64,128]{3,2,1,0:T(8,128)(2,1)S(1)} %get-tuple-element.102.h_ref, bf16[2,2,128,128]{3,2,1,0:T(8,128)(2,1)S(1)} %get-tuple-element.64.d_ref), custom_call_target="tpu_custom_call" | custom-call | flops 45298484 | bytes 458752 | tf_op jit(solution)/shard_map/pallas_call | solution.py:20
  37.7 2.2 %collective-permute-done.12.y = bf16[176,128]{1,0:T(8,128)(2,1)S(1)} collective-permute-done((bf16[176,128]{1,0:T(8,128)(2,1)S(1)}, bf16[176,128]{1,0:T(8,128)(2,1)S(1)}, u32[]{:S(2)}, u32[]{:S(2)}) %collective-permute-start.12) | collective-permute-done | bytes 45088 | tf_op jit(solution)/shard_map/ppermute | solution.py:415
  39.9 1.2 %collective-permute-start.13 = (bf16[176,128]{1,0:T(8,128)(2,1)S(1)}, bf16[176,128]{1,0:T(8,128)(2,1)S(1)}, u32[]{:S(2)}, u32[]{:S(2)}) collective-permute-start(bf16[176,128]{1,0:T(8,128)(2,1)S(1)} %shard_map.86.mine), channel_id=1, source_target_pairs={{0,3},{1,2},{2,1},{3,0},{4,7},{5,6},{6,5},{7,4},{8,11},{9,10},{10,... | collective-permute-start | bytes 135176 | tf_op jit(solution)/shard_map/ppermute | solution.py:415
  41.1 0.2 copy.11.w_ref
  41.4 2.5 %shard_map.89.acc_ref = f32[2,12,64,128]{3,2,1,0:T(8,128)S(1)} custom-call(bf16[8,64,128]{2,1,0:T(8,128)(2,1)S(1)} %get-tuple-element.99.near, bf16[8,64,128]{2,1,0:T(8,128)(2,1)S(1)} %get-tuple-element.100.far, bf16[8,64,128]{2,1,0:T(8,128)(2,1)S(1)} %collective-permute-done.10.near_in, bf16[8,64,128]{2,1,0:T(8,128)(2,1)S(1)} %collective-permute-done.11.far_in, ...), custom_call_target="tpu_custom_call" | custom-call | flops 452984832 | bytes 1531904 | tf_op jit(solution)/shard_map/pallas_call | solution.py:20
  44.0 0.1 collective-permute-start.16
  44.1 1.3 %shard_map.92 = f32[1024,128]{1,0:T(8,128)} custom-call(bf16[4,64,128]{2,1,0:T(8,128)(2,1)S(1)} %collective-permute-done.14.near, bf16[4,64,128]{2,1,0:T(8,128)(2,1)S(1)} %collective-permute-done.15.far, f32[2,12,64,128]{3,2,1,0:T(8,128)S(1)} %shard_map.89.acc_ref, bf16[3,3,64,192]{3,2,1,0:T(8,128)(2,1)S(1)} %copy.11.w_ref), custom_call_target="tpu_custom_call" | custom-call | flops 45298484 | bytes 1662976 | tf_op jit(solution)/shard_map/pallas_call | solution.py:20
  45.4 3.1 %collective-permute-done.16.other = bf16[352,128]{1,0:T(8,128)(2,1)S(1)} collective-permute-done((bf16[352,128]{1,0:T(8,128)(2,1)S(1)}, bf16[352,128]{1,0:T(8,128)(2,1)S(1)}, u32[]{:S(2)}, u32[]{:S(2)}) %collective-permute-start.16) | collective-permute-done | bytes 90144 | tf_op jit(solution)/shard_map/ppermute | solution.py:415
  48.6 0.4 collective-permute-start.17
  48.9 1.1 %collective-permute-done.17.other = bf16[704,128]{1,0:T(8,128)(2,1)S(1)} collective-permute-done((bf16[704,128]{1,0:T(8,128)(2,1)S(1)}, bf16[704,128]{1,0:T(8,128)(2,1)S(1)}, u32[]{:S(2)}, u32[]{:S(2)}) %collective-permute-start.17) | collective-permute-done | bytes 180256 | tf_op jit(solution)/shard_map/ppermute | solution.py:415
  50.0 1.0 %shard_map.93 = (f32[3,3,64,192]{3,2,1,0:T(8,128)}, f32[2,2,128,128]{3,2,1,0:T(8,128)}) custom-call(bf16[704,128]{1,0:T(8,128)(2,1)S(1)} %shard_map.91.mine, bf16[704,128]{1,0:T(8,128)(2,1)S(1)} %collective-permute-done.17.other), custom_call_target="tpu_custom_call" | custom-call | bytes 1064960 | tf_op jit(solution)/shard_map/pallas_call | solution.py:20
  (23 shorter events, 0.2 us)
Async XLA Ops:
  0.6 1.0 %copy-start.1 = (bf16[64,2,8,128]{3,2,1,0:T(8,128)(2,1)S(1)}, bf16[64,2,8,128]{3,2,1,0:T(8,128)(2,1)}, u32[]{:S(2)}) copy-start(bf16[64,2,8,128]{3,2,1,0:T(8,128)(2,1)} %f_ref.1) | copy-start | bytes 786436
  1.6 8.4 %copy-start.2 = (bf16[2,2,128,128]{3,2,1,0:T(8,128)(2,1)S(1)}, bf16[2,2,128,128]{3,2,1,0:T(8,128)(2,1)}, u32[]{:S(2)}) copy-start(bf16[2,2,128,128]{3,2,1,0:T(8,128)(2,1)} %refs_1_.1) | copy-start | bytes 393220
  1.6 8.4 %copy-start.3 = (bf16[128,1,256]{2,0,1:T(8,128)(2,1)S(1)}, bf16[128,1,256]{2,0,1:T(8,128)(2,1)}, u32[]{:S(2)}) copy-start(bf16[128,1,256]{2,0,1:T(8,128)(2,1)} %param.7) | copy-start | bytes 196612
  1.8 12.7 %collective-permute-start = (bf16[8,64,128]{2,1,0:T(8,128)(2,1)S(1)}, bf16[8,64,128]{2,1,0:T(8,128)(2,1)S(1)}, u32[]{:S(2)}, u32[]{:S(2)}) collective-permute-start(bf16[8,64,128]{2,1,0:T(8,128)(2,1)S(1)} %get-tuple-element.61.near), channel_id=1, source_target_pairs={{0,4},{8,12},{16,20},{24,28},{4,0},{12,8},{20,16},{28,24},{1,5},{9... | collective-permute-start | bytes 393224 | tf_op jit(solution)/shard_map/ppermute | solution.py:409
  4.8 9.6 %collective-permute-start.1 = (bf16[8,64,128]{2,1,0:T(8,128)(2,1)S(1)}, bf16[8,64,128]{2,1,0:T(8,128)(2,1)S(1)}, u32[]{:S(2)}, u32[]{:S(2)}) collective-permute-start(bf16[8,64,128]{2,1,0:T(8,128)(2,1)S(1)} %get-tuple-element.62.far), channel_id=1, source_target_pairs={{4,8},{12,16},{20,24},{28,0},{8,4},{16,12},{24,20},{0,28},{5,9},{1... | collective-permute-start | bytes 393224 | tf_op jit(solution)/shard_map/ppermute | solution.py:409
  8.4 6.1 %collective-permute-start.2 = (bf16[2,64,128]{2,1,0:T(8,128)(2,1)S(1)}, bf16[2,64,128]{2,1,0:T(8,128)(2,1)S(1)}, u32[]{:S(2)}, u32[]{:S(2)}) collective-permute-start(bf16[2,64,128]{2,1,0:T(8,128)(2,1)S(1)} %get-tuple-element.67), channel_id=1, source_target_pairs={{0,1},{2,3},{1,0},{3,2},{4,5},{6,7},{5,4},{7,6},{8,9},{10,11},{9,8... | collective-permute-start | bytes 98312 | tf_op jit(solution)/shard_map/ppermute | solution.py:409
  8.4 6.1 %collective-permute-start.3 = (bf16[2,64,128]{2,1,0:T(8,128)(2,1)S(1)}, bf16[2,64,128]{2,1,0:T(8,128)(2,1)S(1)}, u32[]{:S(2)}, u32[]{:S(2)}) collective-permute-start(bf16[2,64,128]{2,1,0:T(8,128)(2,1)S(1)} %get-tuple-element.68), channel_id=1, source_target_pairs={{1,2},{3,0},{2,1},{0,3},{5,6},{7,4},{6,5},{4,7},{9,10},{11,8},{10,... | collective-permute-start | bytes 98312 | tf_op jit(solution)/shard_map/ppermute | solution.py:409
  10.0 1.0 %copy-start = (bf16[3,3,64,192]{3,2,1,0:T(8,128)(2,1)S(1)}, bf16[3,3,64,192]{3,2,1,0:T(8,128)(2,1)}, u32[]{:S(2)}) copy-start(bf16[3,3,64,192]{3,2,1,0:T(8,128)(2,1)} %refs_0_.1) | copy-start | bytes 663556
  12.3 3.0 %copy-start.5 = (bf16[3,3,64,192]{2,3,1,0:T(8,128)(2,1)S(1)}, bf16[3,3,64,192]{2,3,1,0:T(8,128)(2,1)}, u32[]{:S(2)}) copy-start(bf16[3,3,64,192]{2,3,1,0:T(8,128)(2,1)} %copy.9) | copy-start | bytes 663556
  14.5 4.6 %collective-permute-start.4 = (bf16[2,64,128]{2,1,0:T(8,128)(2,1)S(1)}, bf16[2,64,128]{2,1,0:T(8,128)(2,1)S(1)}, u32[]{:S(2)}, u32[]{:S(2)}) collective-permute-start(bf16[2,64,128]{2,1,0:T(8,128)(2,1)S(1)} %get-tuple-element.78), channel_id=1, source_target_pairs={{1,2},{3,0},{2,1},{0,3},{5,6},{7,4},{6,5},{4,7},{9,10},{11,8},{10,... | collective-permute-start | bytes 98312 | tf_op jit(solution)/shard_map/ppermute | solution.py:409
  14.7 4.5 %collective-permute-start.5 = (bf16[2,64,128]{2,1,0:T(8,128)(2,1)S(1)}, bf16[2,64,128]{2,1,0:T(8,128)(2,1)S(1)}, u32[]{:S(2)}, u32[]{:S(2)}) collective-permute-start(bf16[2,64,128]{2,1,0:T(8,128)(2,1)S(1)} %get-tuple-element.79), channel_id=1, source_target_pairs={{0,1},{2,3},{1,0},{3,2},{4,5},{6,7},{5,4},{7,6},{8,9},{10,11},{9,8... | collective-permute-start | bytes 98312 | tf_op jit(solution)/shard_map/ppermute | solution.py:409
  20.7 1.5 %collective-permute-start.6 = (bf16[704,128]{1,0:T(8,128)(2,1)S(1)}, bf16[704,128]{1,0:T(8,128)(2,1)S(1)}, u32[]{:S(2)}, u32[]{:S(2)}) collective-permute-start(bf16[704,128]{1,0:T(8,128)(2,1)S(1)} %get-tuple-element.92), channel_id=1, source_target_pairs={{0,1},{1,0},{2,3},{3,2},{4,5},{5,4},{6,7},{7,6},{8,9},{9,8},{10,11... | collective-permute-start | bytes 540680 | tf_op jit(solution)/shard_map/ppermute | solution.py:415
  22.3 4.7 %collective-permute-start.7 = (bf16[352,128]{1,0:T(8,128)(2,1)S(1)}, bf16[352,128]{1,0:T(8,128)(2,1)S(1)}, u32[]{:S(2)}, u32[]{:S(2)}) collective-permute-start(bf16[352,128]{1,0:T(8,128)(2,1)S(1)} %get-tuple-element.96), channel_id=1, source_target_pairs={{0,9},{1,8},{2,11},{3,10},{4,13},{5,12},{6,15},{7,14},{8,1},{9,0},... | collective-permute-start | bytes 270344 | tf_op jit(solution)/shard_map/ppermute | solution.py:415
  22.4 11.9 %collective-permute-start.10 = (bf16[8,64,128]{2,1,0:T(8,128)(2,1)S(1)}, bf16[8,64,128]{2,1,0:T(8,128)(2,1)S(1)}, u32[]{:S(2)}, u32[]{:S(2)}) collective-permute-start(bf16[8,64,128]{2,1,0:T(8,128)(2,1)S(1)} %get-tuple-element.99.near), channel_id=1, source_target_pairs={{0,4},{8,12},{16,20},{24,28},{4,0},{12,8},{20,16},{28,24},{1,5},{9... | collective-permute-start | bytes 393224 | tf_op jit(solution)/shard_map/ppermute | solution.py:409
  23.2 11.1 %collective-permute-start.11 = (bf16[8,64,128]{2,1,0:T(8,128)(2,1)S(1)}, bf16[8,64,128]{2,1,0:T(8,128)(2,1)S(1)}, u32[]{:S(2)}, u32[]{:S(2)}) collective-permute-start(bf16[8,64,128]{2,1,0:T(8,128)(2,1)S(1)} %get-tuple-element.100.far), channel_id=1, source_target_pairs={{4,8},{12,16},{20,24},{28,0},{8,4},{16,12},{24,20},{0,28},{5,9},{1... | collective-permute-start | bytes 393224 | tf_op jit(solution)/shard_map/ppermute | solution.py:409
  27.0 3.7 %collective-permute-start.8 = (bf16[176,128]{1,0:T(8,128)(2,1)S(1)}, bf16[176,128]{1,0:T(8,128)(2,1)S(1)}, u32[]{:S(2)}, u32[]{:S(2)}) collective-permute-start(bf16[176,128]{1,0:T(8,128)(2,1)S(1)} %get-tuple-element.98), channel_id=1, source_target_pairs={{0,3},{1,2},{2,1},{3,0},{4,7},{5,6},{6,5},{7,4},{8,11},{9,10},{10,... | collective-permute-start | bytes 135176 | tf_op jit(solution)/shard_map/ppermute | solution.py:415
  30.7 3.5 %collective-permute-start.9 = (bf16[176,128]{1,0:T(8,128)(2,1)S(1)}, bf16[176,128]{1,0:T(8,128)(2,1)S(1)}, u32[]{:S(2)}, u32[]{:S(2)}) collective-permute-start(bf16[176,128]{1,0:T(8,128)(2,1)S(1)} %shard_map.84.x), channel_id=1, source_target_pairs={{0,5},{1,4},{2,7},{3,6},{4,1},{5,0},{6,3},{7,2},{8,13},{9,12},{10,... | collective-permute-start | bytes 135176 | tf_op jit(solution)/shard_map/ppermute | solution.py:415
  34.2 6.9 %copy-start.4 = (bf16[3,3,64,3,64]{2,4,3,1,0:T(8,128)(2,1)S(1)}, bf16[3,3,64,3,64]{2,4,3,1,0:T(8,128)(2,1)}, u32[]{:S(2)}) copy-start(bf16[3,3,64,3,64]{2,4,3,1,0:T(8,128)(2,1)} %copy.10) | copy-start | bytes 663556
  34.2 5.7 %collective-permute-start.12 = (bf16[176,128]{1,0:T(8,128)(2,1)S(1)}, bf16[176,128]{1,0:T(8,128)(2,1)S(1)}, u32[]{:S(2)}, u32[]{:S(2)}) collective-permute-start(bf16[176,128]{1,0:T(8,128)(2,1)S(1)} %shard_map.85.x), channel_id=1, source_target_pairs={{0,17},{1,16},{2,19},{3,18},{4,21},{5,20},{6,23},{7,22},{8,25},{9,... | collective-permute-start | bytes 135176 | tf_op jit(solution)/shard_map/ppermute | solution.py:415
  35.0 9.0 %collective-permute-start.14 = (bf16[4,64,128]{2,1,0:T(8,128)(2,1)S(1)}, bf16[4,64,128]{2,1,0:T(8,128)(2,1)S(1)}, u32[]{:S(2)}, u32[]{:S(2)}) collective-permute-start(bf16[4,64,128]{2,1,0:T(8,128)(2,1)S(1)} %get-tuple-element.108), channel_id=1, source_target_pairs={{0,1},{2,3},{1,0},{3,2},{4,5},{6,7},{5,4},{7,6},{8,9},{10,11},{9,8... | collective-permute-start | bytes 196616 | tf_op jit(solution)/shard_map/ppermute | solution.py:409
  35.3 8.7 %collective-permute-start.15 = (bf16[4,64,128]{2,1,0:T(8,128)(2,1)S(1)}, bf16[4,64,128]{2,1,0:T(8,128)(2,1)S(1)}, u32[]{:S(2)}, u32[]{:S(2)}) collective-permute-start(bf16[4,64,128]{2,1,0:T(8,128)(2,1)S(1)} %get-tuple-element.109), channel_id=1, source_target_pairs={{1,2},{3,0},{2,1},{0,3},{5,6},{7,4},{6,5},{4,7},{9,10},{11,8},{10,... | collective-permute-start | bytes 196616 | tf_op jit(solution)/shard_map/ppermute | solution.py:409
  39.9 4.0 %collective-permute-start.13 = (bf16[176,128]{1,0:T(8,128)(2,1)S(1)}, bf16[176,128]{1,0:T(8,128)(2,1)S(1)}, u32[]{:S(2)}, u32[]{:S(2)}) collective-permute-start(bf16[176,128]{1,0:T(8,128)(2,1)S(1)} %shard_map.86.mine), channel_id=1, source_target_pairs={{0,3},{1,2},{2,1},{3,0},{4,7},{5,6},{6,5},{7,4},{8,11},{9,10},{10,... | collective-permute-start | bytes 135176 | tf_op jit(solution)/shard_map/ppermute | solution.py:415
  44.0 4.5 %collective-permute-start.16 = (bf16[352,128]{1,0:T(8,128)(2,1)S(1)}, bf16[352,128]{1,0:T(8,128)(2,1)S(1)}, u32[]{:S(2)}, u32[]{:S(2)}) collective-permute-start(bf16[352,128]{1,0:T(8,128)(2,1)S(1)} %shard_map.88.mine), channel_id=1, source_target_pairs={{0,9},{1,8},{2,11},{3,10},{4,13},{5,12},{6,15},{7,14},{8,1},{9,0},... | collective-permute-start | bytes 270344 | tf_op jit(solution)/shard_map/ppermute | solution.py:415
  48.6 1.5 %collective-permute-start.17 = (bf16[704,128]{1,0:T(8,128)(2,1)S(1)}, bf16[704,128]{1,0:T(8,128)(2,1)S(1)}, u32[]{:S(2)}, u32[]{:S(2)}) collective-permute-start(bf16[704,128]{1,0:T(8,128)(2,1)S(1)} %shard_map.91.mine), channel_id=1, source_target_pairs={{0,1},{1,0},{2,3},{3,2},{4,5},{5,4},{6,7},{7,6},{8,9},{9,8},{10,11... | collective-permute-start | bytes 540680 | tf_op jit(solution)/shard_map/ppermute | solution.py:415

commit v25 on v23

--- a/solution.py
+++ b/solution.py
@@ -51,6 +51,15 @@
     for z in range(2):
         near_row[z] = choose(even_y, ends[rows - 1][z], ends[0][z])
         far_row[z] = choose(even_y, ends[0][z], ends[rows - 1][z])
+
+
+def turn_kernel(w_ref, out):
+    channels = w_ref.shape[2]
+    for a in range(3):
+        for b in range(3):
+            turned = w_ref[a, b].astype(F32).T
+            blocks = [turned[(2 - e) * channels : (3 - e) * channels] for e in range(3)]
+            out[2 - a, 2 - b] = jnp.concatenate(blocks, axis=1).astype(BF16)
 
 
 def fetch_kernel(*refs):
@@ -435,8 +444,7 @@
     grad_scale = 1.0 / math.sqrt(plane_count * row_count * breadth * count)
     cot = cotangent.reshape(out_channels, -1)
     conv_weight, down_weight, cot = fetch(conv_weight, down_weight, cot)
-    turned = conv_weight.reshape(3, 3, channels, 3, channels)[::-1, ::-1, :, ::-1]
-    weight_bwd = turned.transpose(0, 1, 4, 3, 2).reshape(3, 3, channels, 3 * channels)
+    (weight_bwd,) = call(turn_kernel, [(conv_weight.shape, BF16)], [], 0, (conv_weight,))
     plane = ((row_count, channels, breadth), BF16)
     edge = ((plane_count + 2, channels, breadth), BF16)
     cols = ((plane_count, row_count + 2, 3 * channels, breadth), BF16)

time: 48.6 us -> 48.6 us (level)
  local copies, waits for them, and re-layouts: 2.69 us -> 1.91 us
    pallas_call x18 -> x19, Pallas kernels: 10.8 us -> 11.2 us  [call(): pl.pallas_call(kernel, out_shape=[jax.ShapeDtypeStruct(s, d) for s, d in...]
  transfers between devices with their start and end apart: 18 -> 18, of which waited for: 9 -> 9; matrix products, arithmetic and copies ran while one was open for 2% -> 0% of each run, Pallas kernels for 17% -> 18%
where the time goes in v25:
time: 48.6 us; the launch traced here: 48.4 us
  starting transfers between devices  17.4 us (36%)
  waiting for transfers between devices  16.8 us (35%)
  Pallas kernels  11.5 us (24%)
  local copies, waits for them, and re-layouts  1.91 us (4%)
  between operations  0.83 us (2%)
    ppermute x8, waiting for transfers between devices, flip(): lax.ppermute(cells, ('gz', 'gy'), [(i, i ^ mask) for i in range(lax.axis_...  15.2 us
    ppermute x10, starting transfers between devices, swap(): return lax.ppermute(cells, axis, pairs + [(b, a) for a, b in pairs])  13.9 us
    pallas_call x19, Pallas kernels, call(): pl.pallas_call(kernel, out_shape=[jax.ShapeDtypeStruct(s, d) for s, d in...  11.2 us
    ppermute x8, starting transfers between devices, flip(): lax.ppermute(cells, ('gz', 'gy'), [(i, i ^ mask) for i in range(lax.axis_...  3.46 us
    unnamed x8, local copies, waits for them, and re-layouts  1.91 us
    ppermute x10, waiting for transfers between devices, swap(): return lax.ppermute(cells, axis, pairs + [(b, a) for a, b in pairs])  1.54 us
  transfers between devices with their start and end apart: 18, of which 9 were waited for; matrix products, arithmetic and copies ran while one was open for 0% of the time, Pallas kernels for 18%

profile of v25, /device:TPU:0, one launch (start us, length us, event | category | flops | bytes accessed | tf_op | source)
XLA Modules:
  0.0 48.4 jit_solution(1142215022361379199)
XLA Ops:
  0.6 0.9 %copy-done.1 = bf16[64,2,8,128]{3,2,1,0:T(8,128)(2,1)S(1)} copy-done((bf16[64,2,8,128]{3,2,1,0:T(8,128)(2,1)S(1)}, bf16[64,2,8,128]{3,2,1,0:T(8,128)(2,1)}, u32[]{:S(2)}) %copy-start.1) | copy-done | bytes 262168
  1.6 0.2 shard_map.75
  1.8 3.0 %collective-permute-start = (bf16[8,64,128]{2,1,0:T(8,128)(2,1)S(1)}, bf16[8,64,128]{2,1,0:T(8,128)(2,1)S(1)}, u32[]{:S(2)}, u32[]{:S(2)}) collective-permute-start(bf16[8,64,128]{2,1,0:T(8,128)(2,1)S(1)} %get-tuple-element.60.near), channel_id=1, source_target_pairs={{0,4},{8,12},{16,20},{24,28},{4,0},{12,8},{20,16},{28,24},{1,5},{9... | collective-permute-start | bytes 393224 | tf_op jit(solution)/shard_map/ppermute | solution.py:422
  4.8 3.5 %collective-permute-start.1 = (bf16[8,64,128]{2,1,0:T(8,128)(2,1)S(1)}, bf16[8,64,128]{2,1,0:T(8,128)(2,1)S(1)}, u32[]{:S(2)}, u32[]{:S(2)}) collective-permute-start(bf16[8,64,128]{2,1,0:T(8,128)(2,1)S(1)} %get-tuple-element.61.far), channel_id=1, source_target_pairs={{4,8},{12,16},{20,24},{28,0},{8,4},{16,12},{24,20},{0,28},{5,9},{1... | collective-permute-start | bytes 393224 | tf_op jit(solution)/shard_map/ppermute | solution.py:422
  8.4 0.0 collective-permute-start.2
  8.4 1.6 %collective-permute-start.3 = (bf16[2,64,128]{2,1,0:T(8,128)(2,1)S(1)}, bf16[2,64,128]{2,1,0:T(8,128)(2,1)S(1)}, u32[]{:S(2)}, u32[]{:S(2)}) collective-permute-start(bf16[2,64,128]{2,1,0:T(8,128)(2,1)S(1)} %get-tuple-element.67), channel_id=1, source_target_pairs={{1,2},{3,0},{2,1},{0,3},{5,6},{7,4},{6,5},{4,7},{9,10},{11,8},{10,... | collective-permute-start | bytes 98312 | tf_op jit(solution)/shard_map/ppermute | solution.py:422
  10.0 1.0 %copy-done = bf16[3,3,64,192]{3,2,1,0:T(8,128)(2,1)S(1)} copy-done((bf16[3,3,64,192]{3,2,1,0:T(8,128)(2,1)S(1)}, bf16[3,3,64,192]{3,2,1,0:T(8,128)(2,1)}, u32[]{:S(2)}) %copy-start) | copy-done | bytes 221208
  11.0 0.3 shard_map.76
  11.3 1.9 %shard_map.77 = (bf16[2,10,192,128]{3,2,1,0:T(8,128)(2,1)S(1)}, f32[2,8,64,128]{3,2,1,0:T(8,128)S(1)}, f32[2,8,64,128]{3,2,1,0:T(8,128)S(1)}) custom-call(bf16[8,64,128]{2,1,0:T(8,128)(2,1)S(1)} %get-tuple-element.60.near, bf16[8,64,128]{2,1,0:T(8,128)(2,1)S(1)} %get-tuple-element.61.far, bf16[3,3,64,192]{3,2,1,0:T(8,128)(2,1)S(1)} %get-tuple-element.62.w_ref, ...), custom_call_target="tpu_custom_call" | custom-call | flops 301989888 | bytes 2711552 | tf_op jit(solution)/shard_map/pallas_call | solution.py:20
  13.2 0.0 collective-permute-done.2.near_row
  13.2 0.0 collective-permute-done.3.far_row
  13.2 0.0 collective-permute-done.near.near_in
  13.3 0.0 collective-permute-done.1.far.far_in
  13.3 0.4 collective-permute-start.4
  13.7 0.5 collective-permute-start.5
  14.2 1.1 %shard_map.78 = (bf16[2,10,192,128]{3,2,1,0:T(8,128)(2,1)S(1)}, bf16[2,2,192,128]{3,2,1,0:T(8,128)(2,1)S(1)}, f32[2,2,64,128]{3,2,1,0:T(8,128)S(1)}, bf16[8,64,1...) custom-call(bf16[8,64,128]{2,1,0:T(8,128)(2,1)S(1)} %collective-permute-done.near.near_in,, ...), custom_call_target="tpu_custom_call" | custom-call | flops 150994944 | bytes 3432448 | tf_op jit(solution)/shard_map/pallas_call | solution.py:20
  15.3 1.5 %collective-permute-done.4.far = bf16[2,64,128]{2,1,0:T(8,128)(2,1)S(1)} collective-permute-done((bf16[2,64,128]{2,1,0:T(8,128)(2,1)S(1)}, bf16[2,64,128]{2,1,0:T(8,128)(2,1)S(1)}, u32[]{:S(2)}, u32[]{:S(2)}) %collective-permute-start.4) | collective-permute-done | bytes 32800 | tf_op jit(solution)/shard_map/ppermute | solution.py:422
  16.9 0.0 collective-permute-done.5.near
  16.9 0.3 shard_map.80
  17.2 1.2 %shard_map.81 = (f32[704,128]{1,0:T(8,128)S(1)}, bf16[704,128]{1,0:T(8,128)(2,1)S(1)}) custom-call(bf16[2,10,192,128]{3,2,1,0:T(8,128)(2,1)S(1)} %get-tuple-element.65.inner, bf16[2,10,192,128]{3,2,1,0:T(8,128)(2,1)S(1)} %get-tuple-element.75.outer, bf16[2,2,192,128]{3,2,1,0:T(8,128)(2,1)S(1)} %get-tuple-element.76.own_edges, ...), custom_call_target="tpu_custom_call" | custom-call | flops 452984832 | bytes 3489792 | tf_op jit(solution)/shard_map/pallas_call | solution.py:20
  18.4 0.2 collective-permute-start.6
  18.6 1.3 %collective-permute-done.6.other = bf16[704,128]{1,0:T(8,128)(2,1)S(1)} collective-permute-done((bf16[704,128]{1,0:T(8,128)(2,1)S(1)}, bf16[704,128]{1,0:T(8,128)(2,1)S(1)}, u32[]{:S(2)}, u32[]{:S(2)}) %collective-permute-start.6) | collective-permute-done | bytes 180256 | tf_op jit(solution)/shard_map/ppermute | solution.py:428
  19.9 0.1 shard_map.82
  20.0 0.1 collective-permute-start.7
  20.1 1.0 %collective-permute-start.10 = (bf16[8,64,128]{2,1,0:T(8,128)(2,1)S(1)}, bf16[8,64,128]{2,1,0:T(8,128)(2,1)S(1)}, u32[]{:S(2)}, u32[]{:S(2)}) collective-permute-start(bf16[8,64,128]{2,1,0:T(8,128)(2,1)S(1)} %get-tuple-element.98.near), channel_id=1, source_target_pairs={{0,4},{8,12},{16,20},{24,28},{4,0},{12,8},{20,16},{28,24},{1,5},{9... | collective-permute-start | bytes 393224 | tf_op jit(solution)/shard_map/ppermute | solution.py:422
  21.1 2.4 %collective-permute-start.11 = (bf16[8,64,128]{2,1,0:T(8,128)(2,1)S(1)}, bf16[8,64,128]{2,1,0:T(8,128)(2,1)S(1)}, u32[]{:S(2)}, u32[]{:S(2)}) collective-permute-start(bf16[8,64,128]{2,1,0:T(8,128)(2,1)S(1)} %get-tuple-element.99.far), channel_id=1, source_target_pairs={{4,8},{12,16},{20,24},{28,0},{8,4},{16,12},{24,20},{0,28},{5,9},{1... | collective-permute-start | bytes 393224 | tf_op jit(solution)/shard_map/ppermute | solution.py:422
  23.6 1.1 %collective-permute-done.7.other = bf16[352,128]{1,0:T(8,128)(2,1)S(1)} collective-permute-done((bf16[352,128]{1,0:T(8,128)(2,1)S(1)}, bf16[352,128]{1,0:T(8,128)(2,1)S(1)}, u32[]{:S(2)}, u32[]{:S(2)}) %collective-permute-start.7) | collective-permute-done | bytes 90144 | tf_op jit(solution)/shard_map/ppermute | solution.py:428
  24.7 1.1 %collective-permute-start.8 = (bf16[176,128]{1,0:T(8,128)(2,1)S(1)}, bf16[176,128]{1,0:T(8,128)(2,1)S(1)}, u32[]{:S(2)}, u32[]{:S(2)}) collective-permute-start(bf16[176,128]{1,0:T(8,128)(2,1)S(1)} %get-tuple-element.97), channel_id=1, source_target_pairs={{0,3},{1,2},{2,1},{3,0},{4,7},{5,6},{6,5},{7,4},{8,11},{9,10},{10,... | collective-permute-start | bytes 135176 | tf_op jit(solution)/shard_map/ppermute | solution.py:428
  25.8 2.4 %collective-permute-done.8.y = bf16[176,128]{1,0:T(8,128)(2,1)S(1)} collective-permute-done((bf16[176,128]{1,0:T(8,128)(2,1)S(1)}, bf16[176,128]{1,0:T(8,128)(2,1)S(1)}, u32[]{:S(2)}, u32[]{:S(2)}) %collective-permute-start.8) | collective-permute-done | bytes 45088 | tf_op jit(solution)/shard_map/ppermute | solution.py:428
  28.2 0.1 collective-permute-start.9
  28.4 3.4 %collective-permute-done.9.y = bf16[176,128]{1,0:T(8,128)(2,1)S(1)} collective-permute-done((bf16[176,128]{1,0:T(8,128)(2,1)S(1)}, bf16[176,128]{1,0:T(8,128)(2,1)S(1)}, u32[]{:S(2)}, u32[]{:S(2)}) %collective-permute-start.9) | collective-permute-done | bytes 45088 | tf_op jit(solution)/shard_map/ppermute | solution.py:428
  31.8 0.0 collective-permute-done.10.near_in
  31.8 1.2 %collective-permute-start.12 = (bf16[176,128]{1,0:T(8,128)(2,1)S(1)}, bf16[176,128]{1,0:T(8,128)(2,1)S(1)}, u32[]{:S(2)}, u32[]{:S(2)}) collective-permute-start(bf16[176,128]{1,0:T(8,128)(2,1)S(1)} %shard_map.85.x), channel_id=1, source_target_pairs={{0,17},{1,16},{2,19},{3,18},{4,21},{5,20},{6,23},{7,22},{8,25},{9,... | collective-permute-start | bytes 135176 | tf_op jit(solution)/shard_map/ppermute | solution.py:428
  33.1 0.1 collective-permute-start.14
  33.1 1.3 %collective-permute-start.15 = (bf16[4,64,128]{2,1,0:T(8,128)(2,1)S(1)}, bf16[4,64,128]{2,1,0:T(8,128)(2,1)S(1)}, u32[]{:S(2)}, u32[]{:S(2)}) collective-permute-start(bf16[4,64,128]{2,1,0:T(8,128)(2,1)S(1)} %get-tuple-element.107), channel_id=1, source_target_pairs={{1,2},{3,0},{2,1},{0,3},{5,6},{7,4},{6,5},{4,7},{9,10},{11,8},{10,... | collective-permute-start | bytes 196616 | tf_op jit(solution)/shard_map/ppermute | solution.py:422
  34.4 1.1 %shard_map.87 = bf16[128,256]{1,0:T(8,128)(2,1)} custom-call(bf16[2,8,64,128]{3,2,1,0:T(8,128)(2,1)S(1)} %get-tuple-element.101.h_ref, bf16[2,2,128,128]{3,2,1,0:T(8,128)(2,1)S(1)} %get-tuple-element.63.d_ref), custom_call_target="tpu_custom_call" | custom-call | flops 45298484 | bytes 458752 | tf_op jit(solution)/shard_map/pallas_call | solution.py:20
  35.5 1.9 %collective-permute-done.12.y = bf16[176,128]{1,0:T(8,128)(2,1)S(1)} collective-permute-done((bf16[176,128]{1,0:T(8,128)(2,1)S(1)}, bf16[176,128]{1,0:T(8,128)(2,1)S(1)}, u32[]{:S(2)}, u32[]{:S(2)}) %collective-permute-start.12) | collective-permute-done | bytes 45088 | tf_op jit(solution)/shard_map/ppermute | solution.py:428
  37.4 0.5 collective-permute-start.13
  37.9 0.4 shard_map.89.w_ref
  38.3 2.3 %shard_map.90.acc_ref = f32[2,8,64,128]{3,2,1,0:T(8,128)S(1)} custom-call(bf16[8,64,128]{2,1,0:T(8,128)(2,1)S(1)} %get-tuple-element.98.near, bf16[8,64,128]{2,1,0:T(8,128)(2,1)S(1)} %get-tuple-element.99.far, bf16[8,64,128]{2,1,0:T(8,128)(2,1)S(1)} %collective-permute-done.10.near_in, bf16[8,64,128]{2,1,0:T(8,128)(2,1)S(1)} %collective-permute-done.11.far_in, ...), custom_call_target="tpu_custom_call" | custom-call | flops 452984832 | bytes 1269760 | tf_op jit(solution)/shard_map/pallas_call | solution.py:20
  40.6 0.6 %collective-permute-done.13.other = bf16[176,128]{1,0:T(8,128)(2,1)S(1)} collective-permute-done((bf16[176,128]{1,0:T(8,128)(2,1)S(1)}, bf16[176,128]{1,0:T(8,128)(2,1)S(1)}, u32[]{:S(2)}, u32[]{:S(2)}) %collective-permute-start.13) | collective-permute-done | bytes 45088 | tf_op jit(solution)/shard_map/ppermute | solution.py:428
  41.2 0.0 collective-permute-done.14.near
  41.2 0.1 collective-permute-start.16
  41.3 1.3 %shard_map.93 = f32[1024,128]{1,0:T(8,128)} custom-call(bf16[4,64,128]{2,1,0:T(8,128)(2,1)S(1)} %collective-permute-done.14.near, bf16[4,64,128]{2,1,0:T(8,128)(2,1)S(1)} %collective-permute-done.15.far, f32[2,8,64,128]{3,2,1,0:T(8,128)S(1)} %shard_map.90.acc_ref, bf16[3,3,64,192]{3,2,1,0:T(8,128)(2,1)S(1)} %shard_map.89.w_ref), custom_call_target="tpu_custom_call" | custom-call | flops 45298484 | bytes 1400832 | tf_op jit(solution)/shard_map/pallas_call | solution.py:20
  42.6 3.3 %collective-permute-done.16.other = bf16[352,128]{1,0:T(8,128)(2,1)S(1)} collective-permute-done((bf16[352,128]{1,0:T(8,128)(2,1)S(1)}, bf16[352,128]{1,0:T(8,128)(2,1)S(1)}, u32[]{:S(2)}, u32[]{:S(2)}) %collective-permute-start.16) | collective-permute-done | bytes 90144 | tf_op jit(solution)/shard_map/ppermute | solution.py:428
  45.9 0.2 collective-permute-start.17
  46.1 1.3 %collective-permute-done.17.other = bf16[704,128]{1,0:T(8,128)(2,1)S(1)} collective-permute-done((bf16[704,128]{1,0:T(8,128)(2,1)S(1)}, bf16[704,128]{1,0:T(8,128)(2,1)S(1)}, u32[]{:S(2)}, u32[]{:S(2)}) %collective-permute-start.17) | collective-permute-done | bytes 180256 | tf_op jit(solution)/shard_map/ppermute | solution.py:428
  47.4 1.0 %shard_map.94 = (f32[3,3,64,192]{3,2,1,0:T(8,128)}, f32[2,2,128,128]{3,2,1,0:T(8,128)}) custom-call(bf16[704,128]{1,0:T(8,128)(2,1)S(1)} %shard_map.92.mine, bf16[704,128]{1,0:T(8,128)(2,1)S(1)} %collective-permute-done.17.other), custom_call_target="tpu_custom_call" | custom-call | bytes 1064960 | tf_op jit(solution)/shard_map/pallas_call | solution.py:20
  (16 shorter events, 0.2 us)
Async XLA Ops:
  0.6 1.0 %copy-start.1 = (bf16[64,2,8,128]{3,2,1,0:T(8,128)(2,1)S(1)}, bf16[64,2,8,128]{3,2,1,0:T(8,128)(2,1)}, u32[]{:S(2)}) copy-start(bf16[64,2,8,128]{3,2,1,0:T(8,128)(2,1)} %f_ref.1) | copy-start | bytes 786436
  1.6 8.4 %copy-start.2 = (bf16[2,2,128,128]{3,2,1,0:T(8,128)(2,1)S(1)}, bf16[2,2,128,128]{3,2,1,0:T(8,128)(2,1)}, u32[]{:S(2)}) copy-start(bf16[2,2,128,128]{3,2,1,0:T(8,128)(2,1)} %refs_1_.1) | copy-start | bytes 393220
  1.6 8.4 %copy-start.3 = (bf16[128,1,256]{2,0,1:T(8,128)(2,1)S(1)}, bf16[128,1,256]{2,0,1:T(8,128)(2,1)}, u32[]{:S(2)}) copy-start(bf16[128,1,256]{2,0,1:T(8,128)(2,1)} %param.7) | copy-start | bytes 196612
  1.8 11.4 %collective-permute-start = (bf16[8,64,128]{2,1,0:T(8,128)(2,1)S(1)}, bf16[8,64,128]{2,1,0:T(8,128)(2,1)S(1)}, u32[]{:S(2)}, u32[]{:S(2)}) collective-permute-start(bf16[8,64,128]{2,1,0:T(8,128)(2,1)S(1)} %get-tuple-element.60.near), channel_id=1, source_target_pairs={{0,4},{8,12},{16,20},{24,28},{4,0},{12,8},{20,16},{28,24},{1,5},{9... | collective-permute-start | bytes 393224 | tf_op jit(solution)/shard_map/ppermute | solution.py:422
  4.8 8.4 %collective-permute-start.1 = (bf16[8,64,128]{2,1,0:T(8,128)(2,1)S(1)}, bf16[8,64,128]{2,1,0:T(8,128)(2,1)S(1)}, u32[]{:S(2)}, u32[]{:S(2)}) collective-permute-start(bf16[8,64,128]{2,1,0:T(8,128)(2,1)S(1)} %get-tuple-element.61.far), channel_id=1, source_target_pairs={{4,8},{12,16},{20,24},{28,0},{8,4},{16,12},{24,20},{0,28},{5,9},{1... | collective-permute-start | bytes 393224 | tf_op jit(solution)/shard_map/ppermute | solution.py:422
  8.4 4.8 %collective-permute-start.2 = (bf16[2,64,128]{2,1,0:T(8,128)(2,1)S(1)}, bf16[2,64,128]{2,1,0:T(8,128)(2,1)S(1)}, u32[]{:S(2)}, u32[]{:S(2)}) collective-permute-start(bf16[2,64,128]{2,1,0:T(8,128)(2,1)S(1)} %get-tuple-element.66), channel_id=1, source_target_pairs={{0,1},{2,3},{1,0},{3,2},{4,5},{6,7},{5,4},{7,6},{8,9},{10,11},{9,8... | collective-permute-start | bytes 98312 | tf_op jit(solution)/shard_map/ppermute | solution.py:422
  8.4 4.9 %collective-permute-start.3 = (bf16[2,64,128]{2,1,0:T(8,128)(2,1)S(1)}, bf16[2,64,128]{2,1,0:T(8,128)(2,1)S(1)}, u32[]{:S(2)}, u32[]{:S(2)}) collective-permute-start(bf16[2,64,128]{2,1,0:T(8,128)(2,1)S(1)} %get-tuple-element.67), channel_id=1, source_target_pairs={{1,2},{3,0},{2,1},{0,3},{5,6},{7,4},{6,5},{4,7},{9,10},{11,8},{10,... | collective-permute-start | bytes 98312 | tf_op jit(solution)/shard_map/ppermute | solution.py:422
  10.0 1.0 %copy-start = (bf16[3,3,64,192]{3,2,1,0:T(8,128)(2,1)S(1)}, bf16[3,3,64,192]{3,2,1,0:T(8,128)(2,1)}, u32[]{:S(2)}) copy-start(bf16[3,3,64,192]{3,2,1,0:T(8,128)(2,1)} %refs_0_.1) | copy-start | bytes 663556
  13.3 3.6 %collective-permute-start.4 = (bf16[2,64,128]{2,1,0:T(8,128)(2,1)S(1)}, bf16[2,64,128]{2,1,0:T(8,128)(2,1)S(1)}, u32[]{:S(2)}, u32[]{:S(2)}) collective-permute-start(bf16[2,64,128]{2,1,0:T(8,128)(2,1)S(1)} %get-tuple-element.77), channel_id=1, source_target_pairs={{1,2},{3,0},{2,1},{0,3},{5,6},{7,4},{6,5},{4,7},{9,10},{11,8},{10,... | collective-permute-start | bytes 98312 | tf_op jit(solution)/shard_map/ppermute | solution.py:422
  13.7 3.1 %collective-permute-start.5 = (bf16[2,64,128]{2,1,0:T(8,128)(2,1)S(1)}, bf16[2,64,128]{2,1,0:T(8,128)(2,1)S(1)}, u32[]{:S(2)}, u32[]{:S(2)}) collective-permute-start(bf16[2,64,128]{2,1,0:T(8,128)(2,1)S(1)} %get-tuple-element.78), channel_id=1, source_target_pairs={{0,1},{2,3},{1,0},{3,2},{4,5},{6,7},{5,4},{7,6},{8,9},{10,11},{9,8... | collective-permute-start | bytes 98312 | tf_op jit(solution)/shard_map/ppermute | solution.py:422
  18.4 1.5 %collective-permute-start.6 = (bf16[704,128]{1,0:T(8,128)(2,1)S(1)}, bf16[704,128]{1,0:T(8,128)(2,1)S(1)}, u32[]{:S(2)}, u32[]{:S(2)}) collective-permute-start(bf16[704,128]{1,0:T(8,128)(2,1)S(1)} %get-tuple-element.91), channel_id=1, source_target_pairs={{0,1},{1,0},{2,3},{3,2},{4,5},{5,4},{6,7},{7,6},{8,9},{9,8},{10,11... | collective-permute-start | bytes 540680 | tf_op jit(solution)/shard_map/ppermute | solution.py:428
  20.0 4.7 %collective-permute-start.7 = (bf16[352,128]{1,0:T(8,128)(2,1)S(1)}, bf16[352,128]{1,0:T(8,128)(2,1)S(1)}, u32[]{:S(2)}, u32[]{:S(2)}) collective-permute-start(bf16[352,128]{1,0:T(8,128)(2,1)S(1)} %get-tuple-element.95), channel_id=1, source_target_pairs={{0,9},{1,8},{2,11},{3,10},{4,13},{5,12},{6,15},{7,14},{8,1},{9,0},... | collective-permute-start | bytes 270344 | tf_op jit(solution)/shard_map/ppermute | solution.py:428
  20.1 11.7 %collective-permute-start.10 = (bf16[8,64,128]{2,1,0:T(8,128)(2,1)S(1)}, bf16[8,64,128]{2,1,0:T(8,128)(2,1)S(1)}, u32[]{:S(2)}, u32[]{:S(2)}) collective-permute-start(bf16[8,64,128]{2,1,0:T(8,128)(2,1)S(1)} %get-tuple-element.98.near), channel_id=1, source_target_pairs={{0,4},{8,12},{16,20},{24,28},{4,0},{12,8},{20,16},{28,24},{1,5},{9... | collective-permute-start | bytes 393224 | tf_op jit(solution)/shard_map/ppermute | solution.py:422
  21.1 10.7 %collective-permute-start.11 = (bf16[8,64,128]{2,1,0:T(8,128)(2,1)S(1)}, bf16[8,64,128]{2,1,0:T(8,128)(2,1)S(1)}, u32[]{:S(2)}, u32[]{:S(2)}) collective-permute-start(bf16[8,64,128]{2,1,0:T(8,128)(2,1)S(1)} %get-tuple-element.99.far), channel_id=1, source_target_pairs={{4,8},{12,16},{20,24},{28,0},{8,4},{16,12},{24,20},{0,28},{5,9},{1... | collective-permute-start | bytes 393224 | tf_op jit(solution)/shard_map/ppermute | solution.py:422
  24.7 3.5 %collective-permute-start.8 = (bf16[176,128]{1,0:T(8,128)(2,1)S(1)}, bf16[176,128]{1,0:T(8,128)(2,1)S(1)}, u32[]{:S(2)}, u32[]{:S(2)}) collective-permute-start(bf16[176,128]{1,0:T(8,128)(2,1)S(1)} %get-tuple-element.97), channel_id=1, source_target_pairs={{0,3},{1,2},{2,1},{3,0},{4,7},{5,6},{6,5},{7,4},{8,11},{9,10},{10,... | collective-permute-start | bytes 135176 | tf_op jit(solution)/shard_map/ppermute | solution.py:428
  28.2 3.5 %collective-permute-start.9 = (bf16[176,128]{1,0:T(8,128)(2,1)S(1)}, bf16[176,128]{1,0:T(8,128)(2,1)S(1)}, u32[]{:S(2)}, u32[]{:S(2)}) collective-permute-start(bf16[176,128]{1,0:T(8,128)(2,1)S(1)} %shard_map.84.x), channel_id=1, source_target_pairs={{0,5},{1,4},{2,7},{3,6},{4,1},{5,0},{6,3},{7,2},{8,13},{9,12},{10,... | collective-permute-start | bytes 135176 | tf_op jit(solution)/shard_map/ppermute | solution.py:428
  31.8 5.6 %collective-permute-start.12 = (bf16[176,128]{1,0:T(8,128)(2,1)S(1)}, bf16[176,128]{1,0:T(8,128)(2,1)S(1)}, u32[]{:S(2)}, u32[]{:S(2)}) collective-permute-start(bf16[176,128]{1,0:T(8,128)(2,1)S(1)} %shard_map.85.x), channel_id=1, source_target_pairs={{0,17},{1,16},{2,19},{3,18},{4,21},{5,20},{6,23},{7,22},{8,25},{9,... | collective-permute-start | bytes 135176 | tf_op jit(solution)/shard_map/ppermute | solution.py:428
  33.1 8.1 %collective-permute-start.14 = (bf16[4,64,128]{2,1,0:T(8,128)(2,1)S(1)}, bf16[4,64,128]{2,1,0:T(8,128)(2,1)S(1)}, u32[]{:S(2)}, u32[]{:S(2)}) collective-permute-start(bf16[4,64,128]{2,1,0:T(8,128)(2,1)S(1)} %get-tuple-element.106), channel_id=1, source_target_pairs={{0,1},{2,3},{1,0},{3,2},{4,5},{6,7},{5,4},{7,6},{8,9},{10,11},{9,8... | collective-permute-start | bytes 196616 | tf_op jit(solution)/shard_map/ppermute | solution.py:422
  33.1 8.0 %collective-permute-start.15 = (bf16[4,64,128]{2,1,0:T(8,128)(2,1)S(1)}, bf16[4,64,128]{2,1,0:T(8,128)(2,1)S(1)}, u32[]{:S(2)}, u32[]{:S(2)}) collective-permute-start(bf16[4,64,128]{2,1,0:T(8,128)(2,1)S(1)} %get-tuple-element.107), channel_id=1, source_target_pairs={{1,2},{3,0},{2,1},{0,3},{5,6},{7,4},{6,5},{4,7},{9,10},{11,8},{10,... | collective-permute-start | bytes 196616 | tf_op jit(solution)/shard_map/ppermute | solution.py:422
  37.4 3.7 %collective-permute-start.13 = (bf16[176,128]{1,0:T(8,128)(2,1)S(1)}, bf16[176,128]{1,0:T(8,128)(2,1)S(1)}, u32[]{:S(2)}, u32[]{:S(2)}) collective-permute-start(bf16[176,128]{1,0:T(8,128)(2,1)S(1)} %shard_map.86.mine), channel_id=1, source_target_pairs={{0,3},{1,2},{2,1},{3,0},{4,7},{5,6},{6,5},{7,4},{8,11},{9,10},{10,... | collective-permute-start | bytes 135176 | tf_op jit(solution)/shard_map/ppermute | solution.py:428
  41.2 4.7 %collective-permute-start.16 = (bf16[352,128]{1,0:T(8,128)(2,1)S(1)}, bf16[352,128]{1,0:T(8,128)(2,1)S(1)}, u32[]{:S(2)}, u32[]{:S(2)}) collective-permute-start(bf16[352,128]{1,0:T(8,128)(2,1)S(1)} %shard_map.88.mine), channel_id=1, source_target_pairs={{0,9},{1,8},{2,11},{3,10},{4,13},{5,12},{6,15},{7,14},{8,1},{9,0},... | collective-permute-start | bytes 270344 | tf_op jit(solution)/shard_map/ppermute | solution.py:428
  45.9 1.5 %collective-permute-start.17 = (bf16[704,128]{1,0:T(8,128)(2,1)S(1)}, bf16[704,128]{1,0:T(8,128)(2,1)S(1)}, u32[]{:S(2)}, u32[]{:S(2)}) collective-permute-start(bf16[704,128]{1,0:T(8,128)(2,1)S(1)} %shard_map.92.mine), channel_id=1, source_target_pairs={{0,1},{1,0},{2,3},{3,2},{4,5},{5,4},{6,7},{7,6},{8,9},{9,8},{10,11... | collective-permute-start | bytes 540680 | tf_op jit(solution)/shard_map/ppermute | solution.py:428

commit v26 on v25

--- a/solution.py
+++ b/solution.py
@@ -507,7 +507,8 @@
     shard = ((rows // 8, 128), BF16)
     (sums,) = call(add_kernel, [shard], [], 0, (keep, flip(send, "gy", 2)))
     (sums,) = call(add_kernel, [shard], [], 0, (sums, flip(sums, "gz", 1)))
-    sums, outside = tied(sums, near_in, far_in)
+    sums, (near_in, far_in, weight_bwd) = tied(sums, near_in, far_in, weight_bwd)
+    outside = (near_in, far_in)
     sends = call(edges_kernel, [edge, edge], [], 0, (*gates, *outside))
     beside = swapped(*sends, "gy")
     (acc,) = call(

time: 48.6 us -> 48.6 us (level)
  no operation moved by 1% of the time
where the time goes in v26:
time: 48.6 us; the launch traced here: 48.4 us
  starting transfers between devices  17.4 us (36%)
  waiting for transfers between devices  16.8 us (35%)
  Pallas kernels  11.5 us (24%)
  local copies, waits for them, and re-layouts  1.91 us (4%)
  between operations  0.83 us (2%)
    ppermute x8, waiting for transfers between devices, flip(): lax.ppermute(cells, ('gz', 'gy'), [(i, i ^ mask) for i in range(lax.axis_...  15.2 us
    ppermute x10, starting transfers between devices, swap(): return lax.ppermute(cells, axis, pairs + [(b, a) for a, b in pairs])  13.9 us
    pallas_call x19, Pallas kernels, call(): pl.pallas_call(kernel, out_shape=[jax.ShapeDtypeStruct(s, d) for s, d in...  11.1 us
    ppermute x8, starting transfers between devices, flip(): lax.ppermute(cells, ('gz', 'gy'), [(i, i ^ mask) for i in range(lax.axis_...  3.46 us
    unnamed x8, local copies, waits for them, and re-layouts  1.91 us
    ppermute x10, waiting for transfers between devices, swap(): return lax.ppermute(cells, axis, pairs + [(b, a) for a, b in pairs])  1.54 us
  transfers between devices with their start and end apart: 18, of which 9 were waited for; matrix products, arithmetic and copies ran while one was open for 0% of the time, Pallas kernels for 18%

profile of v26, /device:TPU:0, one launch (start us, length us, event | category | flops | bytes accessed | tf_op | source)
XLA Modules:
  0.0 48.4 jit_solution(6336727499400244987)
XLA Ops:
  0.6 0.9 %copy-done.1 = bf16[64,2,8,128]{3,2,1,0:T(8,128)(2,1)S(1)} copy-done((bf16[64,2,8,128]{3,2,1,0:T(8,128)(2,1)S(1)}, bf16[64,2,8,128]{3,2,1,0:T(8,128)(2,1)}, u32[]{:S(2)}) %copy-start.1) | copy-done | bytes 262168
  1.6 0.2 shard_map.75
  1.8 3.0 %collective-permute-start = (bf16[8,64,128]{2,1,0:T(8,128)(2,1)S(1)}, bf16[8,64,128]{2,1,0:T(8,128)(2,1)S(1)}, u32[]{:S(2)}, u32[]{:S(2)}) collective-permute-start(bf16[8,64,128]{2,1,0:T(8,128)(2,1)S(1)} %get-tuple-element.61.near), channel_id=1, source_target_pairs={{0,4},{8,12},{16,20},{24,28},{4,0},{12,8},{20,16},{28,24},{1,5},{9... | collective-permute-start | bytes 393224 | tf_op jit(solution)/shard_map/ppermute | solution.py:422
  4.8 3.5 %collective-permute-start.1 = (bf16[8,64,128]{2,1,0:T(8,128)(2,1)S(1)}, bf16[8,64,128]{2,1,0:T(8,128)(2,1)S(1)}, u32[]{:S(2)}, u32[]{:S(2)}) collective-permute-start(bf16[8,64,128]{2,1,0:T(8,128)(2,1)S(1)} %get-tuple-element.62.far), channel_id=1, source_target_pairs={{4,8},{12,16},{20,24},{28,0},{8,4},{16,12},{24,20},{0,28},{5,9},{1... | collective-permute-start | bytes 393224 | tf_op jit(solution)/shard_map/ppermute | solution.py:422
  8.4 0.0 collective-permute-start.2
  8.4 1.6 %collective-permute-start.3 = (bf16[2,64,128]{2,1,0:T(8,128)(2,1)S(1)}, bf16[2,64,128]{2,1,0:T(8,128)(2,1)S(1)}, u32[]{:S(2)}, u32[]{:S(2)}) collective-permute-start(bf16[2,64,128]{2,1,0:T(8,128)(2,1)S(1)} %get-tuple-element.68), channel_id=1, source_target_pairs={{1,2},{3,0},{2,1},{0,3},{5,6},{7,4},{6,5},{4,7},{9,10},{11,8},{10,... | collective-permute-start | bytes 98312 | tf_op jit(solution)/shard_map/ppermute | solution.py:422
  10.0 1.0 %copy-done = bf16[3,3,64,192]{3,2,1,0:T(8,128)(2,1)S(1)} copy-done((bf16[3,3,64,192]{3,2,1,0:T(8,128)(2,1)S(1)}, bf16[3,3,64,192]{3,2,1,0:T(8,128)(2,1)}, u32[]{:S(2)}) %copy-start) | copy-done | bytes 221208
  11.0 0.3 shard_map.76
  11.3 1.9 %shard_map.77 = (bf16[2,10,192,128]{3,2,1,0:T(8,128)(2,1)S(1)}, f32[2,8,64,128]{3,2,1,0:T(8,128)S(1)}, f32[2,8,64,128]{3,2,1,0:T(8,128)S(1)}) custom-call(bf16[8,64,128]{2,1,0:T(8,128)(2,1)S(1)} %get-tuple-element.61.near, bf16[8,64,128]{2,1,0:T(8,128)(2,1)S(1)} %get-tuple-element.62.far, bf16[3,3,64,192]{3,2,1,0:T(8,128)(2,1)S(1)} %get-tuple-element.63.w_ref, ...), custom_call_target="tpu_custom_call" | custom-call | flops 301989888 | bytes 2711552 | tf_op jit(solution)/shard_map/pallas_call | solution.py:20
  13.2 0.0 collective-permute-done.2.near_row
  13.2 0.0 collective-permute-done.3.far_row
  13.2 0.0 collective-permute-done.near.near_in
  13.3 0.0 collective-permute-done.1.far.far_in
  13.3 0.4 collective-permute-start.4
  13.7 0.5 collective-permute-start.5
  14.2 1.1 %shard_map.78 = (bf16[2,10,192,128]{3,2,1,0:T(8,128)(2,1)S(1)}, bf16[2,2,192,128]{3,2,1,0:T(8,128)(2,1)S(1)}, f32[2,2,64,128]{3,2,1,0:T(8,128)S(1)}, bf16[8,64,1...) custom-call(bf16[8,64,128]{2,1,0:T(8,128)(2,1)S(1)} %collective-permute-done.near.near_in,, ...), custom_call_target="tpu_custom_call" | custom-call | flops 150994944 | bytes 3432448 | tf_op jit(solution)/shard_map/pallas_call | solution.py:20
  15.3 1.5 %collective-permute-done.4.far = bf16[2,64,128]{2,1,0:T(8,128)(2,1)S(1)} collective-permute-done((bf16[2,64,128]{2,1,0:T(8,128)(2,1)S(1)}, bf16[2,64,128]{2,1,0:T(8,128)(2,1)S(1)}, u32[]{:S(2)}, u32[]{:S(2)}) %collective-permute-start.4) | collective-permute-done | bytes 32800 | tf_op jit(solution)/shard_map/ppermute | solution.py:422
  16.9 0.0 collective-permute-done.5.near
  16.9 0.3 shard_map.80
  17.2 1.2 %shard_map.81 = (f32[704,128]{1,0:T(8,128)S(1)}, bf16[704,128]{1,0:T(8,128)(2,1)S(1)}) custom-call(bf16[2,10,192,128]{3,2,1,0:T(8,128)(2,1)S(1)} %get-tuple-element.66.inner, bf16[2,10,192,128]{3,2,1,0:T(8,128)(2,1)S(1)} %get-tuple-element.76.outer, bf16[2,2,192,128]{3,2,1,0:T(8,128)(2,1)S(1)} %get-tuple-element.77.own_edges, ...), custom_call_target="tpu_custom_call" | custom-call | flops 452984832 | bytes 3489792 | tf_op jit(solution)/shard_map/pallas_call | solution.py:20
  18.4 0.2 collective-permute-start.6
  18.6 1.3 %collective-permute-done.6.other = bf16[704,128]{1,0:T(8,128)(2,1)S(1)} collective-permute-done((bf16[704,128]{1,0:T(8,128)(2,1)S(1)}, bf16[704,128]{1,0:T(8,128)(2,1)S(1)}, u32[]{:S(2)}, u32[]{:S(2)}) %collective-permute-start.6) | collective-permute-done | bytes 180256 | tf_op jit(solution)/shard_map/ppermute | solution.py:428
  19.9 0.1 shard_map.82
  20.0 0.1 collective-permute-start.7
  20.1 1.0 %collective-permute-start.10 = (bf16[8,64,128]{2,1,0:T(8,128)(2,1)S(1)}, bf16[8,64,128]{2,1,0:T(8,128)(2,1)S(1)}, u32[]{:S(2)}, u32[]{:S(2)}) collective-permute-start(bf16[8,64,128]{2,1,0:T(8,128)(2,1)S(1)} %get-tuple-element.99.near), channel_id=1, source_target_pairs={{0,4},{8,12},{16,20},{24,28},{4,0},{12,8},{20,16},{28,24},{1,5},{9... | collective-permute-start | bytes 393224 | tf_op jit(solution)/shard_map/ppermute | solution.py:422
  21.1 2.4 %collective-permute-start.11 = (bf16[8,64,128]{2,1,0:T(8,128)(2,1)S(1)}, bf16[8,64,128]{2,1,0:T(8,128)(2,1)S(1)}, u32[]{:S(2)}, u32[]{:S(2)}) collective-permute-start(bf16[8,64,128]{2,1,0:T(8,128)(2,1)S(1)} %get-tuple-element.100.far), channel_id=1, source_target_pairs={{4,8},{12,16},{20,24},{28,0},{8,4},{16,12},{24,20},{0,28},{5,9},{1... | collective-permute-start | bytes 393224 | tf_op jit(solution)/shard_map/ppermute | solution.py:422
  23.6 1.1 %collective-permute-done.7.other = bf16[352,128]{1,0:T(8,128)(2,1)S(1)} collective-permute-done((bf16[352,128]{1,0:T(8,128)(2,1)S(1)}, bf16[352,128]{1,0:T(8,128)(2,1)S(1)}, u32[]{:S(2)}, u32[]{:S(2)}) %collective-permute-start.7) | collective-permute-done | bytes 90144 | tf_op jit(solution)/shard_map/ppermute | solution.py:428
  24.7 1.1 %collective-permute-start.8 = (bf16[176,128]{1,0:T(8,128)(2,1)S(1)}, bf16[176,128]{1,0:T(8,128)(2,1)S(1)}, u32[]{:S(2)}, u32[]{:S(2)}) collective-permute-start(bf16[176,128]{1,0:T(8,128)(2,1)S(1)} %get-tuple-element.98), channel_id=1, source_target_pairs={{0,3},{1,2},{2,1},{3,0},{4,7},{5,6},{6,5},{7,4},{8,11},{9,10},{10,... | collective-permute-start | bytes 135176 | tf_op jit(solution)/shard_map/ppermute | solution.py:428
  25.8 2.4 %collective-permute-done.8.y = bf16[176,128]{1,0:T(8,128)(2,1)S(1)} collective-permute-done((bf16[176,128]{1,0:T(8,128)(2,1)S(1)}, bf16[176,128]{1,0:T(8,128)(2,1)S(1)}, u32[]{:S(2)}, u32[]{:S(2)}) %collective-permute-start.8) | collective-permute-done | bytes 45088 | tf_op jit(solution)/shard_map/ppermute | solution.py:428
  28.2 0.1 collective-permute-start.9
  28.4 0.4 shard_map.86.w_ref
  28.8 3.0 %collective-permute-done.9.y = bf16[176,128]{1,0:T(8,128)(2,1)S(1)} collective-permute-done((bf16[176,128]{1,0:T(8,128)(2,1)S(1)}, bf16[176,128]{1,0:T(8,128)(2,1)S(1)}, u32[]{:S(2)}, u32[]{:S(2)}) %collective-permute-start.9) | collective-permute-done | bytes 45088 | tf_op jit(solution)/shard_map/ppermute | solution.py:428
  31.8 0.0 collective-permute-done.10.near_in
  31.8 1.2 %collective-permute-start.12 = (bf16[176,128]{1,0:T(8,128)(2,1)S(1)}, bf16[176,128]{1,0:T(8,128)(2,1)S(1)}, u32[]{:S(2)}, u32[]{:S(2)}) collective-permute-start(bf16[176,128]{1,0:T(8,128)(2,1)S(1)} %shard_map.85.x), channel_id=1, source_target_pairs={{0,17},{1,16},{2,19},{3,18},{4,21},{5,20},{6,23},{7,22},{8,25},{9,... | collective-permute-start | bytes 135176 | tf_op jit(solution)/shard_map/ppermute | solution.py:428
  33.1 0.1 collective-permute-start.14
  33.1 1.3 %collective-permute-start.15 = (bf16[4,64,128]{2,1,0:T(8,128)(2,1)S(1)}, bf16[4,64,128]{2,1,0:T(8,128)(2,1)S(1)}, u32[]{:S(2)}, u32[]{:S(2)}) collective-permute-start(bf16[4,64,128]{2,1,0:T(8,128)(2,1)S(1)} %get-tuple-element.109), channel_id=1, source_target_pairs={{1,2},{3,0},{2,1},{0,3},{5,6},{7,4},{6,5},{4,7},{9,10},{11,8},{10,... | collective-permute-start | bytes 196616 | tf_op jit(solution)/shard_map/ppermute | solution.py:422
  34.4 1.1 %shard_map.88 = bf16[128,256]{1,0:T(8,128)(2,1)} custom-call(bf16[2,8,64,128]{3,2,1,0:T(8,128)(2,1)S(1)} %get-tuple-element.102.h_ref, bf16[2,2,128,128]{3,2,1,0:T(8,128)(2,1)S(1)} %get-tuple-element.64.d_ref), custom_call_target="tpu_custom_call" | custom-call | flops 45298484 | bytes 458752 | tf_op jit(solution)/shard_map/pallas_call | solution.py:20
  35.5 1.9 %collective-permute-done.12.y = bf16[176,128]{1,0:T(8,128)(2,1)S(1)} collective-permute-done((bf16[176,128]{1,0:T(8,128)(2,1)S(1)}, bf16[176,128]{1,0:T(8,128)(2,1)S(1)}, u32[]{:S(2)}, u32[]{:S(2)}) %collective-permute-start.12) | collective-permute-done | bytes 45088 | tf_op jit(solution)/shard_map/ppermute | solution.py:428
  37.4 0.5 collective-permute-start.13
  37.9 2.3 %shard_map.90.acc_ref = f32[2,8,64,128]{3,2,1,0:T(8,128)S(1)} custom-call(bf16[8,64,128]{2,1,0:T(8,128)(2,1)S(1)} %get-tuple-element.99.near, bf16[8,64,128]{2,1,0:T(8,128)(2,1)S(1)} %get-tuple-element.100.far, bf16[8,64,128]{2,1,0:T(8,128)(2,1)S(1)} %collective-permute-done.10.near_in, bf16[8,64,128]{2,1,0:T(8,128)(2,1)S(1)} %collective-permute-done.11.far_in, ...), custom_call_target="tpu_custom_call" | custom-call | flops 452984832 | bytes 1269760 | tf_op jit(solution)/shard_map/pallas_call | solution.py:20
  40.2 1.0 %collective-permute-done.13.other = bf16[176,128]{1,0:T(8,128)(2,1)S(1)} collective-permute-done((bf16[176,128]{1,0:T(8,128)(2,1)S(1)}, bf16[176,128]{1,0:T(8,128)(2,1)S(1)}, u32[]{:S(2)}, u32[]{:S(2)}) %collective-permute-start.13) | collective-permute-done | bytes 45088 | tf_op jit(solution)/shard_map/ppermute | solution.py:428
  41.2 0.0 collective-permute-done.14.near
  41.2 0.1 collective-permute-start.16
  41.3 1.3 %shard_map.93 = f32[1024,128]{1,0:T(8,128)} custom-call(bf16[4,64,128]{2,1,0:T(8,128)(2,1)S(1)} %collective-permute-done.14.near, bf16[4,64,128]{2,1,0:T(8,128)(2,1)S(1)} %collective-permute-done.15.far, f32[2,8,64,128]{3,2,1,0:T(8,128)S(1)} %shard_map.90.acc_ref, bf16[3,3,64,192]{3,2,1,0:T(8,128)(2,1)S(1)} %shard_map.86.w_ref), custom_call_target="tpu_custom_call" | custom-call | flops 45298484 | bytes 1400832 | tf_op jit(solution)/shard_map/pallas_call | solution.py:20
  42.6 3.3 %collective-permute-done.16.other = bf16[352,128]{1,0:T(8,128)(2,1)S(1)} collective-permute-done((bf16[352,128]{1,0:T(8,128)(2,1)S(1)}, bf16[352,128]{1,0:T(8,128)(2,1)S(1)}, u32[]{:S(2)}, u32[]{:S(2)}) %collective-permute-start.16) | collective-permute-done | bytes 90144 | tf_op jit(solution)/shard_map/ppermute | solution.py:428
  45.9 0.2 collective-permute-start.17
  46.1 1.3 %collective-permute-done.17.other = bf16[704,128]{1,0:T(8,128)(2,1)S(1)} collective-permute-done((bf16[704,128]{1,0:T(8,128)(2,1)S(1)}, bf16[704,128]{1,0:T(8,128)(2,1)S(1)}, u32[]{:S(2)}, u32[]{:S(2)}) %collective-permute-start.17) | collective-permute-done | bytes 180256 | tf_op jit(solution)/shard_map/ppermute | solution.py:428
  47.4 1.0 %shard_map.94 = (f32[3,3,64,192]{3,2,1,0:T(8,128)}, f32[2,2,128,128]{3,2,1,0:T(8,128)}) custom-call(bf16[704,128]{1,0:T(8,128)(2,1)S(1)} %shard_map.92.mine, bf16[704,128]{1,0:T(8,128)(2,1)S(1)} %collective-permute-done.17.other), custom_call_target="tpu_custom_call" | custom-call | bytes 1064960 | tf_op jit(solution)/shard_map/pallas_call | solution.py:20
  (16 shorter events, 0.2 us)
Async XLA Ops:
  0.6 1.0 %copy-start.1 = (bf16[64,2,8,128]{3,2,1,0:T(8,128)(2,1)S(1)}, bf16[64,2,8,128]{3,2,1,0:T(8,128)(2,1)}, u32[]{:S(2)}) copy-start(bf16[64,2,8,128]{3,2,1,0:T(8,128)(2,1)} %f_ref.1) | copy-start | bytes 786436
  1.6 8.4 %copy-start.2 = (bf16[2,2,128,128]{3,2,1,0:T(8,128)(2,1)S(1)}, bf16[2,2,128,128]{3,2,1,0:T(8,128)(2,1)}, u32[]{:S(2)}) copy-start(bf16[2,2,128,128]{3,2,1,0:T(8,128)(2,1)} %refs_1_.1) | copy-start | bytes 393220
  1.6 8.4 %copy-start.3 = (bf16[128,1,256]{2,0,1:T(8,128)(2,1)S(1)}, bf16[128,1,256]{2,0,1:T(8,128)(2,1)}, u32[]{:S(2)}) copy-start(bf16[128,1,256]{2,0,1:T(8,128)(2,1)} %param.7) | copy-start | bytes 196612
  1.8 11.4 %collective-permute-start = (bf16[8,64,128]{2,1,0:T(8,128)(2,1)S(1)}, bf16[8,64,128]{2,1,0:T(8,128)(2,1)S(1)}, u32[]{:S(2)}, u32[]{:S(2)}) collective-permute-start(bf16[8,64,128]{2,1,0:T(8,128)(2,1)S(1)} %get-tuple-element.61.near), channel_id=1, source_target_pairs={{0,4},{8,12},{16,20},{24,28},{4,0},{12,8},{20,16},{28,24},{1,5},{9... | collective-permute-start | bytes 393224 | tf_op jit(solution)/shard_map/ppermute | solution.py:422
  4.8 8.4 %collective-permute-start.1 = (bf16[8,64,128]{2,1,0:T(8,128)(2,1)S(1)}, bf16[8,64,128]{2,1,0:T(8,128)(2,1)S(1)}, u32[]{:S(2)}, u32[]{:S(2)}) collective-permute-start(bf16[8,64,128]{2,1,0:T(8,128)(2,1)S(1)} %get-tuple-element.62.far), channel_id=1, source_target_pairs={{4,8},{12,16},{20,24},{28,0},{8,4},{16,12},{24,20},{0,28},{5,9},{1... | collective-permute-start | bytes 393224 | tf_op jit(solution)/shard_map/ppermute | solution.py:422
  8.4 4.8 %collective-permute-start.2 = (bf16[2,64,128]{2,1,0:T(8,128)(2,1)S(1)}, bf16[2,64,128]{2,1,0:T(8,128)(2,1)S(1)}, u32[]{:S(2)}, u32[]{:S(2)}) collective-permute-start(bf16[2,64,128]{2,1,0:T(8,128)(2,1)S(1)} %get-tuple-element.67), channel_id=1, source_target_pairs={{0,1},{2,3},{1,0},{3,2},{4,5},{6,7},{5,4},{7,6},{8,9},{10,11},{9,8... | collective-permute-start | bytes 98312 | tf_op jit(solution)/shard_map/ppermute | solution.py:422
  8.4 4.9 %collective-permute-start.3 = (bf16[2,64,128]{2,1,0:T(8,128)(2,1)S(1)}, bf16[2,64,128]{2,1,0:T(8,128)(2,1)S(1)}, u32[]{:S(2)}, u32[]{:S(2)}) collective-permute-start(bf16[2,64,128]{2,1,0:T(8,128)(2,1)S(1)} %get-tuple-element.68), channel_id=1, source_target_pairs={{1,2},{3,0},{2,1},{0,3},{5,6},{7,4},{6,5},{4,7},{9,10},{11,8},{10,... | collective-permute-start | bytes 98312 | tf_op jit(solution)/shard_map/ppermute | solution.py:422
  10.0 1.0 %copy-start = (bf16[3,3,64,192]{3,2,1,0:T(8,128)(2,1)S(1)}, bf16[3,3,64,192]{3,2,1,0:T(8,128)(2,1)}, u32[]{:S(2)}) copy-start(bf16[3,3,64,192]{3,2,1,0:T(8,128)(2,1)} %refs_0_.1) | copy-start | bytes 663556
  13.3 3.6 %collective-permute-start.4 = (bf16[2,64,128]{2,1,0:T(8,128)(2,1)S(1)}, bf16[2,64,128]{2,1,0:T(8,128)(2,1)S(1)}, u32[]{:S(2)}, u32[]{:S(2)}) collective-permute-start(bf16[2,64,128]{2,1,0:T(8,128)(2,1)S(1)} %get-tuple-element.78), channel_id=1, source_target_pairs={{1,2},{3,0},{2,1},{0,3},{5,6},{7,4},{6,5},{4,7},{9,10},{11,8},{10,... | collective-permute-start | bytes 98312 | tf_op jit(solution)/shard_map/ppermute | solution.py:422
  13.7 3.1 %collective-permute-start.5 = (bf16[2,64,128]{2,1,0:T(8,128)(2,1)S(1)}, bf16[2,64,128]{2,1,0:T(8,128)(2,1)S(1)}, u32[]{:S(2)}, u32[]{:S(2)}) collective-permute-start(bf16[2,64,128]{2,1,0:T(8,128)(2,1)S(1)} %get-tuple-element.79), channel_id=1, source_target_pairs={{0,1},{2,3},{1,0},{3,2},{4,5},{6,7},{5,4},{7,6},{8,9},{10,11},{9,8... | collective-permute-start | bytes 98312 | tf_op jit(solution)/shard_map/ppermute | solution.py:422
  18.4 1.5 %collective-permute-start.6 = (bf16[704,128]{1,0:T(8,128)(2,1)S(1)}, bf16[704,128]{1,0:T(8,128)(2,1)S(1)}, u32[]{:S(2)}, u32[]{:S(2)}) collective-permute-start(bf16[704,128]{1,0:T(8,128)(2,1)S(1)} %get-tuple-element.92), channel_id=1, source_target_pairs={{0,1},{1,0},{2,3},{3,2},{4,5},{5,4},{6,7},{7,6},{8,9},{9,8},{10,11... | collective-permute-start | bytes 540680 | tf_op jit(solution)/shard_map/ppermute | solution.py:428
  20.0 4.7 %collective-permute-start.7 = (bf16[352,128]{1,0:T(8,128)(2,1)S(1)}, bf16[352,128]{1,0:T(8,128)(2,1)S(1)}, u32[]{:S(2)}, u32[]{:S(2)}) collective-permute-start(bf16[352,128]{1,0:T(8,128)(2,1)S(1)} %get-tuple-element.96), channel_id=1, source_target_pairs={{0,9},{1,8},{2,11},{3,10},{4,13},{5,12},{6,15},{7,14},{8,1},{9,0},... | collective-permute-start | bytes 270344 | tf_op jit(solution)/shard_map/ppermute | solution.py:428
  20.1 11.7 %collective-permute-start.10 = (bf16[8,64,128]{2,1,0:T(8,128)(2,1)S(1)}, bf16[8,64,128]{2,1,0:T(8,128)(2,1)S(1)}, u32[]{:S(2)}, u32[]{:S(2)}) collective-permute-start(bf16[8,64,128]{2,1,0:T(8,128)(2,1)S(1)} %get-tuple-element.99.near), channel_id=1, source_target_pairs={{0,4},{8,12},{16,20},{24,28},{4,0},{12,8},{20,16},{28,24},{1,5},{9... | collective-permute-start | bytes 393224 | tf_op jit(solution)/shard_map/ppermute | solution.py:422
  21.1 10.7 %collective-permute-start.11 = (bf16[8,64,128]{2,1,0:T(8,128)(2,1)S(1)}, bf16[8,64,128]{2,1,0:T(8,128)(2,1)S(1)}, u32[]{:S(2)}, u32[]{:S(2)}) collective-permute-start(bf16[8,64,128]{2,1,0:T(8,128)(2,1)S(1)} %get-tuple-element.100.far), channel_id=1, source_target_pairs={{4,8},{12,16},{20,24},{28,0},{8,4},{16,12},{24,20},{0,28},{5,9},{1... | collective-permute-start | bytes 393224 | tf_op jit(solution)/shard_map/ppermute | solution.py:422
  24.7 3.5 %collective-permute-start.8 = (bf16[176,128]{1,0:T(8,128)(2,1)S(1)}, bf16[176,128]{1,0:T(8,128)(2,1)S(1)}, u32[]{:S(2)}, u32[]{:S(2)}) collective-permute-start(bf16[176,128]{1,0:T(8,128)(2,1)S(1)} %get-tuple-element.98), channel_id=1, source_target_pairs={{0,3},{1,2},{2,1},{3,0},{4,7},{5,6},{6,5},{7,4},{8,11},{9,10},{10,... | collective-permute-start | bytes 135176 | tf_op jit(solution)/shard_map/ppermute | solution.py:428
  28.2 3.5 %collective-permute-start.9 = (bf16[176,128]{1,0:T(8,128)(2,1)S(1)}, bf16[176,128]{1,0:T(8,128)(2,1)S(1)}, u32[]{:S(2)}, u32[]{:S(2)}) collective-permute-start(bf16[176,128]{1,0:T(8,128)(2,1)S(1)} %shard_map.84.x), channel_id=1, source_target_pairs={{0,5},{1,4},{2,7},{3,6},{4,1},{5,0},{6,3},{7,2},{8,13},{9,12},{10,... | collective-permute-start | bytes 135176 | tf_op jit(solution)/shard_map/ppermute | solution.py:428
  31.8 5.6 %collective-permute-start.12 = (bf16[176,128]{1,0:T(8,128)(2,1)S(1)}, bf16[176,128]{1,0:T(8,128)(2,1)S(1)}, u32[]{:S(2)}, u32[]{:S(2)}) collective-permute-start(bf16[176,128]{1,0:T(8,128)(2,1)S(1)} %shard_map.85.x), channel_id=1, source_target_pairs={{0,17},{1,16},{2,19},{3,18},{4,21},{5,20},{6,23},{7,22},{8,25},{9,... | collective-permute-start | bytes 135176 | tf_op jit(solution)/shard_map/ppermute | solution.py:428
  33.1 8.1 %collective-permute-start.14 = (bf16[4,64,128]{2,1,0:T(8,128)(2,1)S(1)}, bf16[4,64,128]{2,1,0:T(8,128)(2,1)S(1)}, u32[]{:S(2)}, u32[]{:S(2)}) collective-permute-start(bf16[4,64,128]{2,1,0:T(8,128)(2,1)S(1)} %get-tuple-element.108), channel_id=1, source_target_pairs={{0,1},{2,3},{1,0},{3,2},{4,5},{6,7},{5,4},{7,6},{8,9},{10,11},{9,8... | collective-permute-start | bytes 196616 | tf_op jit(solution)/shard_map/ppermute | solution.py:422
  33.1 8.0 %collective-permute-start.15 = (bf16[4,64,128]{2,1,0:T(8,128)(2,1)S(1)}, bf16[4,64,128]{2,1,0:T(8,128)(2,1)S(1)}, u32[]{:S(2)}, u32[]{:S(2)}) collective-permute-start(bf16[4,64,128]{2,1,0:T(8,128)(2,1)S(1)} %get-tuple-element.109), channel_id=1, source_target_pairs={{1,2},{3,0},{2,1},{0,3},{5,6},{7,4},{6,5},{4,7},{9,10},{11,8},{10,... | collective-permute-start | bytes 196616 | tf_op jit(solution)/shard_map/ppermute | solution.py:422
  37.4 3.7 %collective-permute-start.13 = (bf16[176,128]{1,0:T(8,128)(2,1)S(1)}, bf16[176,128]{1,0:T(8,128)(2,1)S(1)}, u32[]{:S(2)}, u32[]{:S(2)}) collective-permute-start(bf16[176,128]{1,0:T(8,128)(2,1)S(1)} %shard_map.87.mine), channel_id=1, source_target_pairs={{0,3},{1,2},{2,1},{3,0},{4,7},{5,6},{6,5},{7,4},{8,11},{9,10},{10,... | collective-permute-start | bytes 135176 | tf_op jit(solution)/shard_map/ppermute | solution.py:428
  41.2 4.7 %collective-permute-start.16 = (bf16[352,128]{1,0:T(8,128)(2,1)S(1)}, bf16[352,128]{1,0:T(8,128)(2,1)S(1)}, u32[]{:S(2)}, u32[]{:S(2)}) collective-permute-start(bf16[352,128]{1,0:T(8,128)(2,1)S(1)} %shard_map.89.mine), channel_id=1, source_target_pairs={{0,9},{1,8},{2,11},{3,10},{4,13},{5,12},{6,15},{7,14},{8,1},{9,0},... | collective-permute-start | bytes 270344 | tf_op jit(solution)/shard_map/ppermute | solution.py:428
  45.9 1.5 %collective-permute-start.17 = (bf16[704,128]{1,0:T(8,128)(2,1)S(1)}, bf16[704,128]{1,0:T(8,128)(2,1)S(1)}, u32[]{:S(2)}, u32[]{:S(2)}) collective-permute-start(bf16[704,128]{1,0:T(8,128)(2,1)S(1)} %shard_map.92.mine), channel_id=1, source_target_pairs={{0,1},{1,0},{2,3},{3,2},{4,5},{5,4},{6,7},{7,6},{8,9},{9,8},{10,11... | collective-permute-start | bytes 540680 | tf_op jit(solution)/shard_map/ppermute | solution.py:428

commit v27 on v25

--- a/solution.py
+++ b/solution.py
@@ -256,6 +256,11 @@
             h_ref[z, y] = h_in[z, y]
 
 
+def tap_row(tap, rows, channels):
+    size = 3 * channels // 2
+    return tap * size if tap < 7 else 7 * size + 8 * channels + (tap - 7) * size
+
+
 def coarse_hidden(h_ref):
     rows, channels, breadth = h_ref.shape[1:]
     source = lax.broadcasted_iota(jnp.int32, (2 * breadth, 2 * breadth), 0)
@@ -311,17 +316,17 @@
         for b in range(3):
             at = b * channels + (0 if a == 2 else 3 * channels)
             total = parts[a][b * channels : (b + 1) * channels] + parts[a + 1][at : at + channels]
-            base = (a * 3 + b) * 3 * channels // 2
+            base = tap_row(a * 3 + b, packed.shape[0], channels)
             packed[base : base + channels] = total[:, 0:breadth]
             rest = jnp.concatenate([total[:, breadth:], total[:, breadth:]], axis=1)
             mix = jnp.where(lane < channels, rest[0 : channels // 2], rest[channels // 2 :])
             packed[base + channels : base + 3 * channels // 2] = mix
-    base = 9 * 3 * channels // 2
     height = cot_ref.shape[0]
     down = lax.dot_general(cot_ref[...], coarse_hidden(h_ref), across, preferred_element_type=F32)
+    base = 7 * 3 * channels // 2
     for tap in range(4):
         packed[base + tap * height : base + (tap + 1) * height] = down[:, tap * breadth : (tap + 1) * breadth]
-    end = base + 4 * height
+    end = base + 4 * height + 2 * 3 * channels // 2
     if end < packed.shape[0]:
         packed[end:] = jnp.zeros((packed.shape[0] - end, packed.shape[1]), F32)
     split(packed, keep, send, owned_half())
@@ -398,22 +403,59 @@
             out_ref[pl.ds(z * rows + y, channels, stride=2 * rows), :] = line
 
 
-def unpack_kernel(mine, other, conv_ref, down_ref, sums_ref, *, scale):
-    join(mine, other, sums_ref, owned_half())
-    channels = conv_ref.shape[2]
-    for a in range(3):
-        for b in range(3):
-            base = (a * 3 + b) * 3 * channels // 2
-            conv_ref[a, b, :, 0 : 2 * channels] = sums_ref[base : base + channels].astype(F32) * scale
-            rest = sums_ref[base + channels : base + 3 * channels // 2].astype(F32) * scale
-            conv_ref[a, b, 0 : channels // 2, 2 * channels :] = rest[:, 0:channels]
-            conv_ref[a, b, channels // 2 :, 2 * channels :] = rest[:, channels:]
-    base = 9 * 3 * channels // 2
-    height = down_ref.shape[2]
-    for a in range(2):
-        for b in range(2):
-            at = base + (2 * a + b) * height
-            down_ref[a, b] = sums_ref[at : at + height].astype(F32) * scale
+def write_half(half, sums, conv_out, down_out, conv, down, sems, scale):
+    channels, height = conv.shape[2], down.shape[2]
+    size, rows = 3 * channels // 2, sums.shape[0]
+    for tap in range(7) if half == 0 else range(7, 9):
+        base = tap_row(tap, 2 * rows, channels) - half * rows
+        a, b = divmod(tap, 3)
+        conv[a, b, :, 0 : 2 * channels] = sums[base : base + channels].astype(F32) * scale
+        rest = sums[base + channels : base + size].astype(F32) * scale
+        conv[a, b, 0 : channels // 2, 2 * channels :] = rest[:, 0:channels]
+        conv[a, b, channels // 2 :, 2 * channels :] = rest[:, channels:]
+    first = rows - 7 * size
+    if half == 0:
+        down[0, 0, 0:first] = sums[7 * size :].astype(F32) * scale
+        spans = [(conv, conv_out, (pl.ds(0, 2),)), (conv, conv_out, (2, 0)), (down, down_out, (0, 0, pl.ds(0, first)))]
+    else:
+        down[0, 0, first:] = sums[0 : height - first].astype(F32) * scale
+        for tap in range(1, 4):
+            at = tap * height - first
+            down[tap // 2, tap % 2] = sums[at : at + height].astype(F32) * scale
+        spans = [
+            (conv, conv_out, (2, pl.ds(1, 2))), (down, down_out, (0, 0, pl.ds(first, height - first))),
+            (down, down_out, (0, 1)), (down, down_out, (1,)),
+        ]
+    copies = [pltpu.make_async_copy(x.at[at], y.at[at], sems.at[k]) for k, (x, y, at) in enumerate(spans)]
+    for copy in copies:
+        copy.start()
+    for copy in copies:
+        copy.wait()
+
+
+def write_kernel(sums, *refs, own, scale):
+    conv_out, down_out, conv, down, sems = refs[-5:]
+    half = owned_half() if own else 1 - owned_half()
+
+    @pl.when(half == 0)
+    def _():
+        write_half(0, sums, conv_out, down_out, conv, down, sems, scale)
+
+    @pl.when(half == 1)
+    def _():
+        write_half(1, sums, conv_out, down_out, conv, down, sems, scale)
+
+
+def write(sums, shapes, scale, outs=()):
+    return pl.pallas_call(
+        functools.partial(write_kernel, own=len(outs) == 0, scale=scale),
+        out_shape=[jax.ShapeDtypeStruct(shape, F32) for shape in shapes],
+        in_specs=[pl.BlockSpec(memory_space=pltpu.VMEM)] + [pl.BlockSpec(memory_space=pltpu.HBM)] * len(outs),
+        out_specs=[pl.BlockSpec(memory_space=pltpu.HBM)] * 2,
+        scratch_shapes=[pltpu.VMEM(shape, F32) for shape in shapes] + [pltpu.SemaphoreType.DMA((4,))],
+        input_output_aliases={1 + k: k for k in range(len(outs))},
+        compiler_params=PARAMS,
+    )(sums, *outs)
 
 
 def swap(cells, axis, low):
@@ -532,11 +574,9 @@
         (sums, flip(sums, "gz", 2)),
     )
     sums, (field,) = tied(sums, field)
-    grad_conv, grad_down = call(
-        functools.partial(unpack_kernel, scale=grad_scale),
-        [(conv_weight.shape, F32), (down_weight.shape, F32)], [((rows, 128), BF16)], 0,
-        (sums, flip(sums, "gy", 1)),
-    )
+    shapes = (conv_weight.shape, down_weight.shape)
+    other = flip(sums, "gy", 1)
+    grad_conv, grad_down = write(other, shapes, grad_scale, write(sums, shapes, grad_scale))
     section_out = section_out.reshape(out_channels, plane_count // 2, -1)
     return (section_out, field.reshape(features.shape), grad_conv, grad_down)
 

time: 48.6 us -> 48.4 us (level)
  waiting for transfers between devices: 16.8 us -> 15.9 us
  Pallas kernels: 11.5 us -> 12.2 us
    pallas_call x0 -> x2, Pallas kernels: none -> 1.74 us  [write(): pl.pallas_call(functools.partial(write_kernel, own=len(outs) == 0, scale=...]
    pallas_call x19 -> x18, Pallas kernels: 11.2 us -> 10.1 us  [call(): pl.pallas_call(kernel, out_shape=[jax.ShapeDtypeStruct(s, d) for s, d in...]
    ppermute x8, waiting for transfers between devices: 15.2 us -> 14.3 us  [flip(): lax.ppermute(cells, ('gz', 'gy'), [(i, i ^ mask) for i in range(lax.axis_...]
  transfers between devices with their start and end apart: 18 -> 18, of which waited for: 9 -> 9; matrix products, arithmetic and copies ran while one was open for 0% -> 0% of each run, Pallas kernels for 18% -> 20%
where the time goes in v27:
time: 48.4 us; the launch traced here: 48.2 us
  starting transfers between devices  17.4 us (36%)
  waiting for transfers between devices  15.9 us (33%)
  Pallas kernels  12.2 us (25%)
  local copies, waits for them, and re-layouts  1.91 us (4%)
  between operations  0.84 us (2%)
    ppermute x8, waiting for transfers between devices, flip(): lax.ppermute(cells, ('gz', 'gy'), [(i, i ^ mask) for i in range(lax.axis_...  14.3 us
    ppermute x10, starting transfers between devices, swap(): return lax.ppermute(cells, axis, pairs + [(b, a) for a, b in pairs])  13.9 us
    pallas_call x18, Pallas kernels, call(): pl.pallas_call(kernel, out_shape=[jax.ShapeDtypeStruct(s, d) for s, d in...  10.1 us
    ppermute x8, starting transfers between devices, flip(): lax.ppermute(cells, ('gz', 'gy'), [(i, i ^ mask) for i in range(lax.axis_...  3.46 us
    unnamed x8, local copies, waits for them, and re-layouts  1.91 us
    pallas_call x2, Pallas kernels, write(): pl.pallas_call(functools.partial(write_kernel, own=len(outs) == 0, scale=...  1.74 us
    ppermute x10, waiting for transfers between devices, swap(): return lax.ppermute(cells, axis, pairs + [(b, a) for a, b in pairs])  1.54 us
  transfers between devices with their start and end apart: 18, of which 9 were waited for; matrix products, arithmetic and copies ran while one was open for 0% of the time, Pallas kernels for 20%

profile of v27, /device:TPU:0, one launch (start us, length us, event | category | flops | bytes accessed | tf_op | source)
XLA Modules:
  0.0 48.2 jit_solution(16098994151502936776)
XLA Ops:
  0.6 0.9 %copy-done.1 = bf16[64,2,8,128]{3,2,1,0:T(8,128)(2,1)S(1)} copy-done((bf16[64,2,8,128]{3,2,1,0:T(8,128)(2,1)S(1)}, bf16[64,2,8,128]{3,2,1,0:T(8,128)(2,1)}, u32[]{:S(2)}) %copy-start.1) | copy-done | bytes 262168
  1.6 0.2 shard_map.75
  1.8 3.0 %collective-permute-start = (bf16[8,64,128]{2,1,0:T(8,128)(2,1)S(1)}, bf16[8,64,128]{2,1,0:T(8,128)(2,1)S(1)}, u32[]{:S(2)}, u32[]{:S(2)}) collective-permute-start(bf16[8,64,128]{2,1,0:T(8,128)(2,1)S(1)} %get-tuple-element.62.near), channel_id=1, source_target_pairs={{0,4},{8,12},{16,20},{24,28},{4,0},{12,8},{20,16},{28,24},{1,5},{9... | collective-permute-start | bytes 393224 | tf_op jit(solution)/shard_map/ppermute | solution.py:464
  4.8 3.5 %collective-permute-start.1 = (bf16[8,64,128]{2,1,0:T(8,128)(2,1)S(1)}, bf16[8,64,128]{2,1,0:T(8,128)(2,1)S(1)}, u32[]{:S(2)}, u32[]{:S(2)}) collective-permute-start(bf16[8,64,128]{2,1,0:T(8,128)(2,1)S(1)} %get-tuple-element.63.far), channel_id=1, source_target_pairs={{4,8},{12,16},{20,24},{28,0},{8,4},{16,12},{24,20},{0,28},{5,9},{1... | collective-permute-start | bytes 393224 | tf_op jit(solution)/shard_map/ppermute | solution.py:464
  8.4 0.0 collective-permute-start.2
  8.4 1.6 %collective-permute-start.3 = (bf16[2,64,128]{2,1,0:T(8,128)(2,1)S(1)}, bf16[2,64,128]{2,1,0:T(8,128)(2,1)S(1)}, u32[]{:S(2)}, u32[]{:S(2)}) collective-permute-start(bf16[2,64,128]{2,1,0:T(8,128)(2,1)S(1)} %get-tuple-element.69), channel_id=1, source_target_pairs={{1,2},{3,0},{2,1},{0,3},{5,6},{7,4},{6,5},{4,7},{9,10},{11,8},{10,... | collective-permute-start | bytes 98312 | tf_op jit(solution)/shard_map/ppermute | solution.py:464
  10.0 1.0 %copy-done = bf16[3,3,64,192]{3,2,1,0:T(8,128)(2,1)S(1)} copy-done((bf16[3,3,64,192]{3,2,1,0:T(8,128)(2,1)S(1)}, bf16[3,3,64,192]{3,2,1,0:T(8,128)(2,1)}, u32[]{:S(2)}) %copy-start) | copy-done | bytes 221208
  11.0 0.3 shard_map.76
  11.3 1.9 %shard_map.77 = (bf16[2,10,192,128]{3,2,1,0:T(8,128)(2,1)S(1)}, f32[2,8,64,128]{3,2,1,0:T(8,128)S(1)}, f32[2,8,64,128]{3,2,1,0:T(8,128)S(1)}) custom-call(bf16[8,64,128]{2,1,0:T(8,128)(2,1)S(1)} %get-tuple-element.62.near, bf16[8,64,128]{2,1,0:T(8,128)(2,1)S(1)} %get-tuple-element.63.far, bf16[3,3,64,192]{3,2,1,0:T(8,128)(2,1)S(1)} %get-tuple-element.64.w_ref, ...), custom_call_target="tpu_custom_call" | custom-call | flops 301989888 | bytes 2711552 | tf_op jit(solution)/shard_map/pallas_call | solution.py:20
  13.2 0.0 collective-permute-done.3.far_row
  13.2 0.0 collective-permute-done.near.near_in
  13.3 0.4 collective-permute-start.4
  13.7 0.5 collective-permute-start.5
  14.2 1.1 %shard_map.78 = (bf16[2,10,192,128]{3,2,1,0:T(8,128)(2,1)S(1)}, bf16[2,2,192,128]{3,2,1,0:T(8,128)(2,1)S(1)}, f32[2,2,64,128]{3,2,1,0:T(8,128)S(1)}, bf16[8,64,1...) custom-call(bf16[8,64,128]{2,1,0:T(8,128)(2,1)S(1)} %collective-permute-done.near.near_in,, ...), custom_call_target="tpu_custom_call" | custom-call | flops 150994944 | bytes 3432448 | tf_op jit(solution)/shard_map/pallas_call | solution.py:20
  15.3 1.5 %collective-permute-done.4.far = bf16[2,64,128]{2,1,0:T(8,128)(2,1)S(1)} collective-permute-done((bf16[2,64,128]{2,1,0:T(8,128)(2,1)S(1)}, bf16[2,64,128]{2,1,0:T(8,128)(2,1)S(1)}, u32[]{:S(2)}, u32[]{:S(2)}) %collective-permute-start.4) | collective-permute-done | bytes 32800 | tf_op jit(solution)/shard_map/ppermute | solution.py:464
  16.9 0.0 collective-permute-done.5.near
  16.9 0.3 shard_map.80
  17.2 1.2 %shard_map.81 = (f32[704,128]{1,0:T(8,128)S(1)}, bf16[704,128]{1,0:T(8,128)(2,1)S(1)}) custom-call(bf16[2,10,192,128]{3,2,1,0:T(8,128)(2,1)S(1)} %get-tuple-element.67.inner, bf16[2,10,192,128]{3,2,1,0:T(8,128)(2,1)S(1)} %get-tuple-element.77.outer, bf16[2,2,192,128]{3,2,1,0:T(8,128)(2,1)S(1)} %get-tuple-element.78.own_edges, ...), custom_call_target="tpu_custom_call" | custom-call | flops 452984832 | bytes 3489792 | tf_op jit(solution)/shard_map/pallas_call | solution.py:20
  18.4 0.2 collective-permute-start.6
  18.6 1.3 %collective-permute-done.6.other = bf16[704,128]{1,0:T(8,128)(2,1)S(1)} collective-permute-done((bf16[704,128]{1,0:T(8,128)(2,1)S(1)}, bf16[704,128]{1,0:T(8,128)(2,1)S(1)}, u32[]{:S(2)}, u32[]{:S(2)}) %collective-permute-start.6) | collective-permute-done | bytes 180256 | tf_op jit(solution)/shard_map/ppermute | solution.py:470
  19.9 0.1 shard_map.82
  20.0 0.1 collective-permute-start.7
  20.1 1.0 %collective-permute-start.10 = (bf16[8,64,128]{2,1,0:T(8,128)(2,1)S(1)}, bf16[8,64,128]{2,1,0:T(8,128)(2,1)S(1)}, u32[]{:S(2)}, u32[]{:S(2)}) collective-permute-start(bf16[8,64,128]{2,1,0:T(8,128)(2,1)S(1)} %get-tuple-element.100.near), channel_id=1, source_target_pairs={{0,4},{8,12},{16,20},{24,28},{4,0},{12,8},{20,16},{28,24},{1,5},{9... | collective-permute-start | bytes 393224 | tf_op jit(solution)/shard_map/ppermute | solution.py:464
  21.1 2.4 %collective-permute-start.11 = (bf16[8,64,128]{2,1,0:T(8,128)(2,1)S(1)}, bf16[8,64,128]{2,1,0:T(8,128)(2,1)S(1)}, u32[]{:S(2)}, u32[]{:S(2)}) collective-permute-start(bf16[8,64,128]{2,1,0:T(8,128)(2,1)S(1)} %get-tuple-element.101.far), channel_id=1, source_target_pairs={{4,8},{12,16},{20,24},{28,0},{8,4},{16,12},{24,20},{0,28},{5,9},{1... | collective-permute-start | bytes 393224 | tf_op jit(solution)/shard_map/ppermute | solution.py:464
  23.6 1.1 %collective-permute-done.7.other = bf16[352,128]{1,0:T(8,128)(2,1)S(1)} collective-permute-done((bf16[352,128]{1,0:T(8,128)(2,1)S(1)}, bf16[352,128]{1,0:T(8,128)(2,1)S(1)}, u32[]{:S(2)}, u32[]{:S(2)}) %collective-permute-start.7) | collective-permute-done | bytes 90144 | tf_op jit(solution)/shard_map/ppermute | solution.py:470
  24.7 1.1 %collective-permute-start.8 = (bf16[176,128]{1,0:T(8,128)(2,1)S(1)}, bf16[176,128]{1,0:T(8,128)(2,1)S(1)}, u32[]{:S(2)}, u32[]{:S(2)}) collective-permute-start(bf16[176,128]{1,0:T(8,128)(2,1)S(1)} %get-tuple-element.99), channel_id=1, source_target_pairs={{0,3},{1,2},{2,1},{3,0},{4,7},{5,6},{6,5},{7,4},{8,11},{9,10},{10,... | collective-permute-start | bytes 135176 | tf_op jit(solution)/shard_map/ppermute | solution.py:470
  25.8 2.4 %collective-permute-done.8.y = bf16[176,128]{1,0:T(8,128)(2,1)S(1)} collective-permute-done((bf16[176,128]{1,0:T(8,128)(2,1)S(1)}, bf16[176,128]{1,0:T(8,128)(2,1)S(1)}, u32[]{:S(2)}, u32[]{:S(2)}) %collective-permute-start.8) | collective-permute-done | bytes 45088 | tf_op jit(solution)/shard_map/ppermute | solution.py:470
  28.2 0.1 collective-permute-start.9
  28.4 3.4 %collective-permute-done.9.y = bf16[176,128]{1,0:T(8,128)(2,1)S(1)} collective-permute-done((bf16[176,128]{1,0:T(8,128)(2,1)S(1)}, bf16[176,128]{1,0:T(8,128)(2,1)S(1)}, u32[]{:S(2)}, u32[]{:S(2)}) %collective-permute-start.9) | collective-permute-done | bytes 45088 | tf_op jit(solution)/shard_map/ppermute | solution.py:470
  31.8 0.0 collective-permute-done.10.near_in
  31.8 0.0 collective-permute-done.11.far_in
  31.8 1.2 %collective-permute-start.12 = (bf16[176,128]{1,0:T(8,128)(2,1)S(1)}, bf16[176,128]{1,0:T(8,128)(2,1)S(1)}, u32[]{:S(2)}, u32[]{:S(2)}) collective-permute-start(bf16[176,128]{1,0:T(8,128)(2,1)S(1)} %shard_map.85.x), channel_id=1, source_target_pairs={{0,17},{1,16},{2,19},{3,18},{4,21},{5,20},{6,23},{7,22},{8,25},{9,... | collective-permute-start | bytes 135176 | tf_op jit(solution)/shard_map/ppermute | solution.py:470
  33.1 0.1 collective-permute-start.14
  33.1 1.3 %collective-permute-start.15 = (bf16[4,64,128]{2,1,0:T(8,128)(2,1)S(1)}, bf16[4,64,128]{2,1,0:T(8,128)(2,1)S(1)}, u32[]{:S(2)}, u32[]{:S(2)}) collective-permute-start(bf16[4,64,128]{2,1,0:T(8,128)(2,1)S(1)} %get-tuple-element.109), channel_id=1, source_target_pairs={{1,2},{3,0},{2,1},{0,3},{5,6},{7,4},{6,5},{4,7},{9,10},{11,8},{10,... | collective-permute-start | bytes 196616 | tf_op jit(solution)/shard_map/ppermute | solution.py:464
  34.4 1.1 %shard_map.87 = bf16[128,256]{1,0:T(8,128)(2,1)} custom-call(bf16[2,8,64,128]{3,2,1,0:T(8,128)(2,1)S(1)} %get-tuple-element.103.h_ref, bf16[2,2,128,128]{3,2,1,0:T(8,128)(2,1)S(1)} %get-tuple-element.65.d_ref), custom_call_target="tpu_custom_call" | custom-call | flops 45298484 | bytes 458752 | tf_op jit(solution)/shard_map/pallas_call | solution.py:20
  35.5 1.9 %collective-permute-done.12.y = bf16[176,128]{1,0:T(8,128)(2,1)S(1)} collective-permute-done((bf16[176,128]{1,0:T(8,128)(2,1)S(1)}, bf16[176,128]{1,0:T(8,128)(2,1)S(1)}, u32[]{:S(2)}, u32[]{:S(2)}) %collective-permute-start.12) | collective-permute-done | bytes 45088 | tf_op jit(solution)/shard_map/ppermute | solution.py:470
  37.4 0.5 collective-permute-start.13
  37.9 0.4 shard_map.89.w_ref
  38.3 2.3 %shard_map.90.acc_ref = f32[2,8,64,128]{3,2,1,0:T(8,128)S(1)} custom-call(bf16[8,64,128]{2,1,0:T(8,128)(2,1)S(1)} %get-tuple-element.100.near, bf16[8,64,128]{2,1,0:T(8,128)(2,1)S(1)} %get-tuple-element.101.far, bf16[8,64,128]{2,1,0:T(8,128)(2,1)S(1)} %collective-permute-done.10.near_in, bf16[8,64,128]{2,1,0:T(8,128)(2,1)S(1)} %collective-permute-done.11.far_in, ...), custom_call_target="tpu_custom_call" | custom-call | flops 452984832 | bytes 1269760 | tf_op jit(solution)/shard_map/pallas_call | solution.py:20
  40.6 0.6 %collective-permute-done.13.other = bf16[176,128]{1,0:T(8,128)(2,1)S(1)} collective-permute-done((bf16[176,128]{1,0:T(8,128)(2,1)S(1)}, bf16[176,128]{1,0:T(8,128)(2,1)S(1)}, u32[]{:S(2)}, u32[]{:S(2)}) %collective-permute-start.13) | collective-permute-done | bytes 45088 | tf_op jit(solution)/shard_map/ppermute | solution.py:470
  41.2 0.0 collective-permute-done.14.near
  41.2 0.1 collective-permute-start.16
  41.3 1.3 %shard_map.93 = f32[1024,128]{1,0:T(8,128)} custom-call(bf16[4,64,128]{2,1,0:T(8,128)(2,1)S(1)} %collective-permute-done.14.near, bf16[4,64,128]{2,1,0:T(8,128)(2,1)S(1)} %collective-permute-done.15.far, f32[2,8,64,128]{3,2,1,0:T(8,128)S(1)} %shard_map.90.acc_ref, bf16[3,3,64,192]{3,2,1,0:T(8,128)(2,1)S(1)} %shard_map.89.w_ref), custom_call_target="tpu_custom_call" | custom-call | flops 45298484 | bytes 1400832 | tf_op jit(solution)/shard_map/pallas_call | solution.py:20
  42.6 3.3 %collective-permute-done.16.other = bf16[352,128]{1,0:T(8,128)(2,1)S(1)} collective-permute-done((bf16[352,128]{1,0:T(8,128)(2,1)S(1)}, bf16[352,128]{1,0:T(8,128)(2,1)S(1)}, u32[]{:S(2)}, u32[]{:S(2)}) %collective-permute-start.16) | collective-permute-done | bytes 90144 | tf_op jit(solution)/shard_map/ppermute | solution.py:470
  45.9 0.2 collective-permute-start.17
  46.1 0.9 %shard_map.94 = (f32[3,3,64,192]{3,2,1,0:T(8,128)}, f32[2,2,128,128]{3,2,1,0:T(8,128)}) custom-call(bf16[704,128]{1,0:T(8,128)(2,1)S(1)} %shard_map.92.sums), custom_call_target="tpu_custom_call" | custom-call | tf_op jit(solution)/shard_map/pallas_call | solution.py:450
  47.0 0.4 collective-permute-done.17.sums
  47.4 0.8 %shard_map.95 = (f32[3,3,64,192]{3,2,1,0:T(8,128)}, f32[2,2,128,128]{3,2,1,0:T(8,128)}) custom-call(bf16[704,128]{1,0:T(8,128)(2,1)S(1)} %collective-permute-done.17.sums, f32[3,3,64,192]{3,2,1,0:T(8,128)} %get-tuple-element.116.refs_0_, f32[2,2,128,128]{3,2,1,0:T(8,128)} %get-tuple-element.117.refs_1_), custom_call_target="tpu_custom_call", output_to_operand_aliasing={{0}: (1, {}), {1}: (2, {})} | custom-call | tf_op jit(solution)/shard_map/pallas_call | solution.py:450
  (17 shorter events, 0.2 us)
Async XLA Ops:
  0.6 1.0 %copy-start.1 = (bf16[64,2,8,128]{3,2,1,0:T(8,128)(2,1)S(1)}, bf16[64,2,8,128]{3,2,1,0:T(8,128)(2,1)}, u32[]{:S(2)}) copy-start(bf16[64,2,8,128]{3,2,1,0:T(8,128)(2,1)} %f_ref.1) | copy-start | bytes 786436
  1.6 8.4 %copy-start.2 = (bf16[2,2,128,128]{3,2,1,0:T(8,128)(2,1)S(1)}, bf16[2,2,128,128]{3,2,1,0:T(8,128)(2,1)}, u32[]{:S(2)}) copy-start(bf16[2,2,128,128]{3,2,1,0:T(8,128)(2,1)} %refs_1_.1) | copy-start | bytes 393220
  1.6 8.4 %copy-start.3 = (bf16[128,1,256]{2,0,1:T(8,128)(2,1)S(1)}, bf16[128,1,256]{2,0,1:T(8,128)(2,1)}, u32[]{:S(2)}) copy-start(bf16[128,1,256]{2,0,1:T(8,128)(2,1)} %param.7) | copy-start | bytes 196612
  1.8 11.4 %collective-permute-start = (bf16[8,64,128]{2,1,0:T(8,128)(2,1)S(1)}, bf16[8,64,128]{2,1,0:T(8,128)(2,1)S(1)}, u32[]{:S(2)}, u32[]{:S(2)}) collective-permute-start(bf16[8,64,128]{2,1,0:T(8,128)(2,1)S(1)} %get-tuple-element.62.near), channel_id=1, source_target_pairs={{0,4},{8,12},{16,20},{24,28},{4,0},{12,8},{20,16},{28,24},{1,5},{9... | collective-permute-start | bytes 393224 | tf_op jit(solution)/shard_map/ppermute | solution.py:464
  4.8 8.4 %collective-permute-start.1 = (bf16[8,64,128]{2,1,0:T(8,128)(2,1)S(1)}, bf16[8,64,128]{2,1,0:T(8,128)(2,1)S(1)}, u32[]{:S(2)}, u32[]{:S(2)}) collective-permute-start(bf16[8,64,128]{2,1,0:T(8,128)(2,1)S(1)} %get-tuple-element.63.far), channel_id=1, source_target_pairs={{4,8},{12,16},{20,24},{28,0},{8,4},{16,12},{24,20},{0,28},{5,9},{1... | collective-permute-start | bytes 393224 | tf_op jit(solution)/shard_map/ppermute | solution.py:464
  8.4 4.8 %collective-permute-start.2 = (bf16[2,64,128]{2,1,0:T(8,128)(2,1)S(1)}, bf16[2,64,128]{2,1,0:T(8,128)(2,1)S(1)}, u32[]{:S(2)}, u32[]{:S(2)}) collective-permute-start(bf16[2,64,128]{2,1,0:T(8,128)(2,1)S(1)} %get-tuple-element.68), channel_id=1, source_target_pairs={{0,1},{2,3},{1,0},{3,2},{4,5},{6,7},{5,4},{7,6},{8,9},{10,11},{9,8... | collective-permute-start | bytes 98312 | tf_op jit(solution)/shard_map/ppermute | solution.py:464
  8.4 4.9 %collective-permute-start.3 = (bf16[2,64,128]{2,1,0:T(8,128)(2,1)S(1)}, bf16[2,64,128]{2,1,0:T(8,128)(2,1)S(1)}, u32[]{:S(2)}, u32[]{:S(2)}) collective-permute-start(bf16[2,64,128]{2,1,0:T(8,128)(2,1)S(1)} %get-tuple-element.69), channel_id=1, source_target_pairs={{1,2},{3,0},{2,1},{0,3},{5,6},{7,4},{6,5},{4,7},{9,10},{11,8},{10,... | collective-permute-start | bytes 98312 | tf_op jit(solution)/shard_map/ppermute | solution.py:464
  10.0 1.0 %copy-start = (bf16[3,3,64,192]{3,2,1,0:T(8,128)(2,1)S(1)}, bf16[3,3,64,192]{3,2,1,0:T(8,128)(2,1)}, u32[]{:S(2)}) copy-start(bf16[3,3,64,192]{3,2,1,0:T(8,128)(2,1)} %refs_0_.1) | copy-start | bytes 663556
  13.3 3.6 %collective-permute-start.4 = (bf16[2,64,128]{2,1,0:T(8,128)(2,1)S(1)}, bf16[2,64,128]{2,1,0:T(8,128)(2,1)S(1)}, u32[]{:S(2)}, u32[]{:S(2)}) collective-permute-start(bf16[2,64,128]{2,1,0:T(8,128)(2,1)S(1)} %get-tuple-element.79), channel_id=1, source_target_pairs={{1,2},{3,0},{2,1},{0,3},{5,6},{7,4},{6,5},{4,7},{9,10},{11,8},{10,... | collective-permute-start | bytes 98312 | tf_op jit(solution)/shard_map/ppermute | solution.py:464
  13.7 3.1 %collective-permute-start.5 = (bf16[2,64,128]{2,1,0:T(8,128)(2,1)S(1)}, bf16[2,64,128]{2,1,0:T(8,128)(2,1)S(1)}, u32[]{:S(2)}, u32[]{:S(2)}) collective-permute-start(bf16[2,64,128]{2,1,0:T(8,128)(2,1)S(1)} %get-tuple-element.80), channel_id=1, source_target_pairs={{0,1},{2,3},{1,0},{3,2},{4,5},{6,7},{5,4},{7,6},{8,9},{10,11},{9,8... | collective-permute-start | bytes 98312 | tf_op jit(solution)/shard_map/ppermute | solution.py:464
  18.4 1.5 %collective-permute-start.6 = (bf16[704,128]{1,0:T(8,128)(2,1)S(1)}, bf16[704,128]{1,0:T(8,128)(2,1)S(1)}, u32[]{:S(2)}, u32[]{:S(2)}) collective-permute-start(bf16[704,128]{1,0:T(8,128)(2,1)S(1)} %get-tuple-element.93), channel_id=1, source_target_pairs={{0,1},{1,0},{2,3},{3,2},{4,5},{5,4},{6,7},{7,6},{8,9},{9,8},{10,11... | collective-permute-start | bytes 540680 | tf_op jit(solution)/shard_map/ppermute | solution.py:470
  20.0 4.7 %collective-permute-start.7 = (bf16[352,128]{1,0:T(8,128)(2,1)S(1)}, bf16[352,128]{1,0:T(8,128)(2,1)S(1)}, u32[]{:S(2)}, u32[]{:S(2)}) collective-permute-start(bf16[352,128]{1,0:T(8,128)(2,1)S(1)} %get-tuple-element.97), channel_id=1, source_target_pairs={{0,9},{1,8},{2,11},{3,10},{4,13},{5,12},{6,15},{7,14},{8,1},{9,0},... | collective-permute-start | bytes 270344 | tf_op jit(solution)/shard_map/ppermute | solution.py:470
  20.1 11.7 %collective-permute-start.10 = (bf16[8,64,128]{2,1,0:T(8,128)(2,1)S(1)}, bf16[8,64,128]{2,1,0:T(8,128)(2,1)S(1)}, u32[]{:S(2)}, u32[]{:S(2)}) collective-permute-start(bf16[8,64,128]{2,1,0:T(8,128)(2,1)S(1)} %get-tuple-element.100.near), channel_id=1, source_target_pairs={{0,4},{8,12},{16,20},{24,28},{4,0},{12,8},{20,16},{28,24},{1,5},{9... | collective-permute-start | bytes 393224 | tf_op jit(solution)/shard_map/ppermute | solution.py:464
  21.1 10.7 %collective-permute-start.11 = (bf16[8,64,128]{2,1,0:T(8,128)(2,1)S(1)}, bf16[8,64,128]{2,1,0:T(8,128)(2,1)S(1)}, u32[]{:S(2)}, u32[]{:S(2)}) collective-permute-start(bf16[8,64,128]{2,1,0:T(8,128)(2,1)S(1)} %get-tuple-element.101.far), channel_id=1, source_target_pairs={{4,8},{12,16},{20,24},{28,0},{8,4},{16,12},{24,20},{0,28},{5,9},{1... | collective-permute-start | bytes 393224 | tf_op jit(solution)/shard_map/ppermute | solution.py:464
  24.7 3.5 %collective-permute-start.8 = (bf16[176,128]{1,0:T(8,128)(2,1)S(1)}, bf16[176,128]{1,0:T(8,128)(2,1)S(1)}, u32[]{:S(2)}, u32[]{:S(2)}) collective-permute-start(bf16[176,128]{1,0:T(8,128)(2,1)S(1)} %get-tuple-element.99), channel_id=1, source_target_pairs={{0,3},{1,2},{2,1},{3,0},{4,7},{5,6},{6,5},{7,4},{8,11},{9,10},{10,... | collective-permute-start | bytes 135176 | tf_op jit(solution)/shard_map/ppermute | solution.py:470
  28.2 3.5 %collective-permute-start.9 = (bf16[176,128]{1,0:T(8,128)(2,1)S(1)}, bf16[176,128]{1,0:T(8,128)(2,1)S(1)}, u32[]{:S(2)}, u32[]{:S(2)}) collective-permute-start(bf16[176,128]{1,0:T(8,128)(2,1)S(1)} %shard_map.84.x), channel_id=1, source_target_pairs={{0,5},{1,4},{2,7},{3,6},{4,1},{5,0},{6,3},{7,2},{8,13},{9,12},{10,... | collective-permute-start | bytes 135176 | tf_op jit(solution)/shard_map/ppermute | solution.py:470
  31.8 5.6 %collective-permute-start.12 = (bf16[176,128]{1,0:T(8,128)(2,1)S(1)}, bf16[176,128]{1,0:T(8,128)(2,1)S(1)}, u32[]{:S(2)}, u32[]{:S(2)}) collective-permute-start(bf16[176,128]{1,0:T(8,128)(2,1)S(1)} %shard_map.85.x), channel_id=1, source_target_pairs={{0,17},{1,16},{2,19},{3,18},{4,21},{5,20},{6,23},{7,22},{8,25},{9,... | collective-permute-start | bytes 135176 | tf_op jit(solution)/shard_map/ppermute | solution.py:470
  33.1 8.1 %collective-permute-start.14 = (bf16[4,64,128]{2,1,0:T(8,128)(2,1)S(1)}, bf16[4,64,128]{2,1,0:T(8,128)(2,1)S(1)}, u32[]{:S(2)}, u32[]{:S(2)}) collective-permute-start(bf16[4,64,128]{2,1,0:T(8,128)(2,1)S(1)} %get-tuple-element.108), channel_id=1, source_target_pairs={{0,1},{2,3},{1,0},{3,2},{4,5},{6,7},{5,4},{7,6},{8,9},{10,11},{9,8... | collective-permute-start | bytes 196616 | tf_op jit(solution)/shard_map/ppermute | solution.py:464
  33.1 8.0 %collective-permute-start.15 = (bf16[4,64,128]{2,1,0:T(8,128)(2,1)S(1)}, bf16[4,64,128]{2,1,0:T(8,128)(2,1)S(1)}, u32[]{:S(2)}, u32[]{:S(2)}) collective-permute-start(bf16[4,64,128]{2,1,0:T(8,128)(2,1)S(1)} %get-tuple-element.109), channel_id=1, source_target_pairs={{1,2},{3,0},{2,1},{0,3},{5,6},{7,4},{6,5},{4,7},{9,10},{11,8},{10,... | collective-permute-start | bytes 196616 | tf_op jit(solution)/shard_map/ppermute | solution.py:464
  37.4 3.7 %collective-permute-start.13 = (bf16[176,128]{1,0:T(8,128)(2,1)S(1)}, bf16[176,128]{1,0:T(8,128)(2,1)S(1)}, u32[]{:S(2)}, u32[]{:S(2)}) collective-permute-start(bf16[176,128]{1,0:T(8,128)(2,1)S(1)} %shard_map.86.mine), channel_id=1, source_target_pairs={{0,3},{1,2},{2,1},{3,0},{4,7},{5,6},{6,5},{7,4},{8,11},{9,10},{10,... | collective-permute-start | bytes 135176 | tf_op jit(solution)/shard_map/ppermute | solution.py:470
  41.2 4.7 %collective-permute-start.16 = (bf16[352,128]{1,0:T(8,128)(2,1)S(1)}, bf16[352,128]{1,0:T(8,128)(2,1)S(1)}, u32[]{:S(2)}, u32[]{:S(2)}) collective-permute-start(bf16[352,128]{1,0:T(8,128)(2,1)S(1)} %shard_map.88.mine), channel_id=1, source_target_pairs={{0,9},{1,8},{2,11},{3,10},{4,13},{5,12},{6,15},{7,14},{8,1},{9,0},... | collective-permute-start | bytes 270344 | tf_op jit(solution)/shard_map/ppermute | solution.py:470
  45.9 1.5 %collective-permute-start.17 = (bf16[704,128]{1,0:T(8,128)(2,1)S(1)}, bf16[704,128]{1,0:T(8,128)(2,1)S(1)}, u32[]{:S(2)}, u32[]{:S(2)}) collective-permute-start(bf16[704,128]{1,0:T(8,128)(2,1)S(1)} %shard_map.92.sums), channel_id=1, source_target_pairs={{0,1},{1,0},{2,3},{3,2},{4,5},{5,4},{6,7},{7,6},{8,9},{9,8},{10,11... | collective-permute-start | bytes 540680 | tf_op jit(solution)/shard_map/ppermute | solution.py:470

commit v28 on v27

--- a/solution.py
+++ b/solution.py
@@ -406,6 +406,12 @@
 def write_half(half, sums, conv_out, down_out, conv, down, sems, scale):
     channels, height = conv.shape[2], down.shape[2]
     size, rows = 3 * channels // 2, sums.shape[0]
+    copies = []
+
+    def send(staged, out, at):
+        copies.append(pltpu.make_async_copy(staged.at[at], out.at[at], sems.at[len(copies)]))
+        copies[-1].start()
+
     for tap in range(7) if half == 0 else range(7, 9):
         base = tap_row(tap, 2 * rows, channels) - half * rows
         a, b = divmod(tap, 3)
@@ -413,22 +419,21 @@
         rest = sums[base + channels : base + size].astype(F32) * scale
         conv[a, b, 0 : channels // 2, 2 * channels :] = rest[:, 0:channels]
         conv[a, b, channels // 2 :, 2 * channels :] = rest[:, channels:]
+        if tap in (2, 5):
+            send(conv, conv_out, (a,))
+    send(conv, conv_out, (2, 0) if half == 0 else (2, pl.ds(1, 2)))
     first = rows - 7 * size
     if half == 0:
         down[0, 0, 0:first] = sums[7 * size :].astype(F32) * scale
-        spans = [(conv, conv_out, (pl.ds(0, 2),)), (conv, conv_out, (2, 0)), (down, down_out, (0, 0, pl.ds(0, first)))]
+        send(down, down_out, (0, 0, pl.ds(0, first)))
     else:
         down[0, 0, first:] = sums[0 : height - first].astype(F32) * scale
+        send(down, down_out, (0, 0, pl.ds(first, height - first)))
         for tap in range(1, 4):
             at = tap * height - first
             down[tap // 2, tap % 2] = sums[at : at + height].astype(F32) * scale
-        spans = [
-            (conv, conv_out, (2, pl.ds(1, 2))), (down, down_out, (0, 0, pl.ds(first, height - first))),
-            (down, down_out, (0, 1)), (down, down_out, (1,)),
-        ]
-    copies = [pltpu.make_async_copy(x.at[at], y.at[at], sems.at[k]) for k, (x, y, at) in enumerate(spans)]
-    for copy in copies:
-        copy.start()
+            if tap in (1, 3):
+                send(down, down_out, (0, 1) if tap == 1 else (1,))
     for copy in copies:
         copy.wait()
 

time: 48.4 us -> 48.4 us (level)
  no operation moved by 1% of the time
where the time goes in v28:
time: 48.4 us; the launch traced here: 48.2 us
  starting transfers between devices  17.4 us (36%)
  waiting for transfers between devices  15.9 us (33%)
  Pallas kernels  12.2 us (25%)
  local copies, waits for them, and re-layouts  1.91 us (4%)
  between operations  0.84 us (2%)
    ppermute x8, waiting for transfers between devices, flip(): lax.ppermute(cells, ('gz', 'gy'), [(i, i ^ mask) for i in range(lax.axis_...  14.3 us
    ppermute x10, starting transfers between devices, swap(): return lax.ppermute(cells, axis, pairs + [(b, a) for a, b in pairs])  13.9 us
    pallas_call x18, Pallas kernels, call(): pl.pallas_call(kernel, out_shape=[jax.ShapeDtypeStruct(s, d) for s, d in...  10.1 us
    ppermute x8, starting transfers between devices, flip(): lax.ppermute(cells, ('gz', 'gy'), [(i, i ^ mask) for i in range(lax.axis_...  3.46 us
    unnamed x8, local copies, waits for them, and re-layouts  1.91 us
    pallas_call x2, Pallas kernels, write(): pl.pallas_call(functools.partial(write_kernel, own=len(outs) == 0, scale=...  1.72 us
    ppermute x10, waiting for transfers between devices, swap(): return lax.ppermute(cells, axis, pairs + [(b, a) for a, b in pairs])  1.54 us
  transfers between devices with their start and end apart: 18, of which 9 were waited for; matrix products, arithmetic and copies ran while one was open for 0% of the time, Pallas kernels for 20%

profile of v28, /device:TPU:0, one launch (start us, length us, event | category | flops | bytes accessed | tf_op | source)
XLA Modules:
  0.0 48.2 jit_solution(1948054584649661222)
XLA Ops:
  0.6 0.9 %copy-done.1 = bf16[64,2,8,128]{3,2,1,0:T(8,128)(2,1)S(1)} copy-done((bf16[64,2,8,128]{3,2,1,0:T(8,128)(2,1)S(1)}, bf16[64,2,8,128]{3,2,1,0:T(8,128)(2,1)}, u32[]{:S(2)}) %copy-start.1) | copy-done | bytes 262168
  1.6 0.2 shard_map.75
  1.8 3.0 %collective-permute-start = (bf16[8,64,128]{2,1,0:T(8,128)(2,1)S(1)}, bf16[8,64,128]{2,1,0:T(8,128)(2,1)S(1)}, u32[]{:S(2)}, u32[]{:S(2)}) collective-permute-start(bf16[8,64,128]{2,1,0:T(8,128)(2,1)S(1)} %get-tuple-element.62.near), channel_id=1, source_target_pairs={{0,4},{8,12},{16,20},{24,28},{4,0},{12,8},{20,16},{28,24},{1,5},{9... | collective-permute-start | bytes 393224 | tf_op jit(solution)/shard_map/ppermute | solution.py:469
  4.8 3.5 %collective-permute-start.1 = (bf16[8,64,128]{2,1,0:T(8,128)(2,1)S(1)}, bf16[8,64,128]{2,1,0:T(8,128)(2,1)S(1)}, u32[]{:S(2)}, u32[]{:S(2)}) collective-permute-start(bf16[8,64,128]{2,1,0:T(8,128)(2,1)S(1)} %get-tuple-element.63.far), channel_id=1, source_target_pairs={{4,8},{12,16},{20,24},{28,0},{8,4},{16,12},{24,20},{0,28},{5,9},{1... | collective-permute-start | bytes 393224 | tf_op jit(solution)/shard_map/ppermute | solution.py:469
  8.4 0.0 collective-permute-start.2
  8.4 1.6 %collective-permute-start.3 = (bf16[2,64,128]{2,1,0:T(8,128)(2,1)S(1)}, bf16[2,64,128]{2,1,0:T(8,128)(2,1)S(1)}, u32[]{:S(2)}, u32[]{:S(2)}) collective-permute-start(bf16[2,64,128]{2,1,0:T(8,128)(2,1)S(1)} %get-tuple-element.69), channel_id=1, source_target_pairs={{1,2},{3,0},{2,1},{0,3},{5,6},{7,4},{6,5},{4,7},{9,10},{11,8},{10,... | collective-permute-start | bytes 98312 | tf_op jit(solution)/shard_map/ppermute | solution.py:469
  10.0 1.0 %copy-done = bf16[3,3,64,192]{3,2,1,0:T(8,128)(2,1)S(1)} copy-done((bf16[3,3,64,192]{3,2,1,0:T(8,128)(2,1)S(1)}, bf16[3,3,64,192]{3,2,1,0:T(8,128)(2,1)}, u32[]{:S(2)}) %copy-start) | copy-done | bytes 221208
  11.0 0.3 shard_map.76
  11.3 1.9 %shard_map.77 = (bf16[2,10,192,128]{3,2,1,0:T(8,128)(2,1)S(1)}, f32[2,8,64,128]{3,2,1,0:T(8,128)S(1)}, f32[2,8,64,128]{3,2,1,0:T(8,128)S(1)}) custom-call(bf16[8,64,128]{2,1,0:T(8,128)(2,1)S(1)} %get-tuple-element.62.near, bf16[8,64,128]{2,1,0:T(8,128)(2,1)S(1)} %get-tuple-element.63.far, bf16[3,3,64,192]{3,2,1,0:T(8,128)(2,1)S(1)} %get-tuple-element.64.w_ref, ...), custom_call_target="tpu_custom_call" | custom-call | flops 301989888 | bytes 2711552 | tf_op jit(solution)/shard_map/pallas_call | solution.py:20
  13.2 0.0 collective-permute-done.3.far_row
  13.2 0.0 collective-permute-done.near.near_in
  13.3 0.4 collective-permute-start.4
  13.7 0.5 collective-permute-start.5
  14.2 1.1 %shard_map.78 = (bf16[2,10,192,128]{3,2,1,0:T(8,128)(2,1)S(1)}, bf16[2,2,192,128]{3,2,1,0:T(8,128)(2,1)S(1)}, f32[2,2,64,128]{3,2,1,0:T(8,128)S(1)}, bf16[8,64,1...) custom-call(bf16[8,64,128]{2,1,0:T(8,128)(2,1)S(1)} %collective-permute-done.near.near_in,, ...), custom_call_target="tpu_custom_call" | custom-call | flops 150994944 | bytes 3432448 | tf_op jit(solution)/shard_map/pallas_call | solution.py:20
  15.3 1.5 %collective-permute-done.4.far = bf16[2,64,128]{2,1,0:T(8,128)(2,1)S(1)} collective-permute-done((bf16[2,64,128]{2,1,0:T(8,128)(2,1)S(1)}, bf16[2,64,128]{2,1,0:T(8,128)(2,1)S(1)}, u32[]{:S(2)}, u32[]{:S(2)}) %collective-permute-start.4) | collective-permute-done | bytes 32800 | tf_op jit(solution)/shard_map/ppermute | solution.py:469
  16.9 0.0 collective-permute-done.5.near
  16.9 0.3 shard_map.80
  17.2 1.2 %shard_map.81 = (f32[704,128]{1,0:T(8,128)S(1)}, bf16[704,128]{1,0:T(8,128)(2,1)S(1)}) custom-call(bf16[2,10,192,128]{3,2,1,0:T(8,128)(2,1)S(1)} %get-tuple-element.67.inner, bf16[2,10,192,128]{3,2,1,0:T(8,128)(2,1)S(1)} %get-tuple-element.77.outer, bf16[2,2,192,128]{3,2,1,0:T(8,128)(2,1)S(1)} %get-tuple-element.78.own_edges, ...), custom_call_target="tpu_custom_call" | custom-call | flops 452984832 | bytes 3489792 | tf_op jit(solution)/shard_map/pallas_call | solution.py:20
  18.4 0.2 collective-permute-start.6
  18.6 1.3 %collective-permute-done.6.other = bf16[704,128]{1,0:T(8,128)(2,1)S(1)} collective-permute-done((bf16[704,128]{1,0:T(8,128)(2,1)S(1)}, bf16[704,128]{1,0:T(8,128)(2,1)S(1)}, u32[]{:S(2)}, u32[]{:S(2)}) %collective-permute-start.6) | collective-permute-done | bytes 180256 | tf_op jit(solution)/shard_map/ppermute | solution.py:475
  19.9 0.1 shard_map.82
  20.0 0.1 collective-permute-start.7
  20.1 1.0 %collective-permute-start.10 = (bf16[8,64,128]{2,1,0:T(8,128)(2,1)S(1)}, bf16[8,64,128]{2,1,0:T(8,128)(2,1)S(1)}, u32[]{:S(2)}, u32[]{:S(2)}) collective-permute-start(bf16[8,64,128]{2,1,0:T(8,128)(2,1)S(1)} %get-tuple-element.100.near), channel_id=1, source_target_pairs={{0,4},{8,12},{16,20},{24,28},{4,0},{12,8},{20,16},{28,24},{1,5},{9... | collective-permute-start | bytes 393224 | tf_op jit(solution)/shard_map/ppermute | solution.py:469
  21.1 2.4 %collective-permute-start.11 = (bf16[8,64,128]{2,1,0:T(8,128)(2,1)S(1)}, bf16[8,64,128]{2,1,0:T(8,128)(2,1)S(1)}, u32[]{:S(2)}, u32[]{:S(2)}) collective-permute-start(bf16[8,64,128]{2,1,0:T(8,128)(2,1)S(1)} %get-tuple-element.101.far), channel_id=1, source_target_pairs={{4,8},{12,16},{20,24},{28,0},{8,4},{16,12},{24,20},{0,28},{5,9},{1... | collective-permute-start | bytes 393224 | tf_op jit(solution)/shard_map/ppermute | solution.py:469
  23.6 1.1 %collective-permute-done.7.other = bf16[352,128]{1,0:T(8,128)(2,1)S(1)} collective-permute-done((bf16[352,128]{1,0:T(8,128)(2,1)S(1)}, bf16[352,128]{1,0:T(8,128)(2,1)S(1)}, u32[]{:S(2)}, u32[]{:S(2)}) %collective-permute-start.7) | collective-permute-done | bytes 90144 | tf_op jit(solution)/shard_map/ppermute | solution.py:475
  24.7 1.1 %collective-permute-start.8 = (bf16[176,128]{1,0:T(8,128)(2,1)S(1)}, bf16[176,128]{1,0:T(8,128)(2,1)S(1)}, u32[]{:S(2)}, u32[]{:S(2)}) collective-permute-start(bf16[176,128]{1,0:T(8,128)(2,1)S(1)} %get-tuple-element.99), channel_id=1, source_target_pairs={{0,3},{1,2},{2,1},{3,0},{4,7},{5,6},{6,5},{7,4},{8,11},{9,10},{10,... | collective-permute-start | bytes 135176 | tf_op jit(solution)/shard_map/ppermute | solution.py:475
  25.8 2.4 %collective-permute-done.8.y = bf16[176,128]{1,0:T(8,128)(2,1)S(1)} collective-permute-done((bf16[176,128]{1,0:T(8,128)(2,1)S(1)}, bf16[176,128]{1,0:T(8,128)(2,1)S(1)}, u32[]{:S(2)}, u32[]{:S(2)}) %collective-permute-start.8) | collective-permute-done | bytes 45088 | tf_op jit(solution)/shard_map/ppermute | solution.py:475
  28.2 0.1 collective-permute-start.9
  28.4 3.4 %collective-permute-done.9.y = bf16[176,128]{1,0:T(8,128)(2,1)S(1)} collective-permute-done((bf16[176,128]{1,0:T(8,128)(2,1)S(1)}, bf16[176,128]{1,0:T(8,128)(2,1)S(1)}, u32[]{:S(2)}, u32[]{:S(2)}) %collective-permute-start.9) | collective-permute-done | bytes 45088 | tf_op jit(solution)/shard_map/ppermute | solution.py:475
  31.8 0.0 collective-permute-done.10.near_in
  31.8 0.0 collective-permute-done.11.far_in
  31.8 1.2 %collective-permute-start.12 = (bf16[176,128]{1,0:T(8,128)(2,1)S(1)}, bf16[176,128]{1,0:T(8,128)(2,1)S(1)}, u32[]{:S(2)}, u32[]{:S(2)}) collective-permute-start(bf16[176,128]{1,0:T(8,128)(2,1)S(1)} %shard_map.85.x), channel_id=1, source_target_pairs={{0,17},{1,16},{2,19},{3,18},{4,21},{5,20},{6,23},{7,22},{8,25},{9,... | collective-permute-start | bytes 135176 | tf_op jit(solution)/shard_map/ppermute | solution.py:475
  33.1 0.1 collective-permute-start.14
  33.1 1.3 %collective-permute-start.15 = (bf16[4,64,128]{2,1,0:T(8,128)(2,1)S(1)}, bf16[4,64,128]{2,1,0:T(8,128)(2,1)S(1)}, u32[]{:S(2)}, u32[]{:S(2)}) collective-permute-start(bf16[4,64,128]{2,1,0:T(8,128)(2,1)S(1)} %get-tuple-element.109), channel_id=1, source_target_pairs={{1,2},{3,0},{2,1},{0,3},{5,6},{7,4},{6,5},{4,7},{9,10},{11,8},{10,... | collective-permute-start | bytes 196616 | tf_op jit(solution)/shard_map/ppermute | solution.py:469
  34.4 1.1 %shard_map.87 = bf16[128,256]{1,0:T(8,128)(2,1)} custom-call(bf16[2,8,64,128]{3,2,1,0:T(8,128)(2,1)S(1)} %get-tuple-element.103.h_ref, bf16[2,2,128,128]{3,2,1,0:T(8,128)(2,1)S(1)} %get-tuple-element.65.d_ref), custom_call_target="tpu_custom_call" | custom-call | flops 45298484 | bytes 458752 | tf_op jit(solution)/shard_map/pallas_call | solution.py:20
  35.5 1.9 %collective-permute-done.12.y = bf16[176,128]{1,0:T(8,128)(2,1)S(1)} collective-permute-done((bf16[176,128]{1,0:T(8,128)(2,1)S(1)}, bf16[176,128]{1,0:T(8,128)(2,1)S(1)}, u32[]{:S(2)}, u32[]{:S(2)}) %collective-permute-start.12) | collective-permute-done | bytes 45088 | tf_op jit(solution)/shard_map/ppermute | solution.py:475
  37.4 0.5 collective-permute-start.13
  37.9 0.4 shard_map.89.w_ref
  38.3 2.3 %shard_map.90.acc_ref = f32[2,8,64,128]{3,2,1,0:T(8,128)S(1)} custom-call(bf16[8,64,128]{2,1,0:T(8,128)(2,1)S(1)} %get-tuple-element.100.near, bf16[8,64,128]{2,1,0:T(8,128)(2,1)S(1)} %get-tuple-element.101.far, bf16[8,64,128]{2,1,0:T(8,128)(2,1)S(1)} %collective-permute-done.10.near_in, bf16[8,64,128]{2,1,0:T(8,128)(2,1)S(1)} %collective-permute-done.11.far_in, ...), custom_call_target="tpu_custom_call" | custom-call | flops 452984832 | bytes 1269760 | tf_op jit(solution)/shard_map/pallas_call | solution.py:20
  40.6 0.6 %collective-permute-done.13.other = bf16[176,128]{1,0:T(8,128)(2,1)S(1)} collective-permute-done((bf16[176,128]{1,0:T(8,128)(2,1)S(1)}, bf16[176,128]{1,0:T(8,128)(2,1)S(1)}, u32[]{:S(2)}, u32[]{:S(2)}) %collective-permute-start.13) | collective-permute-done | bytes 45088 | tf_op jit(solution)/shard_map/ppermute | solution.py:475
  41.2 0.0 collective-permute-done.14.near
  41.2 0.1 collective-permute-start.16
  41.3 1.3 %shard_map.93 = f32[1024,128]{1,0:T(8,128)} custom-call(bf16[4,64,128]{2,1,0:T(8,128)(2,1)S(1)} %collective-permute-done.14.near, bf16[4,64,128]{2,1,0:T(8,128)(2,1)S(1)} %collective-permute-done.15.far, f32[2,8,64,128]{3,2,1,0:T(8,128)S(1)} %shard_map.90.acc_ref, bf16[3,3,64,192]{3,2,1,0:T(8,128)(2,1)S(1)} %shard_map.89.w_ref), custom_call_target="tpu_custom_call" | custom-call | flops 45298484 | bytes 1400832 | tf_op jit(solution)/shard_map/pallas_call | solution.py:20
  42.6 3.3 %collective-permute-done.16.other = bf16[352,128]{1,0:T(8,128)(2,1)S(1)} collective-permute-done((bf16[352,128]{1,0:T(8,128)(2,1)S(1)}, bf16[352,128]{1,0:T(8,128)(2,1)S(1)}, u32[]{:S(2)}, u32[]{:S(2)}) %collective-permute-start.16) | collective-permute-done | bytes 90144 | tf_op jit(solution)/shard_map/ppermute | solution.py:475
  45.9 0.2 collective-permute-start.17
  46.1 0.9 %shard_map.94 = (f32[3,3,64,192]{3,2,1,0:T(8,128)}, f32[2,2,128,128]{3,2,1,0:T(8,128)}) custom-call(bf16[704,128]{1,0:T(8,128)(2,1)S(1)} %shard_map.92.sums), custom_call_target="tpu_custom_call" | custom-call | tf_op jit(solution)/shard_map/pallas_call | solution.py:455
  47.0 0.4 collective-permute-done.17.sums
  47.4 0.8 %shard_map.95 = (f32[3,3,64,192]{3,2,1,0:T(8,128)}, f32[2,2,128,128]{3,2,1,0:T(8,128)}) custom-call(bf16[704,128]{1,0:T(8,128)(2,1)S(1)} %collective-permute-done.17.sums, f32[3,3,64,192]{3,2,1,0:T(8,128)} %get-tuple-element.116.refs_0_, f32[2,2,128,128]{3,2,1,0:T(8,128)} %get-tuple-element.117.refs_1_), custom_call_target="tpu_custom_call", output_to_operand_aliasing={{0}: (1, {}), {1}: (2, {})} | custom-call | tf_op jit(solution)/shard_map/pallas_call | solution.py:455
  (17 shorter events, 0.2 us)
Async XLA Ops:
  0.6 1.0 %copy-start.1 = (bf16[64,2,8,128]{3,2,1,0:T(8,128)(2,1)S(1)}, bf16[64,2,8,128]{3,2,1,0:T(8,128)(2,1)}, u32[]{:S(2)}) copy-start(bf16[64,2,8,128]{3,2,1,0:T(8,128)(2,1)} %f_ref.1) | copy-start | bytes 786436
  1.6 8.4 %copy-start.2 = (bf16[2,2,128,128]{3,2,1,0:T(8,128)(2,1)S(1)}, bf16[2,2,128,128]{3,2,1,0:T(8,128)(2,1)}, u32[]{:S(2)}) copy-start(bf16[2,2,128,128]{3,2,1,0:T(8,128)(2,1)} %refs_1_.1) | copy-start | bytes 393220
  1.6 8.4 %copy-start.3 = (bf16[128,1,256]{2,0,1:T(8,128)(2,1)S(1)}, bf16[128,1,256]{2,0,1:T(8,128)(2,1)}, u32[]{:S(2)}) copy-start(bf16[128,1,256]{2,0,1:T(8,128)(2,1)} %param.7) | copy-start | bytes 196612
  1.8 11.4 %collective-permute-start = (bf16[8,64,128]{2,1,0:T(8,128)(2,1)S(1)}, bf16[8,64,128]{2,1,0:T(8,128)(2,1)S(1)}, u32[]{:S(2)}, u32[]{:S(2)}) collective-permute-start(bf16[8,64,128]{2,1,0:T(8,128)(2,1)S(1)} %get-tuple-element.62.near), channel_id=1, source_target_pairs={{0,4},{8,12},{16,20},{24,28},{4,0},{12,8},{20,16},{28,24},{1,5},{9... | collective-permute-start | bytes 393224 | tf_op jit(solution)/shard_map/ppermute | solution.py:469
  4.8 8.4 %collective-permute-start.1 = (bf16[8,64,128]{2,1,0:T(8,128)(2,1)S(1)}, bf16[8,64,128]{2,1,0:T(8,128)(2,1)S(1)}, u32[]{:S(2)}, u32[]{:S(2)}) collective-permute-start(bf16[8,64,128]{2,1,0:T(8,128)(2,1)S(1)} %get-tuple-element.63.far), channel_id=1, source_target_pairs={{4,8},{12,16},{20,24},{28,0},{8,4},{16,12},{24,20},{0,28},{5,9},{1... | collective-permute-start | bytes 393224 | tf_op jit(solution)/shard_map/ppermute | solution.py:469
  8.4 4.8 %collective-permute-start.2 = (bf16[2,64,128]{2,1,0:T(8,128)(2,1)S(1)}, bf16[2,64,128]{2,1,0:T(8,128)(2,1)S(1)}, u32[]{:S(2)}, u32[]{:S(2)}) collective-permute-start(bf16[2,64,128]{2,1,0:T(8,128)(2,1)S(1)} %get-tuple-element.68), channel_id=1, source_target_pairs={{0,1},{2,3},{1,0},{3,2},{4,5},{6,7},{5,4},{7,6},{8,9},{10,11},{9,8... | collective-permute-start | bytes 98312 | tf_op jit(solution)/shard_map/ppermute | solution.py:469
  8.4 4.9 %collective-permute-start.3 = (bf16[2,64,128]{2,1,0:T(8,128)(2,1)S(1)}, bf16[2,64,128]{2,1,0:T(8,128)(2,1)S(1)}, u32[]{:S(2)}, u32[]{:S(2)}) collective-permute-start(bf16[2,64,128]{2,1,0:T(8,128)(2,1)S(1)} %get-tuple-element.69), channel_id=1, source_target_pairs={{1,2},{3,0},{2,1},{0,3},{5,6},{7,4},{6,5},{4,7},{9,10},{11,8},{10,... | collective-permute-start | bytes 98312 | tf_op jit(solution)/shard_map/ppermute | solution.py:469
  10.0 1.0 %copy-start = (bf16[3,3,64,192]{3,2,1,0:T(8,128)(2,1)S(1)}, bf16[3,3,64,192]{3,2,1,0:T(8,128)(2,1)}, u32[]{:S(2)}) copy-start(bf16[3,3,64,192]{3,2,1,0:T(8,128)(2,1)} %refs_0_.1) | copy-start | bytes 663556
  13.3 3.6 %collective-permute-start.4 = (bf16[2,64,128]{2,1,0:T(8,128)(2,1)S(1)}, bf16[2,64,128]{2,1,0:T(8,128)(2,1)S(1)}, u32[]{:S(2)}, u32[]{:S(2)}) collective-permute-start(bf16[2,64,128]{2,1,0:T(8,128)(2,1)S(1)} %get-tuple-element.79), channel_id=1, source_target_pairs={{1,2},{3,0},{2,1},{0,3},{5,6},{7,4},{6,5},{4,7},{9,10},{11,8},{10,... | collective-permute-start | bytes 98312 | tf_op jit(solution)/shard_map/ppermute | solution.py:469
  13.7 3.1 %collective-permute-start.5 = (bf16[2,64,128]{2,1,0:T(8,128)(2,1)S(1)}, bf16[2,64,128]{2,1,0:T(8,128)(2,1)S(1)}, u32[]{:S(2)}, u32[]{:S(2)}) collective-permute-start(bf16[2,64,128]{2,1,0:T(8,128)(2,1)S(1)} %get-tuple-element.80), channel_id=1, source_target_pairs={{0,1},{2,3},{1,0},{3,2},{4,5},{6,7},{5,4},{7,6},{8,9},{10,11},{9,8... | collective-permute-start | bytes 98312 | tf_op jit(solution)/shard_map/ppermute | solution.py:469
  18.4 1.5 %collective-permute-start.6 = (bf16[704,128]{1,0:T(8,128)(2,1)S(1)}, bf16[704,128]{1,0:T(8,128)(2,1)S(1)}, u32[]{:S(2)}, u32[]{:S(2)}) collective-permute-start(bf16[704,128]{1,0:T(8,128)(2,1)S(1)} %get-tuple-element.93), channel_id=1, source_target_pairs={{0,1},{1,0},{2,3},{3,2},{4,5},{5,4},{6,7},{7,6},{8,9},{9,8},{10,11... | collective-permute-start | bytes 540680 | tf_op jit(solution)/shard_map/ppermute | solution.py:475
  20.0 4.7 %collective-permute-start.7 = (bf16[352,128]{1,0:T(8,128)(2,1)S(1)}, bf16[352,128]{1,0:T(8,128)(2,1)S(1)}, u32[]{:S(2)}, u32[]{:S(2)}) collective-permute-start(bf16[352,128]{1,0:T(8,128)(2,1)S(1)} %get-tuple-element.97), channel_id=1, source_target_pairs={{0,9},{1,8},{2,11},{3,10},{4,13},{5,12},{6,15},{7,14},{8,1},{9,0},... | collective-permute-start | bytes 270344 | tf_op jit(solution)/shard_map/ppermute | solution.py:475
  20.1 11.7 %collective-permute-start.10 = (bf16[8,64,128]{2,1,0:T(8,128)(2,1)S(1)}, bf16[8,64,128]{2,1,0:T(8,128)(2,1)S(1)}, u32[]{:S(2)}, u32[]{:S(2)}) collective-permute-start(bf16[8,64,128]{2,1,0:T(8,128)(2,1)S(1)} %get-tuple-element.100.near), channel_id=1, source_target_pairs={{0,4},{8,12},{16,20},{24,28},{4,0},{12,8},{20,16},{28,24},{1,5},{9... | collective-permute-start | bytes 393224 | tf_op jit(solution)/shard_map/ppermute | solution.py:469
  21.1 10.7 %collective-permute-start.11 = (bf16[8,64,128]{2,1,0:T(8,128)(2,1)S(1)}, bf16[8,64,128]{2,1,0:T(8,128)(2,1)S(1)}, u32[]{:S(2)}, u32[]{:S(2)}) collective-permute-start(bf16[8,64,128]{2,1,0:T(8,128)(2,1)S(1)} %get-tuple-element.101.far), channel_id=1, source_target_pairs={{4,8},{12,16},{20,24},{28,0},{8,4},{16,12},{24,20},{0,28},{5,9},{1... | collective-permute-start | bytes 393224 | tf_op jit(solution)/shard_map/ppermute | solution.py:469
  24.7 3.5 %collective-permute-start.8 = (bf16[176,128]{1,0:T(8,128)(2,1)S(1)}, bf16[176,128]{1,0:T(8,128)(2,1)S(1)}, u32[]{:S(2)}, u32[]{:S(2)}) collective-permute-start(bf16[176,128]{1,0:T(8,128)(2,1)S(1)} %get-tuple-element.99), channel_id=1, source_target_pairs={{0,3},{1,2},{2,1},{3,0},{4,7},{5,6},{6,5},{7,4},{8,11},{9,10},{10,... | collective-permute-start | bytes 135176 | tf_op jit(solution)/shard_map/ppermute | solution.py:475
  28.2 3.5 %collective-permute-start.9 = (bf16[176,128]{1,0:T(8,128)(2,1)S(1)}, bf16[176,128]{1,0:T(8,128)(2,1)S(1)}, u32[]{:S(2)}, u32[]{:S(2)}) collective-permute-start(bf16[176,128]{1,0:T(8,128)(2,1)S(1)} %shard_map.84.x), channel_id=1, source_target_pairs={{0,5},{1,4},{2,7},{3,6},{4,1},{5,0},{6,3},{7,2},{8,13},{9,12},{10,... | collective-permute-start | bytes 135176 | tf_op jit(solution)/shard_map/ppermute | solution.py:475
  31.8 5.6 %collective-permute-start.12 = (bf16[176,128]{1,0:T(8,128)(2,1)S(1)}, bf16[176,128]{1,0:T(8,128)(2,1)S(1)}, u32[]{:S(2)}, u32[]{:S(2)}) collective-permute-start(bf16[176,128]{1,0:T(8,128)(2,1)S(1)} %shard_map.85.x), channel_id=1, source_target_pairs={{0,17},{1,16},{2,19},{3,18},{4,21},{5,20},{6,23},{7,22},{8,25},{9,... | collective-permute-start | bytes 135176 | tf_op jit(solution)/shard_map/ppermute | solution.py:475
  33.1 8.1 %collective-permute-start.14 = (bf16[4,64,128]{2,1,0:T(8,128)(2,1)S(1)}, bf16[4,64,128]{2,1,0:T(8,128)(2,1)S(1)}, u32[]{:S(2)}, u32[]{:S(2)}) collective-permute-start(bf16[4,64,128]{2,1,0:T(8,128)(2,1)S(1)} %get-tuple-element.108), channel_id=1, source_target_pairs={{0,1},{2,3},{1,0},{3,2},{4,5},{6,7},{5,4},{7,6},{8,9},{10,11},{9,8... | collective-permute-start | bytes 196616 | tf_op jit(solution)/shard_map/ppermute | solution.py:469
  33.1 8.0 %collective-permute-start.15 = (bf16[4,64,128]{2,1,0:T(8,128)(2,1)S(1)}, bf16[4,64,128]{2,1,0:T(8,128)(2,1)S(1)}, u32[]{:S(2)}, u32[]{:S(2)}) collective-permute-start(bf16[4,64,128]{2,1,0:T(8,128)(2,1)S(1)} %get-tuple-element.109), channel_id=1, source_target_pairs={{1,2},{3,0},{2,1},{0,3},{5,6},{7,4},{6,5},{4,7},{9,10},{11,8},{10,... | collective-permute-start | bytes 196616 | tf_op jit(solution)/shard_map/ppermute | solution.py:469
  37.4 3.7 %collective-permute-start.13 = (bf16[176,128]{1,0:T(8,128)(2,1)S(1)}, bf16[176,128]{1,0:T(8,128)(2,1)S(1)}, u32[]{:S(2)}, u32[]{:S(2)}) collective-permute-start(bf16[176,128]{1,0:T(8,128)(2,1)S(1)} %shard_map.86.mine), channel_id=1, source_target_pairs={{0,3},{1,2},{2,1},{3,0},{4,7},{5,6},{6,5},{7,4},{8,11},{9,10},{10,... | collective-permute-start | bytes 135176 | tf_op jit(solution)/shard_map/ppermute | solution.py:475
  41.2 4.7 %collective-permute-start.16 = (bf16[352,128]{1,0:T(8,128)(2,1)S(1)}, bf16[352,128]{1,0:T(8,128)(2,1)S(1)}, u32[]{:S(2)}, u32[]{:S(2)}) collective-permute-start(bf16[352,128]{1,0:T(8,128)(2,1)S(1)} %shard_map.88.mine), channel_id=1, source_target_pairs={{0,9},{1,8},{2,11},{3,10},{4,13},{5,12},{6,15},{7,14},{8,1},{9,0},... | collective-permute-start | bytes 270344 | tf_op jit(solution)/shard_map/ppermute | solution.py:475
  45.9 1.5 %collective-permute-start.17 = (bf16[704,128]{1,0:T(8,128)(2,1)S(1)}, bf16[704,128]{1,0:T(8,128)(2,1)S(1)}, u32[]{:S(2)}, u32[]{:S(2)}) collective-permute-start(bf16[704,128]{1,0:T(8,128)(2,1)S(1)} %shard_map.92.sums), channel_id=1, source_target_pairs={{0,1},{1,0},{2,3},{3,2},{4,5},{5,4},{6,7},{7,6},{8,9},{9,8},{10,11... | collective-permute-start | bytes 540680 | tf_op jit(solution)/shard_map/ppermute | solution.py:475

commit v29 on v26

--- a/solution.py
+++ b/solution.py
@@ -507,7 +507,7 @@
     shard = ((rows // 8, 128), BF16)
     (sums,) = call(add_kernel, [shard], [], 0, (keep, flip(send, "gy", 2)))
     (sums,) = call(add_kernel, [shard], [], 0, (sums, flip(sums, "gz", 1)))
-    sums, (near_in, far_in, weight_bwd) = tied(sums, near_in, far_in, weight_bwd)
+    sums, (near_in, far_in, section_out) = tied(sums, near_in, far_in, section_out)
     outside = (near_in, far_in)
     sends = call(edges_kernel, [edge, edge], [], 0, (*gates, *outside))
     beside = swapped(*sends, "gy")
@@ -518,7 +518,6 @@
     wide += [("gz", 1 << k) for k in range(2, lax.axis_size("gz").bit_length() - 1)]
     for axis, bit in wide:
         (sums,) = call(add_kernel, [shard], [], 0, (sums, flip(sums, axis, bit)))
-    sums, (section_out,) = tied(sums, section_out)
     (sums,) = call(
         functools.partial(join_kernel, axis="gy", bit=2), [((rows // 4, 128), BF16)], [], 0,
         (sums, flip(sums, "gy", 2)),

time: 48.6 us -> 48.6 us (level)
  no operation moved by 1% of the time
where the time goes in v29:
time: 48.6 us; the launch traced here: 48.4 us
  starting transfers between devices  17.4 us (36%)
  waiting for transfers between devices  16.8 us (35%)
  Pallas kernels  11.5 us (24%)
  local copies, waits for them, and re-layouts  1.91 us (4%)
  between operations  0.83 us (2%)
    ppermute x8, waiting for transfers between devices, flip(): lax.ppermute(cells, ('gz', 'gy'), [(i, i ^ mask) for i in range(lax.axis_...  15.2 us
    ppermute x10, starting transfers between devices, swap(): return lax.ppermute(cells, axis, pairs + [(b, a) for a, b in pairs])  13.9 us
    pallas_call x19, Pallas kernels, call(): pl.pallas_call(kernel, out_shape=[jax.ShapeDtypeStruct(s, d) for s, d in...  11.2 us
    ppermute x8, starting transfers between devices, flip(): lax.ppermute(cells, ('gz', 'gy'), [(i, i ^ mask) for i in range(lax.axis_...  3.46 us
    unnamed x8, local copies, waits for them, and re-layouts  1.91 us
    ppermute x10, waiting for transfers between devices, swap(): return lax.ppermute(cells, axis, pairs + [(b, a) for a, b in pairs])  1.54 us
  transfers between devices with their start and end apart: 18, of which 9 were waited for; matrix products, arithmetic and copies ran while one was open for 0% of the time, Pallas kernels for 18%

profile of v29, /device:TPU:0, one launch (start us, length us, event | category | flops | bytes accessed | tf_op | source)
XLA Modules:
  0.0 48.4 jit_solution(994551345116625979)
XLA Ops:
  0.6 0.9 %copy-done.1 = bf16[64,2,8,128]{3,2,1,0:T(8,128)(2,1)S(1)} copy-done((bf16[64,2,8,128]{3,2,1,0:T(8,128)(2,1)S(1)}, bf16[64,2,8,128]{3,2,1,0:T(8,128)(2,1)}, u32[]{:S(2)}) %copy-start.1) | copy-done | bytes 262168
  1.6 0.2 shard_map.75
  1.8 3.0 %collective-permute-start = (bf16[8,64,128]{2,1,0:T(8,128)(2,1)S(1)}, bf16[8,64,128]{2,1,0:T(8,128)(2,1)S(1)}, u32[]{:S(2)}, u32[]{:S(2)}) collective-permute-start(bf16[8,64,128]{2,1,0:T(8,128)(2,1)S(1)} %get-tuple-element.59.near), channel_id=1, source_target_pairs={{0,4},{8,12},{16,20},{24,28},{4,0},{12,8},{20,16},{28,24},{1,5},{9... | collective-permute-start | bytes 393224 | tf_op jit(solution)/shard_map/ppermute | solution.py:422
  4.8 3.5 %collective-permute-start.1 = (bf16[8,64,128]{2,1,0:T(8,128)(2,1)S(1)}, bf16[8,64,128]{2,1,0:T(8,128)(2,1)S(1)}, u32[]{:S(2)}, u32[]{:S(2)}) collective-permute-start(bf16[8,64,128]{2,1,0:T(8,128)(2,1)S(1)} %get-tuple-element.60.far), channel_id=1, source_target_pairs={{4,8},{12,16},{20,24},{28,0},{8,4},{16,12},{24,20},{0,28},{5,9},{1... | collective-permute-start | bytes 393224 | tf_op jit(solution)/shard_map/ppermute | solution.py:422
  8.4 0.0 collective-permute-start.2
  8.4 1.6 %collective-permute-start.3 = (bf16[2,64,128]{2,1,0:T(8,128)(2,1)S(1)}, bf16[2,64,128]{2,1,0:T(8,128)(2,1)S(1)}, u32[]{:S(2)}, u32[]{:S(2)}) collective-permute-start(bf16[2,64,128]{2,1,0:T(8,128)(2,1)S(1)} %get-tuple-element.66), channel_id=1, source_target_pairs={{1,2},{3,0},{2,1},{0,3},{5,6},{7,4},{6,5},{4,7},{9,10},{11,8},{10,... | collective-permute-start | bytes 98312 | tf_op jit(solution)/shard_map/ppermute | solution.py:422
  10.0 1.0 %copy-done = bf16[3,3,64,192]{3,2,1,0:T(8,128)(2,1)S(1)} copy-done((bf16[3,3,64,192]{3,2,1,0:T(8,128)(2,1)S(1)}, bf16[3,3,64,192]{3,2,1,0:T(8,128)(2,1)}, u32[]{:S(2)}) %copy-start) | copy-done | bytes 221208
  11.0 0.3 shard_map.76
  11.3 1.9 %shard_map.77 = (bf16[2,10,192,128]{3,2,1,0:T(8,128)(2,1)S(1)}, f32[2,8,64,128]{3,2,1,0:T(8,128)S(1)}, f32[2,8,64,128]{3,2,1,0:T(8,128)S(1)}) custom-call(bf16[8,64,128]{2,1,0:T(8,128)(2,1)S(1)} %get-tuple-element.59.near, bf16[8,64,128]{2,1,0:T(8,128)(2,1)S(1)} %get-tuple-element.60.far, bf16[3,3,64,192]{3,2,1,0:T(8,128)(2,1)S(1)} %get-tuple-element.61.w_ref, ...), custom_call_target="tpu_custom_call" | custom-call | flops 301989888 | bytes 2711552 | tf_op jit(solution)/shard_map/pallas_call | solution.py:20
  13.2 0.0 collective-permute-done.2.near_row
  13.2 0.0 collective-permute-done.3.far_row
  13.2 0.0 collective-permute-done.near.near_in
  13.3 0.0 collective-permute-done.1.far.far_in
  13.3 0.4 collective-permute-start.4
  13.7 0.5 collective-permute-start.5
  14.2 1.1 %shard_map.78 = (bf16[2,10,192,128]{3,2,1,0:T(8,128)(2,1)S(1)}, bf16[2,2,192,128]{3,2,1,0:T(8,128)(2,1)S(1)}, f32[2,2,64,128]{3,2,1,0:T(8,128)S(1)}, bf16[8,64,1...) custom-call(bf16[8,64,128]{2,1,0:T(8,128)(2,1)S(1)} %collective-permute-done.near.near_in,, ...), custom_call_target="tpu_custom_call" | custom-call | flops 150994944 | bytes 3432448 | tf_op jit(solution)/shard_map/pallas_call | solution.py:20
  15.3 1.5 %collective-permute-done.4.far = bf16[2,64,128]{2,1,0:T(8,128)(2,1)S(1)} collective-permute-done((bf16[2,64,128]{2,1,0:T(8,128)(2,1)S(1)}, bf16[2,64,128]{2,1,0:T(8,128)(2,1)S(1)}, u32[]{:S(2)}, u32[]{:S(2)}) %collective-permute-start.4) | collective-permute-done | bytes 32800 | tf_op jit(solution)/shard_map/ppermute | solution.py:422
  16.9 0.0 collective-permute-done.5.near
  16.9 0.3 shard_map.80
  17.2 1.2 %shard_map.81 = (f32[704,128]{1,0:T(8,128)S(1)}, bf16[704,128]{1,0:T(8,128)(2,1)S(1)}) custom-call(bf16[2,10,192,128]{3,2,1,0:T(8,128)(2,1)S(1)} %get-tuple-element.64.inner, bf16[2,10,192,128]{3,2,1,0:T(8,128)(2,1)S(1)} %get-tuple-element.74.outer, bf16[2,2,192,128]{3,2,1,0:T(8,128)(2,1)S(1)} %get-tuple-element.75.own_edges, ...), custom_call_target="tpu_custom_call" | custom-call | flops 452984832 | bytes 3489792 | tf_op jit(solution)/shard_map/pallas_call | solution.py:20
  18.4 0.2 collective-permute-start.6
  18.6 1.3 %collective-permute-done.6.other = bf16[704,128]{1,0:T(8,128)(2,1)S(1)} collective-permute-done((bf16[704,128]{1,0:T(8,128)(2,1)S(1)}, bf16[704,128]{1,0:T(8,128)(2,1)S(1)}, u32[]{:S(2)}, u32[]{:S(2)}) %collective-permute-start.6) | collective-permute-done | bytes 180256 | tf_op jit(solution)/shard_map/ppermute | solution.py:428
  19.9 0.1 shard_map.82
  20.0 0.1 collective-permute-start.7
  20.1 1.0 %collective-permute-start.10 = (bf16[8,64,128]{2,1,0:T(8,128)(2,1)S(1)}, bf16[8,64,128]{2,1,0:T(8,128)(2,1)S(1)}, u32[]{:S(2)}, u32[]{:S(2)}) collective-permute-start(bf16[8,64,128]{2,1,0:T(8,128)(2,1)S(1)} %get-tuple-element.97.near), channel_id=1, source_target_pairs={{0,4},{8,12},{16,20},{24,28},{4,0},{12,8},{20,16},{28,24},{1,5},{9... | collective-permute-start | bytes 393224 | tf_op jit(solution)/shard_map/ppermute | solution.py:422
  21.1 2.4 %collective-permute-start.11 = (bf16[8,64,128]{2,1,0:T(8,128)(2,1)S(1)}, bf16[8,64,128]{2,1,0:T(8,128)(2,1)S(1)}, u32[]{:S(2)}, u32[]{:S(2)}) collective-permute-start(bf16[8,64,128]{2,1,0:T(8,128)(2,1)S(1)} %get-tuple-element.98.far), channel_id=1, source_target_pairs={{4,8},{12,16},{20,24},{28,0},{8,4},{16,12},{24,20},{0,28},{5,9},{1... | collective-permute-start | bytes 393224 | tf_op jit(solution)/shard_map/ppermute | solution.py:422
  23.6 1.1 %collective-permute-done.7.other = bf16[352,128]{1,0:T(8,128)(2,1)S(1)} collective-permute-done((bf16[352,128]{1,0:T(8,128)(2,1)S(1)}, bf16[352,128]{1,0:T(8,128)(2,1)S(1)}, u32[]{:S(2)}, u32[]{:S(2)}) %collective-permute-start.7) | collective-permute-done | bytes 90144 | tf_op jit(solution)/shard_map/ppermute | solution.py:428
  24.7 1.1 %collective-permute-start.8 = (bf16[176,128]{1,0:T(8,128)(2,1)S(1)}, bf16[176,128]{1,0:T(8,128)(2,1)S(1)}, u32[]{:S(2)}, u32[]{:S(2)}) collective-permute-start(bf16[176,128]{1,0:T(8,128)(2,1)S(1)} %get-tuple-element.96), channel_id=1, source_target_pairs={{0,3},{1,2},{2,1},{3,0},{4,7},{5,6},{6,5},{7,4},{8,11},{9,10},{10,... | collective-permute-start | bytes 135176 | tf_op jit(solution)/shard_map/ppermute | solution.py:428
  25.8 2.4 %collective-permute-done.8.y = bf16[176,128]{1,0:T(8,128)(2,1)S(1)} collective-permute-done((bf16[176,128]{1,0:T(8,128)(2,1)S(1)}, bf16[176,128]{1,0:T(8,128)(2,1)S(1)}, u32[]{:S(2)}, u32[]{:S(2)}) %collective-permute-start.8) | collective-permute-done | bytes 45088 | tf_op jit(solution)/shard_map/ppermute | solution.py:428
  28.2 0.1 collective-permute-start.9
  28.4 1.1 %shard_map.86 = bf16[128,256]{1,0:T(8,128)(2,1)} custom-call(bf16[2,8,64,128]{3,2,1,0:T(8,128)(2,1)S(1)} %get-tuple-element.99.h_ref, bf16[2,2,128,128]{3,2,1,0:T(8,128)(2,1)S(1)} %get-tuple-element.62.d_ref), custom_call_target="tpu_custom_call" | custom-call | flops 45298484 | bytes 458752 | tf_op jit(solution)/shard_map/pallas_call | solution.py:20
  29.4 2.3 %collective-permute-done.9.y = bf16[176,128]{1,0:T(8,128)(2,1)S(1)} collective-permute-done((bf16[176,128]{1,0:T(8,128)(2,1)S(1)}, bf16[176,128]{1,0:T(8,128)(2,1)S(1)}, u32[]{:S(2)}, u32[]{:S(2)}) %collective-permute-start.9) | collective-permute-done | bytes 45088 | tf_op jit(solution)/shard_map/ppermute | solution.py:428
  31.8 0.0 collective-permute-done.10.near_in
  31.8 1.2 %collective-permute-start.12 = (bf16[176,128]{1,0:T(8,128)(2,1)S(1)}, bf16[176,128]{1,0:T(8,128)(2,1)S(1)}, u32[]{:S(2)}, u32[]{:S(2)}) collective-permute-start(bf16[176,128]{1,0:T(8,128)(2,1)S(1)} %shard_map.85.x), channel_id=1, source_target_pairs={{0,17},{1,16},{2,19},{3,18},{4,21},{5,20},{6,23},{7,22},{8,25},{9,... | collective-permute-start | bytes 135176 | tf_op jit(solution)/shard_map/ppermute | solution.py:428
  33.1 0.1 collective-permute-start.14
  33.1 1.3 %collective-permute-start.15 = (bf16[4,64,128]{2,1,0:T(8,128)(2,1)S(1)}, bf16[4,64,128]{2,1,0:T(8,128)(2,1)S(1)}, u32[]{:S(2)}, u32[]{:S(2)}) collective-permute-start(bf16[4,64,128]{2,1,0:T(8,128)(2,1)S(1)} %get-tuple-element.105), channel_id=1, source_target_pairs={{1,2},{3,0},{2,1},{0,3},{5,6},{7,4},{6,5},{4,7},{9,10},{11,8},{10,... | collective-permute-start | bytes 196616 | tf_op jit(solution)/shard_map/ppermute | solution.py:422
  34.4 3.0 %collective-permute-done.12.y = bf16[176,128]{1,0:T(8,128)(2,1)S(1)} collective-permute-done((bf16[176,128]{1,0:T(8,128)(2,1)S(1)}, bf16[176,128]{1,0:T(8,128)(2,1)S(1)}, u32[]{:S(2)}, u32[]{:S(2)}) %collective-permute-start.12) | collective-permute-done | bytes 45088 | tf_op jit(solution)/shard_map/ppermute | solution.py:428
  37.4 0.5 collective-permute-start.13
  37.9 0.4 shard_map.89.w_ref
  38.3 2.3 %shard_map.90.acc_ref = f32[2,8,64,128]{3,2,1,0:T(8,128)S(1)} custom-call(bf16[8,64,128]{2,1,0:T(8,128)(2,1)S(1)} %get-tuple-element.97.near, bf16[8,64,128]{2,1,0:T(8,128)(2,1)S(1)} %get-tuple-element.98.far, bf16[8,64,128]{2,1,0:T(8,128)(2,1)S(1)} %collective-permute-done.10.near_in, bf16[8,64,128]{2,1,0:T(8,128)(2,1)S(1)} %collective-permute-done.11.far_in, ...), custom_call_target="tpu_custom_call" | custom-call | flops 452984832 | bytes 1269760 | tf_op jit(solution)/shard_map/pallas_call | solution.py:20
  40.6 0.6 %collective-permute-done.13.other = bf16[176,128]{1,0:T(8,128)(2,1)S(1)} collective-permute-done((bf16[176,128]{1,0:T(8,128)(2,1)S(1)}, bf16[176,128]{1,0:T(8,128)(2,1)S(1)}, u32[]{:S(2)}, u32[]{:S(2)}) %collective-permute-start.13) | collective-permute-done | bytes 45088 | tf_op jit(solution)/shard_map/ppermute | solution.py:428
  41.2 0.0 collective-permute-done.14.near
  41.2 0.1 collective-permute-start.16
  41.3 1.3 %shard_map.93 = f32[1024,128]{1,0:T(8,128)} custom-call(bf16[4,64,128]{2,1,0:T(8,128)(2,1)S(1)} %collective-permute-done.14.near, bf16[4,64,128]{2,1,0:T(8,128)(2,1)S(1)} %collective-permute-done.15.far, f32[2,8,64,128]{3,2,1,0:T(8,128)S(1)} %shard_map.90.acc_ref, bf16[3,3,64,192]{3,2,1,0:T(8,128)(2,1)S(1)} %shard_map.89.w_ref), custom_call_target="tpu_custom_call" | custom-call | flops 45298484 | bytes 1400832 | tf_op jit(solution)/shard_map/pallas_call | solution.py:20
  42.6 3.3 %collective-permute-done.16.other = bf16[352,128]{1,0:T(8,128)(2,1)S(1)} collective-permute-done((bf16[352,128]{1,0:T(8,128)(2,1)S(1)}, bf16[352,128]{1,0:T(8,128)(2,1)S(1)}, u32[]{:S(2)}, u32[]{:S(2)}) %collective-permute-start.16) | collective-permute-done | bytes 90144 | tf_op jit(solution)/shard_map/ppermute | solution.py:428
  45.9 0.2 collective-permute-start.17
  46.1 1.3 %collective-permute-done.17.other = bf16[704,128]{1,0:T(8,128)(2,1)S(1)} collective-permute-done((bf16[704,128]{1,0:T(8,128)(2,1)S(1)}, bf16[704,128]{1,0:T(8,128)(2,1)S(1)}, u32[]{:S(2)}, u32[]{:S(2)}) %collective-permute-start.17) | collective-permute-done | bytes 180256 | tf_op jit(solution)/shard_map/ppermute | solution.py:428
  47.4 1.0 %shard_map.94 = (f32[3,3,64,192]{3,2,1,0:T(8,128)}, f32[2,2,128,128]{3,2,1,0:T(8,128)}) custom-call(bf16[704,128]{1,0:T(8,128)(2,1)S(1)} %shard_map.92.mine, bf16[704,128]{1,0:T(8,128)(2,1)S(1)} %collective-permute-done.17.other), custom_call_target="tpu_custom_call" | custom-call | bytes 1064960 | tf_op jit(solution)/shard_map/pallas_call | solution.py:20
  (16 shorter events, 0.2 us)
Async XLA Ops:
  0.6 1.0 %copy-start.1 = (bf16[64,2,8,128]{3,2,1,0:T(8,128)(2,1)S(1)}, bf16[64,2,8,128]{3,2,1,0:T(8,128)(2,1)}, u32[]{:S(2)}) copy-start(bf16[64,2,8,128]{3,2,1,0:T(8,128)(2,1)} %f_ref.1) | copy-start | bytes 786436
  1.6 8.4 %copy-start.2 = (bf16[2,2,128,128]{3,2,1,0:T(8,128)(2,1)S(1)}, bf16[2,2,128,128]{3,2,1,0:T(8,128)(2,1)}, u32[]{:S(2)}) copy-start(bf16[2,2,128,128]{3,2,1,0:T(8,128)(2,1)} %refs_1_.1) | copy-start | bytes 393220
  1.6 8.4 %copy-start.3 = (bf16[128,1,256]{2,0,1:T(8,128)(2,1)S(1)}, bf16[128,1,256]{2,0,1:T(8,128)(2,1)}, u32[]{:S(2)}) copy-start(bf16[128,1,256]{2,0,1:T(8,128)(2,1)} %param.7) | copy-start | bytes 196612
  1.8 11.4 %collective-permute-start = (bf16[8,64,128]{2,1,0:T(8,128)(2,1)S(1)}, bf16[8,64,128]{2,1,0:T(8,128)(2,1)S(1)}, u32[]{:S(2)}, u32[]{:S(2)}) collective-permute-start(bf16[8,64,128]{2,1,0:T(8,128)(2,1)S(1)} %get-tuple-element.59.near), channel_id=1, source_target_pairs={{0,4},{8,12},{16,20},{24,28},{4,0},{12,8},{20,16},{28,24},{1,5},{9... | collective-permute-start | bytes 393224 | tf_op jit(solution)/shard_map/ppermute | solution.py:422
  4.8 8.4 %collective-permute-start.1 = (bf16[8,64,128]{2,1,0:T(8,128)(2,1)S(1)}, bf16[8,64,128]{2,1,0:T(8,128)(2,1)S(1)}, u32[]{:S(2)}, u32[]{:S(2)}) collective-permute-start(bf16[8,64,128]{2,1,0:T(8,128)(2,1)S(1)} %get-tuple-element.60.far), channel_id=1, source_target_pairs={{4,8},{12,16},{20,24},{28,0},{8,4},{16,12},{24,20},{0,28},{5,9},{1... | collective-permute-start | bytes 393224 | tf_op jit(solution)/shard_map/ppermute | solution.py:422
  8.4 4.8 %collective-permute-start.2 = (bf16[2,64,128]{2,1,0:T(8,128)(2,1)S(1)}, bf16[2,64,128]{2,1,0:T(8,128)(2,1)S(1)}, u32[]{:S(2)}, u32[]{:S(2)}) collective-permute-start(bf16[2,64,128]{2,1,0:T(8,128)(2,1)S(1)} %get-tuple-element.65), channel_id=1, source_target_pairs={{0,1},{2,3},{1,0},{3,2},{4,5},{6,7},{5,4},{7,6},{8,9},{10,11},{9,8... | collective-permute-start | bytes 98312 | tf_op jit(solution)/shard_map/ppermute | solution.py:422
  8.4 4.9 %collective-permute-start.3 = (bf16[2,64,128]{2,1,0:T(8,128)(2,1)S(1)}, bf16[2,64,128]{2,1,0:T(8,128)(2,1)S(1)}, u32[]{:S(2)}, u32[]{:S(2)}) collective-permute-start(bf16[2,64,128]{2,1,0:T(8,128)(2,1)S(1)} %get-tuple-element.66), channel_id=1, source_target_pairs={{1,2},{3,0},{2,1},{0,3},{5,6},{7,4},{6,5},{4,7},{9,10},{11,8},{10,... | collective-permute-start | bytes 98312 | tf_op jit(solution)/shard_map/ppermute | solution.py:422
  10.0 1.0 %copy-start = (bf16[3,3,64,192]{3,2,1,0:T(8,128)(2,1)S(1)}, bf16[3,3,64,192]{3,2,1,0:T(8,128)(2,1)}, u32[]{:S(2)}) copy-start(bf16[3,3,64,192]{3,2,1,0:T(8,128)(2,1)} %refs_0_.1) | copy-start | bytes 663556
  13.3 3.6 %collective-permute-start.4 = (bf16[2,64,128]{2,1,0:T(8,128)(2,1)S(1)}, bf16[2,64,128]{2,1,0:T(8,128)(2,1)S(1)}, u32[]{:S(2)}, u32[]{:S(2)}) collective-permute-start(bf16[2,64,128]{2,1,0:T(8,128)(2,1)S(1)} %get-tuple-element.76), channel_id=1, source_target_pairs={{1,2},{3,0},{2,1},{0,3},{5,6},{7,4},{6,5},{4,7},{9,10},{11,8},{10,... | collective-permute-start | bytes 98312 | tf_op jit(solution)/shard_map/ppermute | solution.py:422
  13.7 3.1 %collective-permute-start.5 = (bf16[2,64,128]{2,1,0:T(8,128)(2,1)S(1)}, bf16[2,64,128]{2,1,0:T(8,128)(2,1)S(1)}, u32[]{:S(2)}, u32[]{:S(2)}) collective-permute-start(bf16[2,64,128]{2,1,0:T(8,128)(2,1)S(1)} %get-tuple-element.77), channel_id=1, source_target_pairs={{0,1},{2,3},{1,0},{3,2},{4,5},{6,7},{5,4},{7,6},{8,9},{10,11},{9,8... | collective-permute-start | bytes 98312 | tf_op jit(solution)/shard_map/ppermute | solution.py:422
  18.4 1.5 %collective-permute-start.6 = (bf16[704,128]{1,0:T(8,128)(2,1)S(1)}, bf16[704,128]{1,0:T(8,128)(2,1)S(1)}, u32[]{:S(2)}, u32[]{:S(2)}) collective-permute-start(bf16[704,128]{1,0:T(8,128)(2,1)S(1)} %get-tuple-element.90), channel_id=1, source_target_pairs={{0,1},{1,0},{2,3},{3,2},{4,5},{5,4},{6,7},{7,6},{8,9},{9,8},{10,11... | collective-permute-start | bytes 540680 | tf_op jit(solution)/shard_map/ppermute | solution.py:428
  20.0 4.7 %collective-permute-start.7 = (bf16[352,128]{1,0:T(8,128)(2,1)S(1)}, bf16[352,128]{1,0:T(8,128)(2,1)S(1)}, u32[]{:S(2)}, u32[]{:S(2)}) collective-permute-start(bf16[352,128]{1,0:T(8,128)(2,1)S(1)} %get-tuple-element.94), channel_id=1, source_target_pairs={{0,9},{1,8},{2,11},{3,10},{4,13},{5,12},{6,15},{7,14},{8,1},{9,0},... | collective-permute-start | bytes 270344 | tf_op jit(solution)/shard_map/ppermute | solution.py:428
  20.1 11.7 %collective-permute-start.10 = (bf16[8,64,128]{2,1,0:T(8,128)(2,1)S(1)}, bf16[8,64,128]{2,1,0:T(8,128)(2,1)S(1)}, u32[]{:S(2)}, u32[]{:S(2)}) collective-permute-start(bf16[8,64,128]{2,1,0:T(8,128)(2,1)S(1)} %get-tuple-element.97.near), channel_id=1, source_target_pairs={{0,4},{8,12},{16,20},{24,28},{4,0},{12,8},{20,16},{28,24},{1,5},{9... | collective-permute-start | bytes 393224 | tf_op jit(solution)/shard_map/ppermute | solution.py:422
  21.1 10.7 %collective-permute-start.11 = (bf16[8,64,128]{2,1,0:T(8,128)(2,1)S(1)}, bf16[8,64,128]{2,1,0:T(8,128)(2,1)S(1)}, u32[]{:S(2)}, u32[]{:S(2)}) collective-permute-start(bf16[8,64,128]{2,1,0:T(8,128)(2,1)S(1)} %get-tuple-element.98.far), channel_id=1, source_target_pairs={{4,8},{12,16},{20,24},{28,0},{8,4},{16,12},{24,20},{0,28},{5,9},{1... | collective-permute-start | bytes 393224 | tf_op jit(solution)/shard_map/ppermute | solution.py:422
  24.7 3.5 %collective-permute-start.8 = (bf16[176,128]{1,0:T(8,128)(2,1)S(1)}, bf16[176,128]{1,0:T(8,128)(2,1)S(1)}, u32[]{:S(2)}, u32[]{:S(2)}) collective-permute-start(bf16[176,128]{1,0:T(8,128)(2,1)S(1)} %get-tuple-element.96), channel_id=1, source_target_pairs={{0,3},{1,2},{2,1},{3,0},{4,7},{5,6},{6,5},{7,4},{8,11},{9,10},{10,... | collective-permute-start | bytes 135176 | tf_op jit(solution)/shard_map/ppermute | solution.py:428
  28.2 3.5 %collective-permute-start.9 = (bf16[176,128]{1,0:T(8,128)(2,1)S(1)}, bf16[176,128]{1,0:T(8,128)(2,1)S(1)}, u32[]{:S(2)}, u32[]{:S(2)}) collective-permute-start(bf16[176,128]{1,0:T(8,128)(2,1)S(1)} %shard_map.84.x), channel_id=1, source_target_pairs={{0,5},{1,4},{2,7},{3,6},{4,1},{5,0},{6,3},{7,2},{8,13},{9,12},{10,... | collective-permute-start | bytes 135176 | tf_op jit(solution)/shard_map/ppermute | solution.py:428
  31.8 5.6 %collective-permute-start.12 = (bf16[176,128]{1,0:T(8,128)(2,1)S(1)}, bf16[176,128]{1,0:T(8,128)(2,1)S(1)}, u32[]{:S(2)}, u32[]{:S(2)}) collective-permute-start(bf16[176,128]{1,0:T(8,128)(2,1)S(1)} %shard_map.85.x), channel_id=1, source_target_pairs={{0,17},{1,16},{2,19},{3,18},{4,21},{5,20},{6,23},{7,22},{8,25},{9,... | collective-permute-start | bytes 135176 | tf_op jit(solution)/shard_map/ppermute | solution.py:428
  33.1 8.1 %collective-permute-start.14 = (bf16[4,64,128]{2,1,0:T(8,128)(2,1)S(1)}, bf16[4,64,128]{2,1,0:T(8,128)(2,1)S(1)}, u32[]{:S(2)}, u32[]{:S(2)}) collective-permute-start(bf16[4,64,128]{2,1,0:T(8,128)(2,1)S(1)} %get-tuple-element.104), channel_id=1, source_target_pairs={{0,1},{2,3},{1,0},{3,2},{4,5},{6,7},{5,4},{7,6},{8,9},{10,11},{9,8... | collective-permute-start | bytes 196616 | tf_op jit(solution)/shard_map/ppermute | solution.py:422
  33.1 8.0 %collective-permute-start.15 = (bf16[4,64,128]{2,1,0:T(8,128)(2,1)S(1)}, bf16[4,64,128]{2,1,0:T(8,128)(2,1)S(1)}, u32[]{:S(2)}, u32[]{:S(2)}) collective-permute-start(bf16[4,64,128]{2,1,0:T(8,128)(2,1)S(1)} %get-tuple-element.105), channel_id=1, source_target_pairs={{1,2},{3,0},{2,1},{0,3},{5,6},{7,4},{6,5},{4,7},{9,10},{11,8},{10,... | collective-permute-start | bytes 196616 | tf_op jit(solution)/shard_map/ppermute | solution.py:422
  37.4 3.7 %collective-permute-start.13 = (bf16[176,128]{1,0:T(8,128)(2,1)S(1)}, bf16[176,128]{1,0:T(8,128)(2,1)S(1)}, u32[]{:S(2)}, u32[]{:S(2)}) collective-permute-start(bf16[176,128]{1,0:T(8,128)(2,1)S(1)} %shard_map.87.mine), channel_id=1, source_target_pairs={{0,3},{1,2},{2,1},{3,0},{4,7},{5,6},{6,5},{7,4},{8,11},{9,10},{10,... | collective-permute-start | bytes 135176 | tf_op jit(solution)/shard_map/ppermute | solution.py:428
  41.2 4.7 %collective-permute-start.16 = (bf16[352,128]{1,0:T(8,128)(2,1)S(1)}, bf16[352,128]{1,0:T(8,128)(2,1)S(1)}, u32[]{:S(2)}, u32[]{:S(2)}) collective-permute-start(bf16[352,128]{1,0:T(8,128)(2,1)S(1)} %shard_map.88.mine), channel_id=1, source_target_pairs={{0,9},{1,8},{2,11},{3,10},{4,13},{5,12},{6,15},{7,14},{8,1},{9,0},... | collective-permute-start | bytes 270344 | tf_op jit(solution)/shard_map/ppermute | solution.py:428
  45.9 1.5 %collective-permute-start.17 = (bf16[704,128]{1,0:T(8,128)(2,1)S(1)}, bf16[704,128]{1,0:T(8,128)(2,1)S(1)}, u32[]{:S(2)}, u32[]{:S(2)}) collective-permute-start(bf16[704,128]{1,0:T(8,128)(2,1)S(1)} %shard_map.92.mine), channel_id=1, source_target_pairs={{0,1},{1,0},{2,3},{3,2},{4,5},{5,4},{6,7},{7,6},{8,9},{9,8},{10,11... | collective-permute-start | bytes 540680 | tf_op jit(solution)/shard_map/ppermute | solution.py:428
